TPU v7x, 32 devices: a whole 2x2x4 slice. The times are simulated.
32 devices in a mesh: dp: 8 (over z, x), mp: 4 (over y, core).
Axes of the slice: x: 2, y: 2, z: 4, core: 2. Of those that a mesh axis runs over, the one named last changes fastest.
Arguments:
- hidden: bfloat16 [8192, 1536], P('dp'), may hold values from -6 to 6
- segments: int32 [8, 1024], P('dp'), may hold values from 0 to 15, never falling along the last dimension, each value on 1 to 512 neighbouring positions
- cotangent: bfloat16 [8192, 1536], P('dp', 'mp'), may hold values from -6 to 6
- in_weight: float32 [1536, 2, 3072], P('dp', None, 'mp'), may hold values from -0.15625 to 0.15625
- in_moment: float32 [1536, 2, 3072], P('dp', None, 'mp'), may hold values from -192 to 192
- bc_weight: float32 [1536, 256], P('dp'), may hold values from -0.15625 to 0.15625
- bc_moment: float32 [1536, 256], P('dp'), may hold values from -192 to 192
- step_weight: float32 [1536, 48], P('dp', 'mp'), may hold values from -0.15625 to 0.15625
- step_moment: float32 [1536, 48], P('dp', 'mp'), may hold values from -384 to 384
- out_weight: float32 [3072, 1536], P('mp', 'dp'), may hold values from -0.109375 to 0.109375
- out_moment: float32 [3072, 1536], P('mp', 'dp'), may hold values from -384 to 384
- conv_table: float32 [6, 3072], P(None, 'mp'), may hold values from -0.6 to 1.5
- conv_moment: float32 [6, 3072], P(None, 'mp'), may hold values from -192 to 192
- bc_table: float32 [5, 256], replicated, may hold values from -0.6 to 0.6
- bc_table_moment: float32 [5, 256], replicated, may hold values from -192 to 192
- head_table: float32 [3, 48], P(None, 'mp'), may hold values from -7 to 3
- head_moment: float32 [3, 48], P(None, 'mp'), may hold values from -1536 to 1536
- norm_gain: float32 [1536], replicated, may hold values from 0.5 to 1.5
- gain_moment: float32 [1536], replicated, may hold values from -192 to 192
Outputs:
- output: bfloat16 [8192, 1536], P('dp', 'mp')
- input_grad: bfloat16 [8192, 1536], P('dp')
- in_moment_next: float32 [1536, 2, 3072], P('dp', None, 'mp')
- in_weight_next: float32 [1536, 2, 3072], P('dp', None, 'mp')
- bc_moment_next: float32 [1536, 256], P('dp')
- bc_weight_next: float32 [1536, 256], P('dp')
- step_moment_next: float32 [1536, 48], P('dp', 'mp')
- step_weight_next: float32 [1536, 48], P('dp', 'mp')
- out_moment_next: float32 [3072, 1536], P('mp', 'dp')
- out_weight_next: float32 [3072, 1536], P('mp', 'dp')
- conv_moment_next: float32 [6, 3072], P(None, 'mp')
- bc_table_moment_next: float32 [5, 256], replicated
- head_moment_next: float32 [3, 48], P(None, 'mp')
- gain_moment_next: float32 [1536], replicated
Inputs may be any that keep to these rules, and one draw needn't show every extreme that they name: `segments`: within each sequence segment numbers never fall; a document spans 1 to 512 tokens and one spans exactly 512.
All inputs are finite; a program needn't handle non-finite values.
Results may differ from a plain program's by a relative error of at most 0.01.
Values may be sent and summed in bfloat16 or wider, within the bound.
No kernel may reach another device: no remote copies, remote signals or barrier semaphores. Data moves between devices by JAX's collectives and lax.ppermute only.
A program may use at most 128 MiB of HBM per device.

v0:
```python
import jax
import jax.numpy as jnp
from jax import lax
from jax.sharding import PartitionSpec as P

STRETCH = 256


epsilon = 1e-05
learn_rate = 0.0001
decay_rate = 0.1
highest = lax.Precision.HIGHEST


def causal_conv(values, taps, offset, seg):
    total = offset + taps[0] * values
    for lag in range(1, taps.shape[0]):
        moved = jnp.pad(values[:, :-lag], ((0, 0), (lag, 0), (0, 0)))
        seg_moved = jnp.pad(seg[:, :-lag], ((0, 0), (lag, 0)), constant_values=-1)
        keep = (seg_moved == seg).astype(values.dtype)
        total = total + taps[lag] * moved * keep[..., None]
    return total


def ssd_scan(x_act, steps, b_mat, c_mat, a_log, skip, seg):
    batch_seqs, seq_len, head_count, head_width = x_act.shape
    count = seq_len // STRETCH
    rates = -jnp.exp(a_log)
    dtype = x_act.dtype

    def split(array):
        return jnp.moveaxis(array.reshape((batch_seqs, count, STRETCH) + array.shape[2:]), 1, 0)

    order = jnp.arange(STRETCH)
    causal = order[:, None] >= order[None, :]

    def block(carry, pieces):
        state, last_seg = carry
        x_block, step_block, b_block, c_block, seg_block = pieces
        cum = jnp.cumsum(step_block * rates, axis=1)
        cum_heads = jnp.moveaxis(cum, 2, 1)
        step_heads = jnp.moveaxis(step_block, 2, 1)
        mask = (causal[None] & (seg_block[:, :, None] == seg_block[:, None, :]))[:, None]
        diff = cum_heads[:, :, :, None] - cum_heads[:, :, None, :]
        decay = jnp.where(mask, jnp.exp(jnp.where(mask, diff, 0.0)), 0.0)
        scores = jnp.einsum("stn,sun->stu", c_block, b_block, precision=highest)
        weights = scores[:, None] * decay * step_heads[:, :, None, :]
        inner_part = jnp.einsum("shtu,suhp->sthp", weights, x_block, precision=highest)
        carried = (seg_block == last_seg[:, None]).astype(dtype)
        entry = jnp.exp(cum) * carried[..., None]
        state_part = (
            jnp.einsum("stn,shpn->sthp", c_block, state, precision=highest) * entry[..., None]
        )
        tail = cum[:, -1, :]
        final_seg = seg_block[:, -1]
        same_end = (seg_block == final_seg[:, None]).astype(dtype)
        to_end = jnp.exp(tail[:, None, :] - cum) * same_end[..., None] * step_block
        kept = jnp.exp(tail) * (final_seg == last_seg).astype(dtype)[:, None]
        new_state = state * kept[:, :, None, None] + jnp.einsum(
            "suh,suhp,sun->shpn", to_end, x_block, b_block, precision=highest
        )
        result = inner_part + state_part + skip[None, None, :, None] * x_block
        return ((new_state, final_seg), result)

    start = (
        jnp.zeros((batch_seqs, head_count, head_width, b_mat.shape[-1]), dtype),
        jnp.full((batch_seqs,), -1, seg.dtype),
    )
    final_carry, blocks = lax.scan(
        jax.checkpoint(block),
        start,
        (split(x_act), split(steps), split(b_mat), split(c_mat), split(seg)),
    )
    return jnp.moveaxis(blocks, 0, 1).reshape(batch_seqs, seq_len, head_count, head_width)


def local_mix(x_pre, bc_pre, step_pre, conv_x, conv_bc, heads, seg):
    batch_seqs, seq_len = seg.shape
    x_act = jax.nn.silu(
        causal_conv(x_pre.reshape(batch_seqs, seq_len, -1), conv_x[:-1], conv_x[-1], seg)
    )
    bc_act = jax.nn.silu(
        causal_conv(bc_pre.reshape(batch_seqs, seq_len, -1), conv_bc[:-1], conv_bc[-1], seg)
    )
    half = bc_act.shape[-1] // 2
    steps = jax.nn.softplus(step_pre.reshape(batch_seqs, seq_len, -1) + heads[0])
    head_count = steps.shape[-1]
    head_width = x_act.shape[-1] // head_count
    mixed = ssd_scan(
        x_act.reshape(batch_seqs, seq_len, head_count, head_width),
        steps,
        bc_act[..., :half],
        bc_act[..., half:],
        heads[1],
        heads[2],
        seg,
    )
    return mixed.reshape(batch_seqs * seq_len, head_count * head_width)


def momentum(moment, grad):
    return 0.5 * moment + 0.5 * grad


def advance(weight, moment, grad):
    fresh = momentum(moment, grad)
    return (fresh, weight - learn_rate * fresh - learn_rate * decay_rate * weight)


def contract_last(left, right):
    return lax.dot_general(
        left, right, (((1,), (1,)), ((), ())), preferred_element_type=jnp.float32
    )


def contract_first(left, right):
    return lax.dot_general(
        left, right, (((0,), (0,)), ((), ())), preferred_element_type=jnp.float32
    )


def norm_back(grad_normed, normed, inv_rms, norm_gain, cot_rows):
    scaled = grad_normed * norm_gain
    return inv_rms * (
        scaled - normed * jnp.mean(scaled * normed, axis=-1, keepdims=True)
    ) + cot_rows.astype(jnp.float32)


def body(
    hidden,
    segments,
    cotangent,
    in_weight,
    in_moment,
    bc_weight,
    bc_moment,
    step_weight,
    step_moment,
    out_weight,
    out_moment,
    conv_table,
    conv_moment,
    bc_table,
    bc_table_moment,
    head_table,
    head_moment,
    norm_gain,
    gain_moment,
):
    packed = (
        in_weight.astype(jnp.bfloat16),
        bc_weight.astype(jnp.bfloat16),
        step_weight.astype(jnp.bfloat16),
        out_weight.astype(jnp.bfloat16),
    )
    full_in, full_bc, full_step, full_out = (
        lax.all_gather(packed[0], "dp", axis=0, tiled=True),
        lax.all_gather(packed[1], "dp", axis=0, tiled=True),
        lax.all_gather(packed[2], "dp", axis=0, tiled=True),
        lax.all_gather(packed[3], "dp", axis=1, tiled=True),
    )
    taps_count = conv_table.shape[0] - 2
    inputs = hidden.astype(jnp.float32)
    inv_rms = lax.rsqrt(jnp.mean(inputs * inputs, axis=-1, keepdims=True) + epsilon)
    normed = inputs * inv_rms
    normed_low = (normed * norm_gain).astype(jnp.bfloat16)
    both = jnp.einsum("td,dkc->tkc", normed_low, full_in, preferred_element_type=jnp.float32)
    gate_pre = both[:, 0]
    x_pre = both[:, 1]
    bc_pre = jnp.dot(normed_low, full_bc, preferred_element_type=jnp.float32)
    step_pre = jnp.dot(normed_low, full_step, preferred_element_type=jnp.float32)
    conv_part = conv_table[: taps_count + 1]
    gate_gain = conv_table[taps_count + 1]

    def mixer(x_in, bc_in, step_in, conv_in, bc_conv, heads):
        return local_mix(x_in, bc_in, step_in, conv_in, bc_conv, heads, segments)

    mixed, pullback = jax.vjp(mixer, x_pre, bc_pre, step_pre, conv_part, bc_table, head_table)
    gate_act = jax.nn.silu(gate_pre)
    gated = mixed * gate_act
    square_sum = lax.psum(jnp.sum(gated * gated, axis=-1), "mp")
    inner_total = gated.shape[1] * lax.axis_size("mp")
    scale_row = lax.rsqrt(square_sum / inner_total + epsilon)[:, None]
    gated_out = (gated * scale_row * gate_gain).astype(jnp.bfloat16)
    partial_out = jnp.dot(gated_out, full_out, preferred_element_type=jnp.float32)
    out_mine = lax.psum_scatter(partial_out, "mp", scatter_dimension=1, tiled=True)
    width = out_mine.shape[1]
    resid_mine = lax.dynamic_slice_in_dim(inputs, lax.axis_index("mp") * width, width, 1)
    output = (resid_mine + out_mine).astype(jnp.bfloat16)
    back_in, back_bc, back_step, back_out = (
        lax.all_gather(packed[0], "dp", axis=0, tiled=True),
        lax.all_gather(packed[1], "dp", axis=0, tiled=True),
        lax.all_gather(packed[2], "dp", axis=0, tiled=True),
        lax.all_gather(packed[3], "dp", axis=1, tiled=True),
    )
    full_cot = lax.all_gather(cotangent, "mp", axis=1, tiled=True)
    grad_gout = contract_last(full_cot, back_out)
    grad_outw = contract_first(gated_out, full_cot)
    grad_gate_gain = jnp.sum(grad_gout * gated * scale_row, axis=0)
    row_dot = lax.psum(jnp.sum(grad_gout * gate_gain * gated, axis=-1), "mp")
    grad_gated = (
        scale_row * gate_gain * grad_gout - gated * (scale_row**3 / inner_total) * row_dot[:, None]
    )
    grad_mixed = grad_gated * gate_act
    sigma = jax.nn.sigmoid(gate_pre)
    grad_gate_pre = grad_gated * mixed * sigma * (1.0 + gate_pre * (1.0 - sigma))
    grad_x_pre, grad_bc_part, grad_step_pre, grad_conv, grad_bct_part, grad_head = pullback(
        grad_mixed
    )
    grad_bc_pre, grad_bc_table = lax.psum((grad_bc_part, grad_bct_part), "mp")
    grad_both = jnp.stack([grad_gate_pre, grad_x_pre], axis=1).astype(jnp.bfloat16)
    grad_bc_low = grad_bc_pre.astype(jnp.bfloat16)
    grad_step_low = grad_step_pre.astype(jnp.bfloat16)
    grad_inw = jnp.einsum("td,tkc->dkc", normed_low, grad_both, preferred_element_type=jnp.float32)
    grad_bcw = contract_first(normed_low, grad_bc_low)
    grad_stepw = contract_first(normed_low, grad_step_low)
    share = grad_bc_low.shape[1] // lax.axis_size("mp")
    share_start = lax.axis_index("mp") * share
    bc_share = lax.dynamic_slice_in_dim(grad_bc_low, share_start, share, 1)
    weight_share = lax.dynamic_slice_in_dim(back_bc, share_start, share, 1)
    term = jnp.einsum("tkc,dkc->td", grad_both, back_in, preferred_element_type=jnp.float32)
    grad_normed = lax.psum(
        term + contract_last(grad_step_low, back_step) + contract_last(bc_share, weight_share), "mp"
    )
    grad_norm_gain = jnp.sum(grad_normed * normed, axis=0)
    input_grad = norm_back(grad_normed, normed, inv_rms, norm_gain, full_cot).astype(jnp.bfloat16)
    shard_in, shard_bc, shard_step, shard_out = (
        lax.psum_scatter(grad_inw, "dp", scatter_dimension=0, tiled=True),
        lax.psum_scatter(grad_bcw, "dp", scatter_dimension=0, tiled=True),
        lax.psum_scatter(grad_stepw, "dp", scatter_dimension=0, tiled=True),
        lax.psum_scatter(grad_outw, "dp", scatter_dimension=1, tiled=True),
    )
    grad_conv_all = jnp.concatenate([grad_conv, grad_gate_gain[None]], axis=0)
    total_gain, total_conv, total_bct, total_head = lax.psum(
        (grad_norm_gain, grad_conv_all, grad_bc_table, grad_head), "dp"
    )
    in_m, in_w = advance(in_weight, in_moment, shard_in)
    bc_m, bc_w = advance(bc_weight, bc_moment, shard_bc)
    step_m, step_w = advance(step_weight, step_moment, shard_step)
    out_m, out_w = advance(out_weight, out_moment, shard_out)
    conv_m = momentum(conv_moment, total_conv)
    bct_m = momentum(bc_table_moment, total_bct)
    head_m = momentum(head_moment, total_head)
    gain_m = momentum(gain_moment, total_gain)
    return (
        output,
        input_grad,
        in_m,
        in_w,
        bc_m,
        bc_w,
        step_m,
        step_w,
        out_m,
        out_w,
        conv_m,
        bct_m,
        head_m,
        gain_m,
    )


def solution(mesh):
    placed = (
        P("dp", None),
        P("dp", None),
        P("dp", "mp"),
        P("dp", None, "mp"),
        P("dp", None, "mp"),
        P("dp", None),
        P("dp", None),
        P("dp", "mp"),
        P("dp", "mp"),
        P("mp", "dp"),
        P("mp", "dp"),
        P(None, "mp"),
        P(None, "mp"),
        P(),
        P(),
        P(None, "mp"),
        P(None, "mp"),
        P(),
        P(),
    )
    return jax.shard_map(
        body,
        mesh=mesh,
        in_specs=placed,
        out_specs=(
            P("dp", "mp"),
            P("dp", None),
            P("dp", None, "mp"),
            P("dp", None, "mp"),
            P("dp", None),
            P("dp", None),
            P("dp", "mp"),
            P("dp", "mp"),
            P("mp", "dp"),
            P("mp", "dp"),
            P(None, "mp"),
            P(),
            P(None, "mp"),
            P(),
        ),
        check_vma=False,
    )
```

profile of v0, /device:TPU:0, one launch (start us, length us, event | category | flops | bytes accessed | tf_op | source)
XLA Modules:
  0.0 1168.4 jit_solution(6376375035031857652)
XLA Ops:
  14.2 32.7 %all-gather = bf16[8,192,12]{1,2,0:T(8,128)(2,1)S(1)} all-gather(bf16[1,192,12]{1,2,0:T(8,128)(2,1)S(1)} %convert_bitcast_fusion), channel_id=1, replica_groups=mesh['dp'=8,'mp'=4] {'dp'}, dimensions={0}, use_global_device_ids=true | all-gather | bytes 41472 | tf_op jit(solution)/shard_map/all_gather | solution.py:159
  49.0 2.5 multiply_convert_fusion
  51.6 3.5 compare_select_fusion.2
  56.3 34.1 %all_gather.21 = bf16[1536,256]{1,0:T(8,128)(2,1)S(1)} all-gather(bf16[192,256]{1,0:T(8,128)(2,1)S(1)} %convert_element_type.112), channel_id=1, replica_groups=mesh['dp'=8,'mp'=4] {'dp'}, dimensions={0}, use_global_device_ids=true | all-gather | bytes 884736 | tf_op jit(solution)/shard_map/all_gather | solution.py:158
  90.4 3.2 fusion.177
  97.9 10.1 all-gather.5.cloned.1.call-done
  108.0 8.1 fusion.137
  118.5 4.3 fusion.139
  125.2 3.4 reshape.1351
  131.0 85.8 %while.48 = (s32[]{:T(128)}, f32[1,12,64,128]{3,2,1,0:T(8,128)S(1)}, s32[1]{0:T(128)}, f32[4,1,256,12,64]{2,4,3,1,0:T(8,128)}, f32[4,1,12,64,128]{4,3,2,1,0:T(8,...) while((s32[]{:T(128)}, ...), condition=%wide.region_4.5_spmd.clone, body=%wide.region_1.4_spmd.clone.sunk | while | flops 1314638848 | bytes 8433130 | solution.py:69
  144.5 6.0 fusion.253
  165.8 6.1 fusion.253
  187.2 6.2 fusion.253
  208.7 6.1 fusion.253
  219.2 3.0 squeeze.145
  222.1 4.1 copy.263
  232.1 5.7 psum.63
  237.8 9.9 multiply_reduce_fusion.7
  247.7 6.7 psum.64
  254.4 6.2 fusion.143
  263.0 3.0 reshape.1355
  270.7 275.1 %while.49 = (s32[]{:T(128)}, f32[12]{0:T(128)}, f32[12]{0:T(128)}, f32[1,12,64,128]{3,2,1,0:T(8,128)}, f32[4,1,256,12,64]{2,0,4,3,1:T(4,128)}, /*index=5*/f32[4,...) while((s32[]{:T(128)}, f32[12]{0:T(128)}, f32[12]{0:T(128)}, ...), condition=%wide.region_24.25_spmd.clone, body=%wide.region_10.24_spmd.clone.sunk | while | flops 3039735808 | bytes 32546276 | solution.py:69
  283.4 2.7 constant_dynamic-slice_fusion.12
  293.3 5.6 fusion.272
  307.3 2.5 reduce-window.74
  313.7 4.3 fusion.278
  318.9 17.9 %dynamic_update_slice.84 = f32[4,1,256,12,64]{2,0,4,3,1:T(4,128)} dynamic-update-slice(f32[4,1,256,12,64]{2,0,4,3,1:T(4,128)} %get-tuple-element.1445, f32[1,1,256,12,64]{2,0,4,3,1:T(1,128)S(1)} %copy.436, s32[]{:T(128)S(6)} %sub.351, s32[]{:T(128)} %constant.171.clone.1..sunk.1, s32[]{:T(128)} %constant.171.clone.1..sunk.1, s32[]{:T(128)} %constant.171.clone.1..sunk.1, s32[]{:T(128)} %constant.171.clone.1..sunk.1) | dynamic-update-slice | bytes 1572868 | tf_op jit(solution)/shard_map/transpose(jvp())/while/body/jit(dynamic_update_index_in_dim)/dynamic_update_slice | solution.py:69
  347.9 2.7 constant_dynamic-slice_fusion.12
  358.8 5.6 fusion.272
  372.7 2.5 reduce-window.74
  380.4 4.3 fusion.278
  385.5 17.9 %dynamic_update_slice.84 = f32[4,1,256,12,64]{2,0,4,3,1:T(4,128)} dynamic-update-slice(f32[4,1,256,12,64]{2,0,4,3,1:T(4,128)} %get-tuple-element.1445, f32[1,1,256,12,64]{2,0,4,3,1:T(1,128)S(1)} %copy.436, s32[]{:T(128)S(6)} %sub.351, s32[]{:T(128)} %constant.171.clone.1..sunk.1, s32[]{:T(128)} %constant.171.clone.1..sunk.1, s32[]{:T(128)} %constant.171.clone.1..sunk.1, s32[]{:T(128)} %constant.171.clone.1..sunk.1) | dynamic-update-slice | bytes 1572868 | tf_op jit(solution)/shard_map/transpose(jvp())/while/body/jit(dynamic_update_index_in_dim)/dynamic_update_slice | solution.py:69
  414.5 2.7 constant_dynamic-slice_fusion.12
  425.4 5.6 fusion.272
  447.0 4.3 fusion.278
  452.2 17.9 %dynamic_update_slice.84 = f32[4,1,256,12,64]{2,0,4,3,1:T(4,128)} dynamic-update-slice(f32[4,1,256,12,64]{2,0,4,3,1:T(4,128)} %get-tuple-element.1445, f32[1,1,256,12,64]{2,0,4,3,1:T(1,128)S(1)} %copy.436, s32[]{:T(128)S(6)} %sub.351, s32[]{:T(128)} %constant.171.clone.1..sunk.1, s32[]{:T(128)} %constant.171.clone.1..sunk.1, s32[]{:T(128)} %constant.171.clone.1..sunk.1, s32[]{:T(128)} %constant.171.clone.1..sunk.1) | dynamic-update-slice | bytes 1572868 | tf_op jit(solution)/shard_map/transpose(jvp())/while/body/jit(dynamic_update_index_in_dim)/dynamic_update_slice | solution.py:69
  481.1 2.7 constant_dynamic-slice_fusion.12
  492.0 5.6 fusion.272
  513.6 4.3 fusion.278
  518.8 17.9 %dynamic_update_slice.84 = f32[4,1,256,12,64]{2,0,4,3,1:T(4,128)} dynamic-update-slice(f32[4,1,256,12,64]{2,0,4,3,1:T(4,128)} %get-tuple-element.1445, f32[1,1,256,12,64]{2,0,4,3,1:T(1,128)S(1)} %copy.436, s32[]{:T(128)S(6)} %sub.351, s32[]{:T(128)} %constant.171.clone.1..sunk.1, s32[]{:T(128)} %constant.171.clone.1..sunk.1, s32[]{:T(128)} %constant.171.clone.1..sunk.1, s32[]{:T(128)} %constant.171.clone.1..sunk.1) | dynamic-update-slice | bytes 1572868 | tf_op jit(solution)/shard_map/transpose(jvp())/while/body/jit(dynamic_update_index_in_dim)/dynamic_update_slice | solution.py:69
  548.1 4.5 fusion.157
  552.5 4.0 fusion.155
  556.5 3.0 transpose.199
  559.5 3.7 copy.277
  563.2 4.2 multiply_reduce_fusion.11
  579.5 27.4 %all-reduce.39 = (bf16[1024,256]{1,0:T(8,128)(2,1)}, f32[5,256]{1,0:T(8,128)}) all-reduce(f32[1024,256]{1,0:T(8,128)} %get-tuple-element.1087, f32[5,256]{1,0:T(8,128)S(1)} %pad_add_fusion.2), channel_id=1, replica_groups=mesh['dp'=8,'mp'=4] {'mp'}, use_global_device_ids=true, to_apply=%region_25.26 | all-reduce | flops 263424 | bytes 1583104 | tf_op jit(solution)/shard_map/psum | solution.py:210
  606.9 5.4 fusion.166
  612.4 7.6 fusion.140
  620.0 3.8 fusion.126
  624.1 4.3 fusion.178
  628.6 6.9 fusion.164
  635.5 6.4 fusion.165
  643.8 9.5 fusion.135
  655.2 3.5 convert_element_type.108
  662.4 98.8 %all-reduce.38.cloned.1.call-done = f32[1024,1536]{1,0:T(8,128)} async-done(((f32[1024,1536]{1,0:T(8,128)}), f32[1024,1536]{1,0:T(8,128)}) %all-reduce.38.cloned.1.call-update) | async-done | bytes 6291472 | tf_op jit(solution)/shard_map/psum | solution.py:222
  761.2 4.5 multiply_reduce_fusion.4
  765.7 39.6 %all-reduce.33 = (f32[6,768]{1,0:T(8,128)}, f32[5,256]{1,0:T(8,128)}, f32[3,12]{1,0:T(4,128)}, f32[1536]{0:T(1024)}) all-reduce(f32[6,768]{1,0:T(8,128)} %pad_maximum_fusion.3, f32[5,256]{1,0:T(8,128)} %get-tuple-element.1036, f32[3,12]{1,0:T(4,128)S(1)} %pad_add_fusion.4, ...), channel_id=1, replica_groups=mesh['dp'=8,'mp'=4] {'dp'}, use_global_device_ids=true, to_apply=%region_38.39 | all-reduce | flops 7460 | bytes 59680 | tf_op jit(solution)/shard_map/psum | solution.py:234
  811.2 18.9 %reduce-scatter.12.cloned.1.call-done = f32[192,256]{1,0:T(8,128)} async-done(((f32[1536,256]{1,0:T(8,128)}), f32[192,256]{1,0:T(8,128)}) %reduce-scatter.12.cloned.1.call-update) | async-done | bytes 196624 | tf_op jit(solution)/shard_map/reduce_scatter | solution.py:229
  831.8 5.9 add_convert_fusion
  837.7 90.5 %reduce-scatter.14.cloned.1.call-done = f32[768,192]{0,1:T(8,128)} async-done(((f32[768,1536]{0,1:T(8,128)}), f32[768,192]{0,1:T(8,128)}) %reduce-scatter.14.cloned.1.call-update) | async-done | bytes 589840 | tf_op jit(solution)/shard_map/reduce_scatter | solution.py:231
  928.2 2.6 multiply_subtract_fusion.2
  930.7 58.1 %reduce-scatter.8.cloned.1.call-done = f32[1024,384]{1,0:T(8,128)} async-done(((f32[1024,1536]{1,0:T(8,128)}), f32[1024,384]{1,0:T(8,128)}) %reduce-scatter.8.cloned.1.call-update) | async-done | bytes 1572880 | tf_op jit(solution)/shard_map/reduce_scatter | solution.py:186
  988.9 2.9 add_convert_fusion.2
  991.8 164.5 %reduce-scatter.10.cloned.1.call-done = f32[192,2,768]{2,0,1:T(8,128)} async-done(((f32[1536,2,768]{2,0,1:T(8,128)}), f32[192,2,768]{2,0,1:T(8,128)}) %reduce-scatter.10.cloned.1.call-update) | async-done | bytes 1179664 | tf_op jit(solution)/shard_map/reduce_scatter | solution.py:228
  (719 shorter events, 258.0 us)
Async XLA Ops:
  7.2 6.2 copy-start.2
  7.2 100.8 %all-gather.5.cloned.1.call-start = ((), (), s32[]{:S(2)}) async-start(), calls=%async_computation.5 | async-start | bytes 5308416 | tf_op jit(solution)/shard_map/all_gather | solution.py:157
  9.6 39.5 %copy-start.47 = (f32[1536]{0:T(1024)S(1)}, f32[1536]{0:T(1024)}, u32[]{:S(2)}) copy-start(f32[1536]{0:T(1024)} %param.40) | copy-start | bytes 18436
  9.6 228.2 %all-gather.7.cloned.1.call-start = ((), (), s32[]{:S(2)}) async-start(), calls=%async_computation.6 | async-start | bytes 2654208 | tf_op jit(solution)/shard_map/all_gather | solution.py:160
  11.5 226.3 %all-gather.9.cloned.1.call-start = ((), (), s32[]{:S(2)}) async-start(), calls=%async_computation.8 | async-start | bytes 3932160 | tf_op jit(solution)/shard_map/all_gather | solution.py:196
  12.2 648.6 %reduce-scatter.16.cloned.1.call-start = ((), (), s32[]{:S(2)}) async-start(), calls=%async_computation.13 | async-start | bytes 884736
  14.1 37.4 %copy-start.51 = (f32[1024]{0:T(1024)}, f32[1024]{0:T(1024)S(1)}, u32[]{:S(2)}) copy-start(f32[1024]{0:T(1024)S(1)} %add_rsqrt_fusion.1) | copy-start | bytes 12292
  56.3 62.2 %copy-start.53 = (f32[768]{0:T(1024)}, f32[768]{0:T(1024)S(1)}, u32[]{:S(2)}) copy-start(f32[768]{0:T(1024)S(1)} %get-tuple-element.966) | copy-start | bytes 9220
  94.7 23.8 %copy-start.41 = (f32[1,1024]{1,0:T(1,128)}, f32[1,1024]{1,0:T(1,128)S(1)}, u32[]{:S(2)}) copy-start(f32[1,1024]{1,0:T(1,128)S(1)} %get-tuple-element.1103) | copy-start | bytes 12292
  94.7 23.8 %copy-start.43 = (f32[1,1024]{1,0:T(1,128)}, f32[1,1024]{1,0:T(1,128)S(1)}, u32[]{:S(2)}) copy-start(f32[1,1024]{1,0:T(1,128)S(1)} %get-tuple-element.1104) | copy-start | bytes 12292
  94.7 23.8 %copy-start.45 = (f32[1,1024]{1,0:T(1,128)}, f32[1,1024]{1,0:T(1,128)S(1)}, u32[]{:S(2)}) copy-start(f32[1,1024]{1,0:T(1,128)S(1)} %get-tuple-element.1105) | copy-start | bytes 12292
  116.1 6.7 copy-start.9
  229.7 8.1 copy-start.64
  237.7 16.7 %copy-start.62 = (f32[1024]{0:T(1024)}, f32[1024]{0:T(1024)S(1)}, u32[]{:S(2)}) copy-start(f32[1024]{0:T(1024)S(1)} %get-tuple-element.1102) | copy-start | bytes 12292
  289.3 12.7 %copy-start.6 = (f32[1,256,128]{2,1,0:T(8,128)}, f32[1,256,128]{2,1,0:T(8,128)S(1)}, u32[]{:S(2)}) copy-start(f32[1,256,128]{2,1,0:T(8,128)S(1)} %get-tuple-element.1350) | copy-start | bytes 393220 | tf_op jit(solution)/shard_map/transpose(jvp())/while
  292.7 6.3 copy-start.35
  292.8 6.2 copy-start.36
  301.8 9.6 copy-start.37
  302.1 9.4 copy-start.40
  303.9 9.8 copy-start.8
  318.9 25.6 %copy-start.7 = (f32[1,256,128]{2,1,0:T(8,128)S(1)}, f32[1,256,128]{2,1,0:T(8,128)}, u32[]{:S(2)}) copy-start(f32[1,256,128]{2,1,0:T(8,128)} %copy-done.6) | copy-start | bytes 393220 | tf_op jit(solution)/shard_map/transpose(jvp())/while
  336.8 7.7 copy-start.12
  353.8 13.7 %copy-start.6 = (f32[1,256,128]{2,1,0:T(8,128)}, f32[1,256,128]{2,1,0:T(8,128)S(1)}, u32[]{:S(2)}) copy-start(f32[1,256,128]{2,1,0:T(8,128)S(1)} %get-tuple-element.1350) | copy-start | bytes 393220 | tf_op jit(solution)/shard_map/transpose(jvp())/while
  358.1 6.3 copy-start.35
  358.2 6.2 copy-start.36
  367.2 10.2 copy-start.37
  367.5 10.0 copy-start.40
  369.3 11.0 copy-start.8
  385.5 25.5 %copy-start.7 = (f32[1,256,128]{2,1,0:T(8,128)S(1)}, f32[1,256,128]{2,1,0:T(8,128)}, u32[]{:S(2)}) copy-start(f32[1,256,128]{2,1,0:T(8,128)} %copy-done.6) | copy-start | bytes 393220 | tf_op jit(solution)/shard_map/transpose(jvp())/while
  403.4 7.7 copy-start.12
  420.4 13.7 %copy-start.6 = (f32[1,256,128]{2,1,0:T(8,128)}, f32[1,256,128]{2,1,0:T(8,128)S(1)}, u32[]{:S(2)}) copy-start(f32[1,256,128]{2,1,0:T(8,128)S(1)} %get-tuple-element.1350) | copy-start | bytes 393220 | tf_op jit(solution)/shard_map/transpose(jvp())/while
  424.8 6.3 copy-start.35
  433.9 10.2 copy-start.37
  434.2 10.0 copy-start.40
  436.0 11.0 copy-start.8
  452.2 25.5 %copy-start.7 = (f32[1,256,128]{2,1,0:T(8,128)S(1)}, f32[1,256,128]{2,1,0:T(8,128)}, u32[]{:S(2)}) copy-start(f32[1,256,128]{2,1,0:T(8,128)} %copy-done.6) | copy-start | bytes 393220 | tf_op jit(solution)/shard_map/transpose(jvp())/while
  470.1 7.7 copy-start.12
  487.1 13.7 %copy-start.6 = (f32[1,256,128]{2,1,0:T(8,128)}, f32[1,256,128]{2,1,0:T(8,128)S(1)}, u32[]{:S(2)}) copy-start(f32[1,256,128]{2,1,0:T(8,128)S(1)} %get-tuple-element.1350) | copy-start | bytes 393220 | tf_op jit(solution)/shard_map/transpose(jvp())/while
  491.4 6.3 copy-start.35
  500.5 10.2 copy-start.37
  500.8 10.0 copy-start.40
  502.6 11.0 copy-start.8
  518.8 25.6 %copy-start.7 = (f32[1,256,128]{2,1,0:T(8,128)S(1)}, f32[1,256,128]{2,1,0:T(8,128)}, u32[]{:S(2)}) copy-start(f32[1,256,128]{2,1,0:T(8,128)} %copy-done.6) | copy-start | bytes 393220 | tf_op jit(solution)/shard_map/transpose(jvp())/while
  536.7 7.7 copy-start.12
  578.1 28.9 %copy-start.11 = (f32[1,1024,768]{2,1,0:T(8,128)S(1)}, f32[1,1024,768]{2,1,0:T(8,128)}, u32[]{:S(2)}) copy-start(f32[1,1024,768]{2,1,0:T(8,128)} %copy-done.10) | copy-start | bytes 9437188
  578.1 28.9 %copy-start.54 = (f32[768]{0:T(1024)S(1)}, f32[768]{0:T(1024)}, u32[]{:S(2)}) copy-start(f32[768]{0:T(1024)} %copy-done.53) | copy-start | bytes 9220
  579.4 181.8 %all-reduce.38.cloned.1.call-start = ((), (), s32[]{:S(2)}) async-start(), calls=%async_computation.9 | async-start | bytes 12582912 | tf_op jit(solution)/shard_map/psum | solution.py:222
  606.9 13.1 %slice-start = ((s8[6291456]{0:T(1024)(128)(4,1)}), s8[4194304]{0:T(1024)(128)(4,1)S(1)}, s32[]{:S(2)}) async-start(s8[6291456]{0:T(1024)(128)(4,1)} %bitcast.723), calls=%async_computation.14 | async-start | bytes 8388608
  612.3 7.6 copy-start.29
  612.3 7.6 slice-start.1
  612.3 7.6 copy-start.24
  612.4 7.6 copy-start.39
  623.9 206.2 %reduce-scatter.12.cloned.1.call-start = ((), (), s32[]{:S(2)}) async-start(), calls=%async_computation.11 | async-start | bytes 1769472 | tf_op jit(solution)/shard_map/reduce_scatter | solution.py:229
  628.5 299.7 %reduce-scatter.14.cloned.1.call-start = ((), (), s32[]{:S(2)}) async-start(), calls=%async_computation.12 | async-start | bytes 5308416 | tf_op jit(solution)/shard_map/reduce_scatter | solution.py:231
  635.4 353.4 %reduce-scatter.8.cloned.1.call-start = ((), (), s32[]{:S(2)}) async-start(), calls=%async_computation.7 | async-start | bytes 7864320 | tf_op jit(solution)/shard_map/reduce_scatter | solution.py:186
  641.9 514.3 %reduce-scatter.10.cloned.1.call-start = ((), (), s32[]{:S(2)}) async-start(), calls=%async_computation.10 | async-start | bytes 10616832 | tf_op jit(solution)/shard_map/reduce_scatter | solution.py:228
  655.2 6.5 copy-start.50
  655.2 6.6 copy-start.67
  655.2 106.0 %copy-start.48 = (f32[1536]{0:T(1024)S(1)}, f32[1536]{0:T(1024)}, u32[]{:S(2)}) copy-start(f32[1536]{0:T(1024)} %param.40) | copy-start | bytes 18436
  655.2 106.0 %copy-start.52 = (f32[1024]{0:T(1024)S(1)}, f32[1024]{0:T(1024)}, u32[]{:S(2)}) copy-start(f32[1024]{0:T(1024)} %copy-done.51) | copy-start | bytes 12292
  662.4 167.7 %copy-start.33 = (f32[192,256]{1,0:T(8,128)S(1)}, f32[192,256]{1,0:T(8,128)}, u32[]{:S(2)}) copy-start(f32[192,256]{1,0:T(8,128)} %param.28) | copy-start | bytes 589828
  662.4 167.7 %copy-start.38 = (f32[192,256]{1,0:T(8,128)S(1)}, f32[192,256]{1,0:T(8,128)}, u32[]{:S(2)}) copy-start(f32[192,256]{1,0:T(8,128)} %param.29) | copy-start | bytes 589828
  837.7 318.5 %copy-start.18 = (f32[192,2,768]{2,1,0:T(2,128)S(1)}, f32[192,2,768]{2,1,0:T(2,128)}, u32[]{:S(2)}) copy-start(f32[192,2,768]{2,1,0:T(2,128)} %param.26) | copy-start | bytes 3538948
  837.7 318.5 %copy-start.31 = (f32[192,2,768]{2,1,0:T(2,128)S(1)}, f32[192,2,768]{2,1,0:T(2,128)}, u32[]{:S(2)}) copy-start(f32[192,2,768]{2,1,0:T(2,128)} %param.27) | copy-start | bytes 3538948
  (64 other events, 225.0 us)
Sparse Core Ops, SparseCore 0:
  10.8 97.1 all-gather.4
  110.2 50.8 all-gather.6
  162.6 27.0 all-gather.8
  579.5 60.6 reduce-scatter.15
  642.6 118.5 all-reduce.37
  764.9 65.1 reduce-scatter.11
  833.7 94.3 reduce-scatter.13
  930.7 58.1 reduce-scatter.7
  992.9 163.2 reduce-scatter.9
where the time goes:
time: 1180 us; the launch traced here: 1170 us
  waiting for transfers between devices  442 us (37%)
  local copies, waits for them, and re-layouts  210 us (18%)
  matrix products  195 us (17%)
  blocking collectives  146 us (12%)
  other arithmetic  136 us (12%)
  loops' own time  23.3 us (2%)
  between operations  15 us (1%)
    reduce_scatter x1, waiting for transfers between devices, body(): lax.psum_scatter(grad_inw, 'dp', scatter_dimension=0, tiled=True)  164 us
    psum x1, waiting for transfers between devices, body(): lax.psum(term + contract_last(grad_step_low, back_step) + contract_last(b...  98.8 us
    reduce_scatter x1, waiting for transfers between devices, body(): lax.psum_scatter(grad_outw, 'dp', scatter_dimension=1, tiled=True)  90.5 us
    dynamic_update_slice x20, local copies, waits for them, and re-layouts, ssd_scan(): lax.scan(jax.checkpoint(block), start, (split(x_act), split(steps), split...  83.1 us
    dot_general x12, matrix products, block(): jnp.einsum('shtu,suhp->sthp', weights, x_block, precision=highest)  64.2 us
    reduce_scatter x1, waiting for transfers between devices, body(): lax.psum_scatter(partial_out, 'mp', scatter_dimension=1, tiled=True)  58.1 us
    psum x1, blocking collectives, body(): lax.psum((grad_norm_gain, grad_conv_all, grad_bc_table, grad_head), 'dp')  39.6 us
    all_gather x1, blocking collectives, body(): lax.all_gather(packed[1], 'dp', axis=0, tiled=True)  34.1 us
  transfers between devices with their start and end apart: 9, of which 6 were waited for; matrix products, arithmetic and copies ran while one was open for 18% of the time, Pallas kernels for 0%

commit v1 on v0

v1 whole, which is shorter than its diff:
```python
import functools

import jax
import jax.numpy as jnp
from jax import lax
from jax.experimental import pallas as pl
from jax.experimental.pallas import tpu as pltpu
from jax.sharding import PartitionSpec as P

CHUNK = 128
EPSILON = 1e-05
LEARN_RATE = 0.0001
DECAY_RATE = 0.1
WIDTH = 64
LANES = 128
HALO = 8
bf16 = jnp.bfloat16
f32 = jnp.float32
VMEM_LIMIT = 56 * 1024 * 1024


def dot_nn(a, b):
    return lax.dot_general(a, b, (((1,), (0,)), ((), ())), preferred_element_type=f32)


def dot_nt(a, b):
    return lax.dot_general(a, b, (((1,), (1,)), ((), ())), preferred_element_type=f32)


def dot_tn(a, b):
    return lax.dot_general(a, b, (((0,), (0,)), ((), ())), preferred_element_type=f32)


def split3(v):
    high = v.astype(bf16)
    rest = v - high.astype(f32)
    mid = rest.astype(bf16)
    low = (rest - mid.astype(f32)).astype(bf16)
    return high, mid, low


def exact_left(ones, v):
    high, mid, low = split3(v)
    return dot_nn(ones, high) + dot_nn(ones, mid) + dot_nn(ones, low)


def spread(v, expand):
    high, mid, low = split3(v)
    return dot_nn(high, expand) + dot_nn(mid, expand) + dot_nn(low, expand)


def gather_heads(v, expand):
    high = v.astype(bf16)
    mid = (v - high.astype(f32)).astype(bf16)
    return dot_nt(high, expand) + dot_nt(mid, expand)


def sigmoid(v):
    return 1.0 / (1.0 + jnp.exp(-v))


def conv_block(scratch, before, now, taps, keep):
    rows = now.shape[0]
    scratch[0:HALO, :] = before
    scratch[HALO:HALO + rows, :] = now
    total = taps[4:5, :] + taps[0:1, :] * now
    for lag in (1, 2, 3):
        moved = scratch[HALO - lag:HALO - lag + rows, :]
        total = total + taps[lag:lag + 1, :] * (moved * keep[:, lag - 1:lag])
    return total


def step_parts(step_pre, heads):
    raw = step_pre + heads[0:1, :]
    steps = jnp.maximum(raw, 0.0) + jnp.log1p(jnp.exp(-jnp.abs(raw)))
    rates = -jnp.exp(heads[1:2, :])
    return raw, steps, rates


def triangle(lower):
    row = lax.broadcasted_iota(jnp.int32, (CHUNK, CHUNK), 0)
    col = lax.broadcasted_iota(jnp.int32, (CHUNK, CHUNK), 1)
    return row >= col if lower else row <= col


def ssd_forward_kernel(
    x_ref, xb_ref, bc_ref, bcb_ref, st_ref, aux_ref, seg_ref, conv_ref, bct_ref, heads_ref, expand_ref,
    mixed_ref, state_ref, state, xs_scr, bc_scr,
):
    chunk = pl.program_id(0)

    @pl.when(chunk == 0)
    def _():
        state[...] = jnp.zeros_like(state)

    channels = x_ref.shape[1]
    aux = aux_ref[...]
    expand = expand_ref[...]
    u = conv_block(xs_scr, xb_ref[...], x_ref[...], conv_ref, aux)
    x_act = u * sigmoid(u)
    ubc = conv_block(bc_scr, bcb_ref[...], bc_ref[...], bct_ref, aux)
    bc_act = (ubc * sigmoid(ubc)).astype(bf16)
    b_mat, c_mat = bc_act[:, :LANES], bc_act[:, LANES:]
    _, steps, rates = step_parts(st_ref[...], heads_ref)
    lower = triangle(True)
    cum = exact_left(lower.astype(bf16), steps * rates)
    cum_t = cum.T
    tail = cum[CHUNK - 1:CHUNK, :]
    entry = jnp.exp(cum) * aux[:, 6:7]
    to_end = jnp.exp(tail - cum) * aux[:, 7:8]
    wide = spread(jnp.concatenate([steps, entry, to_end], axis=0), expand)
    step_e, entry_e, to_end_e = wide[:CHUNK], wide[CHUNK:2 * CHUNK], wide[2 * CHUNK:]
    skip_e = spread(jnp.broadcast_to(heads_ref[2:3, :], (8, LANES)), expand)[0:1, :]
    mask = lower & (aux[:, 8:9] == seg_ref[...])
    scores = jnp.where(mask, dot_nt(c_mat, b_mat), 0.0)
    xs = x_act * step_e
    xs_low = xs.astype(bf16)
    held = state[...]
    held_low = held.astype(bf16)
    state_ref[...] = held_low
    out = dot_nn(c_mat, held_low) * entry_e + skip_e * x_act
    state[...] = held * entry_e[CHUNK - 1:CHUNK, :] + dot_tn(b_mat, (xs * to_end_e).astype(bf16))
    first = lax.broadcasted_iota(jnp.int32, (CHUNK, LANES), 1) < WIDTH
    zero = jnp.zeros((CHUNK, LANES), bf16)
    for pair in range(channels // LANES):
        span = slice(pair * LANES, (pair + 1) * LANES)
        parts = []
        for head in (2 * pair, 2 * pair + 1):
            diff = cum[:, head:head + 1] - cum_t[head:head + 1, :]
            parts.append((scores * jnp.exp(jnp.minimum(diff, 0.0))).astype(bf16))
        own = xs_low[:, span]
        both = jnp.concatenate([jnp.where(first, own, zero), jnp.where(first, zero, own)], axis=0)
        mixed_ref[:, span] = out[:, span] + dot_nn(jnp.concatenate(parts, axis=1), both)


def ssd_backward_kernel(
    x_ref, xb_ref, bc_ref, bcb_ref, st_ref, aux_ref, seg_ref, conv_ref, bct_ref, heads_ref, expand_ref,
    mixed_ref, dy_ref, state_ref,
    dx_ref, dbc_ref, dst_ref, dconv_ref, dbct_ref, dheads_ref,
    dstate, xs_scr, bc_scr, du_scr, dubc_scr,
):
    at = pl.program_id(0)

    @pl.when(at == 0)
    def _():
        dstate[...] = jnp.zeros_like(dstate)
        du_scr[...] = jnp.zeros_like(du_scr)
        dubc_scr[...] = jnp.zeros_like(dubc_scr)
        dconv_ref[...] = jnp.zeros_like(dconv_ref)
        dbct_ref[...] = jnp.zeros_like(dbct_ref)
        dheads_ref[...] = jnp.zeros_like(dheads_ref)

    channels = x_ref.shape[1]
    aux = aux_ref[...]
    expand = expand_ref[...]
    x_now, bc_now = x_ref[...], bc_ref[...]
    u = conv_block(xs_scr, xb_ref[...], x_now, conv_ref, aux)
    sg = sigmoid(u)
    x_act = u * sg
    ubc = conv_block(bc_scr, bcb_ref[...], bc_now, bct_ref, aux)
    sgbc = sigmoid(ubc)
    bc_act = (ubc * sgbc).astype(bf16)
    b_mat, c_mat = bc_act[:, :LANES], bc_act[:, LANES:]
    raw, steps, rates = step_parts(st_ref[...], heads_ref)
    lower = triangle(True)
    cum = exact_left(lower.astype(bf16), steps * rates)
    cum_t = cum.T
    tail = cum[CHUNK - 1:CHUNK, :]
    entry = jnp.exp(cum) * aux[:, 6:7]
    to_end = jnp.exp(tail - cum) * aux[:, 7:8]
    wide = spread(jnp.concatenate([steps, entry, to_end], axis=0), expand)
    step_e, entry_e, to_end_e = wide[:CHUNK], wide[CHUNK:2 * CHUNK], wide[2 * CHUNK:]
    skip_e = spread(jnp.broadcast_to(heads_ref[2:3, :], (8, LANES)), expand)[0:1, :]
    upper = triangle(False)
    mask = upper & (aux[:, 8:9] == seg_ref[...])
    scores = jnp.where(mask, dot_nt(b_mat, c_mat), 0.0)
    xs = x_act * step_e
    xs_low = xs.astype(bf16)
    dy_low = dy_ref[...]
    dy = dy_low.astype(f32)
    held_low = state_ref[...]
    grad = dstate[...]
    grad_low = grad.astype(bf16)
    entry_dy = (entry_e * dy).astype(bf16)
    kept_e = entry_e[CHUNK - 1:CHUNK, :]
    dstate[...] = grad * kept_e + dot_tn(c_mat, entry_dy)
    dc = dot_nt(entry_dy, held_low)
    db = dot_nt((xs * to_end_e).astype(bf16), grad_low)
    q_state = dot_nn(b_mat, grad_low) * to_end_e
    first = lax.broadcasted_iota(jnp.int32, (CHUNK, LANES), 1) < WIDTH
    zero = jnp.zeros((CHUNK, LANES), bf16)
    dscores = jnp.zeros((CHUNK, CHUNK), f32)
    q_parts = []
    for pair in range(channels // LANES):
        span = slice(pair * LANES, (pair + 1) * LANES)
        own = dy_low[:, span]
        both = jnp.concatenate([jnp.where(first, own, zero), jnp.where(first, zero, own)], axis=0)
        dweights = dot_nt(xs_low[:, span], both)
        parts = []
        for i, head in enumerate((2 * pair, 2 * pair + 1)):
            diff = cum_t[head:head + 1, :] - cum[:, head:head + 1]
            decay = jnp.exp(jnp.minimum(diff, 0.0))
            parts.append((scores * decay).astype(bf16))
            dscores = dscores + dweights[:, i * LANES:(i + 1) * LANES] * decay
        q_parts.append(dot_nn(jnp.concatenate(parts, axis=1), both))
    q = jnp.concatenate(q_parts, axis=1) + q_state
    dscores_low = jnp.where(mask, dscores, 0.0).astype(bf16)
    db = db + dot_nn(dscores_low, c_mat)
    dc = dc + dot_tn(dscores_low, b_mat)
    xs_round = xs_low.astype(f32)
    rows = gather_heads(
        jnp.concatenate(
            [
                dy * (mixed_ref[...] - skip_e * x_act) - xs_round * q,
                x_act * q,
            ],
            axis=0,
        ),
        expand,
    )
    flow, dstep = rows[:CHUNK], rows[CHUNK:]
    sums = jnp.concatenate(
        [
            jnp.sum(xs_round * q_state + kept_e * (held_low.astype(f32) * grad), axis=0, keepdims=True),
            jnp.sum(dy * x_act, axis=0, keepdims=True),
            jnp.zeros((6, channels), f32),
        ],
        axis=0,
    )
    sums = gather_heads(sums, expand)
    dlog = exact_left(upper.astype(bf16), flow) + sums[0:1, :]
    dstep = dstep + rates * dlog
    draw = dstep * sigmoid(raw)
    dst_ref[...] = draw
    dheads_ref[0:1, :] += jnp.sum(draw, axis=0, keepdims=True)
    dheads_ref[1:2, :] += rates * jnp.sum(dlog * steps, axis=0, keepdims=True)
    dheads_ref[2:3, :] += sums[1:2, :]

    def conv_back(scratch, du, now, taps, dtaps):
        scratch[0:CHUNK, :] = du
        total = taps[0:1, :] * du
        dtaps[0:1, :] += jnp.sum(now * du, axis=0, keepdims=True)
        dtaps[4:5, :] += jnp.sum(du, axis=0, keepdims=True)
        for lag in (1, 2, 3):
            moved = scratch[lag:lag + CHUNK, :] * aux[:, 2 + lag:3 + lag]
            total = total + taps[lag:lag + 1, :] * moved
            dtaps[lag:lag + 1, :] += jnp.sum(now * moved, axis=0, keepdims=True)
        scratch[CHUNK:CHUNK + HALO, :] = du[0:HALO, :]
        return total

    du = (skip_e * dy + step_e * q) * (sg * (1.0 + u * (1.0 - sg)))
    dx_ref[...] = conv_back(du_scr, du, x_now, conv_ref, dconv_ref).astype(dx_ref.dtype)
    dubc = jnp.concatenate([db, dc], axis=1) * (sgbc * (1.0 + ubc * (1.0 - sgbc)))
    dbc_ref[...] = conv_back(dubc_scr, dubc, bc_now, bct_ref, dbct_ref)


def common_specs(place, channels):
    before = lambda i: (jnp.maximum(place(i) * (CHUNK // HALO) - 1, 0), 0)
    now = lambda i: (place(i), 0)
    whole = lambda i: (0, 0)
    return [
        pl.BlockSpec((CHUNK, channels), now),
        pl.BlockSpec((HALO, channels), before),
        pl.BlockSpec((CHUNK, 2 * LANES), now),
        pl.BlockSpec((HALO, 2 * LANES), before),
        pl.BlockSpec((CHUNK, LANES), now),
        pl.BlockSpec((CHUNK, 16), now),
        pl.BlockSpec((1, CHUNK), lambda i: (0, place(i))),
        pl.BlockSpec((8, channels), whole),
        pl.BlockSpec((8, 2 * LANES), whole),
        pl.BlockSpec((8, LANES), whole),
        pl.BlockSpec((LANES, channels), whole),
    ]


def ssd_forward(x_pre, bc_pre, step_pre, aux, seg_row, conv_rows, bc_rows, head_rows, expand):
    tokens, channels = x_pre.shape
    count = tokens // CHUNK
    now = lambda i: (i, 0)
    return pl.pallas_call(
        ssd_forward_kernel,
        grid=(count,),
        in_specs=common_specs(lambda i: i, channels),
        out_specs=[
            pl.BlockSpec((CHUNK, channels), now),
            pl.BlockSpec((None, LANES, channels), lambda i: (i, 0, 0)),
        ],
        out_shape=[
            jax.ShapeDtypeStruct((tokens, channels), f32),
            jax.ShapeDtypeStruct((count, LANES, channels), bf16),
        ],
        scratch_shapes=[
            pltpu.VMEM((LANES, channels), f32),
            pltpu.VMEM((HALO + CHUNK, channels), f32),
            pltpu.VMEM((HALO + CHUNK, 2 * LANES), f32),
        ],
        compiler_params=pltpu.CompilerParams(vmem_limit_bytes=VMEM_LIMIT),
        name="ssd_forward",
    )(x_pre, x_pre, bc_pre, bc_pre, step_pre, aux, seg_row, conv_rows, bc_rows, head_rows, expand)


def ssd_backward(x_pre, bc_pre, step_pre, aux, seg_row, conv_rows, bc_rows, head_rows, expand, mixed, dy, states):
    tokens, channels = x_pre.shape
    count = tokens // CHUNK
    place = lambda i: count - 1 - i
    now = lambda i: (place(i), 0)
    whole = lambda i: (0, 0)
    return pl.pallas_call(
        ssd_backward_kernel,
        grid=(count,),
        in_specs=common_specs(place, channels) + [
            pl.BlockSpec((CHUNK, channels), now),
            pl.BlockSpec((CHUNK, channels), now),
            pl.BlockSpec((None, LANES, channels), lambda i: (place(i), 0, 0)),
        ],
        out_specs=[
            pl.BlockSpec((CHUNK, channels), now),
            pl.BlockSpec((CHUNK, 2 * LANES), now),
            pl.BlockSpec((CHUNK, LANES), now),
            pl.BlockSpec((8, channels), whole),
            pl.BlockSpec((8, 2 * LANES), whole),
            pl.BlockSpec((8, LANES), whole),
        ],
        out_shape=[
            jax.ShapeDtypeStruct((tokens, channels), bf16),
            jax.ShapeDtypeStruct((tokens, 2 * LANES), f32),
            jax.ShapeDtypeStruct((tokens, LANES), f32),
            jax.ShapeDtypeStruct((8, channels), f32),
            jax.ShapeDtypeStruct((8, 2 * LANES), f32),
            jax.ShapeDtypeStruct((8, LANES), f32),
        ],
        scratch_shapes=[
            pltpu.VMEM((LANES, channels), f32),
            pltpu.VMEM((HALO + CHUNK, channels), f32),
            pltpu.VMEM((HALO + CHUNK, 2 * LANES), f32),
            pltpu.VMEM((HALO + CHUNK, channels), f32),
            pltpu.VMEM((HALO + CHUNK, 2 * LANES), f32),
        ],
        compiler_params=pltpu.CompilerParams(vmem_limit_bytes=VMEM_LIMIT),
        name="ssd_backward",
    )(x_pre, x_pre, bc_pre, bc_pre, step_pre, aux, seg_row, conv_rows, bc_rows, head_rows, expand, mixed, dy, states)


def segment_facts(seg):
    row = seg[0]
    tokens = row.shape[0]
    cols = []
    for lag in (1, 2, 3):
        cols.append(jnp.pad(row[:-lag], (lag, 0), constant_values=-1) == row)
    for lag in (1, 2, 3):
        cols.append(jnp.pad(row[lag:], (0, lag), constant_values=-1) == row)
    blocks = row.reshape(tokens // CHUNK, CHUNK)
    ends = blocks[:, -1:]
    before = jnp.concatenate([jnp.full((1, 1), -1, row.dtype), ends[:-1]], axis=0)
    cols.append((blocks == before).reshape(-1))
    cols.append((blocks == ends).reshape(-1))
    cols.append(row)
    facts = jnp.stack([c.astype(f32) for c in cols], axis=1)
    return jnp.pad(facts, ((0, 0), (0, 16 - facts.shape[1]))), seg.astype(f32)


def pad_rows(table, rows=8):
    return jnp.pad(table, ((0, rows - table.shape[0]), (0, 0)))


def pad_lanes(table, lanes=LANES):
    return jnp.pad(table, ((0, 0), (0, lanes - table.shape[1])))


def head_expand(channels):
    head = jnp.arange(LANES)[:, None]
    return (head == (jnp.arange(channels) // WIDTH)[None, :]).astype(bf16)


def place_kernel(idx_ref, lhs_ref, *refs, widths, count):
    groups = len(widths)
    pieces = refs[: groups * count]
    outs = refs[groups * count: groups * count + groups]
    weights = refs[groups * count + groups:]

    @pl.when(pl.program_id(0) == 0)
    def _():
        for g in range(groups):
            for s in range(count):
                piece = pieces[g * count + s]
                rows = piece.shape[0]
                weights[g][pl.ds(pl.multiple_of(idx_ref[s] * rows, rows), rows), :] = piece[...]

    lhs = lhs_ref[...]
    for g in range(groups):
        outs[g][...] = dot_nn(lhs, weights[g][...])


TILE = 256


def project(lhs, groups, idx):
    tokens, depth = lhs.shape
    count = len(groups[0])
    widths = tuple(g[0].shape[1] for g in groups)
    whole = lambda i: (0, 0)
    flat = [p for g in groups for p in g]
    return pl.pallas_call(
        functools.partial(place_kernel, widths=widths, count=count),
        grid=(tokens // TILE,),
        in_specs=[pl.BlockSpec(memory_space=pltpu.SMEM), pl.BlockSpec((TILE, depth), lambda i: (i, 0))]
        + [pl.BlockSpec(p.shape, whole) for p in flat],
        out_specs=[pl.BlockSpec((TILE, w), lambda i: (i, 0)) for w in widths]
        + [pl.BlockSpec((depth, w), whole) for w in widths],
        out_shape=[jax.ShapeDtypeStruct((tokens, w), f32) for w in widths]
        + [jax.ShapeDtypeStruct((depth, w), bf16) for w in widths],
        compiler_params=pltpu.CompilerParams(vmem_limit_bytes=VMEM_LIMIT),
        cost_estimate=pl.CostEstimate(
            flops=2 * tokens * depth * sum(widths), bytes_accessed=6 * depth * sum(widths), transcendentals=0
        ),
        name="project",
    )(idx, lhs, *flat)


def column_to_row(col):
    return jnp.broadcast_to(col, (col.shape[0], LANES)).T[0:1, :]


def row_to_column(row):
    return jnp.broadcast_to(row, (LANES, row.shape[1])).T[:, 0:1]


def gate_kernel(idx_ref, lhs_ref, cot_ref, mixed_ref, conv_ref, *refs, count):
    gate_pieces, out_pieces = refs[:count], refs[count: 2 * count]
    gate_ref, gout_ref, sums_ref, wg_ref, wo_ref = refs[2 * count:]

    @pl.when(pl.program_id(0) == 0)
    def _():
        for dest, source in ((wg_ref, gate_pieces), (wo_ref, out_pieces)):
            for s in range(count):
                rows = source[s].shape[0]
                dest[pl.ds(pl.multiple_of(idx_ref[s] * rows, rows), rows), :] = source[s][...]

    gate = dot_nn(lhs_ref[...], wg_ref[...])
    gout = dot_nn(cot_ref[...], wo_ref[...])
    gate_ref[...] = gate
    gout_ref[...] = gout
    gated = mixed_ref[...] * (gate * sigmoid(gate))
    square = jnp.sum(gated * gated, axis=1, keepdims=True)
    inner = jnp.sum(gout * conv_ref[5:6, :] * gated, axis=1, keepdims=True)
    sums_ref[...] = jnp.concatenate(
        [column_to_row(square), column_to_row(inner), jnp.zeros((6, square.shape[0]), f32)], axis=0
    )


def gate_forward(lhs, cot, mixed, conv_rows, gate_pieces, out_pieces, idx):
    tokens, depth = lhs.shape
    channels = mixed.shape[1]
    count = len(gate_pieces)
    whole = lambda i: (0, 0)
    now = lambda i: (i, 0)
    return pl.pallas_call(
        functools.partial(gate_kernel, count=count),
        grid=(tokens // TILE,),
        in_specs=[
            pl.BlockSpec(memory_space=pltpu.SMEM),
            pl.BlockSpec((TILE, depth), now),
            pl.BlockSpec((TILE, depth), now),
            pl.BlockSpec((TILE, channels), now),
            pl.BlockSpec((8, channels), whole),
        ]
        + [pl.BlockSpec(p.shape, whole) for p in (*gate_pieces, *out_pieces)],
        out_specs=[
            pl.BlockSpec((TILE, channels), now),
            pl.BlockSpec((TILE, channels), now),
            pl.BlockSpec((8, TILE), lambda i: (0, i)),
            pl.BlockSpec((depth, channels), whole),
            pl.BlockSpec((depth, channels), whole),
        ],
        out_shape=[
            jax.ShapeDtypeStruct((tokens, channels), f32),
            jax.ShapeDtypeStruct((tokens, channels), f32),
            jax.ShapeDtypeStruct((8, tokens), f32),
            jax.ShapeDtypeStruct((depth, channels), bf16),
            jax.ShapeDtypeStruct((depth, channels), bf16),
        ],
        compiler_params=pltpu.CompilerParams(vmem_limit_bytes=VMEM_LIMIT),
        cost_estimate=pl.CostEstimate(
            flops=4 * tokens * depth * channels, bytes_accessed=8 * depth * channels, transcendentals=0
        ),
        name="gate_forward",
    )(idx, lhs, cot, mixed, conv_rows, *gate_pieces, *out_pieces)


def gate_back_kernel(gate_ref, gout_ref, mixed_ref, sums_ref, conv_ref, gated_out_ref, dmixed_ref, dgate_ref, dgain_ref, *, inner_total):
    gate, gout, mixed = gate_ref[...], gout_ref[...], mixed_ref[...]
    gain = conv_ref[5:6, :]
    square, inner = row_to_column(sums_ref[0:1, :]), row_to_column(sums_ref[1:2, :])
    scale = lax.rsqrt(square / inner_total + EPSILON)
    sg = sigmoid(gate)
    act = gate * sg
    gated = mixed * act
    normal = gated * scale
    gated_out_ref[...] = (normal * gain).astype(bf16)
    dgated = scale * (gain * gout) - gated * (scale * scale * scale * inner / inner_total)
    dmixed_ref[...] = (dgated * act).astype(bf16)
    dgate_ref[...] = (dgated * mixed * sg * (1.0 + gate * (1.0 - sg))).astype(bf16)

    @pl.when(pl.program_id(0) == 0)
    def _():
        dgain_ref[...] = jnp.zeros_like(dgain_ref)

    dgain_ref[0:1, :] += jnp.sum(gout * normal, axis=0, keepdims=True)


def gate_backward(gate, gout, mixed, sums, conv_rows, inner_total):
    tokens, channels = gate.shape
    whole = lambda i: (0, 0)
    now = lambda i: (i, 0)
    block = pl.BlockSpec((TILE, channels), now)
    return pl.pallas_call(
        functools.partial(gate_back_kernel, inner_total=inner_total),
        grid=(tokens // TILE,),
        in_specs=[block, block, block, pl.BlockSpec((8, TILE), lambda i: (0, i)), pl.BlockSpec((8, channels), whole)],
        out_specs=[block, block, block, pl.BlockSpec((8, channels), whole)],
        out_shape=[
            jax.ShapeDtypeStruct((tokens, channels), bf16),
            jax.ShapeDtypeStruct((tokens, channels), bf16),
            jax.ShapeDtypeStruct((tokens, channels), bf16),
            jax.ShapeDtypeStruct((8, channels), f32),
        ],
        compiler_params=pltpu.CompilerParams(vmem_limit_bytes=VMEM_LIMIT),
        name="gate_backward",
    )(gate, gout, mixed, sums, conv_rows)


def weight_grad_kernel(slot_ref, lhs_ref, rhs_ref, out_ref, *, rows):
    per = TILE_D // rows
    product = dot_tn(lhs_ref[...], rhs_ref[...])
    for p in range(per):
        block = pl.program_id(0) * per + p
        out_ref[slot_ref[block]] = product[p * rows:(p + 1) * rows, :].astype(out_ref.dtype)


TILE_D = 384


def weight_grad(lhs, rhs, slots):
    tokens, depth = lhs.shape
    width = rhs.shape[1]
    count = slots.shape[0]
    rows = depth // count
    return pl.pallas_call(
        functools.partial(weight_grad_kernel, rows=rows),
        grid=(depth // TILE_D,),
        in_specs=[
            pl.BlockSpec(memory_space=pltpu.SMEM),
            pl.BlockSpec((tokens, TILE_D), lambda i: (0, i)),
            pl.BlockSpec((tokens, width), lambda i: (0, 0)),
        ],
        out_specs=pl.BlockSpec((count, rows, width), lambda i: (0, 0, 0)),
        out_shape=jax.ShapeDtypeStruct((count, rows, width), bf16),
        compiler_params=pltpu.CompilerParams(vmem_limit_bytes=VMEM_LIMIT),
        cost_estimate=pl.CostEstimate(flops=2 * tokens * depth * width, bytes_accessed=4 * depth * width, transcendentals=0),
        name="weight_grad",
    )(slots, lhs, rhs)


def out_kernel(rank_ref, lhs_ref, w_ref, *outs):
    lhs = lhs_ref[...]
    width = outs[0].shape[1]
    for r, out in enumerate(outs):
        start = pl.multiple_of((rank_ref[0] ^ r) * width, width)
        out[...] = dot_nt(lhs, w_ref[pl.ds(start, width), :]).astype(out.dtype)


def out_partial(gated_out, w_out, rank, ranks):
    tokens, channels = gated_out.shape
    depth = w_out.shape[0]
    width = depth // ranks
    now = lambda i: (i, 0)
    return pl.pallas_call(
        out_kernel,
        grid=(tokens // TILE,),
        in_specs=[
            pl.BlockSpec(memory_space=pltpu.SMEM),
            pl.BlockSpec((TILE, channels), now),
            pl.BlockSpec((depth, channels), lambda i: (0, 0)),
        ],
        out_specs=[pl.BlockSpec((TILE, width), now)] * ranks,
        out_shape=[jax.ShapeDtypeStruct((tokens, width), bf16)] * ranks,
        compiler_params=pltpu.CompilerParams(vmem_limit_bytes=VMEM_LIMIT),
        cost_estimate=pl.CostEstimate(flops=2 * tokens * depth * channels, bytes_accessed=4 * depth * channels, transcendentals=0),
        name="out_partial",
    )(rank, gated_out, w_out)


def term_kernel(rank_ref, gx_ref, wx_ref, gg_ref, wg_ref, gs_ref, ws_ref, gb_ref, wb_ref, out_ref):
    total = dot_nt(gx_ref[...], wx_ref[...]) + dot_nt(gg_ref[...], wg_ref[...])
    total = total + dot_nt(gs_ref[...], ws_ref[...]) + dot_nt(gb_ref[...], wb_ref[...])
    out_ref[...] = total.astype(out_ref.dtype)


def normed_term(pairs, rank, ranks):
    tokens = pairs[0][0].shape[0]
    depth = pairs[0][1].shape[0]
    rows = tokens // ranks
    specs, flat = [], []
    for g, w in pairs:
        specs.append(pl.BlockSpec((rows, g.shape[1]), lambda i, rank_ref: (i ^ rank_ref[0], 0)))
        specs.append(pl.BlockSpec(w.shape, lambda i, rank_ref: (0, 0)))
        flat += [g, w]
    return pl.pallas_call(
        term_kernel,
        grid_spec=pltpu.PrefetchScalarGridSpec(
            num_scalar_prefetch=1,
            grid=(ranks,),
            in_specs=specs,
            out_specs=pl.BlockSpec((None, rows, depth), lambda i, rank_ref: (i, 0, 0)),
        ),
        out_shape=jax.ShapeDtypeStruct((ranks, rows, depth), bf16),
        compiler_params=pltpu.CompilerParams(vmem_limit_bytes=VMEM_LIMIT),
        cost_estimate=pl.CostEstimate(flops=4 * tokens * depth * 800, bytes_accessed=8 * depth * 768, transcendentals=0),
        name="normed_term",
    )(rank, *flat)


def norm_back_kernel(rank_ref, a_ref, b_ref, hidden_ref, cot_ref, gain_ref, out_ref, dgain_ref):
    grad = a_ref[...].astype(f32) + b_ref[...].astype(f32)
    inputs = hidden_ref[...].astype(f32)
    inv_rms = lax.rsqrt(jnp.mean(inputs * inputs, axis=1, keepdims=True) + EPSILON)
    normed = inputs * inv_rms
    scaled = grad * gain_ref[0:1, :]
    mean = jnp.mean(scaled * normed, axis=1, keepdims=True)
    out_ref[...] = (inv_rms * (scaled - normed * mean) + cot_ref[...].astype(f32)).astype(out_ref.dtype)
    dgain_ref[...] = jnp.broadcast_to(jnp.sum(grad * normed, axis=0, keepdims=True), dgain_ref.shape)


def norm_backward(a, b, hidden, cot, gain_rows, rank):
    rows, depth = a.shape
    mine = lambda i, rank_ref: (rank_ref[0], 0)
    whole = lambda i, rank_ref: (0, 0)
    return pl.pallas_call(
        norm_back_kernel,
        grid_spec=pltpu.PrefetchScalarGridSpec(
            num_scalar_prefetch=1,
            grid=(1,),
            in_specs=[
                pl.BlockSpec((rows, depth), whole),
                pl.BlockSpec((rows, depth), whole),
                pl.BlockSpec((rows, depth), mine),
                pl.BlockSpec((rows, depth), mine),
                pl.BlockSpec((8, depth), whole),
            ],
            out_specs=[pl.BlockSpec((rows, depth), whole), pl.BlockSpec((8, depth), whole)],
        ),
        out_shape=[jax.ShapeDtypeStruct((rows, depth), bf16), jax.ShapeDtypeStruct((8, depth), f32)],
        compiler_params=pltpu.CompilerParams(vmem_limit_bytes=VMEM_LIMIT),
        name="norm_backward",
    )(rank, a, b, hidden, cot, gain_rows)


def outer_from(v, k):
    size = lax.axis_size("dp")
    n = size // 2
    return lax.ppermute(v, "dp", [(((o + k) % n) * 2 + x, o * 2 + x) for o in range(n) for x in range(2)])


def outer_flip(v, bit):
    n = lax.axis_size("dp") // 2
    return lax.ppermute(v, "dp", [((o ^ bit) * 2 + x, o * 2 + x) for o in range(n) for x in range(2)])


def inner_flip(v):
    return lax.ppermute(v, "dp", [(d ^ 1, d) for d in range(lax.axis_size("dp"))])


def rank_flip(v, bit):
    return lax.ppermute(v, "mp", [(m ^ bit, m) for m in range(lax.axis_size("mp"))])


def dp_pieces(piece):
    n = lax.axis_size("dp") // 2
    found = []
    for k in range(n):
        here = piece if k == 0 else outer_from(piece, k)
        found += [here, inner_flip(here)]
    return found


def dp_scatter(blocks):
    n = lax.axis_size("dp") // 2
    total = None
    for k in list(range(1, n)) + [0]:
        here = blocks[2 * k].astype(f32) + inner_flip(blocks[2 * k + 1]).astype(f32)
        if k > 0:
            here = outer_from(here.astype(bf16), -k).astype(f32)
        total = here if total is None else total + here
    return total


def dp_sum(v):
    v = v + inner_flip(v)
    bit = 1
    while bit < lax.axis_size("dp") // 2:
        v = v + outer_flip(v, bit)
        bit *= 2
    return v


def mp_sum(v):
    v = v + rank_flip(v, 1)
    return v + rank_flip(v, 2)


def mp_reduce(blocks):
    near = blocks[0].astype(f32) + rank_flip(blocks[1], 1).astype(f32)
    far = blocks[2].astype(f32) + rank_flip(blocks[3], 1).astype(f32)
    return near, rank_flip(far.astype(bf16), 2)


def mp_pieces(v):
    far = rank_flip(v, 2)
    return [v, rank_flip(v, 1), far, rank_flip(far, 1)]


def in_rank_order(pieces, rank, axis):
    width = pieces[0].shape[axis]
    shape = list(pieces[0].shape)
    shape[axis] = width * len(pieces)
    full = jnp.zeros(shape, pieces[0].dtype)
    for r, piece in enumerate(pieces):
        full = lax.dynamic_update_slice_in_dim(full, piece, (rank ^ r) * width, axis)
    return full


def momentum(moment, grad):
    return 0.5 * moment + 0.5 * grad


def advance(weight, moment, grad):
    fresh = momentum(moment, grad)
    return (fresh, weight - LEARN_RATE * fresh - LEARN_RATE * DECAY_RATE * weight)


def body(
    hidden, segments, cotangent, in_weight, in_moment, bc_weight, bc_moment, step_weight, step_moment,
    out_weight, out_moment, conv_table, conv_moment, bc_table, bc_table_moment, head_table, head_moment,
    norm_gain, gain_moment,
):
    size = lax.axis_size("dp")
    ranks = lax.axis_size("mp")
    n = size // 2
    place, rank = lax.axis_index("dp"), lax.axis_index("mp")
    outer, inner = place // 2, place % 2
    slot = jnp.arange(size)
    idx = (((outer + slot // 2) % n) * 2 + (inner ^ (slot % 2))).astype(jnp.int32)
    slots = ((((slot // 2) - outer) % n) * 2 + (inner ^ (slot % 2))).astype(jnp.int32)
    rank1 = rank.reshape(1).astype(jnp.int32)
    channels = in_weight.shape[2]
    heads = head_table.shape[1]
    tokens, depth = hidden.shape

    x_pieces = dp_pieces(in_weight[:, 1].astype(bf16))
    bc_pieces = dp_pieces(bc_weight.astype(bf16))
    gate_pieces = dp_pieces(in_weight[:, 0].astype(bf16))
    out_pieces = dp_pieces(out_weight.T.astype(bf16))
    w_step = lax.all_gather(step_weight.astype(bf16), "dp", axis=0, tiled=True)
    w_step = pad_lanes(w_step)
    cot = in_rank_order(mp_pieces(cotangent), rank, 1)

    inputs = hidden.astype(f32)
    inv_rms = lax.rsqrt(jnp.mean(inputs * inputs, axis=-1, keepdims=True) + EPSILON)
    normed_low = (inputs * inv_rms * norm_gain).astype(bf16)
    aux, seg_row = segment_facts(segments)
    conv_rows, bc_rows = pad_rows(conv_table), pad_rows(bc_table)
    head_rows = pad_lanes(pad_rows(head_table))
    expand = head_expand(channels)

    x_pre, bc_pre, w_x, w_bc = project(normed_low, [x_pieces, bc_pieces], idx)
    step_pre = dot_nn(normed_low, w_step)
    facts = (aux, seg_row, conv_rows, bc_rows, head_rows, expand)
    mixed, states = ssd_forward(x_pre, bc_pre, step_pre, *facts)
    gate_pre, gout, sums, w_gate, w_out = gate_forward(
        normed_low, cot, mixed, conv_rows, gate_pieces, out_pieces, idx
    )
    sums = mp_sum(sums)
    gated_out, dmixed, dgate, dgain = gate_backward(gate_pre, gout, mixed, sums, conv_rows, channels * ranks)

    grad_out = weight_grad(cot, gated_out, slots)
    grad_gate = weight_grad(normed_low, dgate, slots)
    shard_out = dp_scatter(grad_out)
    shard_gate = dp_scatter(grad_gate)
    near, far = mp_reduce(out_partial(gated_out, w_out, rank1, ranks))
    width = depth // ranks
    resid = lax.dynamic_slice_in_dim(hidden, rank * width, width, 1).astype(f32)
    output = (resid + near + far.astype(f32)).astype(bf16)

    dx, dbc_part, dstep, dconv, dbct_part, dheads = ssd_backward(
        x_pre, bc_pre, step_pre, *facts, mixed, dmixed, states
    )
    grad_x = weight_grad(normed_low, dx, slots)
    shard_x = dp_scatter(grad_x)
    dstep_low = dstep.astype(bf16)
    grad_step = dot_tn(normed_low, dstep_low[:, :heads])
    shard_step = lax.psum_scatter(grad_step, "dp", scatter_dimension=0, tiled=True)

    share = dbc_part.shape[1] // ranks
    dbc_low_part = dbc_part.astype(bf16)
    parts = [lax.dynamic_slice_in_dim(dbc_low_part, (rank ^ r) * share, share, 1) for r in range(ranks)]
    near, far = mp_reduce(parts)
    dbc_low = (near + far.astype(f32)).astype(bf16)
    wb_share = lax.dynamic_slice_in_dim(w_bc, rank * share, share, 1)
    grad_bc = dot_tn(normed_low, dbc_low)
    shard_bc_mine = lax.psum_scatter(grad_bc, "dp", scatter_dimension=0, tiled=True)
    shard_bc = in_rank_order(mp_pieces(shard_bc_mine), rank, 1)

    term = normed_term([(dx, w_x), (dgate, w_gate), (dstep_low, w_step), (dbc_low, wb_share)], rank1, ranks)
    near, far = mp_reduce([term[r] for r in range(ranks)])
    mine, dgain_mine = norm_backward(near, far, hidden, cot, pad_rows(norm_gain[None]), rank1)
    input_grad = in_rank_order(mp_pieces(mine), rank, 0)

    dconv_all = jnp.concatenate([dconv[:5], dgain[:1]], axis=0)
    shared = mp_sum(jnp.concatenate([dbct_part[:5].reshape(-1, LANES), dgain_mine[:1].reshape(-1, LANES)], axis=0))
    packed = jnp.concatenate([shared, dconv_all.reshape(-1, LANES), dheads], axis=0)
    packed = dp_sum(packed)
    cut1 = 5 * 2
    cut2 = cut1 + depth // LANES
    cut3 = cut2 + 6 * channels // LANES
    total_bct = packed[:cut1].reshape(5, 2 * LANES)
    total_gain = packed[cut1:cut2].reshape(-1)
    total_conv = packed[cut2:cut3].reshape(6, channels)
    total_head = packed[cut3:cut3 + 3, :heads]

    in_m, in_w = advance(in_weight, in_moment, jnp.stack([shard_gate, shard_x], axis=1))
    bc_m, bc_w = advance(bc_weight, bc_moment, shard_bc)
    step_m, step_w = advance(step_weight, step_moment, shard_step)
    out_m, out_w = advance(out_weight, out_moment, shard_out.T)
    return (
        output, input_grad, in_m, in_w, bc_m, bc_w, step_m, step_w, out_m, out_w,
        momentum(conv_moment, total_conv),
        momentum(bc_table_moment, total_bct),
        momentum(head_moment, total_head),
        momentum(gain_moment, total_gain),
    )


def solution(mesh):
    placed = (
        P("dp", None),
        P("dp", None),
        P("dp", "mp"),
        P("dp", None, "mp"),
        P("dp", None, "mp"),
        P("dp", None),
        P("dp", None),
        P("dp", "mp"),
        P("dp", "mp"),
        P("mp", "dp"),
        P("mp", "dp"),
        P(None, "mp"),
        P(None, "mp"),
        P(),
        P(),
        P(None, "mp"),
        P(None, "mp"),
        P(),
        P(),
    )
    return jax.shard_map(
        body,
        mesh=mesh,
        in_specs=placed,
        out_specs=(
            P("dp", "mp"),
            P("dp", None),
            P("dp", None, "mp"),
            P("dp", None, "mp"),
            P("dp", None),
            P("dp", None),
            P("dp", "mp"),
            P("dp", "mp"),
            P("mp", "dp"),
            P("mp", "dp"),
            P(None, "mp"),
            P(),
            P(None, "mp"),
            P(),
        ),
        check_vma=False,
    )
```

time: 1180 us -> 547 us (0.46)
  waiting for transfers between devices: 442 us -> 197 us
  matrix products: 195 us -> 5.61 us
  local copies, waits for them, and re-layouts: 210 us -> 48.7 us
  blocking collectives: 146 us -> 32 us
  Pallas kernels: 0 us -> 113 us
  other arithmetic: 136 us -> 30.9 us
  starting transfers between devices: 0.54 us -> 101 us
  loops' own time: 23.3 us -> 0 us
    reduce_scatter x4 -> x1, waiting for transfers between devices: 332 us -> 0.02 us  [body(): lax.psum_scatter(grad_bc, 'dp', scatter_dimension=0, tiled=True)]
    dot_general x67 -> x1, matrix products: 191 us -> 1.77 us  [dot_nn(): lax.dot_general(a, b, (((1,), (0,)), ((), ())), preferred_element_type=f32)]
    ppermute x0 -> x74, waiting for transfers between devices: none -> 145 us  [the longest x21 67.2 us: outer_from(): lax.ppermute(v, 'dp', [((o + k) % n * 2 + x, o * 2 + x) for o in range(n)...]
    pallas_call x0 -> x11, Pallas kernels: none -> 113 us  [the longest x1 27.6 us: ssd_backward(): pl.pallas_call(ssd_backward_kernel, grid=(count,), in_specs=common_specs(...]
    ppermute x0 -> x74, starting transfers between devices: none -> 101 us  [the longest x21 49.9 us: outer_from(): lax.ppermute(v, 'dp', [((o + k) % n * 2 + x, o * 2 + x) for o in range(n)...]
    psum x1 -> x0, waiting for transfers between devices: 98.8 us -> none  [body(): lax.psum(term + contract_last(grad_step_low, back_step) + contract_last(b...]
    psum x4 -> x0, blocking collectives: 79.3 us -> none  [the longest x1 39.6 us: body(): lax.psum((grad_norm_gain, grad_conv_all, grad_bc_table, grad_head), 'dp')]
    dynamic_update_slice x20 -> x12, local copies, waits for them, and re-layouts: 83.1 us -> 13.3 us  [in_rank_order(): lax.dynamic_update_slice_in_dim(full, piece, (rank ^ r) * width, axis)]
  transfers between devices with their start and end apart: 9 -> 76, of which waited for: 6 -> 30; matrix products, arithmetic and copies ran while one was open for 18% -> 14% of each run, Pallas kernels for 0% -> 12%
where the time goes in v1:
time: 547 us; the launch traced here: 544 us
  waiting for transfers between devices  197 us (36%)
  Pallas kernels  113 us (21%)
  starting transfers between devices  101 us (18%)
  local copies, waits for them, and re-layouts  48.7 us (9%)
  blocking collectives  32 us (6%)
  other arithmetic  30.9 us (6%)
  between operations  14.9 us (3%)
  matrix products  5.61 us (1%)
    ppermute x21, waiting for transfers between devices, outer_from(): lax.ppermute(v, 'dp', [((o + k) % n * 2 + x, o * 2 + x) for o in range(n)...  67.2 us
    ppermute x29, waiting for transfers between devices, inner_flip(): lax.ppermute(v, 'dp', [(d ^ 1, d) for d in range(lax.axis_size('dp'))])  57.5 us
    unnamed x3, waiting for transfers between devices  52.6 us
    ppermute x21, starting transfers between devices, outer_from(): lax.ppermute(v, 'dp', [((o + k) % n * 2 + x, o * 2 + x) for o in range(n)...  49.9 us
    ppermute x29, starting transfers between devices, inner_flip(): lax.ppermute(v, 'dp', [(d ^ 1, d) for d in range(lax.axis_size('dp'))])  33.5 us
    all_gather x1, blocking collectives, body(): w_step = lax.all_gather(step_weight.astype(bf16), 'dp', axis=0, tiled=True)  32 us
    pallas_call x1, Pallas kernels, ssd_backward(): pl.pallas_call(ssd_backward_kernel, grid=(count,), in_specs=common_specs(...  27.6 us
    pallas_call x3, Pallas kernels, weight_grad(): pl.pallas_call(functools.partial(weight_grad_kernel, rows=rows), grid=(de...  20.8 us
  transfers between devices with their start and end apart: 76, of which 30 were waited for; matrix products, arithmetic and copies ran while one was open for 14% of the time, Pallas kernels for 12%

profile of v1, /device:TPU:0, one launch (start us, length us, event | category | flops | bytes accessed | tf_op | source)
XLA Modules:
  0.0 543.7 jit_solution(16100850204723479754)
XLA Ops:
  9.5 5.0 collective-permute-start.4
  16.3 2.2 collective-permute-start.13
  18.6 1.9 collective-permute-start.15
  23.7 6.7 %collective-permute-done.11.refs_10_ = bf16[192,256]{1,0:T(8,128)(2,1)S(1)} collective-permute-done((bf16[192,256]{1,0:T(8,128)(2,1)S(1)}, bf16[192,256]{1,0:T(8,128)(2,1)S(1)}, u32[]{:S(2)}, u32[]{:S(2)}) %collective-permute-start.11) | collective-permute-done | bytes 98336 | tf_op jit(solution)/shard_map/ppermute | solution.py:661
  31.9 9.8 %collective-permute-done.13.refs_12_ = bf16[192,256]{1,0:T(8,128)(2,1)S(1)} collective-permute-done((bf16[192,256]{1,0:T(8,128)(2,1)S(1)}, bf16[192,256]{1,0:T(8,128)(2,1)S(1)}, u32[]{:S(2)}, u32[]{:S(2)}) %collective-permute-start.13) | collective-permute-done | bytes 98336 | tf_op jit(solution)/shard_map/ppermute | solution.py:661
  43.9 2.7 collective-permute-start.8
  50.0 4.0 collective-permute-done.16.refs_15_
  55.5 2.4 collective-permute-start.18
  58.8 3.9 collective-permute-done.3.refs_1_
  64.2 5.8 %collective-permute-done.18.refs_2_ = bf16[192,768]{1,0:T(8,128)(2,1)S(1)} collective-permute-done((bf16[192,768]{1,0:T(8,128)(2,1)}, bf16[192,768]{1,0:T(8,128)(2,1)S(1)}, u32[]{:S(2)}, u32[]{:S(2)}) %collective-permute-start.18) | collective-permute-done | bytes 294944 | tf_op jit(solution)/shard_map/ppermute | solution.py:661
  70.0 16.8 %collective-permute-done.20.refs_4_ = bf16[192,768]{1,0:T(8,128)(2,1)S(1)} collective-permute-done((bf16[192,768]{1,0:T(8,128)(2,1)}, bf16[192,768]{1,0:T(8,128)(2,1)S(1)}, u32[]{:S(2)}, u32[]{:S(2)}) %collective-permute-start.20) | collective-permute-done | bytes 294944 | tf_op jit(solution)/shard_map/ppermute | solution.py:661
  89.6 32.0 %all-gather = bf16[8,192,12]{1,2,0:T(8,128)(2,1)} all-gather(bf16[1,192,12]{1,2,0:T(8,128)(2,1)S(1)} %convert_bitcast_fusion.1), channel_id=1, replica_groups=mesh['dp'=8,'mp'=4] {'dp'}, dimensions={0}, use_global_device_ids=true | all-gather | bytes 41472 | tf_op jit(solution)/shard_map/all_gather | solution.py:763
  130.1 1.9 collective-permute-start.5
  135.8 4.5 collective-permute-done.5.refs_3_
  140.3 6.4 %collective-permute-done.7.refs_5_ = bf16[192,768]{1,0:T(8,128)(2,1)} collective-permute-done((bf16[192,768]{1,0:T(8,128)(2,1)}, bf16[192,768]{1,0:T(8,128)(2,1)}, u32[]{:S(2)}, u32[]{:S(2)}) %collective-permute-start.7) | collective-permute-done | bytes 294944 | tf_op jit(solution)/shard_map/ppermute | solution.py:670
  148.6 4.0 collective-permute-done.9.refs_7_
  153.9 8.6 %project.1 = (f32[1024,768]{1,0:T(8,128)}, f32[1024,256]{1,0:T(8,128)}, bf16[1536,768]{1,0:T(8,128)(2,1)}, bf16[1536,256]{1,0:T(8,128)(2,1)}) custom-call(s32[8]{0:T(128)} %fusion.37.idx_ref, bf16[1024,1536]{1,0:T(8,128)(2,1)} %copy-done, bf16[192,768]{1,0:T(8,128)(2,1)} %copy-done.27, bf16[192,768]{1,0:T(8,128)(2,1)} %copy-done.50, ...), custom_call_target="tpu_custom_call" | custom-call | flops 3221225472 | bytes 9437184 | tf_op jit(solution)/shard_map/project/pallas_call | solution.py:403
  162.5 13.6 %ssd_forward.1 = (f32[1024,768]{1,0:T(8,128)}, bf16[8,128,768]{2,1,0:T(8,128)(2,1)}) custom-call(f32[1024,768]{1,0:T(8,128)} %get-tuple-element.41.x_ref.xb_ref, f32[1024,768]{1,0:T(8,128)} %get-tuple-element.41.x_ref.xb_ref, f32[1024,256]{1,0:T(8,128)} %get-tuple-element.42.bc_ref.bcb_ref, f32[1024,256]{1,0:T(8,128)} %get-tuple-element.42.bc_ref.bcb_ref, ...), custom_call_target="tpu_custom_call" | custom-call | tf_op jit(solution)/shard_map/ssd_forward/pallas_call | solution.py:280
  185.0 2.0 collective-permute-done.23.refs_7_
  187.0 3.2 collective-permute-done.26.refs_11_
  190.2 3.2 collective-permute-done.28.refs_13_
  193.3 3.2 collective-permute-done.30.refs_15_
  197.2 12.6 %gate_forward.1 = (f32[1024,768]{1,0:T(8,128)}, f32[1024,768]{1,0:T(8,128)}, f32[8,1024]{1,0:T(8,128)}, bf16[1536,768]{1,0:T(8,128)(2,1)}, bf16[1536,768]{1,0:T(8,128)(2,1)}) custom-call(s32[8]{0:T(128)} %fusion.37.idx_ref, bf16[1024,1536]{1,0:T(8,128)(2,1)} %copy-done, bf16[1024,1536]{1,0:T(8,128)(2,1)} %copy-done.4, ...), custom_call_target="tpu_custom_call" | custom-call | flops 4831838208 | bytes 9437184 | tf_op jit(solution)/shard_map/gate_forward/pallas_call | solution.py:457
  212.6 2.7 collective-permute-start.32
  218.0 7.7 %gate_backward.1 = (bf16[1024,768]{1,0:T(8,128)(2,1)}, bf16[1024,768]{1,0:T(8,128)(2,1)}, bf16[1024,768]{1,0:T(8,128)(2,1)}, f32[8,768]{1,0:T(8,128)}) custom-call(f32[1024,768]{1,0:T(8,128)} %get-tuple-element.44.gate_ref, f32[1024,768]{1,0:T(8,128)} %get-tuple-element.45.gout_ref, f32[1024,768]{1,0:T(8,128)} %get-tuple-element.43.mixed_ref, ...), custom_call_target="tpu_custom_call" | custom-call | tf_op jit(solution)/shard_map/gate_backward/pallas_call | solution.py:516
  225.7 27.6 %ssd_backward.1 = (bf16[1024,768]{1,0:T(8,128)(2,1)}, f32[1024,256]{1,0:T(8,128)}, f32[1024,128]{1,0:T(8,128)}, f32[8,768]{1,0:T(8,128)}, f32[8,256]{1,0:T(8,128)}, /*index=5*/f32[8,128]{1,0:T(8,128)}) custom-call(f32[1024,768]{1,0:T(8,128)} %get-tuple-element.41.x_ref.xb_ref, f32[1024,768]{1,0:T(8,128)} %get-tuple-element.41.x_ref.xb_ref, ...), custom_call_target="tpu_custom_call" | custom-call | tf_op jit(solution)/shard_map/ssd_backward/pallas_call | solution.py:308
  257.8 6.8 %weight_grad.5 = bf16[8,192,768]{2,1,0:T(8,128)(2,1)} custom-call(s32[8]{0:T(128)} %fusion.39.slot_ref, bf16[1024,1536]{1,0:T(8,128)(2,1)} %copy-done.4, bf16[1024,768]{1,0:T(8,128)(2,1)} %get-tuple-element.47.lhs_ref.rhs_ref), custom_call_target="tpu_custom_call" | custom-call | flops 2415919104 | bytes 4718592 | tf_op jit(solution)/shard_map/weight_grad/pallas_call | solution.py:548
  264.6 2.3 slice_bitcast_fusion.10
  270.5 6.9 %weight_grad.3 = bf16[8,192,768]{2,1,0:T(8,128)(2,1)} custom-call(s32[8]{0:T(128)} %fusion.39.slot_ref, bf16[1024,1536]{1,0:T(8,128)(2,1)} %copy-done, bf16[1024,768]{1,0:T(8,128)(2,1)} %get-tuple-element.57.gg_ref.rhs_ref), custom_call_target="tpu_custom_call" | custom-call | flops 2415919104 | bytes 4718592 | tf_op jit(solution)/shard_map/weight_grad/pallas_call | solution.py:548
  277.3 2.3 slice_bitcast_fusion.26
  279.6 7.1 %weight_grad.4 = bf16[8,192,768]{2,1,0:T(8,128)(2,1)} custom-call(s32[8]{0:T(128)} %fusion.39.slot_ref, bf16[1024,1536]{1,0:T(8,128)(2,1)} %copy-done, bf16[1024,768]{1,0:T(8,128)(2,1)} %get-tuple-element.55.gx_ref.rhs_ref), custom_call_target="tpu_custom_call" | custom-call | flops 2415919104 | bytes 4718592 | tf_op jit(solution)/shard_map/weight_grad/pallas_call | solution.py:548
  286.7 2.3 slice_bitcast_fusion.18
  289.0 1.9 fusion.21
  291.0 6.7 %out_partial.1 = (bf16[1024,384]{1,0:T(8,128)(2,1)}, bf16[1024,384]{1,0:T(8,128)(2,1)}, bf16[1024,384]{1,0:T(8,128)(2,1)}, bf16[1024,384]{1,0:T(8,128)(2,1)}) custom-call(s32[1]{0:T(128)} %bitcast.rank_ref, bf16[1024,768]{1,0:T(8,128)(2,1)} %get-tuple-element.47.lhs_ref.rhs_ref, bf16[1536,768]{1,0:T(8,128)(2,1)} %get-tuple-element.48.w_ref), custom_call_target="tpu_custom_call" | custom-call | flops 2415919104 | bytes 4718592 | tf_op jit(solution)/shard_map/out_partial/pallas_call | solution.py:577
  299.5 1.9 collective-permute-start.38
  301.4 52.6 %reduce-scatter.9.cloned.1.call-done = f32[192,12]{1,0:T(8,128)} async-done(((f32[1536,12]{1,0:T(8,128)}), f32[192,12]{1,0:T(8,128)}) %reduce-scatter.9.cloned.1.call-update) | async-done | bytes 9232
  357.6 1.9 add_convert_fusion.2.gb_ref
  359.5 11.3 %normed_term.1 = bf16[4,256,1536]{2,1,0:T(8,128)(2,1)} custom-call(s32[1]{0:T(128)} %bitcast.rank_ref, bf16[1024,768]{1,0:T(8,128)(2,1)} %get-tuple-element.55.gx_ref.rhs_ref, bf16[1536,768]{1,0:T(8,128)(2,1)} %get-tuple-element.56.wx_ref, bf16[1024,768]{1,0:T(8,128)(2,1)} %get-tuple-element.57.gg_ref.rhs_ref, bf16[1536,768]{1,0:T(8,128)(2,1)} %get-tuple-element.58.wg_ref, ...), custom_call_target="tpu_custom_call" | custom-call | flops 5033164800 | bytes 9437184 | tf_op jit(solution)/shard_map/normed_term/pallas_call | solution.py:608
  370.8 2.7 slice_bitcast_fusion
  378.8 1.9 fusion.51
  383.8 6.9 %collective-permute-done.49 = bf16[192,768]{1,0:T(8,128)(2,1)} collective-permute-done((bf16[192,768]{1,0:T(8,128)(2,1)}, bf16[192,768]{1,0:T(8,128)(2,1)}, u32[]{:S(2)}, u32[]{:S(2)}) %collective-permute-start.49) | collective-permute-done | bytes 294944 | tf_op jit(solution)/shard_map/ppermute | solution.py:670
  390.7 6.8 %collective-permute-done.52 = bf16[192,768]{1,0:T(8,128)(2,1)} collective-permute-done((bf16[192,768]{1,0:T(8,128)(2,1)}, bf16[192,768]{1,0:T(8,128)(2,1)}, u32[]{:S(2)}, u32[]{:S(2)}) %collective-permute-start.52) | collective-permute-done | bytes 294944 | tf_op jit(solution)/shard_map/ppermute | solution.py:670
  398.7 5.7 %collective-permute-done.54 = bf16[192,768]{1,0:T(8,128)(2,1)} collective-permute-done((bf16[192,768]{1,0:T(8,128)(2,1)}, bf16[192,768]{1,0:T(8,128)(2,1)}, u32[]{:S(2)}, u32[]{:S(2)}) %collective-permute-start.54) | collective-permute-done | bytes 294944 | tf_op jit(solution)/shard_map/ppermute | solution.py:670
  405.7 2.0 collective-permute-done.56
  407.7 2.2 collective-permute-start.67
  413.3 6.8 %collective-permute-done.65 = bf16[192,768]{1,0:T(8,128)(2,1)S(1)} collective-permute-done((bf16[192,768]{1,0:T(8,128)(2,1)S(1)}, bf16[192,768]{1,0:T(8,128)(2,1)S(1)}, u32[]{:S(2)}, u32[]{:S(2)}) %collective-permute-start.65) | collective-permute-done | bytes 294944 | tf_op jit(solution)/shard_map/ppermute | solution.py:661
  420.1 10.0 %collective-permute-start.46 = (bf16[192,768]{1,0:T(8,128)(2,1)S(1)}, bf16[192,768]{1,0:T(8,128)(2,1)S(1)}, u32[]{:S(2)}, u32[]{:S(2)}) collective-permute-start(bf16[192,768]{1,0:T(8,128)(2,1)S(1)} %get-tuple-element.125), channel_id=1, source_target_pairs={{24,0},{28,4},{0,8},{4,12},{8,16},{12,20},{16,24},{20,28},{25,1},{... | collective-permute-start | bytes 884744 | tf_op jit(solution)/shard_map/ppermute | solution.py:661
  430.1 3.5 collective-permute-start.48
  433.7 2.1 multiply_subtract_fusion.1
  435.8 5.2 collective-permute-done.46
  441.0 2.5 collective-permute-start.50
  443.6 9.2 %collective-permute-done.48 = bf16[192,768]{1,0:T(8,128)(2,1)S(1)} collective-permute-done((bf16[192,768]{1,0:T(8,128)(2,1)S(1)}, bf16[192,768]{1,0:T(8,128)(2,1)S(1)}, u32[]{:S(2)}, u32[]{:S(2)}) %collective-permute-start.48) | collective-permute-done | bytes 294944 | tf_op jit(solution)/shard_map/ppermute | solution.py:661
  452.8 9.9 %collective-permute-start.53 = (bf16[192,768]{1,0:T(8,128)(2,1)S(1)}, bf16[192,768]{1,0:T(8,128)(2,1)S(1)}, u32[]{:S(2)}, u32[]{:S(2)}) collective-permute-start(bf16[192,768]{1,0:T(8,128)(2,1)S(1)} %get-tuple-element.132), channel_id=1, source_target_pairs={{24,0},{28,4},{0,8},{4,12},{8,16},{12,20},{16,24},{20,28},{25,1},{... | collective-permute-start | bytes 884744 | tf_op jit(solution)/shard_map/ppermute | solution.py:661
  462.7 3.4 collective-permute-start.55
  470.3 6.1 %collective-permute-done.55 = bf16[192,768]{1,0:T(8,128)(2,1)S(1)} collective-permute-done((bf16[192,768]{1,0:T(8,128)(2,1)S(1)}, bf16[192,768]{1,0:T(8,128)(2,1)S(1)}, u32[]{:S(2)}, u32[]{:S(2)}) %collective-permute-start.55) | collective-permute-done | bytes 294944 | tf_op jit(solution)/shard_map/ppermute | solution.py:661
  480.9 4.0 norm_backward.1
  485.8 2.2 add_convert_fusion.1
  491.5 1.9 copy.82
  493.5 1.9 copy.83
  499.1 9.3 %collective-permute-done.70 = f32[22,128]{1,0:T(8,128)S(1)} collective-permute-done((f32[22,128]{1,0:T(8,128)S(1)}, f32[22,128]{1,0:T(8,128)S(1)}, u32[]{:S(2)}, u32[]{:S(2)}) %collective-permute-start.70) | collective-permute-done | bytes 11296 | tf_op jit(solution)/shard_map/ppermute | solution.py:674
  512.5 3.5 collective-permute-start.72
  516.0 2.9 add_convert_fusion
  520.8 3.1 collective-permute-done.73
  525.2 5.2 collective-permute-done.43
  (337 shorter events, 109.4 us)
Async XLA Ops:
  7.2 346.7 %reduce-scatter.9.cloned.1.call-start = ((), (), s32[]{:S(2)}) async-start(), calls=%async_computation.3 | async-start | bytes 884736
  9.5 46.0 %collective-permute-start.4 = (bf16[192,768]{1,0:T(8,128)(2,1)S(1)}, bf16[192,768]{1,0:T(8,128)(2,1)}, u32[]{:S(2)}, u32[]{:S(2)}) collective-permute-start(bf16[192,768]{1,0:T(8,128)(2,1)S(1)} %get-tuple-element.140.refs_0_), channel_id=1, source_target_pairs={{8,0},{12,4},{16,8},{20,12},{24,16},{28,20},{0,24},{4,28},{9,1},{1... | collective-permute-start | bytes 884744 | tf_op jit(solution)/shard_map/ppermute | solution.py:661
  14.6 43.3 %collective-permute-start.6 = (bf16[192,768]{1,0:T(8,128)(2,1)S(1)}, bf16[192,768]{1,0:T(8,128)(2,1)}, u32[]{:S(2)}, u32[]{:S(2)}) collective-permute-start(bf16[192,768]{1,0:T(8,128)(2,1)S(1)} %get-tuple-element.140.refs_0_), channel_id=1, source_target_pairs={{16,0},{20,4},{24,8},{28,12},{0,16},{4,20},{8,24},{12,28},{17,1},{... | collective-permute-start | bytes 884744 | tf_op jit(solution)/shard_map/ppermute | solution.py:661
  15.5 14.9 %collective-permute-start.11 = (bf16[192,256]{1,0:T(8,128)(2,1)S(1)}, bf16[192,256]{1,0:T(8,128)(2,1)S(1)}, u32[]{:S(2)}, u32[]{:S(2)}) collective-permute-start(bf16[192,256]{1,0:T(8,128)(2,1)S(1)} %convert_element_type.319.refs_8_), channel_id=1, source_target_pairs={{8,0},{12,4},{16,8},{20,12},{24,16},{28,20},{0,24},{4,28},{9,1},{1... | collective-permute-start | bytes 294920 | tf_op jit(solution)/shard_map/ppermute | solution.py:661
  16.3 25.4 %collective-permute-start.13 = (bf16[192,256]{1,0:T(8,128)(2,1)S(1)}, bf16[192,256]{1,0:T(8,128)(2,1)S(1)}, u32[]{:S(2)}, u32[]{:S(2)}) collective-permute-start(bf16[192,256]{1,0:T(8,128)(2,1)S(1)} %convert_element_type.319.refs_8_), channel_id=1, source_target_pairs={{16,0},{20,4},{24,8},{28,12},{0,16},{4,20},{8,24},{12,28},{17,1},{... | collective-permute-start | bytes 294920 | tf_op jit(solution)/shard_map/ppermute | solution.py:661
  18.6 24.7 %collective-permute-start.15 = (bf16[192,256]{1,0:T(8,128)(2,1)S(1)}, bf16[192,256]{1,0:T(8,128)(2,1)}, u32[]{:S(2)}, u32[]{:S(2)}) collective-permute-start(bf16[192,256]{1,0:T(8,128)(2,1)S(1)} %convert_element_type.319.refs_8_), channel_id=1, source_target_pairs={{24,0},{28,4},{0,8},{4,12},{8,16},{12,20},{16,24},{20,28},{25,1},{... | collective-permute-start | bytes 294920 | tf_op jit(solution)/shard_map/ppermute | solution.py:661
  30.4 13.4 %collective-permute-start.10 = (bf16[192,256]{1,0:T(8,128)(2,1)S(1)}, bf16[192,256]{1,0:T(8,128)(2,1)S(1)}, u32[]{:S(2)}, u32[]{:S(2)}) collective-permute-start(bf16[192,256]{1,0:T(8,128)(2,1)S(1)} %convert_element_type.319.refs_8_), channel_id=1, source_target_pairs={{4,0},{0,4},{12,8},{8,12},{20,16},{16,20},{28,24},{24,28},{5,1},{1... | collective-permute-start | bytes 294920 | tf_op jit(solution)/shard_map/ppermute | solution.py:670
  43.9 14.2 %collective-permute-start.8 = (bf16[192,768]{1,0:T(8,128)(2,1)S(1)}, bf16[192,768]{1,0:T(8,128)(2,1)}, u32[]{:S(2)}, u32[]{:S(2)}) collective-permute-start(bf16[192,768]{1,0:T(8,128)(2,1)S(1)} %get-tuple-element.140.refs_0_), channel_id=1, source_target_pairs={{24,0},{28,4},{0,8},{4,12},{8,16},{12,20},{16,24},{20,28},{25,1},{... | collective-permute-start | bytes 884744 | tf_op jit(solution)/shard_map/ppermute | solution.py:661
  46.6 40.9 %collective-permute-start.1 = (bf16[1024,384]{1,0:T(8,128)(2,1)}, bf16[1024,384]{1,0:T(8,128)(2,1)}, u32[]{:S(2)}, u32[]{:S(2)}) collective-permute-start(bf16[1024,384]{1,0:T(8,128)(2,1)} %param.21), channel_id=1, source_target_pairs={{2,0},{3,1},{0,2},{1,3},{6,4},{7,5},{4,6},{5,7},{10,8},{11,9},{8,1... | collective-permute-start | bytes 2359304 | tf_op jit(solution)/shard_map/ppermute | solution.py:674
  54.0 8.7 %collective-permute-start.3 = (bf16[192,768]{1,0:T(8,128)(2,1)S(1)}, bf16[192,768]{1,0:T(8,128)(2,1)S(1)}, u32[]{:S(2)}, u32[]{:S(2)}) collective-permute-start(bf16[192,768]{1,0:T(8,128)(2,1)S(1)} %get-tuple-element.140.refs_0_), channel_id=1, source_target_pairs={{4,0},{0,4},{12,8},{8,12},{20,16},{16,20},{28,24},{24,28},{5,1},{1... | collective-permute-start | bytes 884744 | tf_op jit(solution)/shard_map/ppermute | solution.py:670
  55.5 14.4 %collective-permute-start.18 = (bf16[192,768]{1,0:T(8,128)(2,1)}, bf16[192,768]{1,0:T(8,128)(2,1)S(1)}, u32[]{:S(2)}, u32[]{:S(2)}) collective-permute-start(bf16[192,768]{1,0:T(8,128)(2,1)} %get-tuple-element.139.refs_0_), channel_id=1, source_target_pairs={{8,0},{12,4},{16,8},{20,12},{24,16},{28,20},{0,24},{4,28},{9,1},{1... | collective-permute-start | bytes 884744 | tf_op jit(solution)/shard_map/ppermute | solution.py:661
  57.9 28.8 %collective-permute-start.20 = (bf16[192,768]{1,0:T(8,128)(2,1)}, bf16[192,768]{1,0:T(8,128)(2,1)S(1)}, u32[]{:S(2)}, u32[]{:S(2)}) collective-permute-start(bf16[192,768]{1,0:T(8,128)(2,1)} %get-tuple-element.139.refs_0_), channel_id=1, source_target_pairs={{16,0},{20,4},{24,8},{28,12},{0,16},{4,20},{8,24},{12,28},{17,1},{... | collective-permute-start | bytes 884744 | tf_op jit(solution)/shard_map/ppermute | solution.py:661
  58.1 29.4 %collective-permute-start.22 = (bf16[192,768]{1,0:T(8,128)(2,1)}, bf16[192,768]{1,0:T(8,128)(2,1)}, u32[]{:S(2)}, u32[]{:S(2)}) collective-permute-start(bf16[192,768]{1,0:T(8,128)(2,1)} %get-tuple-element.139.refs_0_), channel_id=1, source_target_pairs={{24,0},{28,4},{0,8},{4,12},{8,16},{12,20},{16,24},{20,28},{25,1},{... | collective-permute-start | bytes 884744 | tf_op jit(solution)/shard_map/ppermute | solution.py:661
  62.7 67.4 %collective-permute-start.17 = (bf16[192,768]{1,0:T(8,128)(2,1)}, bf16[192,768]{1,0:T(8,128)(2,1)}, u32[]{:S(2)}, u32[]{:S(2)}) collective-permute-start(bf16[192,768]{1,0:T(8,128)(2,1)} %get-tuple-element.139.refs_0_), channel_id=1, source_target_pairs={{4,0},{0,4},{12,8},{8,12},{20,16},{16,20},{28,24},{24,28},{5,1},{1... | collective-permute-start | bytes 884744 | tf_op jit(solution)/shard_map/ppermute | solution.py:670
  70.0 62.0 %collective-permute-start.25 = (bf16[192,768]{1,0:T(8,128)(2,1)}, bf16[192,768]{1,0:T(8,128)(2,1)}, u32[]{:S(2)}, u32[]{:S(2)}) collective-permute-start(bf16[192,768]{1,0:T(8,128)(2,1)} %convert_bitcast_fusion.refs_8_), channel_id=1, source_target_pairs={{8,0},{12,4},{16,8},{20,12},{24,16},{28,20},{0,24},{4,28},{9,1},{1... | collective-permute-start | bytes 884744 | tf_op jit(solution)/shard_map/ppermute | solution.py:661
  86.7 45.4 %collective-permute-start.27 = (bf16[192,768]{1,0:T(8,128)(2,1)}, bf16[192,768]{1,0:T(8,128)(2,1)}, u32[]{:S(2)}, u32[]{:S(2)}) collective-permute-start(bf16[192,768]{1,0:T(8,128)(2,1)} %convert_bitcast_fusion.refs_8_), channel_id=1, source_target_pairs={{16,0},{20,4},{24,8},{28,12},{0,16},{4,20},{8,24},{12,28},{17,1},{... | collective-permute-start | bytes 884744 | tf_op jit(solution)/shard_map/ppermute | solution.py:661
  87.5 91.5 %collective-permute-start = (bf16[1024,384]{1,0:T(8,128)(2,1)}, bf16[1024,384]{1,0:T(8,128)(2,1)}, u32[]{:S(2)}, u32[]{:S(2)}) collective-permute-start(bf16[1024,384]{1,0:T(8,128)(2,1)} %param.21), channel_id=1, source_target_pairs={{1,0},{0,1},{3,2},{2,3},{5,4},{4,5},{7,6},{6,7},{9,8},{8,9},{11,10... | collective-permute-start | bytes 2359304 | tf_op jit(solution)/shard_map/ppermute | solution.py:674
  87.5 92.8 %collective-permute-start.2 = (bf16[1024,384]{1,0:T(8,128)(2,1)}, bf16[1024,384]{1,0:T(8,128)(2,1)}, u32[]{:S(2)}, u32[]{:S(2)}) collective-permute-start(bf16[1024,384]{1,0:T(8,128)(2,1)} %collective-permute-done.1), channel_id=1, source_target_pairs={{1,0},{0,1},{3,2},{2,3},{5,4},{4,5},{7,6},{6,7},{9,8},{8,9},{11,10... | collective-permute-start | bytes 2359304 | tf_op jit(solution)/shard_map/ppermute | solution.py:674
  130.1 10.2 %collective-permute-start.5 = (bf16[192,768]{1,0:T(8,128)(2,1)}, bf16[192,768]{1,0:T(8,128)(2,1)S(1)}, u32[]{:S(2)}, u32[]{:S(2)}) collective-permute-start(bf16[192,768]{1,0:T(8,128)(2,1)} %collective-permute-done.4.refs_2_), channel_id=1, source_target_pairs={{4,0},{0,4},{12,8},{8,12},{20,16},{16,20},{28,24},{24,28},{5,1},{1... | collective-permute-start | bytes 884744 | tf_op jit(solution)/shard_map/ppermute | solution.py:670
  132.0 14.7 %collective-permute-start.7 = (bf16[192,768]{1,0:T(8,128)(2,1)}, bf16[192,768]{1,0:T(8,128)(2,1)}, u32[]{:S(2)}, u32[]{:S(2)}) collective-permute-start(bf16[192,768]{1,0:T(8,128)(2,1)} %collective-permute-done.6.refs_4_), channel_id=1, source_target_pairs={{4,0},{0,4},{12,8},{8,12},{20,16},{16,20},{28,24},{24,28},{5,1},{1... | collective-permute-start | bytes 884744 | tf_op jit(solution)/shard_map/ppermute | solution.py:670
  132.2 20.4 %collective-permute-start.9 = (bf16[192,768]{1,0:T(8,128)(2,1)}, bf16[192,768]{1,0:T(8,128)(2,1)}, u32[]{:S(2)}, u32[]{:S(2)}) collective-permute-start(bf16[192,768]{1,0:T(8,128)(2,1)} %collective-permute-done.8.refs_6_), channel_id=1, source_target_pairs={{4,0},{0,4},{12,8},{8,12},{20,16},{16,20},{28,24},{24,28},{5,1},{1... | collective-permute-start | bytes 884744 | tf_op jit(solution)/shard_map/ppermute | solution.py:670
  140.3 35.8 %collective-permute-start.29 = (bf16[192,768]{1,0:T(8,128)(2,1)}, bf16[192,768]{1,0:T(8,128)(2,1)S(1)}, u32[]{:S(2)}, u32[]{:S(2)}) collective-permute-start(bf16[192,768]{1,0:T(8,128)(2,1)} %convert_bitcast_fusion.refs_8_), channel_id=1, source_target_pairs={{24,0},{28,4},{0,8},{4,12},{8,16},{12,20},{16,24},{20,28},{25,1},{... | collective-permute-start | bytes 884744 | tf_op jit(solution)/shard_map/ppermute | solution.py:661
  146.7 30.2 %collective-permute-start.24 = (bf16[192,768]{1,0:T(8,128)(2,1)}, bf16[192,768]{1,0:T(8,128)(2,1)S(1)}, u32[]{:S(2)}, u32[]{:S(2)}) collective-permute-start(bf16[192,768]{1,0:T(8,128)(2,1)} %convert_bitcast_fusion.refs_8_), channel_id=1, source_target_pairs={{4,0},{0,4},{12,8},{8,12},{20,16},{16,20},{28,24},{24,28},{5,1},{1... | collective-permute-start | bytes 884744 | tf_op jit(solution)/shard_map/ppermute | solution.py:670
  152.6 25.6 %collective-permute-start.19 = (bf16[192,768]{1,0:T(8,128)(2,1)S(1)}, bf16[192,768]{1,0:T(8,128)(2,1)S(1)}, u32[]{:S(2)}, u32[]{:S(2)}) collective-permute-start(bf16[192,768]{1,0:T(8,128)(2,1)S(1)} %copy-done.47), channel_id=1, source_target_pairs={{4,0},{0,4},{12,8},{8,12},{20,16},{16,20},{28,24},{24,28},{5,1},{1... | collective-permute-start | bytes 884744 | tf_op jit(solution)/shard_map/ppermute | solution.py:670
  176.1 8.8 %collective-permute-start.21 = (bf16[192,768]{1,0:T(8,128)(2,1)S(1)}, bf16[192,768]{1,0:T(8,128)(2,1)S(1)}, u32[]{:S(2)}, u32[]{:S(2)}) collective-permute-start(bf16[192,768]{1,0:T(8,128)(2,1)S(1)} %copy-done.49), channel_id=1, source_target_pairs={{4,0},{0,4},{12,8},{8,12},{20,16},{16,20},{28,24},{24,28},{5,1},{1... | collective-permute-start | bytes 884744 | tf_op jit(solution)/shard_map/ppermute | solution.py:670
  176.9 10.1 %collective-permute-start.23 = (bf16[192,768]{1,0:T(8,128)(2,1)}, bf16[192,768]{1,0:T(8,128)(2,1)S(1)}, u32[]{:S(2)}, u32[]{:S(2)}) collective-permute-start(bf16[192,768]{1,0:T(8,128)(2,1)} %collective-permute-done.22.refs_6_), channel_id=1, source_target_pairs={{4,0},{0,4},{12,8},{8,12},{20,16},{16,20},{28,24},{24,28},{5,1},{1... | collective-permute-start | bytes 884744 | tf_op jit(solution)/shard_map/ppermute | solution.py:670
  178.2 11.9 %collective-permute-start.26 = (bf16[192,768]{1,0:T(8,128)(2,1)}, bf16[192,768]{1,0:T(8,128)(2,1)S(1)}, u32[]{:S(2)}, u32[]{:S(2)}) collective-permute-start(bf16[192,768]{1,0:T(8,128)(2,1)} %collective-permute-done.25.refs_10_), channel_id=1, source_target_pairs={{4,0},{0,4},{12,8},{8,12},{20,16},{16,20},{28,24},{24,28},{5,1},{1... | collective-permute-start | bytes 884744 | tf_op jit(solution)/shard_map/ppermute | solution.py:670
  179.0 14.3 %collective-permute-start.28 = (bf16[192,768]{1,0:T(8,128)(2,1)}, bf16[192,768]{1,0:T(8,128)(2,1)S(1)}, u32[]{:S(2)}, u32[]{:S(2)}) collective-permute-start(bf16[192,768]{1,0:T(8,128)(2,1)} %collective-permute-done.27.refs_12_), channel_id=1, source_target_pairs={{4,0},{0,4},{12,8},{8,12},{20,16},{16,20},{28,24},{24,28},{5,1},{1... | collective-permute-start | bytes 884744 | tf_op jit(solution)/shard_map/ppermute | solution.py:670
  180.3 16.2 %collective-permute-start.30 = (bf16[192,768]{1,0:T(8,128)(2,1)S(1)}, bf16[192,768]{1,0:T(8,128)(2,1)S(1)}, u32[]{:S(2)}, u32[]{:S(2)}) collective-permute-start(bf16[192,768]{1,0:T(8,128)(2,1)S(1)} %collective-permute-done.29.refs_14_), channel_id=1, source_target_pairs={{4,0},{0,4},{12,8},{8,12},{20,16},{16,20},{28,24},{24,28},{5,1},{1... | collective-permute-start | bytes 884744 | tf_op jit(solution)/shard_map/ppermute | solution.py:670
  256.4 41.3 %collective-permute-start.37 = (bf16[1024,64]{1,0:T(8,128)(2,1)}, bf16[1024,64]{1,0:T(8,128)(2,1)}, u32[]{:S(2)}, u32[]{:S(2)}) collective-permute-start(bf16[1024,64]{1,0:T(8,128)(2,1)} %get-tuple-element.142), channel_id=1, source_target_pairs={{1,0},{0,1},{3,2},{2,3},{5,4},{4,5},{7,6},{6,7},{9,8},{8,9},{11,10... | collective-permute-start | bytes 393224 | tf_op jit(solution)/shard_map/ppermute | solution.py:674
  256.4 99.1 %collective-permute-start.36 = (bf16[1024,64]{1,0:T(8,128)(2,1)}, bf16[1024,64]{1,0:T(8,128)(2,1)}, u32[]{:S(2)}, u32[]{:S(2)}) collective-permute-start(bf16[1024,64]{1,0:T(8,128)(2,1)} %get-tuple-element.141), channel_id=1, source_target_pairs={{1,0},{0,1},{3,2},{2,3},{5,4},{4,5},{7,6},{6,7},{9,8},{8,9},{11,10... | collective-permute-start | bytes 393224 | tf_op jit(solution)/shard_map/ppermute | solution.py:674
  266.8 106.7 %collective-permute-start.62 = (bf16[192,768]{1,0:T(8,128)(2,1)}, bf16[192,768]{1,0:T(8,128)(2,1)}, u32[]{:S(2)}, u32[]{:S(2)}) collective-permute-start(bf16[192,768]{1,0:T(8,128)(2,1)} %get-tuple-element.119), channel_id=1, source_target_pairs={{4,0},{0,4},{12,8},{8,12},{20,16},{16,20},{28,24},{24,28},{5,1},{1... | collective-permute-start | bytes 884744 | tf_op jit(solution)/shard_map/ppermute | solution.py:670
  268.5 106.2 %collective-permute-start.64 = (bf16[192,768]{1,0:T(8,128)(2,1)}, bf16[192,768]{1,0:T(8,128)(2,1)}, u32[]{:S(2)}, u32[]{:S(2)}) collective-permute-start(bf16[192,768]{1,0:T(8,128)(2,1)} %get-tuple-element.122), channel_id=1, source_target_pairs={{4,0},{0,4},{12,8},{8,12},{20,16},{16,20},{28,24},{24,28},{5,1},{1... | collective-permute-start | bytes 884744 | tf_op jit(solution)/shard_map/ppermute | solution.py:670
  268.9 106.7 %collective-permute-start.66 = (bf16[192,768]{1,0:T(8,128)(2,1)}, bf16[192,768]{1,0:T(8,128)(2,1)}, u32[]{:S(2)}, u32[]{:S(2)}) collective-permute-start(bf16[192,768]{1,0:T(8,128)(2,1)} %get-tuple-element.121), channel_id=1, source_target_pairs={{4,0},{0,4},{12,8},{8,12},{20,16},{16,20},{28,24},{24,28},{5,1},{1... | collective-permute-start | bytes 884744 | tf_op jit(solution)/shard_map/ppermute | solution.py:670
  290.9 186.1 %reduce-scatter.7.cloned.1.call-start = ((), (), s32[]{:S(2)}) async-start(), calls=%async_computation.2 | async-start | bytes 884736 | tf_op jit(solution)/shard_map/reduce_scatter | solution.py:810
  299.5 57.3 %collective-permute-start.38 = (bf16[1024,64]{1,0:T(8,128)(2,1)}, bf16[1024,64]{1,0:T(8,128)(2,1)S(1)}, u32[]{:S(2)}, u32[]{:S(2)}) collective-permute-start(bf16[1024,64]{1,0:T(8,128)(2,1)} %add_convert_fusion.3), channel_id=1, source_target_pairs={{2,0},{3,1},{0,2},{1,3},{6,4},{7,5},{4,6},{5,7},{10,8},{11,9},{8,1... | collective-permute-start | bytes 393224 | tf_op jit(solution)/shard_map/ppermute | solution.py:674
  355.5 21.2 %collective-permute-start.68 = (bf16[192,768]{1,0:T(8,128)(2,1)}, bf16[192,768]{1,0:T(8,128)(2,1)S(1)}, u32[]{:S(2)}, u32[]{:S(2)}) collective-permute-start(bf16[192,768]{1,0:T(8,128)(2,1)} %get-tuple-element.120), channel_id=1, source_target_pairs={{4,0},{0,4},{12,8},{8,12},{20,16},{16,20},{28,24},{24,28},{5,1},{1... | collective-permute-start | bytes 884744 | tf_op jit(solution)/shard_map/ppermute | solution.py:670
  356.8 20.8 %collective-permute-start.45 = (bf16[192,768]{1,0:T(8,128)(2,1)}, bf16[192,768]{1,0:T(8,128)(2,1)S(1)}, u32[]{:S(2)}, u32[]{:S(2)}) collective-permute-start(bf16[192,768]{1,0:T(8,128)(2,1)} %get-tuple-element.128), channel_id=1, source_target_pairs={{4,0},{0,4},{12,8},{8,12},{20,16},{16,20},{28,24},{24,28},{5,1},{1... | collective-permute-start | bytes 884744 | tf_op jit(solution)/shard_map/ppermute | solution.py:670
  373.5 10.3 %collective-permute-start.47 = (bf16[192,768]{1,0:T(8,128)(2,1)}, bf16[192,768]{1,0:T(8,128)(2,1)}, u32[]{:S(2)}, u32[]{:S(2)}) collective-permute-start(bf16[192,768]{1,0:T(8,128)(2,1)} %get-tuple-element.131), channel_id=1, source_target_pairs={{4,0},{0,4},{12,8},{8,12},{20,16},{16,20},{28,24},{24,28},{5,1},{1... | collective-permute-start | bytes 884744 | tf_op jit(solution)/shard_map/ppermute | solution.py:670
  374.7 16.0 %collective-permute-start.49 = (bf16[192,768]{1,0:T(8,128)(2,1)}, bf16[192,768]{1,0:T(8,128)(2,1)}, u32[]{:S(2)}, u32[]{:S(2)}) collective-permute-start(bf16[192,768]{1,0:T(8,128)(2,1)} %get-tuple-element.130), channel_id=1, source_target_pairs={{4,0},{0,4},{12,8},{8,12},{20,16},{16,20},{28,24},{24,28},{5,1},{1... | collective-permute-start | bytes 884744 | tf_op jit(solution)/shard_map/ppermute | solution.py:670
  375.5 21.9 %collective-permute-start.52 = (bf16[192,768]{1,0:T(8,128)(2,1)}, bf16[192,768]{1,0:T(8,128)(2,1)}, u32[]{:S(2)}, u32[]{:S(2)}) collective-permute-start(bf16[192,768]{1,0:T(8,128)(2,1)} %get-tuple-element.135), channel_id=1, source_target_pairs={{4,0},{0,4},{12,8},{8,12},{20,16},{16,20},{28,24},{24,28},{5,1},{1... | collective-permute-start | bytes 884744 | tf_op jit(solution)/shard_map/ppermute | solution.py:670
  376.7 27.7 %collective-permute-start.54 = (bf16[192,768]{1,0:T(8,128)(2,1)}, bf16[192,768]{1,0:T(8,128)(2,1)}, u32[]{:S(2)}, u32[]{:S(2)}) collective-permute-start(bf16[192,768]{1,0:T(8,128)(2,1)} %get-tuple-element.138), channel_id=1, source_target_pairs={{4,0},{0,4},{12,8},{8,12},{20,16},{16,20},{28,24},{24,28},{5,1},{1... | collective-permute-start | bytes 884744 | tf_op jit(solution)/shard_map/ppermute | solution.py:670
  377.6 30.1 %collective-permute-start.56 = (bf16[192,768]{1,0:T(8,128)(2,1)S(1)}, bf16[192,768]{1,0:T(8,128)(2,1)}, u32[]{:S(2)}, u32[]{:S(2)}) collective-permute-start(bf16[192,768]{1,0:T(8,128)(2,1)S(1)} %copy-done.26), channel_id=1, source_target_pairs={{4,0},{0,4},{12,8},{8,12},{20,16},{16,20},{28,24},{24,28},{5,1},{1... | collective-permute-start | bytes 884744 | tf_op jit(solution)/shard_map/ppermute | solution.py:670
  383.8 78.9 %collective-permute-start.39 = (bf16[256,1536]{1,0:T(8,128)(2,1)}, bf16[256,1536]{1,0:T(8,128)(2,1)S(1)}, u32[]{:S(2)}, u32[]{:S(2)}) collective-permute-start(bf16[256,1536]{1,0:T(8,128)(2,1)} %get-tuple-element.115), channel_id=1, source_target_pairs={{1,0},{0,1},{3,2},{2,3},{5,4},{4,5},{7,6},{6,7},{9,8},{8,9},{11,10... | collective-permute-start | bytes 2359304 | tf_op jit(solution)/shard_map/ppermute | solution.py:674
  390.7 75.4 %collective-permute-start.40 = (bf16[256,1536]{1,0:T(8,128)(2,1)}, bf16[256,1536]{1,0:T(8,128)(2,1)S(1)}, u32[]{:S(2)}, u32[]{:S(2)}) collective-permute-start(bf16[256,1536]{1,0:T(8,128)(2,1)} %get-tuple-element.114), channel_id=1, source_target_pairs={{1,0},{0,1},{3,2},{2,3},{5,4},{4,5},{7,6},{6,7},{9,8},{8,9},{11,10... | collective-permute-start | bytes 2359304 | tf_op jit(solution)/shard_map/ppermute | solution.py:674
  397.4 15.1 %collective-permute-start.63 = (bf16[192,768]{1,0:T(8,128)(2,1)S(1)}, bf16[192,768]{1,0:T(8,128)(2,1)S(1)}, u32[]{:S(2)}, u32[]{:S(2)}) collective-permute-start(bf16[192,768]{1,0:T(8,128)(2,1)S(1)} %get-tuple-element.116), channel_id=1, source_target_pairs={{24,0},{28,4},{0,8},{4,12},{8,16},{12,20},{16,24},{20,28},{25,1},{... | collective-permute-start | bytes 884744 | tf_op jit(solution)/shard_map/ppermute | solution.py:661
  404.4 15.7 %collective-permute-start.65 = (bf16[192,768]{1,0:T(8,128)(2,1)S(1)}, bf16[192,768]{1,0:T(8,128)(2,1)S(1)}, u32[]{:S(2)}, u32[]{:S(2)}) collective-permute-start(bf16[192,768]{1,0:T(8,128)(2,1)S(1)} %get-tuple-element.118), channel_id=1, source_target_pairs={{16,0},{20,4},{24,8},{28,12},{0,16},{4,20},{8,24},{12,28},{17,1},{... | collective-permute-start | bytes 884744 | tf_op jit(solution)/shard_map/ppermute | solution.py:661
  407.7 22.5 %collective-permute-start.67 = (bf16[192,768]{1,0:T(8,128)(2,1)S(1)}, bf16[192,768]{1,0:T(8,128)(2,1)S(1)}, u32[]{:S(2)}, u32[]{:S(2)}) collective-permute-start(bf16[192,768]{1,0:T(8,128)(2,1)S(1)} %get-tuple-element.117), channel_id=1, source_target_pairs={{8,0},{12,4},{16,8},{20,12},{24,16},{28,20},{0,24},{4,28},{9,1},{1... | collective-permute-start | bytes 884744 | tf_op jit(solution)/shard_map/ppermute | solution.py:661
  412.6 23.2 %collective-permute-start.51 = (bf16[192,768]{1,0:T(8,128)(2,1)S(1)}, bf16[192,768]{1,0:T(8,128)(2,1)S(1)}, u32[]{:S(2)}, u32[]{:S(2)}) collective-permute-start(bf16[192,768]{1,0:T(8,128)(2,1)S(1)} %copy-done.25), channel_id=1, source_target_pairs={{4,0},{0,4},{12,8},{8,12},{20,16},{16,20},{28,24},{24,28},{5,1},{1... | collective-permute-start | bytes 884744 | tf_op jit(solution)/shard_map/ppermute | solution.py:670
  420.1 20.9 %collective-permute-start.46 = (bf16[192,768]{1,0:T(8,128)(2,1)S(1)}, bf16[192,768]{1,0:T(8,128)(2,1)S(1)}, u32[]{:S(2)}, u32[]{:S(2)}) collective-permute-start(bf16[192,768]{1,0:T(8,128)(2,1)S(1)} %get-tuple-element.125), channel_id=1, source_target_pairs={{24,0},{28,4},{0,8},{4,12},{8,16},{12,20},{16,24},{20,28},{25,1},{... | collective-permute-start | bytes 884744 | tf_op jit(solution)/shard_map/ppermute | solution.py:661
  430.1 22.6 %collective-permute-start.48 = (bf16[192,768]{1,0:T(8,128)(2,1)S(1)}, bf16[192,768]{1,0:T(8,128)(2,1)S(1)}, u32[]{:S(2)}, u32[]{:S(2)}) collective-permute-start(bf16[192,768]{1,0:T(8,128)(2,1)S(1)} %get-tuple-element.127), channel_id=1, source_target_pairs={{16,0},{20,4},{24,8},{28,12},{0,16},{4,20},{8,24},{12,28},{17,1},{... | collective-permute-start | bytes 884744 | tf_op jit(solution)/shard_map/ppermute | solution.py:661
  435.8 33.8 %collective-permute-start.58 = (bf16[192,768]{1,0:T(8,128)(2,1)S(1)}, bf16[192,768]{1,0:T(8,128)(2,1)S(1)}, u32[]{:S(2)}, u32[]{:S(2)}) collective-permute-start(bf16[192,768]{1,0:T(8,128)(2,1)S(1)} %copy-done.24), channel_id=1, source_target_pairs={{4,0},{0,4},{12,8},{8,12},{20,16},{16,20},{28,24},{24,28},{5,1},{1... | collective-permute-start | bytes 884744 | tf_op jit(solution)/shard_map/ppermute | solution.py:670
  441.0 26.8 %collective-permute-start.50 = (bf16[192,768]{1,0:T(8,128)(2,1)S(1)}, bf16[192,768]{1,0:T(8,128)(2,1)S(1)}, u32[]{:S(2)}, u32[]{:S(2)}) collective-permute-start(bf16[192,768]{1,0:T(8,128)(2,1)S(1)} %get-tuple-element.126), channel_id=1, source_target_pairs={{8,0},{12,4},{16,8},{20,12},{24,16},{28,20},{0,24},{4,28},{9,1},{1... | collective-permute-start | bytes 884744 | tf_op jit(solution)/shard_map/ppermute | solution.py:661
  452.8 17.6 %collective-permute-start.53 = (bf16[192,768]{1,0:T(8,128)(2,1)S(1)}, bf16[192,768]{1,0:T(8,128)(2,1)S(1)}, u32[]{:S(2)}, u32[]{:S(2)}) collective-permute-start(bf16[192,768]{1,0:T(8,128)(2,1)S(1)} %get-tuple-element.132), channel_id=1, source_target_pairs={{24,0},{28,4},{0,8},{4,12},{8,16},{12,20},{16,24},{20,28},{25,1},{... | collective-permute-start | bytes 884744 | tf_op jit(solution)/shard_map/ppermute | solution.py:661
  462.7 13.8 %collective-permute-start.55 = (bf16[192,768]{1,0:T(8,128)(2,1)S(1)}, bf16[192,768]{1,0:T(8,128)(2,1)S(1)}, u32[]{:S(2)}, u32[]{:S(2)}) collective-permute-start(bf16[192,768]{1,0:T(8,128)(2,1)S(1)} %get-tuple-element.134), channel_id=1, source_target_pairs={{16,0},{20,4},{24,8},{28,12},{0,16},{4,20},{8,24},{12,28},{17,1},{... | collective-permute-start | bytes 884744 | tf_op jit(solution)/shard_map/ppermute | solution.py:661
  466.0 10.5 %collective-permute-start.57 = (bf16[192,768]{1,0:T(8,128)(2,1)S(1)}, bf16[192,768]{1,0:T(8,128)(2,1)S(1)}, u32[]{:S(2)}, u32[]{:S(2)}) collective-permute-start(bf16[192,768]{1,0:T(8,128)(2,1)S(1)} %get-tuple-element.133), channel_id=1, source_target_pairs={{8,0},{12,4},{16,8},{20,12},{24,16},{28,20},{0,24},{4,28},{9,1},{1... | collective-permute-start | bytes 884744 | tf_op jit(solution)/shard_map/ppermute | solution.py:661
  467.8 13.1 %collective-permute-start.41 = (bf16[256,1536]{1,0:T(8,128)(2,1)}, bf16[256,1536]{1,0:T(8,128)(2,1)}, u32[]{:S(2)}, u32[]{:S(2)}) collective-permute-start(bf16[256,1536]{1,0:T(8,128)(2,1)} %get-tuple-element.112), channel_id=1, source_target_pairs={{2,0},{3,1},{0,2},{1,3},{6,4},{7,5},{4,6},{5,7},{10,8},{11,9},{8,1... | collective-permute-start | bytes 2359304 | tf_op jit(solution)/shard_map/ppermute | solution.py:674
  469.6 16.2 %collective-permute-start.34 = (bf16[1024,384]{1,0:T(8,128)(2,1)}, bf16[1024,384]{1,0:T(8,128)(2,1)}, u32[]{:S(2)}, u32[]{:S(2)}) collective-permute-start(bf16[1024,384]{1,0:T(8,128)(2,1)} %get-tuple-element.52), channel_id=1, source_target_pairs={{1,0},{0,1},{3,2},{2,3},{5,4},{4,5},{7,6},{6,7},{9,8},{8,9},{11,10... | collective-permute-start | bytes 2359304 | tf_op jit(solution)/shard_map/ppermute | solution.py:674
  470.3 45.7 %collective-permute-start.33 = (bf16[1024,384]{1,0:T(8,128)(2,1)}, bf16[1024,384]{1,0:T(8,128)(2,1)}, u32[]{:S(2)}, u32[]{:S(2)}) collective-permute-start(bf16[1024,384]{1,0:T(8,128)(2,1)} %get-tuple-element.50), channel_id=1, source_target_pairs={{1,0},{0,1},{3,2},{2,3},{5,4},{4,5},{7,6},{6,7},{9,8},{8,9},{11,10... | collective-permute-start | bytes 2359304 | tf_op jit(solution)/shard_map/ppermute | solution.py:674
  478.0 11.7 %collective-permute-start.60 = (f32[192,64]{0,1:T(8,128)S(1)}, f32[192,64]{0,1:T(8,128)S(1)}, u32[]{:S(2)}, u32[]{:S(2)}) collective-permute-start(f32[192,64]{0,1:T(8,128)S(1)} %copy.85), channel_id=1, source_target_pairs={{2,0},{3,1},{0,2},{1,3},{6,4},{7,5},{4,6},{5,7},{10,8},{11,9},{8,1... | collective-permute-start | bytes 147464 | tf_op jit(solution)/shard_map/ppermute | solution.py:674
  488.0 28.0 %collective-permute-start.35 = (bf16[1024,384]{1,0:T(8,128)(2,1)}, bf16[1024,384]{1,0:T(8,128)(2,1)}, u32[]{:S(2)}, u32[]{:S(2)}) collective-permute-start(bf16[1024,384]{1,0:T(8,128)(2,1)} %add_convert_fusion.1), channel_id=1, source_target_pairs={{2,0},{3,1},{0,2},{1,3},{6,4},{7,5},{4,6},{5,7},{10,8},{11,9},{8,1... | collective-permute-start | bytes 2359304 | tf_op jit(solution)/shard_map/ppermute | solution.py:674
  490.1 18.4 %collective-permute-start.70 = (f32[22,128]{1,0:T(8,128)S(1)}, f32[22,128]{1,0:T(8,128)S(1)}, u32[]{:S(2)}, u32[]{:S(2)}) collective-permute-start(f32[22,128]{1,0:T(8,128)S(1)} %fusion.56), channel_id=1, source_target_pairs={{2,0},{3,1},{0,2},{1,3},{6,4},{7,5},{4,6},{5,7},{10,8},{11,9},{8,1... | collective-permute-start | bytes 33800 | tf_op jit(solution)/shard_map/ppermute | solution.py:674
  511.1 19.3 %collective-permute-start.43 = (bf16[256,1536]{1,0:T(8,128)(2,1)}, bf16[256,1536]{1,0:T(8,128)(2,1)}, u32[]{:S(2)}, u32[]{:S(2)}) collective-permute-start(bf16[256,1536]{1,0:T(8,128)(2,1)} %get-tuple-element.62), channel_id=1, source_target_pairs={{2,0},{3,1},{0,2},{1,3},{6,4},{7,5},{4,6},{5,7},{10,8},{11,9},{8,1... | collective-permute-start | bytes 2359304 | tf_op jit(solution)/shard_map/ppermute | solution.py:674
  518.9 12.7 %collective-permute-start.42 = (bf16[256,1536]{1,0:T(8,128)(2,1)}, bf16[256,1536]{1,0:T(8,128)(2,1)}, u32[]{:S(2)}, u32[]{:S(2)}) collective-permute-start(bf16[256,1536]{1,0:T(8,128)(2,1)} %get-tuple-element.62), channel_id=1, source_target_pairs={{1,0},{0,1},{3,2},{2,3},{5,4},{4,5},{7,6},{6,7},{9,8},{8,9},{11,10... | collective-permute-start | bytes 2359304 | tf_op jit(solution)/shard_map/ppermute | solution.py:674
  (77 other events, 1073.1 us)
Sparse Core Ops, SparseCore 0:
  291.1 62.8 reduce-scatter.8
  380.9 74.0 reduce-scatter.6

commit v2 on v1

--- a/solution.py
+++ b/solution.py
@@ -372,131 +372,217 @@
     return (head == (jnp.arange(channels) // WIDTH)[None, :]).astype(bf16)
 
 
-def place_kernel(idx_ref, lhs_ref, *refs, widths, count):
-    groups = len(widths)
-    pieces = refs[: groups * count]
-    outs = refs[groups * count: groups * count + groups]
-    weights = refs[groups * count + groups:]
+TILE = 256
+TILE_D = 384
+
+
+def fill(dest, pieces, idx_ref):
+    for s, piece in enumerate(pieces):
+        rows = piece.shape[0]
+        dest[pl.ds(pl.multiple_of(idx_ref[s] * rows, rows), rows), :] = piece[...]
+
+
+def params():
+    return pltpu.CompilerParams(vmem_limit_bytes=VMEM_LIMIT)
+
+
+def cost(flops, moved):
+    return pl.CostEstimate(flops=int(flops), bytes_accessed=int(moved), transcendentals=0)
+
+
+def prepare_kernel(hidden_ref, gain_ref, cot_ref, low_ref, low_t_ref, cot_t_ref):
+    inputs = hidden_ref[...].astype(f32)
+    inv_rms = lax.rsqrt(jnp.mean(inputs * inputs, axis=1, keepdims=True) + EPSILON)
+    low = (inputs * inv_rms * gain_ref[0:1, :]).astype(bf16)
+    low_ref[...] = low
+    low_t_ref[...] = low.T
+    cot_t_ref[...] = cot_ref[...].T
+
+
+def prepare(hidden, gain_rows, cot):
+    tokens, depth = hidden.shape
+    block = pl.BlockSpec((TILE, depth), lambda i: (i, 0))
+    turned = pl.BlockSpec((depth, TILE), lambda i: (0, i))
+    return pl.pallas_call(
+        prepare_kernel,
+        grid=(tokens // TILE,),
+        in_specs=[block, pl.BlockSpec((8, depth), lambda i: (0, 0)), block],
+        out_specs=[block, turned, turned],
+        out_shape=[
+            jax.ShapeDtypeStruct((tokens, depth), bf16),
+            jax.ShapeDtypeStruct((depth, tokens), bf16),
+            jax.ShapeDtypeStruct((depth, tokens), bf16),
+        ],
+        compiler_params=params(),
+        name="prepare",
+    )(hidden, gain_rows, cot)
+
+
+def project_kernel(idx_ref, lhs_ref, *refs, count):
+    pieces, (x_ref, small_ref, w_ref) = refs[:count], refs[count:]
 
     @pl.when(pl.program_id(0) == 0)
     def _():
-        for g in range(groups):
-            for s in range(count):
-                piece = pieces[g * count + s]
-                rows = piece.shape[0]
-                weights[g][pl.ds(pl.multiple_of(idx_ref[s] * rows, rows), rows), :] = piece[...]
-
-    lhs = lhs_ref[...]
-    for g in range(groups):
-        outs[g][...] = dot_nn(lhs, weights[g][...])
-
-
-TILE = 256
-
-
-def project(lhs, groups, idx):
+        fill(w_ref, pieces, idx_ref)
+
+    product = dot_nn(lhs_ref[...], w_ref[...])
+    channels = x_ref.shape[1]
+    x_ref[...] = product[:, :channels]
+    small_ref[...] = product[:, channels:].T
+
+
+def project(lhs, pieces, idx, channels):
     tokens, depth = lhs.shape
-    count = len(groups[0])
-    widths = tuple(g[0].shape[1] for g in groups)
+    count, width = len(pieces), pieces[0].shape[1]
     whole = lambda i: (0, 0)
-    flat = [p for g in groups for p in g]
-    return pl.pallas_call(
-        functools.partial(place_kernel, widths=widths, count=count),
+    return pl.pallas_call(
+        functools.partial(project_kernel, count=count),
         grid=(tokens // TILE,),
         in_specs=[pl.BlockSpec(memory_space=pltpu.SMEM), pl.BlockSpec((TILE, depth), lambda i: (i, 0))]
-        + [pl.BlockSpec(p.shape, whole) for p in flat],
-        out_specs=[pl.BlockSpec((TILE, w), lambda i: (i, 0)) for w in widths]
-        + [pl.BlockSpec((depth, w), whole) for w in widths],
-        out_shape=[jax.ShapeDtypeStruct((tokens, w), f32) for w in widths]
-        + [jax.ShapeDtypeStruct((depth, w), bf16) for w in widths],
-        compiler_params=pltpu.CompilerParams(vmem_limit_bytes=VMEM_LIMIT),
-        cost_estimate=pl.CostEstimate(
-            flops=2 * tokens * depth * sum(widths), bytes_accessed=6 * depth * sum(widths), transcendentals=0
-        ),
+        + [pl.BlockSpec(p.shape, whole) for p in pieces],
+        out_specs=[
+            pl.BlockSpec((TILE, channels), lambda i: (i, 0)),
+            pl.BlockSpec((width - channels, TILE), lambda i: (0, i)),
+            pl.BlockSpec((depth, width), whole),
+        ],
+        out_shape=[
+            jax.ShapeDtypeStruct((tokens, channels), f32),
+            jax.ShapeDtypeStruct((width - channels, tokens), f32),
+            jax.ShapeDtypeStruct((depth, width), bf16),
+        ],
+        compiler_params=params(),
+        cost_estimate=cost(2 * tokens * depth * width, 6 * depth * width),
         name="project",
-    )(idx, lhs, *flat)
+    )(idx, lhs, *pieces)
 
 
 def column_to_row(col):
-    return jnp.broadcast_to(col, (col.shape[0], LANES)).T[0:1, :]
+    return jnp.broadcast_to(col, (col.shape[0], LANES)).T[0:8, :]
 
 
 def row_to_column(row):
     return jnp.broadcast_to(row, (LANES, row.shape[1])).T[:, 0:1]
 
 
-def gate_kernel(idx_ref, lhs_ref, cot_ref, mixed_ref, conv_ref, *refs, count):
-    gate_pieces, out_pieces = refs[:count], refs[count: 2 * count]
-    gate_ref, gout_ref, sums_ref, wg_ref, wo_ref = refs[2 * count:]
+def gate_kernel(idx_ref, lhs_ref, mixed_ref, *refs, count):
+    pieces, (gate_ref, sums_ref, w_ref) = refs[:count], refs[count:]
 
     @pl.when(pl.program_id(0) == 0)
     def _():
-        for dest, source in ((wg_ref, gate_pieces), (wo_ref, out_pieces)):
-            for s in range(count):
-                rows = source[s].shape[0]
-                dest[pl.ds(pl.multiple_of(idx_ref[s] * rows, rows), rows), :] = source[s][...]
-
-    gate = dot_nn(lhs_ref[...], wg_ref[...])
-    gout = dot_nn(cot_ref[...], wo_ref[...])
+        fill(w_ref, pieces, idx_ref)
+
+    gate = dot_nn(lhs_ref[...], w_ref[...])
     gate_ref[...] = gate
-    gout_ref[...] = gout
     gated = mixed_ref[...] * (gate * sigmoid(gate))
-    square = jnp.sum(gated * gated, axis=1, keepdims=True)
-    inner = jnp.sum(gout * conv_ref[5:6, :] * gated, axis=1, keepdims=True)
-    sums_ref[...] = jnp.concatenate(
-        [column_to_row(square), column_to_row(inner), jnp.zeros((6, square.shape[0]), f32)], axis=0
-    )
-
-
-def gate_forward(lhs, cot, mixed, conv_rows, gate_pieces, out_pieces, idx):
+    sums_ref[...] = column_to_row(jnp.sum(gated * gated, axis=1, keepdims=True))
+
+
+def gate_forward(lhs, mixed, pieces, idx):
     tokens, depth = lhs.shape
     channels = mixed.shape[1]
-    count = len(gate_pieces)
     whole = lambda i: (0, 0)
     now = lambda i: (i, 0)
     return pl.pallas_call(
-        functools.partial(gate_kernel, count=count),
+        functools.partial(gate_kernel, count=len(pieces)),
         grid=(tokens // TILE,),
         in_specs=[
             pl.BlockSpec(memory_space=pltpu.SMEM),
             pl.BlockSpec((TILE, depth), now),
+            pl.BlockSpec((TILE, channels), now),
+        ]
+        + [pl.BlockSpec(p.shape, whole) for p in pieces],
+        out_specs=[
+            pl.BlockSpec((TILE, channels), now),
+            pl.BlockSpec((8, TILE), lambda i: (0, i)),
+            pl.BlockSpec((depth, channels), whole),
+        ],
+        out_shape=[
+            jax.ShapeDtypeStruct((tokens, channels), f32),
+            jax.ShapeDtypeStruct((8, tokens), f32),
+            jax.ShapeDtypeStruct((depth, channels), bf16),
+        ],
+        compiler_params=params(),
+        cost_estimate=cost(2 * tokens * depth * channels, 8 * depth * channels),
+        name="gate_forward",
+    )(idx, lhs, mixed, *pieces)
+
+
+def gated_kernel(gate_ref, mixed_ref, square_ref, conv_ref, out_ref, *, inner_total):
+    gate = gate_ref[...]
+    scale = lax.rsqrt(row_to_column(square_ref[0:1, :]) / inner_total + EPSILON)
+    gated = mixed_ref[...] * (gate * sigmoid(gate))
+    out_ref[...] = (gated * scale * conv_ref[5:6, :]).astype(bf16)
+
+
+def gated_norm(gate, mixed, square, conv_rows, inner_total):
+    tokens, channels = gate.shape
+    block = pl.BlockSpec((TILE, channels), lambda i: (i, 0))
+    return pl.pallas_call(
+        functools.partial(gated_kernel, inner_total=inner_total),
+        grid=(tokens // TILE,),
+        in_specs=[block, block, pl.BlockSpec((8, TILE), lambda i: (0, i)), pl.BlockSpec((8, channels), lambda i: (0, 0))],
+        out_specs=block,
+        out_shape=jax.ShapeDtypeStruct((tokens, channels), bf16),
+        compiler_params=params(),
+        cost_estimate=cost(20 * tokens * channels, 10 * tokens * channels),
+        name="gated_norm",
+    )(gate, mixed, square, conv_rows)
+
+
+def gout_kernel(idx_ref, cot_ref, gate_ref, mixed_ref, conv_ref, *refs, count):
+    pieces, (gout_ref, sums_ref, w_ref) = refs[:count], refs[count:]
+
+    @pl.when(pl.program_id(0) == 0)
+    def _():
+        fill(w_ref, pieces, idx_ref)
+
+    gout = dot_nn(cot_ref[...], w_ref[...])
+    gout_ref[...] = gout
+    gate = gate_ref[...]
+    gated = mixed_ref[...] * (gate * sigmoid(gate))
+    sums_ref[...] = column_to_row(jnp.sum(gout * conv_ref[5:6, :] * gated, axis=1, keepdims=True))
+
+
+def grad_gout(cot, gate, mixed, conv_rows, pieces, idx):
+    tokens, depth = cot.shape
+    channels = mixed.shape[1]
+    whole = lambda i: (0, 0)
+    now = lambda i: (i, 0)
+    return pl.pallas_call(
+        functools.partial(gout_kernel, count=len(pieces)),
+        grid=(tokens // TILE,),
+        in_specs=[
+            pl.BlockSpec(memory_space=pltpu.SMEM),
             pl.BlockSpec((TILE, depth), now),
+            pl.BlockSpec((TILE, channels), now),
             pl.BlockSpec((TILE, channels), now),
             pl.BlockSpec((8, channels), whole),
         ]
-        + [pl.BlockSpec(p.shape, whole) for p in (*gate_pieces, *out_pieces)],
+        + [pl.BlockSpec(p.shape, whole) for p in pieces],
         out_specs=[
-            pl.BlockSpec((TILE, channels), now),
             pl.BlockSpec((TILE, channels), now),
             pl.BlockSpec((8, TILE), lambda i: (0, i)),
             pl.BlockSpec((depth, channels), whole),
-            pl.BlockSpec((depth, channels), whole),
         ],
         out_shape=[
-            jax.ShapeDtypeStruct((tokens, channels), f32),
             jax.ShapeDtypeStruct((tokens, channels), f32),
             jax.ShapeDtypeStruct((8, tokens), f32),
             jax.ShapeDtypeStruct((depth, channels), bf16),
-            jax.ShapeDtypeStruct((depth, channels), bf16),
-        ],
-        compiler_params=pltpu.CompilerParams(vmem_limit_bytes=VMEM_LIMIT),
-        cost_estimate=pl.CostEstimate(
-            flops=4 * tokens * depth * channels, bytes_accessed=8 * depth * channels, transcendentals=0
-        ),
-        name="gate_forward",
-    )(idx, lhs, cot, mixed, conv_rows, *gate_pieces, *out_pieces)
-
-
-def gate_back_kernel(gate_ref, gout_ref, mixed_ref, sums_ref, conv_ref, gated_out_ref, dmixed_ref, dgate_ref, dgain_ref, *, inner_total):
+        ],
+        compiler_params=params(),
+        cost_estimate=cost(2 * tokens * depth * channels, 8 * depth * channels),
+        name="grad_gout",
+    )(idx, cot, gate, mixed, conv_rows, *pieces)
+
+
+def gate_back_kernel(gate_ref, gout_ref, mixed_ref, square_ref, inner_ref, conv_ref, dmixed_ref, dgate_ref, dgain_ref, *, inner_total):
     gate, gout, mixed = gate_ref[...], gout_ref[...], mixed_ref[...]
     gain = conv_ref[5:6, :]
-    square, inner = row_to_column(sums_ref[0:1, :]), row_to_column(sums_ref[1:2, :])
+    square, inner = row_to_column(square_ref[0:1, :]), row_to_column(inner_ref[0:1, :])
     scale = lax.rsqrt(square / inner_total + EPSILON)
     sg = sigmoid(gate)
     act = gate * sg
     gated = mixed * act
-    normal = gated * scale
-    gated_out_ref[...] = (normal * gain).astype(bf16)
     dgated = scale * (gain * gout) - gated * (scale * scale * scale * inner / inner_total)
     dmixed_ref[...] = (dgated * act).astype(bf16)
     dgate_ref[...] = (dgated * mixed * sg * (1.0 + gate * (1.0 - sg))).astype(bf16)
@@ -505,117 +591,128 @@
     def _():
         dgain_ref[...] = jnp.zeros_like(dgain_ref)
 
-    dgain_ref[0:1, :] += jnp.sum(gout * normal, axis=0, keepdims=True)
-
-
-def gate_backward(gate, gout, mixed, sums, conv_rows, inner_total):
+    dgain_ref[0:1, :] += jnp.sum(gout * gated * scale, axis=0, keepdims=True)
+
+
+def gate_backward(gate, gout, mixed, square, inner, conv_rows, inner_total):
     tokens, channels = gate.shape
     whole = lambda i: (0, 0)
-    now = lambda i: (i, 0)
-    block = pl.BlockSpec((TILE, channels), now)
+    block = pl.BlockSpec((TILE, channels), lambda i: (i, 0))
+    row = pl.BlockSpec((8, TILE), lambda i: (0, i))
     return pl.pallas_call(
         functools.partial(gate_back_kernel, inner_total=inner_total),
         grid=(tokens // TILE,),
-        in_specs=[block, block, block, pl.BlockSpec((8, TILE), lambda i: (0, i)), pl.BlockSpec((8, channels), whole)],
-        out_specs=[block, block, block, pl.BlockSpec((8, channels), whole)],
+        in_specs=[block, block, block, row, row, pl.BlockSpec((8, channels), whole)],
+        out_specs=[block, block, pl.BlockSpec((8, channels), whole)],
         out_shape=[
             jax.ShapeDtypeStruct((tokens, channels), bf16),
             jax.ShapeDtypeStruct((tokens, channels), bf16),
-            jax.ShapeDtypeStruct((tokens, channels), bf16),
             jax.ShapeDtypeStruct((8, channels), f32),
         ],
-        compiler_params=pltpu.CompilerParams(vmem_limit_bytes=VMEM_LIMIT),
+        compiler_params=params(),
+        cost_estimate=cost(30 * tokens * channels, 16 * tokens * channels),
         name="gate_backward",
-    )(gate, gout, mixed, sums, conv_rows)
-
-
-def weight_grad_kernel(slot_ref, lhs_ref, rhs_ref, out_ref, *, rows):
-    per = TILE_D // rows
-    product = dot_tn(lhs_ref[...], rhs_ref[...])
-    for p in range(per):
-        block = pl.program_id(0) * per + p
-        out_ref[slot_ref[block]] = product[p * rows:(p + 1) * rows, :].astype(out_ref.dtype)
-
-
-TILE_D = 384
-
-
-def weight_grad(lhs, rhs, slots):
-    tokens, depth = lhs.shape
-    width = rhs.shape[1]
-    count = slots.shape[0]
+    )(gate, gout, mixed, square, inner, conv_rows)
+
+
+def weight_grad_kernel(idx_ref, lhs_ref, *refs, count, parts):
+    rhs, outs, scratch = refs[:parts], refs[parts:parts + count], refs[parts + count]
+    at = pl.program_id(0)
+    start = 0
+    for part in rhs:
+        width = part.shape[1]
+        scratch[pl.ds(pl.multiple_of(at * TILE_D, TILE_D), TILE_D), start:start + width] = dot_nn(lhs_ref[...], part[...]).astype(bf16)
+        start += width
+
+    @pl.when(at == pl.num_programs(0) - 1)
+    def _():
+        for s, out in enumerate(outs):
+            rows = out.shape[0]
+            out[...] = scratch[pl.ds(pl.multiple_of(idx_ref[s] * rows, rows), rows), :]
+
+
+def weight_grad(lhs_t, rhs, idx):
+    depth, tokens = lhs_t.shape
+    width = sum(r.shape[1] for r in rhs)
+    count = idx.shape[0]
     rows = depth // count
-    return pl.pallas_call(
-        functools.partial(weight_grad_kernel, rows=rows),
+    whole = lambda i: (0, 0)
+    return pl.pallas_call(
+        functools.partial(weight_grad_kernel, count=count, parts=len(rhs)),
         grid=(depth // TILE_D,),
-        in_specs=[
-            pl.BlockSpec(memory_space=pltpu.SMEM),
-            pl.BlockSpec((tokens, TILE_D), lambda i: (0, i)),
-            pl.BlockSpec((tokens, width), lambda i: (0, 0)),
-        ],
-        out_specs=pl.BlockSpec((count, rows, width), lambda i: (0, 0, 0)),
-        out_shape=jax.ShapeDtypeStruct((count, rows, width), bf16),
-        compiler_params=pltpu.CompilerParams(vmem_limit_bytes=VMEM_LIMIT),
-        cost_estimate=pl.CostEstimate(flops=2 * tokens * depth * width, bytes_accessed=4 * depth * width, transcendentals=0),
+        in_specs=[pl.BlockSpec(memory_space=pltpu.SMEM), pl.BlockSpec((TILE_D, tokens), lambda i: (i, 0))]
+        + [pl.BlockSpec(r.shape, whole) for r in rhs],
+        out_specs=[pl.BlockSpec((rows, width), whole)] * count,
+        out_shape=[jax.ShapeDtypeStruct((rows, width), bf16)] * count,
+        scratch_shapes=[pltpu.VMEM((depth, width), bf16)],
+        compiler_params=params(),
+        cost_estimate=cost(2 * tokens * depth * width, 4 * depth * width),
         name="weight_grad",
-    )(slots, lhs, rhs)
+    )(idx, lhs_t, *rhs)
 
 
 def out_kernel(rank_ref, lhs_ref, w_ref, *outs):
-    lhs = lhs_ref[...]
-    width = outs[0].shape[1]
+    product = dot_nt(lhs_ref[...], w_ref[...]).astype(bf16)
     for r, out in enumerate(outs):
-        start = pl.multiple_of((rank_ref[0] ^ r) * width, width)
-        out[...] = dot_nt(lhs, w_ref[pl.ds(start, width), :]).astype(out.dtype)
+        @pl.when(pl.program_id(0) == r)
+        def _():
+            out[...] = product
 
 
 def out_partial(gated_out, w_out, rank, ranks):
     tokens, channels = gated_out.shape
     depth = w_out.shape[0]
     width = depth // ranks
-    now = lambda i: (i, 0)
+    whole = lambda i, rank_ref: (0, 0)
     return pl.pallas_call(
         out_kernel,
-        grid=(tokens // TILE,),
-        in_specs=[
-            pl.BlockSpec(memory_space=pltpu.SMEM),
-            pl.BlockSpec((TILE, channels), now),
-            pl.BlockSpec((depth, channels), lambda i: (0, 0)),
-        ],
-        out_specs=[pl.BlockSpec((TILE, width), now)] * ranks,
+        grid_spec=pltpu.PrefetchScalarGridSpec(
+            num_scalar_prefetch=1,
+            grid=(ranks,),
+            in_specs=[
+                pl.BlockSpec((tokens, channels), whole),
+                pl.BlockSpec((width, channels), lambda i, rank_ref: (i ^ rank_ref[0], 0)),
+            ],
+            out_specs=[pl.BlockSpec((tokens, width), whole)] * ranks,
+        ),
         out_shape=[jax.ShapeDtypeStruct((tokens, width), bf16)] * ranks,
-        compiler_params=pltpu.CompilerParams(vmem_limit_bytes=VMEM_LIMIT),
-        cost_estimate=pl.CostEstimate(flops=2 * tokens * depth * channels, bytes_accessed=4 * depth * channels, transcendentals=0),
+        compiler_params=params(),
+        cost_estimate=cost(2 * tokens * depth * channels, 4 * depth * channels),
         name="out_partial",
     )(rank, gated_out, w_out)
 
 
-def term_kernel(rank_ref, gx_ref, wx_ref, gg_ref, wg_ref, gs_ref, ws_ref, gb_ref, wb_ref, out_ref):
-    total = dot_nt(gx_ref[...], wx_ref[...]) + dot_nt(gg_ref[...], wg_ref[...])
-    total = total + dot_nt(gs_ref[...], ws_ref[...]) + dot_nt(gb_ref[...], wb_ref[...])
-    out_ref[...] = total.astype(out_ref.dtype)
+def term_kernel(rank_ref, *refs, parts, ranks):
+    pairs, outs, scratch = refs[:2 * parts], refs[2 * parts:2 * parts + ranks], refs[2 * parts + ranks]
+    total = None
+    for p in range(parts):
+        product = dot_nt(pairs[2 * p][...], pairs[2 * p + 1][...])
+        total = product if total is None else total + product
+    scratch[...] = total.astype(bf16)
+    for r, out in enumerate(outs):
+        rows = out.shape[0]
+        out[...] = scratch[pl.ds(pl.multiple_of((rank_ref[0] ^ r) * rows, rows), rows), :]
 
 
 def normed_term(pairs, rank, ranks):
     tokens = pairs[0][0].shape[0]
     depth = pairs[0][1].shape[0]
     rows = tokens // ranks
-    specs, flat = [], []
+    specs, flat, inner = [], [], 0
     for g, w in pairs:
-        specs.append(pl.BlockSpec((rows, g.shape[1]), lambda i, rank_ref: (i ^ rank_ref[0], 0)))
-        specs.append(pl.BlockSpec(w.shape, lambda i, rank_ref: (0, 0)))
+        specs.append(pl.BlockSpec(g.shape, lambda i: (0, 0)))
+        specs.append(pl.BlockSpec((TILE_D, w.shape[1]), lambda i: (i, 0)))
         flat += [g, w]
-    return pl.pallas_call(
-        term_kernel,
-        grid_spec=pltpu.PrefetchScalarGridSpec(
-            num_scalar_prefetch=1,
-            grid=(ranks,),
-            in_specs=specs,
-            out_specs=pl.BlockSpec((None, rows, depth), lambda i, rank_ref: (i, 0, 0)),
-        ),
-        out_shape=jax.ShapeDtypeStruct((ranks, rows, depth), bf16),
-        compiler_params=pltpu.CompilerParams(vmem_limit_bytes=VMEM_LIMIT),
-        cost_estimate=pl.CostEstimate(flops=4 * tokens * depth * 800, bytes_accessed=8 * depth * 768, transcendentals=0),
+        inner += w.shape[1]
+    return pl.pallas_call(
+        functools.partial(term_kernel, parts=len(pairs), ranks=ranks),
+        grid=(depth // TILE_D,),
+        in_specs=[pl.BlockSpec(memory_space=pltpu.SMEM)] + specs,
+        out_specs=[pl.BlockSpec((rows, TILE_D), lambda i: (0, i))] * ranks,
+        out_shape=[jax.ShapeDtypeStruct((rows, depth), bf16)] * ranks,
+        scratch_shapes=[pltpu.VMEM((tokens, TILE_D), bf16)],
+        compiler_params=params(),
+        cost_estimate=cost(2 * tokens * depth * inner, 4 * depth * inner),
         name="normed_term",
     )(rank, *flat)
 
@@ -650,14 +747,17 @@
             out_specs=[pl.BlockSpec((rows, depth), whole), pl.BlockSpec((8, depth), whole)],
         ),
         out_shape=[jax.ShapeDtypeStruct((rows, depth), bf16), jax.ShapeDtypeStruct((8, depth), f32)],
-        compiler_params=pltpu.CompilerParams(vmem_limit_bytes=VMEM_LIMIT),
+        compiler_params=params(),
         name="norm_backward",
     )(rank, a, b, hidden, cot, gain_rows)
 
 
+def after(v, *done):
+    return lax.optimization_barrier((v, *done))[0]
+
+
 def outer_from(v, k):
-    size = lax.axis_size("dp")
-    n = size // 2
+    n = lax.axis_size("dp") // 2
     return lax.ppermute(v, "dp", [(((o + k) % n) * 2 + x, o * 2 + x) for o in range(n) for x in range(2)])
 
 
@@ -674,24 +774,38 @@
     return lax.ppermute(v, "mp", [(m ^ bit, m) for m in range(lax.axis_size("mp"))])
 
 
-def dp_pieces(piece):
+def hops(n):
+    order = []
+    for k in range(1, n // 2 + 1):
+        order.append(k)
+        if n - k != k:
+            order.append(n - k)
+    return order
+
+
+def dp_pieces(piece, ready=None):
     n = lax.axis_size("dp") // 2
-    found = []
-    for k in range(n):
-        here = piece if k == 0 else outer_from(piece, k)
-        found += [here, inner_flip(here)]
-    return found
-
-
-def dp_scatter(blocks):
+    found = [None] * (2 * n)
+    start = piece if ready is None else after(piece, ready)
+    arrived = {0: start}
+    for k in hops(n):
+        arrived[k] = outer_from(start, k)
+    for k in [0] + hops(n):
+        found[2 * k], found[2 * k + 1] = arrived[k], inner_flip(arrived[k])
+    return found, arrived[hops(n)[-1]]
+
+
+def dp_scatter(blocks, ready=None):
     n = lax.axis_size("dp") // 2
-    total = None
-    for k in list(range(1, n)) + [0]:
-        here = blocks[2 * k].astype(f32) + inner_flip(blocks[2 * k + 1]).astype(f32)
+    total, last = None, ready
+    for k in hops(n)[::-1] + [0]:
+        send = blocks[2 * k + 1] if last is None else after(blocks[2 * k + 1], last)
+        last = inner_flip(send)
+        here = blocks[2 * k].astype(f32) + last.astype(f32)
         if k > 0:
-            here = outer_from(here.astype(bf16), -k).astype(f32)
+            here = outer_from(here.astype(bf16), n - k).astype(f32)
         total = here if total is None else total + here
-    return total
+    return total, last
 
 
 def dp_sum(v):
@@ -708,9 +822,13 @@
     return v + rank_flip(v, 2)
 
 
+def mp_sum_direct(v):
+    return (v + rank_flip(v, 1)) + (rank_flip(v, 2) + rank_flip(v, 3))
+
+
 def mp_reduce(blocks):
+    far = blocks[2].astype(f32) + rank_flip(blocks[3], 1).astype(f32)
     near = blocks[0].astype(f32) + rank_flip(blocks[1], 1).astype(f32)
-    far = blocks[2].astype(f32) + rank_flip(blocks[3], 1).astype(f32)
     return near, rank_flip(far.astype(bf16), 2)
 
 
@@ -750,43 +868,43 @@
     outer, inner = place // 2, place % 2
     slot = jnp.arange(size)
     idx = (((outer + slot // 2) % n) * 2 + (inner ^ (slot % 2))).astype(jnp.int32)
-    slots = ((((slot // 2) - outer) % n) * 2 + (inner ^ (slot % 2))).astype(jnp.int32)
     rank1 = rank.reshape(1).astype(jnp.int32)
-    channels = in_weight.shape[2]
+    rows, _, channels = in_weight.shape
     heads = head_table.shape[1]
     tokens, depth = hidden.shape
-
-    x_pieces = dp_pieces(in_weight[:, 1].astype(bf16))
-    bc_pieces = dp_pieces(bc_weight.astype(bf16))
-    gate_pieces = dp_pieces(in_weight[:, 0].astype(bf16))
-    out_pieces = dp_pieces(out_weight.T.astype(bf16))
-    w_step = lax.all_gather(step_weight.astype(bf16), "dp", axis=0, tiled=True)
-    w_step = pad_lanes(w_step)
+    share = bc_weight.shape[1] // ranks
+    spare = LANES - share - heads
+
+    own_bc = lax.dynamic_slice_in_dim(bc_weight, rank * share, share, 1)
+    set_a = jnp.concatenate([in_weight[:, 1], own_bc, step_weight, jnp.zeros((rows, spare), f32)], axis=1)
+    a_pieces, a_last = dp_pieces(set_a.astype(bf16))
+    b_pieces, b_last = dp_pieces(in_weight[:, 0].astype(bf16), a_last)
+    c_pieces, _ = dp_pieces(out_weight.T.astype(bf16), b_last)
     cot = in_rank_order(mp_pieces(cotangent), rank, 1)
 
-    inputs = hidden.astype(f32)
-    inv_rms = lax.rsqrt(jnp.mean(inputs * inputs, axis=-1, keepdims=True) + EPSILON)
-    normed_low = (inputs * inv_rms * norm_gain).astype(bf16)
+    gain_rows = pad_rows(norm_gain[None])
+    normed_low, normed_t, cot_t = prepare(hidden, gain_rows, cot)
     aux, seg_row = segment_facts(segments)
     conv_rows, bc_rows = pad_rows(conv_table), pad_rows(bc_table)
     head_rows = pad_lanes(pad_rows(head_table))
     expand = head_expand(channels)
 
-    x_pre, bc_pre, w_x, w_bc = project(normed_low, [x_pieces, bc_pieces], idx)
-    step_pre = dot_nn(normed_low, w_step)
+    x_pre, small, w_a = project(normed_low, a_pieces, idx, channels)
+    bc_pre = in_rank_order(mp_pieces(small[:share].astype(bf16)), rank, 0).T.astype(f32)
+    step_pre = pad_lanes(small[share:share + heads].T)
     facts = (aux, seg_row, conv_rows, bc_rows, head_rows, expand)
     mixed, states = ssd_forward(x_pre, bc_pre, step_pre, *facts)
-    gate_pre, gout, sums, w_gate, w_out = gate_forward(
-        normed_low, cot, mixed, conv_rows, gate_pieces, out_pieces, idx
-    )
-    sums = mp_sum(sums)
-    gated_out, dmixed, dgate, dgain = gate_backward(gate_pre, gout, mixed, sums, conv_rows, channels * ranks)
-
-    grad_out = weight_grad(cot, gated_out, slots)
-    grad_gate = weight_grad(normed_low, dgate, slots)
-    shard_out = dp_scatter(grad_out)
-    shard_gate = dp_scatter(grad_gate)
-    near, far = mp_reduce(out_partial(gated_out, w_out, rank1, ranks))
+    gate_pre, square, w_b = gate_forward(normed_low, mixed, b_pieces, idx)
+    square = mp_sum_direct(square)
+    gated_out = gated_norm(gate_pre, mixed, square, conv_rows, channels * ranks)
+    shard_c, c_flip = dp_scatter(weight_grad(cot_t, [gated_out], idx))
+
+    gout, inner_dot, w_c = grad_gout(cot, gate_pre, mixed, conv_rows, c_pieces, idx)
+    inner_dot = mp_sum_direct(inner_dot)
+    dmixed, dgate, dgain = gate_backward(gate_pre, gout, mixed, square, inner_dot, conv_rows, channels * ranks)
+    shard_b, b_flip = dp_scatter(weight_grad(normed_t, [dgate], idx), c_flip)
+
+    near, far = mp_reduce(out_partial(gated_out, w_c, rank1, ranks))
     width = depth // ranks
     resid = lax.dynamic_slice_in_dim(hidden, rank * width, width, 1).astype(f32)
     output = (resid + near + far.astype(f32)).astype(bf16)
@@ -794,43 +912,37 @@
     dx, dbc_part, dstep, dconv, dbct_part, dheads = ssd_backward(
         x_pre, bc_pre, step_pre, *facts, mixed, dmixed, states
     )
-    grad_x = weight_grad(normed_low, dx, slots)
-    shard_x = dp_scatter(grad_x)
-    dstep_low = dstep.astype(bf16)
-    grad_step = dot_tn(normed_low, dstep_low[:, :heads])
-    shard_step = lax.psum_scatter(grad_step, "dp", scatter_dimension=0, tiled=True)
-
-    share = dbc_part.shape[1] // ranks
-    dbc_low_part = dbc_part.astype(bf16)
-    parts = [lax.dynamic_slice_in_dim(dbc_low_part, (rank ^ r) * share, share, 1) for r in range(ranks)]
+    dbc_low_part = dbc_part.astype(bf16).T
+    parts = [lax.dynamic_slice_in_dim(dbc_low_part, (rank ^ r) * share, share, 0) for r in range(ranks)]
     near, far = mp_reduce(parts)
-    dbc_low = (near + far.astype(f32)).astype(bf16)
-    wb_share = lax.dynamic_slice_in_dim(w_bc, rank * share, share, 1)
-    grad_bc = dot_tn(normed_low, dbc_low)
-    shard_bc_mine = lax.psum_scatter(grad_bc, "dp", scatter_dimension=0, tiled=True)
-    shard_bc = in_rank_order(mp_pieces(shard_bc_mine), rank, 1)
-
-    term = normed_term([(dx, w_x), (dgate, w_gate), (dstep_low, w_step), (dbc_low, wb_share)], rank1, ranks)
-    near, far = mp_reduce([term[r] for r in range(ranks)])
-    mine, dgain_mine = norm_backward(near, far, hidden, cot, pad_rows(norm_gain[None]), rank1)
+    dbc_low = (near + far.astype(f32)).astype(bf16).T
+    dsmall = jnp.concatenate([dbc_low, dstep[:, :heads].astype(bf16), jnp.zeros((tokens, spare), bf16)], axis=1)
+    shard_a, _ = dp_scatter(weight_grad(normed_t, [dx, dsmall], idx), b_flip)
+
+    term = normed_term([(dx, w_a[:, :channels]), (dsmall, w_a[:, channels:]), (dgate, w_b)], rank1, ranks)
+    near, far = mp_reduce(term)
+    mine, dgain_mine = norm_backward(near, far, hidden, cot, gain_rows, rank1)
     input_grad = in_rank_order(mp_pieces(mine), rank, 0)
 
     dconv_all = jnp.concatenate([dconv[:5], dgain[:1]], axis=0)
-    shared = mp_sum(jnp.concatenate([dbct_part[:5].reshape(-1, LANES), dgain_mine[:1].reshape(-1, LANES)], axis=0))
-    packed = jnp.concatenate([shared, dconv_all.reshape(-1, LANES), dheads], axis=0)
+    packed = jnp.concatenate(
+        [mp_sum(dbct_part[:5].reshape(-1, LANES)), dconv_all.reshape(-1, LANES), dheads], axis=0
+    )
     packed = dp_sum(packed)
     cut1 = 5 * 2
-    cut2 = cut1 + depth // LANES
-    cut3 = cut2 + 6 * channels // LANES
+    cut2 = cut1 + 6 * channels // LANES
     total_bct = packed[:cut1].reshape(5, 2 * LANES)
-    total_gain = packed[cut1:cut2].reshape(-1)
-    total_conv = packed[cut2:cut3].reshape(6, channels)
-    total_head = packed[cut3:cut3 + 3, :heads]
-
-    in_m, in_w = advance(in_weight, in_moment, jnp.stack([shard_gate, shard_x], axis=1))
+    total_conv = packed[cut1:cut2].reshape(6, channels)
+    total_head = packed[cut2:cut2 + 3, :heads]
+    total_gain = dp_sum(mp_sum(dgain_mine[:1].reshape(-1, LANES))).reshape(-1)
+
+    shard_x = shard_a[:, :channels]
+    shard_bc = in_rank_order(mp_pieces(shard_a[:, channels:channels + share]), rank, 1)
+    shard_step = shard_a[:, channels + share:channels + share + heads]
+    in_m, in_w = advance(in_weight, in_moment, jnp.stack([shard_b, shard_x], axis=1))
     bc_m, bc_w = advance(bc_weight, bc_moment, shard_bc)
     step_m, step_w = advance(step_weight, step_moment, shard_step)
-    out_m, out_w = advance(out_weight, out_moment, shard_out.T)
+    out_m, out_w = advance(out_weight, out_moment, shard_c.T)
     return (
         output, input_grad, in_m, in_w, bc_m, bc_w, step_m, step_w, out_m, out_w,
         momentum(conv_moment, total_conv),

time: 547 us -> 468 us (0.86)
  blocking collectives: 32 us -> 0 us
  waiting for transfers between devices: 197 us -> 170 us
  starting transfers between devices: 101 us -> 77.4 us
  Pallas kernels: 113 us -> 132 us
  between operations: 14.9 us -> 2.2 us
  other arithmetic: 30.9 us -> 24.5 us
  matrix products: 5.61 us -> 0 us
    unnamed x3 -> x0, waiting for transfers between devices: 52.6 us -> none
    all_gather x1 -> x0, blocking collectives: 32 us -> none  [body(): w_step = lax.all_gather(step_weight.astype(bf16), 'dp', axis=0, tiled=True)]
    ppermute x22 -> x31, waiting for transfers between devices: 17 us -> 48.1 us  [rank_flip(): lax.ppermute(v, 'mp', [(m ^ bit, m) for m in range(lax.axis_size('mp'))])]
    ppermute x21 -> x18, starting transfers between devices: 49.9 us -> 27.6 us  [outer_from(): lax.ppermute(v, 'dp', [((o + k) % n * 2 + x, o * 2 + x) for o in range(n)...]
    pallas_call x7 -> x10, Pallas kernels: 59.9 us -> 79.6 us  [the longest x3 21.5 us: weight_grad(): pl.pallas_call(functools.partial(weight_grad_kernel, count=count, parts=l...]
    ppermute x21 -> x18, waiting for transfers between devices: 67.2 us -> 54.9 us  [outer_from(): lax.ppermute(v, 'dp', [((o + k) % n * 2 + x, o * 2 + x) for o in range(n)...]
    squeeze x4 -> x0, local copies, waits for them, and re-layouts: 9.49 us -> none  [the longest x3 6.78 us: dp_scatter(): here = blocks[2 * k].astype(f32) + inner_flip(blocks[2 * k + 1]).astype(f32)]
    ppermute x29 -> x26, starting transfers between devices: 33.5 us -> 25.3 us  [inner_flip(): lax.ppermute(v, 'dp', [(d ^ 1, d) for d in range(lax.axis_size('dp'))])]
  transfers between devices with their start and end apart: 76 -> 79, of which waited for: 30 -> 26; matrix products, arithmetic and copies ran while one was open for 14% -> 14% of each run, Pallas kernels for 12% -> 15%
where the time goes in v2:
time: 468 us; the launch traced here: 460 us
  waiting for transfers between devices  170 us (36%)
  Pallas kernels  132 us (28%)
  starting transfers between devices  77.4 us (17%)
  local copies, waits for them, and re-layouts  54.1 us (12%)
  other arithmetic  24.5 us (5%)
    ppermute x26, waiting for transfers between devices, inner_flip(): lax.ppermute(v, 'dp', [(d ^ 1, d) for d in range(lax.axis_size('dp'))])  61 us
    ppermute x18, waiting for transfers between devices, outer_from(): lax.ppermute(v, 'dp', [((o + k) % n * 2 + x, o * 2 + x) for o in range(n)...  54.9 us
    ppermute x31, waiting for transfers between devices, rank_flip(): lax.ppermute(v, 'mp', [(m ^ bit, m) for m in range(lax.axis_size('mp'))])  48.1 us
    ppermute x18, starting transfers between devices, outer_from(): lax.ppermute(v, 'dp', [((o + k) % n * 2 + x, o * 2 + x) for o in range(n)...  27.6 us
    pallas_call x1, Pallas kernels, ssd_backward(): pl.pallas_call(ssd_backward_kernel, grid=(count,), in_specs=common_specs(...  27.6 us
    ppermute x26, starting transfers between devices, inner_flip(): lax.ppermute(v, 'dp', [(d ^ 1, d) for d in range(lax.axis_size('dp'))])  25.3 us
    pallas_call x3, Pallas kernels, weight_grad(): pl.pallas_call(functools.partial(weight_grad_kernel, count=count, parts=l...  21.5 us
    dynamic_update_slice x16, local copies, waits for them, and re-layouts, in_rank_order(): lax.dynamic_update_slice_in_dim(full, piece, (rank ^ r) * width, axis)  21 us
  transfers between devices with their start and end apart: 79, of which 26 were waited for; matrix products, arithmetic and copies ran while one was open for 14% of the time, Pallas kernels for 15%

profile of v2, /device:TPU:0, one launch (start us, length us, event | category | flops | bytes accessed | tf_op | source)
XLA Modules:
  0.0 460.4 jit_solution(13942778891640617684)
XLA Ops:
  1.2 2.6 collective-permute-start.1
  8.4 3.7 collective-permute-start.4
  15.4 6.9 %collective-permute-done.1 = bf16[1024,384]{1,0:T(8,128)(2,1)} collective-permute-done((bf16[1024,384]{1,0:T(8,128)(2,1)}, bf16[1024,384]{1,0:T(8,128)(2,1)}, u32[]{:S(2)}, u32[]{:S(2)}) %collective-permute-start.1) | collective-permute-done | bytes 786464 | tf_op jit(solution)/shard_map/ppermute | solution.py:774
  24.8 17.0 %collective-permute-done.6.refs_4_ = bf16[192,896]{1,0:T(8,128)(2,1)} collective-permute-done((bf16[192,896]{1,0:T(8,128)(2,1)S(1)}, bf16[192,896]{1,0:T(8,128)(2,1)}, u32[]{:S(2)}, u32[]{:S(2)}) %collective-permute-start.6) | collective-permute-done | bytes 344096 | tf_op jit(solution)/shard_map/ppermute | solution.py:761
  49.9 1.7 copy-done
  51.5 7.3 %prepare.1 = (bf16[1024,1536]{1,0:T(8,128)(2,1)}, bf16[1536,1024]{1,0:T(8,128)(2,1)}, bf16[1536,1024]{1,0:T(8,128)(2,1)}) custom-call(bf16[1024,1536]{1,0:T(8,128)(2,1)} %hidden_ref.3, f32[8,1536]{1,0:T(8,128)} %pad.52.gain_ref, bf16[1024,1536]{1,0:T(8,128)(2,1)} %copy-done), custom_call_target="tpu_custom_call" | custom-call | tf_op jit(solution)/shard_map/prepare/pallas_call | solution.py:406
  59.7 7.8 %collective-permute-done.5.refs_3_ = bf16[192,896]{1,0:T(8,128)(2,1)S(1)} collective-permute-done((bf16[192,896]{1,0:T(8,128)(2,1)}, bf16[192,896]{1,0:T(8,128)(2,1)S(1)}, u32[]{:S(2)}, u32[]{:S(2)}) %collective-permute-start.5) | collective-permute-done | bytes 344096 | tf_op jit(solution)/shard_map/ppermute | solution.py:770
  67.8 5.5 %collective-permute-done.9.refs_7_ = bf16[192,896]{1,0:T(8,128)(2,1)S(1)} collective-permute-done((bf16[192,896]{1,0:T(8,128)(2,1)}, bf16[192,896]{1,0:T(8,128)(2,1)S(1)}, u32[]{:S(2)}, u32[]{:S(2)}) %collective-permute-start.9) | collective-permute-done | bytes 344096 | tf_op jit(solution)/shard_map/ppermute | solution.py:770
  74.0 8.6 %project.1 = (f32[1024,768]{1,0:T(8,128)}, f32[128,1024]{1,0:T(8,128)}, bf16[1536,896]{1,0:T(8,128)(2,1)}) custom-call(s32[8]{0:T(128)} %fusion.17.idx_ref, bf16[1024,1536]{1,0:T(8,128)(2,1)} %get-tuple-element.84.lhs_ref, bf16[192,896]{1,0:T(8,128)(2,1)} %copy-done.20, bf16[192,896]{1,0:T(8,128)(2,1)} %copy-done.61, ...), custom_call_target="tpu_custom_call" | custom-call | flops 2818572288 | bytes 8257536 | tf_op jit(solution)/shard_map/project/pallas_call | solution.py:438
  84.7 1.6 collective-permute-start.13
  88.8 3.8 collective-permute-done.11
  99.4 2.0 dynamic_update_slice.53
  102.4 1.8 dynamic_update_slice.55
  105.3 13.5 %ssd_forward.1 = (f32[1024,768]{1,0:T(8,128)}, bf16[8,128,768]{2,1,0:T(8,128)(2,1)}) custom-call(f32[1024,768]{1,0:T(8,128)} %get-tuple-element.85.x_ref.xb_ref, f32[1024,768]{1,0:T(8,128)} %get-tuple-element.85.x_ref.xb_ref, f32[1024,256]{1,0:T(8,128)} %convert_bitcast_fusion.bc_ref.bcb_ref, f32[1024,256]{1,0:T(8,128)} %convert_bitcast_fusion.bc_ref.bcb_ref, ...), custom_call_target="tpu_custom_call" | custom-call | tf_op jit(solution)/shard_map/ssd_forward/pallas_call | solution.py:280
  119.7 8.5 %gate_forward.1 = (f32[1024,768]{1,0:T(8,128)}, f32[8,1024]{1,0:T(8,128)}, bf16[1536,768]{1,0:T(8,128)(2,1)}) custom-call(s32[8]{0:T(128)} %fusion.17.idx_ref, bf16[1024,1536]{1,0:T(8,128)(2,1)} %get-tuple-element.84.lhs_ref, f32[1024,768]{1,0:T(8,128)} %get-tuple-element.87.mixed_ref, bf16[192,768]{1,0:T(8,128)(2,1)} %get-tuple-element.88.refs_0_, ...), custom_call_target="tpu_custom_call" | custom-call | flops 2415919104 | bytes 9437184 | tf_op jit(solution)/shard_map/gate_forward/pallas_call | solution.py:485
  130.4 2.3 collective-permute-done.21
  134.0 5.4 %gated_norm.1.lhs_ref.refs_0_ = bf16[1024,768]{1,0:T(8,128)(2,1)} custom-call(f32[1024,768]{1,0:T(8,128)} %get-tuple-element.89.gate_ref, f32[1024,768]{1,0:T(8,128)} %get-tuple-element.87.mixed_ref, f32[8,1024]{1,0:T(8,128)} %add_add_fusion.2.square_ref, f32[8,768]{1,0:T(8,128)} %pad.61.conv_ref), custom_call_target="tpu_custom_call" | custom-call | flops 15728640 | bytes 7864320 | tf_op jit(solution)/shard_map/gated_norm/pallas_call | solution.py:520
  139.5 6.8 %weight_grad.4 = (bf16[192,768]{1,0:T(8,128)(2,1)}, bf16[192,768]{1,0:T(8,128)(2,1)}, bf16[192,768]{1,0:T(8,128)(2,1)}, bf16[192,768]{1,0:T(8,128)(2,1)}, bf16[1...) custom-call(s32[8]{0:T(128)} %fusion.17.idx_ref, ...), custom_call_target="tpu_custom_call" | custom-call | flops 2415919104 | bytes 4718592 | tf_op jit(solution)/shard_map/weight_grad/pallas_call | solution.py:640
  147.9 7.8 %collective-permute-done.45 = bf16[192,768]{1,0:T(8,128)(2,1)S(1)} collective-permute-done((bf16[192,768]{1,0:T(8,128)(2,1)}, bf16[192,768]{1,0:T(8,128)(2,1)S(1)}, u32[]{:S(2)}, u32[]{:S(2)}) %collective-permute-start.45) | collective-permute-done | bytes 294944 | tf_op jit(solution)/shard_map/ppermute | solution.py:770
  157.2 7.0 %collective-permute-done.46 = bf16[192,768]{1,0:T(8,128)(2,1)S(1)} collective-permute-done((bf16[192,768]{1,0:T(8,128)(2,1)}, bf16[192,768]{1,0:T(8,128)(2,1)S(1)}, u32[]{:S(2)}, u32[]{:S(2)}) %collective-permute-start.46) | collective-permute-done | bytes 294944 | tf_op jit(solution)/shard_map/ppermute | solution.py:770
  167.9 3.8 collective-permute-done.47
  173.3 10.6 %collective-permute-done.66 = bf16[192,768]{1,0:T(8,128)(2,1)S(1)} collective-permute-done((bf16[192,768]{1,0:T(8,128)(2,1)S(1)}, bf16[192,768]{1,0:T(8,128)(2,1)S(1)}, u32[]{:S(2)}, u32[]{:S(2)}) %collective-permute-start.66) | collective-permute-done | bytes 294944 | tf_op jit(solution)/shard_map/ppermute | solution.py:761
  184.0 3.6 collective-permute-done.67
  190.0 12.5 %collective-permute-start.26 = (bf16[192,768]{1,0:T(8,128)(2,1)S(1)}, bf16[192,768]{1,0:T(8,128)(2,1)S(1)}, u32[]{:S(2)}, u32[]{:S(2)}) collective-permute-start(bf16[192,768]{1,0:T(8,128)(2,1)S(1)} %get-tuple-element.91.refs_0_), channel_id=1, source_target_pairs={{16,0},{20,4},{24,8},{28,12},{0,16},{4,20},{8,24},{12,28},{17,1},{... | collective-permute-start | bytes 884744 | tf_op jit(solution)/shard_map/ppermute | solution.py:761
  202.5 2.0 collective-permute-start.28
  204.5 3.8 collective-permute-done.24.refs_2_
  208.2 9.7 %collective-permute-done.26.refs_4_ = bf16[192,768]{1,0:T(8,128)(2,1)S(1)} collective-permute-done((bf16[192,768]{1,0:T(8,128)(2,1)S(1)}, bf16[192,768]{1,0:T(8,128)(2,1)S(1)}, u32[]{:S(2)}, u32[]{:S(2)}) %collective-permute-start.26) | collective-permute-done | bytes 294944 | tf_op jit(solution)/shard_map/ppermute | solution.py:761
  218.4 1.6 collective-permute-start.29
  220.0 7.1 %collective-permute-done.27.refs_5_ = bf16[192,768]{1,0:T(8,128)(2,1)S(1)} collective-permute-done((bf16[192,768]{1,0:T(8,128)(2,1)S(1)}, bf16[192,768]{1,0:T(8,128)(2,1)S(1)}, u32[]{:S(2)}, u32[]{:S(2)}) %collective-permute-start.27) | collective-permute-done | bytes 294944 | tf_op jit(solution)/shard_map/ppermute | solution.py:770
  227.1 3.2 collective-permute-done.29.refs_7_
  231.0 8.7 %grad_gout.1 = (f32[1024,768]{1,0:T(8,128)}, f32[8,1024]{1,0:T(8,128)}, bf16[1536,768]{1,0:T(8,128)(2,1)}) custom-call(s32[8]{0:T(128)} %fusion.17.idx_ref, bf16[1024,1536]{1,0:T(8,128)(2,1)} %copy-done, f32[1024,768]{1,0:T(8,128)} %get-tuple-element.89.gate_ref, f32[1024,768]{1,0:T(8,128)} %get-tuple-element.87.mixed_ref, f32[8,768]{1,0:T(8,128)} %pad.61.conv_ref, ...), custom_call_target="tpu_custom_call" | custom-call | flops 2415919104 | bytes 9437184 | tf_op jit(solution)/shard_map/grad_gout/pallas_call | solution.py:551
  239.7 1.6 collective-permute-start.34
  244.1 1.6 slice.116.refs_1_
  247.9 7.3 %gate_backward.1 = (bf16[1024,768]{1,0:T(8,128)(2,1)}, bf16[1024,768]{1,0:T(8,128)(2,1)}, f32[8,768]{1,0:T(8,128)}) custom-call(f32[1024,768]{1,0:T(8,128)} %get-tuple-element.89.gate_ref, f32[1024,768]{1,0:T(8,128)} %get-tuple-element.97.gout_ref, f32[1024,768]{1,0:T(8,128)} %get-tuple-element.87.mixed_ref, f32[8,1024]{1,0:T(8,128)} %add_add_fusion.2.square_ref, ...), custom_call_target="tpu_custom_call" | custom-call | flops 23592960 | bytes 12582912 | tf_op jit(solution)/shard_map/gate_backward/pallas_call | solution.py:602
  255.3 27.6 %ssd_backward.1 = (bf16[1024,768]{1,0:T(8,128)(2,1)}, f32[1024,256]{1,0:T(8,128)}, f32[1024,128]{1,0:T(8,128)}, f32[8,768]{1,0:T(8,128)}, f32[8,256]{1,0:T(8,128)}, /*index=5*/f32[8,128]{1,0:T(8,128)}) custom-call(f32[1024,768]{1,0:T(8,128)} %get-tuple-element.85.x_ref.xb_ref, f32[1024,768]{1,0:T(8,128)} %get-tuple-element.85.x_ref.xb_ref, ...), custom_call_target="tpu_custom_call" | custom-call | tf_op jit(solution)/shard_map/ssd_backward/pallas_call | solution.py:308
  285.1 1.6 collective-permute-start.70
  289.5 1.7 collective-permute-start.71
  291.3 7.8 %out_partial.1 = (bf16[1024,384]{1,0:T(8,128)(2,1)}, bf16[1024,384]{1,0:T(8,128)(2,1)}, bf16[1024,384]{1,0:T(8,128)(2,1)}, bf16[1024,384]{1,0:T(8,128)(2,1)}) custom-call(s32[1]{0:T(128)} %bitcast.rank_ref, bf16[1024,768]{1,0:T(8,128)(2,1)} %gated_norm.1.lhs_ref.refs_0_, bf16[1536,768]{1,0:T(8,128)(2,1)} %get-tuple-element.92.w_ref), custom_call_target="tpu_custom_call" | custom-call | flops 2415919104 | bytes 4718592 | tf_op jit(solution)/shard_map/out_partial/pallas_call | solution.py:667
  300.7 3.0 collective-permute-done.72
  304.4 6.9 %weight_grad.3 = (bf16[192,768]{1,0:T(8,128)(2,1)}, bf16[192,768]{1,0:T(8,128)(2,1)}, bf16[192,768]{1,0:T(8,128)(2,1)}, bf16[192,768]{1,0:T(8,128)(2,1)}, bf16[1...) custom-call(s32[8]{0:T(128)} %fusion.17.idx_ref, ...), custom_call_target="tpu_custom_call" | custom-call | flops 2415919104 | bytes 4718592 | tf_op jit(solution)/shard_map/weight_grad/pallas_call | solution.py:640
  314.2 4.7 %collective-permute-done.38 = bf16[64,1024]{0,1:T(8,128)(2,1)S(1)} collective-permute-done((bf16[64,1024]{0,1:T(8,128)(2,1)S(1)}, bf16[64,1024]{0,1:T(8,128)(2,1)S(1)}, u32[]{:S(2)}, u32[]{:S(2)}) %collective-permute-start.38) | collective-permute-done | bytes 131104 | tf_op jit(solution)/shard_map/ppermute | solution.py:774
  319.9 11.7 %normed_term.1 = (bf16[256,1536]{1,0:T(8,128)(2,1)}, bf16[256,1536]{1,0:T(8,128)(2,1)}, bf16[256,1536]{1,0:T(8,128)(2,1)}, bf16[256,1536]{1,0:T(8,128)(2,1)}) custom-call(s32[1]{0:T(128)} %bitcast.rank_ref, bf16[1024,768]{1,0:T(8,128)(2,1)} %get-tuple-element.101.refs_0_, bf16[1536,768]{1,0:T(8,128)(2,1)} %slice.116.refs_1_, ...), custom_call_target="tpu_custom_call" | custom-call | flops 5234491392 | bytes 10223616 | tf_op jit(solution)/shard_map/normed_term/pallas_call | solution.py:707
  332.3 1.8 collective-permute-start.51
  334.1 7.8 %weight_grad.5 = (bf16[192,896]{1,0:T(8,128)(2,1)}, bf16[192,896]{1,0:T(8,128)(2,1)}, bf16[192,896]{1,0:T(8,128)(2,1)}, bf16[192,896]{1,0:T(8,128)(2,1)}, bf16[1...) custom-call(s32[8]{0:T(128)} %fusion.17.idx_ref, ...), custom_call_target="tpu_custom_call" | custom-call | flops 2818572288 | bytes 5505024 | tf_op jit(solution)/shard_map/weight_grad/pallas_call | solution.py:640
  342.2 2.3 collective-permute-start.50
  345.9 7.6 %collective-permute-done.53 = bf16[192,768]{1,0:T(8,128)(2,1)S(1)} collective-permute-done((bf16[192,768]{1,0:T(8,128)(2,1)S(1)}, bf16[192,768]{1,0:T(8,128)(2,1)S(1)}, u32[]{:S(2)}, u32[]{:S(2)}) %collective-permute-start.53) | collective-permute-done | bytes 294944 | tf_op jit(solution)/shard_map/ppermute | solution.py:770
  357.0 15.1 %collective-permute-done.41.b_ref = bf16[256,1536]{1,0:T(8,128)(2,1)S(1)} collective-permute-done((bf16[256,1536]{1,0:T(8,128)(2,1)S(1)}, bf16[256,1536]{1,0:T(8,128)(2,1)S(1)}, u32[]{:S(2)}, u32[]{:S(2)}) %collective-permute-start.41) | collective-permute-done | bytes 786464 | tf_op jit(solution)/shard_map/ppermute | solution.py:774
  373.0 3.9 norm_backward.1
  381.3 8.7 %collective-permute-done.56 = bf16[192,896]{1,0:T(8,128)(2,1)S(1)} collective-permute-done((bf16[192,896]{1,0:T(8,128)(2,1)S(1)}, bf16[192,896]{1,0:T(8,128)(2,1)S(1)}, u32[]{:S(2)}, u32[]{:S(2)}) %collective-permute-start.56) | collective-permute-done | bytes 344096 | tf_op jit(solution)/shard_map/ppermute | solution.py:770
  390.4 8.0 %collective-permute-done.75 = f32[12,128]{1,0:T(8,128)S(1)} collective-permute-done((f32[12,128]{1,0:T(8,128)S(1)}, f32[12,128]{1,0:T(8,128)S(1)}, u32[]{:S(2)}, u32[]{:S(2)}) %collective-permute-start.75) | collective-permute-done | bytes 6176 | tf_op jit(solution)/shard_map/ppermute | solution.py:774
  399.6 2.5 collective-permute-done.76
  402.5 1.6 collective-permute-start.60
  404.2 2.5 add_convert_fusion.1
  406.7 3.2 collective-permute-start.78
  411.2 1.7 collective-permute-start.62
  415.3 3.4 collective-permute-done.78
  420.9 10.3 %collective-permute-done.59 = bf16[192,896]{1,0:T(8,128)(2,1)S(1)} collective-permute-done((bf16[192,896]{1,0:T(8,128)(2,1)S(1)}, bf16[192,896]{1,0:T(8,128)(2,1)S(1)}, u32[]{:S(2)}, u32[]{:S(2)}) %collective-permute-start.59) | collective-permute-done | bytes 344096 | tf_op jit(solution)/shard_map/ppermute | solution.py:761
  434.1 5.9 %collective-permute-done.43 = bf16[256,1536]{1,0:T(8,128)(2,1)} collective-permute-done((bf16[256,1536]{1,0:T(8,128)(2,1)}, bf16[256,1536]{1,0:T(8,128)(2,1)}, u32[]{:S(2)}, u32[]{:S(2)}) %collective-permute-start.43) | collective-permute-done | bytes 786464 | tf_op jit(solution)/shard_map/ppermute | solution.py:774
  440.8 1.9 copy.109
  442.7 1.9 copy.110
  448.3 1.7 dynamic_update_slice.61
  453.8 1.6 dynamic_update_slice.63
  455.4 1.7 multiply_subtract_fusion.2
  458.3 1.7 copy-done.2
  (372 shorter events, 98.0 us)
Async XLA Ops:
  0.6 44.7 %collective-permute-start = (bf16[1024,384]{1,0:T(8,128)(2,1)}, bf16[1024,384]{1,0:T(8,128)(2,1)}, u32[]{:S(2)}, u32[]{:S(2)}) collective-permute-start(bf16[1024,384]{1,0:T(8,128)(2,1)} %param.21), channel_id=1, source_target_pairs={{1,0},{0,1},{3,2},{2,3},{5,4},{4,5},{7,6},{6,7},{9,8},{8,9},{11,10... | collective-permute-start | bytes 2359304 | tf_op jit(solution)/shard_map/ppermute | solution.py:774
  1.2 21.0 %collective-permute-start.1 = (bf16[1024,384]{1,0:T(8,128)(2,1)}, bf16[1024,384]{1,0:T(8,128)(2,1)}, u32[]{:S(2)}, u32[]{:S(2)}) collective-permute-start(bf16[1024,384]{1,0:T(8,128)(2,1)} %param.21), channel_id=1, source_target_pairs={{2,0},{3,1},{0,2},{1,3},{6,4},{7,5},{4,6},{5,7},{10,8},{11,9},{8,1... | collective-permute-start | bytes 2359304 | tf_op jit(solution)/shard_map/ppermute | solution.py:774
  8.4 34.9 %collective-permute-start.4 = (bf16[192,896]{1,0:T(8,128)(2,1)S(1)}, bf16[192,896]{1,0:T(8,128)(2,1)}, u32[]{:S(2)}, u32[]{:S(2)}) collective-permute-start(bf16[192,896]{1,0:T(8,128)(2,1)S(1)} %maximum_maximum_fusion.refs_0_), channel_id=1, source_target_pairs={{8,0},{12,4},{16,8},{20,12},{24,16},{28,20},{0,24},{4,28},{9,1},{1... | collective-permute-start | bytes 1032200 | tf_op jit(solution)/shard_map/ppermute | solution.py:761
  12.1 29.8 %collective-permute-start.6 = (bf16[192,896]{1,0:T(8,128)(2,1)S(1)}, bf16[192,896]{1,0:T(8,128)(2,1)}, u32[]{:S(2)}, u32[]{:S(2)}) collective-permute-start(bf16[192,896]{1,0:T(8,128)(2,1)S(1)} %maximum_maximum_fusion.refs_0_), channel_id=1, source_target_pairs={{16,0},{20,4},{24,8},{28,12},{0,16},{4,20},{8,24},{12,28},{17,1},{... | collective-permute-start | bytes 1032200 | tf_op jit(solution)/shard_map/ppermute | solution.py:761
  12.1 31.8 %collective-permute-start.8 = (bf16[192,896]{1,0:T(8,128)(2,1)S(1)}, bf16[192,896]{1,0:T(8,128)(2,1)}, u32[]{:S(2)}, u32[]{:S(2)}) collective-permute-start(bf16[192,896]{1,0:T(8,128)(2,1)S(1)} %maximum_maximum_fusion.refs_0_), channel_id=1, source_target_pairs={{24,0},{28,4},{0,8},{4,12},{8,16},{12,20},{16,24},{20,28},{25,1},{... | collective-permute-start | bytes 1032200 | tf_op jit(solution)/shard_map/ppermute | solution.py:761
  22.2 26.3 %collective-permute-start.2 = (bf16[1024,384]{1,0:T(8,128)(2,1)}, bf16[1024,384]{1,0:T(8,128)(2,1)}, u32[]{:S(2)}, u32[]{:S(2)}) collective-permute-start(bf16[1024,384]{1,0:T(8,128)(2,1)} %collective-permute-done.1), channel_id=1, source_target_pairs={{1,0},{0,1},{3,2},{2,3},{5,4},{4,5},{7,6},{6,7},{9,8},{8,9},{11,10... | collective-permute-start | bytes 2359304 | tf_op jit(solution)/shard_map/ppermute | solution.py:774
  41.8 17.1 %collective-permute-start.3 = (bf16[192,896]{1,0:T(8,128)(2,1)S(1)}, bf16[192,896]{1,0:T(8,128)(2,1)S(1)}, u32[]{:S(2)}, u32[]{:S(2)}) collective-permute-start(bf16[192,896]{1,0:T(8,128)(2,1)S(1)} %maximum_maximum_fusion.refs_0_), channel_id=1, source_target_pairs={{4,0},{0,4},{12,8},{8,12},{20,16},{16,20},{28,24},{24,28},{5,1},{1... | collective-permute-start | bytes 1032200 | tf_op jit(solution)/shard_map/ppermute | solution.py:770
  43.3 24.4 %collective-permute-start.7 = (bf16[192,896]{1,0:T(8,128)(2,1)}, bf16[192,896]{1,0:T(8,128)(2,1)S(1)}, u32[]{:S(2)}, u32[]{:S(2)}) collective-permute-start(bf16[192,896]{1,0:T(8,128)(2,1)} %collective-permute-done.6.refs_4_), channel_id=1, source_target_pairs={{4,0},{0,4},{12,8},{8,12},{20,16},{16,20},{28,24},{24,28},{5,1},{1... | collective-permute-start | bytes 1032200 | tf_op jit(solution)/shard_map/ppermute | solution.py:770
  43.9 23.7 %collective-permute-start.5 = (bf16[192,896]{1,0:T(8,128)(2,1)}, bf16[192,896]{1,0:T(8,128)(2,1)S(1)}, u32[]{:S(2)}, u32[]{:S(2)}) collective-permute-start(bf16[192,896]{1,0:T(8,128)(2,1)} %collective-permute-done.4.refs_2_), channel_id=1, source_target_pairs={{4,0},{0,4},{12,8},{8,12},{20,16},{16,20},{28,24},{24,28},{5,1},{1... | collective-permute-start | bytes 1032200 | tf_op jit(solution)/shard_map/ppermute | solution.py:770
  45.3 27.9 %collective-permute-start.9 = (bf16[192,896]{1,0:T(8,128)(2,1)}, bf16[192,896]{1,0:T(8,128)(2,1)S(1)}, u32[]{:S(2)}, u32[]{:S(2)}) collective-permute-start(bf16[192,896]{1,0:T(8,128)(2,1)} %collective-permute-done.8.refs_6_), channel_id=1, source_target_pairs={{4,0},{0,4},{12,8},{8,12},{20,16},{16,20},{28,24},{24,28},{5,1},{1... | collective-permute-start | bytes 1032200 | tf_op jit(solution)/shard_map/ppermute | solution.py:770
  48.5 36.2 %collective-permute-start.14 = (bf16[192,768]{1,0:T(8,128)(2,1)}, bf16[192,768]{1,0:T(8,128)(2,1)}, u32[]{:S(2)}, u32[]{:S(2)}) collective-permute-start(bf16[192,768]{1,0:T(8,128)(2,1)} %get-tuple-element.88.refs_0_), channel_id=1, source_target_pairs={{8,0},{12,4},{16,8},{20,12},{24,16},{28,20},{0,24},{4,28},{9,1},{1... | collective-permute-start | bytes 884744 | tf_op jit(solution)/shard_map/ppermute | solution.py:761
  58.9 27.3 %collective-permute-start.16 = (bf16[192,768]{1,0:T(8,128)(2,1)}, bf16[192,768]{1,0:T(8,128)(2,1)S(1)}, u32[]{:S(2)}, u32[]{:S(2)}) collective-permute-start(bf16[192,768]{1,0:T(8,128)(2,1)} %get-tuple-element.88.refs_0_), channel_id=1, source_target_pairs={{16,0},{20,4},{24,8},{28,12},{0,16},{4,20},{8,24},{12,28},{17,1},{... | collective-permute-start | bytes 884744 | tf_op jit(solution)/shard_map/ppermute | solution.py:761
  67.6 19.2 %collective-permute-start.18 = (bf16[192,768]{1,0:T(8,128)(2,1)}, bf16[192,768]{1,0:T(8,128)(2,1)S(1)}, u32[]{:S(2)}, u32[]{:S(2)}) collective-permute-start(bf16[192,768]{1,0:T(8,128)(2,1)} %get-tuple-element.88.refs_0_), channel_id=1, source_target_pairs={{24,0},{28,4},{0,8},{4,12},{8,16},{12,20},{16,24},{20,28},{25,1},{... | collective-permute-start | bytes 884744 | tf_op jit(solution)/shard_map/ppermute | solution.py:761
  83.9 8.7 %collective-permute-start.11 = (bf16[64,1024]{0,1:T(8,128)(2,1)S(1)}, bf16[64,1024]{0,1:T(8,128)(2,1)S(1)}, u32[]{:S(2)}, u32[]{:S(2)}) collective-permute-start(bf16[64,1024]{0,1:T(8,128)(2,1)S(1)} %bitcast.71), channel_id=1, source_target_pairs={{2,0},{3,1},{0,2},{1,3},{6,4},{7,5},{4,6},{5,7},{10,8},{11,9},{8,1... | collective-permute-start | bytes 393224 | tf_op jit(solution)/shard_map/ppermute | solution.py:774
  84.7 34.2 %collective-permute-start.13 = (bf16[192,768]{1,0:T(8,128)(2,1)}, bf16[192,768]{1,0:T(8,128)(2,1)S(1)}, u32[]{:S(2)}, u32[]{:S(2)}) collective-permute-start(bf16[192,768]{1,0:T(8,128)(2,1)} %get-tuple-element.88.refs_0_), channel_id=1, source_target_pairs={{4,0},{0,4},{12,8},{8,12},{20,16},{16,20},{28,24},{24,28},{5,1},{1... | collective-permute-start | bytes 884744 | tf_op jit(solution)/shard_map/ppermute | solution.py:770
  86.2 32.6 %collective-permute-start.15 = (bf16[192,768]{1,0:T(8,128)(2,1)}, bf16[192,768]{1,0:T(8,128)(2,1)S(1)}, u32[]{:S(2)}, u32[]{:S(2)}) collective-permute-start(bf16[192,768]{1,0:T(8,128)(2,1)} %collective-permute-done.14.refs_2_), channel_id=1, source_target_pairs={{4,0},{0,4},{12,8},{8,12},{20,16},{16,20},{28,24},{24,28},{5,1},{1... | collective-permute-start | bytes 884744 | tf_op jit(solution)/shard_map/ppermute | solution.py:770
  86.8 32.1 %collective-permute-start.17 = (bf16[192,768]{1,0:T(8,128)(2,1)S(1)}, bf16[192,768]{1,0:T(8,128)(2,1)}, u32[]{:S(2)}, u32[]{:S(2)}) collective-permute-start(bf16[192,768]{1,0:T(8,128)(2,1)S(1)} %collective-permute-done.16.refs_4_), channel_id=1, source_target_pairs={{4,0},{0,4},{12,8},{8,12},{20,16},{16,20},{28,24},{24,28},{5,1},{1... | collective-permute-start | bytes 884744 | tf_op jit(solution)/shard_map/ppermute | solution.py:770
  88.3 30.6 %collective-permute-start.19 = (bf16[192,768]{1,0:T(8,128)(2,1)S(1)}, bf16[192,768]{1,0:T(8,128)(2,1)}, u32[]{:S(2)}, u32[]{:S(2)}) collective-permute-start(bf16[192,768]{1,0:T(8,128)(2,1)S(1)} %collective-permute-done.18.refs_6_), channel_id=1, source_target_pairs={{4,0},{0,4},{12,8},{8,12},{20,16},{16,20},{28,24},{24,28},{5,1},{1... | collective-permute-start | bytes 884744 | tf_op jit(solution)/shard_map/ppermute | solution.py:770
  92.7 9.7 %collective-permute-start.12 = (bf16[64,1024]{0,1:T(8,128)(2,1)S(1)}, bf16[64,1024]{0,1:T(8,128)(2,1)S(1)}, u32[]{:S(2)}, u32[]{:S(2)}) collective-permute-start(bf16[64,1024]{0,1:T(8,128)(2,1)S(1)} %collective-permute-done.11), channel_id=1, source_target_pairs={{1,0},{0,1},{3,2},{2,3},{5,4},{4,5},{7,6},{6,7},{9,8},{8,9},{11,10... | collective-permute-start | bytes 393224 | tf_op jit(solution)/shard_map/ppermute | solution.py:774
  146.3 9.4 %collective-permute-start.45 = (bf16[192,768]{1,0:T(8,128)(2,1)}, bf16[192,768]{1,0:T(8,128)(2,1)S(1)}, u32[]{:S(2)}, u32[]{:S(2)}) collective-permute-start(bf16[192,768]{1,0:T(8,128)(2,1)} %get-tuple-element.119), channel_id=1, source_target_pairs={{4,0},{0,4},{12,8},{8,12},{20,16},{16,20},{28,24},{24,28},{5,1},{1... | collective-permute-start | bytes 884744 | tf_op jit(solution)/shard_map/ppermute | solution.py:770
  155.7 8.5 %collective-permute-start.46 = (bf16[192,768]{1,0:T(8,128)(2,1)}, bf16[192,768]{1,0:T(8,128)(2,1)S(1)}, u32[]{:S(2)}, u32[]{:S(2)}) collective-permute-start(bf16[192,768]{1,0:T(8,128)(2,1)} %get-tuple-element.120), channel_id=1, source_target_pairs={{4,0},{0,4},{12,8},{8,12},{20,16},{16,20},{28,24},{24,28},{5,1},{1... | collective-permute-start | bytes 884744 | tf_op jit(solution)/shard_map/ppermute | solution.py:770
  164.1 7.5 %collective-permute-start.47 = (bf16[192,768]{1,0:T(8,128)(2,1)}, bf16[192,768]{1,0:T(8,128)(2,1)S(1)}, u32[]{:S(2)}, u32[]{:S(2)}) collective-permute-start(bf16[192,768]{1,0:T(8,128)(2,1)} %get-tuple-element.121), channel_id=1, source_target_pairs={{4,0},{0,4},{12,8},{8,12},{20,16},{16,20},{28,24},{24,28},{5,1},{1... | collective-permute-start | bytes 884744 | tf_op jit(solution)/shard_map/ppermute | solution.py:770
  166.7 17.3 %collective-permute-start.66 = (bf16[192,768]{1,0:T(8,128)(2,1)S(1)}, bf16[192,768]{1,0:T(8,128)(2,1)S(1)}, u32[]{:S(2)}, u32[]{:S(2)}) collective-permute-start(bf16[192,768]{1,0:T(8,128)(2,1)S(1)} %add_convert_fusion.8), channel_id=1, source_target_pairs={{16,0},{20,4},{24,8},{28,12},{0,16},{4,20},{8,24},{12,28},{17,1},{... | collective-permute-start | bytes 884744 | tf_op jit(solution)/shard_map/ppermute | solution.py:761
  167.8 19.7 %collective-permute-start.67 = (bf16[192,768]{1,0:T(8,128)(2,1)S(1)}, bf16[192,768]{1,0:T(8,128)(2,1)S(1)}, u32[]{:S(2)}, u32[]{:S(2)}) collective-permute-start(bf16[192,768]{1,0:T(8,128)(2,1)S(1)} %add_convert_fusion.7), channel_id=1, source_target_pairs={{8,0},{12,4},{16,8},{20,12},{24,16},{28,20},{0,24},{4,28},{9,1},{1... | collective-permute-start | bytes 884744 | tf_op jit(solution)/shard_map/ppermute | solution.py:761
  171.7 15.9 %collective-permute-start.48 = (bf16[192,768]{1,0:T(8,128)(2,1)}, bf16[192,768]{1,0:T(8,128)(2,1)S(1)}, u32[]{:S(2)}, u32[]{:S(2)}) collective-permute-start(bf16[192,768]{1,0:T(8,128)(2,1)} %get-tuple-element.122), channel_id=1, source_target_pairs={{4,0},{0,4},{12,8},{8,12},{20,16},{16,20},{28,24},{24,28},{5,1},{1... | collective-permute-start | bytes 884744 | tf_op jit(solution)/shard_map/ppermute | solution.py:770
  173.3 14.3 %collective-permute-start.68 = (bf16[192,768]{1,0:T(8,128)(2,1)S(1)}, bf16[192,768]{1,0:T(8,128)(2,1)S(1)}, u32[]{:S(2)}, u32[]{:S(2)}) collective-permute-start(bf16[192,768]{1,0:T(8,128)(2,1)S(1)} %add_convert_fusion.6), channel_id=1, source_target_pairs={{24,0},{28,4},{0,8},{4,12},{8,16},{12,20},{16,24},{20,28},{25,1},{... | collective-permute-start | bytes 884744 | tf_op jit(solution)/shard_map/ppermute | solution.py:761
  188.7 19.5 %collective-permute-start.24 = (bf16[192,768]{1,0:T(8,128)(2,1)S(1)}, bf16[192,768]{1,0:T(8,128)(2,1)S(1)}, u32[]{:S(2)}, u32[]{:S(2)}) collective-permute-start(bf16[192,768]{1,0:T(8,128)(2,1)S(1)} %get-tuple-element.91.refs_0_), channel_id=1, source_target_pairs={{8,0},{12,4},{16,8},{20,12},{24,16},{28,20},{0,24},{4,28},{9,1},{1... | collective-permute-start | bytes 884744 | tf_op jit(solution)/shard_map/ppermute | solution.py:761
  190.0 27.9 %collective-permute-start.26 = (bf16[192,768]{1,0:T(8,128)(2,1)S(1)}, bf16[192,768]{1,0:T(8,128)(2,1)S(1)}, u32[]{:S(2)}, u32[]{:S(2)}) collective-permute-start(bf16[192,768]{1,0:T(8,128)(2,1)S(1)} %get-tuple-element.91.refs_0_), channel_id=1, source_target_pairs={{16,0},{20,4},{24,8},{28,12},{0,16},{4,20},{8,24},{12,28},{17,1},{... | collective-permute-start | bytes 884744 | tf_op jit(solution)/shard_map/ppermute | solution.py:761
  202.5 15.8 %collective-permute-start.28 = (bf16[192,768]{1,0:T(8,128)(2,1)S(1)}, bf16[192,768]{1,0:T(8,128)(2,1)S(1)}, u32[]{:S(2)}, u32[]{:S(2)}) collective-permute-start(bf16[192,768]{1,0:T(8,128)(2,1)S(1)} %get-tuple-element.91.refs_0_), channel_id=1, source_target_pairs={{24,0},{28,4},{0,8},{4,12},{8,16},{12,20},{16,24},{20,28},{25,1},{... | collective-permute-start | bytes 884744 | tf_op jit(solution)/shard_map/ppermute | solution.py:761
  204.5 15.5 %collective-permute-start.23 = (bf16[192,768]{1,0:T(8,128)(2,1)S(1)}, bf16[192,768]{1,0:T(8,128)(2,1)S(1)}, u32[]{:S(2)}, u32[]{:S(2)}) collective-permute-start(bf16[192,768]{1,0:T(8,128)(2,1)S(1)} %get-tuple-element.91.refs_0_), channel_id=1, source_target_pairs={{4,0},{0,4},{12,8},{8,12},{20,16},{16,20},{28,24},{24,28},{5,1},{1... | collective-permute-start | bytes 884744 | tf_op jit(solution)/shard_map/ppermute | solution.py:770
  208.2 11.7 %collective-permute-start.25 = (bf16[192,768]{1,0:T(8,128)(2,1)S(1)}, bf16[192,768]{1,0:T(8,128)(2,1)S(1)}, u32[]{:S(2)}, u32[]{:S(2)}) collective-permute-start(bf16[192,768]{1,0:T(8,128)(2,1)S(1)} %collective-permute-done.24.refs_2_), channel_id=1, source_target_pairs={{4,0},{0,4},{12,8},{8,12},{20,16},{16,20},{28,24},{24,28},{5,1},{1... | collective-permute-start | bytes 884744 | tf_op jit(solution)/shard_map/ppermute | solution.py:770
  217.9 9.2 %collective-permute-start.27 = (bf16[192,768]{1,0:T(8,128)(2,1)S(1)}, bf16[192,768]{1,0:T(8,128)(2,1)S(1)}, u32[]{:S(2)}, u32[]{:S(2)}) collective-permute-start(bf16[192,768]{1,0:T(8,128)(2,1)S(1)} %collective-permute-done.26.refs_4_), channel_id=1, source_target_pairs={{4,0},{0,4},{12,8},{8,12},{20,16},{16,20},{28,24},{24,28},{5,1},{1... | collective-permute-start | bytes 884744 | tf_op jit(solution)/shard_map/ppermute | solution.py:770
  218.4 11.9 %collective-permute-start.29 = (bf16[192,768]{1,0:T(8,128)(2,1)S(1)}, bf16[192,768]{1,0:T(8,128)(2,1)S(1)}, u32[]{:S(2)}, u32[]{:S(2)}) collective-permute-start(bf16[192,768]{1,0:T(8,128)(2,1)S(1)} %collective-permute-done.28.refs_6_), channel_id=1, source_target_pairs={{4,0},{0,4},{12,8},{8,12},{20,16},{16,20},{28,24},{24,28},{5,1},{1... | collective-permute-start | bytes 884744 | tf_op jit(solution)/shard_map/ppermute | solution.py:770
  289.5 9.6 %collective-permute-start.71 = (f32[54,128]{1,0:T(8,128)S(1)}, f32[54,128]{1,0:T(8,128)S(1)}, u32[]{:S(2)}, u32[]{:S(2)}) collective-permute-start(f32[54,128]{1,0:T(8,128)S(1)} %pad_maximum_fusion), channel_id=1, source_target_pairs={{4,0},{0,4},{12,8},{8,12},{20,16},{16,20},{28,24},{24,28},{5,1},{1... | collective-permute-start | bytes 82952 | tf_op jit(solution)/shard_map/ppermute | solution.py:770
  299.0 78.8 %collective-permute-start.31 = (bf16[1024,384]{1,0:T(8,128)(2,1)}, bf16[1024,384]{1,0:T(8,128)(2,1)S(1)}, u32[]{:S(2)}, u32[]{:S(2)}) collective-permute-start(bf16[1024,384]{1,0:T(8,128)(2,1)} %get-tuple-element.96), channel_id=1, source_target_pairs={{1,0},{0,1},{3,2},{2,3},{5,4},{4,5},{7,6},{6,7},{9,8},{8,9},{11,10... | collective-permute-start | bytes 2359304 | tf_op jit(solution)/shard_map/ppermute | solution.py:774
  300.1 11.9 %collective-permute-start.37 = (bf16[64,1024]{0,1:T(8,128)(2,1)S(1)}, bf16[64,1024]{0,1:T(8,128)(2,1)S(1)}, u32[]{:S(2)}, u32[]{:S(2)}) collective-permute-start(bf16[64,1024]{0,1:T(8,128)(2,1)S(1)} %get-tuple-element.220), channel_id=1, source_target_pairs={{1,0},{0,1},{3,2},{2,3},{5,4},{4,5},{7,6},{6,7},{9,8},{8,9},{11,10... | collective-permute-start | bytes 393224 | tf_op jit(solution)/shard_map/ppermute | solution.py:774
  300.2 14.0 %collective-permute-start.36 = (bf16[64,1024]{0,1:T(8,128)(2,1)S(1)}, bf16[64,1024]{0,1:T(8,128)(2,1)S(1)}, u32[]{:S(2)}, u32[]{:S(2)}) collective-permute-start(bf16[64,1024]{0,1:T(8,128)(2,1)S(1)} %get-tuple-element.219), channel_id=1, source_target_pairs={{1,0},{0,1},{3,2},{2,3},{5,4},{4,5},{7,6},{6,7},{9,8},{8,9},{11,10... | collective-permute-start | bytes 393224 | tf_op jit(solution)/shard_map/ppermute | solution.py:774
  303.7 7.6 %collective-permute-start.73 = (f32[54,128]{1,0:T(8,128)S(1)}, f32[54,128]{1,0:T(8,128)S(1)}, u32[]{:S(2)}, u32[]{:S(2)}) collective-permute-start(f32[54,128]{1,0:T(8,128)S(1)} %add.333), channel_id=1, source_target_pairs={{16,0},{20,4},{24,8},{28,12},{0,16},{4,20},{8,24},{12,28},{17,1},{... | collective-permute-start | bytes 82952 | tf_op jit(solution)/shard_map/ppermute | solution.py:766
  311.2 21.0 %collective-permute-start.49 = (bf16[192,768]{1,0:T(8,128)(2,1)}, bf16[192,768]{1,0:T(8,128)(2,1)S(1)}, u32[]{:S(2)}, u32[]{:S(2)}) collective-permute-start(bf16[192,768]{1,0:T(8,128)(2,1)} %get-tuple-element.123), channel_id=1, source_target_pairs={{4,0},{0,4},{12,8},{8,12},{20,16},{16,20},{28,24},{24,28},{5,1},{1... | collective-permute-start | bytes 884744 | tf_op jit(solution)/shard_map/ppermute | solution.py:770
  331.7 13.4 %collective-permute-start.40 = (bf16[256,1536]{1,0:T(8,128)(2,1)}, bf16[256,1536]{1,0:T(8,128)(2,1)S(1)}, u32[]{:S(2)}, u32[]{:S(2)}) collective-permute-start(bf16[256,1536]{1,0:T(8,128)(2,1)} %get-tuple-element.110), channel_id=1, source_target_pairs={{1,0},{0,1},{3,2},{2,3},{5,4},{4,5},{7,6},{6,7},{9,8},{8,9},{11,10... | collective-permute-start | bytes 2359304 | tf_op jit(solution)/shard_map/ppermute | solution.py:774
  332.3 12.3 %collective-permute-start.51 = (bf16[192,768]{1,0:T(8,128)(2,1)S(1)}, bf16[192,768]{1,0:T(8,128)(2,1)S(1)}, u32[]{:S(2)}, u32[]{:S(2)}) collective-permute-start(bf16[192,768]{1,0:T(8,128)(2,1)S(1)} %copy-done.71), channel_id=1, source_target_pairs={{4,0},{0,4},{12,8},{8,12},{20,16},{16,20},{28,24},{24,28},{5,1},{1... | collective-permute-start | bytes 884744 | tf_op jit(solution)/shard_map/ppermute | solution.py:770
  341.9 13.2 %collective-permute-start.39 = (bf16[256,1536]{1,0:T(8,128)(2,1)S(1)}, bf16[256,1536]{1,0:T(8,128)(2,1)S(1)}, u32[]{:S(2)}, u32[]{:S(2)}) collective-permute-start(bf16[256,1536]{1,0:T(8,128)(2,1)S(1)} %copy-done.56), channel_id=1, source_target_pairs={{1,0},{0,1},{3,2},{2,3},{5,4},{4,5},{7,6},{6,7},{9,8},{8,9},{11,10... | collective-permute-start | bytes 2359304 | tf_op jit(solution)/shard_map/ppermute | solution.py:774
  342.2 36.5 %collective-permute-start.50 = (bf16[192,768]{1,0:T(8,128)(2,1)S(1)}, bf16[192,768]{1,0:T(8,128)(2,1)S(1)}, u32[]{:S(2)}, u32[]{:S(2)}) collective-permute-start(bf16[192,768]{1,0:T(8,128)(2,1)S(1)} %add_convert_fusion.11), channel_id=1, source_target_pairs={{16,0},{20,4},{24,8},{28,12},{0,16},{4,20},{8,24},{12,28},{17,1},{... | collective-permute-start | bytes 884744 | tf_op jit(solution)/shard_map/ppermute | solution.py:761
  344.6 8.9 %collective-permute-start.53 = (bf16[192,768]{1,0:T(8,128)(2,1)S(1)}, bf16[192,768]{1,0:T(8,128)(2,1)S(1)}, u32[]{:S(2)}, u32[]{:S(2)}) collective-permute-start(bf16[192,768]{1,0:T(8,128)(2,1)S(1)} %copy-done.69), channel_id=1, source_target_pairs={{4,0},{0,4},{12,8},{8,12},{20,16},{16,20},{28,24},{24,28},{5,1},{1... | collective-permute-start | bytes 884744 | tf_op jit(solution)/shard_map/ppermute | solution.py:770
  345.1 35.6 %collective-permute-start.52 = (bf16[192,768]{1,0:T(8,128)(2,1)S(1)}, bf16[192,768]{1,0:T(8,128)(2,1)S(1)}, u32[]{:S(2)}, u32[]{:S(2)}) collective-permute-start(bf16[192,768]{1,0:T(8,128)(2,1)S(1)} %add_convert_fusion.10), channel_id=1, source_target_pairs={{8,0},{12,4},{16,8},{20,12},{24,16},{28,20},{0,24},{4,28},{9,1},{1... | collective-permute-start | bytes 884744 | tf_op jit(solution)/shard_map/ppermute | solution.py:761
  353.5 18.6 %collective-permute-start.41 = (bf16[256,1536]{1,0:T(8,128)(2,1)S(1)}, bf16[256,1536]{1,0:T(8,128)(2,1)S(1)}, u32[]{:S(2)}, u32[]{:S(2)}) collective-permute-start(bf16[256,1536]{1,0:T(8,128)(2,1)S(1)} %add_convert_fusion), channel_id=1, source_target_pairs={{2,0},{3,1},{0,2},{1,3},{6,4},{7,5},{4,6},{5,7},{10,8},{11,9},{8,1... | collective-permute-start | bytes 2359304 | tf_op jit(solution)/shard_map/ppermute | solution.py:774
  355.1 23.0 %collective-permute-start.55 = (bf16[192,768]{1,0:T(8,128)(2,1)S(1)}, bf16[192,768]{1,0:T(8,128)(2,1)S(1)}, u32[]{:S(2)}, u32[]{:S(2)}) collective-permute-start(bf16[192,768]{1,0:T(8,128)(2,1)S(1)} %copy-done.65), channel_id=1, source_target_pairs={{4,0},{0,4},{12,8},{8,12},{20,16},{16,20},{28,24},{24,28},{5,1},{1... | collective-permute-start | bytes 884744 | tf_op jit(solution)/shard_map/ppermute | solution.py:770
  372.1 9.0 %collective-permute-start.54 = (bf16[192,768]{1,0:T(8,128)(2,1)S(1)}, bf16[192,768]{1,0:T(8,128)(2,1)S(1)}, u32[]{:S(2)}, u32[]{:S(2)}) collective-permute-start(bf16[192,768]{1,0:T(8,128)(2,1)S(1)} %add_convert_fusion.9), channel_id=1, source_target_pairs={{24,0},{28,4},{0,8},{4,12},{8,16},{12,20},{16,24},{20,28},{25,1},{... | collective-permute-start | bytes 884744 | tf_op jit(solution)/shard_map/ppermute | solution.py:761
  378.2 26.0 %collective-permute-start.30 = (bf16[1024,384]{1,0:T(8,128)(2,1)S(1)}, bf16[1024,384]{1,0:T(8,128)(2,1)S(1)}, u32[]{:S(2)}, u32[]{:S(2)}) collective-permute-start(bf16[1024,384]{1,0:T(8,128)(2,1)S(1)} %copy-done.55), channel_id=1, source_target_pairs={{1,0},{0,1},{3,2},{2,3},{5,4},{4,5},{7,6},{6,7},{9,8},{8,9},{11,10... | collective-permute-start | bytes 2359304 | tf_op jit(solution)/shard_map/ppermute | solution.py:774
  378.7 25.4 %collective-permute-start.32 = (bf16[1024,384]{1,0:T(8,128)(2,1)S(1)}, bf16[1024,384]{1,0:T(8,128)(2,1)S(1)}, u32[]{:S(2)}, u32[]{:S(2)}) collective-permute-start(bf16[1024,384]{1,0:T(8,128)(2,1)S(1)} %add_convert_fusion.2), channel_id=1, source_target_pairs={{2,0},{3,1},{0,2},{1,3},{6,4},{7,5},{4,6},{5,7},{10,8},{11,9},{8,1... | collective-permute-start | bytes 2359304 | tf_op jit(solution)/shard_map/ppermute | solution.py:774
  380.3 9.8 %collective-permute-start.56 = (bf16[192,896]{1,0:T(8,128)(2,1)S(1)}, bf16[192,896]{1,0:T(8,128)(2,1)S(1)}, u32[]{:S(2)}, u32[]{:S(2)}) collective-permute-start(bf16[192,896]{1,0:T(8,128)(2,1)S(1)} %copy-done.60), channel_id=1, source_target_pairs={{4,0},{0,4},{12,8},{8,12},{20,16},{16,20},{28,24},{24,28},{5,1},{1... | collective-permute-start | bytes 1032200 | tf_op jit(solution)/shard_map/ppermute | solution.py:770
  380.7 17.8 %collective-permute-start.75 = (f32[12,128]{1,0:T(8,128)S(1)}, f32[12,128]{1,0:T(8,128)S(1)}, u32[]{:S(2)}, u32[]{:S(2)}) collective-permute-start(f32[12,128]{1,0:T(8,128)S(1)} %bitcast_add_fusion.4), channel_id=1, source_target_pairs={{2,0},{3,1},{0,2},{1,3},{6,4},{7,5},{4,6},{5,7},{10,8},{11,9},{8,1... | collective-permute-start | bytes 18440 | tf_op jit(solution)/shard_map/ppermute | solution.py:774
  390.0 12.5 %collective-permute-start.58 = (bf16[192,896]{1,0:T(8,128)(2,1)S(1)}, bf16[192,896]{1,0:T(8,128)(2,1)S(1)}, u32[]{:S(2)}, u32[]{:S(2)}) collective-permute-start(bf16[192,896]{1,0:T(8,128)(2,1)S(1)} %copy-done.59), channel_id=1, source_target_pairs={{4,0},{0,4},{12,8},{8,12},{20,16},{16,20},{28,24},{24,28},{5,1},{1... | collective-permute-start | bytes 1032200 | tf_op jit(solution)/shard_map/ppermute | solution.py:770
  398.9 20.5 %collective-permute-start.57 = (bf16[192,896]{1,0:T(8,128)(2,1)S(1)}, bf16[192,896]{1,0:T(8,128)(2,1)S(1)}, u32[]{:S(2)}, u32[]{:S(2)}) collective-permute-start(bf16[192,896]{1,0:T(8,128)(2,1)S(1)} %add_convert_fusion.5), channel_id=1, source_target_pairs={{16,0},{20,4},{24,8},{28,12},{0,16},{4,20},{8,24},{12,28},{17,1},{... | collective-permute-start | bytes 1032200 | tf_op jit(solution)/shard_map/ppermute | solution.py:761
  402.5 8.7 %collective-permute-start.60 = (bf16[192,896]{1,0:T(8,128)(2,1)S(1)}, bf16[192,896]{1,0:T(8,128)(2,1)S(1)}, u32[]{:S(2)}, u32[]{:S(2)}) collective-permute-start(bf16[192,896]{1,0:T(8,128)(2,1)S(1)} %copy-done.58), channel_id=1, source_target_pairs={{4,0},{0,4},{12,8},{8,12},{20,16},{16,20},{28,24},{24,28},{5,1},{1... | collective-permute-start | bytes 1032200 | tf_op jit(solution)/shard_map/ppermute | solution.py:770
  406.7 12.1 %collective-permute-start.78 = (f32[12,128]{1,0:T(8,128)S(1)}, f32[12,128]{1,0:T(8,128)S(1)}, u32[]{:S(2)}, u32[]{:S(2)}) collective-permute-start(f32[12,128]{1,0:T(8,128)S(1)} %add.341), channel_id=1, source_target_pairs={{16,0},{20,4},{24,8},{28,12},{0,16},{4,20},{8,24},{12,28},{17,1},{... | collective-permute-start | bytes 18440 | tf_op jit(solution)/shard_map/ppermute | solution.py:766
  410.0 21.2 %collective-permute-start.59 = (bf16[192,896]{1,0:T(8,128)(2,1)S(1)}, bf16[192,896]{1,0:T(8,128)(2,1)S(1)}, u32[]{:S(2)}, u32[]{:S(2)}) collective-permute-start(bf16[192,896]{1,0:T(8,128)(2,1)S(1)} %add_convert_fusion.4), channel_id=1, source_target_pairs={{8,0},{12,4},{16,8},{20,12},{24,16},{28,20},{0,24},{4,28},{9,1},{1... | collective-permute-start | bytes 1032200 | tf_op jit(solution)/shard_map/ppermute | solution.py:761
  411.2 20.0 %collective-permute-start.62 = (bf16[192,896]{1,0:T(8,128)(2,1)S(1)}, bf16[192,896]{1,0:T(8,128)(2,1)S(1)}, u32[]{:S(2)}, u32[]{:S(2)}) collective-permute-start(bf16[192,896]{1,0:T(8,128)(2,1)S(1)} %copy-done.57), channel_id=1, source_target_pairs={{4,0},{0,4},{12,8},{8,12},{20,16},{16,20},{28,24},{24,28},{5,1},{1... | collective-permute-start | bytes 1032200 | tf_op jit(solution)/shard_map/ppermute | solution.py:770
  413.1 18.1 %collective-permute-start.61 = (bf16[192,896]{1,0:T(8,128)(2,1)S(1)}, bf16[192,896]{1,0:T(8,128)(2,1)S(1)}, u32[]{:S(2)}, u32[]{:S(2)}) collective-permute-start(bf16[192,896]{1,0:T(8,128)(2,1)S(1)} %add_convert_fusion.3), channel_id=1, source_target_pairs={{24,0},{28,4},{0,8},{4,12},{8,16},{12,20},{16,24},{20,28},{25,1},{... | collective-permute-start | bytes 1032200 | tf_op jit(solution)/shard_map/ppermute | solution.py:761
  418.8 32.6 %collective-permute-start.42 = (bf16[256,1536]{1,0:T(8,128)(2,1)}, bf16[256,1536]{1,0:T(8,128)(2,1)}, u32[]{:S(2)}, u32[]{:S(2)}) collective-permute-start(bf16[256,1536]{1,0:T(8,128)(2,1)} %get-tuple-element.111), channel_id=1, source_target_pairs={{1,0},{0,1},{3,2},{2,3},{5,4},{4,5},{7,6},{6,7},{9,8},{8,9},{11,10... | collective-permute-start | bytes 2359304 | tf_op jit(solution)/shard_map/ppermute | solution.py:774
  419.4 20.7 %collective-permute-start.43 = (bf16[256,1536]{1,0:T(8,128)(2,1)}, bf16[256,1536]{1,0:T(8,128)(2,1)}, u32[]{:S(2)}, u32[]{:S(2)}) collective-permute-start(bf16[256,1536]{1,0:T(8,128)(2,1)} %get-tuple-element.111), channel_id=1, source_target_pairs={{2,0},{3,1},{0,2},{1,3},{6,4},{7,5},{4,6},{5,7},{10,8},{11,9},{8,1... | collective-permute-start | bytes 2359304 | tf_op jit(solution)/shard_map/ppermute | solution.py:774
  432.1 16.2 %collective-permute-start.63 = (f32[192,64]{1,0:T(8,128)}, f32[192,64]{1,0:T(8,128)}, u32[]{:S(2)}, u32[]{:S(2)}) collective-permute-start(f32[192,64]{1,0:T(8,128)} %slice.134), channel_id=1, source_target_pairs={{1,0},{0,1},{3,2},{2,3},{5,4},{4,5},{7,6},{6,7},{9,8},{8,9},{11,10... | collective-permute-start | bytes 147464 | tf_op jit(solution)/shard_map/ppermute | solution.py:774
  432.1 15.5 %collective-permute-start.64 = (f32[192,64]{1,0:T(8,128)}, f32[192,64]{1,0:T(8,128)}, u32[]{:S(2)}, u32[]{:S(2)}) collective-permute-start(f32[192,64]{1,0:T(8,128)} %slice.134), channel_id=1, source_target_pairs={{2,0},{3,1},{0,2},{1,3},{6,4},{7,5},{4,6},{5,7},{10,8},{11,9},{8,1... | collective-permute-start | bytes 147464 | tf_op jit(solution)/shard_map/ppermute | solution.py:774
  440.0 17.1 %collective-permute-start.44 = (bf16[256,1536]{1,0:T(8,128)(2,1)}, bf16[256,1536]{1,0:T(8,128)(2,1)}, u32[]{:S(2)}, u32[]{:S(2)}) collective-permute-start(bf16[256,1536]{1,0:T(8,128)(2,1)} %collective-permute-done.43), channel_id=1, source_target_pairs={{1,0},{0,1},{3,2},{2,3},{5,4},{4,5},{7,6},{6,7},{9,8},{8,9},{11,10... | collective-permute-start | bytes 2359304 | tf_op jit(solution)/shard_map/ppermute | solution.py:774
  (87 other events, 923.2 us)

commit v3 on v2

--- a/solution.py
+++ b/solution.py
@@ -16,7 +16,7 @@
 HALO = 8
 bf16 = jnp.bfloat16
 f32 = jnp.float32
-VMEM_LIMIT = 56 * 1024 * 1024
+MIB = 1024 * 1024
 
 
 def dot_nn(a, b):
@@ -136,7 +136,7 @@
 def ssd_backward_kernel(
     x_ref, xb_ref, bc_ref, bcb_ref, st_ref, aux_ref, seg_ref, conv_ref, bct_ref, heads_ref, expand_ref,
     mixed_ref, dy_ref, state_ref,
-    dx_ref, dbc_ref, dst_ref, dconv_ref, dbct_ref, dheads_ref,
+    dx_ref, dbc_ref, dbc_t_ref, dst_ref, dst_t_ref, dconv_ref, dbct_ref, dheads_ref,
     dstate, xs_scr, bc_scr, du_scr, dubc_scr,
 ):
     at = pl.program_id(0)
@@ -231,7 +231,8 @@
     dlog = exact_left(upper.astype(bf16), flow) + sums[0:1, :]
     dstep = dstep + rates * dlog
     draw = dstep * sigmoid(raw)
-    dst_ref[...] = draw
+    dst_ref[...] = pltpu.roll(draw, WIDTH, 1).astype(bf16)
+    dst_t_ref[...] = draw.T[0:16, :].astype(bf16)
     dheads_ref[0:1, :] += jnp.sum(draw, axis=0, keepdims=True)
     dheads_ref[1:2, :] += rates * jnp.sum(dlog * steps, axis=0, keepdims=True)
     dheads_ref[2:3, :] += sums[1:2, :]
@@ -251,7 +252,9 @@
     du = (skip_e * dy + step_e * q) * (sg * (1.0 + u * (1.0 - sg)))
     dx_ref[...] = conv_back(du_scr, du, x_now, conv_ref, dconv_ref).astype(dx_ref.dtype)
     dubc = jnp.concatenate([db, dc], axis=1) * (sgbc * (1.0 + ubc * (1.0 - sgbc)))
-    dbc_ref[...] = conv_back(dubc_scr, dubc, bc_now, bct_ref, dbct_ref)
+    dbc = conv_back(dubc_scr, dubc, bc_now, bct_ref, dbct_ref).astype(bf16)
+    dbc_ref[...] = dbc
+    dbc_t_ref[...] = dbc.T
 
 
 def common_specs(place, channels):
@@ -294,7 +297,8 @@
             pltpu.VMEM((HALO + CHUNK, channels), f32),
             pltpu.VMEM((HALO + CHUNK, 2 * LANES), f32),
         ],
-        compiler_params=pltpu.CompilerParams(vmem_limit_bytes=VMEM_LIMIT),
+        compiler_params=pltpu.CompilerParams(vmem_limit_bytes=32 * MIB),
+        cost_estimate=pl.CostEstimate(flops=14 * 10**9, bytes_accessed=40 * 10**6, transcendentals=0),
         name="ssd_forward",
     )(x_pre, x_pre, bc_pre, bc_pre, step_pre, aux, seg_row, conv_rows, bc_rows, head_rows, expand)
 
@@ -316,15 +320,19 @@
         out_specs=[
             pl.BlockSpec((CHUNK, channels), now),
             pl.BlockSpec((CHUNK, 2 * LANES), now),
+            pl.BlockSpec((2 * LANES, CHUNK), lambda i: (0, place(i))),
             pl.BlockSpec((CHUNK, LANES), now),
+            pl.BlockSpec((16, CHUNK), lambda i: (0, place(i))),
             pl.BlockSpec((8, channels), whole),
             pl.BlockSpec((8, 2 * LANES), whole),
             pl.BlockSpec((8, LANES), whole),
         ],
         out_shape=[
             jax.ShapeDtypeStruct((tokens, channels), bf16),
-            jax.ShapeDtypeStruct((tokens, 2 * LANES), f32),
-            jax.ShapeDtypeStruct((tokens, LANES), f32),
+            jax.ShapeDtypeStruct((tokens, 2 * LANES), bf16),
+            jax.ShapeDtypeStruct((2 * LANES, tokens), bf16),
+            jax.ShapeDtypeStruct((tokens, LANES), bf16),
+            jax.ShapeDtypeStruct((16, tokens), bf16),
             jax.ShapeDtypeStruct((8, channels), f32),
             jax.ShapeDtypeStruct((8, 2 * LANES), f32),
             jax.ShapeDtypeStruct((8, LANES), f32),
@@ -336,7 +344,8 @@
             pltpu.VMEM((HALO + CHUNK, channels), f32),
             pltpu.VMEM((HALO + CHUNK, 2 * LANES), f32),
         ],
-        compiler_params=pltpu.CompilerParams(vmem_limit_bytes=VMEM_LIMIT),
+        compiler_params=pltpu.CompilerParams(vmem_limit_bytes=32 * MIB),
+        cost_estimate=pl.CostEstimate(flops=28 * 10**9, bytes_accessed=80 * 10**6, transcendentals=0),
         name="ssd_backward",
     )(x_pre, x_pre, bc_pre, bc_pre, step_pre, aux, seg_row, conv_rows, bc_rows, head_rows, expand, mixed, dy, states)
 
@@ -377,61 +386,138 @@
 
 
 def fill(dest, pieces, idx_ref):
-    for s, piece in enumerate(pieces):
-        rows = piece.shape[0]
-        dest[pl.ds(pl.multiple_of(idx_ref[s] * rows, rows), rows), :] = piece[...]
-
-
-def params():
-    return pltpu.CompilerParams(vmem_limit_bytes=VMEM_LIMIT)
+    rows = pieces[0].shape[0]
+    s = 0
+    for piece in pieces:
+        for b in range(piece.shape[0] // rows):
+            start = pl.multiple_of(idx_ref[s] * rows, rows)
+            dest[pl.ds(start, rows), :] = piece[b * rows:(b + 1) * rows, :]
+            s += 1
+
+
+def params(mib=24):
+    return pltpu.CompilerParams(vmem_limit_bytes=mib * MIB)
 
 
 def cost(flops, moved):
     return pl.CostEstimate(flops=int(flops), bytes_accessed=int(moved), transcendentals=0)
 
 
-def prepare_kernel(hidden_ref, gain_ref, cot_ref, low_ref, low_t_ref, cot_t_ref):
+def prepare_kernel(hidden_ref, gain_ref, low_ref, low_t_ref):
     inputs = hidden_ref[...].astype(f32)
     inv_rms = lax.rsqrt(jnp.mean(inputs * inputs, axis=1, keepdims=True) + EPSILON)
     low = (inputs * inv_rms * gain_ref[0:1, :]).astype(bf16)
     low_ref[...] = low
     low_t_ref[...] = low.T
-    cot_t_ref[...] = cot_ref[...].T
-
-
-def prepare(hidden, gain_rows, cot):
+
+
+def prepare(hidden, gain_rows):
     tokens, depth = hidden.shape
     block = pl.BlockSpec((TILE, depth), lambda i: (i, 0))
-    turned = pl.BlockSpec((depth, TILE), lambda i: (0, i))
     return pl.pallas_call(
         prepare_kernel,
         grid=(tokens // TILE,),
-        in_specs=[block, pl.BlockSpec((8, depth), lambda i: (0, 0)), block],
-        out_specs=[block, turned, turned],
-        out_shape=[
-            jax.ShapeDtypeStruct((tokens, depth), bf16),
-            jax.ShapeDtypeStruct((depth, tokens), bf16),
-            jax.ShapeDtypeStruct((depth, tokens), bf16),
-        ],
+        in_specs=[block, pl.BlockSpec((8, depth), lambda i: (0, 0))],
+        out_specs=[block, pl.BlockSpec((depth, TILE), lambda i: (0, i))],
+        out_shape=[jax.ShapeDtypeStruct((tokens, depth), bf16), jax.ShapeDtypeStruct((depth, tokens), bf16)],
         compiler_params=params(),
+        cost_estimate=cost(6 * 10**9, 20 * 10**6),
         name="prepare",
-    )(hidden, gain_rows, cot)
+    )(hidden, gain_rows)
+
+
+def columns_kernel(rank_ref, *refs, count):
+    pieces, (full_ref, full_t_ref) = refs[:count], refs[count:]
+    for r, piece in enumerate(pieces):
+        width = piece.shape[1]
+        start = pl.multiple_of((rank_ref[0] ^ r) * width, LANES)
+        value = piece[...]
+        full_ref[:, pl.ds(start, width)] = value
+        full_t_ref[pl.ds(start, width), :] = value.T
+
+
+def join_columns(pieces, rank):
+    tokens, width = pieces[0].shape
+    depth = width * len(pieces)
+    return pl.pallas_call(
+        functools.partial(columns_kernel, count=len(pieces)),
+        grid=(tokens // TILE,),
+        in_specs=[pl.BlockSpec(memory_space=pltpu.SMEM)] + [pl.BlockSpec((TILE, width), lambda i: (i, 0))] * len(pieces),
+        out_specs=[pl.BlockSpec((TILE, depth), lambda i: (i, 0)), pl.BlockSpec((depth, TILE), lambda i: (0, i))],
+        out_shape=[jax.ShapeDtypeStruct((tokens, depth), bf16), jax.ShapeDtypeStruct((depth, tokens), bf16)],
+        compiler_params=params(),
+        cost_estimate=cost(4 * 10**9, 16 * 10**6),
+        name="join_columns",
+    )(rank, *pieces)
+
+
+def rows_kernel(rank_ref, *refs, count):
+    pieces, full_ref = refs[:count], refs[count]
+    for r, piece in enumerate(pieces):
+        rows = piece.shape[0]
+        full_ref[pl.ds(pl.multiple_of((rank_ref[0] ^ r) * rows, rows), rows), :] = piece[...]
+
+
+def join_rows(pieces, rank):
+    rows, width = pieces[0].shape
+    shape = (rows * len(pieces), width)
+    return pl.pallas_call(
+        functools.partial(rows_kernel, count=len(pieces)),
+        in_specs=[pl.BlockSpec(memory_space=pltpu.SMEM)] + [pl.BlockSpec(memory_space=pltpu.VMEM)] * len(pieces),
+        out_specs=pl.BlockSpec(memory_space=pltpu.VMEM),
+        out_shape=jax.ShapeDtypeStruct(shape, pieces[0].dtype),
+        compiler_params=params(),
+        cost_estimate=cost(10**9, 4 * shape[0] * shape[1]),
+        name="join_rows",
+    )(rank, *pieces)
+
+
+def small_kernel(rank_ref, *refs, count):
+    pieces, (small_ref, bc_ref, step_ref, scratch) = refs[:count], refs[count:]
+    share = pieces[0].shape[0]
+    for r, piece in enumerate(pieces):
+        scratch[pl.ds(pl.multiple_of((rank_ref[0] ^ r) * share, share), share), :] = piece[...].astype(f32)
+    bc_ref[...] = scratch[...].T
+    turned = small_ref[...].T
+    lane = lax.broadcasted_iota(jnp.int32, turned.shape, 1)
+    step_ref[...] = jnp.where(lane < LANES - share, pltpu.roll(turned, LANES - share, 1), 0.0)
+
+
+def join_small(pieces, small, rank):
+    share, tokens = pieces[0].shape
+    width = share * len(pieces)
+    return pl.pallas_call(
+        functools.partial(small_kernel, count=len(pieces)),
+        grid=(tokens // TILE,),
+        in_specs=[pl.BlockSpec(memory_space=pltpu.SMEM)]
+        + [pl.BlockSpec((share, TILE), lambda i: (0, i))] * len(pieces)
+        + [pl.BlockSpec((LANES, TILE), lambda i: (0, i))],
+        out_specs=[pl.BlockSpec((TILE, width), lambda i: (i, 0)), pl.BlockSpec((TILE, LANES), lambda i: (i, 0))],
+        out_shape=[jax.ShapeDtypeStruct((tokens, width), f32), jax.ShapeDtypeStruct((tokens, LANES), f32)],
+        scratch_shapes=[pltpu.VMEM((width, TILE), f32)],
+        compiler_params=params(),
+        cost_estimate=cost(2 * 10**9, 4 * 10**6),
+        name="join_small",
+    )(rank, *pieces, small)
 
 
 def project_kernel(idx_ref, lhs_ref, *refs, count):
-    pieces, (x_ref, small_ref, w_ref) = refs[:count], refs[count:]
+    pieces, (x_ref, small_ref, share_ref, w_ref, wt_ref) = refs[:count], refs[count:]
+    channels = x_ref.shape[1]
 
     @pl.when(pl.program_id(0) == 0)
     def _():
         fill(w_ref, pieces, idx_ref)
+        wt_ref[...] = w_ref[:, channels:].T[0:wt_ref.shape[0], :]
 
     product = dot_nn(lhs_ref[...], w_ref[...])
-    channels = x_ref.shape[1]
     x_ref[...] = product[:, :channels]
-    small_ref[...] = product[:, channels:].T
-
-
-def project(lhs, pieces, idx, channels):
+    small = product[:, channels:].T
+    small_ref[...] = small
+    share_ref[...] = small[0:share_ref.shape[0], :].astype(bf16)
+
+
+def project(lhs, pieces, idx, channels, share):
     tokens, depth = lhs.shape
     count, width = len(pieces), pieces[0].shape[1]
     whole = lambda i: (0, 0)
@@ -443,12 +529,16 @@
         out_specs=[
             pl.BlockSpec((TILE, channels), lambda i: (i, 0)),
             pl.BlockSpec((width - channels, TILE), lambda i: (0, i)),
+            pl.BlockSpec((share, TILE), lambda i: (0, i)),
             pl.BlockSpec((depth, width), whole),
+            pl.BlockSpec((share, depth), whole),
         ],
         out_shape=[
             jax.ShapeDtypeStruct((tokens, channels), f32),
             jax.ShapeDtypeStruct((width - channels, tokens), f32),
+            jax.ShapeDtypeStruct((share, tokens), bf16),
             jax.ShapeDtypeStruct((depth, width), bf16),
+            jax.ShapeDtypeStruct((share, depth), bf16),
         ],
         compiler_params=params(),
         cost_estimate=cost(2 * tokens * depth * width, 6 * depth * width),
@@ -591,7 +681,7 @@
     def _():
         dgain_ref[...] = jnp.zeros_like(dgain_ref)
 
-    dgain_ref[0:1, :] += jnp.sum(gout * gated * scale, axis=0, keepdims=True)
+    dgain_ref[5:6, :] += jnp.sum(gout * gated * scale, axis=0, keepdims=True)
 
 
 def gate_backward(gate, gout, mixed, square, inner, conv_rows, inner_total):
@@ -615,40 +705,43 @@
     )(gate, gout, mixed, square, inner, conv_rows)
 
 
-def weight_grad_kernel(idx_ref, lhs_ref, *refs, count, parts):
-    rhs, outs, scratch = refs[:parts], refs[parts:parts + count], refs[parts + count]
+def weight_grad_kernel(idx_ref, lhs_ref, rhs_ref, *refs, rows, turned):
+    outs, scratch = refs[:-1], refs[-1]
     at = pl.program_id(0)
-    start = 0
-    for part in rhs:
-        width = part.shape[1]
-        scratch[pl.ds(pl.multiple_of(at * TILE_D, TILE_D), TILE_D), start:start + width] = dot_nn(lhs_ref[...], part[...]).astype(bf16)
-        start += width
+    scratch[pl.ds(pl.multiple_of(at * TILE_D, TILE_D), TILE_D), :] = (dot_nt if turned else dot_nn)(
+        lhs_ref[...], rhs_ref[...]
+    ).astype(bf16)
 
     @pl.when(at == pl.num_programs(0) - 1)
     def _():
-        for s, out in enumerate(outs):
-            rows = out.shape[0]
-            out[...] = scratch[pl.ds(pl.multiple_of(idx_ref[s] * rows, rows), rows), :]
-
-
-def weight_grad(lhs_t, rhs, idx):
+        s = 0
+        for out in outs:
+            for b in range(out.shape[0] // rows):
+                start = pl.multiple_of(idx_ref[s] * rows, rows)
+                out[b * rows:(b + 1) * rows, :] = scratch[pl.ds(start, rows), :]
+                s += 1
+
+
+def weight_grad(lhs_t, rhs, idx, sizes, turned=False):
     depth, tokens = lhs_t.shape
-    width = sum(r.shape[1] for r in rhs)
-    count = idx.shape[0]
-    rows = depth // count
+    width = rhs.shape[0 if turned else 1]
+    rows = depth // idx.shape[0]
     whole = lambda i: (0, 0)
     return pl.pallas_call(
-        functools.partial(weight_grad_kernel, count=count, parts=len(rhs)),
+        functools.partial(weight_grad_kernel, rows=rows, turned=turned),
         grid=(depth // TILE_D,),
-        in_specs=[pl.BlockSpec(memory_space=pltpu.SMEM), pl.BlockSpec((TILE_D, tokens), lambda i: (i, 0))]
-        + [pl.BlockSpec(r.shape, whole) for r in rhs],
-        out_specs=[pl.BlockSpec((rows, width), whole)] * count,
-        out_shape=[jax.ShapeDtypeStruct((rows, width), bf16)] * count,
+        in_specs=[
+            pl.BlockSpec(memory_space=pltpu.SMEM),
+            pl.BlockSpec((TILE_D, tokens), lambda i: (i, 0)),
+            pl.BlockSpec(rhs.shape, whole),
+        ],
+        out_specs=[pl.BlockSpec((size * rows, width), whole) for size in sizes],
+        out_shape=[jax.ShapeDtypeStruct((size * rows, width), bf16) for size in sizes],
         scratch_shapes=[pltpu.VMEM((depth, width), bf16)],
         compiler_params=params(),
         cost_estimate=cost(2 * tokens * depth * width, 4 * depth * width),
         name="weight_grad",
-    )(idx, lhs_t, *rhs)
+    )(idx, lhs_t, rhs)
 
 
 def out_kernel(rank_ref, lhs_ref, w_ref, *outs):
@@ -682,39 +775,42 @@
     )(rank, gated_out, w_out)
 
 
-def term_kernel(rank_ref, *refs, parts, ranks):
-    pairs, outs, scratch = refs[:2 * parts], refs[2 * parts:2 * parts + ranks], refs[2 * parts + ranks]
-    total = None
-    for p in range(parts):
-        product = dot_nt(pairs[2 * p][...], pairs[2 * p + 1][...])
-        total = product if total is None else total + product
+def term_kernel(rank_ref, gx_ref, wx_ref, gg_ref, wg_ref, gs_ref, ws_ref, gb_ref, wbt_ref, *refs):
+    outs, scratch = refs[:-1], refs[-1]
+    total = dot_nt(gx_ref[...], wx_ref[...]) + dot_nt(gg_ref[...], wg_ref[...])
+    total = total + dot_nt(gs_ref[...], ws_ref[...]) + dot_nn(gb_ref[...], wbt_ref[...])
     scratch[...] = total.astype(bf16)
     for r, out in enumerate(outs):
         rows = out.shape[0]
         out[...] = scratch[pl.ds(pl.multiple_of((rank_ref[0] ^ r) * rows, rows), rows), :]
 
 
-def normed_term(pairs, rank, ranks):
-    tokens = pairs[0][0].shape[0]
-    depth = pairs[0][1].shape[0]
+def normed_term(dx, dgate, dstep, dbc, w_a, w_b, w_bct, rank, ranks):
+    tokens, channels = dx.shape
+    depth = w_a.shape[0]
     rows = tokens // ranks
-    specs, flat, inner = [], [], 0
-    for g, w in pairs:
-        specs.append(pl.BlockSpec(g.shape, lambda i: (0, 0)))
-        specs.append(pl.BlockSpec((TILE_D, w.shape[1]), lambda i: (i, 0)))
-        flat += [g, w]
-        inner += w.shape[1]
-    return pl.pallas_call(
-        functools.partial(term_kernel, parts=len(pairs), ranks=ranks),
+    whole = lambda i: (0, 0)
+    return pl.pallas_call(
+        term_kernel,
         grid=(depth // TILE_D,),
-        in_specs=[pl.BlockSpec(memory_space=pltpu.SMEM)] + specs,
+        in_specs=[
+            pl.BlockSpec(memory_space=pltpu.SMEM),
+            pl.BlockSpec(dx.shape, whole),
+            pl.BlockSpec((TILE_D, channels), lambda i: (i, 0)),
+            pl.BlockSpec(dgate.shape, whole),
+            pl.BlockSpec((TILE_D, channels), lambda i: (i, 0)),
+            pl.BlockSpec(dstep.shape, whole),
+            pl.BlockSpec((TILE_D, LANES), lambda i: (i, channels // LANES)),
+            pl.BlockSpec(dbc.shape, whole),
+            pl.BlockSpec((w_bct.shape[0], TILE_D), lambda i: (0, i)),
+        ],
         out_specs=[pl.BlockSpec((rows, TILE_D), lambda i: (0, i))] * ranks,
         out_shape=[jax.ShapeDtypeStruct((rows, depth), bf16)] * ranks,
         scratch_shapes=[pltpu.VMEM((tokens, TILE_D), bf16)],
-        compiler_params=params(),
-        cost_estimate=cost(2 * tokens * depth * inner, 4 * depth * inner),
+        compiler_params=params(32),
+        cost_estimate=cost(2 * tokens * depth * 1920, 4 * depth * 1920),
         name="normed_term",
-    )(rank, *flat)
+    )(rank, dx, w_a, dgate, w_b, dstep, w_a, dbc, w_bct)
 
 
 def norm_back_kernel(rank_ref, a_ref, b_ref, hidden_ref, cot_ref, gain_ref, out_ref, dgain_ref):
@@ -748,12 +844,14 @@
         ),
         out_shape=[jax.ShapeDtypeStruct((rows, depth), bf16), jax.ShapeDtypeStruct((8, depth), f32)],
         compiler_params=params(),
+        cost_estimate=cost(4 * 10**9, 12 * 10**6),
         name="norm_backward",
     )(rank, a, b, hidden, cot, gain_rows)
 
 
-def after(v, *done):
-    return lax.optimization_barrier((v, *done))[0]
+def fence(*values):
+    leaves, tree = jax.tree.flatten(values)
+    return jax.tree.unflatten(tree, lax.optimization_barrier(leaves))
 
 
 def outer_from(v, k):
@@ -783,29 +881,17 @@
     return order
 
 
-def dp_pieces(piece, ready=None):
+def outer_blocks(own, here, back, ks):
+    rows = own.shape[0]
+    return [
+        (here[i * rows:(i + 1) * rows].astype(f32) + back[i * rows:(i + 1) * rows].astype(f32)).astype(bf16)
+        for i in range(len(ks))
+    ]
+
+
+def outer_send(blocks, ks):
     n = lax.axis_size("dp") // 2
-    found = [None] * (2 * n)
-    start = piece if ready is None else after(piece, ready)
-    arrived = {0: start}
-    for k in hops(n):
-        arrived[k] = outer_from(start, k)
-    for k in [0] + hops(n):
-        found[2 * k], found[2 * k + 1] = arrived[k], inner_flip(arrived[k])
-    return found, arrived[hops(n)[-1]]
-
-
-def dp_scatter(blocks, ready=None):
-    n = lax.axis_size("dp") // 2
-    total, last = None, ready
-    for k in hops(n)[::-1] + [0]:
-        send = blocks[2 * k + 1] if last is None else after(blocks[2 * k + 1], last)
-        last = inner_flip(send)
-        here = blocks[2 * k].astype(f32) + last.astype(f32)
-        if k > 0:
-            here = outer_from(here.astype(bf16), n - k).astype(f32)
-        total = here if total is None else total + here
-    return total, last
+    return [outer_from(block, n - k) for block, k in zip(blocks, ks)]
 
 
 def dp_sum(v):
@@ -866,8 +952,6 @@
     n = size // 2
     place, rank = lax.axis_index("dp"), lax.axis_index("mp")
     outer, inner = place // 2, place % 2
-    slot = jnp.arange(size)
-    idx = (((outer + slot // 2) % n) * 2 + (inner ^ (slot % 2))).astype(jnp.int32)
     rank1 = rank.reshape(1).astype(jnp.int32)
     rows, _, channels = in_weight.shape
     heads = head_table.shape[1]
@@ -875,71 +959,147 @@
     share = bc_weight.shape[1] // ranks
     spare = LANES - share - heads
 
+    ks = hops(n)
+    near_ks, far_k = ks[:-1], ks[-1]
+
+    def members(order):
+        return jnp.stack([((outer + k) % n) * 2 + (inner ^ j) for k, j in order]).astype(jnp.int32)
+
+    first = [(0, 0), (0, 1)]
+    idx = members(first + [(k, 0) for k in ks] + [(k, 1) for k in ks])
+    idx_c = members(first + [(k, j) for j in (0, 1) for k in near_ks] + [(far_k, 0), (far_k, 1)])
+    sizes = (1, 1, n - 1, n - 1)
+    width = depth // ranks
+
     own_bc = lax.dynamic_slice_in_dim(bc_weight, rank * share, share, 1)
-    set_a = jnp.concatenate([in_weight[:, 1], own_bc, step_weight, jnp.zeros((rows, spare), f32)], axis=1)
-    a_pieces, a_last = dp_pieces(set_a.astype(bf16))
-    b_pieces, b_last = dp_pieces(in_weight[:, 0].astype(bf16), a_last)
-    c_pieces, _ = dp_pieces(out_weight.T.astype(bf16), b_last)
-    cot = in_rank_order(mp_pieces(cotangent), rank, 1)
-
+    set_a = jnp.concatenate([in_weight[:, 1], own_bc, step_weight, jnp.zeros((rows, spare), f32)], axis=1).astype(bf16)
+    set_b = in_weight[:, 0].astype(bf16)
+    set_c = out_weight.T.astype(bf16)
+    wide_a = set_a.shape[1]
+
+    a_z = [outer_from(set_a, k) for k in ks]
+    own_x = inner_flip(jnp.concatenate([set_a, set_b, set_c], axis=1))
+    cot_far = rank_flip(cotangent, 2)
     gain_rows = pad_rows(norm_gain[None])
-    normed_low, normed_t, cot_t = prepare(hidden, gain_rows, cot)
+    normed_low, normed_t = prepare(hidden, gain_rows)
     aux, seg_row = segment_facts(segments)
-    conv_rows, bc_rows = pad_rows(conv_table), pad_rows(bc_table)
     head_rows = pad_lanes(pad_rows(head_table))
-    expand = head_expand(channels)
-
-    x_pre, small, w_a = project(normed_low, a_pieces, idx, channels)
-    bc_pre = in_rank_order(mp_pieces(small[:share].astype(bf16)), rank, 0).T.astype(f32)
-    step_pre = pad_lanes(small[share:share + heads].T)
-    facts = (aux, seg_row, conv_rows, bc_rows, head_rows, expand)
+    facts = (aux, seg_row, pad_rows(conv_table), pad_rows(bc_table), head_rows, head_expand(channels))
+    set_a, set_b, set_c, a_z, own_x, cot_far, normed_low, normed_t, facts = fence(
+        set_a, set_b, set_c, a_z, own_x, cot_far, normed_low, normed_t, facts
+    )
+    a_own, b_own, c_own = own_x[:, :wide_a], own_x[:, wide_a:wide_a + channels], own_x[:, wide_a + channels:]
+
+    b_z = [outer_from(set_b, k) for k in ks]
+    a_z = jnp.concatenate(a_z, axis=0)
+    a_x = inner_flip(a_z)
+    cot, cot_t = join_columns([cotangent, rank_flip(cotangent, 1), cot_far, rank_flip(cot_far, 1)], rank1)
+    set_c, b_z, a_z, a_x, a_own, b_own, c_own, cot, cot_t, normed_low = fence(
+        set_c, b_z, a_z, a_x, a_own, b_own, c_own, cot, cot_t, normed_low
+    )
+
+    c_near = [outer_from(set_c, k) for k in near_ks]
+    b_z = jnp.concatenate(b_z, axis=0)
+    b_x = inner_flip(b_z)
+    x_pre, small, bc_share, w_a, w_bct_share = project(normed_low, [set_a, a_own, a_z, a_x], idx, channels, share)
+    bc_pre, step_pre = join_small([bc_share] + [rank_flip(bc_share, r) for r in (1, 2, 3)], small, rank1)
+    set_c, c_near, b_z, b_x, x_pre, bc_pre, step_pre, w_bct_share = fence(
+        set_c, c_near, b_z, b_x, x_pre, bc_pre, step_pre, w_bct_share
+    )
+
+    c_far = outer_from(set_c, far_k)
+    c_near = jnp.concatenate(c_near, axis=0)
+    c_near_x = inner_flip(c_near)
     mixed, states = ssd_forward(x_pre, bc_pre, step_pre, *facts)
-    gate_pre, square, w_b = gate_forward(normed_low, mixed, b_pieces, idx)
+    c_far, c_near, c_near_x, mixed, states, w_bct_share = fence(c_far, c_near, c_near_x, mixed, states, w_bct_share)
+
+    c_far_x = inner_flip(c_far)
+    w_bct = [w_bct_share] + [rank_flip(w_bct_share, r) for r in (1, 2, 3)]
+    gate_pre, square, w_b = gate_forward(normed_low, mixed, [set_b, b_own, b_z, b_x], idx)
+    c_far_x, w_bct, gate_pre, square, mixed = fence(c_far_x, w_bct, gate_pre, square, mixed)
+
+    conv_rows = facts[2]
     square = mp_sum_direct(square)
+    gout, inner_dot, w_c = grad_gout(
+        cot, gate_pre, mixed, conv_rows, [set_c, c_own, c_near, c_near_x, c_far, c_far_x], idx_c
+    )
+    square, gout, inner_dot, w_c = fence(square, gout, inner_dot, w_c)
+
+    inner_dot = mp_sum_direct(inner_dot)
     gated_out = gated_norm(gate_pre, mixed, square, conv_rows, channels * ranks)
-    shard_c, c_flip = dp_scatter(weight_grad(cot_t, [gated_out], idx))
-
-    gout, inner_dot, w_c = grad_gout(cot, gate_pre, mixed, conv_rows, c_pieces, idx)
-    inner_dot = mp_sum_direct(inner_dot)
+    gc_own, gc_own1, gc_here, gc_send = weight_grad(cot_t, gated_out, idx, sizes)
+    inner_dot, gated_out, gc_own, gc_own1, gc_here, gc_send = fence(
+        inner_dot, gated_out, gc_own, gc_own1, gc_here, gc_send
+    )
+
+    gc_back = inner_flip(gc_send)
     dmixed, dgate, dgain = gate_backward(gate_pre, gout, mixed, square, inner_dot, conv_rows, channels * ranks)
-    shard_b, b_flip = dp_scatter(weight_grad(normed_t, [dgate], idx), c_flip)
-
-    near, far = mp_reduce(out_partial(gated_out, w_c, rank1, ranks))
-    width = depth // ranks
+    dmixed, dgate, dgain, w_c, w_bct = fence(dmixed, dgate, dgain, w_c, w_bct)
+    gb_own, gb_own1, gb_here, gb_send = weight_grad(normed_t, dgate, idx, sizes)
+    partial = out_partial(gated_out, w_c, rank1, ranks)
+    w_bct = join_rows(w_bct, rank1)
+    gc_back, gb_own, gb_own1, gb_here, gb_send, partial, dmixed, w_bct = fence(
+        gc_back, gb_own, gb_own1, gb_here, gb_send, partial, dmixed, w_bct
+    )
+    out_far = (partial[2].astype(f32) + rank_flip(partial[3], 1).astype(f32)).astype(bf16)
+    out_near = partial[0].astype(f32) + rank_flip(partial[1], 1).astype(f32)
+    gc_send_z = outer_blocks(gc_own, gc_here, gc_back, ks)
+    out_far, out_near, gc_send_z, gb_send, dmixed, w_bct = fence(out_far, out_near, gc_send_z, gb_send, dmixed, w_bct)
+
+    c_got = outer_send(gc_send_z, ks)
+    gb_back = inner_flip(gb_send)
+    out_got = rank_flip(out_far, 2)
+    dx, dbc, dbc_t, dstep, dstep_t, dconv, dbct_part, dheads = ssd_backward(
+        x_pre, bc_pre, step_pre, *facts, mixed, dmixed, states
+    )
+    c_got, gb_back, out_got, dx, dbc, dbc_t, dstep, dstep_t, dconv, dbct_part, dheads, gc_own1, gb_own1 = fence(
+        c_got, gb_back, out_got, dx, dbc, dbc_t, dstep, dstep_t, dconv, dbct_part, dheads, gc_own1, gb_own1
+    )
+
+    b_got = outer_send(outer_blocks(gb_own, gb_here, gb_back, ks), ks)
+    c_own_got = inner_flip(gc_own1)
+    ga_own, ga_own1, ga_here, ga_send = weight_grad(normed_t, dx, idx, sizes)
+    ga_own, ga_own1, ga_here, ga_send, dx, dbc_t = fence(ga_own, ga_own1, ga_here, ga_send, dx, dbc_t)
+    ga_back = inner_flip(ga_send)
+    term = normed_term(dx, dgate, dstep, dbc, w_a, w_b, w_bct, rank1, ranks)
+    term, dbc_t = fence(term, dbc_t)
+    near, far = mp_reduce(term)
+    parts = lax.all_to_all(dbc_t.reshape(ranks, share, tokens), "mp", 0, 0)
+    dbc_share = jnp.sum(parts.astype(f32), axis=0).astype(bf16)
+    dsmall_t = jnp.concatenate([dbc_share, dstep_t, jnp.zeros((LANES - share - 16, tokens), bf16)], axis=0)
+    gs_own, gs_own1, gs_here, gs_send = weight_grad(normed_t, dsmall_t, idx, sizes, turned=True)
+    b_got, c_own_got, ga_back, near, far, gs_own, gs_own1, gs_here, gs_send = fence(
+        b_got, c_own_got, ga_back, near, far, gs_own, gs_own1, gs_here, gs_send
+    )
+
+    def total(own, own_got, got):
+        value = own.astype(f32) + own_got.astype(f32)
+        for part in got:
+            value = value + part.astype(f32)
+        return value
+
+    a_got = outer_send(outer_blocks(ga_own, ga_here, ga_back, ks), ks)
+    mine, dgain_mine = norm_backward(near, far, hidden, cot, gain_rows, rank1)
+    a_own_got, b_own_got = inner_flip(ga_own1), inner_flip(gb_own1)
+    gs_back, s_own_got = inner_flip(gs_send), inner_flip(gs_own1)
+    s_got = outer_send(outer_blocks(gs_own, gs_here, gs_back, ks), ks)
+    input_grad = join_rows(mp_pieces(mine), rank1)
     resid = lax.dynamic_slice_in_dim(hidden, rank * width, width, 1).astype(f32)
-    output = (resid + near + far.astype(f32)).astype(bf16)
-
-    dx, dbc_part, dstep, dconv, dbct_part, dheads = ssd_backward(
-        x_pre, bc_pre, step_pre, *facts, mixed, dmixed, states
-    )
-    dbc_low_part = dbc_part.astype(bf16).T
-    parts = [lax.dynamic_slice_in_dim(dbc_low_part, (rank ^ r) * share, share, 0) for r in range(ranks)]
-    near, far = mp_reduce(parts)
-    dbc_low = (near + far.astype(f32)).astype(bf16).T
-    dsmall = jnp.concatenate([dbc_low, dstep[:, :heads].astype(bf16), jnp.zeros((tokens, spare), bf16)], axis=1)
-    shard_a, _ = dp_scatter(weight_grad(normed_t, [dx, dsmall], idx), b_flip)
-
-    term = normed_term([(dx, w_a[:, :channels]), (dsmall, w_a[:, channels:]), (dgate, w_b)], rank1, ranks)
-    near, far = mp_reduce(term)
-    mine, dgain_mine = norm_backward(near, far, hidden, cot, gain_rows, rank1)
-    input_grad = in_rank_order(mp_pieces(mine), rank, 0)
-
-    dconv_all = jnp.concatenate([dconv[:5], dgain[:1]], axis=0)
-    packed = jnp.concatenate(
-        [mp_sum(dbct_part[:5].reshape(-1, LANES)), dconv_all.reshape(-1, LANES), dheads], axis=0
-    )
-    packed = dp_sum(packed)
-    cut1 = 5 * 2
-    cut2 = cut1 + 6 * channels // LANES
-    total_bct = packed[:cut1].reshape(5, 2 * LANES)
-    total_conv = packed[cut1:cut2].reshape(6, channels)
-    total_head = packed[cut2:cut2 + 3, :heads]
-    total_gain = dp_sum(mp_sum(dgain_mine[:1].reshape(-1, LANES))).reshape(-1)
-
-    shard_x = shard_a[:, :channels]
-    shard_bc = in_rank_order(mp_pieces(shard_a[:, channels:channels + share]), rank, 1)
-    shard_step = shard_a[:, channels + share:channels + share + heads]
-    in_m, in_w = advance(in_weight, in_moment, jnp.stack([shard_b, shard_x], axis=1))
+    output = (resid + out_near + out_got.astype(f32)).astype(bf16)
+    shard_c = total(gc_own, c_own_got, c_got)
+    shard_b = total(gb_own, b_own_got, b_got)
+    shard_a = total(ga_own, a_own_got, a_got)
+    shard_s = total(gs_own, s_own_got, s_got)
+
+    packed = dp_sum(jnp.concatenate([dconv + dgain, mp_sum(dbct_part), dheads], axis=1))
+    total_conv = packed[:6, :channels]
+    total_bct = packed[:5, channels:channels + 2 * LANES]
+    total_head = packed[:3, channels + 2 * LANES:channels + 2 * LANES + heads]
+    total_gain = dp_sum(mp_sum(dgain_mine))[0]
+
+    shard_bc = in_rank_order(mp_pieces(shard_s[:, :share]), rank, 1)
+    shard_step = shard_s[:, share:share + heads]
+    in_m, in_w = advance(in_weight, in_moment, jnp.stack([shard_b, shard_a], axis=1))
     bc_m, bc_w = advance(bc_weight, bc_moment, shard_bc)
     step_m, step_w = advance(step_weight, step_moment, shard_step)
     out_m, out_w = advance(out_weight, out_moment, shard_c.T)

time: 468 us -> 350 us (0.75); the launches traced: 460 us -> 349 us
  waiting for transfers between devices: 170 us -> 87.9 us
  Pallas kernels: 132 us -> 97.5 us
  other arithmetic: 24.5 us -> 30.2 us
  starting transfers between devices: 77.4 us -> 72.3 us
    ppermute x26 -> x15, waiting for transfers between devices: 61 us -> 6.16 us  [inner_flip(): lax.ppermute(v, 'dp', [(d ^ 1, d) for d in range(lax.axis_size('dp'))])]
    ppermute x31, waiting for transfers between devices: 48.1 us -> 12.2 us  [rank_flip(): lax.ppermute(v, 'mp', [(m ^ bit, m) for m in range(lax.axis_size('mp'))])]
    unnamed x153 -> x238, local copies, waits for them, and re-layouts: 17.1 us -> 47.4 us
    dynamic_update_slice x16 -> x4, local copies, waits for them, and re-layouts: 21 us -> 5.37 us  [in_rank_order(): lax.dynamic_update_slice_in_dim(full, piece, (rank ^ r) * width, axis)]
    ppermute x18 -> x21, waiting for transfers between devices: 54.9 us -> 67.5 us  [outer_from(): lax.ppermute(v, 'dp', [((o + k) % n * 2 + x, o * 2 + x) for o in range(n)...]
    ppermute x26 -> x15, starting transfers between devices: 25.3 us -> 15.9 us  [inner_flip(): lax.ppermute(v, 'dp', [(d ^ 1, d) for d in range(lax.axis_size('dp'))])]
    ppermute x4, waiting for transfers between devices: 6.39 us -> 0.76 us  [outer_flip(): lax.ppermute(v, 'dp', [((o ^ bit) * 2 + x, o * 2 + x) for o in range(n) f...]
    pallas_call x1, Pallas kernels: 7.35 us -> 2.27 us  [prepare(): pl.pallas_call(prepare_kernel, grid=(tokens // TILE,), in_specs=[block, p...]
  transfers between devices with their start and end apart: 79 -> 72, of which waited for: 26 -> 20; matrix products, arithmetic and copies ran while one was open for 14% -> 13% of each run, Pallas kernels for 15% -> 27%
where the time goes in v3:
time: 350 us; the launch traced here: 349 us
  Pallas kernels  97.5 us (28%)
  waiting for transfers between devices  87.9 us (25%)
  starting transfers between devices  72.3 us (21%)
  local copies, waits for them, and re-layouts  58.7 us (17%)
  other arithmetic  30.2 us (9%)
    ppermute x21, waiting for transfers between devices, outer_from(): lax.ppermute(v, 'dp', [((o + k) % n * 2 + x, o * 2 + x) for o in range(n)...  67.5 us
    unnamed x238, local copies, waits for them, and re-layouts  47.4 us
    ppermute x21, starting transfers between devices, outer_from(): lax.ppermute(v, 'dp', [((o + k) % n * 2 + x, o * 2 + x) for o in range(n)...  30.7 us
    pallas_call x1, Pallas kernels, ssd_backward(): pl.pallas_call(ssd_backward_kernel, grid=(count,), in_specs=common_specs(...  26.3 us
    ppermute x31, starting transfers between devices, rank_flip(): lax.ppermute(v, 'mp', [(m ^ bit, m) for m in range(lax.axis_size('mp'))])  18.1 us
    ppermute x15, starting transfers between devices, inner_flip(): lax.ppermute(v, 'dp', [(d ^ 1, d) for d in range(lax.axis_size('dp'))])  15.9 us
    pallas_call x4, Pallas kernels, weight_grad(): pl.pallas_call(functools.partial(weight_grad_kernel, rows=rows, turned=tu...  14.6 us
    ppermute x31, waiting for transfers between devices, rank_flip(): lax.ppermute(v, 'mp', [(m ^ bit, m) for m in range(lax.axis_size('mp'))])  12.2 us
  transfers between devices with their start and end apart: 72, of which 20 were waited for; matrix products, arithmetic and copies ran while one was open for 13% of the time, Pallas kernels for 27%

profile of v3, /device:TPU:0, one launch (start us, length us, event | category | flops | bytes accessed | tf_op | source)
XLA Modules:
  0.0 348.8 jit_solution(7314843050965566508)
XLA Ops:
  4.2 5.1 %collective-permute-start = (bf16[192,896]{1,0:T(8,128)(2,1)S(1)}, bf16[192,896]{1,0:T(8,128)(2,1)}, u32[]{:S(2)}, u32[]{:S(2)}) collective-permute-start(bf16[192,896]{1,0:T(8,128)(2,1)S(1)} %pad_maximum_fusion.refs_0_), channel_id=1, source_target_pairs={{8,0},{12,4},{16,8},{20,12},{24,16},{28,20},{0,24},{4,28},{9,1},{1... | collective-permute-start | bytes 1032200 | tf_op jit(solution)/shard_map/ppermute | solution.py:859
  14.8 1.9 copy-done.29
  16.7 2.3 prepare.1
  18.9 1.7 copy-done
  20.6 1.7 copy-done.51
  26.2 12.5 %collective-permute-done.2 = bf16[192,896]{1,0:T(8,128)(2,1)S(1)} collective-permute-done((bf16[192,896]{1,0:T(8,128)(2,1)S(1)}, bf16[192,896]{1,0:T(8,128)(2,1)S(1)}, u32[]{:S(2)}, u32[]{:S(2)}) %collective-permute-start.2) | collective-permute-done | bytes 344096 | tf_op jit(solution)/shard_map/ppermute | solution.py:859
  40.9 1.6 collective-permute-start.8
  42.4 2.6 collective-permute-start.5
  46.5 3.3 join_columns.1
  49.8 1.7 copy-done.3
  51.5 1.6 copy-done.56
  53.2 6.3 %collective-permute-done.5 = bf16[192,768]{1,0:T(8,128)(2,1)S(1)} collective-permute-done((bf16[192,768]{1,0:T(8,128)(2,1)S(1)}, bf16[192,768]{1,0:T(8,128)(2,1)S(1)}, u32[]{:S(2)}, u32[]{:S(2)}) %collective-permute-start.5) | collective-permute-done | bytes 294944 | tf_op jit(solution)/shard_map/ppermute | solution.py:859
  59.5 10.3 %collective-permute-done.7 = bf16[192,768]{1,0:T(8,128)(2,1)S(1)} collective-permute-done((bf16[192,768]{1,0:T(8,128)(2,1)S(1)}, bf16[192,768]{1,0:T(8,128)(2,1)S(1)}, u32[]{:S(2)}, u32[]{:S(2)}) %collective-permute-start.7) | collective-permute-done | bytes 294944 | tf_op jit(solution)/shard_map/ppermute | solution.py:859
  72.8 1.9 copy-done.52
  74.7 5.3 %project.1 = (f32[1024,768]{1,0:T(8,128)S(1)}, f32[128,1024]{1,0:T(8,128)S(1)}, bf16[64,1024]{1,0:T(8,128)(2,1)S(1)}, bf16[1536,896]{1,0:T(8,128)(2,1)S(1)}, bf16[64,1536]{1,0:T(8,128)(2,1)S(1)}) custom-call(s32[8]{0:T(128)S(1)} %stack.110.idx_ref, bf16[1024,1536]{1,0:T(8,128)(2,1)S(1)} %copy-done.52, bf16[192,896]{1,0:T(8,128)(2,1)S(1)} %pad_maximum_fusion.refs_0_, ...), custom_call_target="tpu_custom_call" | custom-call | flops 2818572288 | bytes 8257536 | tf_op jit(solution)/shard_map/project/pallas_call | solution.py:524
  80.1 1.6 collective-permute-start.15
  81.9 3.1 collective-permute-start.11
  86.4 1.9 collective-permute-done.16.refs_3_
  89.7 2.7 collective-permute-done.11
  92.4 6.4 %collective-permute-done.12 = bf16[192,768]{1,0:T(8,128)(2,1)S(1)} collective-permute-done((bf16[192,768]{1,0:T(8,128)(2,1)S(1)}, bf16[192,768]{1,0:T(8,128)(2,1)S(1)}, u32[]{:S(2)}, u32[]{:S(2)}) %collective-permute-start.12) | collective-permute-done | bytes 294944 | tf_op jit(solution)/shard_map/ppermute | solution.py:859
  100.6 11.1 %ssd_forward.1 = (f32[1024,768]{1,0:T(8,128)S(1)}, bf16[8,128,768]{2,1,0:T(8,128)(2,1)S(1)}) custom-call(f32[1024,768]{1,0:T(8,128)S(1)} %get-tuple-element.225.x_ref.xb_ref, f32[1024,768]{1,0:T(8,128)S(1)} %get-tuple-element.225.x_ref.xb_ref, f32[1024,256]{1,0:T(8,128)S(1)} %get-tuple-element.226.bc_ref.bcb_ref, ...), custom_call_target="tpu_custom_call" | custom-call | flops 14000000000 | bytes 40000000 | tf_op jit(solution)/shard_map/ssd_forward/pallas_call | solution.py:283
  112.9 1.9 collective-permute-done.17.refs_4_
  117.3 1.6 collective-permute-start.21
  122.2 1.9 copy-done.53
  124.1 5.6 %gate_forward.1 = (f32[1024,768]{1,0:T(8,128)S(1)}, f32[8,1024]{1,0:T(8,128)S(1)}, bf16[1536,768]{1,0:T(8,128)(2,1)S(1)}) custom-call(s32[8]{0:T(128)S(1)} %stack.110.idx_ref, bf16[1024,1536]{1,0:T(8,128)(2,1)S(1)} %copy-done.53, f32[1024,768]{1,0:T(8,128)S(1)} %get-tuple-element.248.mixed_ref, bf16[192,768]{1,0:T(8,128)(2,1)S(1)} %copy-done.9, ...), custom_call_target="tpu_custom_call" | custom-call | flops 2415919104 | bytes 9437184 | tf_op jit(solution)/shard_map/gate_forward/pallas_call | solution.py:575
  129.7 1.6 collective-permute-start.24
  132.0 5.1 %grad_gout.1 = (f32[1024,768]{1,0:T(8,128)S(1)}, f32[8,1024]{1,0:T(8,128)S(1)}, bf16[1536,768]{1,0:T(8,128)(2,1)S(1)}) custom-call(s32[8]{0:T(128)S(1)} %stack.111.idx_ref, bf16[1024,1536]{1,0:T(8,128)(2,1)S(1)} %copy-done.4, f32[1024,768]{1,0:T(8,128)S(1)} %get-tuple-element.247.gate_ref, f32[1024,768]{1,0:T(8,128)S(1)} %get-tuple-element.248.mixed_ref, ...), custom_call_target="tpu_custom_call" | custom-call | flops 2415919104 | bytes 9437184 | tf_op jit(solution)/shard_map/grad_gout/pallas_call | solution.py:641
  137.1 1.6 collective-permute-start.27
  140.8 3.9 %weight_grad.4 = (bf16[192,768]{1,0:T(8,128)(2,1)S(1)}, bf16[192,768]{1,0:T(8,128)(2,1)S(1)}, bf16[576,768]{1,0:T(8,128)(2,1)S(1)}, bf16[576,768]{1,0:T(8,128)(2,1)S(1)}) custom-call(s32[8]{0:T(128)S(1)} %stack.110.idx_ref, bf16[1536,1024]{1,0:T(8,128)(2,1)S(1)} %copy-done.57, bf16[1024,768]{1,0:T(8,128)(2,1)S(1)} %gated_norm.1.rhs_ref.lhs_ref), custom_call_target="tpu_custom_call" | custom-call | flops 2415919104 | bytes 4718592 | tf_op jit(solution)/shard_map/weight_grad/pallas_call | solution.py:730
  146.1 3.4 gate_backward.1
  152.0 3.9 %weight_grad.5 = (bf16[192,768]{1,0:T(8,128)(2,1)S(1)}, bf16[192,768]{1,0:T(8,128)(2,1)S(1)}, bf16[576,768]{1,0:T(8,128)(2,1)S(1)}, bf16[576,768]{1,0:T(8,128)(2,1)S(1)}) custom-call(s32[8]{0:T(128)S(1)} %stack.110.idx_ref, bf16[1536,1024]{1,0:T(8,128)(2,1)S(1)} %copy-done.1, bf16[1024,768]{1,0:T(8,128)(2,1)S(1)} %get-tuple-element.275.rhs_ref.gg_ref), custom_call_target="tpu_custom_call" | custom-call | flops 2415919104 | bytes 4718592 | tf_op jit(solution)/shard_map/weight_grad/pallas_call | solution.py:730
  156.6 4.4 %out_partial.1 = (bf16[1024,384]{1,0:T(8,128)(2,1)S(1)}, bf16[1024,384]{1,0:T(8,128)(2,1)S(1)}, bf16[1024,384]{1,0:T(8,128)(2,1)S(1)}, bf16[1024,384]{1,0:T(8,128)(2,1)S(1)}) custom-call(s32[1]{0:T(128)} %bitcast.22.rank_ref, bf16[1024,768]{1,0:T(8,128)(2,1)S(1)} %gated_norm.1.rhs_ref.lhs_ref, bf16[1536,768]{1,0:T(8,128)(2,1)S(1)} %get-tuple-element.281.w_ref), custom_call_target="tpu_custom_call" | custom-call | flops 2415919104 | bytes 4718592 | tf_op jit(solution)/shard_map/out_partial/pallas_call | solution.py:760
  161.0 6.1 %collective-permute-done.29 = bf16[576,768]{1,0:T(8,128)(2,1)S(1)} collective-permute-done((bf16[576,768]{1,0:T(8,128)(2,1)S(1)}, bf16[576,768]{1,0:T(8,128)(2,1)S(1)}, u32[]{:S(2)}, u32[]{:S(2)}) %collective-permute-start.29) | collective-permute-done | bytes 884768 | tf_op jit(solution)/shard_map/ppermute | solution.py:868
  167.8 1.6 collective-permute-done.30
  172.8 2.9 collective-permute-start.33
  177.8 26.3 %ssd_backward.1 = (bf16[1024,768]{1,0:T(8,128)(2,1)S(1)}, bf16[1024,256]{1,0:T(8,128)(2,1)S(1)}, bf16[256,1024]{1,0:T(8,128)(2,1)S(1)}, bf16[1024,128]{1,0:T(8,1...) custom-call(f32[1024,768]{1,0:T(8,128)S(1)} %copy-done.61, ...), custom_call_target="tpu_custom_call" | custom-call | flops 28000000000 | bytes 80000000 | tf_op jit(solution)/shard_map/ssd_backward/pallas_call | solution.py:312
  211.2 2.4 add_convert_fusion.6
  215.1 2.3 collective-permute-start.38
  219.1 2.0 copy-done.65
  221.1 4.8 %weight_grad.6 = (bf16[192,768]{1,0:T(8,128)(2,1)S(1)}, bf16[192,768]{1,0:T(8,128)(2,1)S(1)}, bf16[576,768]{1,0:T(8,128)(2,1)S(1)}, bf16[576,768]{1,0:T(8,128)(2,1)}) custom-call(s32[8]{0:T(128)S(1)} %copy-done.38, bf16[1536,1024]{1,0:T(8,128)(2,1)S(1)} %copy-done.2, bf16[1024,768]{1,0:T(8,128)(2,1)S(1)} %copy-done.65), custom_call_target="tpu_custom_call" | custom-call | flops 2415919104 | bytes 4718592 | tf_op jit(solution)/shard_map/weight_grad/pallas_call | solution.py:730
  230.4 10.7 %normed_term.1 = (bf16[256,1536]{1,0:T(8,128)(2,1)S(1)}, bf16[256,1536]{1,0:T(8,128)(2,1)}, bf16[256,1536]{1,0:T(8,128)(2,1)S(1)}, bf16[256,1536]{1,0:T(8,128)(2,1)}) custom-call(s32[1]{0:T(128)} %bitcast.22.rank_ref, bf16[1024,768]{1,0:T(8,128)(2,1)S(1)} %copy-done.66, bf16[1536,896]{1,0:T(8,128)(2,1)S(1)} %copy-done.63, bf16[1024,768]{1,0:T(8,128)(2,1)S(1)} %copy-done.40, ...), custom_call_target="tpu_custom_call" | custom-call | flops 6039797760 | bytes 11796480 | tf_op jit(solution)/shard_map/normed_term/pallas_call | solution.py:793
  242.9 4.1 %all-to-all-start = ((bf16[4,64,1024]{2,1,0:T(8,128)(2,1)}), bf16[4,64,1024]{2,1,0:T(8,128)(2,1)}, u32[]{:S(2)}, u32[]{:S(2)}) async-start(bf16[4,64,1024]{2,1,0:T(8,128)(2,1)} %bitcast.47), calls=%async_computation | async-start | bytes 1048576 | tf_op jit(solution)/shard_map/all_to_all | solution.py:1067
  249.0 3.0 add_convert_fusion.1
  255.9 1.8 reduce_sum.12
  257.7 1.7 add_convert_fusion
  260.3 2.1 weight_grad.7
  263.8 1.8 collective-permute-start.40
  267.2 11.6 %collective-permute-done.39 = bf16[192,768]{1,0:T(8,128)(2,1)S(1)} collective-permute-done((bf16[192,768]{1,0:T(8,128)(2,1)S(1)}, bf16[192,768]{1,0:T(8,128)(2,1)S(1)}, u32[]{:S(2)}, u32[]{:S(2)}) %collective-permute-start.39) | collective-permute-done | bytes 294944 | tf_op jit(solution)/shard_map/ppermute | solution.py:859
  278.9 1.8 collective-permute-start.54
  283.2 2.1 add_bitcast_fusion.1
  286.6 2.2 add_convert_fusion.5
  289.5 1.8 collective-permute-start.68
  292.3 3.2 collective-permute-start.56
  296.7 1.6 collective-permute-start.46
  299.1 2.8 collective-permute-done.55
  309.9 1.7 dynamic_update_slice.13
  311.5 5.6 %collective-permute-done.59 = f32[192,64]{1,0:T(8,128)} collective-permute-done((f32[192,64]{1,0:T(8,128)S(1)}, f32[192,64]{1,0:T(8,128)}, u32[]{:S(2)}, u32[]{:S(2)}) %collective-permute-start.59) | collective-permute-done | bytes 49184 | tf_op jit(solution)/shard_map/ppermute | solution.py:872
  317.1 3.5 %collective-permute-start.51 = (bf16[192,768]{1,0:T(8,128)(2,1)}, bf16[192,768]{1,0:T(8,128)(2,1)}, u32[]{:S(2)}, u32[]{:S(2)}) collective-permute-start(bf16[192,768]{1,0:T(8,128)(2,1)} %get-tuple-element.438), channel_id=1, source_target_pairs={{8,0},{12,4},{16,8},{20,12},{24,16},{28,20},{0,24},{4,28},{9,1},{1... | collective-permute-start | bytes 884744 | tf_op jit(solution)/shard_map/ppermute | solution.py:859
  324.8 11.4 %collective-permute-done.51 = bf16[192,768]{1,0:T(8,128)(2,1)} collective-permute-done((bf16[192,768]{1,0:T(8,128)(2,1)}, bf16[192,768]{1,0:T(8,128)(2,1)}, u32[]{:S(2)}, u32[]{:S(2)}) %collective-permute-start.51) | collective-permute-done | bytes 294944 | tf_op jit(solution)/shard_map/ppermute | solution.py:859
  337.5 2.2 multiply_subtract_fusion
  339.7 1.9 copy.101
  341.7 1.9 copy.102
  345.1 1.8 multiply_subtract_fusion.2
  346.9 1.9 join_rows.3
  (418 shorter events, 92.8 us)
Async XLA Ops:
  4.2 20.7 %collective-permute-start = (bf16[192,896]{1,0:T(8,128)(2,1)S(1)}, bf16[192,896]{1,0:T(8,128)(2,1)}, u32[]{:S(2)}, u32[]{:S(2)}) collective-permute-start(bf16[192,896]{1,0:T(8,128)(2,1)S(1)} %pad_maximum_fusion.refs_0_), channel_id=1, source_target_pairs={{8,0},{12,4},{16,8},{20,12},{24,16},{28,20},{0,24},{4,28},{9,1},{1... | collective-permute-start | bytes 1032200 | tf_op jit(solution)/shard_map/ppermute | solution.py:859
  9.3 16.8 %collective-permute-start.1 = (bf16[192,896]{1,0:T(8,128)(2,1)S(1)}, bf16[192,896]{1,0:T(8,128)(2,1)S(1)}, u32[]{:S(2)}, u32[]{:S(2)}) collective-permute-start(bf16[192,896]{1,0:T(8,128)(2,1)S(1)} %pad_maximum_fusion.refs_0_), channel_id=1, source_target_pairs={{24,0},{28,4},{0,8},{4,12},{8,16},{12,20},{16,24},{20,28},{25,1},{... | collective-permute-start | bytes 1032200 | tf_op jit(solution)/shard_map/ppermute | solution.py:859
  9.3 29.3 %collective-permute-start.2 = (bf16[192,896]{1,0:T(8,128)(2,1)S(1)}, bf16[192,896]{1,0:T(8,128)(2,1)S(1)}, u32[]{:S(2)}, u32[]{:S(2)}) collective-permute-start(bf16[192,896]{1,0:T(8,128)(2,1)S(1)} %pad_maximum_fusion.refs_0_), channel_id=1, source_target_pairs={{16,0},{20,4},{24,8},{28,12},{0,16},{4,20},{8,24},{12,28},{17,1},{... | collective-permute-start | bytes 1032200 | tf_op jit(solution)/shard_map/ppermute | solution.py:859
  11.5 27.2 %collective-permute-start.3 = (bf16[192,2432]{1,0:T(8,128)(2,1)}, bf16[192,2432]{1,0:T(8,128)(2,1)S(1)}, u32[]{:S(2)}, u32[]{:S(2)}) collective-permute-start(bf16[192,2432]{1,0:T(8,128)(2,1)} %concatenate.27), channel_id=1, source_target_pairs={{4,0},{0,4},{12,8},{8,12},{20,16},{16,20},{28,24},{24,28},{5,1},{1... | collective-permute-start | bytes 2801672 | tf_op jit(solution)/shard_map/ppermute | solution.py:868
  13.0 25.7 %collective-permute-start.4 = (bf16[1024,384]{1,0:T(8,128)(2,1)}, bf16[1024,384]{1,0:T(8,128)(2,1)}, u32[]{:S(2)}, u32[]{:S(2)}) collective-permute-start(bf16[1024,384]{1,0:T(8,128)(2,1)} %refs_0_.1), channel_id=1, source_target_pairs={{2,0},{3,1},{0,2},{1,3},{6,4},{7,5},{4,6},{5,7},{10,8},{11,9},{8,1... | collective-permute-start | bytes 2359304 | tf_op jit(solution)/shard_map/ppermute | solution.py:872
  24.9 21.1 %collective-permute-start.9 = (bf16[1024,384]{1,0:T(8,128)(2,1)}, bf16[1024,384]{1,0:T(8,128)(2,1)S(1)}, u32[]{:S(2)}, u32[]{:S(2)}) collective-permute-start(bf16[1024,384]{1,0:T(8,128)(2,1)} %refs_0_.1), channel_id=1, source_target_pairs={{1,0},{0,1},{3,2},{2,3},{5,4},{4,5},{7,6},{6,7},{9,8},{8,9},{11,10... | collective-permute-start | bytes 2359304 | tf_op jit(solution)/shard_map/ppermute | solution.py:872
  40.7 5.9 %collective-permute-start.10 = (bf16[1024,384]{1,0:T(8,128)(2,1)}, bf16[1024,384]{1,0:T(8,128)(2,1)S(1)}, u32[]{:S(2)}, u32[]{:S(2)}) collective-permute-start(bf16[1024,384]{1,0:T(8,128)(2,1)} %collective-permute-done.4.refs_2_), channel_id=1, source_target_pairs={{1,0},{0,1},{3,2},{2,3},{5,4},{4,5},{7,6},{6,7},{9,8},{8,9},{11,10... | collective-permute-start | bytes 2359304 | tf_op jit(solution)/shard_map/ppermute | solution.py:872
  40.9 29.0 %collective-permute-start.8 = (bf16[576,896]{1,0:T(8,128)(2,1)S(1)}, bf16[576,896]{1,0:T(8,128)(2,1)S(1)}, u32[]{:S(2)}, u32[]{:S(2)}) collective-permute-start(bf16[576,896]{1,0:T(8,128)(2,1)S(1)} %constant_dynamic-update-slice_fusion.refs_2_), channel_id=1, source_target_pairs={{4,0},{0,4},{12,8},{8,12},{20,16},{16,20},{28,24},{24,28},{5,1},{1... | collective-permute-start | bytes 3096584 | tf_op jit(solution)/shard_map/ppermute | solution.py:868
  42.4 17.0 %collective-permute-start.5 = (bf16[192,768]{1,0:T(8,128)(2,1)S(1)}, bf16[192,768]{1,0:T(8,128)(2,1)S(1)}, u32[]{:S(2)}, u32[]{:S(2)}) collective-permute-start(bf16[192,768]{1,0:T(8,128)(2,1)S(1)} %get-tuple-element.198.refs_0_), channel_id=1, source_target_pairs={{8,0},{12,4},{16,8},{20,12},{24,16},{28,20},{0,24},{4,28},{9,1},{1... | collective-permute-start | bytes 884744 | tf_op jit(solution)/shard_map/ppermute | solution.py:859
  45.1 14.4 %collective-permute-start.6 = (bf16[192,768]{1,0:T(8,128)(2,1)S(1)}, bf16[192,768]{1,0:T(8,128)(2,1)S(1)}, u32[]{:S(2)}, u32[]{:S(2)}) collective-permute-start(bf16[192,768]{1,0:T(8,128)(2,1)S(1)} %get-tuple-element.198.refs_0_), channel_id=1, source_target_pairs={{24,0},{28,4},{0,8},{4,12},{8,16},{12,20},{16,24},{20,28},{25,1},{... | collective-permute-start | bytes 884744 | tf_op jit(solution)/shard_map/ppermute | solution.py:859
  46.0 23.8 %collective-permute-start.7 = (bf16[192,768]{1,0:T(8,128)(2,1)S(1)}, bf16[192,768]{1,0:T(8,128)(2,1)S(1)}, u32[]{:S(2)}, u32[]{:S(2)}) collective-permute-start(bf16[192,768]{1,0:T(8,128)(2,1)S(1)} %get-tuple-element.198.refs_0_), channel_id=1, source_target_pairs={{16,0},{20,4},{24,8},{28,12},{0,16},{4,20},{8,24},{12,28},{17,1},{... | collective-permute-start | bytes 884744 | tf_op jit(solution)/shard_map/ppermute | solution.py:859
  70.9 28.0 %collective-permute-start.13 = (bf16[576,768]{1,0:T(8,128)(2,1)S(1)}, bf16[576,768]{1,0:T(8,128)(2,1)}, u32[]{:S(2)}, u32[]{:S(2)}) collective-permute-start(bf16[576,768]{1,0:T(8,128)(2,1)S(1)} %constant_dynamic-update-slice_fusion.3.refs_2_), channel_id=1, source_target_pairs={{4,0},{0,4},{12,8},{8,12},{20,16},{16,20},{28,24},{24,28},{5,1},{1... | collective-permute-start | bytes 2654216 | tf_op jit(solution)/shard_map/ppermute | solution.py:868
  80.1 6.4 %collective-permute-start.15 = (bf16[64,1024]{1,0:T(8,128)(2,1)S(1)}, bf16[64,1024]{1,0:T(8,128)(2,1)S(1)}, u32[]{:S(2)}, u32[]{:S(2)}) collective-permute-start(bf16[64,1024]{1,0:T(8,128)(2,1)S(1)} %get-tuple-element.217.refs_0_), channel_id=1, source_target_pairs={{2,0},{3,1},{0,2},{1,3},{6,4},{7,5},{4,6},{5,7},{10,8},{11,9},{8,1... | collective-permute-start | bytes 393224 | tf_op jit(solution)/shard_map/ppermute | solution.py:872
  81.6 6.7 %collective-permute-start.16 = (bf16[64,1024]{1,0:T(8,128)(2,1)S(1)}, bf16[64,1024]{1,0:T(8,128)(2,1)S(1)}, u32[]{:S(2)}, u32[]{:S(2)}) collective-permute-start(bf16[64,1024]{1,0:T(8,128)(2,1)S(1)} %get-tuple-element.217.refs_0_), channel_id=1, source_target_pairs={{3,0},{2,1},{1,2},{0,3},{7,4},{6,5},{5,6},{4,7},{11,8},{10,9},{9,1... | collective-permute-start | bytes 393224 | tf_op jit(solution)/shard_map/ppermute | solution.py:872
  81.9 10.4 %collective-permute-start.11 = (bf16[192,768]{1,0:T(8,128)(2,1)S(1)}, bf16[192,768]{1,0:T(8,128)(2,1)S(1)}, u32[]{:S(2)}, u32[]{:S(2)}) collective-permute-start(bf16[192,768]{1,0:T(8,128)(2,1)S(1)} %convert_bitcast_fusion.refs_0_), channel_id=1, source_target_pairs={{8,0},{12,4},{16,8},{20,12},{24,16},{28,20},{0,24},{4,28},{9,1},{1... | collective-permute-start | bytes 884744 | tf_op jit(solution)/shard_map/ppermute | solution.py:859
  85.0 13.8 %collective-permute-start.12 = (bf16[192,768]{1,0:T(8,128)(2,1)S(1)}, bf16[192,768]{1,0:T(8,128)(2,1)S(1)}, u32[]{:S(2)}, u32[]{:S(2)}) collective-permute-start(bf16[192,768]{1,0:T(8,128)(2,1)S(1)} %convert_bitcast_fusion.refs_0_), channel_id=1, source_target_pairs={{24,0},{28,4},{0,8},{4,12},{8,16},{12,20},{16,24},{20,28},{25,1},{... | collective-permute-start | bytes 884744 | tf_op jit(solution)/shard_map/ppermute | solution.py:859
  98.8 16.0 %collective-permute-start.17 = (bf16[192,768]{1,0:T(8,128)(2,1)S(1)}, bf16[192,768]{1,0:T(8,128)(2,1)}, u32[]{:S(2)}, u32[]{:S(2)}) collective-permute-start(bf16[192,768]{1,0:T(8,128)(2,1)S(1)} %convert_bitcast_fusion.refs_0_), channel_id=1, source_target_pairs={{16,0},{20,4},{24,8},{28,12},{0,16},{4,20},{8,24},{12,28},{17,1},{... | collective-permute-start | bytes 884744 | tf_op jit(solution)/shard_map/ppermute | solution.py:859
  99.0 15.8 %collective-permute-start.18 = (bf16[384,768]{1,0:T(8,128)(2,1)S(1)}, bf16[384,768]{1,0:T(8,128)(2,1)S(1)}, u32[]{:S(2)}, u32[]{:S(2)}) collective-permute-start(bf16[384,768]{1,0:T(8,128)(2,1)S(1)} %constant_dynamic-update-slice_fusion.6.refs_2_), channel_id=1, source_target_pairs={{4,0},{0,4},{12,8},{8,12},{20,16},{16,20},{28,24},{24,28},{5,1},{1... | collective-permute-start | bytes 1769480 | tf_op jit(solution)/shard_map/ppermute | solution.py:868
  115.6 14.1 %collective-permute-start.19 = (bf16[192,768]{1,0:T(8,128)(2,1)}, bf16[192,768]{1,0:T(8,128)(2,1)}, u32[]{:S(2)}, u32[]{:S(2)}) collective-permute-start(bf16[192,768]{1,0:T(8,128)(2,1)} %collective-permute-done.17.refs_4_), channel_id=1, source_target_pairs={{4,0},{0,4},{12,8},{8,12},{20,16},{16,20},{28,24},{24,28},{5,1},{1... | collective-permute-start | bytes 884744 | tf_op jit(solution)/shard_map/ppermute | solution.py:868
  117.2 12.5 %collective-permute-start.20 = (bf16[64,1536]{1,0:T(8,128)(2,1)}, bf16[64,1536]{1,0:T(8,128)(2,1)S(1)}, u32[]{:S(2)}, u32[]{:S(2)}) collective-permute-start(bf16[64,1536]{1,0:T(8,128)(2,1)} %copy-done.49), channel_id=1, source_target_pairs={{1,0},{0,1},{3,2},{2,3},{5,4},{4,5},{7,6},{6,7},{9,8},{8,9},{11,10... | collective-permute-start | bytes 589832 | tf_op jit(solution)/shard_map/ppermute | solution.py:872
  117.3 12.4 %collective-permute-start.21 = (bf16[64,1536]{1,0:T(8,128)(2,1)}, bf16[64,1536]{1,0:T(8,128)(2,1)S(1)}, u32[]{:S(2)}, u32[]{:S(2)}) collective-permute-start(bf16[64,1536]{1,0:T(8,128)(2,1)} %copy-done.49), channel_id=1, source_target_pairs={{2,0},{3,1},{0,2},{1,3},{6,4},{7,5},{4,6},{5,7},{10,8},{11,9},{8,1... | collective-permute-start | bytes 589832 | tf_op jit(solution)/shard_map/ppermute | solution.py:872
  118.9 10.8 %collective-permute-start.22 = (bf16[64,1536]{1,0:T(8,128)(2,1)}, bf16[64,1536]{1,0:T(8,128)(2,1)S(1)}, u32[]{:S(2)}, u32[]{:S(2)}) collective-permute-start(bf16[64,1536]{1,0:T(8,128)(2,1)} %copy-done.49), channel_id=1, source_target_pairs={{3,0},{2,1},{1,2},{0,3},{7,4},{6,5},{5,6},{4,7},{11,8},{10,9},{9,1... | collective-permute-start | bytes 589832 | tf_op jit(solution)/shard_map/ppermute | solution.py:872
  129.7 7.3 %collective-permute-start.24 = (f32[8,1024]{1,0:T(8,128)S(1)}, f32[8,1024]{1,0:T(8,128)S(1)}, u32[]{:S(2)}, u32[]{:S(2)}) collective-permute-start(f32[8,1024]{1,0:T(8,128)S(1)} %get-tuple-element.245), channel_id=1, source_target_pairs={{2,0},{3,1},{0,2},{1,3},{6,4},{7,5},{4,6},{5,7},{10,8},{11,9},{8,1... | collective-permute-start | bytes 98312 | tf_op jit(solution)/shard_map/ppermute | solution.py:872
  131.3 5.7 %collective-permute-start.25 = (f32[8,1024]{1,0:T(8,128)S(1)}, f32[8,1024]{1,0:T(8,128)S(1)}, u32[]{:S(2)}, u32[]{:S(2)}) collective-permute-start(f32[8,1024]{1,0:T(8,128)S(1)} %get-tuple-element.245), channel_id=1, source_target_pairs={{3,0},{2,1},{1,2},{0,3},{7,4},{6,5},{5,6},{4,7},{11,8},{10,9},{9,1... | collective-permute-start | bytes 98312 | tf_op jit(solution)/shard_map/ppermute | solution.py:872
  131.5 5.6 %collective-permute-start.23 = (f32[8,1024]{1,0:T(8,128)S(1)}, f32[8,1024]{1,0:T(8,128)S(1)}, u32[]{:S(2)}, u32[]{:S(2)}) collective-permute-start(f32[8,1024]{1,0:T(8,128)S(1)} %get-tuple-element.245), channel_id=1, source_target_pairs={{1,0},{0,1},{3,2},{2,3},{5,4},{4,5},{7,6},{6,7},{9,8},{8,9},{11,10... | collective-permute-start | bytes 98312 | tf_op jit(solution)/shard_map/ppermute | solution.py:872
  137.1 8.3 %collective-permute-start.27 = (f32[8,1024]{1,0:T(8,128)S(1)}, f32[8,1024]{1,0:T(8,128)S(1)}, u32[]{:S(2)}, u32[]{:S(2)}) collective-permute-start(f32[8,1024]{1,0:T(8,128)S(1)} %get-tuple-element.256), channel_id=1, source_target_pairs={{2,0},{3,1},{0,2},{1,3},{6,4},{7,5},{4,6},{5,7},{10,8},{11,9},{8,1... | collective-permute-start | bytes 98312 | tf_op jit(solution)/shard_map/ppermute | solution.py:872
  138.7 6.7 %collective-permute-start.28 = (f32[8,1024]{1,0:T(8,128)S(1)}, f32[8,1024]{1,0:T(8,128)S(1)}, u32[]{:S(2)}, u32[]{:S(2)}) collective-permute-start(f32[8,1024]{1,0:T(8,128)S(1)} %get-tuple-element.256), channel_id=1, source_target_pairs={{3,0},{2,1},{1,2},{0,3},{7,4},{6,5},{5,6},{4,7},{11,8},{10,9},{9,1... | collective-permute-start | bytes 98312 | tf_op jit(solution)/shard_map/ppermute | solution.py:872
  138.7 6.8 %collective-permute-start.26 = (f32[8,1024]{1,0:T(8,128)S(1)}, f32[8,1024]{1,0:T(8,128)S(1)}, u32[]{:S(2)}, u32[]{:S(2)}) collective-permute-start(f32[8,1024]{1,0:T(8,128)S(1)} %get-tuple-element.256), channel_id=1, source_target_pairs={{1,0},{0,1},{3,2},{2,3},{5,4},{4,5},{7,6},{6,7},{9,8},{8,9},{11,10... | collective-permute-start | bytes 98312 | tf_op jit(solution)/shard_map/ppermute | solution.py:872
  145.5 21.6 %collective-permute-start.29 = (bf16[576,768]{1,0:T(8,128)(2,1)S(1)}, bf16[576,768]{1,0:T(8,128)(2,1)S(1)}, u32[]{:S(2)}, u32[]{:S(2)}) collective-permute-start(bf16[576,768]{1,0:T(8,128)(2,1)S(1)} %get-tuple-element.263), channel_id=1, source_target_pairs={{4,0},{0,4},{12,8},{8,12},{20,16},{16,20},{28,24},{24,28},{5,1},{1... | collective-permute-start | bytes 2654216 | tf_op jit(solution)/shard_map/ppermute | solution.py:868
  171.9 35.7 %collective-permute-start.32 = (bf16[192,768]{1,0:T(8,128)(2,1)S(1)}, bf16[192,768]{1,0:T(8,128)(2,1)S(1)}, u32[]{:S(2)}, u32[]{:S(2)}) collective-permute-start(bf16[192,768]{1,0:T(8,128)(2,1)S(1)} %get-tuple-element.301), channel_id=1, source_target_pairs={{24,0},{28,4},{0,8},{4,12},{8,16},{12,20},{16,24},{20,28},{25,1},{... | collective-permute-start | bytes 884744 | tf_op jit(solution)/shard_map/ppermute | solution.py:859
  172.8 34.8 %collective-permute-start.33 = (bf16[192,768]{1,0:T(8,128)(2,1)S(1)}, bf16[192,768]{1,0:T(8,128)(2,1)S(1)}, u32[]{:S(2)}, u32[]{:S(2)}) collective-permute-start(bf16[192,768]{1,0:T(8,128)(2,1)S(1)} %get-tuple-element.302), channel_id=1, source_target_pairs={{8,0},{12,4},{16,8},{20,12},{24,16},{28,20},{0,24},{4,28},{9,1},{1... | collective-permute-start | bytes 884744 | tf_op jit(solution)/shard_map/ppermute | solution.py:859
  175.7 31.9 %collective-permute-start.34 = (bf16[192,768]{1,0:T(8,128)(2,1)S(1)}, bf16[192,768]{1,0:T(8,128)(2,1)S(1)}, u32[]{:S(2)}, u32[]{:S(2)}) collective-permute-start(bf16[192,768]{1,0:T(8,128)(2,1)S(1)} %get-tuple-element.303), channel_id=1, source_target_pairs={{16,0},{20,4},{24,8},{28,12},{0,16},{4,20},{8,24},{12,28},{17,1},{... | collective-permute-start | bytes 884744 | tf_op jit(solution)/shard_map/ppermute | solution.py:859
  175.7 31.9 %collective-permute-start.35 = (bf16[576,768]{1,0:T(8,128)(2,1)S(1)}, bf16[576,768]{1,0:T(8,128)(2,1)S(1)}, u32[]{:S(2)}, u32[]{:S(2)}) collective-permute-start(bf16[576,768]{1,0:T(8,128)(2,1)S(1)} %get-tuple-element.304), channel_id=1, source_target_pairs={{4,0},{0,4},{12,8},{8,12},{20,16},{16,20},{28,24},{24,28},{5,1},{1... | collective-permute-start | bytes 2654216 | tf_op jit(solution)/shard_map/ppermute | solution.py:868
  176.2 31.4 %collective-permute-start.36 = (bf16[1024,384]{1,0:T(8,128)(2,1)S(1)}, bf16[1024,384]{1,0:T(8,128)(2,1)S(1)}, u32[]{:S(2)}, u32[]{:S(2)}) collective-permute-start(bf16[1024,384]{1,0:T(8,128)(2,1)S(1)} %add_convert_fusion.2), channel_id=1, source_target_pairs={{2,0},{3,1},{0,2},{1,3},{6,4},{7,5},{4,6},{5,7},{10,8},{11,9},{8,1... | collective-permute-start | bytes 2359304 | tf_op jit(solution)/shard_map/ppermute | solution.py:872
  210.6 6.8 %collective-permute-start.62 = (f32[8,256]{1,0:T(8,128)S(1)}, f32[8,256]{1,0:T(8,128)S(1)}, u32[]{:S(2)}, u32[]{:S(2)}) collective-permute-start(f32[8,256]{1,0:T(8,128)S(1)} %add.375), channel_id=1, source_target_pairs={{2,0},{3,1},{0,2},{1,3},{6,4},{7,5},{4,6},{5,7},{10,8},{11,9},{8,1... | collective-permute-start | bytes 24584 | tf_op jit(solution)/shard_map/ppermute | solution.py:872
  213.6 48.8 %collective-permute-start.37 = (bf16[192,768]{1,0:T(8,128)(2,1)}, bf16[192,768]{1,0:T(8,128)(2,1)}, u32[]{:S(2)}, u32[]{:S(2)}) collective-permute-start(bf16[192,768]{1,0:T(8,128)(2,1)} %get-tuple-element.441), channel_id=1, source_target_pairs={{24,0},{28,4},{0,8},{4,12},{8,16},{12,20},{16,24},{20,28},{25,1},{... | collective-permute-start | bytes 884744 | tf_op jit(solution)/shard_map/ppermute | solution.py:859
  215.1 51.8 %collective-permute-start.38 = (bf16[192,768]{1,0:T(8,128)(2,1)}, bf16[192,768]{1,0:T(8,128)(2,1)}, u32[]{:S(2)}, u32[]{:S(2)}) collective-permute-start(bf16[192,768]{1,0:T(8,128)(2,1)} %get-tuple-element.440), channel_id=1, source_target_pairs={{8,0},{12,4},{16,8},{20,12},{24,16},{28,20},{0,24},{4,28},{9,1},{1... | collective-permute-start | bytes 884744 | tf_op jit(solution)/shard_map/ppermute | solution.py:859
  217.5 10.3 %collective-permute-start.63 = (f32[8,1152]{1,0:T(8,128)S(1)}, f32[8,1152]{1,0:T(8,128)S(1)}, u32[]{:S(2)}, u32[]{:S(2)}) collective-permute-start(f32[8,1152]{1,0:T(8,128)S(1)} %pad_maximum_fusion.1), channel_id=1, source_target_pairs={{4,0},{0,4},{12,8},{8,12},{20,16},{16,20},{28,24},{24,28},{5,1},{1... | collective-permute-start | bytes 110600 | tf_op jit(solution)/shard_map/ppermute | solution.py:868
  227.5 51.4 %collective-permute-start.41 = (bf16[576,768]{1,0:T(8,128)(2,1)}, bf16[576,768]{1,0:T(8,128)(2,1)}, u32[]{:S(2)}, u32[]{:S(2)}) collective-permute-start(bf16[576,768]{1,0:T(8,128)(2,1)} %get-tuple-element.328), channel_id=1, source_target_pairs={{4,0},{0,4},{12,8},{8,12},{20,16},{16,20},{28,24},{24,28},{5,1},{1... | collective-permute-start | bytes 2654216 | tf_op jit(solution)/shard_map/ppermute | solution.py:868
  228.4 18.6 %collective-permute-start.64 = (f32[8,1152]{1,0:T(8,128)}, f32[8,1152]{1,0:T(8,128)}, u32[]{:S(2)}, u32[]{:S(2)}) collective-permute-start(f32[8,1152]{1,0:T(8,128)} %fusion.14), channel_id=1, source_target_pairs={{8,0},{12,4},{0,8},{4,12},{24,16},{28,20},{16,24},{20,28},{9,1},{1... | collective-permute-start | bytes 110600 | tf_op jit(solution)/shard_map/ppermute | solution.py:864
  242.9 14.9 %collective-permute-start.43 = (bf16[256,1536]{1,0:T(8,128)(2,1)}, bf16[256,1536]{1,0:T(8,128)(2,1)}, u32[]{:S(2)}, u32[]{:S(2)}) collective-permute-start(bf16[256,1536]{1,0:T(8,128)(2,1)} %get-tuple-element.343), channel_id=1, source_target_pairs={{1,0},{0,1},{3,2},{2,3},{5,4},{4,5},{7,6},{6,7},{9,8},{8,9},{11,10... | collective-permute-start | bytes 2359304 | tf_op jit(solution)/shard_map/ppermute | solution.py:872
  242.9 13.0 %all-to-all-start = ((bf16[4,64,1024]{2,1,0:T(8,128)(2,1)}), bf16[4,64,1024]{2,1,0:T(8,128)(2,1)}, u32[]{:S(2)}, u32[]{:S(2)}) async-start(bf16[4,64,1024]{2,1,0:T(8,128)(2,1)} %bitcast.47), calls=%async_computation | async-start | bytes 1048576 | tf_op jit(solution)/shard_map/all_to_all | solution.py:1067
  252.8 11.0 %collective-permute-start.42 = (bf16[256,1536]{1,0:T(8,128)(2,1)}, bf16[256,1536]{1,0:T(8,128)(2,1)}, u32[]{:S(2)}, u32[]{:S(2)}) collective-permute-start(bf16[256,1536]{1,0:T(8,128)(2,1)} %get-tuple-element.341), channel_id=1, source_target_pairs={{1,0},{0,1},{3,2},{2,3},{5,4},{4,5},{7,6},{6,7},{9,8},{8,9},{11,10... | collective-permute-start | bytes 2359304 | tf_op jit(solution)/shard_map/ppermute | solution.py:872
  259.4 19.4 %collective-permute-start.44 = (bf16[256,1536]{1,0:T(8,128)(2,1)S(1)}, bf16[256,1536]{1,0:T(8,128)(2,1)S(1)}, u32[]{:S(2)}, u32[]{:S(2)}) collective-permute-start(bf16[256,1536]{1,0:T(8,128)(2,1)S(1)} %add_convert_fusion), channel_id=1, source_target_pairs={{2,0},{3,1},{0,2},{1,3},{6,4},{7,5},{4,6},{5,7},{10,8},{11,9},{8,1... | collective-permute-start | bytes 2359304 | tf_op jit(solution)/shard_map/ppermute | solution.py:872
  262.4 16.4 %collective-permute-start.39 = (bf16[192,768]{1,0:T(8,128)(2,1)S(1)}, bf16[192,768]{1,0:T(8,128)(2,1)S(1)}, u32[]{:S(2)}, u32[]{:S(2)}) collective-permute-start(bf16[192,768]{1,0:T(8,128)(2,1)S(1)} %copy-done.92), channel_id=1, source_target_pairs={{16,0},{20,4},{24,8},{28,12},{0,16},{4,20},{8,24},{12,28},{17,1},{... | collective-permute-start | bytes 884744 | tf_op jit(solution)/shard_map/ppermute | solution.py:859
  263.8 15.1 %collective-permute-start.40 = (bf16[192,768]{1,0:T(8,128)(2,1)S(1)}, bf16[192,768]{1,0:T(8,128)(2,1)S(1)}, u32[]{:S(2)}, u32[]{:S(2)}) collective-permute-start(bf16[192,768]{1,0:T(8,128)(2,1)S(1)} %copy-done.46), channel_id=1, source_target_pairs={{4,0},{0,4},{12,8},{8,12},{20,16},{16,20},{28,24},{24,28},{5,1},{1... | collective-permute-start | bytes 884744 | tf_op jit(solution)/shard_map/ppermute | solution.py:868
  266.9 16.3 %collective-permute-start.48 = (bf16[192,768]{1,0:T(8,128)(2,1)S(1)}, bf16[192,768]{1,0:T(8,128)(2,1)S(1)}, u32[]{:S(2)}, u32[]{:S(2)}) collective-permute-start(bf16[192,768]{1,0:T(8,128)(2,1)S(1)} %copy-done.44), channel_id=1, source_target_pairs={{4,0},{0,4},{12,8},{8,12},{20,16},{16,20},{28,24},{24,28},{5,1},{1... | collective-permute-start | bytes 884744 | tf_op jit(solution)/shard_map/ppermute | solution.py:868
  278.9 12.4 %collective-permute-start.54 = (bf16[576,128]{1,0:T(8,128)(2,1)S(1)}, bf16[576,128]{1,0:T(8,128)(2,1)S(1)}, u32[]{:S(2)}, u32[]{:S(2)}) collective-permute-start(bf16[576,128]{1,0:T(8,128)(2,1)S(1)} %get-tuple-element.365), channel_id=1, source_target_pairs={{4,0},{0,4},{12,8},{8,12},{20,16},{16,20},{28,24},{24,28},{5,1},{1... | collective-permute-start | bytes 442376 | tf_op jit(solution)/shard_map/ppermute | solution.py:868
  280.8 15.9 %collective-permute-start.53 = (bf16[192,128]{1,0:T(8,128)(2,1)S(1)}, bf16[192,128]{1,0:T(8,128)(2,1)S(1)}, u32[]{:S(2)}, u32[]{:S(2)}) collective-permute-start(bf16[192,128]{1,0:T(8,128)(2,1)S(1)} %get-tuple-element.363), channel_id=1, source_target_pairs={{4,0},{0,4},{12,8},{8,12},{20,16},{16,20},{28,24},{24,28},{5,1},{1... | collective-permute-start | bytes 147464 | tf_op jit(solution)/shard_map/ppermute | solution.py:868
  289.5 6.9 %collective-permute-start.68 = (f32[8,1536]{1,0:T(8,128)S(1)}, f32[8,1536]{1,0:T(8,128)S(1)}, u32[]{:S(2)}, u32[]{:S(2)}) collective-permute-start(f32[8,1536]{1,0:T(8,128)S(1)} %add.384), channel_id=1, source_target_pairs={{4,0},{0,4},{12,8},{8,12},{20,16},{16,20},{28,24},{24,28},{5,1},{1... | collective-permute-start | bytes 147464 | tf_op jit(solution)/shard_map/ppermute | solution.py:868
  291.4 6.8 %collective-permute-start.57 = (bf16[192,128]{1,0:T(8,128)(2,1)S(1)}, bf16[192,128]{1,0:T(8,128)(2,1)S(1)}, u32[]{:S(2)}, u32[]{:S(2)}) collective-permute-start(bf16[192,128]{1,0:T(8,128)(2,1)S(1)} %get-tuple-element.452), channel_id=1, source_target_pairs={{16,0},{20,4},{24,8},{28,12},{0,16},{4,20},{8,24},{12,28},{17,1},{... | collective-permute-start | bytes 147464 | tf_op jit(solution)/shard_map/ppermute | solution.py:859
  292.3 6.7 %collective-permute-start.56 = (bf16[192,128]{1,0:T(8,128)(2,1)S(1)}, bf16[192,128]{1,0:T(8,128)(2,1)S(1)}, u32[]{:S(2)}, u32[]{:S(2)}) collective-permute-start(bf16[192,128]{1,0:T(8,128)(2,1)S(1)} %get-tuple-element.453), channel_id=1, source_target_pairs={{8,0},{12,4},{16,8},{20,12},{24,16},{28,20},{0,24},{4,28},{9,1},{1... | collective-permute-start | bytes 147464 | tf_op jit(solution)/shard_map/ppermute | solution.py:859
  295.5 6.3 %collective-permute-start.55 = (bf16[192,128]{1,0:T(8,128)(2,1)S(1)}, bf16[192,128]{1,0:T(8,128)(2,1)S(1)}, u32[]{:S(2)}, u32[]{:S(2)}) collective-permute-start(bf16[192,128]{1,0:T(8,128)(2,1)S(1)} %get-tuple-element.451), channel_id=1, source_target_pairs={{24,0},{28,4},{0,8},{4,12},{8,16},{12,20},{16,24},{20,28},{25,1},{... | collective-permute-start | bytes 147464 | tf_op jit(solution)/shard_map/ppermute | solution.py:859
  296.4 27.1 %collective-permute-start.49 = (bf16[192,768]{1,0:T(8,128)(2,1)S(1)}, bf16[192,768]{1,0:T(8,128)(2,1)S(1)}, u32[]{:S(2)}, u32[]{:S(2)}) collective-permute-start(bf16[192,768]{1,0:T(8,128)(2,1)S(1)} %copy-done.48), channel_id=1, source_target_pairs={{4,0},{0,4},{12,8},{8,12},{20,16},{16,20},{28,24},{24,28},{5,1},{1... | collective-permute-start | bytes 884744 | tf_op jit(solution)/shard_map/ppermute | solution.py:868
  296.7 27.7 %collective-permute-start.46 = (bf16[256,1536]{1,0:T(8,128)(2,1)S(1)}, bf16[256,1536]{1,0:T(8,128)(2,1)S(1)}, u32[]{:S(2)}, u32[]{:S(2)}) collective-permute-start(bf16[256,1536]{1,0:T(8,128)(2,1)S(1)} %get-tuple-element.352.refs_0_), channel_id=1, source_target_pairs={{2,0},{3,1},{0,2},{1,3},{6,4},{7,5},{4,6},{5,7},{10,8},{11,9},{8,1... | collective-permute-start | bytes 2359304 | tf_op jit(solution)/shard_map/ppermute | solution.py:872
  301.9 5.8 %collective-permute-start.58 = (f32[192,64]{1,0:T(8,128)S(1)}, f32[192,64]{1,0:T(8,128)S(1)}, u32[]{:S(2)}, u32[]{:S(2)}) collective-permute-start(f32[192,64]{1,0:T(8,128)S(1)} %bitcast.48), channel_id=1, source_target_pairs={{1,0},{0,1},{3,2},{2,3},{5,4},{4,5},{7,6},{6,7},{9,8},{8,9},{11,10... | collective-permute-start | bytes 147464 | tf_op jit(solution)/shard_map/ppermute | solution.py:872
  302.0 15.1 %collective-permute-start.59 = (f32[192,64]{1,0:T(8,128)S(1)}, f32[192,64]{1,0:T(8,128)}, u32[]{:S(2)}, u32[]{:S(2)}) collective-permute-start(f32[192,64]{1,0:T(8,128)S(1)} %bitcast.49), channel_id=1, source_target_pairs={{2,0},{3,1},{0,2},{1,3},{6,4},{7,5},{4,6},{5,7},{10,8},{11,9},{8,1... | collective-permute-start | bytes 147464 | tf_op jit(solution)/shard_map/ppermute | solution.py:872
  303.9 18.1 %collective-permute-start.70 = (f32[8,1536]{1,0:T(8,128)}, f32[8,1536]{1,0:T(8,128)}, u32[]{:S(2)}, u32[]{:S(2)}) collective-permute-start(f32[8,1536]{1,0:T(8,128)} %add.386), channel_id=1, source_target_pairs={{16,0},{20,4},{24,8},{28,12},{0,16},{4,20},{8,24},{12,28},{17,1},{... | collective-permute-start | bytes 147464 | tf_op jit(solution)/shard_map/ppermute | solution.py:864
  308.4 15.3 %collective-permute-start.52 = (bf16[192,768]{1,0:T(8,128)(2,1)S(1)}, bf16[192,768]{1,0:T(8,128)(2,1)S(1)}, u32[]{:S(2)}, u32[]{:S(2)}) collective-permute-start(bf16[192,768]{1,0:T(8,128)(2,1)S(1)} %get-tuple-element.437), channel_id=1, source_target_pairs={{16,0},{20,4},{24,8},{28,12},{0,16},{4,20},{8,24},{12,28},{17,1},{... | collective-permute-start | bytes 884744 | tf_op jit(solution)/shard_map/ppermute | solution.py:859
  317.1 19.1 %collective-permute-start.51 = (bf16[192,768]{1,0:T(8,128)(2,1)}, bf16[192,768]{1,0:T(8,128)(2,1)}, u32[]{:S(2)}, u32[]{:S(2)}) collective-permute-start(bf16[192,768]{1,0:T(8,128)(2,1)} %get-tuple-element.438), channel_id=1, source_target_pairs={{8,0},{12,4},{16,8},{20,12},{24,16},{28,20},{0,24},{4,28},{9,1},{1... | collective-permute-start | bytes 884744 | tf_op jit(solution)/shard_map/ppermute | solution.py:859
  321.9 14.3 %collective-permute-start.50 = (bf16[192,768]{1,0:T(8,128)(2,1)}, bf16[192,768]{1,0:T(8,128)(2,1)S(1)}, u32[]{:S(2)}, u32[]{:S(2)}) collective-permute-start(bf16[192,768]{1,0:T(8,128)(2,1)} %get-tuple-element.436), channel_id=1, source_target_pairs={{24,0},{28,4},{0,8},{4,12},{8,16},{12,20},{16,24},{20,28},{25,1},{... | collective-permute-start | bytes 884744 | tf_op jit(solution)/shard_map/ppermute | solution.py:859
  323.5 23.5 %collective-permute-start.45 = (bf16[256,1536]{1,0:T(8,128)(2,1)S(1)}, bf16[256,1536]{1,0:T(8,128)(2,1)S(1)}, u32[]{:S(2)}, u32[]{:S(2)}) collective-permute-start(bf16[256,1536]{1,0:T(8,128)(2,1)S(1)} %get-tuple-element.352.refs_0_), channel_id=1, source_target_pairs={{1,0},{0,1},{3,2},{2,3},{5,4},{4,5},{7,6},{6,7},{9,8},{8,9},{11,10... | collective-permute-start | bytes 2359304 | tf_op jit(solution)/shard_map/ppermute | solution.py:872
  323.7 19.9 %collective-permute-start.60 = (f32[192,64]{1,0:T(8,128)}, f32[192,64]{1,0:T(8,128)}, u32[]{:S(2)}, u32[]{:S(2)}) collective-permute-start(f32[192,64]{1,0:T(8,128)} %collective-permute-done.59), channel_id=1, source_target_pairs={{1,0},{0,1},{3,2},{2,3},{5,4},{4,5},{7,6},{6,7},{9,8},{8,9},{11,10... | collective-permute-start | bytes 147464 | tf_op jit(solution)/shard_map/ppermute | solution.py:872
  324.4 22.5 %collective-permute-start.47 = (bf16[256,1536]{1,0:T(8,128)(2,1)S(1)}, bf16[256,1536]{1,0:T(8,128)(2,1)S(1)}, u32[]{:S(2)}, u32[]{:S(2)}) collective-permute-start(bf16[256,1536]{1,0:T(8,128)(2,1)S(1)} %collective-permute-done.46.refs_2_), channel_id=1, source_target_pairs={{1,0},{0,1},{3,2},{2,3},{5,4},{4,5},{7,6},{6,7},{9,8},{8,9},{11,10... | collective-permute-start | bytes 2359304 | tf_op jit(solution)/shard_map/ppermute | solution.py:872
  (120 other events, 997.1 us)

commit v4 on v3

--- a/solution.py
+++ b/solution.py
@@ -134,10 +134,10 @@
 
 
 def ssd_backward_kernel(
-    x_ref, xb_ref, bc_ref, bcb_ref, st_ref, aux_ref, seg_ref, conv_ref, bct_ref, heads_ref, expand_ref,
+    rank_ref, x_ref, xb_ref, bc_ref, bcb_ref, st_ref, aux_ref, seg_ref, conv_ref, bct_ref, heads_ref, expand_ref,
     mixed_ref, dy_ref, state_ref,
-    dx_ref, dbc_ref, dbc_t_ref, dst_ref, dst_t_ref, dconv_ref, dbct_ref, dheads_ref,
-    dstate, xs_scr, bc_scr, du_scr, dubc_scr,
+    dx_ref, dbc_ref, keep_ref, send_ref, dst_ref, dst_t_ref, dconv_ref, dbct_ref, dheads_ref,
+    dstate, xs_scr, bc_scr, du_scr, dubc_scr, share_scr,
 ):
     at = pl.program_id(0)
 
@@ -254,7 +254,14 @@
     dubc = jnp.concatenate([db, dc], axis=1) * (sgbc * (1.0 + ubc * (1.0 - sgbc)))
     dbc = conv_back(dubc_scr, dubc, bc_now, bct_ref, dbct_ref).astype(bf16)
     dbc_ref[...] = dbc
-    dbc_t_ref[...] = dbc.T
+    share = 2 * LANES // 4
+    turned = dbc.T
+    for member in range(4):
+        apart = member ^ rank_ref[0]
+        start = pl.multiple_of((apart & 1) * 2 * share + (apart >> 1) * share, share)
+        share_scr[pl.ds(start, share), :] = turned[member * share:(member + 1) * share, :]
+    keep_ref[...] = share_scr[0:2 * share, :]
+    send_ref[...] = share_scr[2 * share:4 * share, :]
 
 
 def common_specs(place, channels):
@@ -297,13 +304,13 @@
             pltpu.VMEM((HALO + CHUNK, channels), f32),
             pltpu.VMEM((HALO + CHUNK, 2 * LANES), f32),
         ],
-        compiler_params=pltpu.CompilerParams(vmem_limit_bytes=32 * MIB),
+        compiler_params=pltpu.CompilerParams(vmem_limit_bytes=14 * MIB),
         cost_estimate=pl.CostEstimate(flops=14 * 10**9, bytes_accessed=40 * 10**6, transcendentals=0),
         name="ssd_forward",
     )(x_pre, x_pre, bc_pre, bc_pre, step_pre, aux, seg_row, conv_rows, bc_rows, head_rows, expand)
 
 
-def ssd_backward(x_pre, bc_pre, step_pre, aux, seg_row, conv_rows, bc_rows, head_rows, expand, mixed, dy, states):
+def ssd_backward(rank, x_pre, bc_pre, step_pre, aux, seg_row, conv_rows, bc_rows, head_rows, expand, mixed, dy, states):
     tokens, channels = x_pre.shape
     count = tokens // CHUNK
     place = lambda i: count - 1 - i
@@ -312,7 +319,7 @@
     return pl.pallas_call(
         ssd_backward_kernel,
         grid=(count,),
-        in_specs=common_specs(place, channels) + [
+        in_specs=[pl.BlockSpec(memory_space=pltpu.SMEM)] + common_specs(place, channels) + [
             pl.BlockSpec((CHUNK, channels), now),
             pl.BlockSpec((CHUNK, channels), now),
             pl.BlockSpec((None, LANES, channels), lambda i: (place(i), 0, 0)),
@@ -320,7 +327,8 @@
         out_specs=[
             pl.BlockSpec((CHUNK, channels), now),
             pl.BlockSpec((CHUNK, 2 * LANES), now),
-            pl.BlockSpec((2 * LANES, CHUNK), lambda i: (0, place(i))),
+            pl.BlockSpec((LANES, CHUNK), lambda i: (0, place(i))),
+            pl.BlockSpec((LANES, CHUNK), lambda i: (0, place(i))),
             pl.BlockSpec((CHUNK, LANES), now),
             pl.BlockSpec((16, CHUNK), lambda i: (0, place(i))),
             pl.BlockSpec((8, channels), whole),
@@ -330,7 +338,8 @@
         out_shape=[
             jax.ShapeDtypeStruct((tokens, channels), bf16),
             jax.ShapeDtypeStruct((tokens, 2 * LANES), bf16),
-            jax.ShapeDtypeStruct((2 * LANES, tokens), bf16),
+            jax.ShapeDtypeStruct((LANES, tokens), bf16),
+            jax.ShapeDtypeStruct((LANES, tokens), bf16),
             jax.ShapeDtypeStruct((tokens, LANES), bf16),
             jax.ShapeDtypeStruct((16, tokens), bf16),
             jax.ShapeDtypeStruct((8, channels), f32),
@@ -343,11 +352,12 @@
             pltpu.VMEM((HALO + CHUNK, 2 * LANES), f32),
             pltpu.VMEM((HALO + CHUNK, channels), f32),
             pltpu.VMEM((HALO + CHUNK, 2 * LANES), f32),
-        ],
-        compiler_params=pltpu.CompilerParams(vmem_limit_bytes=32 * MIB),
+            pltpu.VMEM((2 * LANES, CHUNK), bf16),
+        ],
+        compiler_params=pltpu.CompilerParams(vmem_limit_bytes=14 * MIB),
         cost_estimate=pl.CostEstimate(flops=28 * 10**9, bytes_accessed=80 * 10**6, transcendentals=0),
         name="ssd_backward",
-    )(x_pre, x_pre, bc_pre, bc_pre, step_pre, aux, seg_row, conv_rows, bc_rows, head_rows, expand, mixed, dy, states)
+    )(rank, x_pre, x_pre, bc_pre, bc_pre, step_pre, aux, seg_row, conv_rows, bc_rows, head_rows, expand, mixed, dy, states)
 
 
 def segment_facts(seg):
@@ -395,20 +405,21 @@
             s += 1
 
 
-def params(mib=24):
+def params(mib=18):
     return pltpu.CompilerParams(vmem_limit_bytes=mib * MIB)
 
 
-def cost(flops, moved):
-    return pl.CostEstimate(flops=int(flops), bytes_accessed=int(moved), transcendentals=0)
-
-
-def prepare_kernel(hidden_ref, gain_ref, low_ref, low_t_ref):
+def cost(us):
+    return pl.CostEstimate(flops=int(us * 10**9), bytes_accessed=int(us * 2 * 10**6), transcendentals=0)
+
+
+def prepare_kernel(hidden_ref, gain_ref, low_ref, low_t_ref, inv_ref):
     inputs = hidden_ref[...].astype(f32)
     inv_rms = lax.rsqrt(jnp.mean(inputs * inputs, axis=1, keepdims=True) + EPSILON)
     low = (inputs * inv_rms * gain_ref[0:1, :]).astype(bf16)
     low_ref[...] = low
     low_t_ref[...] = low.T
+    inv_ref[...] = column_to_row(inv_rms)
 
 
 def prepare(hidden, gain_rows):
@@ -418,12 +429,52 @@
         prepare_kernel,
         grid=(tokens // TILE,),
         in_specs=[block, pl.BlockSpec((8, depth), lambda i: (0, 0))],
-        out_specs=[block, pl.BlockSpec((depth, TILE), lambda i: (0, i))],
-        out_shape=[jax.ShapeDtypeStruct((tokens, depth), bf16), jax.ShapeDtypeStruct((depth, tokens), bf16)],
-        compiler_params=params(),
-        cost_estimate=cost(6 * 10**9, 20 * 10**6),
+        out_specs=[block, pl.BlockSpec((depth, TILE), lambda i: (0, i)), pl.BlockSpec((8, TILE), lambda i: (0, i))],
+        out_shape=[
+            jax.ShapeDtypeStruct((tokens, depth), bf16),
+            jax.ShapeDtypeStruct((depth, tokens), bf16),
+            jax.ShapeDtypeStruct((8, tokens), f32),
+        ],
+        compiler_params=params(),
+        cost_estimate=cost(12),
         name="prepare",
     )(hidden, gain_rows)
+
+
+def pack_kernel(rank_ref, in_ref, bc_ref, step_ref, a_ref, b_ref, scratch):
+    channels = b_ref.shape[1]
+    rows, width = bc_ref.shape
+    share = width // 4
+    heads = step_ref.shape[0]
+    b_ref[...] = in_ref[:, 0, :].astype(bf16)
+    a_ref[:, :channels] = in_ref[:, 1, :].astype(bf16)
+    scratch[...] = jnp.zeros_like(scratch)
+    scratch[share:share + heads, 0:rows] = step_ref[...]
+    step = scratch[...].T[0:rows, :]
+    own = bc_ref[:, 0:LANES]
+    for member in range(1, 4):
+        moved = pltpu.roll(bc_ref[...], width - member * share, 1)[:, 0:LANES]
+        own = jnp.where(rank_ref[0] == member, moved, own)
+    lane = lax.broadcasted_iota(jnp.int32, (rows, LANES), 1)
+    a_ref[:, channels:] = jnp.where(lane < share, own, step).astype(bf16)
+
+
+def pack(in_weight, bc_weight, step_t, rank):
+    rows, _, channels = in_weight.shape
+    vmem = pl.BlockSpec(memory_space=pltpu.VMEM)
+    return pl.pallas_call(
+        pack_kernel,
+        in_specs=[pl.BlockSpec(memory_space=pltpu.SMEM), vmem, vmem, vmem],
+        out_specs=[vmem, vmem],
+        out_shape=[
+            jax.ShapeDtypeStruct((rows, channels + LANES), bf16),
+            jax.ShapeDtypeStruct((rows, channels), bf16),
+        ],
+        scratch_shapes=[pltpu.VMEM((LANES, 2 * LANES), f32)],
+        compiler_params=params(),
+        cost_estimate=cost(2),
+        name="pack",
+    )(rank, in_weight, bc_weight, step_t)
 
 
 def columns_kernel(rank_ref, *refs, count):
@@ -446,7 +497,7 @@
         out_specs=[pl.BlockSpec((TILE, depth), lambda i: (i, 0)), pl.BlockSpec((depth, TILE), lambda i: (0, i))],
         out_shape=[jax.ShapeDtypeStruct((tokens, depth), bf16), jax.ShapeDtypeStruct((depth, tokens), bf16)],
         compiler_params=params(),
-        cost_estimate=cost(4 * 10**9, 16 * 10**6),
+        cost_estimate=cost(12),
         name="join_columns",
     )(rank, *pieces)
 
@@ -467,7 +518,7 @@
         out_specs=pl.BlockSpec(memory_space=pltpu.VMEM),
         out_shape=jax.ShapeDtypeStruct(shape, pieces[0].dtype),
         compiler_params=params(),
-        cost_estimate=cost(10**9, 4 * shape[0] * shape[1]),
+        cost_estimate=cost(0.1),
         name="join_rows",
     )(rank, *pieces)
 
@@ -496,52 +547,76 @@
         out_shape=[jax.ShapeDtypeStruct((tokens, width), f32), jax.ShapeDtypeStruct((tokens, LANES), f32)],
         scratch_shapes=[pltpu.VMEM((width, TILE), f32)],
         compiler_params=params(),
-        cost_estimate=cost(2 * 10**9, 4 * 10**6),
+        cost_estimate=cost(0.1),
         name="join_small",
     )(rank, *pieces, small)
 
 
-def project_kernel(idx_ref, lhs_ref, *refs, count):
-    pieces, (x_ref, small_ref, share_ref, w_ref, wt_ref) = refs[:count], refs[count:]
-    channels = x_ref.shape[1]
+def project_small_kernel(idx_ref, lhs_ref, *refs, count):
+    pieces, (small_ref, share_ref, w_ref, wt_ref) = refs[:count], refs[count:]
 
     @pl.when(pl.program_id(0) == 0)
     def _():
         fill(w_ref, pieces, idx_ref)
-        wt_ref[...] = w_ref[:, channels:].T[0:wt_ref.shape[0], :]
-
-    product = dot_nn(lhs_ref[...], w_ref[...])
-    x_ref[...] = product[:, :channels]
-    small = product[:, channels:].T
+        wt_ref[...] = w_ref[...].T[0:wt_ref.shape[0], :]
+
+    small = dot_nn(lhs_ref[...], w_ref[...]).T
     small_ref[...] = small
     share_ref[...] = small[0:share_ref.shape[0], :].astype(bf16)
 
 
-def project(lhs, pieces, idx, channels, share):
+def project_small(lhs, pieces, idx, share):
     tokens, depth = lhs.shape
-    count, width = len(pieces), pieces[0].shape[1]
+    count, last = len(pieces), pieces[0].shape[1] // LANES - 1
     whole = lambda i: (0, 0)
     return pl.pallas_call(
-        functools.partial(project_kernel, count=count),
+        functools.partial(project_small_kernel, count=count),
         grid=(tokens // TILE,),
         in_specs=[pl.BlockSpec(memory_space=pltpu.SMEM), pl.BlockSpec((TILE, depth), lambda i: (i, 0))]
-        + [pl.BlockSpec(p.shape, whole) for p in pieces],
+        + [pl.BlockSpec((p.shape[0], LANES), lambda i: (0, last)) for p in pieces],
         out_specs=[
-            pl.BlockSpec((TILE, channels), lambda i: (i, 0)),
-            pl.BlockSpec((width - channels, TILE), lambda i: (0, i)),
+            pl.BlockSpec((LANES, TILE), lambda i: (0, i)),
             pl.BlockSpec((share, TILE), lambda i: (0, i)),
-            pl.BlockSpec((depth, width), whole),
+            pl.BlockSpec((depth, LANES), whole),
             pl.BlockSpec((share, depth), whole),
         ],
+        out_shape=[
+            jax.ShapeDtypeStruct((LANES, tokens), f32),
+            jax.ShapeDtypeStruct((share, tokens), bf16),
+            jax.ShapeDtypeStruct((depth, LANES), bf16),
+            jax.ShapeDtypeStruct((share, depth), bf16),
+        ],
+        compiler_params=params(),
+        cost_estimate=cost(0.1),
+        name="project_small",
+    )(idx, lhs, *pieces)
+
+
+def project_kernel(idx_ref, lhs_ref, *refs, count):
+    pieces, (x_ref, w_ref) = refs[:count], refs[count:]
+
+    @pl.when(pl.program_id(0) == 0)
+    def _():
+        fill(w_ref, pieces, idx_ref)
+
+    x_ref[...] = dot_nn(lhs_ref[...], w_ref[...])
+
+
+def project(lhs, pieces, idx, channels):
+    tokens, depth = lhs.shape
+    whole = lambda i: (0, 0)
+    return pl.pallas_call(
+        functools.partial(project_kernel, count=len(pieces)),
+        grid=(tokens // TILE,),
+        in_specs=[pl.BlockSpec(memory_space=pltpu.SMEM), pl.BlockSpec((TILE, depth), lambda i: (i, 0))]
+        + [pl.BlockSpec((p.shape[0], channels), whole) for p in pieces],
+        out_specs=[pl.BlockSpec((TILE, channels), lambda i: (i, 0)), pl.BlockSpec((depth, channels), whole)],
         out_shape=[
             jax.ShapeDtypeStruct((tokens, channels), f32),
-            jax.ShapeDtypeStruct((width - channels, tokens), f32),
-            jax.ShapeDtypeStruct((share, tokens), bf16),
-            jax.ShapeDtypeStruct((depth, width), bf16),
-            jax.ShapeDtypeStruct((share, depth), bf16),
-        ],
-        compiler_params=params(),
-        cost_estimate=cost(2 * tokens * depth * width, 6 * depth * width),
+            jax.ShapeDtypeStruct((depth, channels), bf16),
+        ],
+        compiler_params=params(),
+        cost_estimate=cost(20),
         name="project",
     )(idx, lhs, *pieces)
 
@@ -592,7 +667,7 @@
             jax.ShapeDtypeStruct((depth, channels), bf16),
         ],
         compiler_params=params(),
-        cost_estimate=cost(2 * tokens * depth * channels, 8 * depth * channels),
+        cost_estimate=cost(0.1),
         name="gate_forward",
     )(idx, lhs, mixed, *pieces)
 
@@ -614,7 +689,7 @@
         out_specs=block,
         out_shape=jax.ShapeDtypeStruct((tokens, channels), bf16),
         compiler_params=params(),
-        cost_estimate=cost(20 * tokens * channels, 10 * tokens * channels),
+        cost_estimate=cost(0.1),
         name="gated_norm",
     )(gate, mixed, square, conv_rows)
 
@@ -660,7 +735,7 @@
             jax.ShapeDtypeStruct((depth, channels), bf16),
         ],
         compiler_params=params(),
-        cost_estimate=cost(2 * tokens * depth * channels, 8 * depth * channels),
+        cost_estimate=cost(20),
         name="grad_gout",
     )(idx, cot, gate, mixed, conv_rows, *pieces)
 
@@ -700,7 +775,7 @@
             jax.ShapeDtypeStruct((8, channels), f32),
         ],
         compiler_params=params(),
-        cost_estimate=cost(30 * tokens * channels, 16 * tokens * channels),
+        cost_estimate=cost(0.1),
         name="gate_backward",
     )(gate, gout, mixed, square, inner, conv_rows)
 
@@ -722,7 +797,7 @@
                 s += 1
 
 
-def weight_grad(lhs_t, rhs, idx, sizes, turned=False):
+def weight_grad(lhs_t, rhs, idx, sizes, us=0.1, turned=False):
     depth, tokens = lhs_t.shape
     width = rhs.shape[0 if turned else 1]
     rows = depth // idx.shape[0]
@@ -739,7 +814,7 @@
         out_shape=[jax.ShapeDtypeStruct((size * rows, width), bf16) for size in sizes],
         scratch_shapes=[pltpu.VMEM((depth, width), bf16)],
         compiler_params=params(),
-        cost_estimate=cost(2 * tokens * depth * width, 4 * depth * width),
+        cost_estimate=cost(us),
         name="weight_grad",
     )(idx, lhs_t, rhs)
 
@@ -770,22 +845,24 @@
         ),
         out_shape=[jax.ShapeDtypeStruct((tokens, width), bf16)] * ranks,
         compiler_params=params(),
-        cost_estimate=cost(2 * tokens * depth * channels, 4 * depth * channels),
+        cost_estimate=cost(0.1),
         name="out_partial",
     )(rank, gated_out, w_out)
 
 
-def term_kernel(rank_ref, gx_ref, wx_ref, gg_ref, wg_ref, gs_ref, ws_ref, gb_ref, wbt_ref, *refs):
-    outs, scratch = refs[:-1], refs[-1]
+def term_kernel(rank_ref, gx_ref, wx_ref, gg_ref, wg_ref, gs_ref, ws_ref, gb_ref, wbt_ref, hidden_ref, inv_ref, *refs):
+    outs, dgain_ref, scratch = refs[:-2], refs[-2], refs[-1]
     total = dot_nt(gx_ref[...], wx_ref[...]) + dot_nt(gg_ref[...], wg_ref[...])
     total = total + dot_nt(gs_ref[...], ws_ref[...]) + dot_nn(gb_ref[...], wbt_ref[...])
     scratch[...] = total.astype(bf16)
+    normed = hidden_ref[...].astype(f32) * row_to_column(inv_ref[0:1, :])
+    dgain_ref[...] = jnp.broadcast_to(jnp.sum(total * normed, axis=0, keepdims=True), dgain_ref.shape)
     for r, out in enumerate(outs):
         rows = out.shape[0]
         out[...] = scratch[pl.ds(pl.multiple_of((rank_ref[0] ^ r) * rows, rows), rows), :]
 
 
-def normed_term(dx, dgate, dstep, dbc, w_a, w_b, w_bct, rank, ranks):
+def normed_term(dx, dgate, dstep, dbc, w_a, w_b, w_s, w_bct, hidden, inv_rms, rank, ranks):
     tokens, channels = dx.shape
     depth = w_a.shape[0]
     rows = tokens // ranks
@@ -800,20 +877,22 @@
             pl.BlockSpec(dgate.shape, whole),
             pl.BlockSpec((TILE_D, channels), lambda i: (i, 0)),
             pl.BlockSpec(dstep.shape, whole),
-            pl.BlockSpec((TILE_D, LANES), lambda i: (i, channels // LANES)),
+            pl.BlockSpec((TILE_D, LANES), lambda i: (i, 0)),
             pl.BlockSpec(dbc.shape, whole),
             pl.BlockSpec((w_bct.shape[0], TILE_D), lambda i: (0, i)),
-        ],
-        out_specs=[pl.BlockSpec((rows, TILE_D), lambda i: (0, i))] * ranks,
-        out_shape=[jax.ShapeDtypeStruct((rows, depth), bf16)] * ranks,
+            pl.BlockSpec((tokens, TILE_D), lambda i: (0, i)),
+            pl.BlockSpec(inv_rms.shape, whole),
+        ],
+        out_specs=[pl.BlockSpec((rows, TILE_D), lambda i: (0, i))] * ranks + [pl.BlockSpec((8, TILE_D), lambda i: (0, i))],
+        out_shape=[jax.ShapeDtypeStruct((rows, depth), bf16)] * ranks + [jax.ShapeDtypeStruct((8, depth), f32)],
         scratch_shapes=[pltpu.VMEM((tokens, TILE_D), bf16)],
         compiler_params=params(32),
-        cost_estimate=cost(2 * tokens * depth * 1920, 4 * depth * 1920),
+        cost_estimate=cost(0.1),
         name="normed_term",
-    )(rank, dx, w_a, dgate, w_b, dstep, w_a, dbc, w_bct)
-
-
-def norm_back_kernel(rank_ref, a_ref, b_ref, hidden_ref, cot_ref, gain_ref, out_ref, dgain_ref):
+    )(rank, dx, w_a, dgate, w_b, dstep, w_s, dbc, w_bct, hidden, inv_rms)
+
+
+def norm_back_kernel(rank_ref, a_ref, b_ref, hidden_ref, cot_ref, gain_ref, out_ref):
     grad = a_ref[...].astype(f32) + b_ref[...].astype(f32)
     inputs = hidden_ref[...].astype(f32)
     inv_rms = lax.rsqrt(jnp.mean(inputs * inputs, axis=1, keepdims=True) + EPSILON)
@@ -821,7 +900,6 @@
     scaled = grad * gain_ref[0:1, :]
     mean = jnp.mean(scaled * normed, axis=1, keepdims=True)
     out_ref[...] = (inv_rms * (scaled - normed * mean) + cot_ref[...].astype(f32)).astype(out_ref.dtype)
-    dgain_ref[...] = jnp.broadcast_to(jnp.sum(grad * normed, axis=0, keepdims=True), dgain_ref.shape)
 
 
 def norm_backward(a, b, hidden, cot, gain_rows, rank):
@@ -840,11 +918,11 @@
                 pl.BlockSpec((rows, depth), mine),
                 pl.BlockSpec((8, depth), whole),
             ],
-            out_specs=[pl.BlockSpec((rows, depth), whole), pl.BlockSpec((8, depth), whole)],
+            out_specs=pl.BlockSpec((rows, depth), whole),
         ),
-        out_shape=[jax.ShapeDtypeStruct((rows, depth), bf16), jax.ShapeDtypeStruct((8, depth), f32)],
-        compiler_params=params(),
-        cost_estimate=cost(4 * 10**9, 12 * 10**6),
+        out_shape=jax.ShapeDtypeStruct((rows, depth), bf16),
+        compiler_params=params(),
+        cost_estimate=cost(0.1),
         name="norm_backward",
     )(rank, a, b, hidden, cot, gain_rows)
 
@@ -881,11 +959,15 @@
     return order
 
 
+def pair_sum(a, b):
+    return (a.astype(f32) + b.astype(f32)).astype(bf16)
+
+
 def outer_blocks(own, here, back, ks):
     rows = own.shape[0]
+    back = [part[i:i + rows] for part in back for i in range(0, part.shape[0], rows)]
     return [
-        (here[i * rows:(i + 1) * rows].astype(f32) + back[i * rows:(i + 1) * rows].astype(f32)).astype(bf16)
-        for i in range(len(ks))
+        (here[i * rows:(i + 1) * rows].astype(f32) + back[i].astype(f32)).astype(bf16) for i in range(len(ks))
     ]
 
 
@@ -894,8 +976,7 @@
     return [outer_from(block, n - k) for block, k in zip(blocks, ks)]
 
 
-def dp_sum(v):
-    v = v + inner_flip(v)
+def outer_sum(v):
     bit = 1
     while bit < lax.axis_size("dp") // 2:
         v = v + outer_flip(v, bit)
@@ -924,13 +1005,11 @@
 
 
 def in_rank_order(pieces, rank, axis):
-    width = pieces[0].shape[axis]
-    shape = list(pieces[0].shape)
-    shape[axis] = width * len(pieces)
-    full = jnp.zeros(shape, pieces[0].dtype)
-    for r, piece in enumerate(pieces):
-        full = lax.dynamic_update_slice_in_dim(full, piece, (rank ^ r) * width, axis)
-    return full
+    odd, high = (rank & 1) == 1, (rank & 2) == 2
+    join = lambda a, b: jnp.concatenate([a, b], axis=axis)
+    low = jnp.where(odd, join(pieces[1], pieces[0]), join(pieces[0], pieces[1]))
+    far = jnp.where(odd, join(pieces[3], pieces[2]), join(pieces[2], pieces[3]))
+    return jnp.where(high, join(far, low), join(low, far))
 
 
 def momentum(moment, grad):
@@ -957,7 +1036,6 @@
     heads = head_table.shape[1]
     tokens, depth = hidden.shape
     share = bc_weight.shape[1] // ranks
-    spare = LANES - share - heads
 
     ks = hops(n)
     near_ks, far_k = ks[:-1], ks[-1]
@@ -967,110 +1045,162 @@
 
     first = [(0, 0), (0, 1)]
     idx = members(first + [(k, 0) for k in ks] + [(k, 1) for k in ks])
-    idx_c = members(first + [(k, j) for j in (0, 1) for k in near_ks] + [(far_k, 0), (far_k, 1)])
+    idx_s = members([(0, 0)] + [(k, 0) for k in ks] + [(0, 1)] + [(k, 1) for k in ks])
     sizes = (1, 1, n - 1, n - 1)
+    split_sizes = (1, 1, n - 1, n - 2, 1)
     width = depth // ranks
 
-    own_bc = lax.dynamic_slice_in_dim(bc_weight, rank * share, share, 1)
-    set_a = jnp.concatenate([in_weight[:, 1], own_bc, step_weight, jnp.zeros((rows, spare), f32)], axis=1).astype(bf16)
-    set_b = in_weight[:, 0].astype(bf16)
+    set_a, set_b = pack(in_weight, bc_weight, step_weight.T, rank1)
     set_c = out_weight.T.astype(bf16)
-    wide_a = set_a.shape[1]
-
-    a_z = [outer_from(set_a, k) for k in ks]
-    own_x = inner_flip(jnp.concatenate([set_a, set_b, set_c], axis=1))
+
+    def blocks(own, z, x):
+        return [own, x[0]] + [z[k] for k in ks] + [x[k] for k in ks]
+
+    def block(v, i):
+        return v[i * rows:(i + 1) * rows]
+
+    def blocks(own, z, x):
+        return [own, x[0]] + [z[k] for k in ks] + [x[k] for k in ks]
+
+    def block(v, i):
+        return v[i * rows:(i + 1) * rows]
+
+    def outer_all(v, some):
+        return {k: outer_from(v, k) for k in some}
+
+    def flip_all(z, some):
+        return {k: inner_flip(z[k]) for k in some}
+
+    a_z = outer_all(set_a, ks)
+    a_x = {0: inner_flip(set_a)}
     cot_far = rank_flip(cotangent, 2)
     gain_rows = pad_rows(norm_gain[None])
-    normed_low, normed_t = prepare(hidden, gain_rows)
+    normed_low, normed_t, inv_rms = prepare(hidden, gain_rows)
+    a_x.update(flip_all(a_z, near_ks))
     aux, seg_row = segment_facts(segments)
     head_rows = pad_lanes(pad_rows(head_table))
     facts = (aux, seg_row, pad_rows(conv_table), pad_rows(bc_table), head_rows, head_expand(channels))
-    set_a, set_b, set_c, a_z, own_x, cot_far, normed_low, normed_t, facts = fence(
-        set_a, set_b, set_c, a_z, own_x, cot_far, normed_low, normed_t, facts
-    )
-    a_own, b_own, c_own = own_x[:, :wide_a], own_x[:, wide_a:wide_a + channels], own_x[:, wide_a + channels:]
-
-    b_z = [outer_from(set_b, k) for k in ks]
-    a_z = jnp.concatenate(a_z, axis=0)
-    a_x = inner_flip(a_z)
+    set_a, set_b, set_c, a_z, a_x, cot_far, normed_low, normed_t, inv_rms, facts = fence(
+        set_a, set_b, set_c, a_z, a_x, cot_far, normed_low, normed_t, inv_rms, facts
+    )
+
+    a_x[far_k] = inner_flip(a_z[far_k])
+    b_z = outer_all(set_b, near_ks)
     cot, cot_t = join_columns([cotangent, rank_flip(cotangent, 1), cot_far, rank_flip(cot_far, 1)], rank1)
-    set_c, b_z, a_z, a_x, a_own, b_own, c_own, cot, cot_t, normed_low = fence(
-        set_c, b_z, a_z, a_x, a_own, b_own, c_own, cot, cot_t, normed_low
-    )
-
-    c_near = [outer_from(set_c, k) for k in near_ks]
-    b_z = jnp.concatenate(b_z, axis=0)
-    b_x = inner_flip(b_z)
-    x_pre, small, bc_share, w_a, w_bct_share = project(normed_low, [set_a, a_own, a_z, a_x], idx, channels, share)
-    bc_pre, step_pre = join_small([bc_share] + [rank_flip(bc_share, r) for r in (1, 2, 3)], small, rank1)
-    set_c, c_near, b_z, b_x, x_pre, bc_pre, step_pre, w_bct_share = fence(
-        set_c, c_near, b_z, b_x, x_pre, bc_pre, step_pre, w_bct_share
-    )
-
-    c_far = outer_from(set_c, far_k)
-    c_near = jnp.concatenate(c_near, axis=0)
-    c_near_x = inner_flip(c_near)
+    set_b, set_c, b_z, a_z, a_x, cot, cot_t, normed_low = fence(set_b, set_c, b_z, a_z, a_x, cot, cot_t, normed_low)
+
+    b_z[far_k] = outer_from(set_b, far_k)
+    b_x = {0: inner_flip(set_b), **flip_all(b_z, near_ks[:1])}
+    a_blocks = blocks(set_a, a_z, a_x)
+    small, bc_share, w_s, w_bct_share = project_small(normed_low, a_blocks, idx, share)
+    bc_pieces = mp_pieces(bc_share)
+    x_pre, w_a = project(normed_low, a_blocks, idx, channels)
+    bc_pieces, x_pre, small, set_c, w_bct_share, w_s = fence(bc_pieces, x_pre, small, set_c, w_bct_share, w_s)
+    bc_pre, step_pre = join_small(bc_pieces, small, rank1)
+    set_c, b_z, b_x, x_pre, bc_pre, step_pre, w_bct_share = fence(
+        set_c, b_z, b_x, x_pre, bc_pre, step_pre, w_bct_share
+    )
+
+    c_z = outer_all(set_c, near_ks)
+    c_x = {0: inner_flip(set_c)}
+    b_x.update(flip_all(b_z, ks[1:]))
     mixed, states = ssd_forward(x_pre, bc_pre, step_pre, *facts)
-    c_far, c_near, c_near_x, mixed, states, w_bct_share = fence(c_far, c_near, c_near_x, mixed, states, w_bct_share)
-
-    c_far_x = inner_flip(c_far)
-    w_bct = [w_bct_share] + [rank_flip(w_bct_share, r) for r in (1, 2, 3)]
-    gate_pre, square, w_b = gate_forward(normed_low, mixed, [set_b, b_own, b_z, b_x], idx)
-    c_far_x, w_bct, gate_pre, square, mixed = fence(c_far_x, w_bct, gate_pre, square, mixed)
-
+    mixed, states, b_x, b_z, c_z, c_x, w_bct_share, set_c = fence(mixed, states, b_x, b_z, c_z, c_x, w_bct_share, set_c)
+
+    c_z[far_k] = outer_from(set_c, far_k)
+    c_x.update(flip_all(c_z, near_ks))
+    gate_pre, square, w_b = gate_forward(normed_low, mixed, blocks(set_b, b_z, b_x), idx)
+    mixed, gate_pre, square, w_b, w_bct_share = fence(mixed, gate_pre, square, w_b, w_bct_share)
     conv_rows = facts[2]
     square = mp_sum_direct(square)
-    gout, inner_dot, w_c = grad_gout(
-        cot, gate_pre, mixed, conv_rows, [set_c, c_own, c_near, c_near_x, c_far, c_far_x], idx_c
-    )
-    square, gout, inner_dot, w_c = fence(square, gout, inner_dot, w_c)
-
+    gated_out = gated_norm(gate_pre, mixed, square, conv_rows, channels * ranks)
+    gc_own, gc_own1, gc_here, gc_near, gc_far = weight_grad(cot_t, gated_out, idx, split_sizes)
+    square, c_z, c_x, gated_out, gc_own, gc_own1, gc_here, gc_near, gc_far, w_bct_share = fence(
+        square, c_z, c_x, gated_out, gc_own, gc_own1, gc_here, gc_near, gc_far, w_bct_share
+    )
+    c_x[far_k] = inner_flip(c_z[far_k])
+    c_x, gc_far, gc_near = fence(c_x, gc_far, gc_near)
+
+    gc_far_back, gc_near_back = inner_flip(gc_far), inner_flip(gc_near)
+    gout, inner_dot, w_c = grad_gout(cot, gate_pre, mixed, conv_rows, blocks(set_c, c_z, c_x), idx)
     inner_dot = mp_sum_direct(inner_dot)
-    gated_out = gated_norm(gate_pre, mixed, square, conv_rows, channels * ranks)
-    gc_own, gc_own1, gc_here, gc_send = weight_grad(cot_t, gated_out, idx, sizes)
-    inner_dot, gated_out, gc_own, gc_own1, gc_here, gc_send = fence(
-        inner_dot, gated_out, gc_own, gc_own1, gc_here, gc_send
-    )
-
-    gc_back = inner_flip(gc_send)
+    gc_far_back, inner_dot, gout, w_c, w_bct_share = fence(gc_far_back, inner_dot, gout, w_c, w_bct_share)
+    w_bct = [w_bct_share] + [rank_flip(w_bct_share, r) for r in (1, 2, 3)]
     dmixed, dgate, dgain = gate_backward(gate_pre, gout, mixed, square, inner_dot, conv_rows, channels * ranks)
-    dmixed, dgate, dgain, w_c, w_bct = fence(dmixed, dgate, dgain, w_c, w_bct)
     gb_own, gb_own1, gb_here, gb_send = weight_grad(normed_t, dgate, idx, sizes)
     partial = out_partial(gated_out, w_c, rank1, ranks)
-    w_bct = join_rows(w_bct, rank1)
-    gc_back, gb_own, gb_own1, gb_here, gb_send, partial, dmixed, w_bct = fence(
-        gc_back, gb_own, gb_own1, gb_here, gb_send, partial, dmixed, w_bct
-    )
-    out_far = (partial[2].astype(f32) + rank_flip(partial[3], 1).astype(f32)).astype(bf16)
+    gc_near_back, gc_far_back, w_bct, gb_own, gb_own1, gb_here, gb_send, partial, dmixed, dgain = fence(
+        gc_near_back, gc_far_back, w_bct, gb_own, gb_own1, gb_here, gb_send, partial, dmixed, dgain
+    )
+    out_far = pair_sum(partial[2], rank_flip(partial[3], 1))
     out_near = partial[0].astype(f32) + rank_flip(partial[1], 1).astype(f32)
-    gc_send_z = outer_blocks(gc_own, gc_here, gc_back, ks)
-    out_far, out_near, gc_send_z, gb_send, dmixed, w_bct = fence(out_far, out_near, gc_send_z, gb_send, dmixed, w_bct)
-
-    c_got = outer_send(gc_send_z, ks)
+    gc_blocks = [pair_sum(block(gc_here, i), block(gc_near_back, i)) for i in range(n - 2)]
+    gc_blocks.append(pair_sum(block(gc_here, n - 2), gc_far_back))
+    out_far, out_near, gc_blocks, gb_send, dmixed = fence(out_far, out_near, gc_blocks, gb_send, dmixed)
+
+    c_got = dict(zip(ks, outer_send(gc_blocks, ks)))
     gb_back = inner_flip(gb_send)
     out_got = rank_flip(out_far, 2)
-    dx, dbc, dbc_t, dstep, dstep_t, dconv, dbct_part, dheads = ssd_backward(
-        x_pre, bc_pre, step_pre, *facts, mixed, dmixed, states
-    )
-    c_got, gb_back, out_got, dx, dbc, dbc_t, dstep, dstep_t, dconv, dbct_part, dheads, gc_own1, gb_own1 = fence(
-        c_got, gb_back, out_got, dx, dbc, dbc_t, dstep, dstep_t, dconv, dbct_part, dheads, gc_own1, gb_own1
-    )
-
-    b_got = outer_send(outer_blocks(gb_own, gb_here, gb_back, ks), ks)
-    c_own_got = inner_flip(gc_own1)
-    ga_own, ga_own1, ga_here, ga_send = weight_grad(normed_t, dx, idx, sizes)
-    ga_own, ga_own1, ga_here, ga_send, dx, dbc_t = fence(ga_own, ga_own1, ga_here, ga_send, dx, dbc_t)
-    ga_back = inner_flip(ga_send)
-    term = normed_term(dx, dgate, dstep, dbc, w_a, w_b, w_bct, rank1, ranks)
-    term, dbc_t = fence(term, dbc_t)
-    near, far = mp_reduce(term)
-    parts = lax.all_to_all(dbc_t.reshape(ranks, share, tokens), "mp", 0, 0)
-    dbc_share = jnp.sum(parts.astype(f32), axis=0).astype(bf16)
+    dx, dbc, dbc_keep, dbc_send, dstep, dstep_t, dconv, dbct_part, dheads = ssd_backward(
+        rank1, x_pre, bc_pre, step_pre, *facts, mixed, dmixed, states
+    )
+    c_got, gb_back, out_got, dx, dbc, dbc_keep, dbc_send, dstep, dstep_t, dconv, dbct_part, dheads, gc_own1, gb_own1 = fence(
+        c_got, gb_back, out_got, dx, dbc, dbc_keep, dbc_send, dstep, dstep_t, dconv, dbct_part, dheads, gc_own1, gb_own1
+    )
+
+    b_blocks = [pair_sum(block(gb_here, i), block(gb_back, i)) for i in range(n - 1)]
+    b_got = outer_send(b_blocks[:-1], near_ks)
+    own_got = inner_flip(jnp.concatenate([gc_own1, gb_own1], axis=1))
+    dbc_back = rank_flip(dbc_send, 1)
+    *term, dgain_norm = normed_term(
+        dx, dgate, dstep, dbc, w_a, w_b, w_s, join_rows(w_bct, rank1), hidden, inv_rms, rank1, ranks
+    )
+    term, dgain_norm, b_got, own_got, far_block, dx, dbc_back = fence(
+        term, dgain_norm, b_got, own_got, b_blocks[-1], dx, dbc_back
+    )
+
+    b_got = b_got + outer_send([far_block], [far_k])
+    far = pair_sum(term[2], rank_flip(term[3], 1))
+    near = term[0].astype(f32) + rank_flip(term[1], 1).astype(f32)
+    dbc_pair = pair_sum(dbc_keep, dbc_back)
+    dbc_got = rank_flip(dbc_pair[share:], 2)
+    ga_own, ga_own1, ga_here, ga_near, ga_far = weight_grad(normed_t, dx, idx, split_sizes, us=20)
+    shared = jnp.concatenate([dbct_part, dgain_norm], axis=1)
+    shared = shared + rank_flip(shared, 1)
+    far, near, shared, ga_own, ga_own1, ga_here, ga_near, ga_far, dbc_pair, dbc_got = fence(
+        far, near, shared, ga_own, ga_own1, ga_here, ga_near, ga_far, dbc_pair, dbc_got
+    )
+
+    got = rank_flip(far, 2)
+    shared_got = rank_flip(shared, 2)
+    ga_far_back, ga_near_back = inner_flip(ga_far), inner_flip(ga_near)
+    dbc_share = pair_sum(dbc_pair[:share], dbc_got)
     dsmall_t = jnp.concatenate([dbc_share, dstep_t, jnp.zeros((LANES - share - 16, tokens), bf16)], axis=0)
-    gs_own, gs_own1, gs_here, gs_send = weight_grad(normed_t, dsmall_t, idx, sizes, turned=True)
-    b_got, c_own_got, ga_back, near, far, gs_own, gs_own1, gs_here, gs_send = fence(
-        b_got, c_own_got, ga_back, near, far, gs_own, gs_own1, gs_here, gs_send
-    )
+    gs_own, gs_here, gs_send = weight_grad(normed_t, dsmall_t, idx_s, (1, n - 1, n), turned=True)
+    ga_far_back, b_got, a_far, gs_send, shared, shared_got = fence(
+        ga_far_back, b_got, block(ga_here, n - 2), gs_send, shared, shared_got
+    )
+    a_got = {far_k: outer_from(pair_sum(a_far, ga_far_back), n - far_k)}
+    gs_back = inner_flip(gs_send)
+    packed = jnp.concatenate([dconv + dgain, dheads, shared + shared_got], axis=1)
+    packed_got = inner_flip(packed)
+    a_blocks = [pair_sum(block(ga_here, i), block(ga_near_back, i)) for i in range(n - 2)]
+    got, near, gs_back, a_blocks, packed, packed_got, ga_own1 = fence(
+        got, near, gs_back, a_blocks, packed, packed_got, ga_own1
+    )
+
+    mine = norm_backward(near, got, hidden, cot, gain_rows, rank1)
+    mine, a_blocks, packed, packed_got, gs_back, ga_own1 = fence(mine, a_blocks, packed, packed_got, gs_back, ga_own1)
+    mine_far = rank_flip(mine, 2)
+    for k, a_block in zip(near_ks, a_blocks):
+        a_got[k] = outer_from(a_block, n - k)
+    a_own_got = inner_flip(ga_own1)
+    packed = packed + packed_got
+    a_got, a_own_got, packed, gs_back = fence(a_got, a_own_got, packed, gs_back)
+    s_got = outer_send(outer_blocks(gs_own, gs_here, [gs_back[rows:]], ks), ks)
+    packed = outer_sum(packed)
+    mine_far, s_got, packed = fence(mine_far, s_got, packed)
+    input_grad = join_rows([mine, rank_flip(mine, 1), mine_far, rank_flip(mine_far, 1)], rank1)
 
     def total(own, own_got, got):
         value = own.astype(f32) + own_got.astype(f32)
@@ -1078,24 +1208,18 @@
             value = value + part.astype(f32)
         return value
 
-    a_got = outer_send(outer_blocks(ga_own, ga_here, ga_back, ks), ks)
-    mine, dgain_mine = norm_backward(near, far, hidden, cot, gain_rows, rank1)
-    a_own_got, b_own_got = inner_flip(ga_own1), inner_flip(gb_own1)
-    gs_back, s_own_got = inner_flip(gs_send), inner_flip(gs_own1)
-    s_got = outer_send(outer_blocks(gs_own, gs_here, gs_back, ks), ks)
-    input_grad = join_rows(mp_pieces(mine), rank1)
     resid = lax.dynamic_slice_in_dim(hidden, rank * width, width, 1).astype(f32)
     output = (resid + out_near + out_got.astype(f32)).astype(bf16)
-    shard_c = total(gc_own, c_own_got, c_got)
-    shard_b = total(gb_own, b_own_got, b_got)
-    shard_a = total(ga_own, a_own_got, a_got)
-    shard_s = total(gs_own, s_own_got, s_got)
-
-    packed = dp_sum(jnp.concatenate([dconv + dgain, mp_sum(dbct_part), dheads], axis=1))
+    shard_c = total(gc_own, own_got[:, :channels], [c_got[k] for k in ks])
+    shard_b = total(gb_own, own_got[:, channels:], b_got)
+    shard_a = total(ga_own, a_own_got, [a_got[k] for k in ks])
+    shard_s = total(gs_own, gs_back[:rows], s_got)
+
+    cut = channels + LANES
     total_conv = packed[:6, :channels]
-    total_bct = packed[:5, channels:channels + 2 * LANES]
-    total_head = packed[:3, channels + 2 * LANES:channels + 2 * LANES + heads]
-    total_gain = dp_sum(mp_sum(dgain_mine))[0]
+    total_head = packed[:3, channels:channels + heads]
+    total_bct = packed[:5, cut:cut + 2 * LANES]
+    total_gain = packed[0, cut + 2 * LANES:]
 
     shard_bc = in_rank_order(mp_pieces(shard_s[:, :share]), rank, 1)
     shard_step = shard_s[:, share:share + heads]

time: 350 us -> 318 us (0.909)
  local copies, waits for them, and re-layouts: 58.7 us -> 38.7 us
  waiting for transfers between devices: 87.9 us -> 76.1 us
  other arithmetic: 30.2 us -> 18.8 us
  starting transfers between devices: 72.3 us -> 79.4 us
  Pallas kernels: 97.5 us -> 102 us
    ppermute x21, waiting for transfers between devices: 67.5 us -> 43.7 us  [outer_from(): lax.ppermute(v, 'dp', [((o + k) % n * 2 + x, o * 2 + x) for o in range(n)...]
    ppermute x15 -> x21, waiting for transfers between devices: 6.16 us -> 25.3 us  [inner_flip(): lax.ppermute(v, 'dp', [(d ^ 1, d) for d in range(lax.axis_size('dp'))])]
    unnamed x238 -> x221, local copies, waits for them, and re-layouts: 47.4 us -> 32.9 us
    ppermute x15 -> x21, starting transfers between devices: 15.9 us -> 23.9 us  [inner_flip(): lax.ppermute(v, 'dp', [(d ^ 1, d) for d in range(lax.axis_size('dp'))])]
    pallas_call x2 -> x4, Pallas kernels: 31.6 us -> 37.3 us  [the longest x1 27.2 us: ssd_backward(): pl.pallas_call(ssd_backward_kernel, grid=(count,), in_specs=[pl.BlockSpec...]
    dynamic_update_slice x4 -> x0, local copies, waits for them, and re-layouts: 5.37 us -> none  [in_rank_order(): lax.dynamic_update_slice_in_dim(full, piece, (rank ^ r) * width, axis)]
    ppermute x31, waiting for transfers between devices: 12.2 us -> 6.81 us  [rank_flip(): lax.ppermute(v, 'mp', [(m ^ bit, m) for m in range(lax.axis_size('mp'))])]
    all_to_all x1 -> x0, starting transfers between devices: 4.14 us -> none  [body(): parts = lax.all_to_all(dbc_t.reshape(ranks, share, tokens), 'mp', 0, 0)]
  transfers between devices with their start and end apart: 72 -> 75, of which waited for: 20 -> 19; matrix products, arithmetic and copies ran while one was open for 13% -> 10% of each run, Pallas kernels for 27% -> 28%
where the time goes in v4:
time: 318 us
  Pallas kernels  102 us (32%)
  starting transfers between devices  79.4 us (25%)
  waiting for transfers between devices  76.1 us (24%)
  local copies, waits for them, and re-layouts  38.7 us (12%)
  other arithmetic  18.8 us (6%)
    ppermute x21, waiting for transfers between devices, outer_from(): lax.ppermute(v, 'dp', [((o + k) % n * 2 + x, o * 2 + x) for o in range(n)...  43.7 us
    ppermute x21, starting transfers between devices, outer_from(): lax.ppermute(v, 'dp', [((o + k) % n * 2 + x, o * 2 + x) for o in range(n)...  33 us
    unnamed x221, local copies, waits for them, and re-layouts  32.9 us
    pallas_call x1, Pallas kernels, ssd_backward(): pl.pallas_call(ssd_backward_kernel, grid=(count,), in_specs=[pl.BlockSpec...  27.2 us
    ppermute x21, waiting for transfers between devices, inner_flip(): lax.ppermute(v, 'dp', [(d ^ 1, d) for d in range(lax.axis_size('dp'))])  25.3 us
    ppermute x21, starting transfers between devices, inner_flip(): lax.ppermute(v, 'dp', [(d ^ 1, d) for d in range(lax.axis_size('dp'))])  23.9 us
    ppermute x31, starting transfers between devices, rank_flip(): lax.ppermute(v, 'mp', [(m ^ bit, m) for m in range(lax.axis_size('mp'))])  18 us
    pallas_call x4, Pallas kernels, weight_grad(): pl.pallas_call(functools.partial(weight_grad_kernel, rows=rows, turned=tu...  13.8 us
  transfers between devices with their start and end apart: 75, of which 19 were waited for; matrix products, arithmetic and copies ran while one was open for 10% of the time, Pallas kernels for 28%

profile of v4, /device:TPU:0, one launch (start us, length us, event | category | flops | bytes accessed | tf_op | source)
XLA Modules:
  0.0 317.5 jit_solution(17927847127585260215)
XLA Ops:
  3.6 2.4 pack.1
  6.7 5.0 %collective-permute-start = (bf16[192,896]{1,0:T(8,128)(2,1)S(1)}, bf16[192,896]{1,0:T(8,128)(2,1)}, u32[]{:S(2)}, u32[]{:S(2)}) collective-permute-start(bf16[192,896]{1,0:T(8,128)(2,1)S(1)} %get-tuple-element.283.refs_0_), channel_id=1, source_target_pairs={{8,0},{12,4},{16,8},{20,12},{24,16},{28,20},{0,24},{4,28},{9,1},{1... | collective-permute-start | bytes 1032200 | tf_op jit(solution)/shard_map/ppermute | solution.py:937
  12.8 1.5 collective-permute-start.3
  14.3 1.5 collective-permute-start.6
  17.6 2.3 prepare.1
  19.9 1.7 copy-done.2
  21.6 1.7 copy-done.5
  24.8 3.9 %collective-permute-done.2.refs_3_ = bf16[192,896]{1,0:T(8,128)(2,1)} collective-permute-done((bf16[192,896]{1,0:T(8,128)(2,1)S(1)}, bf16[192,896]{1,0:T(8,128)(2,1)}, u32[]{:S(2)}, u32[]{:S(2)}) %collective-permute-start.2) | collective-permute-done | bytes 344096 | tf_op jit(solution)/shard_map/ppermute | solution.py:937
  28.7 1.5 collective-permute-start.5
  33.3 7.8 %collective-permute-done.1.refs_4_ = bf16[192,896]{1,0:T(8,128)(2,1)} collective-permute-done((bf16[192,896]{1,0:T(8,128)(2,1)S(1)}, bf16[192,896]{1,0:T(8,128)(2,1)}, u32[]{:S(2)}, u32[]{:S(2)}) %collective-permute-start.1) | collective-permute-done | bytes 344096 | tf_op jit(solution)/shard_map/ppermute | solution.py:937
  41.9 2.7 collective-permute-start.7
  44.6 2.3 collective-permute-start.8
  46.9 1.5 collective-permute-start.9
  48.4 3.4 %join_columns.1 = (bf16[1024,1536]{1,0:T(8,128)(2,1)S(1)}, bf16[1536,1024]{1,0:T(8,128)(2,1)S(1)}) custom-call(s32[1]{0:T(128)} %bitcast.8.rank_ref, bf16[1024,384]{1,0:T(8,128)(2,1)} %refs_0_.1, bf16[1024,384]{1,0:T(8,128)(2,1)S(1)} %collective-permute-done.10.refs_1_, bf16[1024,384]{1,0:T(8,128)(2,1)} %collective-permute-done.6.refs_2_, ...), custom_call_target="tpu_custom_call" | custom-call | flops 12000000000 | bytes 24000000 | tf_op jit(solution)/shard_map/join_columns/pallas_call | solution.py:493
  51.9 9.0 %collective-permute-done.7.refs_2_ = bf16[192,768]{1,0:T(8,128)(2,1)S(1)} collective-permute-done((bf16[192,768]{1,0:T(8,128)(2,1)S(1)}, bf16[192,768]{1,0:T(8,128)(2,1)S(1)}, u32[]{:S(2)}, u32[]{:S(2)}) %collective-permute-start.7) | collective-permute-done | bytes 294944 | tf_op jit(solution)/shard_map/ppermute | solution.py:937
  60.9 3.1 project_small.1
  64.0 1.6 collective-permute-start.13
  66.4 1.5 collective-permute-start.16
  69.4 4.7 %project.1 = (f32[1024,768]{1,0:T(8,128)S(1)}, bf16[1536,768]{1,0:T(8,128)(2,1)S(1)}) custom-call(s32[8]{0:T(128)S(1)} %stack.97.idx_ref, bf16[1024,1536]{1,0:T(8,128)(2,1)S(1)} %copy-done.6, bf16[192,896]{1,0:T(8,128)(2,1)S(1)} %copy-done.28, bf16[192,896]{1,0:T(8,128)(2,1)} %collective-permute-done.3.refs_1_, ...), custom_call_target="tpu_custom_call" | custom-call | flops 20000000000 | bytes 40000000 | tf_op jit(solution)/shard_map/project/pallas_call | solution.py:608
  76.8 5.4 %collective-permute-done.15.refs_4_ = bf16[192,768]{1,0:T(8,128)(2,1)S(1)} collective-permute-done((bf16[192,768]{1,0:T(8,128)(2,1)S(1)}, bf16[192,768]{1,0:T(8,128)(2,1)S(1)}, u32[]{:S(2)}, u32[]{:S(2)}) %collective-permute-start.15) | collective-permute-done | bytes 294944 | tf_op jit(solution)/shard_map/ppermute | solution.py:937
  82.3 2.9 collective-permute-start.20
  88.8 11.4 %ssd_forward.1 = (f32[1024,768]{1,0:T(8,128)S(1)}, bf16[8,128,768]{2,1,0:T(8,128)(2,1)S(1)}) custom-call(f32[1024,768]{1,0:T(8,128)S(1)} %get-tuple-element.310.x_ref.xb_ref, f32[1024,768]{1,0:T(8,128)S(1)} %get-tuple-element.310.x_ref.xb_ref, f32[1024,256]{1,0:T(8,128)S(1)} %get-tuple-element.311.bc_ref.bcb_ref, ...), custom_call_target="tpu_custom_call" | custom-call | flops 14000000000 | bytes 40000000 | tf_op jit(solution)/shard_map/ssd_forward/pallas_call | solution.py:290
  100.2 1.5 collective-permute-done.18.refs_7_
  101.7 4.4 %collective-permute-done.19.refs_6_ = bf16[192,768]{1,0:T(8,128)(2,1)S(1)} collective-permute-done((bf16[192,768]{1,0:T(8,128)(2,1)S(1)}, bf16[192,768]{1,0:T(8,128)(2,1)S(1)}, u32[]{:S(2)}, u32[]{:S(2)}) %collective-permute-start.19) | collective-permute-done | bytes 294944 | tf_op jit(solution)/shard_map/ppermute | solution.py:946
  106.1 4.8 %gate_forward.1 = (f32[1024,768]{1,0:T(8,128)S(1)}, f32[8,1024]{1,0:T(8,128)S(1)}, bf16[1536,768]{1,0:T(8,128)(2,1)S(1)}) custom-call(s32[8]{0:T(128)S(1)} %stack.97.idx_ref, bf16[1024,1536]{1,0:T(8,128)(2,1)S(1)} %copy-done.6, f32[1024,768]{1,0:T(8,128)S(1)} %get-tuple-element.346.mixed_ref, bf16[192,768]{1,0:T(8,128)(2,1)S(1)} %copy-done.31, ...), custom_call_target="tpu_custom_call" | custom-call | flops 100000000 | bytes 200000 | tf_op jit(solution)/shard_map/gate_forward/pallas_call | solution.py:650
  111.6 1.5 collective-permute-start.27
  114.6 3.2 %collective-permute-done.24 = f32[8,1024]{1,0:T(8,128)S(1)} collective-permute-done((f32[8,1024]{1,0:T(8,128)S(1)}, f32[8,1024]{1,0:T(8,128)S(1)}, u32[]{:S(2)}, u32[]{:S(2)}) %collective-permute-start.24) | collective-permute-done | bytes 32800 | tf_op jit(solution)/shard_map/ppermute | solution.py:950
  119.4 3.9 %weight_grad.4 = (bf16[192,768]{1,0:T(8,128)(2,1)S(1)}, bf16[192,768]{1,0:T(8,128)(2,1)S(1)}, bf16[576,768]{1,0:T(8,128)(2,1)S(1)}, bf16[384,768]{1,0:T(8,128)(2,1)S(1)}, bf16[192,768]{1,0:T(8,128)(2,1)S(1)}) custom-call(s32[8]{0:T(128)S(1)} %stack.97.idx_ref, bf16[1536,1024]{1,0:T(8,128)(2,1)S(1)} %get-tuple-element.347.lhs_ref, ...), custom_call_target="tpu_custom_call" | custom-call | flops 100000000 | bytes 200000 | tf_op jit(solution)/shard_map/weight_grad/pallas_call | solution.py:805
  124.0 3.8 %collective-permute-done.26.refs_4_ = bf16[192,768]{1,0:T(8,128)(2,1)S(1)} collective-permute-done((bf16[192,768]{1,0:T(8,128)(2,1)}, bf16[192,768]{1,0:T(8,128)(2,1)S(1)}, u32[]{:S(2)}, u32[]{:S(2)}) %collective-permute-start.26) | collective-permute-done | bytes 294944 | tf_op jit(solution)/shard_map/ppermute | solution.py:937
  127.8 1.5 collective-permute-start.29
  129.3 7.1 %collective-permute-done.29.refs_7_ = bf16[192,768]{1,0:T(8,128)(2,1)S(1)} collective-permute-done((bf16[192,768]{1,0:T(8,128)(2,1)S(1)}, bf16[192,768]{1,0:T(8,128)(2,1)S(1)}, u32[]{:S(2)}, u32[]{:S(2)}) %collective-permute-start.29) | collective-permute-done | bytes 294944 | tf_op jit(solution)/shard_map/ppermute | solution.py:946
  138.5 5.0 %grad_gout.1 = (f32[1024,768]{1,0:T(8,128)S(1)}, f32[8,1024]{1,0:T(8,128)S(1)}, bf16[1536,768]{1,0:T(8,128)(2,1)S(1)}) custom-call(s32[8]{0:T(128)S(1)} %stack.97.idx_ref, bf16[1024,1536]{1,0:T(8,128)(2,1)S(1)} %get-tuple-element.362.cot_ref, f32[1024,768]{1,0:T(8,128)S(1)} %get-tuple-element.345.gate_ref, f32[1024,768]{1,0:T(8,128)S(1)} %get-tuple-element.346.mixed_ref, ...), custom_call_target="tpu_custom_call" | custom-call | flops 20000000000 | bytes 40000000 | tf_op jit(solution)/shard_map/grad_gout/pallas_call | solution.py:716
  145.4 2.4 collective-permute-done.33
  149.8 5.3 %out_partial.1 = (bf16[1024,384]{1,0:T(8,128)(2,1)S(1)}, bf16[1024,384]{1,0:T(8,128)(2,1)}, bf16[1024,384]{1,0:T(8,128)(2,1)S(1)}, bf16[1024,384]{1,0:T(8,128)(2,1)S(1)}) custom-call(s32[1]{0:T(128)} %bitcast.8.rank_ref, bf16[1024,768]{1,0:T(8,128)(2,1)S(1)} %gated_norm.1.rhs_ref.lhs_ref, bf16[1536,768]{1,0:T(8,128)(2,1)S(1)} %get-tuple-element.385.w_ref), custom_call_target="tpu_custom_call" | custom-call | flops 100000000 | bytes 200000 | tf_op jit(solution)/shard_map/out_partial/pallas_call | solution.py:835
  155.9 3.4 %gate_backward.1 = (bf16[1024,768]{1,0:T(8,128)(2,1)S(1)}, bf16[1024,768]{1,0:T(8,128)(2,1)S(1)}, f32[8,768]{1,0:T(8,128)S(1)}) custom-call(f32[1024,768]{1,0:T(8,128)S(1)} %get-tuple-element.345.gate_ref, f32[1024,768]{1,0:T(8,128)S(1)} %get-tuple-element.376.gout_ref, f32[1024,768]{1,0:T(8,128)S(1)} %get-tuple-element.346.mixed_ref, ...), custom_call_target="tpu_custom_call" | custom-call | flops 100000000 | bytes 200000 | tf_op jit(solution)/shard_map/gate_backward/pallas_call | solution.py:767
  160.0 3.9 %weight_grad.5 = (bf16[192,768]{1,0:T(8,128)(2,1)S(1)}, bf16[192,768]{1,0:T(8,128)(2,1)S(1)}, bf16[576,768]{1,0:T(8,128)(2,1)S(1)}, bf16[576,768]{1,0:T(8,128)(2,1)S(1)}) custom-call(s32[8]{0:T(128)S(1)} %copy-done.63, bf16[1536,1024]{1,0:T(8,128)(2,1)S(1)} %copy-done.3, bf16[1024,768]{1,0:T(8,128)(2,1)S(1)} %get-tuple-element.379.rhs_ref.gg_ref), custom_call_target="tpu_custom_call" | custom-call | flops 100000000 | bytes 200000 | tf_op jit(solution)/shard_map/weight_grad/pallas_call | solution.py:805
  182.2 1.5 convert_add_fusion.1
  183.8 1.5 add_convert_fusion.2
  185.4 1.6 collective-permute-start.43
  188.1 2.4 collective-permute-start.40
  191.0 1.9 collective-permute-start.42
  192.9 1.9 copy-done.82
  194.8 27.2 %ssd_backward.1 = (bf16[1024,768]{1,0:T(8,128)(2,1)S(1)}, bf16[1024,256]{1,0:T(8,128)(2,1)S(1)}, bf16[128,1024]{1,0:T(8,128)(2,1)S(1)}, bf16[128,1024]{1,0:T(8,1...) custom-call(s32[1]{0:T(128)} %bitcast.8.rank_ref, ...), custom_call_target="tpu_custom_call" | custom-call | flops 28000000000 | bytes 80000000 | tf_op jit(solution)/shard_map/ssd_backward/pallas_call | solution.py:319
  223.2 3.7 %collective-permute-start.46 = (bf16[192,768]{1,0:T(8,128)(2,1)S(1)}, bf16[192,768]{1,0:T(8,128)(2,1)S(1)}, u32[]{:S(2)}, u32[]{:S(2)}) collective-permute-start(bf16[192,768]{1,0:T(8,128)(2,1)S(1)} %get-tuple-element.577), channel_id=1, source_target_pairs={{8,0},{12,4},{16,8},{20,12},{24,16},{28,20},{0,24},{4,28},{9,1},{1... | collective-permute-start | bytes 884744 | tf_op jit(solution)/shard_map/ppermute | solution.py:937
  226.9 10.3 %normed_term.1 = (bf16[256,1536]{1,0:T(8,128)(2,1)S(1)}, bf16[256,1536]{1,0:T(8,128)(2,1)S(1)}, bf16[256,1536]{1,0:T(8,128)(2,1)S(1)}, bf16[256,1536]{1,0:T(8,128)(2,1)S(1)}, f32[8,1536]{1,0:T(8,128)S(1)}) custom-call(s32[1]{0:T(128)} %bitcast.8.rank_ref, bf16[1024,768]{1,0:T(8,128)(2,1)S(1)} %get-tuple-element.448.gx_ref.rhs_ref, ...), custom_call_target="tpu_custom_call" | custom-call | flops 100000000 | bytes 200000 | tf_op jit(solution)/shard_map/normed_term/pallas_call | solution.py:870
  239.7 3.9 %weight_grad.6 = (bf16[192,768]{1,0:T(8,128)(2,1)S(1)}, bf16[192,768]{1,0:T(8,128)(2,1)S(1)}, bf16[576,768]{1,0:T(8,128)(2,1)S(1)}, bf16[384,768]{1,0:T(8,128)(2,1)S(1)}, bf16[192,768]{1,0:T(8,128)(2,1)S(1)}) custom-call(s32[8]{0:T(128)S(1)} %copy-done.64, bf16[1536,1024]{1,0:T(8,128)(2,1)S(1)} %copy-done.4, ...), custom_call_target="tpu_custom_call" | custom-call | flops 20000000000 | bytes 40000000 | tf_op jit(solution)/shard_map/weight_grad/pallas_call | solution.py:805
  247.0 1.5 collective-permute-start.54
  251.3 2.1 weight_grad.7
  253.4 6.7 %collective-permute-done.55 = bf16[192,768]{1,0:T(8,128)(2,1)S(1)} collective-permute-done((bf16[192,768]{1,0:T(8,128)(2,1)S(1)}, bf16[192,768]{1,0:T(8,128)(2,1)S(1)}, u32[]{:S(2)}, u32[]{:S(2)}) %collective-permute-start.55) | collective-permute-done | bytes 294944 | tf_op jit(solution)/shard_map/ppermute | solution.py:937
  260.2 1.6 collective-permute-start.59
  262.4 7.1 %collective-permute-done.58 = bf16[384,768]{1,0:T(8,128)(2,1)S(1)} collective-permute-done((bf16[384,768]{1,0:T(8,128)(2,1)S(1)}, bf16[384,768]{1,0:T(8,128)(2,1)S(1)}, u32[]{:S(2)}, u32[]{:S(2)}) %collective-permute-start.58) | collective-permute-done | bytes 589856 | tf_op jit(solution)/shard_map/ppermute | solution.py:946
  269.7 1.7 collective-permute-done.59
  271.4 3.4 %collective-permute-done.57 = bf16[768,128]{1,0:T(8,128)(2,1)S(1)} collective-permute-done((bf16[768,128]{1,0:T(8,128)(2,1)S(1)}, bf16[768,128]{1,0:T(8,128)(2,1)S(1)}, u32[]{:S(2)}, u32[]{:S(2)}) %collective-permute-start.57) | collective-permute-done | bytes 196640 | tf_op jit(solution)/shard_map/ppermute | solution.py:946
  276.0 3.6 %collective-permute-start.64 = (bf16[192,768]{1,0:T(8,128)(2,1)S(1)}, bf16[192,768]{1,0:T(8,128)(2,1)S(1)}, u32[]{:S(2)}, u32[]{:S(2)}) collective-permute-start(bf16[192,768]{1,0:T(8,128)(2,1)S(1)} %get-tuple-element.489), channel_id=1, source_target_pairs={{8,0},{12,4},{16,8},{20,12},{24,16},{28,20},{0,24},{4,28},{9,1},{1... | collective-permute-start | bytes 884744 | tf_op jit(solution)/shard_map/ppermute | solution.py:937
  283.4 4.1 %collective-permute-done.62 = bf16[192,768]{1,0:T(8,128)(2,1)S(1)} collective-permute-done((bf16[192,768]{1,0:T(8,128)(2,1)S(1)}, bf16[192,768]{1,0:T(8,128)(2,1)S(1)}, u32[]{:S(2)}, u32[]{:S(2)}) %collective-permute-start.62) | collective-permute-done | bytes 294944 | tf_op jit(solution)/shard_map/ppermute | solution.py:937
  287.5 2.9 collective-permute-done.64
  290.4 1.5 collective-permute-start.69
  292.5 3.3 %collective-permute-start.67 = (bf16[192,128]{1,0:T(8,128)(2,1)S(1)}, bf16[192,128]{1,0:T(8,128)(2,1)S(1)}, u32[]{:S(2)}, u32[]{:S(2)}) collective-permute-start(bf16[192,128]{1,0:T(8,128)(2,1)S(1)} %get-tuple-element.587), channel_id=1, source_target_pairs={{8,0},{12,4},{16,8},{20,12},{24,16},{28,20},{0,24},{4,28},{9,1},{1... | collective-permute-start | bytes 147464 | tf_op jit(solution)/shard_map/ppermute | solution.py:937
  296.0 3.0 collective-permute-start.70
  299.4 1.9 copy.93
  301.3 1.9 copy.94
  308.9 1.6 copy.95
  313.9 1.7 multiply_subtract_fusion.2
  315.7 1.9 join_rows.3
  (397 shorter events, 77.6 us)
Async XLA Ops:
  6.7 17.6 %collective-permute-start = (bf16[192,896]{1,0:T(8,128)(2,1)S(1)}, bf16[192,896]{1,0:T(8,128)(2,1)}, u32[]{:S(2)}, u32[]{:S(2)}) collective-permute-start(bf16[192,896]{1,0:T(8,128)(2,1)S(1)} %get-tuple-element.283.refs_0_), channel_id=1, source_target_pairs={{8,0},{12,4},{16,8},{20,12},{24,16},{28,20},{0,24},{4,28},{9,1},{1... | collective-permute-start | bytes 1032200 | tf_op jit(solution)/shard_map/ppermute | solution.py:937
  11.8 17.0 %collective-permute-start.2 = (bf16[192,896]{1,0:T(8,128)(2,1)S(1)}, bf16[192,896]{1,0:T(8,128)(2,1)}, u32[]{:S(2)}, u32[]{:S(2)}) collective-permute-start(bf16[192,896]{1,0:T(8,128)(2,1)S(1)} %get-tuple-element.283.refs_0_), channel_id=1, source_target_pairs={{24,0},{28,4},{0,8},{4,12},{8,16},{12,20},{16,24},{20,28},{25,1},{... | collective-permute-start | bytes 1032200 | tf_op jit(solution)/shard_map/ppermute | solution.py:937
  11.8 29.4 %collective-permute-start.1 = (bf16[192,896]{1,0:T(8,128)(2,1)S(1)}, bf16[192,896]{1,0:T(8,128)(2,1)}, u32[]{:S(2)}, u32[]{:S(2)}) collective-permute-start(bf16[192,896]{1,0:T(8,128)(2,1)S(1)} %get-tuple-element.283.refs_0_), channel_id=1, source_target_pairs={{16,0},{20,4},{24,8},{28,12},{0,16},{4,20},{8,24},{12,28},{17,1},{... | collective-permute-start | bytes 1032200 | tf_op jit(solution)/shard_map/ppermute | solution.py:937
  12.8 28.4 %collective-permute-start.3 = (bf16[192,896]{1,0:T(8,128)(2,1)S(1)}, bf16[192,896]{1,0:T(8,128)(2,1)}, u32[]{:S(2)}, u32[]{:S(2)}) collective-permute-start(bf16[192,896]{1,0:T(8,128)(2,1)S(1)} %get-tuple-element.283.refs_0_), channel_id=1, source_target_pairs={{4,0},{0,4},{12,8},{8,12},{20,16},{16,20},{28,24},{24,28},{5,1},{1... | collective-permute-start | bytes 1032200 | tf_op jit(solution)/shard_map/ppermute | solution.py:946
  14.3 27.0 %collective-permute-start.6 = (bf16[1024,384]{1,0:T(8,128)(2,1)}, bf16[1024,384]{1,0:T(8,128)(2,1)}, u32[]{:S(2)}, u32[]{:S(2)}) collective-permute-start(bf16[1024,384]{1,0:T(8,128)(2,1)} %refs_0_.1), channel_id=1, source_target_pairs={{2,0},{3,1},{0,2},{1,3},{6,4},{7,5},{4,6},{5,7},{10,8},{11,9},{8,1... | collective-permute-start | bytes 2359304 | tf_op jit(solution)/shard_map/ppermute | solution.py:950
  24.3 16.9 %collective-permute-start.4 = (bf16[192,896]{1,0:T(8,128)(2,1)}, bf16[192,896]{1,0:T(8,128)(2,1)S(1)}, u32[]{:S(2)}, u32[]{:S(2)}) collective-permute-start(bf16[192,896]{1,0:T(8,128)(2,1)} %collective-permute-done.refs_2_), channel_id=1, source_target_pairs={{4,0},{0,4},{12,8},{8,12},{20,16},{16,20},{28,24},{24,28},{5,1},{1... | collective-permute-start | bytes 1032200 | tf_op jit(solution)/shard_map/ppermute | solution.py:946
  28.7 12.5 %collective-permute-start.5 = (bf16[192,896]{1,0:T(8,128)(2,1)}, bf16[192,896]{1,0:T(8,128)(2,1)S(1)}, u32[]{:S(2)}, u32[]{:S(2)}) collective-permute-start(bf16[192,896]{1,0:T(8,128)(2,1)} %collective-permute-done.2.refs_3_), channel_id=1, source_target_pairs={{4,0},{0,4},{12,8},{8,12},{20,16},{16,20},{28,24},{24,28},{5,1},{1... | collective-permute-start | bytes 1032200 | tf_op jit(solution)/shard_map/ppermute | solution.py:946
  41.2 7.2 %collective-permute-start.10 = (bf16[1024,384]{1,0:T(8,128)(2,1)}, bf16[1024,384]{1,0:T(8,128)(2,1)S(1)}, u32[]{:S(2)}, u32[]{:S(2)}) collective-permute-start(bf16[1024,384]{1,0:T(8,128)(2,1)} %refs_0_.1), channel_id=1, source_target_pairs={{1,0},{0,1},{3,2},{2,3},{5,4},{4,5},{7,6},{6,7},{9,8},{8,9},{11,10... | collective-permute-start | bytes 2359304 | tf_op jit(solution)/shard_map/ppermute | solution.py:950
  41.2 7.2 %collective-permute-start.11 = (bf16[1024,384]{1,0:T(8,128)(2,1)}, bf16[1024,384]{1,0:T(8,128)(2,1)S(1)}, u32[]{:S(2)}, u32[]{:S(2)}) collective-permute-start(bf16[1024,384]{1,0:T(8,128)(2,1)} %collective-permute-done.6.refs_2_), channel_id=1, source_target_pairs={{1,0},{0,1},{3,2},{2,3},{5,4},{4,5},{7,6},{6,7},{9,8},{8,9},{11,10... | collective-permute-start | bytes 2359304 | tf_op jit(solution)/shard_map/ppermute | solution.py:950
  41.9 18.9 %collective-permute-start.7 = (bf16[192,768]{1,0:T(8,128)(2,1)S(1)}, bf16[192,768]{1,0:T(8,128)(2,1)S(1)}, u32[]{:S(2)}, u32[]{:S(2)}) collective-permute-start(bf16[192,768]{1,0:T(8,128)(2,1)S(1)} %copy-done.30), channel_id=1, source_target_pairs={{8,0},{12,4},{16,8},{20,12},{24,16},{28,20},{0,24},{4,28},{9,1},{1... | collective-permute-start | bytes 884744 | tf_op jit(solution)/shard_map/ppermute | solution.py:937
  44.6 16.3 %collective-permute-start.8 = (bf16[192,768]{1,0:T(8,128)(2,1)S(1)}, bf16[192,768]{1,0:T(8,128)(2,1)S(1)}, u32[]{:S(2)}, u32[]{:S(2)}) collective-permute-start(bf16[192,768]{1,0:T(8,128)(2,1)S(1)} %copy-done.30), channel_id=1, source_target_pairs={{24,0},{28,4},{0,8},{4,12},{8,16},{12,20},{16,24},{20,28},{25,1},{... | collective-permute-start | bytes 884744 | tf_op jit(solution)/shard_map/ppermute | solution.py:937
  46.9 13.9 %collective-permute-start.9 = (bf16[192,896]{1,0:T(8,128)(2,1)}, bf16[192,896]{1,0:T(8,128)(2,1)S(1)}, u32[]{:S(2)}, u32[]{:S(2)}) collective-permute-start(bf16[192,896]{1,0:T(8,128)(2,1)} %collective-permute-done.1.refs_4_), channel_id=1, source_target_pairs={{4,0},{0,4},{12,8},{8,12},{20,16},{16,20},{28,24},{24,28},{5,1},{1... | collective-permute-start | bytes 1032200 | tf_op jit(solution)/shard_map/ppermute | solution.py:946
  65.6 9.9 %collective-permute-start.12 = (bf16[64,1024]{1,0:T(8,128)(2,1)S(1)}, bf16[64,1024]{1,0:T(8,128)(2,1)S(1)}, u32[]{:S(2)}, u32[]{:S(2)}) collective-permute-start(bf16[64,1024]{1,0:T(8,128)(2,1)S(1)} %get-tuple-element.302.refs_0_), channel_id=1, source_target_pairs={{1,0},{0,1},{3,2},{2,3},{5,4},{4,5},{7,6},{6,7},{9,8},{8,9},{11,10... | collective-permute-start | bytes 393224 | tf_op jit(solution)/shard_map/ppermute | solution.py:950
  65.6 16.6 %collective-permute-start.15 = (bf16[192,768]{1,0:T(8,128)(2,1)S(1)}, bf16[192,768]{1,0:T(8,128)(2,1)S(1)}, u32[]{:S(2)}, u32[]{:S(2)}) collective-permute-start(bf16[192,768]{1,0:T(8,128)(2,1)S(1)} %copy-done.30), channel_id=1, source_target_pairs={{16,0},{20,4},{24,8},{28,12},{0,16},{4,20},{8,24},{12,28},{17,1},{... | collective-permute-start | bytes 884744 | tf_op jit(solution)/shard_map/ppermute | solution.py:937
  66.4 15.9 %collective-permute-start.16 = (bf16[192,768]{1,0:T(8,128)(2,1)S(1)}, bf16[192,768]{1,0:T(8,128)(2,1)S(1)}, u32[]{:S(2)}, u32[]{:S(2)}) collective-permute-start(bf16[192,768]{1,0:T(8,128)(2,1)S(1)} %copy-done.30), channel_id=1, source_target_pairs={{4,0},{0,4},{12,8},{8,12},{20,16},{16,20},{28,24},{24,28},{5,1},{1... | collective-permute-start | bytes 884744 | tf_op jit(solution)/shard_map/ppermute | solution.py:946
  67.8 14.4 %collective-permute-start.17 = (bf16[192,768]{1,0:T(8,128)(2,1)S(1)}, bf16[192,768]{1,0:T(8,128)(2,1)S(1)}, u32[]{:S(2)}, u32[]{:S(2)}) collective-permute-start(bf16[192,768]{1,0:T(8,128)(2,1)S(1)} %collective-permute-done.7.refs_2_), channel_id=1, source_target_pairs={{4,0},{0,4},{12,8},{8,12},{20,16},{16,20},{28,24},{24,28},{5,1},{1... | collective-permute-start | bytes 884744 | tf_op jit(solution)/shard_map/ppermute | solution.py:946
  69.4 6.1 %collective-permute-start.14 = (bf16[64,1024]{1,0:T(8,128)(2,1)S(1)}, bf16[64,1024]{1,0:T(8,128)(2,1)S(1)}, u32[]{:S(2)}, u32[]{:S(2)}) collective-permute-start(bf16[64,1024]{1,0:T(8,128)(2,1)S(1)} %collective-permute-done.13.refs_2_), channel_id=1, source_target_pairs={{1,0},{0,1},{3,2},{2,3},{5,4},{4,5},{7,6},{6,7},{9,8},{8,9},{11,10... | collective-permute-start | bytes 393224 | tf_op jit(solution)/shard_map/ppermute | solution.py:950
  82.3 23.8 %collective-permute-start.20 = (bf16[192,768]{1,0:T(8,128)(2,1)}, bf16[192,768]{1,0:T(8,128)(2,1)S(1)}, u32[]{:S(2)}, u32[]{:S(2)}) collective-permute-start(bf16[192,768]{1,0:T(8,128)(2,1)} %convert_bitcast_fusion.refs_0_), channel_id=1, source_target_pairs={{8,0},{12,4},{16,8},{20,12},{24,16},{28,20},{0,24},{4,28},{9,1},{1... | collective-permute-start | bytes 884744 | tf_op jit(solution)/shard_map/ppermute | solution.py:937
  85.2 20.9 %collective-permute-start.21 = (bf16[192,768]{1,0:T(8,128)(2,1)}, bf16[192,768]{1,0:T(8,128)(2,1)S(1)}, u32[]{:S(2)}, u32[]{:S(2)}) collective-permute-start(bf16[192,768]{1,0:T(8,128)(2,1)} %convert_bitcast_fusion.refs_0_), channel_id=1, source_target_pairs={{24,0},{28,4},{0,8},{4,12},{8,16},{12,20},{16,24},{20,28},{25,1},{... | collective-permute-start | bytes 884744 | tf_op jit(solution)/shard_map/ppermute | solution.py:937
  85.2 20.9 %collective-permute-start.22 = (bf16[192,768]{1,0:T(8,128)(2,1)}, bf16[192,768]{1,0:T(8,128)(2,1)S(1)}, u32[]{:S(2)}, u32[]{:S(2)}) collective-permute-start(bf16[192,768]{1,0:T(8,128)(2,1)} %convert_bitcast_fusion.refs_0_), channel_id=1, source_target_pairs={{4,0},{0,4},{12,8},{8,12},{20,16},{16,20},{28,24},{24,28},{5,1},{1... | collective-permute-start | bytes 884744 | tf_op jit(solution)/shard_map/ppermute | solution.py:946
  86.7 15.0 %collective-permute-start.18 = (bf16[192,768]{1,0:T(8,128)(2,1)S(1)}, bf16[192,768]{1,0:T(8,128)(2,1)S(1)}, u32[]{:S(2)}, u32[]{:S(2)}) collective-permute-start(bf16[192,768]{1,0:T(8,128)(2,1)S(1)} %collective-permute-done.15.refs_4_), channel_id=1, source_target_pairs={{4,0},{0,4},{12,8},{8,12},{20,16},{16,20},{28,24},{24,28},{5,1},{1... | collective-permute-start | bytes 884744 | tf_op jit(solution)/shard_map/ppermute | solution.py:946
  87.2 18.9 %collective-permute-start.19 = (bf16[192,768]{1,0:T(8,128)(2,1)S(1)}, bf16[192,768]{1,0:T(8,128)(2,1)S(1)}, u32[]{:S(2)}, u32[]{:S(2)}) collective-permute-start(bf16[192,768]{1,0:T(8,128)(2,1)S(1)} %collective-permute-done.8.refs_3_), channel_id=1, source_target_pairs={{4,0},{0,4},{12,8},{8,12},{20,16},{16,20},{28,24},{24,28},{5,1},{1... | collective-permute-start | bytes 884744 | tf_op jit(solution)/shard_map/ppermute | solution.py:946
  111.0 16.9 %collective-permute-start.26 = (bf16[192,768]{1,0:T(8,128)(2,1)}, bf16[192,768]{1,0:T(8,128)(2,1)S(1)}, u32[]{:S(2)}, u32[]{:S(2)}) collective-permute-start(bf16[192,768]{1,0:T(8,128)(2,1)} %convert_bitcast_fusion.refs_0_), channel_id=1, source_target_pairs={{16,0},{20,4},{24,8},{28,12},{0,16},{4,20},{8,24},{12,28},{17,1},{... | collective-permute-start | bytes 884744 | tf_op jit(solution)/shard_map/ppermute | solution.py:937
  111.6 16.2 %collective-permute-start.27 = (bf16[192,768]{1,0:T(8,128)(2,1)S(1)}, bf16[192,768]{1,0:T(8,128)(2,1)S(1)}, u32[]{:S(2)}, u32[]{:S(2)}) collective-permute-start(bf16[192,768]{1,0:T(8,128)(2,1)S(1)} %collective-permute-done.20.refs_2_), channel_id=1, source_target_pairs={{4,0},{0,4},{12,8},{8,12},{20,16},{16,20},{28,24},{24,28},{5,1},{1... | collective-permute-start | bytes 884744 | tf_op jit(solution)/shard_map/ppermute | solution.py:946
  113.1 14.7 %collective-permute-start.28 = (bf16[192,768]{1,0:T(8,128)(2,1)S(1)}, bf16[192,768]{1,0:T(8,128)(2,1)S(1)}, u32[]{:S(2)}, u32[]{:S(2)}) collective-permute-start(bf16[192,768]{1,0:T(8,128)(2,1)S(1)} %collective-permute-done.21.refs_3_), channel_id=1, source_target_pairs={{4,0},{0,4},{12,8},{8,12},{20,16},{16,20},{28,24},{24,28},{5,1},{1... | collective-permute-start | bytes 884744 | tf_op jit(solution)/shard_map/ppermute | solution.py:946
  127.8 8.6 %collective-permute-start.29 = (bf16[192,768]{1,0:T(8,128)(2,1)S(1)}, bf16[192,768]{1,0:T(8,128)(2,1)S(1)}, u32[]{:S(2)}, u32[]{:S(2)}) collective-permute-start(bf16[192,768]{1,0:T(8,128)(2,1)S(1)} %collective-permute-done.26.refs_4_), channel_id=1, source_target_pairs={{4,0},{0,4},{12,8},{8,12},{20,16},{16,20},{28,24},{24,28},{5,1},{1... | collective-permute-start | bytes 884744 | tf_op jit(solution)/shard_map/ppermute | solution.py:946
  136.4 11.4 %collective-permute-start.31 = (bf16[192,768]{1,0:T(8,128)(2,1)S(1)}, bf16[192,768]{1,0:T(8,128)(2,1)}, u32[]{:S(2)}, u32[]{:S(2)}) collective-permute-start(bf16[192,768]{1,0:T(8,128)(2,1)S(1)} %get-tuple-element.361), channel_id=1, source_target_pairs={{4,0},{0,4},{12,8},{8,12},{20,16},{16,20},{28,24},{24,28},{5,1},{1... | collective-permute-start | bytes 884744 | tf_op jit(solution)/shard_map/ppermute | solution.py:946
  137.9 31.4 %collective-permute-start.30 = (bf16[384,768]{1,0:T(8,128)(2,1)S(1)}, bf16[384,768]{1,0:T(8,128)(2,1)S(1)}, u32[]{:S(2)}, u32[]{:S(2)}) collective-permute-start(bf16[384,768]{1,0:T(8,128)(2,1)S(1)} %get-tuple-element.360), channel_id=1, source_target_pairs={{4,0},{0,4},{12,8},{8,12},{20,16},{16,20},{28,24},{24,28},{5,1},{1... | collective-permute-start | bytes 1769480 | tf_op jit(solution)/shard_map/ppermute | solution.py:946
  147.8 19.4 %collective-permute-start.35 = (bf16[64,1536]{1,0:T(8,128)(2,1)S(1)}, bf16[64,1536]{1,0:T(8,128)(2,1)S(1)}, u32[]{:S(2)}, u32[]{:S(2)}) collective-permute-start(bf16[64,1536]{1,0:T(8,128)(2,1)S(1)} %get-tuple-element.427.refs_0_), channel_id=1, source_target_pairs={{1,0},{0,1},{3,2},{2,3},{5,4},{4,5},{7,6},{6,7},{9,8},{8,9},{11,10... | collective-permute-start | bytes 589832 | tf_op jit(solution)/shard_map/ppermute | solution.py:950
  148.3 19.6 %collective-permute-start.36 = (bf16[64,1536]{1,0:T(8,128)(2,1)S(1)}, bf16[64,1536]{1,0:T(8,128)(2,1)S(1)}, u32[]{:S(2)}, u32[]{:S(2)}) collective-permute-start(bf16[64,1536]{1,0:T(8,128)(2,1)S(1)} %get-tuple-element.427.refs_0_), channel_id=1, source_target_pairs={{2,0},{3,1},{0,2},{1,3},{6,4},{7,5},{4,6},{5,7},{10,8},{11,9},{8,1... | collective-permute-start | bytes 589832 | tf_op jit(solution)/shard_map/ppermute | solution.py:950
  149.5 19.1 %collective-permute-start.37 = (bf16[64,1536]{1,0:T(8,128)(2,1)S(1)}, bf16[64,1536]{1,0:T(8,128)(2,1)S(1)}, u32[]{:S(2)}, u32[]{:S(2)}) collective-permute-start(bf16[64,1536]{1,0:T(8,128)(2,1)S(1)} %get-tuple-element.427.refs_0_), channel_id=1, source_target_pairs={{3,0},{2,1},{1,2},{0,3},{7,4},{6,5},{5,6},{4,7},{11,8},{10,9},{9,1... | collective-permute-start | bytes 589832 | tf_op jit(solution)/shard_map/ppermute | solution.py:950
  170.1 12.1 %collective-permute-start.39 = (bf16[1024,384]{1,0:T(8,128)(2,1)}, bf16[1024,384]{1,0:T(8,128)(2,1)}, u32[]{:S(2)}, u32[]{:S(2)}) collective-permute-start(bf16[1024,384]{1,0:T(8,128)(2,1)} %get-tuple-element.395), channel_id=1, source_target_pairs={{1,0},{0,1},{3,2},{2,3},{5,4},{4,5},{7,6},{6,7},{9,8},{8,9},{11,10... | collective-permute-start | bytes 2359304 | tf_op jit(solution)/shard_map/ppermute | solution.py:950
  172.2 11.6 %collective-permute-start.38 = (bf16[1024,384]{1,0:T(8,128)(2,1)}, bf16[1024,384]{1,0:T(8,128)(2,1)}, u32[]{:S(2)}, u32[]{:S(2)}) collective-permute-start(bf16[1024,384]{1,0:T(8,128)(2,1)} %copy-done.78), channel_id=1, source_target_pairs={{1,0},{0,1},{3,2},{2,3},{5,4},{4,5},{7,6},{6,7},{9,8},{8,9},{11,10... | collective-permute-start | bytes 2359304 | tf_op jit(solution)/shard_map/ppermute | solution.py:950
  185.4 36.7 %collective-permute-start.43 = (bf16[576,768]{1,0:T(8,128)(2,1)S(1)}, bf16[576,768]{1,0:T(8,128)(2,1)S(1)}, u32[]{:S(2)}, u32[]{:S(2)}) collective-permute-start(bf16[576,768]{1,0:T(8,128)(2,1)S(1)} %copy-done.77), channel_id=1, source_target_pairs={{4,0},{0,4},{12,8},{8,12},{20,16},{16,20},{28,24},{24,28},{5,1},{1... | collective-permute-start | bytes 2654216 | tf_op jit(solution)/shard_map/ppermute | solution.py:946
  186.9 35.1 %collective-permute-start.44 = (bf16[1024,384]{1,0:T(8,128)(2,1)S(1)}, bf16[1024,384]{1,0:T(8,128)(2,1)S(1)}, u32[]{:S(2)}, u32[]{:S(2)}) collective-permute-start(bf16[1024,384]{1,0:T(8,128)(2,1)S(1)} %add_convert_fusion.2), channel_id=1, source_target_pairs={{2,0},{3,1},{0,2},{1,3},{6,4},{7,5},{4,6},{5,7},{10,8},{11,9},{8,1... | collective-permute-start | bytes 2359304 | tf_op jit(solution)/shard_map/ppermute | solution.py:950
  188.1 33.9 %collective-permute-start.40 = (bf16[192,768]{1,0:T(8,128)(2,1)S(1)}, bf16[192,768]{1,0:T(8,128)(2,1)S(1)}, u32[]{:S(2)}, u32[]{:S(2)}) collective-permute-start(bf16[192,768]{1,0:T(8,128)(2,1)S(1)} %get-tuple-element.402), channel_id=1, source_target_pairs={{24,0},{28,4},{0,8},{4,12},{8,16},{12,20},{16,24},{20,28},{25,1},{... | collective-permute-start | bytes 884744 | tf_op jit(solution)/shard_map/ppermute | solution.py:937
  190.5 31.5 %collective-permute-start.41 = (bf16[192,768]{1,0:T(8,128)(2,1)S(1)}, bf16[192,768]{1,0:T(8,128)(2,1)S(1)}, u32[]{:S(2)}, u32[]{:S(2)}) collective-permute-start(bf16[192,768]{1,0:T(8,128)(2,1)S(1)} %get-tuple-element.403), channel_id=1, source_target_pairs={{16,0},{20,4},{24,8},{28,12},{0,16},{4,20},{8,24},{12,28},{17,1},{... | collective-permute-start | bytes 884744 | tf_op jit(solution)/shard_map/ppermute | solution.py:937
  191.0 31.1 %collective-permute-start.42 = (bf16[192,768]{1,0:T(8,128)(2,1)S(1)}, bf16[192,768]{1,0:T(8,128)(2,1)S(1)}, u32[]{:S(2)}, u32[]{:S(2)}) collective-permute-start(bf16[192,768]{1,0:T(8,128)(2,1)S(1)} %get-tuple-element.404), channel_id=1, source_target_pairs={{8,0},{12,4},{16,8},{20,12},{24,16},{28,20},{0,24},{4,28},{9,1},{1... | collective-permute-start | bytes 884744 | tf_op jit(solution)/shard_map/ppermute | solution.py:937
  222.2 16.3 %collective-permute-start.47 = (bf16[192,1536]{1,0:T(8,128)(2,1)S(1)}, bf16[192,1536]{1,0:T(8,128)(2,1)S(1)}, u32[]{:S(2)}, u32[]{:S(2)}) collective-permute-start(bf16[192,1536]{1,0:T(8,128)(2,1)S(1)} %pad_maximum_fusion), channel_id=1, source_target_pairs={{4,0},{0,4},{12,8},{8,12},{20,16},{16,20},{28,24},{24,28},{5,1},{1... | collective-permute-start | bytes 1769480 | tf_op jit(solution)/shard_map/ppermute | solution.py:946
  223.0 15.5 %collective-permute-start.45 = (bf16[192,768]{1,0:T(8,128)(2,1)S(1)}, bf16[192,768]{1,0:T(8,128)(2,1)S(1)}, u32[]{:S(2)}, u32[]{:S(2)}) collective-permute-start(bf16[192,768]{1,0:T(8,128)(2,1)S(1)} %get-tuple-element.578), channel_id=1, source_target_pairs={{24,0},{28,4},{0,8},{4,12},{8,16},{12,20},{16,24},{20,28},{25,1},{... | collective-permute-start | bytes 884744 | tf_op jit(solution)/shard_map/ppermute | solution.py:937
  223.2 15.3 %collective-permute-start.46 = (bf16[192,768]{1,0:T(8,128)(2,1)S(1)}, bf16[192,768]{1,0:T(8,128)(2,1)S(1)}, u32[]{:S(2)}, u32[]{:S(2)}) collective-permute-start(bf16[192,768]{1,0:T(8,128)(2,1)S(1)} %get-tuple-element.577), channel_id=1, source_target_pairs={{8,0},{12,4},{16,8},{20,12},{24,16},{28,20},{0,24},{4,28},{9,1},{1... | collective-permute-start | bytes 884744 | tf_op jit(solution)/shard_map/ppermute | solution.py:937
  226.9 11.6 %collective-permute-start.48 = (bf16[128,1024]{1,0:T(8,128)(2,1)S(1)}, bf16[128,1024]{1,0:T(8,128)(2,1)S(1)}, u32[]{:S(2)}, u32[]{:S(2)}) collective-permute-start(bf16[128,1024]{1,0:T(8,128)(2,1)S(1)} %get-tuple-element.441), channel_id=1, source_target_pairs={{1,0},{0,1},{3,2},{2,3},{5,4},{4,5},{7,6},{6,7},{9,8},{8,9},{11,10... | collective-permute-start | bytes 786440 | tf_op jit(solution)/shard_map/ppermute | solution.py:950
  238.6 8.4 %collective-permute-start.52 = (bf16[64,1024]{1,0:T(8,128)(2,1)S(1)}, bf16[64,1024]{1,0:T(8,128)(2,1)S(1)}, u32[]{:S(2)}, u32[]{:S(2)}) collective-permute-start(bf16[64,1024]{1,0:T(8,128)(2,1)S(1)} %slice.193), channel_id=1, source_target_pairs={{2,0},{3,1},{0,2},{1,3},{6,4},{7,5},{4,6},{5,7},{10,8},{11,9},{8,1... | collective-permute-start | bytes 393224 | tf_op jit(solution)/shard_map/ppermute | solution.py:950
  239.4 7.1 %collective-permute-start.50 = (bf16[256,1536]{1,0:T(8,128)(2,1)S(1)}, bf16[256,1536]{1,0:T(8,128)(2,1)S(1)}, u32[]{:S(2)}, u32[]{:S(2)}) collective-permute-start(bf16[256,1536]{1,0:T(8,128)(2,1)S(1)} %get-tuple-element.445), channel_id=1, source_target_pairs={{1,0},{0,1},{3,2},{2,3},{5,4},{4,5},{7,6},{6,7},{9,8},{8,9},{11,10... | collective-permute-start | bytes 2359304 | tf_op jit(solution)/shard_map/ppermute | solution.py:950
  244.2 15.9 %collective-permute-start.55 = (bf16[192,768]{1,0:T(8,128)(2,1)S(1)}, bf16[192,768]{1,0:T(8,128)(2,1)S(1)}, u32[]{:S(2)}, u32[]{:S(2)}) collective-permute-start(bf16[192,768]{1,0:T(8,128)(2,1)S(1)} %get-tuple-element.461), channel_id=1, source_target_pairs={{16,0},{20,4},{24,8},{28,12},{0,16},{4,20},{8,24},{12,28},{17,1},{... | collective-permute-start | bytes 884744 | tf_op jit(solution)/shard_map/ppermute | solution.py:937
  247.0 13.1 %collective-permute-start.54 = (bf16[192,768]{1,0:T(8,128)(2,1)S(1)}, bf16[192,768]{1,0:T(8,128)(2,1)S(1)}, u32[]{:S(2)}, u32[]{:S(2)}) collective-permute-start(bf16[192,768]{1,0:T(8,128)(2,1)S(1)} %get-tuple-element.458), channel_id=1, source_target_pairs={{4,0},{0,4},{12,8},{8,12},{20,16},{16,20},{28,24},{24,28},{5,1},{1... | collective-permute-start | bytes 884744 | tf_op jit(solution)/shard_map/ppermute | solution.py:946
  248.5 11.6 %collective-permute-start.56 = (f32[8,1792]{1,0:T(8,128)S(1)}, f32[8,1792]{1,0:T(8,128)S(1)}, u32[]{:S(2)}, u32[]{:S(2)}) collective-permute-start(f32[8,1792]{1,0:T(8,128)S(1)} %add.322), channel_id=1, source_target_pairs={{2,0},{3,1},{0,2},{1,3},{6,4},{7,5},{4,6},{5,7},{10,8},{11,9},{8,1... | collective-permute-start | bytes 172040 | tf_op jit(solution)/shard_map/ppermute | solution.py:950
  249.7 19.8 %collective-permute-start.58 = (bf16[384,768]{1,0:T(8,128)(2,1)S(1)}, bf16[384,768]{1,0:T(8,128)(2,1)S(1)}, u32[]{:S(2)}, u32[]{:S(2)}) collective-permute-start(bf16[384,768]{1,0:T(8,128)(2,1)S(1)} %get-tuple-element.469), channel_id=1, source_target_pairs={{4,0},{0,4},{12,8},{8,12},{20,16},{16,20},{28,24},{24,28},{5,1},{1... | collective-permute-start | bytes 1769480 | tf_op jit(solution)/shard_map/ppermute | solution.py:946
  250.2 24.6 %collective-permute-start.53 = (bf16[256,1536]{1,0:T(8,128)(2,1)S(1)}, bf16[256,1536]{1,0:T(8,128)(2,1)S(1)}, u32[]{:S(2)}, u32[]{:S(2)}) collective-permute-start(bf16[256,1536]{1,0:T(8,128)(2,1)S(1)} %add_convert_fusion), channel_id=1, source_target_pairs={{2,0},{3,1},{0,2},{1,3},{6,4},{7,5},{4,6},{5,7},{10,8},{11,9},{8,1... | collective-permute-start | bytes 2359304 | tf_op jit(solution)/shard_map/ppermute | solution.py:950
  260.2 11.2 %collective-permute-start.59 = (f32[8,2688]{1,0:T(8,128)S(1)}, f32[8,2688]{1,0:T(8,128)S(1)}, u32[]{:S(2)}, u32[]{:S(2)}) collective-permute-start(f32[8,2688]{1,0:T(8,128)S(1)} %pad_maximum_fusion.1), channel_id=1, source_target_pairs={{4,0},{0,4},{12,8},{8,12},{20,16},{16,20},{28,24},{24,28},{5,1},{1... | collective-permute-start | bytes 258056 | tf_op jit(solution)/shard_map/ppermute | solution.py:946
  261.7 13.1 %collective-permute-start.57 = (bf16[768,128]{1,0:T(8,128)(2,1)S(1)}, bf16[768,128]{1,0:T(8,128)(2,1)S(1)}, u32[]{:S(2)}, u32[]{:S(2)}) collective-permute-start(bf16[768,128]{1,0:T(8,128)(2,1)S(1)} %get-tuple-element.468), channel_id=1, source_target_pairs={{4,0},{0,4},{12,8},{8,12},{20,16},{16,20},{28,24},{24,28},{5,1},{1... | collective-permute-start | bytes 589832 | tf_op jit(solution)/shard_map/ppermute | solution.py:946
  262.3 21.0 %collective-permute-start.63 = (bf16[192,768]{1,0:T(8,128)(2,1)S(1)}, bf16[192,768]{1,0:T(8,128)(2,1)S(1)}, u32[]{:S(2)}, u32[]{:S(2)}) collective-permute-start(bf16[192,768]{1,0:T(8,128)(2,1)S(1)} %add_convert_fusion.3), channel_id=1, source_target_pairs={{16,0},{20,4},{24,8},{28,12},{0,16},{4,20},{8,24},{12,28},{17,1},{... | collective-permute-start | bytes 884744 | tf_op jit(solution)/shard_map/ppermute | solution.py:937
  275.7 11.8 %collective-permute-start.62 = (bf16[192,768]{1,0:T(8,128)(2,1)S(1)}, bf16[192,768]{1,0:T(8,128)(2,1)S(1)}, u32[]{:S(2)}, u32[]{:S(2)}) collective-permute-start(bf16[192,768]{1,0:T(8,128)(2,1)S(1)} %get-tuple-element.486), channel_id=1, source_target_pairs={{24,0},{28,4},{0,8},{4,12},{8,16},{12,20},{16,24},{20,28},{25,1},{... | collective-permute-start | bytes 884744 | tf_op jit(solution)/shard_map/ppermute | solution.py:937
  276.0 14.4 %collective-permute-start.64 = (bf16[192,768]{1,0:T(8,128)(2,1)S(1)}, bf16[192,768]{1,0:T(8,128)(2,1)S(1)}, u32[]{:S(2)}, u32[]{:S(2)}) collective-permute-start(bf16[192,768]{1,0:T(8,128)(2,1)S(1)} %get-tuple-element.489), channel_id=1, source_target_pairs={{8,0},{12,4},{16,8},{20,12},{24,16},{28,20},{0,24},{4,28},{9,1},{1... | collective-permute-start | bytes 884744 | tf_op jit(solution)/shard_map/ppermute | solution.py:937
  279.6 10.8 %collective-permute-start.65 = (bf16[192,768]{1,0:T(8,128)(2,1)S(1)}, bf16[192,768]{1,0:T(8,128)(2,1)S(1)}, u32[]{:S(2)}, u32[]{:S(2)}) collective-permute-start(bf16[192,768]{1,0:T(8,128)(2,1)S(1)} %get-tuple-element.490), channel_id=1, source_target_pairs={{4,0},{0,4},{12,8},{8,12},{20,16},{16,20},{28,24},{24,28},{5,1},{1... | collective-permute-start | bytes 884744 | tf_op jit(solution)/shard_map/ppermute | solution.py:946
  282.1 21.5 %collective-permute-start.61 = (bf16[256,1536]{1,0:T(8,128)(2,1)S(1)}, bf16[256,1536]{1,0:T(8,128)(2,1)S(1)}, u32[]{:S(2)}, u32[]{:S(2)}) collective-permute-start(bf16[256,1536]{1,0:T(8,128)(2,1)S(1)} %norm_backward.1.refs_0_), channel_id=1, source_target_pairs={{2,0},{3,1},{0,2},{1,3},{6,4},{7,5},{4,6},{5,7},{10,8},{11,9},{8,1... | collective-permute-start | bytes 2359304 | tf_op jit(solution)/shard_map/ppermute | solution.py:950
  291.9 11.7 %collective-permute-start.66 = (bf16[192,128]{1,0:T(8,128)(2,1)S(1)}, bf16[192,128]{1,0:T(8,128)(2,1)S(1)}, u32[]{:S(2)}, u32[]{:S(2)}) collective-permute-start(bf16[192,128]{1,0:T(8,128)(2,1)S(1)} %get-tuple-element.588), channel_id=1, source_target_pairs={{24,0},{28,4},{0,8},{4,12},{8,16},{12,20},{16,24},{20,28},{25,1},{... | collective-permute-start | bytes 147464 | tf_op jit(solution)/shard_map/ppermute | solution.py:937
  292.5 11.1 %collective-permute-start.67 = (bf16[192,128]{1,0:T(8,128)(2,1)S(1)}, bf16[192,128]{1,0:T(8,128)(2,1)S(1)}, u32[]{:S(2)}, u32[]{:S(2)}) collective-permute-start(bf16[192,128]{1,0:T(8,128)(2,1)S(1)} %get-tuple-element.587), channel_id=1, source_target_pairs={{8,0},{12,4},{16,8},{20,12},{24,16},{28,20},{0,24},{4,28},{9,1},{1... | collective-permute-start | bytes 147464 | tf_op jit(solution)/shard_map/ppermute | solution.py:937
  295.8 7.8 %collective-permute-start.68 = (bf16[192,128]{1,0:T(8,128)(2,1)S(1)}, bf16[192,128]{1,0:T(8,128)(2,1)S(1)}, u32[]{:S(2)}, u32[]{:S(2)}) collective-permute-start(bf16[192,128]{1,0:T(8,128)(2,1)S(1)} %get-tuple-element.586), channel_id=1, source_target_pairs={{16,0},{20,4},{24,8},{28,12},{0,16},{4,20},{8,24},{12,28},{17,1},{... | collective-permute-start | bytes 147464 | tf_op jit(solution)/shard_map/ppermute | solution.py:937
  296.0 7.5 %collective-permute-start.70 = (f32[8,2688]{1,0:T(8,128)S(1)}, f32[8,2688]{1,0:T(8,128)S(1)}, u32[]{:S(2)}, u32[]{:S(2)}) collective-permute-start(f32[8,2688]{1,0:T(8,128)S(1)} %add.334), channel_id=1, source_target_pairs={{16,0},{20,4},{24,8},{28,12},{0,16},{4,20},{8,24},{12,28},{17,1},{... | collective-permute-start | bytes 258056 | tf_op jit(solution)/shard_map/ppermute | solution.py:942
  303.6 12.1 %collective-permute-start.60 = (bf16[256,1536]{1,0:T(8,128)(2,1)S(1)}, bf16[256,1536]{1,0:T(8,128)(2,1)S(1)}, u32[]{:S(2)}, u32[]{:S(2)}) collective-permute-start(bf16[256,1536]{1,0:T(8,128)(2,1)S(1)} %norm_backward.1.refs_0_), channel_id=1, source_target_pairs={{1,0},{0,1},{3,2},{2,3},{5,4},{4,5},{7,6},{6,7},{9,8},{8,9},{11,10... | collective-permute-start | bytes 2359304 | tf_op jit(solution)/shard_map/ppermute | solution.py:950
  303.7 8.0 %collective-permute-start.74 = (f32[192,64]{1,0:T(8,128)S(1)}, f32[192,64]{1,0:T(8,128)}, u32[]{:S(2)}, u32[]{:S(2)}) collective-permute-start(f32[192,64]{1,0:T(8,128)S(1)} %bitcast.44), channel_id=1, source_target_pairs={{1,0},{0,1},{3,2},{2,3},{5,4},{4,5},{7,6},{6,7},{9,8},{8,9},{11,10... | collective-permute-start | bytes 147464 | tf_op jit(solution)/shard_map/ppermute | solution.py:950
  304.2 6.9 %collective-permute-start.72 = (f32[192,64]{1,0:T(8,128)S(1)}, f32[192,64]{1,0:T(8,128)}, u32[]{:S(2)}, u32[]{:S(2)}) collective-permute-start(f32[192,64]{1,0:T(8,128)S(1)} %bitcast.45), channel_id=1, source_target_pairs={{2,0},{3,1},{0,2},{1,3},{6,4},{7,5},{4,6},{5,7},{10,8},{11,9},{8,1... | collective-permute-start | bytes 147464 | tf_op jit(solution)/shard_map/ppermute | solution.py:950
  305.7 10.0 %collective-permute-start.71 = (bf16[256,1536]{1,0:T(8,128)(2,1)S(1)}, bf16[256,1536]{1,0:T(8,128)(2,1)S(1)}, u32[]{:S(2)}, u32[]{:S(2)}) collective-permute-start(bf16[256,1536]{1,0:T(8,128)(2,1)S(1)} %collective-permute-done.61.refs_2_), channel_id=1, source_target_pairs={{1,0},{0,1},{3,2},{2,3},{5,4},{4,5},{7,6},{6,7},{9,8},{8,9},{11,10... | collective-permute-start | bytes 2359304 | tf_op jit(solution)/shard_map/ppermute | solution.py:950
  (117 other events, 1378.5 us)

commit v5 on v4

--- a/solution.py
+++ b/solution.py
@@ -17,6 +17,14 @@
 bf16 = jnp.bfloat16
 f32 = jnp.float32
 MIB = 1024 * 1024
+
+
+def hbm(shape, dtype):
+    return pltpu.HBM(shape, dtype)
+
+
+def from_hbm(v):
+    return pltpu.with_memory_space_constraint(v, pltpu.HBM)
 
 
 def dot_nn(a, b):
@@ -139,16 +147,10 @@
     dx_ref, dbc_ref, keep_ref, send_ref, dst_ref, dst_t_ref, dconv_ref, dbct_ref, dheads_ref,
     dstate, xs_scr, bc_scr, du_scr, dubc_scr, share_scr,
 ):
-    at = pl.program_id(0)
-
-    @pl.when(at == 0)
+    @pl.when(pl.program_id(0) == 0)
     def _():
-        dstate[...] = jnp.zeros_like(dstate)
-        du_scr[...] = jnp.zeros_like(du_scr)
-        dubc_scr[...] = jnp.zeros_like(dubc_scr)
-        dconv_ref[...] = jnp.zeros_like(dconv_ref)
-        dbct_ref[...] = jnp.zeros_like(dbct_ref)
-        dheads_ref[...] = jnp.zeros_like(dheads_ref)
+        for ref in (dstate, du_scr, dubc_scr, dconv_ref, dbct_ref, dheads_ref):
+            ref[...] = jnp.zeros_like(ref)
 
     channels = x_ref.shape[1]
     aux = aux_ref[...]
@@ -296,8 +298,8 @@
             pl.BlockSpec((None, LANES, channels), lambda i: (i, 0, 0)),
         ],
         out_shape=[
-            jax.ShapeDtypeStruct((tokens, channels), f32),
-            jax.ShapeDtypeStruct((count, LANES, channels), bf16),
+            hbm((tokens, channels), f32),
+            hbm((count, LANES, channels), bf16),
         ],
         scratch_shapes=[
             pltpu.VMEM((LANES, channels), f32),
@@ -307,7 +309,9 @@
         compiler_params=pltpu.CompilerParams(vmem_limit_bytes=14 * MIB),
         cost_estimate=pl.CostEstimate(flops=14 * 10**9, bytes_accessed=40 * 10**6, transcendentals=0),
         name="ssd_forward",
-    )(x_pre, x_pre, bc_pre, bc_pre, step_pre, aux, seg_row, conv_rows, bc_rows, head_rows, expand)
+    )(
+        from_hbm(x_pre), from_hbm(x_pre), bc_pre, bc_pre, step_pre, aux, seg_row, conv_rows, bc_rows, head_rows, expand
+    )
 
 
 def ssd_backward(rank, x_pre, bc_pre, step_pre, aux, seg_row, conv_rows, bc_rows, head_rows, expand, mixed, dy, states):
@@ -316,6 +320,11 @@
     place = lambda i: count - 1 - i
     now = lambda i: (place(i), 0)
     whole = lambda i: (0, 0)
+    sums = [
+        jax.ShapeDtypeStruct((8, channels), f32),
+        jax.ShapeDtypeStruct((8, 2 * LANES), f32),
+        jax.ShapeDtypeStruct((8, LANES), f32),
+    ]
     return pl.pallas_call(
         ssd_backward_kernel,
         grid=(count,),
@@ -331,21 +340,15 @@
             pl.BlockSpec((LANES, CHUNK), lambda i: (0, place(i))),
             pl.BlockSpec((CHUNK, LANES), now),
             pl.BlockSpec((16, CHUNK), lambda i: (0, place(i))),
-            pl.BlockSpec((8, channels), whole),
-            pl.BlockSpec((8, 2 * LANES), whole),
-            pl.BlockSpec((8, LANES), whole),
-        ],
+        ] + [pl.BlockSpec(v.shape, whole) for v in sums],
         out_shape=[
-            jax.ShapeDtypeStruct((tokens, channels), bf16),
-            jax.ShapeDtypeStruct((tokens, 2 * LANES), bf16),
-            jax.ShapeDtypeStruct((LANES, tokens), bf16),
-            jax.ShapeDtypeStruct((LANES, tokens), bf16),
-            jax.ShapeDtypeStruct((tokens, LANES), bf16),
-            jax.ShapeDtypeStruct((16, tokens), bf16),
-            jax.ShapeDtypeStruct((8, channels), f32),
-            jax.ShapeDtypeStruct((8, 2 * LANES), f32),
-            jax.ShapeDtypeStruct((8, LANES), f32),
-        ],
+            hbm((tokens, channels), bf16),
+            hbm((tokens, 2 * LANES), bf16),
+            hbm((LANES, tokens), bf16),
+            hbm((LANES, tokens), bf16),
+            hbm((tokens, LANES), bf16),
+            hbm((16, tokens), bf16),
+        ] + sums,
         scratch_shapes=[
             pltpu.VMEM((LANES, channels), f32),
             pltpu.VMEM((HALO + CHUNK, channels), f32),
@@ -354,10 +357,13 @@
             pltpu.VMEM((HALO + CHUNK, 2 * LANES), f32),
             pltpu.VMEM((2 * LANES, CHUNK), bf16),
         ],
-        compiler_params=pltpu.CompilerParams(vmem_limit_bytes=14 * MIB),
-        cost_estimate=pl.CostEstimate(flops=28 * 10**9, bytes_accessed=80 * 10**6, transcendentals=0),
+        compiler_params=pltpu.CompilerParams(vmem_limit_bytes=16 * MIB),
+        cost_estimate=pl.CostEstimate(flops=28 * 10**9, bytes_accessed=40 * 10**6, transcendentals=0),
         name="ssd_backward",
-    )(rank, x_pre, x_pre, bc_pre, bc_pre, step_pre, aux, seg_row, conv_rows, bc_rows, head_rows, expand, mixed, dy, states)
+    )(
+        rank, from_hbm(x_pre), from_hbm(x_pre), bc_pre, bc_pre, step_pre, aux, seg_row, conv_rows, bc_rows, head_rows,
+        expand, from_hbm(mixed), dy, from_hbm(states),
+    )
 
 
 def segment_facts(seg):
@@ -431,8 +437,8 @@
         in_specs=[block, pl.BlockSpec((8, depth), lambda i: (0, 0))],
         out_specs=[block, pl.BlockSpec((depth, TILE), lambda i: (0, i)), pl.BlockSpec((8, TILE), lambda i: (0, i))],
         out_shape=[
-            jax.ShapeDtypeStruct((tokens, depth), bf16),
-            jax.ShapeDtypeStruct((depth, tokens), bf16),
+            hbm((tokens, depth), bf16),
+            hbm((depth, tokens), bf16),
             jax.ShapeDtypeStruct((8, tokens), f32),
         ],
         compiler_params=params(),
@@ -468,13 +474,13 @@
         out_specs=[vmem, vmem],
         out_shape=[
             jax.ShapeDtypeStruct((rows, channels + LANES), bf16),
-            jax.ShapeDtypeStruct((rows, channels), bf16),
+            hbm((rows, channels), bf16),
         ],
         scratch_shapes=[pltpu.VMEM((LANES, 2 * LANES), f32)],
         compiler_params=params(),
         cost_estimate=cost(2),
         name="pack",
-    )(rank, in_weight, bc_weight, step_t)
+    )(rank, from_hbm(in_weight), from_hbm(bc_weight), step_t)
 
 
 def columns_kernel(rank_ref, *refs, count):
@@ -587,7 +593,7 @@
             jax.ShapeDtypeStruct((share, depth), bf16),
         ],
         compiler_params=params(),
-        cost_estimate=cost(0.1),
+        cost_estimate=cost(20),
         name="project_small",
     )(idx, lhs, *pieces)
 
@@ -612,11 +618,11 @@
         + [pl.BlockSpec((p.shape[0], channels), whole) for p in pieces],
         out_specs=[pl.BlockSpec((TILE, channels), lambda i: (i, 0)), pl.BlockSpec((depth, channels), whole)],
         out_shape=[
-            jax.ShapeDtypeStruct((tokens, channels), f32),
-            jax.ShapeDtypeStruct((depth, channels), bf16),
-        ],
-        compiler_params=params(),
-        cost_estimate=cost(20),
+            hbm((tokens, channels), f32),
+            hbm((depth, channels), bf16),
+        ],
+        compiler_params=params(),
+        cost_estimate=cost(0.1),
         name="project",
     )(idx, lhs, *pieces)
 
@@ -664,12 +670,12 @@
         out_shape=[
             jax.ShapeDtypeStruct((tokens, channels), f32),
             jax.ShapeDtypeStruct((8, tokens), f32),
-            jax.ShapeDtypeStruct((depth, channels), bf16),
+            hbm((depth, channels), bf16),
         ],
         compiler_params=params(),
         cost_estimate=cost(0.1),
         name="gate_forward",
-    )(idx, lhs, mixed, *pieces)
+    )(idx, lhs, from_hbm(mixed), *pieces)
 
 
 def gated_kernel(gate_ref, mixed_ref, square_ref, conv_ref, out_ref, *, inner_total):
@@ -777,7 +783,7 @@
         compiler_params=params(),
         cost_estimate=cost(0.1),
         name="gate_backward",
-    )(gate, gout, mixed, square, inner, conv_rows)
+    )(from_hbm(gate), from_hbm(gout), from_hbm(mixed), square, inner, conv_rows)
 
 
 def weight_grad_kernel(idx_ref, lhs_ref, rhs_ref, *refs, rows, turned):
@@ -811,7 +817,7 @@
             pl.BlockSpec(rhs.shape, whole),
         ],
         out_specs=[pl.BlockSpec((size * rows, width), whole) for size in sizes],
-        out_shape=[jax.ShapeDtypeStruct((size * rows, width), bf16) for size in sizes],
+        out_shape=[hbm((size * rows, width), bf16) for size in sizes],
         scratch_shapes=[pltpu.VMEM((depth, width), bf16)],
         compiler_params=params(),
         cost_estimate=cost(us),
@@ -843,32 +849,35 @@
             ],
             out_specs=[pl.BlockSpec((tokens, width), whole)] * ranks,
         ),
-        out_shape=[jax.ShapeDtypeStruct((tokens, width), bf16)] * ranks,
+        out_shape=[hbm((tokens, width), bf16)] * ranks,
         compiler_params=params(),
         cost_estimate=cost(0.1),
         name="out_partial",
     )(rank, gated_out, w_out)
 
 
-def term_kernel(rank_ref, gx_ref, wx_ref, gg_ref, wg_ref, gs_ref, ws_ref, gb_ref, wbt_ref, hidden_ref, inv_ref, *refs):
-    outs, dgain_ref, scratch = refs[:-2], refs[-2], refs[-1]
-    total = dot_nt(gx_ref[...], wx_ref[...]) + dot_nt(gg_ref[...], wg_ref[...])
-    total = total + dot_nt(gs_ref[...], ws_ref[...]) + dot_nn(gb_ref[...], wbt_ref[...])
-    scratch[...] = total.astype(bf16)
-    normed = hidden_ref[...].astype(f32) * row_to_column(inv_ref[0:1, :])
-    dgain_ref[...] = jnp.broadcast_to(jnp.sum(total * normed, axis=0, keepdims=True), dgain_ref.shape)
-    for r, out in enumerate(outs):
+def term_kernel(rank_ref, gx_ref, wx_ref, gg_ref, wg_ref, gs_ref, ws_ref, gb_ref, wbt_ref, hidden_ref, inv_ref, *refs, apart):
+    dgain_ref, outs = refs[-1], refs[:-1]
+    gain = None
+    for r, out in zip(apart, outs):
         rows = out.shape[0]
-        out[...] = scratch[pl.ds(pl.multiple_of((rank_ref[0] ^ r) * rows, rows), rows), :]
-
-
-def normed_term(dx, dgate, dstep, dbc, w_a, w_b, w_s, w_bct, hidden, inv_rms, rank, ranks):
+        span = pl.ds(pl.multiple_of((rank_ref[0] ^ r) * rows, rows), rows)
+        total = dot_nt(gx_ref[span, :], wx_ref[...]) + dot_nt(gg_ref[span, :], wg_ref[...])
+        total = total + dot_nt(gs_ref[span, :], ws_ref[...]) + dot_nn(gb_ref[span, :], wbt_ref[...])
+        out[...] = total.astype(bf16)
+        normed = hidden_ref[span, :].astype(f32) * row_to_column(inv_ref[0:1, span])
+        own = jnp.sum(total * normed, axis=0, keepdims=True)
+        gain = own if gain is None else gain + own
+    dgain_ref[...] = jnp.broadcast_to(gain, dgain_ref.shape)
+
+
+def normed_term(dx, dgate, dstep, dbc, w_a, w_b, w_s, w_bct, hidden, inv_rms, rank, ranks, apart):
     tokens, channels = dx.shape
     depth = w_a.shape[0]
     rows = tokens // ranks
     whole = lambda i: (0, 0)
     return pl.pallas_call(
-        term_kernel,
+        functools.partial(term_kernel, apart=apart),
         grid=(depth // TILE_D,),
         in_specs=[
             pl.BlockSpec(memory_space=pltpu.SMEM),
@@ -883,13 +892,15 @@
             pl.BlockSpec((tokens, TILE_D), lambda i: (0, i)),
             pl.BlockSpec(inv_rms.shape, whole),
         ],
-        out_specs=[pl.BlockSpec((rows, TILE_D), lambda i: (0, i))] * ranks + [pl.BlockSpec((8, TILE_D), lambda i: (0, i))],
-        out_shape=[jax.ShapeDtypeStruct((rows, depth), bf16)] * ranks + [jax.ShapeDtypeStruct((8, depth), f32)],
-        scratch_shapes=[pltpu.VMEM((tokens, TILE_D), bf16)],
+        out_specs=[pl.BlockSpec((rows, TILE_D), lambda i: (0, i))] * len(apart) + [pl.BlockSpec((8, TILE_D), lambda i: (0, i))],
+        out_shape=[jax.ShapeDtypeStruct((rows, depth), bf16)] * len(apart) + [jax.ShapeDtypeStruct((8, depth), f32)],
         compiler_params=params(32),
-        cost_estimate=cost(0.1),
+        cost_estimate=cost(20),
         name="normed_term",
-    )(rank, dx, w_a, dgate, w_b, dstep, w_s, dbc, w_bct, hidden, inv_rms)
+    )(
+        rank, dx, from_hbm(w_a), dgate, from_hbm(w_b), dstep, from_hbm(w_s), dbc,
+        from_hbm(w_bct), from_hbm(hidden), inv_rms,
+    )
 
 
 def norm_back_kernel(rank_ref, a_ref, b_ref, hidden_ref, cot_ref, gain_ref, out_ref):
@@ -924,7 +935,105 @@
         compiler_params=params(),
         cost_estimate=cost(0.1),
         name="norm_backward",
-    )(rank, a, b, hidden, cot, gain_rows)
+    )(rank, a, b, from_hbm(hidden), from_hbm(cot), gain_rows)
+
+
+def moved(weight, moment, grad):
+    fresh = 0.5 * moment + 0.5 * grad
+    return fresh, weight - LEARN_RATE * fresh - LEARN_RATE * DECAY_RATE * weight
+
+
+def add_up(refs):
+    total = refs[0][...].astype(f32)
+    for ref in refs[1:]:
+        total = total + ref[...].astype(f32)
+    return total
+
+
+def update_in_kernel(w_ref, m_ref, *refs, count):
+    gate_refs, x_refs, (m_out, w_out) = refs[:count], refs[count:2 * count], refs[2 * count:]
+    for at, parts in ((0, gate_refs), (1, x_refs)):
+        fresh, weight = moved(w_ref[:, at, :], m_ref[:, at, :], add_up(parts))
+        m_out[:, at, :] = fresh
+        w_out[:, at, :] = weight
+
+
+def update_in(weight, moment, gate_parts, x_parts):
+    rows, _, channels = weight.shape
+    size = min(rows, 48)
+    full = pl.BlockSpec((size, 2, channels), lambda i: (i, 0, 0))
+    parts = [*gate_parts, *x_parts]
+    return pl.pallas_call(
+        functools.partial(update_in_kernel, count=len(gate_parts)),
+        grid=(rows // size,),
+        in_specs=[full, full] + [pl.BlockSpec((size, channels), functools.partial(lambda at, i: (i, at), at)) for _, at in parts],
+        out_specs=[full, full],
+        out_shape=[jax.ShapeDtypeStruct(weight.shape, f32)] * 2,
+        compiler_params=params(),
+        cost_estimate=cost(0.1),
+        name="update_in",
+    )(from_hbm(weight), from_hbm(moment), *[part for part, _ in parts])
+
+
+def update_small_kernel(w_ref, m_ref, *refs, share):
+    parts, (m_out, w_out, share_out, scratch) = refs[:-4], refs[-4:]
+    heads, rows = w_ref.shape
+    total = add_up(parts)
+    share_out[...] = total
+    scratch[0:rows, :] = total
+    grad = scratch[...].T[share:share + heads, 0:rows]
+    fresh, weight = moved(w_ref[...], m_ref[...], grad)
+    m_out[...] = fresh
+    w_out[...] = weight
+
+
+def update_small(weight_t, moment_t, parts, share):
+    rows = weight_t.shape[1]
+    whole = lambda i: (0, 0)
+    spec = pl.BlockSpec(weight_t.shape, whole)
+    return pl.pallas_call(
+        functools.partial(update_small_kernel, share=share),
+        grid=(1,),
+        in_specs=[spec, spec] + [pl.BlockSpec((rows, LANES), functools.partial(lambda at, i: (0, at), at)) for _, at in parts],
+        out_specs=[spec, spec, pl.BlockSpec((rows, LANES), whole)],
+        out_shape=[jax.ShapeDtypeStruct(weight_t.shape, f32)] * 2 + [jax.ShapeDtypeStruct((rows, LANES), f32)],
+        scratch_shapes=[pltpu.VMEM((2 * LANES, LANES), f32)],
+        compiler_params=params(),
+        cost_estimate=cost(0.1),
+        name="update_small",
+    )(weight_t, moment_t, *[part for part, _ in parts])
+
+
+def update_bc_kernel(rank_ref, w_ref, m_ref, *refs):
+    pieces, (m_out, w_out) = refs[:-2], refs[-2:]
+    rows, width = w_ref.shape
+    share = width // len(pieces)
+    lane = lax.broadcasted_iota(jnp.int32, (rows, LANES), 1)
+    for pair in range(width // LANES):
+        halves = []
+        for member in (2 * pair, 2 * pair + 1):
+            own = pieces[0][...]
+            for r in range(1, len(pieces)):
+                own = jnp.where((rank_ref[0] ^ r) == member, pieces[r][...], own)
+            halves.append(own)
+        grad = jnp.where(lane < share, halves[0], pltpu.roll(halves[1], share, 1))
+        span = slice(pair * LANES, (pair + 1) * LANES)
+        fresh, weight = moved(w_ref[:, span], m_ref[:, span], grad)
+        m_out[:, span] = fresh
+        w_out[:, span] = weight
+
+
+def update_bc(weight, moment, pieces, rank):
+    vmem = pl.BlockSpec(memory_space=pltpu.VMEM)
+    return pl.pallas_call(
+        update_bc_kernel,
+        in_specs=[pl.BlockSpec(memory_space=pltpu.SMEM)] + [vmem] * (2 + len(pieces)),
+        out_specs=[vmem, vmem],
+        out_shape=[jax.ShapeDtypeStruct(weight.shape, f32)] * 2,
+        compiler_params=params(),
+        cost_estimate=cost(0.1),
+        name="update_bc",
+    )(rank, weight, moment, *pieces)
 
 
 def fence(*values):
@@ -1065,14 +1174,22 @@
     def block(v, i):
         return v[i * rows:(i + 1) * rows]
 
+    def total(own, own_got, got):
+        value = own.astype(f32) + own_got.astype(f32)
+        for part in got:
+            value = value + part.astype(f32)
+        return value
+
     def outer_all(v, some):
         return {k: outer_from(v, k) for k in some}
 
     def flip_all(z, some):
         return {k: inner_flip(z[k]) for k in some}
 
-    a_z = outer_all(set_a, ks)
+    a_z = outer_all(set_a, near_ks)
     a_x = {0: inner_flip(set_a)}
+    far_a, a_x[0] = fence(set_a, a_x[0])
+    a_z[far_k] = outer_from(far_a, far_k)
     cot_far = rank_flip(cotangent, 2)
     gain_rows = pad_rows(norm_gain[None])
     normed_low, normed_t, inv_rms = prepare(hidden, gain_rows)
@@ -1085,24 +1202,27 @@
     )
 
     a_x[far_k] = inner_flip(a_z[far_k])
+    b_x = {0: inner_flip(set_b)}
     b_z = outer_all(set_b, near_ks)
     cot, cot_t = join_columns([cotangent, rank_flip(cotangent, 1), cot_far, rank_flip(cot_far, 1)], rank1)
-    set_b, set_c, b_z, a_z, a_x, cot, cot_t, normed_low = fence(set_b, set_c, b_z, a_z, a_x, cot, cot_t, normed_low)
+    set_b, set_c, b_z, b_x, a_z, a_x, cot, cot_t, normed_low = fence(
+        set_b, set_c, b_z, b_x, a_z, a_x, cot, cot_t, normed_low
+    )
 
     b_z[far_k] = outer_from(set_b, far_k)
-    b_x = {0: inner_flip(set_b), **flip_all(b_z, near_ks[:1])}
+    b_x.update(flip_all(b_z, near_ks[:1]))
+    c_x = {0: inner_flip(set_c)}
     a_blocks = blocks(set_a, a_z, a_x)
     small, bc_share, w_s, w_bct_share = project_small(normed_low, a_blocks, idx, share)
     bc_pieces = mp_pieces(bc_share)
     x_pre, w_a = project(normed_low, a_blocks, idx, channels)
     bc_pieces, x_pre, small, set_c, w_bct_share, w_s = fence(bc_pieces, x_pre, small, set_c, w_bct_share, w_s)
     bc_pre, step_pre = join_small(bc_pieces, small, rank1)
-    set_c, b_z, b_x, x_pre, bc_pre, step_pre, w_bct_share = fence(
-        set_c, b_z, b_x, x_pre, bc_pre, step_pre, w_bct_share
+    set_c, b_z, b_x, c_x, x_pre, bc_pre, step_pre, w_bct_share = fence(
+        set_c, b_z, b_x, c_x, x_pre, bc_pre, step_pre, w_bct_share
     )
 
     c_z = outer_all(set_c, near_ks)
-    c_x = {0: inner_flip(set_c)}
     b_x.update(flip_all(b_z, ks[1:]))
     mixed, states = ssd_forward(x_pre, bc_pre, step_pre, *facts)
     mixed, states, b_x, b_z, c_z, c_x, w_bct_share, set_c = fence(mixed, states, b_x, b_z, c_z, c_x, w_bct_share, set_c)
@@ -1110,125 +1230,156 @@
     c_z[far_k] = outer_from(set_c, far_k)
     c_x.update(flip_all(c_z, near_ks))
     gate_pre, square, w_b = gate_forward(normed_low, mixed, blocks(set_b, b_z, b_x), idx)
-    mixed, gate_pre, square, w_b, w_bct_share = fence(mixed, gate_pre, square, w_b, w_bct_share)
+    square = mp_sum_direct(square)
+    mixed, gate_pre, square, w_b, w_bct_share, c_z, c_x = fence(mixed, gate_pre, square, w_b, w_bct_share, c_z, c_x)
+
+    c_x[far_k] = inner_flip(c_z[far_k])
     conv_rows = facts[2]
-    square = mp_sum_direct(square)
     gated_out = gated_norm(gate_pre, mixed, square, conv_rows, channels * ranks)
     gc_own, gc_own1, gc_here, gc_near, gc_far = weight_grad(cot_t, gated_out, idx, split_sizes)
-    square, c_z, c_x, gated_out, gc_own, gc_own1, gc_here, gc_near, gc_far, w_bct_share = fence(
-        square, c_z, c_x, gated_out, gc_own, gc_own1, gc_here, gc_near, gc_far, w_bct_share
-    )
-    c_x[far_k] = inner_flip(c_z[far_k])
-    c_x, gc_far, gc_near = fence(c_x, gc_far, gc_near)
+    c_x, square, gated_out, gc_own, gc_own1, gc_here, gc_near, gc_far, w_bct_share = fence(
+        c_x, square, gated_out, gc_own, gc_own1, gc_here, gc_near, gc_far, w_bct_share
+    )
 
     gc_far_back, gc_near_back = inner_flip(gc_far), inner_flip(gc_near)
     gout, inner_dot, w_c = grad_gout(cot, gate_pre, mixed, conv_rows, blocks(set_c, c_z, c_x), idx)
+    gout, inner_dot, w_c = fence(gout, inner_dot, w_c)
     inner_dot = mp_sum_direct(inner_dot)
-    gc_far_back, inner_dot, gout, w_c, w_bct_share = fence(gc_far_back, inner_dot, gout, w_c, w_bct_share)
+    partial = out_partial(gated_out, w_c, rank1, ranks)
+    inner_dot, gout, partial, w_bct_share, gc_far_back = fence(inner_dot, gout, partial, w_bct_share, gc_far_back)
+    out_back = rank_flip(partial[3], 1)
     w_bct = [w_bct_share] + [rank_flip(w_bct_share, r) for r in (1, 2, 3)]
     dmixed, dgate, dgain = gate_backward(gate_pre, gout, mixed, square, inner_dot, conv_rows, channels * ranks)
     gb_own, gb_own1, gb_here, gb_send = weight_grad(normed_t, dgate, idx, sizes)
-    partial = out_partial(gated_out, w_c, rank1, ranks)
-    gc_near_back, gc_far_back, w_bct, gb_own, gb_own1, gb_here, gb_send, partial, dmixed, dgain = fence(
-        gc_near_back, gc_far_back, w_bct, gb_own, gb_own1, gb_here, gb_send, partial, dmixed, dgain
-    )
-    out_far = pair_sum(partial[2], rank_flip(partial[3], 1))
-    out_near = partial[0].astype(f32) + rank_flip(partial[1], 1).astype(f32)
-    gc_blocks = [pair_sum(block(gc_here, i), block(gc_near_back, i)) for i in range(n - 2)]
-    gc_blocks.append(pair_sum(block(gc_here, n - 2), gc_far_back))
-    out_far, out_near, gc_blocks, gb_send, dmixed = fence(out_far, out_near, gc_blocks, gb_send, dmixed)
-
-    c_got = dict(zip(ks, outer_send(gc_blocks, ks)))
+    gc_near_back, gc_far_back, w_bct, out_back, gb_own, gb_own1, gb_here, gb_send, partial, dmixed, dgain = fence(
+        gc_near_back, gc_far_back, w_bct, out_back, gb_own, gb_own1, gb_here, gb_send, partial, dmixed, dgain
+    )
+    c_blocks = [pair_sum(block(gc_here, i), block(gc_near_back, i)) for i in range(n - 2)]
+    c_blocks.append(pair_sum(block(gc_here, n - 2), gc_far_back))
+    out_far = pair_sum(partial[2], out_back)
+    w_bct = join_rows(w_bct, rank1)
+    c_blocks, out_far, w_bct, dmixed, gb_send = fence(c_blocks, out_far, w_bct, dmixed, gb_send)
+
+    c_got = outer_send(c_blocks, ks)
     gb_back = inner_flip(gb_send)
     out_got = rank_flip(out_far, 2)
     dx, dbc, dbc_keep, dbc_send, dstep, dstep_t, dconv, dbct_part, dheads = ssd_backward(
         rank1, x_pre, bc_pre, step_pre, *facts, mixed, dmixed, states
     )
-    c_got, gb_back, out_got, dx, dbc, dbc_keep, dbc_send, dstep, dstep_t, dconv, dbct_part, dheads, gc_own1, gb_own1 = fence(
-        c_got, gb_back, out_got, dx, dbc, dbc_keep, dbc_send, dstep, dstep_t, dconv, dbct_part, dheads, gc_own1, gb_own1
-    )
-
-    b_blocks = [pair_sum(block(gb_here, i), block(gb_back, i)) for i in range(n - 1)]
-    b_got = outer_send(b_blocks[:-1], near_ks)
-    own_got = inner_flip(jnp.concatenate([gc_own1, gb_own1], axis=1))
+    c_got, gb_back, out_got, dx, dbc, dbc_keep, dbc_send, dstep, dstep_t, dconv, dbct_part, dheads = fence(
+        c_got, gb_back, out_got, dx, dbc, dbc_keep, dbc_send, dstep, dstep_t, dconv, dbct_part, dheads
+    )
+
+    b_got = {far_k: outer_from(pair_sum(block(gb_here, n - 2), block(gb_back, n - 2)), n - far_k)}
     dbc_back = rank_flip(dbc_send, 1)
-    *term, dgain_norm = normed_term(
-        dx, dgate, dstep, dbc, w_a, w_b, w_s, join_rows(w_bct, rank1), hidden, inv_rms, rank1, ranks
-    )
-    term, dgain_norm, b_got, own_got, far_block, dx, dbc_back = fence(
-        term, dgain_norm, b_got, own_got, b_blocks[-1], dx, dbc_back
-    )
-
-    b_got = b_got + outer_send([far_block], [far_k])
-    far = pair_sum(term[2], rank_flip(term[3], 1))
-    near = term[0].astype(f32) + rank_flip(term[1], 1).astype(f32)
+    out_near_back = rank_flip(partial[1], 1)
+    ga_own, ga_own1, ga_here, ga_near, ga_far = weight_grad(normed_t, dx, idx, split_sizes, us=20)
+    ga_own, ga_own1, ga_here, ga_near, ga_far, dx, dbc_back, gb_back, gb_here, out_near_back = fence(
+        ga_own, ga_own1, ga_here, ga_near, ga_far, dx, dbc_back, gb_back, gb_here, out_near_back
+    )
+
+    b_near = [pair_sum(block(gb_here, i), block(gb_back, i)) for i in range(n - 2)]
+    b_got.update(zip(near_ks, outer_send(b_near, near_ks)))
+    ga_far_back = inner_flip(ga_far)
     dbc_pair = pair_sum(dbc_keep, dbc_back)
     dbc_got = rank_flip(dbc_pair[share:], 2)
-    ga_own, ga_own1, ga_here, ga_near, ga_far = weight_grad(normed_t, dx, idx, split_sizes, us=20)
-    shared = jnp.concatenate([dbct_part, dgain_norm], axis=1)
-    shared = shared + rank_flip(shared, 1)
-    far, near, shared, ga_own, ga_own1, ga_here, ga_near, ga_far, dbc_pair, dbc_got = fence(
-        far, near, shared, ga_own, ga_own1, ga_here, ga_near, ga_far, dbc_pair, dbc_got
-    )
-
-    got = rank_flip(far, 2)
-    shared_got = rank_flip(shared, 2)
-    ga_far_back, ga_near_back = inner_flip(ga_far), inner_flip(ga_near)
+    operands = (dx, dgate, dstep, dbc, w_a, w_b, w_s, w_bct, hidden, inv_rms, rank1, ranks)
+    far_own, far_send, gain_far = normed_term(*operands, (2, 3))
+    far_own, far_send, gain_far, dx, dbc_got, dbc_pair, dstep_t, b_got[far_k], ga_near, ga_own1 = fence(
+        far_own, far_send, gain_far, dx, dbc_got, dbc_pair, dstep_t, b_got[far_k], ga_near, ga_own1
+    )
+    far_back = rank_flip(far_send, 1)
+    operands = (dx, *operands[1:])
+    near_own, near_send, gain_near = normed_term(*operands, (0, 1))
+    far_back, near_own, near_send, gain_near, ga_far_back, ga_near, b_got = fence(
+        far_back, near_own, near_send, gain_near, ga_far_back, ga_near, b_got
+    )
+    shared = mp_sum_direct(jnp.concatenate([dbct_part, gain_far + gain_near], axis=1))
+    near_back = rank_flip(near_send, 1)
+    far = pair_sum(far_own, far_back)
+    a_far = pair_sum(block(ga_here, n - 2), ga_far_back)
     dbc_share = pair_sum(dbc_pair[:share], dbc_got)
     dsmall_t = jnp.concatenate([dbc_share, dstep_t, jnp.zeros((LANES - share - 16, tokens), bf16)], axis=0)
     gs_own, gs_here, gs_send = weight_grad(normed_t, dsmall_t, idx_s, (1, n - 1, n), turned=True)
-    ga_far_back, b_got, a_far, gs_send, shared, shared_got = fence(
-        ga_far_back, b_got, block(ga_here, n - 2), gs_send, shared, shared_got
-    )
-    a_got = {far_k: outer_from(pair_sum(a_far, ga_far_back), n - far_k)}
+    far, a_far, shared, near_back, gs_send, ga_near = fence(far, a_far, shared, near_back, gs_send, ga_near)
+
+    got = rank_flip(far, 2)
+    a_got = {far_k: outer_from(a_far, n - far_k)}
     gs_back = inner_flip(gs_send)
-    packed = jnp.concatenate([dconv + dgain, dheads, shared + shared_got], axis=1)
+    ga_near_back = inner_flip(ga_near)
+    packed = jnp.concatenate([dconv + dgain, dheads, shared], axis=1)
     packed_got = inner_flip(packed)
-    a_blocks = [pair_sum(block(ga_here, i), block(ga_near_back, i)) for i in range(n - 2)]
-    got, near, gs_back, a_blocks, packed, packed_got, ga_own1 = fence(
-        got, near, gs_back, a_blocks, packed, packed_got, ga_own1
+    near = near_own.astype(f32) + near_back.astype(f32)
+    got, near, a_got, ga_near_back, packed, packed_got, gs_back, ga_own1, gb_own1, gc_own1 = fence(
+        got, near, a_got, ga_near_back, packed, packed_got, gs_back, ga_own1, gb_own1, gc_own1
     )
 
     mine = norm_backward(near, got, hidden, cot, gain_rows, rank1)
-    mine, a_blocks, packed, packed_got, gs_back, ga_own1 = fence(mine, a_blocks, packed, packed_got, gs_back, ga_own1)
+    mine, ga_near_back, gs_back, packed, packed_got, gc_own1, gb_own1, ga_own1 = fence(
+        mine, ga_near_back, gs_back, packed, packed_got, gc_own1, gb_own1, ga_own1
+    )
     mine_far = rank_flip(mine, 2)
-    for k, a_block in zip(near_ks, a_blocks):
-        a_got[k] = outer_from(a_block, n - k)
-    a_own_got = inner_flip(ga_own1)
-    packed = packed + packed_got
-    a_got, a_own_got, packed, gs_back = fence(a_got, a_own_got, packed, gs_back)
-    s_got = outer_send(outer_blocks(gs_own, gs_here, [gs_back[rows:]], ks), ks)
-    packed = outer_sum(packed)
-    mine_far, s_got, packed = fence(mine_far, s_got, packed)
-    input_grad = join_rows([mine, rank_flip(mine, 1), mine_far, rank_flip(mine_far, 1)], rank1)
-
-    def total(own, own_got, got):
-        value = own.astype(f32) + own_got.astype(f32)
-        for part in got:
-            value = value + part.astype(f32)
-        return value
+    own_got = inner_flip(jnp.concatenate([gc_own1, gb_own1, ga_own1], axis=1))
+    s_blocks = outer_blocks(gs_own, gs_here, [gs_back[rows:]], ks)
+    sums = packed + packed_got
+    sums = jnp.concatenate([sums[:, i:i + LANES] for i in range(0, sums.shape[1], LANES)], axis=0)
+    depth_s = -(-sums.shape[0] // 112) * 112
+    sums = pad_rows(sums, depth_s).astype(bf16)
+    wide = (channels + LANES) // LANES
+    sums_wide = jnp.concatenate([sums[i * depth_s // wide:(i + 1) * depth_s // wide] for i in range(wide)], axis=1)
+    a_blocks = [
+        jnp.concatenate(
+            [jnp.concatenate([pair_sum(block(ga_here, i), block(ga_near_back, i)), s_blocks[i]], axis=1), sums_wide], axis=0
+        )
+        for i in range(n - 2)
+    ]
+    as_got = outer_send(a_blocks, near_ks)
+    s_far_got = outer_from(jnp.concatenate([s_blocks[-1], sums], axis=0), n - far_k)
+    mine_far, as_got, s_far_got, own_got, mine, sums = fence(mine_far, as_got, s_far_got, own_got, mine, sums)
+
+    mine_near, mine_far_near = rank_flip(mine, 1), rank_flip(mine_far, 1)
+    last = channels // LANES
+    step_m, step_w, shard_s = update_small(
+        step_weight.T, step_moment.T,
+        [(gs_own, 0), (gs_back, 0), (s_far_got, 0)] + [(got, last) for got in as_got], share,
+    )
+    bc_pieces = [shard_s] + [rank_flip(shard_s, r) for r in (1, 2, 3)]
+    in_m, in_w = update_in(
+        in_weight, in_moment,
+        [(gb_own, 0), (own_got, 1)] + [(b_got[k], 0) for k in ks],
+        [(ga_own, 0), (own_got, 2), (a_got[far_k], 0)] + [(got, 0) for got in as_got],
+    )
+    input_grad = join_rows([mine, mine_near, mine_far, mine_far_near], rank1)
+    bc_m, bc_w = update_bc(bc_weight, bc_moment, bc_pieces, rank1)
+
+    def unpack(v):
+        return v.astype(f32)
+
+    found = {0: unpack(sums), far_k: unpack(s_far_got[rows:])}
+    for k, got in zip(near_ks, as_got):
+        tail = got[rows:]
+        found[n - k] = unpack(jnp.concatenate([tail[:, i:i + LANES] for i in range(0, tail.shape[1], LANES)], axis=0))
+    packed = found
+    step = n // 2
+    while step >= 1:
+        packed = {i: packed[i] + packed[i + step] for i in range(step)}
+        step //= 2
+    packed = packed[0]
+    packed = jnp.concatenate([packed[i:i + 8] for i in range(0, packed.shape[0] // 8 * 8, 8)], axis=1)
 
     resid = lax.dynamic_slice_in_dim(hidden, rank * width, width, 1).astype(f32)
-    output = (resid + out_near + out_got.astype(f32)).astype(bf16)
-    shard_c = total(gc_own, own_got[:, :channels], [c_got[k] for k in ks])
-    shard_b = total(gb_own, own_got[:, channels:], b_got)
-    shard_a = total(ga_own, a_own_got, [a_got[k] for k in ks])
-    shard_s = total(gs_own, gs_back[:rows], s_got)
+    output = (resid + partial[0].astype(f32) + out_near_back.astype(f32) + out_got.astype(f32)).astype(bf16)
+    shard_c = total(gc_own, own_got[:, :channels], c_got)
 
     cut = channels + LANES
     total_conv = packed[:6, :channels]
     total_head = packed[:3, channels:channels + heads]
     total_bct = packed[:5, cut:cut + 2 * LANES]
-    total_gain = packed[0, cut + 2 * LANES:]
-
-    shard_bc = in_rank_order(mp_pieces(shard_s[:, :share]), rank, 1)
-    shard_step = shard_s[:, share:share + heads]
-    in_m, in_w = advance(in_weight, in_moment, jnp.stack([shard_b, shard_a], axis=1))
-    bc_m, bc_w = advance(bc_weight, bc_moment, shard_bc)
-    step_m, step_w = advance(step_weight, step_moment, shard_step)
+    total_gain = packed[0, cut + 2 * LANES:cut + 2 * LANES + depth]
+
     out_m, out_w = advance(out_weight, out_moment, shard_c.T)
     return (
-        output, input_grad, in_m, in_w, bc_m, bc_w, step_m, step_w, out_m, out_w,
+        output, input_grad, in_m, in_w, bc_m, bc_w, step_m.T, step_w.T, out_m, out_w,
         momentum(conv_moment, total_conv),
         momentum(bc_table_moment, total_bct),
         momentum(head_moment, total_head),

time: 318 us -> 296 us (0.931)
  local copies, waits for them, and re-layouts: 38.7 us -> 6.89 us
  Pallas kernels: 102 us -> 133 us
  starting transfers between devices: 79.4 us -> 72.5 us
  other arithmetic: 18.8 us -> 12 us
  waiting for transfers between devices: 76.1 us -> 69.3 us
    unnamed x221 -> x174, local copies, waits for them, and re-layouts: 32.9 us -> 3.84 us
    pallas_call x1 -> x5, Pallas kernels: 10.3 us -> 20.5 us  [the longest x2 14.3 us: normed_term(): pl.pallas_call(functools.partial(term_kernel, apart=apart), grid=(depth /...]
    ppermute x21 -> x20, waiting for transfers between devices: 25.3 us -> 19.2 us  [inner_flip(): lax.ppermute(v, 'dp', [(d ^ 1, d) for d in range(lax.axis_size('dp'))])]
    pallas_call x4, Pallas kernels: 13.8 us -> 18.9 us  [weight_grad(): pl.pallas_call(functools.partial(weight_grad_kernel, rows=rows, turned=tu...]
    ppermute x2 -> x0, starting transfers between devices: 4.5 us -> none  [outer_flip(): lax.ppermute(v, 'dp', [((o ^ bit) * 2 + x, o * 2 + x) for o in range(n) f...]
    ppermute x21 -> x19, waiting for transfers between devices: 43.7 us -> 40.6 us  [outer_from(): lax.ppermute(v, 'dp', [((o + k) % n * 2 + x, o * 2 + x) for o in range(n)...]
    ppermute x31 -> x32, waiting for transfers between devices: 6.81 us -> 9.43 us  [rank_flip(): lax.ppermute(v, 'mp', [(m ^ bit, m) for m in range(lax.axis_size('mp'))])]
    ppermute x21 -> x20, starting transfers between devices: 23.9 us -> 21.8 us  [inner_flip(): lax.ppermute(v, 'dp', [(d ^ 1, d) for d in range(lax.axis_size('dp'))])]
  transfers between devices with their start and end apart: 75 -> 71, of which waited for: 19 -> 18; matrix products, arithmetic and copies ran while one was open for 10% -> 4% of each run, Pallas kernels for 28% -> 42%
where the time goes in v5:
time: 296 us; the launch traced here: 295 us
  Pallas kernels  133 us (45%)
  starting transfers between devices  72.5 us (24%)
  waiting for transfers between devices  69.3 us (23%)
  other arithmetic  12 us (4%)
  local copies, waits for them, and re-layouts  6.89 us (2%)
    ppermute x19, waiting for transfers between devices, outer_from(): lax.ppermute(v, 'dp', [((o + k) % n * 2 + x, o * 2 + x) for o in range(n)...  40.6 us
    ppermute x19, starting transfers between devices, outer_from(): lax.ppermute(v, 'dp', [((o + k) % n * 2 + x, o * 2 + x) for o in range(n)...  32 us
    pallas_call x1, Pallas kernels, ssd_backward(): pl.pallas_call(ssd_backward_kernel, grid=(count,), in_specs=[pl.BlockSpec...  28.3 us
    ppermute x20, starting transfers between devices, inner_flip(): lax.ppermute(v, 'dp', [(d ^ 1, d) for d in range(lax.axis_size('dp'))])  21.8 us
    ppermute x20, waiting for transfers between devices, inner_flip(): lax.ppermute(v, 'dp', [(d ^ 1, d) for d in range(lax.axis_size('dp'))])  19.2 us
    pallas_call x4, Pallas kernels, weight_grad(): pl.pallas_call(functools.partial(weight_grad_kernel, rows=rows, turned=tu...  18.9 us
    ppermute x32, starting transfers between devices, rank_flip(): lax.ppermute(v, 'mp', [(m ^ bit, m) for m in range(lax.axis_size('mp'))])  18.7 us
    pallas_call x2, Pallas kernels, normed_term(): pl.pallas_call(functools.partial(term_kernel, apart=apart), grid=(depth /...  14.3 us
  transfers between devices with their start and end apart: 71, of which 18 were waited for; matrix products, arithmetic and copies ran while one was open for 4% of the time, Pallas kernels for 42%

profile of v5, /device:TPU:0, one launch (start us, length us, event | category | flops | bytes accessed | tf_op | source)
XLA Modules:
  0.0 295.5 jit_solution(9971293573943549924)
XLA Ops:
  1.4 3.8 %pack.1 = (bf16[192,896]{1,0:T(8,128)(2,1)S(1)}, bf16[192,768]{1,0:T(8,128)(2,1)}) custom-call(s32[1]{0:T(128)} %bitcast.8.rank_ref, f32[192,2,768]{2,1,0:T(2,128)} %w_ref.2, f32[192,256]{1,0:T(8,128)} %w_ref.3, f32[12,192]{1,0:T(8,128)S(1)} %bitcast.41), custom_call_target="tpu_custom_call" | custom-call | flops 2000000000 | bytes 4000000 | tf_op jit(solution)/shard_map/pack/pallas_call | solution.py:471
  5.2 3.1 %collective-permute-start.3 = (bf16[192,896]{1,0:T(8,128)(2,1)S(1)}, bf16[192,896]{1,0:T(8,128)(2,1)}, u32[]{:S(2)}, u32[]{:S(2)}) collective-permute-start(bf16[192,896]{1,0:T(8,128)(2,1)S(1)} %get-tuple-element.301.refs_0_), channel_id=1, source_target_pairs={{24,0},{28,4},{0,8},{4,12},{8,16},{12,20},{16,24},{20,28},{25,1},{... | collective-permute-start | bytes 1032200 | tf_op jit(solution)/shard_map/ppermute | solution.py:1046
  8.3 1.5 collective-permute-start.1
  9.8 2.2 collective-permute-start
  12.0 1.5 collective-permute-start.6
  14.2 3.6 %prepare.1 = (bf16[1024,1536]{1,0:T(8,128)(2,1)}, bf16[1536,1024]{1,0:T(8,128)(2,1)}, f32[8,1024]{1,0:T(8,128)S(1)}) custom-call(bf16[1024,1536]{1,0:T(8,128)(2,1)S(1)} %copy-done.4, f32[8,1536]{1,0:T(8,128)S(1)} %pad.53.gain_ref), custom_call_target="tpu_custom_call" | custom-call | flops 12000000000 | bytes 24000000 | tf_op jit(solution)/shard_map/prepare/pallas_call | solution.py:434
  18.2 2.3 collective-permute-start.2
  20.5 1.5 collective-permute-start.5
  22.0 3.9 %collective-permute-done.refs_2_ = bf16[192,896]{1,0:T(8,128)(2,1)} collective-permute-done((bf16[192,896]{1,0:T(8,128)(2,1)S(1)}, bf16[192,896]{1,0:T(8,128)(2,1)}, u32[]{:S(2)}, u32[]{:S(2)}) %collective-permute-start) | collective-permute-done | bytes 344096 | tf_op jit(solution)/shard_map/ppermute | solution.py:1046
  25.8 1.2 collective-permute-start.4
  30.2 10.3 %collective-permute-done.2.refs_4_ = bf16[192,896]{1,0:T(8,128)(2,1)S(1)} collective-permute-done((bf16[192,896]{1,0:T(8,128)(2,1)S(1)}, bf16[192,896]{1,0:T(8,128)(2,1)S(1)}, u32[]{:S(2)}, u32[]{:S(2)}) %collective-permute-start.2) | collective-permute-done | bytes 344096 | tf_op jit(solution)/shard_map/ppermute | solution.py:1046
  40.7 1.6 collective-permute-start.9
  42.2 3.8 %collective-permute-start.7 = (bf16[192,768]{1,0:T(8,128)(2,1)S(1)}, bf16[192,768]{1,0:T(8,128)(2,1)S(1)}, u32[]{:S(2)}, u32[]{:S(2)}) collective-permute-start(bf16[192,768]{1,0:T(8,128)(2,1)S(1)} %copy-done.12), channel_id=1, source_target_pairs={{8,0},{12,4},{16,8},{20,12},{24,16},{28,20},{0,24},{4,28},{9,1},{1... | collective-permute-start | bytes 884744 | tf_op jit(solution)/shard_map/ppermute | solution.py:1046
  46.6 3.4 %join_columns.1 = (bf16[1024,1536]{1,0:T(8,128)(2,1)S(1)}, bf16[1536,1024]{1,0:T(8,128)(2,1)S(1)}) custom-call(s32[1]{0:T(128)} %bitcast.8.rank_ref, bf16[1024,384]{1,0:T(8,128)(2,1)} %refs_0_.1, bf16[1024,384]{1,0:T(8,128)(2,1)} %collective-permute-done.11.refs_1_, bf16[1024,384]{1,0:T(8,128)(2,1)} %collective-permute-done.6.refs_2_, ...), custom_call_target="tpu_custom_call" | custom-call | flops 12000000000 | bytes 24000000 | tf_op jit(solution)/shard_map/join_columns/pallas_call | solution.py:499
  50.6 3.4 %collective-permute-done.8.refs_3_ = bf16[192,768]{1,0:T(8,128)(2,1)S(1)} collective-permute-done((bf16[192,768]{1,0:T(8,128)(2,1)S(1)}, bf16[192,768]{1,0:T(8,128)(2,1)S(1)}, u32[]{:S(2)}, u32[]{:S(2)}) %collective-permute-start.8) | collective-permute-done | bytes 294944 | tf_op jit(solution)/shard_map/ppermute | solution.py:1046
  53.9 5.5 %collective-permute-done.7.refs_2_ = bf16[192,768]{1,0:T(8,128)(2,1)S(1)} collective-permute-done((bf16[192,768]{1,0:T(8,128)(2,1)S(1)}, bf16[192,768]{1,0:T(8,128)(2,1)S(1)}, u32[]{:S(2)}, u32[]{:S(2)}) %collective-permute-start.7) | collective-permute-done | bytes 294944 | tf_op jit(solution)/shard_map/ppermute | solution.py:1046
  60.0 1.5 collective-permute-start.17
  61.4 2.8 collective-permute-start.16
  64.2 3.7 %project_small.1 = (f32[128,1024]{1,0:T(8,128)S(1)}, bf16[64,1024]{1,0:T(8,128)(2,1)S(1)}, bf16[1536,128]{1,0:T(8,128)(2,1)S(1)}, bf16[64,1536]{1,0:T(8,128)(2,1)}) custom-call(s32[8]{0:T(128)S(1)} %stack.88.idx_ref, bf16[1024,1536]{1,0:T(8,128)(2,1)S(1)} %copy-done.2, bf16[192,896]{1,0:T(8,128)(2,1)S(1)} %get-tuple-element.301.refs_0_, ...), custom_call_target="tpu_custom_call" | custom-call | flops 20000000000 | bytes 40000000 | tf_op jit(solution)/shard_map/project_small/pallas_call | solution.py:578
  67.9 1.5 collective-permute-start.14
  69.4 3.4 %collective-permute-done.14.refs_2_ = bf16[64,1024]{1,0:T(8,128)(2,1)S(1)} collective-permute-done((bf16[64,1024]{1,0:T(8,128)(2,1)S(1)}, bf16[64,1024]{1,0:T(8,128)(2,1)S(1)}, u32[]{:S(2)}, u32[]{:S(2)}) %collective-permute-start.14) | collective-permute-done | bytes 131104 | tf_op jit(solution)/shard_map/ppermute | solution.py:1059
  72.9 5.7 %project.1 = (f32[1024,768]{1,0:T(8,128)}, bf16[1536,768]{1,0:T(8,128)(2,1)}) custom-call(s32[8]{0:T(128)S(1)} %stack.88.idx_ref, bf16[1024,1536]{1,0:T(8,128)(2,1)S(1)} %copy-done.2, bf16[192,896]{1,0:T(8,128)(2,1)S(1)} %get-tuple-element.301.refs_0_, bf16[192,896]{1,0:T(8,128)(2,1)} %collective-permute-done.1.refs_1_, ...), custom_call_target="tpu_custom_call" | custom-call | flops 100000000 | bytes 200000 | tf_op jit(solution)/shard_map/project/pallas_call | solution.py:614
  78.6 1.3 join_small.1
  80.3 3.5 %collective-permute-start.21 = (bf16[192,768]{1,0:T(8,128)(2,1)}, bf16[192,768]{1,0:T(8,128)(2,1)S(1)}, u32[]{:S(2)}, u32[]{:S(2)}) collective-permute-start(bf16[192,768]{1,0:T(8,128)(2,1)} %convert_bitcast_fusion.refs_0_), channel_id=1, source_target_pairs={{8,0},{12,4},{16,8},{20,12},{24,16},{28,20},{0,24},{4,28},{9,1},{1... | collective-permute-start | bytes 884744 | tf_op jit(solution)/shard_map/ppermute | solution.py:1046
  83.8 1.3 collective-permute-start.19
  85.9 13.1 %ssd_forward.1 = (f32[1024,768]{1,0:T(8,128)}, bf16[8,128,768]{2,1,0:T(8,128)(2,1)}) custom-call(f32[1024,768]{1,0:T(8,128)} %get-tuple-element.329.x_ref.xb_ref, f32[1024,768]{1,0:T(8,128)} %get-tuple-element.329.x_ref.xb_ref, f32[1024,256]{1,0:T(8,128)S(1)} %get-tuple-element.330.bc_ref.bcb_ref, f32[1024,256]{1,0:T(8,128)S(1)} %get-tuple-element.330.bc_ref.bcb_ref, ...), custom_call_target="tpu_custom_call" | custom-call | flops 14000000000 | bytes 40000000 | tf_op jit(solution)/shard_map/ssd_forward/pallas_call | solution.py:292
  99.0 1.4 collective-permute-start.27
  101.1 6.9 %gate_forward.1 = (f32[1024,768]{1,0:T(8,128)S(1)}, f32[8,1024]{1,0:T(8,128)S(1)}, bf16[1536,768]{1,0:T(8,128)(2,1)}) custom-call(s32[8]{0:T(128)S(1)} %stack.88.idx_ref, bf16[1024,1536]{1,0:T(8,128)(2,1)S(1)} %copy-done.2, f32[1024,768]{1,0:T(8,128)} %get-tuple-element.370.mixed_ref, bf16[192,768]{1,0:T(8,128)(2,1)S(1)} %copy-done.13, ...), custom_call_target="tpu_custom_call" | custom-call | flops 100000000 | bytes 200000 | tf_op jit(solution)/shard_map/gate_forward/pallas_call | solution.py:656
  108.1 1.6 collective-permute-start.24
  109.6 2.1 collective-permute-done.25
  115.0 1.5 gated_norm.1.rhs_ref.lhs_ref
  116.5 5.4 %weight_grad.4 = (bf16[192,768]{1,0:T(8,128)(2,1)}, bf16[192,768]{1,0:T(8,128)(2,1)}, bf16[576,768]{1,0:T(8,128)(2,1)}, bf16[384,768]{1,0:T(8,128)(2,1)}, bf16[192,768]{1,0:T(8,128)(2,1)}) custom-call(s32[8]{0:T(128)S(1)} %stack.88.idx_ref, bf16[1536,1024]{1,0:T(8,128)(2,1)S(1)} %get-tuple-element.371.lhs_ref, bf16[1024,768]{1,0:T(8,128)(2,1)S(1)} %gated_norm.1.rhs_ref.lhs_ref), custom_call_target="tpu_custom_call" | custom-call | flops 100000000 | bytes 200000 | tf_op jit(solution)/shard_map/weight_grad/pallas_call | solution.py:811
  123.7 5.0 %grad_gout.1 = (f32[1024,768]{1,0:T(8,128)S(1)}, f32[8,1024]{1,0:T(8,128)S(1)}, bf16[1536,768]{1,0:T(8,128)(2,1)S(1)}) custom-call(s32[8]{0:T(128)S(1)} %stack.88.idx_ref, bf16[1024,1536]{1,0:T(8,128)(2,1)S(1)} %get-tuple-element.379.cot_ref, f32[1024,768]{1,0:T(8,128)S(1)} %get-tuple-element.369.gate_ref, f32[1024,768]{1,0:T(8,128)S(1)} %copy-done, ...), custom_call_target="tpu_custom_call" | custom-call | flops 20000000000 | bytes 40000000 | tf_op jit(solution)/shard_map/grad_gout/pallas_call | solution.py:722
  128.7 1.6 collective-permute-start.32
  130.6 6.1 %out_partial.1 = (bf16[1024,384]{1,0:T(8,128)(2,1)}, bf16[1024,384]{1,0:T(8,128)(2,1)}, bf16[1024,384]{1,0:T(8,128)(2,1)}, bf16[1024,384]{1,0:T(8,128)(2,1)}) custom-call(s32[1]{0:T(128)} %bitcast.8.rank_ref, bf16[1024,768]{1,0:T(8,128)(2,1)S(1)} %gated_norm.1.rhs_ref.lhs_ref, bf16[1536,768]{1,0:T(8,128)(2,1)S(1)} %get-tuple-element.389.w_ref), custom_call_target="tpu_custom_call" | custom-call | flops 100000000 | bytes 200000 | tf_op jit(solution)/shard_map/out_partial/pallas_call | solution.py:841
  137.0 1.3 collective-permute-start.30
  140.4 6.1 %gate_backward.1 = (bf16[1024,768]{1,0:T(8,128)(2,1)S(1)}, bf16[1024,768]{1,0:T(8,128)(2,1)S(1)}, f32[8,768]{1,0:T(8,128)S(1)}) custom-call(f32[1024,768]{1,0:T(8,128)} %copy-done.3, f32[1024,768]{1,0:T(8,128)} %copy-done.6, f32[1024,768]{1,0:T(8,128)} %get-tuple-element.370.mixed_ref, f32[8,1024]{1,0:T(8,128)S(1)} %add_add_fusion.3.square_ref, ...), custom_call_target="tpu_custom_call" | custom-call | flops 100000000 | bytes 200000 | tf_op jit(solution)/shard_map/gate_backward/pallas_call | solution.py:773
  146.5 5.4 %weight_grad.5 = (bf16[192,768]{1,0:T(8,128)(2,1)}, bf16[192,768]{1,0:T(8,128)(2,1)}, bf16[576,768]{1,0:T(8,128)(2,1)}, bf16[576,768]{1,0:T(8,128)(2,1)}) custom-call(s32[8]{0:T(128)S(1)} %stack.88.idx_ref, bf16[1536,1024]{1,0:T(8,128)(2,1)S(1)} %copy-done.1, bf16[1024,768]{1,0:T(8,128)(2,1)S(1)} %get-tuple-element.403.rhs_ref.gg_ref), custom_call_target="tpu_custom_call" | custom-call | flops 100000000 | bytes 200000 | tf_op jit(solution)/shard_map/weight_grad/pallas_call | solution.py:811
  152.8 1.3 add_convert_fusion.2
  154.2 1.4 add_convert_fusion.10
  158.2 3.2 %collective-permute-start.40 = (bf16[192,768]{1,0:T(8,128)(2,1)S(1)}, bf16[192,768]{1,0:T(8,128)(2,1)S(1)}, u32[]{:S(2)}, u32[]{:S(2)}) collective-permute-start(bf16[192,768]{1,0:T(8,128)(2,1)S(1)} %get-tuple-element.426), channel_id=1, source_target_pairs={{8,0},{12,4},{16,8},{20,12},{24,16},{28,20},{0,24},{4,28},{9,1},{1... | collective-permute-start | bytes 884744 | tf_op jit(solution)/shard_map/ppermute | solution.py:1046
  162.4 1.2 collective-permute-start.43
  164.4 28.3 %ssd_backward.1 = (bf16[1024,768]{1,0:T(8,128)(2,1)}, bf16[1024,256]{1,0:T(8,128)(2,1)}, bf16[128,1024]{1,0:T(8,128)(2,1)}, bf16[128,1024]{1,0:T(8,128)(2,1)}, b...) custom-call(s32[1]{0:T(128)} %bitcast.8.rank_ref, ...), custom_call_target="tpu_custom_call" | custom-call | flops 28000000000 | bytes 40000000 | tf_op jit(solution)/shard_map/ssd_backward/pallas_call | solution.py:328
  193.4 3.0 %collective-permute-start.47 = (bf16[192,768]{1,0:T(8,128)(2,1)S(1)}, bf16[192,768]{1,0:T(8,128)(2,1)S(1)}, u32[]{:S(2)}, u32[]{:S(2)}) collective-permute-start(bf16[192,768]{1,0:T(8,128)(2,1)S(1)} %add_convert_fusion.8), channel_id=1, source_target_pairs={{16,0},{20,4},{24,8},{28,12},{0,16},{4,20},{8,24},{12,28},{17,1},{... | collective-permute-start | bytes 884744 | tf_op jit(solution)/shard_map/ppermute | solution.py:1046
  196.4 1.4 copy-done.28
  197.8 5.3 %weight_grad.6 = (bf16[192,768]{1,0:T(8,128)(2,1)}, bf16[192,768]{1,0:T(8,128)(2,1)}, bf16[576,768]{1,0:T(8,128)(2,1)}, bf16[384,768]{1,0:T(8,128)(2,1)}, bf16[192,768]{1,0:T(8,128)(2,1)}) custom-call(s32[8]{0:T(128)S(1)} %stack.88.idx_ref, bf16[1536,1024]{1,0:T(8,128)(2,1)S(1)} %copy-done.1, bf16[1024,768]{1,0:T(8,128)(2,1)S(1)} %copy-done.28), custom_call_target="tpu_custom_call" | custom-call | flops 20000000000 | bytes 40000000 | tf_op jit(solution)/shard_map/weight_grad/pallas_call | solution.py:811
  205.1 1.7 collective-permute-start.50
  206.7 7.2 %normed_term.2 = (bf16[256,1536]{1,0:T(8,128)(2,1)S(1)}, bf16[256,1536]{1,0:T(8,128)(2,1)S(1)}, f32[8,1536]{1,0:T(8,128)S(1)}) custom-call(s32[1]{0:T(128)} %bitcast.8.rank_ref, bf16[1024,768]{1,0:T(8,128)(2,1)S(1)} %copy-done.28, bf16[1536,768]{1,0:T(8,128)(2,1)} %get-tuple-element.454.wx_ref, bf16[1024,768]{1,0:T(8,128)(2,1)S(1)} %get-tuple-element.403.rhs_ref.gg_ref, ...), custom_call_target="tpu_custom_call" | custom-call | flops 20000000000 | bytes 40000000 | tf_op jit(solution)/shard_map/normed_term/pallas_call | solution.py:879
  214.0 7.2 %normed_term.3 = (bf16[256,1536]{1,0:T(8,128)(2,1)S(1)}, bf16[256,1536]{1,0:T(8,128)(2,1)S(1)}, f32[8,1536]{1,0:T(8,128)S(1)}) custom-call(s32[1]{0:T(128)} %bitcast.8.rank_ref, bf16[1024,768]{1,0:T(8,128)(2,1)S(1)} %copy-done.28, bf16[1536,768]{1,0:T(8,128)(2,1)} %get-tuple-element.454.wx_ref, bf16[1024,768]{1,0:T(8,128)(2,1)S(1)} %get-tuple-element.403.rhs_ref.gg_ref, ...), custom_call_target="tpu_custom_call" | custom-call | flops 20000000000 | bytes 40000000 | tf_op jit(solution)/shard_map/normed_term/pallas_call | solution.py:879
  221.3 2.9 weight_grad.7
  224.3 1.6 collective-permute-start.53
  227.0 1.7 collective-permute-done.53
  229.8 1.4 collective-permute-start.58
  233.2 1.3 collective-permute-start.60
  234.8 13.2 %collective-permute-done.59 = f32[8,2688]{1,0:T(8,128)S(1)} collective-permute-done((f32[8,2688]{1,0:T(8,128)S(1)}, f32[8,2688]{1,0:T(8,128)S(1)}, u32[]{:S(2)}, u32[]{:S(2)}) %collective-permute-start.59) | collective-permute-done | bytes 86048 | tf_op jit(solution)/shard_map/ppermute | solution.py:1055
  247.9 3.4 %collective-permute-done.60.refs_1_ = bf16[768,128]{1,0:T(8,128)(2,1)S(1)} collective-permute-done((bf16[768,128]{1,0:T(8,128)(2,1)S(1)}, bf16[768,128]{1,0:T(8,128)(2,1)S(1)}, u32[]{:S(2)}, u32[]{:S(2)}) %collective-permute-start.60) | collective-permute-done | bytes 196640 | tf_op jit(solution)/shard_map/ppermute | solution.py:1055
  251.3 2.2 norm_backward.1.refs_0_
  254.0 1.4 collective-permute-start.61
  255.4 1.4 collective-permute-start.65
  257.1 3.1 %collective-permute-start.63 = (bf16[224,896]{1,0:T(8,128)(2,1)S(1)}, bf16[224,896]{1,0:T(8,128)(2,1)S(1)}, u32[]{:S(2)}, u32[]{:S(2)}) collective-permute-start(bf16[224,896]{1,0:T(8,128)(2,1)S(1)} %get-tuple-element.574), channel_id=1, source_target_pairs={{8,0},{12,4},{16,8},{20,12},{24,16},{28,20},{0,24},{4,28},{9,1},{1... | collective-permute-start | bytes 1204232 | tf_op jit(solution)/shard_map/ppermute | solution.py:1046
  261.2 2.4 add_convert_fusion.1
  263.6 16.5 %collective-permute-done.64.refs_2_ = bf16[416,128]{1,0:T(8,128)(2,1)S(1)} collective-permute-done((bf16[416,128]{1,0:T(8,128)(2,1)S(1)}, bf16[416,128]{1,0:T(8,128)(2,1)S(1)}, u32[]{:S(2)}, u32[]{:S(2)}) %collective-permute-start.64) | collective-permute-done | bytes 106528 | tf_op jit(solution)/shard_map/ppermute | solution.py:1046
  288.1 4.6 %update_in.1 = (f32[192,2,768]{2,1,0:T(2,128)}, f32[192,2,768]{2,1,0:T(2,128)}) custom-call(f32[192,2,768]{2,1,0:T(2,128)} %w_ref.2, f32[192,2,768]{2,1,0:T(2,128)} %m_ref.2, bf16[192,768]{1,0:T(8,128)(2,1)S(1)} %copy-done.10, bf16[192,2304]{1,0:T(8,128)(2,1)S(1)} %collective-permute-done.65.refs_1_.refs_6_, ...), custom_call_target="tpu_custom_call" | custom-call | flops 100000000 | bytes 200000 | tf_op jit(solution)/shard_map/update_in/pallas_call | solution.py:966
  293.6 1.9 join_rows.3
  (346 shorter events, 38.8 us)
Async XLA Ops:
  5.2 15.3 %collective-permute-start.3 = (bf16[192,896]{1,0:T(8,128)(2,1)S(1)}, bf16[192,896]{1,0:T(8,128)(2,1)}, u32[]{:S(2)}, u32[]{:S(2)}) collective-permute-start(bf16[192,896]{1,0:T(8,128)(2,1)S(1)} %get-tuple-element.301.refs_0_), channel_id=1, source_target_pairs={{24,0},{28,4},{0,8},{4,12},{8,16},{12,20},{16,24},{20,28},{25,1},{... | collective-permute-start | bytes 1032200 | tf_op jit(solution)/shard_map/ppermute | solution.py:1046
  8.3 9.9 %collective-permute-start.1 = (bf16[192,896]{1,0:T(8,128)(2,1)S(1)}, bf16[192,896]{1,0:T(8,128)(2,1)}, u32[]{:S(2)}, u32[]{:S(2)}) collective-permute-start(bf16[192,896]{1,0:T(8,128)(2,1)S(1)} %get-tuple-element.301.refs_0_), channel_id=1, source_target_pairs={{4,0},{0,4},{12,8},{8,12},{20,16},{16,20},{28,24},{24,28},{5,1},{1... | collective-permute-start | bytes 1032200 | tf_op jit(solution)/shard_map/ppermute | solution.py:1055
  9.8 16.1 %collective-permute-start = (bf16[192,896]{1,0:T(8,128)(2,1)S(1)}, bf16[192,896]{1,0:T(8,128)(2,1)}, u32[]{:S(2)}, u32[]{:S(2)}) collective-permute-start(bf16[192,896]{1,0:T(8,128)(2,1)S(1)} %get-tuple-element.301.refs_0_), channel_id=1, source_target_pairs={{8,0},{12,4},{16,8},{20,12},{24,16},{28,20},{0,24},{4,28},{9,1},{1... | collective-permute-start | bytes 1032200 | tf_op jit(solution)/shard_map/ppermute | solution.py:1046
  12.0 28.5 %collective-permute-start.6 = (bf16[1024,384]{1,0:T(8,128)(2,1)}, bf16[1024,384]{1,0:T(8,128)(2,1)}, u32[]{:S(2)}, u32[]{:S(2)}) collective-permute-start(bf16[1024,384]{1,0:T(8,128)(2,1)} %refs_0_.1), channel_id=1, source_target_pairs={{2,0},{3,1},{0,2},{1,3},{6,4},{7,5},{4,6},{5,7},{10,8},{11,9},{8,1... | collective-permute-start | bytes 2359304 | tf_op jit(solution)/shard_map/ppermute | solution.py:1059
  13.5 32.5 %collective-permute-start.11 = (bf16[1024,384]{1,0:T(8,128)(2,1)}, bf16[1024,384]{1,0:T(8,128)(2,1)}, u32[]{:S(2)}, u32[]{:S(2)}) collective-permute-start(bf16[1024,384]{1,0:T(8,128)(2,1)} %refs_0_.1), channel_id=1, source_target_pairs={{1,0},{0,1},{3,2},{2,3},{5,4},{4,5},{7,6},{6,7},{9,8},{8,9},{11,10... | collective-permute-start | bytes 2359304 | tf_op jit(solution)/shard_map/ppermute | solution.py:1059
  18.2 22.3 %collective-permute-start.2 = (bf16[192,896]{1,0:T(8,128)(2,1)S(1)}, bf16[192,896]{1,0:T(8,128)(2,1)S(1)}, u32[]{:S(2)}, u32[]{:S(2)}) collective-permute-start(bf16[192,896]{1,0:T(8,128)(2,1)S(1)} %get-tuple-element.301.refs_0_), channel_id=1, source_target_pairs={{16,0},{20,4},{24,8},{28,12},{0,16},{4,20},{8,24},{12,28},{17,1},{... | collective-permute-start | bytes 1032200 | tf_op jit(solution)/shard_map/ppermute | solution.py:1046
  20.5 9.7 %collective-permute-start.5 = (bf16[192,896]{1,0:T(8,128)(2,1)}, bf16[192,896]{1,0:T(8,128)(2,1)S(1)}, u32[]{:S(2)}, u32[]{:S(2)}) collective-permute-start(bf16[192,896]{1,0:T(8,128)(2,1)} %collective-permute-done.3.refs_3_), channel_id=1, source_target_pairs={{4,0},{0,4},{12,8},{8,12},{20,16},{16,20},{28,24},{24,28},{5,1},{1... | collective-permute-start | bytes 1032200 | tf_op jit(solution)/shard_map/ppermute | solution.py:1055
  25.8 14.6 %collective-permute-start.4 = (bf16[192,896]{1,0:T(8,128)(2,1)}, bf16[192,896]{1,0:T(8,128)(2,1)S(1)}, u32[]{:S(2)}, u32[]{:S(2)}) collective-permute-start(bf16[192,896]{1,0:T(8,128)(2,1)} %collective-permute-done.refs_2_), channel_id=1, source_target_pairs={{4,0},{0,4},{12,8},{8,12},{20,16},{16,20},{28,24},{24,28},{5,1},{1... | collective-permute-start | bytes 1032200 | tf_op jit(solution)/shard_map/ppermute | solution.py:1055
  40.5 6.1 %collective-permute-start.12 = (bf16[1024,384]{1,0:T(8,128)(2,1)}, bf16[1024,384]{1,0:T(8,128)(2,1)S(1)}, u32[]{:S(2)}, u32[]{:S(2)}) collective-permute-start(bf16[1024,384]{1,0:T(8,128)(2,1)} %collective-permute-done.6.refs_2_), channel_id=1, source_target_pairs={{1,0},{0,1},{3,2},{2,3},{5,4},{4,5},{7,6},{6,7},{9,8},{8,9},{11,10... | collective-permute-start | bytes 2359304 | tf_op jit(solution)/shard_map/ppermute | solution.py:1059
  40.7 9.9 %collective-permute-start.9 = (bf16[192,768]{1,0:T(8,128)(2,1)S(1)}, bf16[192,768]{1,0:T(8,128)(2,1)S(1)}, u32[]{:S(2)}, u32[]{:S(2)}) collective-permute-start(bf16[192,768]{1,0:T(8,128)(2,1)S(1)} %copy-done.12), channel_id=1, source_target_pairs={{4,0},{0,4},{12,8},{8,12},{20,16},{16,20},{28,24},{24,28},{5,1},{1... | collective-permute-start | bytes 884744 | tf_op jit(solution)/shard_map/ppermute | solution.py:1055
  42.2 11.7 %collective-permute-start.8 = (bf16[192,768]{1,0:T(8,128)(2,1)S(1)}, bf16[192,768]{1,0:T(8,128)(2,1)S(1)}, u32[]{:S(2)}, u32[]{:S(2)}) collective-permute-start(bf16[192,768]{1,0:T(8,128)(2,1)S(1)} %copy-done.12), channel_id=1, source_target_pairs={{24,0},{28,4},{0,8},{4,12},{8,16},{12,20},{16,24},{20,28},{25,1},{... | collective-permute-start | bytes 884744 | tf_op jit(solution)/shard_map/ppermute | solution.py:1046
  42.2 17.2 %collective-permute-start.7 = (bf16[192,768]{1,0:T(8,128)(2,1)S(1)}, bf16[192,768]{1,0:T(8,128)(2,1)S(1)}, u32[]{:S(2)}, u32[]{:S(2)}) collective-permute-start(bf16[192,768]{1,0:T(8,128)(2,1)S(1)} %copy-done.12), channel_id=1, source_target_pairs={{8,0},{12,4},{16,8},{20,12},{24,16},{28,20},{0,24},{4,28},{9,1},{1... | collective-permute-start | bytes 884744 | tf_op jit(solution)/shard_map/ppermute | solution.py:1046
  46.1 13.4 %collective-permute-start.10 = (bf16[192,896]{1,0:T(8,128)(2,1)S(1)}, bf16[192,896]{1,0:T(8,128)(2,1)S(1)}, u32[]{:S(2)}, u32[]{:S(2)}) collective-permute-start(bf16[192,896]{1,0:T(8,128)(2,1)S(1)} %collective-permute-done.2.refs_4_), channel_id=1, source_target_pairs={{4,0},{0,4},{12,8},{8,12},{20,16},{16,20},{28,24},{24,28},{5,1},{1... | collective-permute-start | bytes 1032200 | tf_op jit(solution)/shard_map/ppermute | solution.py:1055
  59.4 20.5 %collective-permute-start.18 = (bf16[192,768]{1,0:T(8,128)(2,1)}, bf16[192,768]{1,0:T(8,128)(2,1)S(1)}, u32[]{:S(2)}, u32[]{:S(2)}) collective-permute-start(bf16[192,768]{1,0:T(8,128)(2,1)} %convert_bitcast_fusion.refs_0_), channel_id=1, source_target_pairs={{4,0},{0,4},{12,8},{8,12},{20,16},{16,20},{28,24},{24,28},{5,1},{1... | collective-permute-start | bytes 884744 | tf_op jit(solution)/shard_map/ppermute | solution.py:1055
  60.0 20.0 %collective-permute-start.17 = (bf16[192,768]{1,0:T(8,128)(2,1)S(1)}, bf16[192,768]{1,0:T(8,128)(2,1)S(1)}, u32[]{:S(2)}, u32[]{:S(2)}) collective-permute-start(bf16[192,768]{1,0:T(8,128)(2,1)S(1)} %collective-permute-done.7.refs_2_), channel_id=1, source_target_pairs={{4,0},{0,4},{12,8},{8,12},{20,16},{16,20},{28,24},{24,28},{5,1},{1... | collective-permute-start | bytes 884744 | tf_op jit(solution)/shard_map/ppermute | solution.py:1055
  61.4 18.5 %collective-permute-start.16 = (bf16[192,768]{1,0:T(8,128)(2,1)S(1)}, bf16[192,768]{1,0:T(8,128)(2,1)S(1)}, u32[]{:S(2)}, u32[]{:S(2)}) collective-permute-start(bf16[192,768]{1,0:T(8,128)(2,1)S(1)} %copy-done.12), channel_id=1, source_target_pairs={{16,0},{20,4},{24,8},{28,12},{0,16},{4,20},{8,24},{12,28},{17,1},{... | collective-permute-start | bytes 884744 | tf_op jit(solution)/shard_map/ppermute | solution.py:1046
  67.9 5.0 %collective-permute-start.14 = (bf16[64,1024]{1,0:T(8,128)(2,1)S(1)}, bf16[64,1024]{1,0:T(8,128)(2,1)S(1)}, u32[]{:S(2)}, u32[]{:S(2)}) collective-permute-start(bf16[64,1024]{1,0:T(8,128)(2,1)S(1)} %get-tuple-element.321.refs_0_), channel_id=1, source_target_pairs={{2,0},{3,1},{0,2},{1,3},{6,4},{7,5},{4,6},{5,7},{10,8},{11,9},{8,1... | collective-permute-start | bytes 393224 | tf_op jit(solution)/shard_map/ppermute | solution.py:1059
  69.4 9.1 %collective-permute-start.13 = (bf16[64,1024]{1,0:T(8,128)(2,1)S(1)}, bf16[64,1024]{1,0:T(8,128)(2,1)S(1)}, u32[]{:S(2)}, u32[]{:S(2)}) collective-permute-start(bf16[64,1024]{1,0:T(8,128)(2,1)S(1)} %get-tuple-element.321.refs_0_), channel_id=1, source_target_pairs={{1,0},{0,1},{3,2},{2,3},{5,4},{4,5},{7,6},{6,7},{9,8},{8,9},{11,10... | collective-permute-start | bytes 393224 | tf_op jit(solution)/shard_map/ppermute | solution.py:1059
  72.9 5.7 %collective-permute-start.15 = (bf16[64,1024]{1,0:T(8,128)(2,1)S(1)}, bf16[64,1024]{1,0:T(8,128)(2,1)S(1)}, u32[]{:S(2)}, u32[]{:S(2)}) collective-permute-start(bf16[64,1024]{1,0:T(8,128)(2,1)S(1)} %collective-permute-done.14.refs_2_), channel_id=1, source_target_pairs={{1,0},{0,1},{3,2},{2,3},{5,4},{4,5},{7,6},{6,7},{9,8},{8,9},{11,10... | collective-permute-start | bytes 393224 | tf_op jit(solution)/shard_map/ppermute | solution.py:1059
  80.0 19.1 %collective-permute-start.22 = (bf16[192,768]{1,0:T(8,128)(2,1)}, bf16[192,768]{1,0:T(8,128)(2,1)S(1)}, u32[]{:S(2)}, u32[]{:S(2)}) collective-permute-start(bf16[192,768]{1,0:T(8,128)(2,1)} %convert_bitcast_fusion.refs_0_), channel_id=1, source_target_pairs={{24,0},{28,4},{0,8},{4,12},{8,16},{12,20},{16,24},{20,28},{25,1},{... | collective-permute-start | bytes 884744 | tf_op jit(solution)/shard_map/ppermute | solution.py:1046
  80.3 18.7 %collective-permute-start.21 = (bf16[192,768]{1,0:T(8,128)(2,1)}, bf16[192,768]{1,0:T(8,128)(2,1)S(1)}, u32[]{:S(2)}, u32[]{:S(2)}) collective-permute-start(bf16[192,768]{1,0:T(8,128)(2,1)} %convert_bitcast_fusion.refs_0_), channel_id=1, source_target_pairs={{8,0},{12,4},{16,8},{20,12},{24,16},{28,20},{0,24},{4,28},{9,1},{1... | collective-permute-start | bytes 884744 | tf_op jit(solution)/shard_map/ppermute | solution.py:1046
  83.8 15.1 %collective-permute-start.19 = (bf16[192,768]{1,0:T(8,128)(2,1)S(1)}, bf16[192,768]{1,0:T(8,128)(2,1)S(1)}, u32[]{:S(2)}, u32[]{:S(2)}) collective-permute-start(bf16[192,768]{1,0:T(8,128)(2,1)S(1)} %collective-permute-done.16.refs_4_), channel_id=1, source_target_pairs={{4,0},{0,4},{12,8},{8,12},{20,16},{16,20},{28,24},{24,28},{5,1},{1... | collective-permute-start | bytes 884744 | tf_op jit(solution)/shard_map/ppermute | solution.py:1055
  85.2 13.8 %collective-permute-start.20 = (bf16[192,768]{1,0:T(8,128)(2,1)S(1)}, bf16[192,768]{1,0:T(8,128)(2,1)S(1)}, u32[]{:S(2)}, u32[]{:S(2)}) collective-permute-start(bf16[192,768]{1,0:T(8,128)(2,1)S(1)} %collective-permute-done.8.refs_3_), channel_id=1, source_target_pairs={{4,0},{0,4},{12,8},{8,12},{20,16},{16,20},{28,24},{24,28},{5,1},{1... | collective-permute-start | bytes 884744 | tf_op jit(solution)/shard_map/ppermute | solution.py:1055
  99.0 13.9 %collective-permute-start.27 = (bf16[192,768]{1,0:T(8,128)(2,1)S(1)}, bf16[192,768]{1,0:T(8,128)(2,1)S(1)}, u32[]{:S(2)}, u32[]{:S(2)}) collective-permute-start(bf16[192,768]{1,0:T(8,128)(2,1)S(1)} %collective-permute-done.21.refs_2_), channel_id=1, source_target_pairs={{4,0},{0,4},{12,8},{8,12},{20,16},{16,20},{28,24},{24,28},{5,1},{1... | collective-permute-start | bytes 884744 | tf_op jit(solution)/shard_map/ppermute | solution.py:1055
  100.4 13.6 %collective-permute-start.26 = (bf16[192,768]{1,0:T(8,128)(2,1)}, bf16[192,768]{1,0:T(8,128)(2,1)S(1)}, u32[]{:S(2)}, u32[]{:S(2)}) collective-permute-start(bf16[192,768]{1,0:T(8,128)(2,1)} %convert_bitcast_fusion.refs_0_), channel_id=1, source_target_pairs={{16,0},{20,4},{24,8},{28,12},{0,16},{4,20},{8,24},{12,28},{17,1},{... | collective-permute-start | bytes 884744 | tf_op jit(solution)/shard_map/ppermute | solution.py:1046
  100.4 13.6 %collective-permute-start.28 = (bf16[192,768]{1,0:T(8,128)(2,1)S(1)}, bf16[192,768]{1,0:T(8,128)(2,1)S(1)}, u32[]{:S(2)}, u32[]{:S(2)}) collective-permute-start(bf16[192,768]{1,0:T(8,128)(2,1)S(1)} %collective-permute-done.22.refs_3_), channel_id=1, source_target_pairs={{4,0},{0,4},{12,8},{8,12},{20,16},{16,20},{28,24},{24,28},{5,1},{1... | collective-permute-start | bytes 884744 | tf_op jit(solution)/shard_map/ppermute | solution.py:1055
  114.0 8.9 %collective-permute-start.29 = (bf16[192,768]{1,0:T(8,128)(2,1)S(1)}, bf16[192,768]{1,0:T(8,128)(2,1)S(1)}, u32[]{:S(2)}, u32[]{:S(2)}) collective-permute-start(bf16[192,768]{1,0:T(8,128)(2,1)S(1)} %collective-permute-done.26.refs_4_), channel_id=1, source_target_pairs={{4,0},{0,4},{12,8},{8,12},{20,16},{16,20},{28,24},{24,28},{5,1},{1... | collective-permute-start | bytes 884744 | tf_op jit(solution)/shard_map/ppermute | solution.py:1055
  123.0 13.7 %collective-permute-start.34 = (bf16[192,768]{1,0:T(8,128)(2,1)}, bf16[192,768]{1,0:T(8,128)(2,1)S(1)}, u32[]{:S(2)}, u32[]{:S(2)}) collective-permute-start(bf16[192,768]{1,0:T(8,128)(2,1)} %get-tuple-element.395), channel_id=1, source_target_pairs={{4,0},{0,4},{12,8},{8,12},{20,16},{16,20},{28,24},{24,28},{5,1},{1... | collective-permute-start | bytes 884744 | tf_op jit(solution)/shard_map/ppermute | solution.py:1055
  128.6 8.0 %collective-permute-start.33 = (f32[8,1024]{1,0:T(8,128)S(1)}, f32[8,1024]{1,0:T(8,128)S(1)}, u32[]{:S(2)}, u32[]{:S(2)}) collective-permute-start(f32[8,1024]{1,0:T(8,128)S(1)} %get-tuple-element.386), channel_id=1, source_target_pairs={{3,0},{2,1},{1,2},{0,3},{7,4},{6,5},{5,6},{4,7},{11,8},{10,9},{9,1... | collective-permute-start | bytes 98312 | tf_op jit(solution)/shard_map/ppermute | solution.py:1059
  128.7 7.9 %collective-permute-start.32 = (f32[8,1024]{1,0:T(8,128)S(1)}, f32[8,1024]{1,0:T(8,128)S(1)}, u32[]{:S(2)}, u32[]{:S(2)}) collective-permute-start(f32[8,1024]{1,0:T(8,128)S(1)} %get-tuple-element.386), channel_id=1, source_target_pairs={{2,0},{3,1},{0,2},{1,3},{6,4},{7,5},{4,6},{5,7},{10,8},{11,9},{8,1... | collective-permute-start | bytes 98312 | tf_op jit(solution)/shard_map/ppermute | solution.py:1059
  130.3 6.3 %collective-permute-start.31 = (f32[8,1024]{1,0:T(8,128)S(1)}, f32[8,1024]{1,0:T(8,128)S(1)}, u32[]{:S(2)}, u32[]{:S(2)}) collective-permute-start(f32[8,1024]{1,0:T(8,128)S(1)} %get-tuple-element.386), channel_id=1, source_target_pairs={{1,0},{0,1},{3,2},{2,3},{5,4},{4,5},{7,6},{6,7},{9,8},{8,9},{11,10... | collective-permute-start | bytes 98312 | tf_op jit(solution)/shard_map/ppermute | solution.py:1059
  136.7 16.1 %collective-permute-start.38 = (bf16[1024,384]{1,0:T(8,128)(2,1)}, bf16[1024,384]{1,0:T(8,128)(2,1)}, u32[]{:S(2)}, u32[]{:S(2)}) collective-permute-start(bf16[1024,384]{1,0:T(8,128)(2,1)} %get-tuple-element.398), channel_id=1, source_target_pairs={{1,0},{0,1},{3,2},{2,3},{5,4},{4,5},{7,6},{6,7},{9,8},{8,9},{11,10... | collective-permute-start | bytes 2359304 | tf_op jit(solution)/shard_map/ppermute | solution.py:1059
  137.0 15.8 %collective-permute-start.30 = (bf16[384,768]{1,0:T(8,128)(2,1)}, bf16[384,768]{1,0:T(8,128)(2,1)}, u32[]{:S(2)}, u32[]{:S(2)}) collective-permute-start(bf16[384,768]{1,0:T(8,128)(2,1)} %get-tuple-element.378), channel_id=1, source_target_pairs={{4,0},{0,4},{12,8},{8,12},{20,16},{16,20},{28,24},{24,28},{5,1},{1... | collective-permute-start | bytes 1769480 | tf_op jit(solution)/shard_map/ppermute | solution.py:1055
  138.4 13.5 %collective-permute-start.37 = (bf16[64,1536]{1,0:T(8,128)(2,1)}, bf16[64,1536]{1,0:T(8,128)(2,1)S(1)}, u32[]{:S(2)}, u32[]{:S(2)}) collective-permute-start(bf16[64,1536]{1,0:T(8,128)(2,1)} %get-tuple-element.419.refs_0_), channel_id=1, source_target_pairs={{3,0},{2,1},{1,2},{0,3},{7,4},{6,5},{5,6},{4,7},{11,8},{10,9},{9,1... | collective-permute-start | bytes 589832 | tf_op jit(solution)/shard_map/ppermute | solution.py:1059
  139.5 12.4 %collective-permute-start.36 = (bf16[64,1536]{1,0:T(8,128)(2,1)}, bf16[64,1536]{1,0:T(8,128)(2,1)S(1)}, u32[]{:S(2)}, u32[]{:S(2)}) collective-permute-start(bf16[64,1536]{1,0:T(8,128)(2,1)} %get-tuple-element.419.refs_0_), channel_id=1, source_target_pairs={{2,0},{3,1},{0,2},{1,3},{6,4},{7,5},{4,6},{5,7},{10,8},{11,9},{8,1... | collective-permute-start | bytes 589832 | tf_op jit(solution)/shard_map/ppermute | solution.py:1059
  140.0 11.9 %collective-permute-start.35 = (bf16[64,1536]{1,0:T(8,128)(2,1)}, bf16[64,1536]{1,0:T(8,128)(2,1)S(1)}, u32[]{:S(2)}, u32[]{:S(2)}) collective-permute-start(bf16[64,1536]{1,0:T(8,128)(2,1)} %get-tuple-element.419.refs_0_), channel_id=1, source_target_pairs={{1,0},{0,1},{3,2},{2,3},{5,4},{4,5},{7,6},{6,7},{9,8},{8,9},{11,10... | collective-permute-start | bytes 589832 | tf_op jit(solution)/shard_map/ppermute | solution.py:1059
  157.6 35.0 %collective-permute-start.39 = (bf16[192,768]{1,0:T(8,128)(2,1)S(1)}, bf16[192,768]{1,0:T(8,128)(2,1)S(1)}, u32[]{:S(2)}, u32[]{:S(2)}) collective-permute-start(bf16[192,768]{1,0:T(8,128)(2,1)S(1)} %get-tuple-element.425), channel_id=1, source_target_pairs={{24,0},{28,4},{0,8},{4,12},{8,16},{12,20},{16,24},{20,28},{25,1},{... | collective-permute-start | bytes 884744 | tf_op jit(solution)/shard_map/ppermute | solution.py:1046
  158.2 34.5 %collective-permute-start.40 = (bf16[192,768]{1,0:T(8,128)(2,1)S(1)}, bf16[192,768]{1,0:T(8,128)(2,1)S(1)}, u32[]{:S(2)}, u32[]{:S(2)}) collective-permute-start(bf16[192,768]{1,0:T(8,128)(2,1)S(1)} %get-tuple-element.426), channel_id=1, source_target_pairs={{8,0},{12,4},{16,8},{20,12},{24,16},{28,20},{0,24},{4,28},{9,1},{1... | collective-permute-start | bytes 884744 | tf_op jit(solution)/shard_map/ppermute | solution.py:1046
  161.5 31.3 %collective-permute-start.41 = (bf16[192,768]{1,0:T(8,128)(2,1)S(1)}, bf16[192,768]{1,0:T(8,128)(2,1)S(1)}, u32[]{:S(2)}, u32[]{:S(2)}) collective-permute-start(bf16[192,768]{1,0:T(8,128)(2,1)S(1)} %get-tuple-element.427), channel_id=1, source_target_pairs={{16,0},{20,4},{24,8},{28,12},{0,16},{4,20},{8,24},{12,28},{17,1},{... | collective-permute-start | bytes 884744 | tf_op jit(solution)/shard_map/ppermute | solution.py:1046
  162.4 30.4 %collective-permute-start.43 = (bf16[1024,384]{1,0:T(8,128)(2,1)S(1)}, bf16[1024,384]{1,0:T(8,128)(2,1)S(1)}, u32[]{:S(2)}, u32[]{:S(2)}) collective-permute-start(bf16[1024,384]{1,0:T(8,128)(2,1)S(1)} %add_convert_fusion.2), channel_id=1, source_target_pairs={{2,0},{3,1},{0,2},{1,3},{6,4},{7,5},{4,6},{5,7},{10,8},{11,9},{8,1... | collective-permute-start | bytes 2359304 | tf_op jit(solution)/shard_map/ppermute | solution.py:1059
  163.6 29.2 %collective-permute-start.42 = (bf16[576,768]{1,0:T(8,128)(2,1)S(1)}, bf16[576,768]{1,0:T(8,128)(2,1)S(1)}, u32[]{:S(2)}, u32[]{:S(2)}) collective-permute-start(bf16[576,768]{1,0:T(8,128)(2,1)S(1)} %copy-done.60), channel_id=1, source_target_pairs={{4,0},{0,4},{12,8},{8,12},{20,16},{16,20},{28,24},{24,28},{5,1},{1... | collective-permute-start | bytes 2654216 | tf_op jit(solution)/shard_map/ppermute | solution.py:1055
  192.7 10.5 %collective-permute-start.45 = (bf16[1024,384]{1,0:T(8,128)(2,1)S(1)}, bf16[1024,384]{1,0:T(8,128)(2,1)S(1)}, u32[]{:S(2)}, u32[]{:S(2)}) collective-permute-start(bf16[1024,384]{1,0:T(8,128)(2,1)S(1)} %copy-done.61), channel_id=1, source_target_pairs={{1,0},{0,1},{3,2},{2,3},{5,4},{4,5},{7,6},{6,7},{9,8},{8,9},{11,10... | collective-permute-start | bytes 2359304 | tf_op jit(solution)/shard_map/ppermute | solution.py:1059
  192.8 10.4 %collective-permute-start.44 = (bf16[128,1024]{1,0:T(8,128)(2,1)}, bf16[128,1024]{1,0:T(8,128)(2,1)S(1)}, u32[]{:S(2)}, u32[]{:S(2)}) collective-permute-start(bf16[128,1024]{1,0:T(8,128)(2,1)} %get-tuple-element.447), channel_id=1, source_target_pairs={{1,0},{0,1},{3,2},{2,3},{5,4},{4,5},{7,6},{6,7},{9,8},{8,9},{11,10... | collective-permute-start | bytes 786440 | tf_op jit(solution)/shard_map/ppermute | solution.py:1059
  193.4 20.5 %collective-permute-start.47 = (bf16[192,768]{1,0:T(8,128)(2,1)S(1)}, bf16[192,768]{1,0:T(8,128)(2,1)S(1)}, u32[]{:S(2)}, u32[]{:S(2)}) collective-permute-start(bf16[192,768]{1,0:T(8,128)(2,1)S(1)} %add_convert_fusion.8), channel_id=1, source_target_pairs={{16,0},{20,4},{24,8},{28,12},{0,16},{4,20},{8,24},{12,28},{17,1},{... | collective-permute-start | bytes 884744 | tf_op jit(solution)/shard_map/ppermute | solution.py:1046
  203.3 10.6 %collective-permute-start.46 = (bf16[64,1024]{1,0:T(8,128)(2,1)S(1)}, bf16[64,1024]{1,0:T(8,128)(2,1)S(1)}, u32[]{:S(2)}, u32[]{:S(2)}) collective-permute-start(bf16[64,1024]{1,0:T(8,128)(2,1)S(1)} %slice.466), channel_id=1, source_target_pairs={{2,0},{3,1},{0,2},{1,3},{6,4},{7,5},{4,6},{5,7},{10,8},{11,9},{8,1... | collective-permute-start | bytes 393224 | tf_op jit(solution)/shard_map/ppermute | solution.py:1059
  203.8 20.4 %collective-permute-start.49 = (bf16[192,768]{1,0:T(8,128)(2,1)}, bf16[192,768]{1,0:T(8,128)(2,1)S(1)}, u32[]{:S(2)}, u32[]{:S(2)}) collective-permute-start(bf16[192,768]{1,0:T(8,128)(2,1)} %get-tuple-element.475), channel_id=1, source_target_pairs={{4,0},{0,4},{12,8},{8,12},{20,16},{16,20},{28,24},{24,28},{5,1},{1... | collective-permute-start | bytes 884744 | tf_op jit(solution)/shard_map/ppermute | solution.py:1055
  204.6 19.5 %collective-permute-start.51 = (bf16[192,768]{1,0:T(8,128)(2,1)S(1)}, bf16[192,768]{1,0:T(8,128)(2,1)S(1)}, u32[]{:S(2)}, u32[]{:S(2)}) collective-permute-start(bf16[192,768]{1,0:T(8,128)(2,1)S(1)} %get-tuple-element.550), channel_id=1, source_target_pairs={{8,0},{12,4},{16,8},{20,12},{24,16},{28,20},{0,24},{4,28},{9,1},{1... | collective-permute-start | bytes 884744 | tf_op jit(solution)/shard_map/ppermute | solution.py:1046
  205.1 19.1 %collective-permute-start.50 = (bf16[192,768]{1,0:T(8,128)(2,1)S(1)}, bf16[192,768]{1,0:T(8,128)(2,1)S(1)}, u32[]{:S(2)}, u32[]{:S(2)}) collective-permute-start(bf16[192,768]{1,0:T(8,128)(2,1)S(1)} %get-tuple-element.551), channel_id=1, source_target_pairs={{24,0},{28,4},{0,8},{4,12},{8,16},{12,20},{16,24},{20,28},{25,1},{... | collective-permute-start | bytes 884744 | tf_op jit(solution)/shard_map/ppermute | solution.py:1046
  213.9 10.3 %collective-permute-start.48 = (bf16[256,1536]{1,0:T(8,128)(2,1)S(1)}, bf16[256,1536]{1,0:T(8,128)(2,1)S(1)}, u32[]{:S(2)}, u32[]{:S(2)}) collective-permute-start(bf16[256,1536]{1,0:T(8,128)(2,1)S(1)} %get-tuple-element.470), channel_id=1, source_target_pairs={{1,0},{0,1},{3,2},{2,3},{5,4},{4,5},{7,6},{6,7},{9,8},{8,9},{11,10... | collective-permute-start | bytes 2359304 | tf_op jit(solution)/shard_map/ppermute | solution.py:1059
  229.8 21.5 %collective-permute-start.58 = (bf16[384,768]{1,0:T(8,128)(2,1)S(1)}, bf16[384,768]{1,0:T(8,128)(2,1)S(1)}, u32[]{:S(2)}, u32[]{:S(2)}) collective-permute-start(bf16[384,768]{1,0:T(8,128)(2,1)S(1)} %copy-done.62), channel_id=1, source_target_pairs={{4,0},{0,4},{12,8},{8,12},{20,16},{16,20},{28,24},{24,28},{5,1},{1... | collective-permute-start | bytes 1769480 | tf_op jit(solution)/shard_map/ppermute | solution.py:1055
  231.3 20.1 %collective-permute-start.56 = (bf16[256,1536]{1,0:T(8,128)(2,1)S(1)}, bf16[256,1536]{1,0:T(8,128)(2,1)S(1)}, u32[]{:S(2)}, u32[]{:S(2)}) collective-permute-start(bf16[256,1536]{1,0:T(8,128)(2,1)S(1)} %add_convert_fusion), channel_id=1, source_target_pairs={{2,0},{3,1},{0,2},{1,3},{6,4},{7,5},{4,6},{5,7},{10,8},{11,9},{8,1... | collective-permute-start | bytes 2359304 | tf_op jit(solution)/shard_map/ppermute | solution.py:1059
  232.4 15.5 %collective-permute-start.59 = (f32[8,2688]{1,0:T(8,128)S(1)}, f32[8,2688]{1,0:T(8,128)S(1)}, u32[]{:S(2)}, u32[]{:S(2)}) collective-permute-start(f32[8,2688]{1,0:T(8,128)S(1)} %pad_maximum_fusion.4), channel_id=1, source_target_pairs={{4,0},{0,4},{12,8},{8,12},{20,16},{16,20},{28,24},{24,28},{5,1},{1... | collective-permute-start | bytes 258056 | tf_op jit(solution)/shard_map/ppermute | solution.py:1055
  233.2 18.1 %collective-permute-start.60 = (bf16[768,128]{1,0:T(8,128)(2,1)S(1)}, bf16[768,128]{1,0:T(8,128)(2,1)S(1)}, u32[]{:S(2)}, u32[]{:S(2)}) collective-permute-start(bf16[768,128]{1,0:T(8,128)(2,1)S(1)} %copy-done.63), channel_id=1, source_target_pairs={{4,0},{0,4},{12,8},{8,12},{20,16},{16,20},{28,24},{24,28},{5,1},{1... | collective-permute-start | bytes 589832 | tf_op jit(solution)/shard_map/ppermute | solution.py:1055
  234.5 16.8 %collective-permute-start.57 = (bf16[192,768]{1,0:T(8,128)(2,1)S(1)}, bf16[192,768]{1,0:T(8,128)(2,1)S(1)}, u32[]{:S(2)}, u32[]{:S(2)}) collective-permute-start(bf16[192,768]{1,0:T(8,128)(2,1)S(1)} %add_convert_fusion.5), channel_id=1, source_target_pairs={{16,0},{20,4},{24,8},{28,12},{0,16},{4,20},{8,24},{12,28},{17,1},{... | collective-permute-start | bytes 884744 | tf_op jit(solution)/shard_map/ppermute | solution.py:1046
  254.0 26.1 %collective-permute-start.61 = (bf16[256,1536]{1,0:T(8,128)(2,1)S(1)}, bf16[256,1536]{1,0:T(8,128)(2,1)S(1)}, u32[]{:S(2)}, u32[]{:S(2)}) collective-permute-start(bf16[256,1536]{1,0:T(8,128)(2,1)S(1)} %norm_backward.1.refs_0_), channel_id=1, source_target_pairs={{2,0},{3,1},{0,2},{1,3},{6,4},{7,5},{4,6},{5,7},{10,8},{11,9},{8,1... | collective-permute-start | bytes 2359304 | tf_op jit(solution)/shard_map/ppermute | solution.py:1059
  255.4 24.6 %collective-permute-start.65 = (bf16[192,2304]{1,0:T(8,128)(2,1)S(1)}, bf16[192,2304]{1,0:T(8,128)(2,1)S(1)}, u32[]{:S(2)}, u32[]{:S(2)}) collective-permute-start(bf16[192,2304]{1,0:T(8,128)(2,1)S(1)} %pad_maximum_fusion), channel_id=1, source_target_pairs={{4,0},{0,4},{12,8},{8,12},{20,16},{16,20},{28,24},{24,28},{5,1},{1... | collective-permute-start | bytes 2654216 | tf_op jit(solution)/shard_map/ppermute | solution.py:1055
  257.1 23.0 %collective-permute-start.63 = (bf16[224,896]{1,0:T(8,128)(2,1)S(1)}, bf16[224,896]{1,0:T(8,128)(2,1)S(1)}, u32[]{:S(2)}, u32[]{:S(2)}) collective-permute-start(bf16[224,896]{1,0:T(8,128)(2,1)S(1)} %get-tuple-element.574), channel_id=1, source_target_pairs={{8,0},{12,4},{16,8},{20,12},{24,16},{28,20},{0,24},{4,28},{9,1},{1... | collective-permute-start | bytes 1204232 | tf_op jit(solution)/shard_map/ppermute | solution.py:1046
  260.2 19.9 %collective-permute-start.62 = (bf16[224,896]{1,0:T(8,128)(2,1)S(1)}, bf16[224,896]{1,0:T(8,128)(2,1)S(1)}, u32[]{:S(2)}, u32[]{:S(2)}) collective-permute-start(bf16[224,896]{1,0:T(8,128)(2,1)S(1)} %get-tuple-element.575), channel_id=1, source_target_pairs={{24,0},{28,4},{0,8},{4,12},{8,16},{12,20},{16,24},{20,28},{25,1},{... | collective-permute-start | bytes 1204232 | tf_op jit(solution)/shard_map/ppermute | solution.py:1046
  260.2 19.9 %collective-permute-start.64 = (bf16[416,128]{1,0:T(8,128)(2,1)S(1)}, bf16[416,128]{1,0:T(8,128)(2,1)S(1)}, u32[]{:S(2)}, u32[]{:S(2)}) collective-permute-start(bf16[416,128]{1,0:T(8,128)(2,1)S(1)} %pad_maximum_fusion.3), channel_id=1, source_target_pairs={{16,0},{20,4},{24,8},{28,12},{0,16},{4,20},{8,24},{12,28},{17,1},{... | collective-permute-start | bytes 319496 | tf_op jit(solution)/shard_map/ppermute | solution.py:1046
  280.9 11.8 %collective-permute-start.70 = (f32[192,128]{1,0:T(8,128)S(1)}, f32[192,128]{1,0:T(8,128)S(1)}, u32[]{:S(2)}, u32[]{:S(2)}) collective-permute-start(f32[192,128]{1,0:T(8,128)S(1)} %get-tuple-element.538.refs_0_), channel_id=1, source_target_pairs={{3,0},{2,1},{1,2},{0,3},{7,4},{6,5},{5,6},{4,7},{11,8},{10,9},{9,1... | collective-permute-start | bytes 294920 | tf_op jit(solution)/shard_map/ppermute | solution.py:1059
  280.9 11.8 %collective-permute-start.69 = (f32[192,128]{1,0:T(8,128)S(1)}, f32[192,128]{1,0:T(8,128)S(1)}, u32[]{:S(2)}, u32[]{:S(2)}) collective-permute-start(f32[192,128]{1,0:T(8,128)S(1)} %get-tuple-element.538.refs_0_), channel_id=1, source_target_pairs={{2,0},{3,1},{0,2},{1,3},{6,4},{7,5},{4,6},{5,7},{10,8},{11,9},{8,1... | collective-permute-start | bytes 294920 | tf_op jit(solution)/shard_map/ppermute | solution.py:1059
  282.1 10.6 %collective-permute-start.68 = (f32[192,128]{1,0:T(8,128)S(1)}, f32[192,128]{1,0:T(8,128)S(1)}, u32[]{:S(2)}, u32[]{:S(2)}) collective-permute-start(f32[192,128]{1,0:T(8,128)S(1)} %get-tuple-element.538.refs_0_), channel_id=1, source_target_pairs={{1,0},{0,1},{3,2},{2,3},{5,4},{4,5},{7,6},{6,7},{9,8},{8,9},{11,10... | collective-permute-start | bytes 294920 | tf_op jit(solution)/shard_map/ppermute | solution.py:1059
  283.1 10.5 %collective-permute-start.66 = (bf16[256,1536]{1,0:T(8,128)(2,1)S(1)}, bf16[256,1536]{1,0:T(8,128)(2,1)S(1)}, u32[]{:S(2)}, u32[]{:S(2)}) collective-permute-start(bf16[256,1536]{1,0:T(8,128)(2,1)S(1)} %norm_backward.1.refs_0_), channel_id=1, source_target_pairs={{1,0},{0,1},{3,2},{2,3},{5,4},{4,5},{7,6},{6,7},{9,8},{8,9},{11,10... | collective-permute-start | bytes 2359304 | tf_op jit(solution)/shard_map/ppermute | solution.py:1059
  283.1 10.5 %collective-permute-start.67 = (bf16[256,1536]{1,0:T(8,128)(2,1)S(1)}, bf16[256,1536]{1,0:T(8,128)(2,1)S(1)}, u32[]{:S(2)}, u32[]{:S(2)}) collective-permute-start(bf16[256,1536]{1,0:T(8,128)(2,1)S(1)} %collective-permute-done.61.refs_2_), channel_id=1, source_target_pairs={{1,0},{0,1},{3,2},{2,3},{5,4},{4,5},{7,6},{6,7},{9,8},{8,9},{11,10... | collective-permute-start | bytes 2359304 | tf_op jit(solution)/shard_map/ppermute | solution.py:1059
  (71 other events, 898.2 us)

commit v6 on v5

--- a/solution.py
+++ b/solution.py
@@ -57,23 +57,21 @@
     return dot_nn(high, expand) + dot_nn(mid, expand) + dot_nn(low, expand)
 
 
-def gather_heads(v, expand):
+def gather_heads(v, expand_t):
     high = v.astype(bf16)
     mid = (v - high.astype(f32)).astype(bf16)
-    return dot_nt(high, expand) + dot_nt(mid, expand)
+    return dot_nn(high, expand_t) + dot_nn(mid, expand_t)
 
 
 def sigmoid(v):
-    return 1.0 / (1.0 + jnp.exp(-v))
-
-
-def conv_block(scratch, before, now, taps, keep):
-    rows = now.shape[0]
-    scratch[0:HALO, :] = before
-    scratch[HALO:HALO + rows, :] = now
+    return 0.5 * jnp.tanh(0.5 * v) + 0.5
+
+
+def conv_block(before, now, taps, keep):
+    longer = jnp.concatenate([before, now], axis=0)
     total = taps[4:5, :] + taps[0:1, :] * now
     for lag in (1, 2, 3):
-        moved = scratch[HALO - lag:HALO - lag + rows, :]
+        moved = pltpu.roll(longer, lag, 0)[HALO:, :]
         total = total + taps[lag:lag + 1, :] * (moved * keep[:, lag - 1:lag])
     return total
 
@@ -93,7 +91,8 @@
 
 def ssd_forward_kernel(
     x_ref, xb_ref, bc_ref, bcb_ref, st_ref, aux_ref, seg_ref, conv_ref, bct_ref, heads_ref, expand_ref,
-    mixed_ref, state_ref, state, xs_scr, bc_scr,
+    mixed_ref, state_ref, act_ref, slope_ref, xs_ref, xe_ref, step_ref, entry_ref, end_ref, bcact_ref, bcslope_ref,
+    state,
 ):
     chunk = pl.program_id(0)
 
@@ -104,10 +103,16 @@
     channels = x_ref.shape[1]
     aux = aux_ref[...]
     expand = expand_ref[...]
-    u = conv_block(xs_scr, xb_ref[...], x_ref[...], conv_ref, aux)
-    x_act = u * sigmoid(u)
-    ubc = conv_block(bc_scr, bcb_ref[...], bc_ref[...], bct_ref, aux)
-    bc_act = (ubc * sigmoid(ubc)).astype(bf16)
+    u = conv_block(xb_ref[...], x_ref[...], conv_ref, aux)
+    sg = sigmoid(u)
+    x_act = u * sg
+    act_ref[...] = x_act
+    slope_ref[...] = (sg * (1.0 + u * (1.0 - sg))).astype(bf16)
+    ubc = conv_block(bcb_ref[...], bc_ref[...], bct_ref, aux)
+    sgbc = sigmoid(ubc)
+    bc_act = (ubc * sgbc).astype(bf16)
+    bcact_ref[...] = bc_act
+    bcslope_ref[...] = sgbc * (1.0 + ubc * (1.0 - sgbc))
     b_mat, c_mat = bc_act[:, :LANES], bc_act[:, LANES:]
     _, steps, rates = step_parts(st_ref[...], heads_ref)
     lower = triangle(True)
@@ -123,11 +128,17 @@
     scores = jnp.where(mask, dot_nt(c_mat, b_mat), 0.0)
     xs = x_act * step_e
     xs_low = xs.astype(bf16)
+    xe_low = (xs * to_end_e).astype(bf16)
+    xs_ref[...] = xs_low
+    xe_ref[...] = xe_low
+    step_ref[...] = step_e.astype(bf16)
+    entry_ref[...] = entry_e.astype(bf16)
+    end_ref[...] = to_end_e.astype(bf16)
     held = state[...]
     held_low = held.astype(bf16)
     state_ref[...] = held_low
     out = dot_nn(c_mat, held_low) * entry_e + skip_e * x_act
-    state[...] = held * entry_e[CHUNK - 1:CHUNK, :] + dot_tn(b_mat, (xs * to_end_e).astype(bf16))
+    state[...] = held * entry_e[CHUNK - 1:CHUNK, :] + dot_tn(b_mat, xe_low)
     first = lax.broadcasted_iota(jnp.int32, (CHUNK, LANES), 1) < WIDTH
     zero = jnp.zeros((CHUNK, LANES), bf16)
     for pair in range(channels // LANES):
@@ -142,10 +153,10 @@
 
 
 def ssd_backward_kernel(
-    rank_ref, x_ref, xb_ref, bc_ref, bcb_ref, st_ref, aux_ref, seg_ref, conv_ref, bct_ref, heads_ref, expand_ref,
-    mixed_ref, dy_ref, state_ref,
-    dx_ref, dbc_ref, keep_ref, send_ref, dst_ref, dst_t_ref, dconv_ref, dbct_ref, dheads_ref,
-    dstate, xs_scr, bc_scr, du_scr, dubc_scr, share_scr,
+    rank_ref, x_ref, bc_ref, st_ref, aux_ref, seg_ref, conv_ref, bct_ref, heads_ref, expand_ref,
+    expand_t_ref, mixed_ref, dy_ref, state_ref, act_ref, slope_ref, xs_ref, xe_ref, step_ref, entry_ref, end_ref, bcact_ref,
+    bcslope_ref, dx_ref, dbc_ref, keep_ref, send_ref, dst_ref, dst_t_ref, dconv_ref, dbct_ref, dheads_ref,
+    dstate, du_scr, dubc_scr, share_scr,
 ):
     @pl.when(pl.program_id(0) == 0)
     def _():
@@ -155,40 +166,29 @@
     channels = x_ref.shape[1]
     aux = aux_ref[...]
     expand = expand_ref[...]
-    x_now, bc_now = x_ref[...], bc_ref[...]
-    u = conv_block(xs_scr, xb_ref[...], x_now, conv_ref, aux)
-    sg = sigmoid(u)
-    x_act = u * sg
-    ubc = conv_block(bc_scr, bcb_ref[...], bc_now, bct_ref, aux)
-    sgbc = sigmoid(ubc)
-    bc_act = (ubc * sgbc).astype(bf16)
-    b_mat, c_mat = bc_act[:, :LANES], bc_act[:, LANES:]
+    x_act = act_ref[...]
+    b_mat, c_mat = bcact_ref[:, :LANES], bcact_ref[:, LANES:]
     raw, steps, rates = step_parts(st_ref[...], heads_ref)
     lower = triangle(True)
     cum = exact_left(lower.astype(bf16), steps * rates)
     cum_t = cum.T
-    tail = cum[CHUNK - 1:CHUNK, :]
-    entry = jnp.exp(cum) * aux[:, 6:7]
-    to_end = jnp.exp(tail - cum) * aux[:, 7:8]
-    wide = spread(jnp.concatenate([steps, entry, to_end], axis=0), expand)
-    step_e, entry_e, to_end_e = wide[:CHUNK], wide[CHUNK:2 * CHUNK], wide[2 * CHUNK:]
     skip_e = spread(jnp.broadcast_to(heads_ref[2:3, :], (8, LANES)), expand)[0:1, :]
     upper = triangle(False)
     mask = upper & (aux[:, 8:9] == seg_ref[...])
     scores = jnp.where(mask, dot_nt(b_mat, c_mat), 0.0)
-    xs = x_act * step_e
-    xs_low = xs.astype(bf16)
+    xs_low = xs_ref[...]
     dy_low = dy_ref[...]
     dy = dy_low.astype(f32)
     held_low = state_ref[...]
     grad = dstate[...]
     grad_low = grad.astype(bf16)
+    entry_e = entry_ref[...].astype(f32)
     entry_dy = (entry_e * dy).astype(bf16)
     kept_e = entry_e[CHUNK - 1:CHUNK, :]
     dstate[...] = grad * kept_e + dot_tn(c_mat, entry_dy)
     dc = dot_nt(entry_dy, held_low)
-    db = dot_nt((xs * to_end_e).astype(bf16), grad_low)
-    q_state = dot_nn(b_mat, grad_low) * to_end_e
+    db = dot_nt(xe_ref[...], grad_low)
+    q_state = dot_nn(b_mat, grad_low) * end_ref[...].astype(f32)
     first = lax.broadcasted_iota(jnp.int32, (CHUNK, LANES), 1) < WIDTH
     zero = jnp.zeros((CHUNK, LANES), bf16)
     dscores = jnp.zeros((CHUNK, CHUNK), f32)
@@ -210,17 +210,9 @@
     db = db + dot_nn(dscores_low, c_mat)
     dc = dc + dot_tn(dscores_low, b_mat)
     xs_round = xs_low.astype(f32)
-    rows = gather_heads(
-        jnp.concatenate(
-            [
-                dy * (mixed_ref[...] - skip_e * x_act) - xs_round * q,
-                x_act * q,
-            ],
-            axis=0,
-        ),
-        expand,
-    )
-    flow, dstep = rows[:CHUNK], rows[CHUNK:]
+    expand_t = expand_t_ref[...]
+    flow = gather_heads(dy * (mixed_ref[...] - skip_e * x_act) - xs_round * q, expand_t)
+    dstep = dot_nn((x_act * q).astype(bf16), expand_t)
     sums = jnp.concatenate(
         [
             jnp.sum(xs_round * q_state + kept_e * (held_low.astype(f32) * grad), axis=0, keepdims=True),
@@ -229,7 +221,7 @@
         ],
         axis=0,
     )
-    sums = gather_heads(sums, expand)
+    sums = gather_heads(sums, expand_t)
     dlog = exact_left(upper.astype(bf16), flow) + sums[0:1, :]
     dstep = dstep + rates * dlog
     draw = dstep * sigmoid(raw)
@@ -238,22 +230,24 @@
     dheads_ref[0:1, :] += jnp.sum(draw, axis=0, keepdims=True)
     dheads_ref[1:2, :] += rates * jnp.sum(dlog * steps, axis=0, keepdims=True)
     dheads_ref[2:3, :] += sums[1:2, :]
+    x_now, bc_now = x_ref[...], bc_ref[...]
 
     def conv_back(scratch, du, now, taps, dtaps):
-        scratch[0:CHUNK, :] = du
+        longer = jnp.concatenate([du, scratch[...]], axis=0)
         total = taps[0:1, :] * du
-        dtaps[0:1, :] += jnp.sum(now * du, axis=0, keepdims=True)
-        dtaps[4:5, :] += jnp.sum(du, axis=0, keepdims=True)
+        sums = [jnp.sum(now * du, axis=0, keepdims=True)]
         for lag in (1, 2, 3):
-            moved = scratch[lag:lag + CHUNK, :] * aux[:, 2 + lag:3 + lag]
+            moved = pltpu.roll(longer, CHUNK + HALO - lag, 0)[0:CHUNK, :] * aux[:, 2 + lag:3 + lag]
             total = total + taps[lag:lag + 1, :] * moved
-            dtaps[lag:lag + 1, :] += jnp.sum(now * moved, axis=0, keepdims=True)
-        scratch[CHUNK:CHUNK + HALO, :] = du[0:HALO, :]
+            sums.append(jnp.sum(now * moved, axis=0, keepdims=True))
+        sums.append(jnp.sum(du, axis=0, keepdims=True))
+        dtaps[0:5, :] += jnp.concatenate(sums, axis=0)
+        scratch[...] = du[0:HALO, :]
         return total
 
-    du = (skip_e * dy + step_e * q) * (sg * (1.0 + u * (1.0 - sg)))
+    du = (skip_e * dy + step_ref[...].astype(f32) * q) * slope_ref[...].astype(f32)
     dx_ref[...] = conv_back(du_scr, du, x_now, conv_ref, dconv_ref).astype(dx_ref.dtype)
-    dubc = jnp.concatenate([db, dc], axis=1) * (sgbc * (1.0 + ubc * (1.0 - sgbc)))
+    dubc = jnp.concatenate([db, dc], axis=1) * bcslope_ref[...]
     dbc = conv_back(dubc_scr, dubc, bc_now, bct_ref, dbct_ref).astype(bf16)
     dbc_ref[...] = dbc
     share = 2 * LANES // 4
@@ -296,17 +290,21 @@
         out_specs=[
             pl.BlockSpec((CHUNK, channels), now),
             pl.BlockSpec((None, LANES, channels), lambda i: (i, 0, 0)),
-        ],
+        ]
+        + [pl.BlockSpec((CHUNK, channels), now)] * 7
+        + [pl.BlockSpec((CHUNK, 2 * LANES), now)] * 2,
         out_shape=[
             hbm((tokens, channels), f32),
             hbm((count, LANES, channels), bf16),
+            hbm((tokens, channels), f32),
+            *[hbm((tokens, channels), bf16) for _ in range(6)],
+            hbm((tokens, 2 * LANES), bf16),
+            hbm((tokens, 2 * LANES), f32),
         ],
         scratch_shapes=[
             pltpu.VMEM((LANES, channels), f32),
-            pltpu.VMEM((HALO + CHUNK, channels), f32),
-            pltpu.VMEM((HALO + CHUNK, 2 * LANES), f32),
-        ],
-        compiler_params=pltpu.CompilerParams(vmem_limit_bytes=14 * MIB),
+        ],
+        compiler_params=pltpu.CompilerParams(vmem_limit_bytes=18 * MIB),
         cost_estimate=pl.CostEstimate(flops=14 * 10**9, bytes_accessed=40 * 10**6, transcendentals=0),
         name="ssd_forward",
     )(
@@ -314,33 +312,33 @@
     )
 
 
-def ssd_backward(rank, x_pre, bc_pre, step_pre, aux, seg_row, conv_rows, bc_rows, head_rows, expand, mixed, dy, states):
+def ssd_backward(rank, x_pre, bc_pre, step_pre, aux, seg_row, conv_rows, bc_rows, head_rows, expand, expand_t, dy, kept):
     tokens, channels = x_pre.shape
     count = tokens // CHUNK
     place = lambda i: count - 1 - i
     now = lambda i: (place(i), 0)
     whole = lambda i: (0, 0)
-    sums = [
-        jax.ShapeDtypeStruct((8, channels), f32),
-        jax.ShapeDtypeStruct((8, 2 * LANES), f32),
-        jax.ShapeDtypeStruct((8, LANES), f32),
-    ]
+    wide = pl.BlockSpec((CHUNK, channels), now)
+    narrow = pl.BlockSpec((CHUNK, 2 * LANES), now)
+    specs = common_specs(place, channels)
+    mixed, states, *more = kept
     return pl.pallas_call(
         ssd_backward_kernel,
         grid=(count,),
-        in_specs=[pl.BlockSpec(memory_space=pltpu.SMEM)] + common_specs(place, channels) + [
-            pl.BlockSpec((CHUNK, channels), now),
-            pl.BlockSpec((CHUNK, channels), now),
-            pl.BlockSpec((None, LANES, channels), lambda i: (place(i), 0, 0)),
-        ],
+        in_specs=[pl.BlockSpec(memory_space=pltpu.SMEM), specs[0], specs[2], *specs[4:]]
+        + [pl.BlockSpec((channels, LANES), whole), wide, wide, pl.BlockSpec((None, LANES, channels), lambda i: (place(i), 0, 0))]
+        + [wide] * 7 + [narrow] * 2,
         out_specs=[
-            pl.BlockSpec((CHUNK, channels), now),
-            pl.BlockSpec((CHUNK, 2 * LANES), now),
+            wide,
+            narrow,
             pl.BlockSpec((LANES, CHUNK), lambda i: (0, place(i))),
             pl.BlockSpec((LANES, CHUNK), lambda i: (0, place(i))),
             pl.BlockSpec((CHUNK, LANES), now),
             pl.BlockSpec((16, CHUNK), lambda i: (0, place(i))),
-        ] + [pl.BlockSpec(v.shape, whole) for v in sums],
+            pl.BlockSpec((8, channels), whole),
+            pl.BlockSpec((8, 2 * LANES), whole),
+            pl.BlockSpec((8, LANES), whole),
+        ],
         out_shape=[
             hbm((tokens, channels), bf16),
             hbm((tokens, 2 * LANES), bf16),
@@ -348,21 +346,22 @@
             hbm((LANES, tokens), bf16),
             hbm((tokens, LANES), bf16),
             hbm((16, tokens), bf16),
-        ] + sums,
+            jax.ShapeDtypeStruct((8, channels), f32),
+            jax.ShapeDtypeStruct((8, 2 * LANES), f32),
+            jax.ShapeDtypeStruct((8, LANES), f32),
+        ],
         scratch_shapes=[
             pltpu.VMEM((LANES, channels), f32),
-            pltpu.VMEM((HALO + CHUNK, channels), f32),
-            pltpu.VMEM((HALO + CHUNK, 2 * LANES), f32),
-            pltpu.VMEM((HALO + CHUNK, channels), f32),
-            pltpu.VMEM((HALO + CHUNK, 2 * LANES), f32),
+            pltpu.VMEM((HALO, channels), f32),
+            pltpu.VMEM((HALO, 2 * LANES), f32),
             pltpu.VMEM((2 * LANES, CHUNK), bf16),
         ],
-        compiler_params=pltpu.CompilerParams(vmem_limit_bytes=16 * MIB),
+        compiler_params=pltpu.CompilerParams(vmem_limit_bytes=20 * MIB),
         cost_estimate=pl.CostEstimate(flops=28 * 10**9, bytes_accessed=40 * 10**6, transcendentals=0),
         name="ssd_backward",
     )(
-        rank, from_hbm(x_pre), from_hbm(x_pre), bc_pre, bc_pre, step_pre, aux, seg_row, conv_rows, bc_rows, head_rows,
-        expand, from_hbm(mixed), dy, from_hbm(states),
+        rank, from_hbm(x_pre), bc_pre, step_pre, aux, seg_row, conv_rows, bc_rows, head_rows,
+        expand, expand_t, from_hbm(mixed), dy, from_hbm(states), *[from_hbm(v) for v in more],
     )
 
 
@@ -393,8 +392,8 @@
 
 
 def head_expand(channels):
-    head = jnp.arange(LANES)[:, None]
-    return (head == (jnp.arange(channels) // WIDTH)[None, :]).astype(bf16)
+    head, channel = jnp.arange(LANES), jnp.arange(channels) // WIDTH
+    return (head[:, None] == channel[None, :]).astype(bf16), (channel[:, None] == head[None, :]).astype(bf16)
 
 
 TILE = 256
@@ -589,7 +588,7 @@
         out_shape=[
             jax.ShapeDtypeStruct((LANES, tokens), f32),
             jax.ShapeDtypeStruct((share, tokens), bf16),
-            jax.ShapeDtypeStruct((depth, LANES), bf16),
+            hbm((depth, LANES), bf16),
             jax.ShapeDtypeStruct((share, depth), bf16),
         ],
         compiler_params=params(),
@@ -868,7 +867,8 @@
         normed = hidden_ref[span, :].astype(f32) * row_to_column(inv_ref[0:1, span])
         own = jnp.sum(total * normed, axis=0, keepdims=True)
         gain = own if gain is None else gain + own
-    dgain_ref[...] = jnp.broadcast_to(gain, dgain_ref.shape)
+    cut = [gain[:, i:i + LANES] for i in range(0, gain.shape[1], LANES)]
+    dgain_ref[...] = jnp.concatenate(cut + [jnp.zeros((8 - len(cut), LANES), f32)], axis=0)
 
 
 def normed_term(dx, dgate, dstep, dbc, w_a, w_b, w_s, w_bct, hidden, inv_rms, rank, ranks, apart):
@@ -892,10 +892,11 @@
             pl.BlockSpec((tokens, TILE_D), lambda i: (0, i)),
             pl.BlockSpec(inv_rms.shape, whole),
         ],
-        out_specs=[pl.BlockSpec((rows, TILE_D), lambda i: (0, i))] * len(apart) + [pl.BlockSpec((8, TILE_D), lambda i: (0, i))],
-        out_shape=[jax.ShapeDtypeStruct((rows, depth), bf16)] * len(apart) + [jax.ShapeDtypeStruct((8, depth), f32)],
+        out_specs=[pl.BlockSpec((rows, TILE_D), lambda i: (0, i))] * len(apart) + [pl.BlockSpec((8, LANES), lambda i: (i, 0))],
+        out_shape=[jax.ShapeDtypeStruct((rows, depth), bf16)] * len(apart)
+        + [jax.ShapeDtypeStruct((8 * (depth // TILE_D), LANES), f32)],
         compiler_params=params(32),
-        cost_estimate=cost(20),
+        cost_estimate=cost(20 if 2 in apart else 0.1),
         name="normed_term",
     )(
         rank, dx, from_hbm(w_a), dgate, from_hbm(w_b), dstep, from_hbm(w_s), dbc,
@@ -975,46 +976,70 @@
     )(from_hbm(weight), from_hbm(moment), *[part for part, _ in parts])
 
 
-def update_small_kernel(w_ref, m_ref, *refs, share):
-    parts, (m_out, w_out, share_out, scratch) = refs[:-4], refs[-4:]
+def update_small_kernel(w_ref, m_ref, sums_ref, own_ref, back_ref, *refs, share, order, shared):
+    alone, late, (m_out, w_out, exchange, totals, scratch) = refs[:order[0]], refs[order[0]:-5], refs[-5:]
     heads, rows = w_ref.shape
-    total = add_up(parts)
-    share_out[...] = total
-    scratch[0:rows, :] = total
-    grad = scratch[...].T[share:share + heads, 0:rows]
-    fresh, weight = moved(w_ref[...], m_ref[...], grad)
+    count = sums_ref.shape[0]
+    last = late[0].shape[1] - LANES
+    grad = own_ref[...].astype(f32) + back_ref[...].astype(f32)
+    found = {0: sums_ref[...].astype(f32)}
+    for at, ref in zip(order[1], alone):
+        grad = grad + ref[0:rows, :].astype(f32)
+        found[at] = ref[rows:, :].astype(f32)
+    for at, ref in zip(order[2], late):
+        grad = grad + ref[0:rows, last:].astype(f32)
+        tail = ref[rows:, :].astype(f32)
+        found[at] = jnp.concatenate([tail[:, i:i + LANES] for i in range(0, tail.shape[1], LANES)], axis=0)
+    step = len(found) // 2
+    while step >= 1:
+        found = {i: found[i] + found[i + step] for i in range(step)}
+        step //= 2
+    totals[...] = found[0]
+    exchange[0:rows, :] = grad
+    exchange[rows:, :] = found[0][shared[0]:shared[1], :]
+    scratch[0:rows, :] = grad
+    turned = scratch[...].T[share:share + heads, 0:rows]
+    fresh, weight = moved(w_ref[...], m_ref[...], turned)
     m_out[...] = fresh
     w_out[...] = weight
 
 
-def update_small(weight_t, moment_t, parts, share):
+def update_small(weight_t, moment_t, sums, own, back, alone, late, order, shared, share):
     rows = weight_t.shape[1]
+    count = sums.shape[0]
     whole = lambda i: (0, 0)
     spec = pl.BlockSpec(weight_t.shape, whole)
     return pl.pallas_call(
-        functools.partial(update_small_kernel, share=share),
+        functools.partial(update_small_kernel, share=share, order=order, shared=shared),
         grid=(1,),
-        in_specs=[spec, spec] + [pl.BlockSpec((rows, LANES), functools.partial(lambda at, i: (0, at), at)) for _, at in parts],
-        out_specs=[spec, spec, pl.BlockSpec((rows, LANES), whole)],
-        out_shape=[jax.ShapeDtypeStruct(weight_t.shape, f32)] * 2 + [jax.ShapeDtypeStruct((rows, LANES), f32)],
+        in_specs=[spec, spec, pl.BlockSpec(sums.shape, whole)] + [pl.BlockSpec((rows, LANES), whole)] * 2
+        + [pl.BlockSpec(v.shape, whole) for v in (*alone, *late)],
+        out_specs=[
+            spec, spec,
+            pl.BlockSpec((rows + shared[1] - shared[0], LANES), whole),
+            pl.BlockSpec((count, LANES), whole),
+        ],
+        out_shape=[jax.ShapeDtypeStruct(weight_t.shape, f32)] * 2
+        + [jax.ShapeDtypeStruct((rows + shared[1] - shared[0], LANES), f32), jax.ShapeDtypeStruct((count, LANES), f32)],
         scratch_shapes=[pltpu.VMEM((2 * LANES, LANES), f32)],
         compiler_params=params(),
         cost_estimate=cost(0.1),
         name="update_small",
-    )(weight_t, moment_t, *[part for part, _ in parts])
+    )(weight_t, moment_t, sums, own, back, *alone, *late)
 
 
 def update_bc_kernel(rank_ref, w_ref, m_ref, *refs):
-    pieces, (m_out, w_out) = refs[:-2], refs[-2:]
+    pieces, (m_out, w_out, shared_out) = refs[:-3], refs[-3:]
     rows, width = w_ref.shape
     share = width // len(pieces)
+    shared_out[...] = (pieces[0][rows:, :] + pieces[1][rows:, :]) + (pieces[2][rows:, :] + pieces[3][rows:, :])
     lane = lax.broadcasted_iota(jnp.int32, (rows, LANES), 1)
     for pair in range(width // LANES):
         halves = []
         for member in (2 * pair, 2 * pair + 1):
-            own = pieces[0][...]
+            own = pieces[0][0:rows, :]
             for r in range(1, len(pieces)):
-                own = jnp.where((rank_ref[0] ^ r) == member, pieces[r][...], own)
+                own = jnp.where((rank_ref[0] ^ r) == member, pieces[r][0:rows, :], own)
             halves.append(own)
         grad = jnp.where(lane < share, halves[0], pltpu.roll(halves[1], share, 1))
         span = slice(pair * LANES, (pair + 1) * LANES)
@@ -1028,8 +1053,9 @@
     return pl.pallas_call(
         update_bc_kernel,
         in_specs=[pl.BlockSpec(memory_space=pltpu.SMEM)] + [vmem] * (2 + len(pieces)),
-        out_specs=[vmem, vmem],
-        out_shape=[jax.ShapeDtypeStruct(weight.shape, f32)] * 2,
+        out_specs=[vmem] * 3,
+        out_shape=[jax.ShapeDtypeStruct(weight.shape, f32)] * 2
+        + [jax.ShapeDtypeStruct((pieces[0].shape[0] - weight.shape[0], LANES), f32)],
         compiler_params=params(),
         cost_estimate=cost(0.1),
         name="update_bc",
@@ -1196,7 +1222,7 @@
     a_x.update(flip_all(a_z, near_ks))
     aux, seg_row = segment_facts(segments)
     head_rows = pad_lanes(pad_rows(head_table))
-    facts = (aux, seg_row, pad_rows(conv_table), pad_rows(bc_table), head_rows, head_expand(channels))
+    facts = (aux, seg_row, pad_rows(conv_table), pad_rows(bc_table), head_rows, *head_expand(channels))
     set_a, set_b, set_c, a_z, a_x, cot_far, normed_low, normed_t, inv_rms, facts = fence(
         set_a, set_b, set_c, a_z, a_x, cot_far, normed_low, normed_t, inv_rms, facts
     )
@@ -1224,8 +1250,9 @@
 
     c_z = outer_all(set_c, near_ks)
     b_x.update(flip_all(b_z, ks[1:]))
-    mixed, states = ssd_forward(x_pre, bc_pre, step_pre, *facts)
-    mixed, states, b_x, b_z, c_z, c_x, w_bct_share, set_c = fence(mixed, states, b_x, b_z, c_z, c_x, w_bct_share, set_c)
+    kept = ssd_forward(x_pre, bc_pre, step_pre, *facts[:-1])
+    mixed = kept[0]
+    mixed, b_x, b_z, c_z, c_x, w_bct_share, set_c = fence(mixed, b_x, b_z, c_z, c_x, w_bct_share, set_c)
 
     c_z[far_k] = outer_from(set_c, far_k)
     c_x.update(flip_all(c_z, near_ks))
@@ -1234,11 +1261,12 @@
     mixed, gate_pre, square, w_b, w_bct_share, c_z, c_x = fence(mixed, gate_pre, square, w_b, w_bct_share, c_z, c_x)
 
     c_x[far_k] = inner_flip(c_z[far_k])
+    w_bct = [w_bct_share, rank_flip(w_bct_share, 2)]
     conv_rows = facts[2]
     gated_out = gated_norm(gate_pre, mixed, square, conv_rows, channels * ranks)
     gc_own, gc_own1, gc_here, gc_near, gc_far = weight_grad(cot_t, gated_out, idx, split_sizes)
-    c_x, square, gated_out, gc_own, gc_own1, gc_here, gc_near, gc_far, w_bct_share = fence(
-        c_x, square, gated_out, gc_own, gc_own1, gc_here, gc_near, gc_far, w_bct_share
+    c_x, square, gated_out, gc_own, gc_own1, gc_here, gc_near, gc_far, w_bct = fence(
+        c_x, square, gated_out, gc_own, gc_own1, gc_here, gc_near, gc_far, w_bct
     )
 
     gc_far_back, gc_near_back = inner_flip(gc_far), inner_flip(gc_near)
@@ -1246,25 +1274,25 @@
     gout, inner_dot, w_c = fence(gout, inner_dot, w_c)
     inner_dot = mp_sum_direct(inner_dot)
     partial = out_partial(gated_out, w_c, rank1, ranks)
-    inner_dot, gout, partial, w_bct_share, gc_far_back = fence(inner_dot, gout, partial, w_bct_share, gc_far_back)
+    inner_dot, gout, partial, w_bct, gc_far_back = fence(inner_dot, gout, partial, w_bct, gc_far_back)
+    c_far_got = outer_from(pair_sum(block(gc_here, n - 2), gc_far_back), n - far_k)
     out_back = rank_flip(partial[3], 1)
-    w_bct = [w_bct_share] + [rank_flip(w_bct_share, r) for r in (1, 2, 3)]
+    w_bct = [w_bct[0], rank_flip(w_bct[0], 1), w_bct[1], rank_flip(w_bct[1], 1)]
     dmixed, dgate, dgain = gate_backward(gate_pre, gout, mixed, square, inner_dot, conv_rows, channels * ranks)
     gb_own, gb_own1, gb_here, gb_send = weight_grad(normed_t, dgate, idx, sizes)
-    gc_near_back, gc_far_back, w_bct, out_back, gb_own, gb_own1, gb_here, gb_send, partial, dmixed, dgain = fence(
-        gc_near_back, gc_far_back, w_bct, out_back, gb_own, gb_own1, gb_here, gb_send, partial, dmixed, dgain
+    gc_near_back, c_far_got, w_bct, out_back, gb_own, gb_own1, gb_here, gb_send, partial, dmixed, dgain = fence(
+        gc_near_back, c_far_got, w_bct, out_back, gb_own, gb_own1, gb_here, gb_send, partial, dmixed, dgain
     )
     c_blocks = [pair_sum(block(gc_here, i), block(gc_near_back, i)) for i in range(n - 2)]
-    c_blocks.append(pair_sum(block(gc_here, n - 2), gc_far_back))
     out_far = pair_sum(partial[2], out_back)
     w_bct = join_rows(w_bct, rank1)
     c_blocks, out_far, w_bct, dmixed, gb_send = fence(c_blocks, out_far, w_bct, dmixed, gb_send)
 
-    c_got = outer_send(c_blocks, ks)
+    c_got = outer_send(c_blocks, near_ks) + [c_far_got]
     gb_back = inner_flip(gb_send)
     out_got = rank_flip(out_far, 2)
     dx, dbc, dbc_keep, dbc_send, dstep, dstep_t, dconv, dbct_part, dheads = ssd_backward(
-        rank1, x_pre, bc_pre, step_pre, *facts, mixed, dmixed, states
+        rank1, x_pre, bc_pre, step_pre, *facts, dmixed, kept
     )
     c_got, gb_back, out_got, dx, dbc, dbc_keep, dbc_send, dstep, dstep_t, dconv, dbct_part, dheads = fence(
         c_got, gb_back, out_got, dx, dbc, dbc_keep, dbc_send, dstep, dstep_t, dconv, dbct_part, dheads
@@ -1273,109 +1301,97 @@
     b_got = {far_k: outer_from(pair_sum(block(gb_here, n - 2), block(gb_back, n - 2)), n - far_k)}
     dbc_back = rank_flip(dbc_send, 1)
     out_near_back = rank_flip(partial[1], 1)
-    ga_own, ga_own1, ga_here, ga_near, ga_far = weight_grad(normed_t, dx, idx, split_sizes, us=20)
-    ga_own, ga_own1, ga_here, ga_near, ga_far, dx, dbc_back, gb_back, gb_here, out_near_back = fence(
-        ga_own, ga_own1, ga_here, ga_near, ga_far, dx, dbc_back, gb_back, gb_here, out_near_back
+    ga_own, ga_own1, ga_here, ga_send = weight_grad(normed_t, dx, idx, sizes, us=20)
+    ga_own, ga_own1, ga_here, ga_send, dx, dbc_back, gb_back, gb_here, out_near_back = fence(
+        ga_own, ga_own1, ga_here, ga_send, dx, dbc_back, gb_back, gb_here, out_near_back
     )
 
     b_near = [pair_sum(block(gb_here, i), block(gb_back, i)) for i in range(n - 2)]
     b_got.update(zip(near_ks, outer_send(b_near, near_ks)))
-    ga_far_back = inner_flip(ga_far)
+    ga_back = inner_flip(ga_send)
     dbc_pair = pair_sum(dbc_keep, dbc_back)
     dbc_got = rank_flip(dbc_pair[share:], 2)
     operands = (dx, dgate, dstep, dbc, w_a, w_b, w_s, w_bct, hidden, inv_rms, rank1, ranks)
     far_own, far_send, gain_far = normed_term(*operands, (2, 3))
-    far_own, far_send, gain_far, dx, dbc_got, dbc_pair, dstep_t, b_got[far_k], ga_near, ga_own1 = fence(
-        far_own, far_send, gain_far, dx, dbc_got, dbc_pair, dstep_t, b_got[far_k], ga_near, ga_own1
+    far_own, far_send, gain_far, dx, dbc_got, dbc_pair, dstep_t, b_got[far_k] = fence(
+        far_own, far_send, gain_far, dx, dbc_got, dbc_pair, dstep_t, b_got[far_k]
     )
     far_back = rank_flip(far_send, 1)
     operands = (dx, *operands[1:])
     near_own, near_send, gain_near = normed_term(*operands, (0, 1))
-    far_back, near_own, near_send, gain_near, ga_far_back, ga_near, b_got = fence(
-        far_back, near_own, near_send, gain_near, ga_far_back, ga_near, b_got
-    )
-    shared = mp_sum_direct(jnp.concatenate([dbct_part, gain_far + gain_near], axis=1))
+    far_back, near_own, near_send, gain_near, ga_back, b_got = fence(
+        far_back, near_own, near_send, gain_near, ga_back, b_got
+    )
     near_back = rank_flip(near_send, 1)
     far = pair_sum(far_own, far_back)
-    a_far = pair_sum(block(ga_here, n - 2), ga_far_back)
+    a_blocks = [pair_sum(block(ga_here, i), block(ga_back, i)) for i in range(n - 1)]
     dbc_share = pair_sum(dbc_pair[:share], dbc_got)
     dsmall_t = jnp.concatenate([dbc_share, dstep_t, jnp.zeros((LANES - share - 16, tokens), bf16)], axis=0)
     gs_own, gs_here, gs_send = weight_grad(normed_t, dsmall_t, idx_s, (1, n - 1, n), turned=True)
-    far, a_far, shared, near_back, gs_send, ga_near = fence(far, a_far, shared, near_back, gs_send, ga_near)
-
+    far, a_blocks, near_back, gs_send, gc_own1, gb_own1 = fence(far, a_blocks, near_back, gs_send, gc_own1, gb_own1)
+
+    early, late = near_ks[:(n - 2) // 2], near_ks[(n - 2) // 2:]
     got = rank_flip(far, 2)
-    a_got = {far_k: outer_from(a_far, n - far_k)}
-    gs_back = inner_flip(gs_send)
-    ga_near_back = inner_flip(ga_near)
-    packed = jnp.concatenate([dconv + dgain, dheads, shared], axis=1)
-    packed_got = inner_flip(packed)
+    a_got = dict(zip([far_k, *early], outer_send([a_blocks[-1], *a_blocks[:len(early)]], [far_k, *early])))
+    cut = lambda v: [v[:, i:i + LANES] for i in range(0, v.shape[1], LANES)]
+    alone = channels // LANES * 8 + 8
+    sums = jnp.concatenate([*cut(dconv + dgain), dheads, *cut(dbct_part), gain_far + gain_near], axis=0)
+    shared = (alone, sums.shape[0])
+    wide = (channels + LANES) // LANES
+    sums = pad_rows(sums, -(-sums.shape[0] // (16 * wide)) * 16 * wide).astype(bf16)
+    small_back = inner_flip(jnp.concatenate([gs_send, sums], axis=0))
+    own_got = inner_flip(jnp.concatenate([gc_own1, gb_own1], axis=1))
     near = near_own.astype(f32) + near_back.astype(f32)
-    got, near, a_got, ga_near_back, packed, packed_got, gs_back, ga_own1, gb_own1, gc_own1 = fence(
-        got, near, a_got, ga_near_back, packed, packed_got, gs_back, ga_own1, gb_own1, gc_own1
+    got, near, a_got, small_back, sums, own_got, ga_own1, a_late = fence(
+        got, near, a_got, small_back, sums, own_got, ga_own1, a_blocks[len(early):-1]
     )
 
     mine = norm_backward(near, got, hidden, cot, gain_rows, rank1)
-    mine, ga_near_back, gs_back, packed, packed_got, gc_own1, gb_own1, ga_own1 = fence(
-        mine, ga_near_back, gs_back, packed, packed_got, gc_own1, gb_own1, ga_own1
-    )
+    mine, small_back, sums, ga_own1, a_late, gs_here, out_got, out_near_back = fence(
+        mine, small_back, sums, ga_own1, a_late, gs_here, out_got, out_near_back
+    )
+    a_own_got = inner_flip(ga_own1)
+    gs_back, sums_back = small_back[:n * rows], small_back[n * rows:]
+    s_blocks = dict(zip(ks, outer_blocks(gs_own, gs_here, [gs_back[rows:]], ks)))
+    sums = pair_sum(sums, sums_back)
+    size = sums.shape[0] // wide
+    sums_wide = jnp.concatenate([sums[i * size:(i + 1) * size] for i in range(wide)], axis=1)
+    late_got = outer_send(
+        [
+            jnp.concatenate([jnp.concatenate([a_block, s_blocks[k]], axis=1), sums_wide], axis=0)
+            for k, a_block in zip(late, a_late)
+        ],
+        late,
+    )
+    s_got = outer_send([jnp.concatenate([s_blocks[k], sums], axis=0) for k in (far_k, *early)], (far_k, *early))
     mine_far = rank_flip(mine, 2)
-    own_got = inner_flip(jnp.concatenate([gc_own1, gb_own1, ga_own1], axis=1))
-    s_blocks = outer_blocks(gs_own, gs_here, [gs_back[rows:]], ks)
-    sums = packed + packed_got
-    sums = jnp.concatenate([sums[:, i:i + LANES] for i in range(0, sums.shape[1], LANES)], axis=0)
-    depth_s = -(-sums.shape[0] // 112) * 112
-    sums = pad_rows(sums, depth_s).astype(bf16)
-    wide = (channels + LANES) // LANES
-    sums_wide = jnp.concatenate([sums[i * depth_s // wide:(i + 1) * depth_s // wide] for i in range(wide)], axis=1)
-    a_blocks = [
-        jnp.concatenate(
-            [jnp.concatenate([pair_sum(block(ga_here, i), block(ga_near_back, i)), s_blocks[i]], axis=1), sums_wide], axis=0
-        )
-        for i in range(n - 2)
-    ]
-    as_got = outer_send(a_blocks, near_ks)
-    s_far_got = outer_from(jnp.concatenate([s_blocks[-1], sums], axis=0), n - far_k)
-    mine_far, as_got, s_far_got, own_got, mine, sums = fence(mine_far, as_got, s_far_got, own_got, mine, sums)
+    mine_far, mine = fence(mine_far, mine)
+    late_got, s_got, a_own_got, sums = fence(late_got, s_got, a_own_got, sums)
 
     mine_near, mine_far_near = rank_flip(mine, 1), rank_flip(mine_far, 1)
-    last = channels // LANES
-    step_m, step_w, shard_s = update_small(
-        step_weight.T, step_moment.T,
-        [(gs_own, 0), (gs_back, 0), (s_far_got, 0)] + [(got, last) for got in as_got], share,
-    )
-    bc_pieces = [shard_s] + [rank_flip(shard_s, r) for r in (1, 2, 3)]
+    step_m, step_w, exchange, totals = update_small(
+        step_weight.T, step_moment.T, sums, gs_own, gs_back, s_got, late_got,
+        (len(s_got), [n - k for k in (far_k, *early)], [n - k for k in late]), shared, share,
+    )
+    exchanged = [exchange] + [rank_flip(exchange, r) for r in (1, 2, 3)]
     in_m, in_w = update_in(
         in_weight, in_moment,
         [(gb_own, 0), (own_got, 1)] + [(b_got[k], 0) for k in ks],
-        [(ga_own, 0), (own_got, 2), (a_got[far_k], 0)] + [(got, 0) for got in as_got],
+        [(ga_own, 0), (a_own_got, 0)] + [(a_got[k], 0) for k in (far_k, *early)] + [(v, 0) for v in late_got],
     )
     input_grad = join_rows([mine, mine_near, mine_far, mine_far_near], rank1)
-    bc_m, bc_w = update_bc(bc_weight, bc_moment, bc_pieces, rank1)
-
-    def unpack(v):
-        return v.astype(f32)
-
-    found = {0: unpack(sums), far_k: unpack(s_far_got[rows:])}
-    for k, got in zip(near_ks, as_got):
-        tail = got[rows:]
-        found[n - k] = unpack(jnp.concatenate([tail[:, i:i + LANES] for i in range(0, tail.shape[1], LANES)], axis=0))
-    packed = found
-    step = n // 2
-    while step >= 1:
-        packed = {i: packed[i] + packed[i + step] for i in range(step)}
-        step //= 2
-    packed = packed[0]
-    packed = jnp.concatenate([packed[i:i + 8] for i in range(0, packed.shape[0] // 8 * 8, 8)], axis=1)
+    bc_m, bc_w, totals_shared = update_bc(bc_weight, bc_moment, exchanged, rank1)
 
     resid = lax.dynamic_slice_in_dim(hidden, rank * width, width, 1).astype(f32)
     output = (resid + partial[0].astype(f32) + out_near_back.astype(f32) + out_got.astype(f32)).astype(bf16)
     shard_c = total(gc_own, own_got[:, :channels], c_got)
 
-    cut = channels + LANES
-    total_conv = packed[:6, :channels]
-    total_head = packed[:3, channels:channels + heads]
-    total_bct = packed[:5, cut:cut + 2 * LANES]
-    total_gain = packed[0, cut + 2 * LANES:cut + 2 * LANES + depth]
+    side_by_side = lambda v: jnp.concatenate([v[i:i + 8] for i in range(0, v.shape[0], 8)], axis=1)
+    total_conv = side_by_side(totals[:alone - 8])[:6]
+    total_head = totals[alone - 8:alone - 5, :heads]
+    total_bct = side_by_side(totals_shared[:16])[:5]
+    per = TILE_D // LANES
+    total_gain = jnp.concatenate([totals_shared[i:i + per] for i in range(16, totals_shared.shape[0], 8)], axis=0).reshape(-1)
 
     out_m, out_w = advance(out_weight, out_moment, shard_c.T)
     return (

time: 296 us -> 284 us (0.959)
  Pallas kernels: 133 us -> 126 us
  starting transfers between devices: 72.5 us -> 65.8 us
    pallas_call x1, Pallas kernels: 28.3 us -> 19.9 us  [ssd_backward(): pl.pallas_call(ssd_backward_kernel, grid=(count,), in_specs=[pl.BlockSpec...]
    ppermute x32 -> x29, waiting for transfers between devices: 9.43 us -> 15.1 us  [rank_flip(): lax.ppermute(v, 'mp', [(m ^ bit, m) for m in range(lax.axis_size('mp'))])]
    ppermute x19 -> x20, waiting for transfers between devices: 40.6 us -> 35.5 us  [outer_from(): lax.ppermute(v, 'dp', [((o + k) % n * 2 + x, o * 2 + x) for o in range(n)...]
    ppermute x32 -> x29, starting transfers between devices: 18.7 us -> 15.5 us  [rank_flip(): lax.ppermute(v, 'mp', [(m ^ bit, m) for m in range(lax.axis_size('mp'))])]
    ppermute x19 -> x20, starting transfers between devices: 32 us -> 29 us  [outer_from(): lax.ppermute(v, 'dp', [((o + k) % n * 2 + x, o * 2 + x) for o in range(n)...]
    ppermute x20 -> x19, waiting for transfers between devices: 19.2 us -> 20.4 us  [inner_flip(): lax.ppermute(v, 'dp', [(d ^ 1, d) for d in range(lax.axis_size('dp'))])]
    ppermute x20 -> x19, starting transfers between devices: 21.8 us -> 21.2 us  [inner_flip(): lax.ppermute(v, 'dp', [(d ^ 1, d) for d in range(lax.axis_size('dp'))])]
  transfers between devices with their start and end apart: 71 -> 68, of which waited for: 18 -> 23; matrix products, arithmetic and copies ran while one was open for 4% -> 5% of each run, Pallas kernels for 42% -> 41%
where the time goes in v6:
time: 284 us; the launch traced here: 283 us
  Pallas kernels  126 us (44%)
  waiting for transfers between devices  71 us (25%)
  starting transfers between devices  65.8 us (23%)
  other arithmetic  11.3 us (4%)
  local copies, waits for them, and re-layouts  7.73 us (3%)
    ppermute x20, waiting for transfers between devices, outer_from(): lax.ppermute(v, 'dp', [((o + k) % n * 2 + x, o * 2 + x) for o in range(n)...  35.5 us
    ppermute x20, starting transfers between devices, outer_from(): lax.ppermute(v, 'dp', [((o + k) % n * 2 + x, o * 2 + x) for o in range(n)...  29 us
    ppermute x19, starting transfers between devices, inner_flip(): lax.ppermute(v, 'dp', [(d ^ 1, d) for d in range(lax.axis_size('dp'))])  21.2 us
    ppermute x19, waiting for transfers between devices, inner_flip(): lax.ppermute(v, 'dp', [(d ^ 1, d) for d in range(lax.axis_size('dp'))])  20.4 us
    pallas_call x1, Pallas kernels, ssd_backward(): pl.pallas_call(ssd_backward_kernel, grid=(count,), in_specs=[pl.BlockSpec...  19.9 us
    pallas_call x4, Pallas kernels, weight_grad(): pl.pallas_call(functools.partial(weight_grad_kernel, rows=rows, turned=tu...  18.8 us
    ppermute x29, starting transfers between devices, rank_flip(): lax.ppermute(v, 'mp', [(m ^ bit, m) for m in range(lax.axis_size('mp'))])  15.5 us
    ppermute x29, waiting for transfers between devices, rank_flip(): lax.ppermute(v, 'mp', [(m ^ bit, m) for m in range(lax.axis_size('mp'))])  15.1 us
  transfers between devices with their start and end apart: 68, of which 23 were waited for; matrix products, arithmetic and copies ran while one was open for 5% of the time, Pallas kernels for 41%

profile of v6, /device:TPU:0, one launch (start us, length us, event | category | flops | bytes accessed | tf_op | source)
XLA Modules:
  0.0 283.4 jit_solution(17527228769891777351)
XLA Ops:
  1.4 3.8 %pack.1 = (bf16[192,896]{1,0:T(8,128)(2,1)S(1)}, bf16[192,768]{1,0:T(8,128)(2,1)}) custom-call(s32[1]{0:T(128)} %bitcast.8.rank_ref, f32[192,2,768]{2,1,0:T(2,128)} %w_ref.2, f32[192,256]{1,0:T(8,128)} %w_ref.3, f32[12,192]{1,0:T(8,128)S(1)} %bitcast.47), custom_call_target="tpu_custom_call" | custom-call | flops 2000000000 | bytes 4000000 | tf_op jit(solution)/shard_map/pack/pallas_call | solution.py:470
  5.2 3.1 %collective-permute-start.3 = (bf16[192,896]{1,0:T(8,128)(2,1)S(1)}, bf16[192,896]{1,0:T(8,128)(2,1)}, u32[]{:S(2)}, u32[]{:S(2)}) collective-permute-start(bf16[192,896]{1,0:T(8,128)(2,1)S(1)} %get-tuple-element.309.refs_0_), channel_id=1, source_target_pairs={{24,0},{28,4},{0,8},{4,12},{8,16},{12,20},{16,24},{20,28},{25,1},{... | collective-permute-start | bytes 1032200 | tf_op jit(solution)/shard_map/ppermute | solution.py:1072
  8.3 1.5 collective-permute-start.1
  9.8 2.2 collective-permute-start
  12.0 1.5 collective-permute-start.6
  16.2 3.7 %prepare.1 = (bf16[1024,1536]{1,0:T(8,128)(2,1)}, bf16[1536,1024]{1,0:T(8,128)(2,1)}, f32[8,1024]{1,0:T(8,128)S(1)}) custom-call(bf16[1024,1536]{1,0:T(8,128)(2,1)S(1)} %copy-done.1, f32[8,1536]{1,0:T(8,128)S(1)} %pad.53.gain_ref), custom_call_target="tpu_custom_call" | custom-call | flops 12000000000 | bytes 24000000 | tf_op jit(solution)/shard_map/prepare/pallas_call | solution.py:433
  22.0 3.9 %collective-permute-done.refs_2_ = bf16[192,896]{1,0:T(8,128)(2,1)} collective-permute-done((bf16[192,896]{1,0:T(8,128)(2,1)S(1)}, bf16[192,896]{1,0:T(8,128)(2,1)}, u32[]{:S(2)}, u32[]{:S(2)}) %collective-permute-start) | collective-permute-done | bytes 344096 | tf_op jit(solution)/shard_map/ppermute | solution.py:1072
  30.1 2.0 collective-permute-done.5.refs_6_
  32.2 8.3 %collective-permute-done.2.refs_4_ = bf16[192,896]{1,0:T(8,128)(2,1)S(1)} collective-permute-done((bf16[192,896]{1,0:T(8,128)(2,1)S(1)}, bf16[192,896]{1,0:T(8,128)(2,1)S(1)}, u32[]{:S(2)}, u32[]{:S(2)}) %collective-permute-start.2) | collective-permute-done | bytes 344096 | tf_op jit(solution)/shard_map/ppermute | solution.py:1072
  40.7 1.6 collective-permute-start.9
  42.2 3.8 %collective-permute-start.7 = (bf16[192,768]{1,0:T(8,128)(2,1)S(1)}, bf16[192,768]{1,0:T(8,128)(2,1)S(1)}, u32[]{:S(2)}, u32[]{:S(2)}) collective-permute-start(bf16[192,768]{1,0:T(8,128)(2,1)S(1)} %copy-done.13), channel_id=1, source_target_pairs={{8,0},{12,4},{16,8},{20,12},{24,16},{28,20},{0,24},{4,28},{9,1},{1... | collective-permute-start | bytes 884744 | tf_op jit(solution)/shard_map/ppermute | solution.py:1072
  46.6 3.4 %join_columns.1 = (bf16[1024,1536]{1,0:T(8,128)(2,1)S(1)}, bf16[1536,1024]{1,0:T(8,128)(2,1)S(1)}) custom-call(s32[1]{0:T(128)} %bitcast.8.rank_ref, bf16[1024,384]{1,0:T(8,128)(2,1)} %refs_0_.1, bf16[1024,384]{1,0:T(8,128)(2,1)} %collective-permute-done.11.refs_1_, bf16[1024,384]{1,0:T(8,128)(2,1)} %collective-permute-done.6.refs_2_, ...), custom_call_target="tpu_custom_call" | custom-call | flops 12000000000 | bytes 24000000 | tf_op jit(solution)/shard_map/join_columns/pallas_call | solution.py:498
  50.6 3.4 %collective-permute-done.8.refs_3_ = bf16[192,768]{1,0:T(8,128)(2,1)S(1)} collective-permute-done((bf16[192,768]{1,0:T(8,128)(2,1)S(1)}, bf16[192,768]{1,0:T(8,128)(2,1)S(1)}, u32[]{:S(2)}, u32[]{:S(2)}) %collective-permute-start.8) | collective-permute-done | bytes 294944 | tf_op jit(solution)/shard_map/ppermute | solution.py:1072
  53.9 5.5 %collective-permute-done.7.refs_2_ = bf16[192,768]{1,0:T(8,128)(2,1)S(1)} collective-permute-done((bf16[192,768]{1,0:T(8,128)(2,1)S(1)}, bf16[192,768]{1,0:T(8,128)(2,1)S(1)}, u32[]{:S(2)}, u32[]{:S(2)}) %collective-permute-start.7) | collective-permute-done | bytes 294944 | tf_op jit(solution)/shard_map/ppermute | solution.py:1072
  60.0 1.5 collective-permute-start.17
  61.4 2.8 collective-permute-start.16
  64.2 3.8 %project_small.1 = (f32[128,1024]{1,0:T(8,128)S(1)}, bf16[64,1024]{1,0:T(8,128)(2,1)S(1)}, bf16[1536,128]{1,0:T(8,128)(2,1)}, bf16[64,1536]{1,0:T(8,128)(2,1)}) custom-call(s32[8]{0:T(128)S(1)} %stack.88.idx_ref, bf16[1024,1536]{1,0:T(8,128)(2,1)S(1)} %copy-done.3, bf16[192,896]{1,0:T(8,128)(2,1)S(1)} %get-tuple-element.309.refs_0_, ...), custom_call_target="tpu_custom_call" | custom-call | flops 20000000000 | bytes 40000000 | tf_op jit(solution)/shard_map/project_small/pallas_call | solution.py:577
  68.1 1.5 collective-permute-start.14
  69.6 3.4 %collective-permute-done.14.refs_2_ = bf16[64,1024]{1,0:T(8,128)(2,1)S(1)} collective-permute-done((bf16[64,1024]{1,0:T(8,128)(2,1)S(1)}, bf16[64,1024]{1,0:T(8,128)(2,1)S(1)}, u32[]{:S(2)}, u32[]{:S(2)}) %collective-permute-start.14) | collective-permute-done | bytes 131104 | tf_op jit(solution)/shard_map/ppermute | solution.py:1085
  73.0 5.7 %project.1 = (f32[1024,768]{1,0:T(8,128)}, bf16[1536,768]{1,0:T(8,128)(2,1)}) custom-call(s32[8]{0:T(128)S(1)} %stack.88.idx_ref, bf16[1024,1536]{1,0:T(8,128)(2,1)S(1)} %copy-done.3, bf16[192,896]{1,0:T(8,128)(2,1)S(1)} %get-tuple-element.309.refs_0_, bf16[192,896]{1,0:T(8,128)(2,1)} %collective-permute-done.1.refs_1_, ...), custom_call_target="tpu_custom_call" | custom-call | flops 100000000 | bytes 200000 | tf_op jit(solution)/shard_map/project/pallas_call | solution.py:613
  78.7 1.3 join_small.1
  80.4 3.5 %collective-permute-start.21 = (bf16[192,768]{1,0:T(8,128)(2,1)}, bf16[192,768]{1,0:T(8,128)(2,1)S(1)}, u32[]{:S(2)}, u32[]{:S(2)}) collective-permute-start(bf16[192,768]{1,0:T(8,128)(2,1)} %convert_bitcast_fusion.refs_0_), channel_id=1, source_target_pairs={{8,0},{12,4},{16,8},{20,12},{24,16},{28,20},{0,24},{4,28},{9,1},{1... | collective-permute-start | bytes 884744 | tf_op jit(solution)/shard_map/ppermute | solution.py:1072
  84.0 1.3 collective-permute-start.19
  86.0 14.2 %ssd_forward.1 = (f32[1024,768]{1,0:T(8,128)}, bf16[8,128,768]{2,1,0:T(8,128)(2,1)}, f32[1024,768]{1,0:T(8,128)}, bf16[1024,768]{1,0:T(8,128)(2,1)}, bf16[1024,7...) custom-call(f32[1024,768]{1,0:T(8,128)} %get-tuple-element.337.x_ref, ...), custom_call_target="tpu_custom_call" | custom-call | flops 14000000000 | bytes 40000000 | tf_op jit(solution)/shard_map/ssd_forward/pallas_call | solution.py:286
  100.3 1.4 collective-permute-start.27
  102.4 6.9 %gate_forward.1 = (f32[1024,768]{1,0:T(8,128)S(1)}, f32[8,1024]{1,0:T(8,128)S(1)}, bf16[1536,768]{1,0:T(8,128)(2,1)}) custom-call(s32[8]{0:T(128)S(1)} %stack.88.idx_ref, bf16[1024,1536]{1,0:T(8,128)(2,1)S(1)} %copy-done.3, f32[1024,768]{1,0:T(8,128)} %get-tuple-element.377.mixed_ref, bf16[192,768]{1,0:T(8,128)(2,1)S(1)} %copy-done.14, ...), custom_call_target="tpu_custom_call" | custom-call | flops 100000000 | bytes 200000 | tf_op jit(solution)/shard_map/gate_forward/pallas_call | solution.py:655
  109.3 1.5 collective-permute-start.24
  110.9 2.1 collective-permute-done.25
  116.3 1.5 collective-permute-start.30
  117.8 1.3 gated_norm.1.rhs_ref.lhs_ref
  119.1 5.3 %weight_grad.4 = (bf16[192,768]{1,0:T(8,128)(2,1)}, bf16[192,768]{1,0:T(8,128)(2,1)}, bf16[576,768]{1,0:T(8,128)(2,1)}, bf16[384,768]{1,0:T(8,128)(2,1)}, bf16[192,768]{1,0:T(8,128)(2,1)}) custom-call(s32[8]{0:T(128)S(1)} %stack.88.idx_ref, bf16[1536,1024]{1,0:T(8,128)(2,1)S(1)} %get-tuple-element.378.lhs_ref, bf16[1024,768]{1,0:T(8,128)(2,1)S(1)} %gated_norm.1.rhs_ref.lhs_ref), custom_call_target="tpu_custom_call" | custom-call | flops 100000000 | bytes 200000 | tf_op jit(solution)/shard_map/weight_grad/pallas_call | solution.py:810
  125.6 4.8 %grad_gout.1 = (f32[1024,768]{1,0:T(8,128)S(1)}, f32[8,1024]{1,0:T(8,128)S(1)}, bf16[1536,768]{1,0:T(8,128)(2,1)S(1)}) custom-call(s32[8]{0:T(128)S(1)} %stack.88.idx_ref, bf16[1024,1536]{1,0:T(8,128)(2,1)S(1)} %get-tuple-element.387.cot_ref, f32[1024,768]{1,0:T(8,128)S(1)} %get-tuple-element.376.gate_ref, f32[1024,768]{1,0:T(8,128)S(1)} %copy-done, ...), custom_call_target="tpu_custom_call" | custom-call | flops 20000000000 | bytes 40000000 | tf_op jit(solution)/shard_map/grad_gout/pallas_call | solution.py:721
  132.3 6.1 %out_partial.1 = (bf16[1024,384]{1,0:T(8,128)(2,1)}, bf16[1024,384]{1,0:T(8,128)(2,1)}, bf16[1024,384]{1,0:T(8,128)(2,1)}, bf16[1024,384]{1,0:T(8,128)(2,1)}) custom-call(s32[1]{0:T(128)} %bitcast.8.rank_ref, bf16[1024,768]{1,0:T(8,128)(2,1)S(1)} %gated_norm.1.rhs_ref.lhs_ref, bf16[1536,768]{1,0:T(8,128)(2,1)S(1)} %get-tuple-element.397.w_ref), custom_call_target="tpu_custom_call" | custom-call | flops 100000000 | bytes 200000 | tf_op jit(solution)/shard_map/out_partial/pallas_call | solution.py:840
  139.7 2.0 collective-permute-start.36
  142.4 6.1 %gate_backward.1 = (bf16[1024,768]{1,0:T(8,128)(2,1)S(1)}, bf16[1024,768]{1,0:T(8,128)(2,1)S(1)}, f32[8,768]{1,0:T(8,128)S(1)}) custom-call(f32[1024,768]{1,0:T(8,128)} %copy-done.4, f32[1024,768]{1,0:T(8,128)} %copy-done.7, f32[1024,768]{1,0:T(8,128)} %get-tuple-element.377.mixed_ref, f32[8,1024]{1,0:T(8,128)S(1)} %add_add_fusion.1.square_ref, ...), custom_call_target="tpu_custom_call" | custom-call | flops 100000000 | bytes 200000 | tf_op jit(solution)/shard_map/gate_backward/pallas_call | solution.py:772
  148.5 5.3 %weight_grad.5 = (bf16[192,768]{1,0:T(8,128)(2,1)}, bf16[192,768]{1,0:T(8,128)(2,1)}, bf16[576,768]{1,0:T(8,128)(2,1)}, bf16[576,768]{1,0:T(8,128)(2,1)}) custom-call(s32[8]{0:T(128)S(1)} %stack.88.idx_ref, bf16[1536,1024]{1,0:T(8,128)(2,1)S(1)} %copy-done.2, bf16[1024,768]{1,0:T(8,128)(2,1)S(1)} %get-tuple-element.413.rhs_ref.gg_ref), custom_call_target="tpu_custom_call" | custom-call | flops 100000000 | bytes 200000 | tf_op jit(solution)/shard_map/weight_grad/pallas_call | solution.py:810
  155.8 1.2 join_rows.2.wbt_ref
  157.9 3.8 %collective-permute-start.41 = (bf16[192,768]{1,0:T(8,128)(2,1)S(1)}, bf16[192,768]{1,0:T(8,128)(2,1)S(1)}, u32[]{:S(2)}, u32[]{:S(2)}) collective-permute-start(bf16[192,768]{1,0:T(8,128)(2,1)S(1)} %get-tuple-element.434), channel_id=1, source_target_pairs={{8,0},{12,4},{16,8},{20,12},{24,16},{28,20},{0,24},{4,28},{9,1},{1... | collective-permute-start | bytes 884744 | tf_op jit(solution)/shard_map/ppermute | solution.py:1072
  162.6 1.4 collective-permute-start.42
  164.1 19.9 %ssd_backward.1 = (bf16[1024,768]{1,0:T(8,128)(2,1)}, bf16[1024,256]{1,0:T(8,128)(2,1)}, bf16[128,1024]{1,0:T(8,128)(2,1)}, bf16[128,1024]{1,0:T(8,128)(2,1)}, b...) custom-call(s32[1]{0:T(128)} %bitcast.8.rank_ref, ...), custom_call_target="tpu_custom_call" | custom-call | flops 28000000000 | bytes 40000000 | tf_op jit(solution)/shard_map/ssd_backward/pallas_call | solution.py:325
  185.0 1.4 copy-done.8
  186.4 5.3 %weight_grad.6 = (bf16[192,768]{1,0:T(8,128)(2,1)}, bf16[192,768]{1,0:T(8,128)(2,1)}, bf16[576,768]{1,0:T(8,128)(2,1)}, bf16[576,768]{1,0:T(8,128)(2,1)}) custom-call(s32[8]{0:T(128)S(1)} %stack.88.idx_ref, bf16[1536,1024]{1,0:T(8,128)(2,1)S(1)} %copy-done.2, bf16[1024,768]{1,0:T(8,128)(2,1)S(1)} %copy-done.8), custom_call_target="tpu_custom_call" | custom-call | flops 20000000000 | bytes 40000000 | tf_op jit(solution)/shard_map/weight_grad/pallas_call | solution.py:810
  191.9 1.2 collective-permute-start.46
  193.1 1.3 collective-permute-start.49
  194.5 7.1 %normed_term.2 = (bf16[256,1536]{1,0:T(8,128)(2,1)S(1)}, bf16[256,1536]{1,0:T(8,128)(2,1)S(1)}, f32[32,128]{1,0:T(8,128)S(1)}) custom-call(s32[1]{0:T(128)} %bitcast.8.rank_ref, bf16[1024,768]{1,0:T(8,128)(2,1)S(1)} %copy-done.9, bf16[1536,768]{1,0:T(8,128)(2,1)} %get-tuple-element.469.wx_ref, bf16[1024,768]{1,0:T(8,128)(2,1)S(1)} %get-tuple-element.413.rhs_ref.gg_ref, ...), custom_call_target="tpu_custom_call" | custom-call | flops 20000000000 | bytes 40000000 | tf_op jit(solution)/shard_map/normed_term/pallas_call | solution.py:879
  202.8 1.2 collective-permute-start.50
  204.0 7.2 %normed_term.3 = (bf16[256,1536]{1,0:T(8,128)(2,1)S(1)}, bf16[256,1536]{1,0:T(8,128)(2,1)S(1)}, f32[32,128]{1,0:T(8,128)S(1)}) custom-call(s32[1]{0:T(128)} %bitcast.8.rank_ref, bf16[1024,768]{1,0:T(8,128)(2,1)S(1)} %copy-done.9, bf16[1536,768]{1,0:T(8,128)(2,1)} %get-tuple-element.469.wx_ref, bf16[1024,768]{1,0:T(8,128)(2,1)S(1)} %get-tuple-element.413.rhs_ref.gg_ref, ...), custom_call_target="tpu_custom_call" | custom-call | flops 100000000 | bytes 200000 | tf_op jit(solution)/shard_map/normed_term/pallas_call | solution.py:879
  211.3 2.9 %weight_grad.7 = (bf16[192,128]{1,0:T(8,128)(2,1)}, bf16[576,128]{1,0:T(8,128)(2,1)}, bf16[768,128]{1,0:T(8,128)(2,1)}) custom-call(s32[8]{0:T(128)S(1)} %stack.102.idx_ref, bf16[1536,1024]{1,0:T(8,128)(2,1)S(1)} %copy-done.2, bf16[128,1024]{1,0:T(8,128)(2,1)S(1)} %maximum_maximum_fusion.rhs_ref), custom_call_target="tpu_custom_call" | custom-call | flops 100000000 | bytes 200000 | tf_op jit(solution)/shard_map/weight_grad/pallas_call | solution.py:810
  214.1 5.9 %collective-permute-done.50.refs_2_ = bf16[192,768]{1,0:T(8,128)(2,1)S(1)} collective-permute-done((bf16[192,768]{1,0:T(8,128)(2,1)S(1)}, bf16[192,768]{1,0:T(8,128)(2,1)S(1)}, u32[]{:S(2)}, u32[]{:S(2)}) %collective-permute-start.50) | collective-permute-done | bytes 294944 | tf_op jit(solution)/shard_map/ppermute | solution.py:1072
  220.6 1.8 collective-permute-done.52
  224.1 1.4 collective-permute-start.56
  226.8 16.5 %collective-permute-done.56 = bf16[880,128]{1,0:T(8,128)(2,1)S(1)} collective-permute-done((bf16[880,128]{1,0:T(8,128)(2,1)S(1)}, bf16[880,128]{1,0:T(8,128)(2,1)S(1)}, u32[]{:S(2)}, u32[]{:S(2)}) %collective-permute-start.56) | collective-permute-done | bytes 225312 | tf_op jit(solution)/shard_map/ppermute | solution.py:1081
  243.3 4.0 %collective-permute-done.55.refs_7_ = bf16[192,768]{1,0:T(8,128)(2,1)S(1)} collective-permute-done((bf16[192,768]{1,0:T(8,128)(2,1)S(1)}, bf16[192,768]{1,0:T(8,128)(2,1)S(1)}, u32[]{:S(2)}, u32[]{:S(2)}) %collective-permute-start.55) | collective-permute-done | bytes 294944 | tf_op jit(solution)/shard_map/ppermute | solution.py:1072
  247.2 2.2 norm_backward.1.refs_0_
  249.8 1.3 collective-permute-start.64
  251.2 3.1 %collective-permute-start.61 = (bf16[208,896]{1,0:T(8,128)(2,1)S(1)}, bf16[208,896]{1,0:T(8,128)(2,1)S(1)}, u32[]{:S(2)}, u32[]{:S(2)}) collective-permute-start(bf16[208,896]{1,0:T(8,128)(2,1)S(1)} %pad_maximum_fusion.1), channel_id=1, source_target_pairs={{8,0},{12,4},{16,8},{20,12},{24,16},{28,20},{0,24},{4,28},{9,1},{1... | collective-permute-start | bytes 1118216 | tf_op jit(solution)/shard_map/ppermute | solution.py:1072
  255.5 2.1 multiply_subtract_fusion
  257.6 2.4 add_convert_fusion
  260.9 2.7 collective-permute-done.61.refs_9_.refs_2_
  264.4 1.2 collective-permute-start.66
  266.3 4.6 %update_in.1 = (f32[192,2,768]{2,1,0:T(2,128)}, f32[192,2,768]{2,1,0:T(2,128)}) custom-call(f32[192,2,768]{2,1,0:T(2,128)} %w_ref.2, f32[192,2,768]{2,1,0:T(2,128)} %m_ref.2, bf16[192,768]{1,0:T(8,128)(2,1)S(1)} %copy-done.15, bf16[192,1536]{1,0:T(8,128)(2,1)S(1)} %collective-permute-done.57.refs_1_, bf16[192,768]{1,0:T(8,128)(2,1)S(1)} %collective-permute-done.50.refs_2_, ...), custom_call_target="tpu_custom_call" | custom-call | flops 100000000 | bytes 200000 | tf_op jit(solution)/shard_map/update_in/pallas_call | solution.py:967
  272.2 2.4 collective-permute-done.67.refs_3_
  274.6 2.6 collective-permute-done.66.refs_2_
  281.6 1.9 join_rows.3
  (316 shorter events, 40.2 us)
Async XLA Ops:
  5.2 15.9 %collective-permute-start.3 = (bf16[192,896]{1,0:T(8,128)(2,1)S(1)}, bf16[192,896]{1,0:T(8,128)(2,1)}, u32[]{:S(2)}, u32[]{:S(2)}) collective-permute-start(bf16[192,896]{1,0:T(8,128)(2,1)S(1)} %get-tuple-element.309.refs_0_), channel_id=1, source_target_pairs={{24,0},{28,4},{0,8},{4,12},{8,16},{12,20},{16,24},{20,28},{25,1},{... | collective-permute-start | bytes 1032200 | tf_op jit(solution)/shard_map/ppermute | solution.py:1072
  8.3 11.9 %collective-permute-start.1 = (bf16[192,896]{1,0:T(8,128)(2,1)S(1)}, bf16[192,896]{1,0:T(8,128)(2,1)}, u32[]{:S(2)}, u32[]{:S(2)}) collective-permute-start(bf16[192,896]{1,0:T(8,128)(2,1)S(1)} %get-tuple-element.309.refs_0_), channel_id=1, source_target_pairs={{4,0},{0,4},{12,8},{8,12},{20,16},{16,20},{28,24},{24,28},{5,1},{1... | collective-permute-start | bytes 1032200 | tf_op jit(solution)/shard_map/ppermute | solution.py:1081
  9.8 16.1 %collective-permute-start = (bf16[192,896]{1,0:T(8,128)(2,1)S(1)}, bf16[192,896]{1,0:T(8,128)(2,1)}, u32[]{:S(2)}, u32[]{:S(2)}) collective-permute-start(bf16[192,896]{1,0:T(8,128)(2,1)S(1)} %get-tuple-element.309.refs_0_), channel_id=1, source_target_pairs={{8,0},{12,4},{16,8},{20,12},{24,16},{28,20},{0,24},{4,28},{9,1},{1... | collective-permute-start | bytes 1032200 | tf_op jit(solution)/shard_map/ppermute | solution.py:1072
  12.0 28.5 %collective-permute-start.6 = (bf16[1024,384]{1,0:T(8,128)(2,1)}, bf16[1024,384]{1,0:T(8,128)(2,1)}, u32[]{:S(2)}, u32[]{:S(2)}) collective-permute-start(bf16[1024,384]{1,0:T(8,128)(2,1)} %refs_0_.1), channel_id=1, source_target_pairs={{2,0},{3,1},{0,2},{1,3},{6,4},{7,5},{4,6},{5,7},{10,8},{11,9},{8,1... | collective-permute-start | bytes 2359304 | tf_op jit(solution)/shard_map/ppermute | solution.py:1085
  13.5 32.5 %collective-permute-start.11 = (bf16[1024,384]{1,0:T(8,128)(2,1)}, bf16[1024,384]{1,0:T(8,128)(2,1)}, u32[]{:S(2)}, u32[]{:S(2)}) collective-permute-start(bf16[1024,384]{1,0:T(8,128)(2,1)} %refs_0_.1), channel_id=1, source_target_pairs={{1,0},{0,1},{3,2},{2,3},{5,4},{4,5},{7,6},{6,7},{9,8},{8,9},{11,10... | collective-permute-start | bytes 2359304 | tf_op jit(solution)/shard_map/ppermute | solution.py:1085
  20.2 20.3 %collective-permute-start.2 = (bf16[192,896]{1,0:T(8,128)(2,1)S(1)}, bf16[192,896]{1,0:T(8,128)(2,1)S(1)}, u32[]{:S(2)}, u32[]{:S(2)}) collective-permute-start(bf16[192,896]{1,0:T(8,128)(2,1)S(1)} %get-tuple-element.309.refs_0_), channel_id=1, source_target_pairs={{16,0},{20,4},{24,8},{28,12},{0,16},{4,20},{8,24},{12,28},{17,1},{... | collective-permute-start | bytes 1032200 | tf_op jit(solution)/shard_map/ppermute | solution.py:1072
  21.1 11.1 %collective-permute-start.5 = (bf16[192,896]{1,0:T(8,128)(2,1)}, bf16[192,896]{1,0:T(8,128)(2,1)S(1)}, u32[]{:S(2)}, u32[]{:S(2)}) collective-permute-start(bf16[192,896]{1,0:T(8,128)(2,1)} %collective-permute-done.3.refs_3_), channel_id=1, source_target_pairs={{4,0},{0,4},{12,8},{8,12},{20,16},{16,20},{28,24},{24,28},{5,1},{1... | collective-permute-start | bytes 1032200 | tf_op jit(solution)/shard_map/ppermute | solution.py:1081
  25.8 14.6 %collective-permute-start.4 = (bf16[192,896]{1,0:T(8,128)(2,1)}, bf16[192,896]{1,0:T(8,128)(2,1)S(1)}, u32[]{:S(2)}, u32[]{:S(2)}) collective-permute-start(bf16[192,896]{1,0:T(8,128)(2,1)} %collective-permute-done.refs_2_), channel_id=1, source_target_pairs={{4,0},{0,4},{12,8},{8,12},{20,16},{16,20},{28,24},{24,28},{5,1},{1... | collective-permute-start | bytes 1032200 | tf_op jit(solution)/shard_map/ppermute | solution.py:1081
  40.5 6.1 %collective-permute-start.12 = (bf16[1024,384]{1,0:T(8,128)(2,1)}, bf16[1024,384]{1,0:T(8,128)(2,1)S(1)}, u32[]{:S(2)}, u32[]{:S(2)}) collective-permute-start(bf16[1024,384]{1,0:T(8,128)(2,1)} %collective-permute-done.6.refs_2_), channel_id=1, source_target_pairs={{1,0},{0,1},{3,2},{2,3},{5,4},{4,5},{7,6},{6,7},{9,8},{8,9},{11,10... | collective-permute-start | bytes 2359304 | tf_op jit(solution)/shard_map/ppermute | solution.py:1085
  40.7 9.9 %collective-permute-start.9 = (bf16[192,768]{1,0:T(8,128)(2,1)S(1)}, bf16[192,768]{1,0:T(8,128)(2,1)S(1)}, u32[]{:S(2)}, u32[]{:S(2)}) collective-permute-start(bf16[192,768]{1,0:T(8,128)(2,1)S(1)} %copy-done.13), channel_id=1, source_target_pairs={{4,0},{0,4},{12,8},{8,12},{20,16},{16,20},{28,24},{24,28},{5,1},{1... | collective-permute-start | bytes 884744 | tf_op jit(solution)/shard_map/ppermute | solution.py:1081
  42.2 11.7 %collective-permute-start.8 = (bf16[192,768]{1,0:T(8,128)(2,1)S(1)}, bf16[192,768]{1,0:T(8,128)(2,1)S(1)}, u32[]{:S(2)}, u32[]{:S(2)}) collective-permute-start(bf16[192,768]{1,0:T(8,128)(2,1)S(1)} %copy-done.13), channel_id=1, source_target_pairs={{24,0},{28,4},{0,8},{4,12},{8,16},{12,20},{16,24},{20,28},{25,1},{... | collective-permute-start | bytes 884744 | tf_op jit(solution)/shard_map/ppermute | solution.py:1072
  42.2 17.2 %collective-permute-start.7 = (bf16[192,768]{1,0:T(8,128)(2,1)S(1)}, bf16[192,768]{1,0:T(8,128)(2,1)S(1)}, u32[]{:S(2)}, u32[]{:S(2)}) collective-permute-start(bf16[192,768]{1,0:T(8,128)(2,1)S(1)} %copy-done.13), channel_id=1, source_target_pairs={{8,0},{12,4},{16,8},{20,12},{24,16},{28,20},{0,24},{4,28},{9,1},{1... | collective-permute-start | bytes 884744 | tf_op jit(solution)/shard_map/ppermute | solution.py:1072
  46.1 13.4 %collective-permute-start.10 = (bf16[192,896]{1,0:T(8,128)(2,1)S(1)}, bf16[192,896]{1,0:T(8,128)(2,1)S(1)}, u32[]{:S(2)}, u32[]{:S(2)}) collective-permute-start(bf16[192,896]{1,0:T(8,128)(2,1)S(1)} %collective-permute-done.2.refs_4_), channel_id=1, source_target_pairs={{4,0},{0,4},{12,8},{8,12},{20,16},{16,20},{28,24},{24,28},{5,1},{1... | collective-permute-start | bytes 1032200 | tf_op jit(solution)/shard_map/ppermute | solution.py:1081
  59.4 20.6 %collective-permute-start.18 = (bf16[192,768]{1,0:T(8,128)(2,1)}, bf16[192,768]{1,0:T(8,128)(2,1)S(1)}, u32[]{:S(2)}, u32[]{:S(2)}) collective-permute-start(bf16[192,768]{1,0:T(8,128)(2,1)} %convert_bitcast_fusion.refs_0_), channel_id=1, source_target_pairs={{4,0},{0,4},{12,8},{8,12},{20,16},{16,20},{28,24},{24,28},{5,1},{1... | collective-permute-start | bytes 884744 | tf_op jit(solution)/shard_map/ppermute | solution.py:1081
  60.0 20.1 %collective-permute-start.17 = (bf16[192,768]{1,0:T(8,128)(2,1)S(1)}, bf16[192,768]{1,0:T(8,128)(2,1)S(1)}, u32[]{:S(2)}, u32[]{:S(2)}) collective-permute-start(bf16[192,768]{1,0:T(8,128)(2,1)S(1)} %collective-permute-done.7.refs_2_), channel_id=1, source_target_pairs={{4,0},{0,4},{12,8},{8,12},{20,16},{16,20},{28,24},{24,28},{5,1},{1... | collective-permute-start | bytes 884744 | tf_op jit(solution)/shard_map/ppermute | solution.py:1081
  61.4 18.6 %collective-permute-start.16 = (bf16[192,768]{1,0:T(8,128)(2,1)S(1)}, bf16[192,768]{1,0:T(8,128)(2,1)S(1)}, u32[]{:S(2)}, u32[]{:S(2)}) collective-permute-start(bf16[192,768]{1,0:T(8,128)(2,1)S(1)} %copy-done.13), channel_id=1, source_target_pairs={{16,0},{20,4},{24,8},{28,12},{0,16},{4,20},{8,24},{12,28},{17,1},{... | collective-permute-start | bytes 884744 | tf_op jit(solution)/shard_map/ppermute | solution.py:1072
  68.1 5.0 %collective-permute-start.14 = (bf16[64,1024]{1,0:T(8,128)(2,1)S(1)}, bf16[64,1024]{1,0:T(8,128)(2,1)S(1)}, u32[]{:S(2)}, u32[]{:S(2)}) collective-permute-start(bf16[64,1024]{1,0:T(8,128)(2,1)S(1)} %get-tuple-element.329.refs_0_), channel_id=1, source_target_pairs={{2,0},{3,1},{0,2},{1,3},{6,4},{7,5},{4,6},{5,7},{10,8},{11,9},{8,1... | collective-permute-start | bytes 393224 | tf_op jit(solution)/shard_map/ppermute | solution.py:1085
  69.6 9.1 %collective-permute-start.13 = (bf16[64,1024]{1,0:T(8,128)(2,1)S(1)}, bf16[64,1024]{1,0:T(8,128)(2,1)S(1)}, u32[]{:S(2)}, u32[]{:S(2)}) collective-permute-start(bf16[64,1024]{1,0:T(8,128)(2,1)S(1)} %get-tuple-element.329.refs_0_), channel_id=1, source_target_pairs={{1,0},{0,1},{3,2},{2,3},{5,4},{4,5},{7,6},{6,7},{9,8},{8,9},{11,10... | collective-permute-start | bytes 393224 | tf_op jit(solution)/shard_map/ppermute | solution.py:1085
  73.0 5.7 %collective-permute-start.15 = (bf16[64,1024]{1,0:T(8,128)(2,1)S(1)}, bf16[64,1024]{1,0:T(8,128)(2,1)S(1)}, u32[]{:S(2)}, u32[]{:S(2)}) collective-permute-start(bf16[64,1024]{1,0:T(8,128)(2,1)S(1)} %collective-permute-done.14.refs_2_), channel_id=1, source_target_pairs={{1,0},{0,1},{3,2},{2,3},{5,4},{4,5},{7,6},{6,7},{9,8},{8,9},{11,10... | collective-permute-start | bytes 393224 | tf_op jit(solution)/shard_map/ppermute | solution.py:1085
  80.1 20.1 %collective-permute-start.22 = (bf16[192,768]{1,0:T(8,128)(2,1)}, bf16[192,768]{1,0:T(8,128)(2,1)S(1)}, u32[]{:S(2)}, u32[]{:S(2)}) collective-permute-start(bf16[192,768]{1,0:T(8,128)(2,1)} %convert_bitcast_fusion.refs_0_), channel_id=1, source_target_pairs={{24,0},{28,4},{0,8},{4,12},{8,16},{12,20},{16,24},{20,28},{25,1},{... | collective-permute-start | bytes 884744 | tf_op jit(solution)/shard_map/ppermute | solution.py:1072
  80.4 19.8 %collective-permute-start.21 = (bf16[192,768]{1,0:T(8,128)(2,1)}, bf16[192,768]{1,0:T(8,128)(2,1)S(1)}, u32[]{:S(2)}, u32[]{:S(2)}) collective-permute-start(bf16[192,768]{1,0:T(8,128)(2,1)} %convert_bitcast_fusion.refs_0_), channel_id=1, source_target_pairs={{8,0},{12,4},{16,8},{20,12},{24,16},{28,20},{0,24},{4,28},{9,1},{1... | collective-permute-start | bytes 884744 | tf_op jit(solution)/shard_map/ppermute | solution.py:1072
  84.0 16.2 %collective-permute-start.19 = (bf16[192,768]{1,0:T(8,128)(2,1)S(1)}, bf16[192,768]{1,0:T(8,128)(2,1)S(1)}, u32[]{:S(2)}, u32[]{:S(2)}) collective-permute-start(bf16[192,768]{1,0:T(8,128)(2,1)S(1)} %collective-permute-done.16.refs_4_), channel_id=1, source_target_pairs={{4,0},{0,4},{12,8},{8,12},{20,16},{16,20},{28,24},{24,28},{5,1},{1... | collective-permute-start | bytes 884744 | tf_op jit(solution)/shard_map/ppermute | solution.py:1081
  85.3 14.9 %collective-permute-start.20 = (bf16[192,768]{1,0:T(8,128)(2,1)S(1)}, bf16[192,768]{1,0:T(8,128)(2,1)S(1)}, u32[]{:S(2)}, u32[]{:S(2)}) collective-permute-start(bf16[192,768]{1,0:T(8,128)(2,1)S(1)} %collective-permute-done.8.refs_3_), channel_id=1, source_target_pairs={{4,0},{0,4},{12,8},{8,12},{20,16},{16,20},{28,24},{24,28},{5,1},{1... | collective-permute-start | bytes 884744 | tf_op jit(solution)/shard_map/ppermute | solution.py:1081
  100.3 13.9 %collective-permute-start.27 = (bf16[192,768]{1,0:T(8,128)(2,1)S(1)}, bf16[192,768]{1,0:T(8,128)(2,1)S(1)}, u32[]{:S(2)}, u32[]{:S(2)}) collective-permute-start(bf16[192,768]{1,0:T(8,128)(2,1)S(1)} %collective-permute-done.21.refs_2_), channel_id=1, source_target_pairs={{4,0},{0,4},{12,8},{8,12},{20,16},{16,20},{28,24},{24,28},{5,1},{1... | collective-permute-start | bytes 884744 | tf_op jit(solution)/shard_map/ppermute | solution.py:1081
  101.7 13.6 %collective-permute-start.26 = (bf16[192,768]{1,0:T(8,128)(2,1)}, bf16[192,768]{1,0:T(8,128)(2,1)S(1)}, u32[]{:S(2)}, u32[]{:S(2)}) collective-permute-start(bf16[192,768]{1,0:T(8,128)(2,1)} %convert_bitcast_fusion.refs_0_), channel_id=1, source_target_pairs={{16,0},{20,4},{24,8},{28,12},{0,16},{4,20},{8,24},{12,28},{17,1},{... | collective-permute-start | bytes 884744 | tf_op jit(solution)/shard_map/ppermute | solution.py:1072
  101.7 13.6 %collective-permute-start.28 = (bf16[192,768]{1,0:T(8,128)(2,1)S(1)}, bf16[192,768]{1,0:T(8,128)(2,1)S(1)}, u32[]{:S(2)}, u32[]{:S(2)}) collective-permute-start(bf16[192,768]{1,0:T(8,128)(2,1)S(1)} %collective-permute-done.22.refs_3_), channel_id=1, source_target_pairs={{4,0},{0,4},{12,8},{8,12},{20,16},{16,20},{28,24},{24,28},{5,1},{1... | collective-permute-start | bytes 884744 | tf_op jit(solution)/shard_map/ppermute | solution.py:1081
  109.3 3.6 %collective-permute-start.25 = (f32[8,1024]{1,0:T(8,128)S(1)}, f32[8,1024]{1,0:T(8,128)S(1)}, u32[]{:S(2)}, u32[]{:S(2)}) collective-permute-start(f32[8,1024]{1,0:T(8,128)S(1)} %get-tuple-element.364), channel_id=1, source_target_pairs={{3,0},{2,1},{1,2},{0,3},{7,4},{6,5},{5,6},{4,7},{11,8},{10,9},{9,1... | collective-permute-start | bytes 98312 | tf_op jit(solution)/shard_map/ppermute | solution.py:1085
  109.3 4.0 %collective-permute-start.24 = (f32[8,1024]{1,0:T(8,128)S(1)}, f32[8,1024]{1,0:T(8,128)S(1)}, u32[]{:S(2)}, u32[]{:S(2)}) collective-permute-start(f32[8,1024]{1,0:T(8,128)S(1)} %get-tuple-element.364), channel_id=1, source_target_pairs={{2,0},{3,1},{0,2},{1,3},{6,4},{7,5},{4,6},{5,7},{10,8},{11,9},{8,1... | collective-permute-start | bytes 98312 | tf_op jit(solution)/shard_map/ppermute | solution.py:1085
  115.3 9.2 %collective-permute-start.29 = (bf16[192,768]{1,0:T(8,128)(2,1)S(1)}, bf16[192,768]{1,0:T(8,128)(2,1)S(1)}, u32[]{:S(2)}, u32[]{:S(2)}) collective-permute-start(bf16[192,768]{1,0:T(8,128)(2,1)S(1)} %collective-permute-done.26.refs_4_), channel_id=1, source_target_pairs={{4,0},{0,4},{12,8},{8,12},{20,16},{16,20},{28,24},{24,28},{5,1},{1... | collective-permute-start | bytes 884744 | tf_op jit(solution)/shard_map/ppermute | solution.py:1081
  116.3 8.2 %collective-permute-start.30 = (bf16[64,1536]{1,0:T(8,128)(2,1)}, bf16[64,1536]{1,0:T(8,128)(2,1)S(1)}, u32[]{:S(2)}, u32[]{:S(2)}) collective-permute-start(bf16[64,1536]{1,0:T(8,128)(2,1)} %get-tuple-element.427.refs_0_), channel_id=1, source_target_pairs={{2,0},{3,1},{0,2},{1,3},{6,4},{7,5},{4,6},{5,7},{10,8},{11,9},{8,1... | collective-permute-start | bytes 589832 | tf_op jit(solution)/shard_map/ppermute | solution.py:1085
  124.5 14.0 %collective-permute-start.35 = (bf16[192,768]{1,0:T(8,128)(2,1)}, bf16[192,768]{1,0:T(8,128)(2,1)S(1)}, u32[]{:S(2)}, u32[]{:S(2)}) collective-permute-start(bf16[192,768]{1,0:T(8,128)(2,1)} %get-tuple-element.404), channel_id=1, source_target_pairs={{4,0},{0,4},{12,8},{8,12},{20,16},{16,20},{28,24},{24,28},{5,1},{1... | collective-permute-start | bytes 884744 | tf_op jit(solution)/shard_map/ppermute | solution.py:1081
  130.4 8.0 %collective-permute-start.34 = (f32[8,1024]{1,0:T(8,128)S(1)}, f32[8,1024]{1,0:T(8,128)S(1)}, u32[]{:S(2)}, u32[]{:S(2)}) collective-permute-start(f32[8,1024]{1,0:T(8,128)S(1)} %get-tuple-element.394), channel_id=1, source_target_pairs={{3,0},{2,1},{1,2},{0,3},{7,4},{6,5},{5,6},{4,7},{11,8},{10,9},{9,1... | collective-permute-start | bytes 98312 | tf_op jit(solution)/shard_map/ppermute | solution.py:1085
  130.5 8.0 %collective-permute-start.33 = (f32[8,1024]{1,0:T(8,128)S(1)}, f32[8,1024]{1,0:T(8,128)S(1)}, u32[]{:S(2)}, u32[]{:S(2)}) collective-permute-start(f32[8,1024]{1,0:T(8,128)S(1)} %get-tuple-element.394), channel_id=1, source_target_pairs={{2,0},{3,1},{0,2},{1,3},{6,4},{7,5},{4,6},{5,7},{10,8},{11,9},{8,1... | collective-permute-start | bytes 98312 | tf_op jit(solution)/shard_map/ppermute | solution.py:1085
  131.4 7.0 %collective-permute-start.32 = (f32[8,1024]{1,0:T(8,128)S(1)}, f32[8,1024]{1,0:T(8,128)S(1)}, u32[]{:S(2)}, u32[]{:S(2)}) collective-permute-start(f32[8,1024]{1,0:T(8,128)S(1)} %get-tuple-element.394), channel_id=1, source_target_pairs={{1,0},{0,1},{3,2},{2,3},{5,4},{4,5},{7,6},{6,7},{9,8},{8,9},{11,10... | collective-permute-start | bytes 98312 | tf_op jit(solution)/shard_map/ppermute | solution.py:1085
  138.5 16.9 %collective-permute-start.39 = (bf16[1024,384]{1,0:T(8,128)(2,1)}, bf16[1024,384]{1,0:T(8,128)(2,1)S(1)}, u32[]{:S(2)}, u32[]{:S(2)}) collective-permute-start(bf16[1024,384]{1,0:T(8,128)(2,1)} %get-tuple-element.408), channel_id=1, source_target_pairs={{1,0},{0,1},{3,2},{2,3},{5,4},{4,5},{7,6},{6,7},{9,8},{8,9},{11,10... | collective-permute-start | bytes 2359304 | tf_op jit(solution)/shard_map/ppermute | solution.py:1085
  138.6 16.0 %collective-permute-start.31 = (bf16[384,768]{1,0:T(8,128)(2,1)}, bf16[384,768]{1,0:T(8,128)(2,1)S(1)}, u32[]{:S(2)}, u32[]{:S(2)}) collective-permute-start(bf16[384,768]{1,0:T(8,128)(2,1)} %get-tuple-element.385), channel_id=1, source_target_pairs={{4,0},{0,4},{12,8},{8,12},{20,16},{16,20},{28,24},{24,28},{5,1},{1... | collective-permute-start | bytes 1769480 | tf_op jit(solution)/shard_map/ppermute | solution.py:1081
  139.7 15.7 %collective-permute-start.36 = (bf16[192,768]{1,0:T(8,128)(2,1)S(1)}, bf16[192,768]{1,0:T(8,128)(2,1)}, u32[]{:S(2)}, u32[]{:S(2)}) collective-permute-start(bf16[192,768]{1,0:T(8,128)(2,1)S(1)} %add_convert_fusion.11), channel_id=1, source_target_pairs={{16,0},{20,4},{24,8},{28,12},{0,16},{4,20},{8,24},{12,28},{17,1},{... | collective-permute-start | bytes 884744 | tf_op jit(solution)/shard_map/ppermute | solution.py:1072
  141.7 12.1 %collective-permute-start.37 = (bf16[64,1536]{1,0:T(8,128)(2,1)}, bf16[64,1536]{1,0:T(8,128)(2,1)S(1)}, u32[]{:S(2)}, u32[]{:S(2)}) collective-permute-start(bf16[64,1536]{1,0:T(8,128)(2,1)} %get-tuple-element.427.refs_0_), channel_id=1, source_target_pairs={{1,0},{0,1},{3,2},{2,3},{5,4},{4,5},{7,6},{6,7},{9,8},{8,9},{11,10... | collective-permute-start | bytes 589832 | tf_op jit(solution)/shard_map/ppermute | solution.py:1085
  141.7 12.1 %collective-permute-start.38 = (bf16[64,1536]{1,0:T(8,128)(2,1)S(1)}, bf16[64,1536]{1,0:T(8,128)(2,1)S(1)}, u32[]{:S(2)}, u32[]{:S(2)}) collective-permute-start(bf16[64,1536]{1,0:T(8,128)(2,1)S(1)} %collective-permute-done.30.refs_2_), channel_id=1, source_target_pairs={{1,0},{0,1},{3,2},{2,3},{5,4},{4,5},{7,6},{6,7},{9,8},{8,9},{11,10... | collective-permute-start | bytes 589832 | tf_op jit(solution)/shard_map/ppermute | solution.py:1085
  157.9 26.1 %collective-permute-start.40 = (bf16[192,768]{1,0:T(8,128)(2,1)S(1)}, bf16[192,768]{1,0:T(8,128)(2,1)S(1)}, u32[]{:S(2)}, u32[]{:S(2)}) collective-permute-start(bf16[192,768]{1,0:T(8,128)(2,1)S(1)} %get-tuple-element.433), channel_id=1, source_target_pairs={{24,0},{28,4},{0,8},{4,12},{8,16},{12,20},{16,24},{20,28},{25,1},{... | collective-permute-start | bytes 884744 | tf_op jit(solution)/shard_map/ppermute | solution.py:1072
  157.9 26.1 %collective-permute-start.41 = (bf16[192,768]{1,0:T(8,128)(2,1)S(1)}, bf16[192,768]{1,0:T(8,128)(2,1)S(1)}, u32[]{:S(2)}, u32[]{:S(2)}) collective-permute-start(bf16[192,768]{1,0:T(8,128)(2,1)S(1)} %get-tuple-element.434), channel_id=1, source_target_pairs={{8,0},{12,4},{16,8},{20,12},{24,16},{28,20},{0,24},{4,28},{9,1},{1... | collective-permute-start | bytes 884744 | tf_op jit(solution)/shard_map/ppermute | solution.py:1072
  161.8 22.3 %collective-permute-start.43 = (bf16[1024,384]{1,0:T(8,128)(2,1)S(1)}, bf16[1024,384]{1,0:T(8,128)(2,1)S(1)}, u32[]{:S(2)}, u32[]{:S(2)}) collective-permute-start(bf16[1024,384]{1,0:T(8,128)(2,1)S(1)} %add_convert_fusion.2), channel_id=1, source_target_pairs={{2,0},{3,1},{0,2},{1,3},{6,4},{7,5},{4,6},{5,7},{10,8},{11,9},{8,1... | collective-permute-start | bytes 2359304 | tf_op jit(solution)/shard_map/ppermute | solution.py:1085
  162.6 29.1 %collective-permute-start.45 = (bf16[1024,384]{1,0:T(8,128)(2,1)S(1)}, bf16[1024,384]{1,0:T(8,128)(2,1)S(1)}, u32[]{:S(2)}, u32[]{:S(2)}) collective-permute-start(bf16[1024,384]{1,0:T(8,128)(2,1)S(1)} %copy-done.65), channel_id=1, source_target_pairs={{1,0},{0,1},{3,2},{2,3},{5,4},{4,5},{7,6},{6,7},{9,8},{8,9},{11,10... | collective-permute-start | bytes 2359304 | tf_op jit(solution)/shard_map/ppermute | solution.py:1085
  162.6 22.1 %collective-permute-start.42 = (bf16[576,768]{1,0:T(8,128)(2,1)S(1)}, bf16[576,768]{1,0:T(8,128)(2,1)S(1)}, u32[]{:S(2)}, u32[]{:S(2)}) collective-permute-start(bf16[576,768]{1,0:T(8,128)(2,1)S(1)} %copy-done.64), channel_id=1, source_target_pairs={{4,0},{0,4},{12,8},{8,12},{20,16},{16,20},{28,24},{24,28},{5,1},{1... | collective-permute-start | bytes 2654216 | tf_op jit(solution)/shard_map/ppermute | solution.py:1081
  184.7 7.0 %collective-permute-start.44 = (bf16[128,1024]{1,0:T(8,128)(2,1)}, bf16[128,1024]{1,0:T(8,128)(2,1)S(1)}, u32[]{:S(2)}, u32[]{:S(2)}) collective-permute-start(bf16[128,1024]{1,0:T(8,128)(2,1)} %get-tuple-element.464), channel_id=1, source_target_pairs={{1,0},{0,1},{3,2},{2,3},{5,4},{4,5},{7,6},{6,7},{9,8},{8,9},{11,10... | collective-permute-start | bytes 786440 | tf_op jit(solution)/shard_map/ppermute | solution.py:1085
  184.9 16.7 %collective-permute-start.47 = (bf16[192,768]{1,0:T(8,128)(2,1)S(1)}, bf16[192,768]{1,0:T(8,128)(2,1)S(1)}, u32[]{:S(2)}, u32[]{:S(2)}) collective-permute-start(bf16[192,768]{1,0:T(8,128)(2,1)S(1)} %add_convert_fusion.8), channel_id=1, source_target_pairs={{16,0},{20,4},{24,8},{28,12},{0,16},{4,20},{8,24},{12,28},{17,1},{... | collective-permute-start | bytes 884744 | tf_op jit(solution)/shard_map/ppermute | solution.py:1072
  191.9 9.7 %collective-permute-start.46 = (bf16[64,1024]{1,0:T(8,128)(2,1)S(1)}, bf16[64,1024]{1,0:T(8,128)(2,1)S(1)}, u32[]{:S(2)}, u32[]{:S(2)}) collective-permute-start(bf16[64,1024]{1,0:T(8,128)(2,1)S(1)} %slice.312), channel_id=1, source_target_pairs={{2,0},{3,1},{0,2},{1,3},{6,4},{7,5},{4,6},{5,7},{10,8},{11,9},{8,1... | collective-permute-start | bytes 393224 | tf_op jit(solution)/shard_map/ppermute | solution.py:1085
  193.1 26.9 %collective-permute-start.49 = (bf16[576,768]{1,0:T(8,128)(2,1)}, bf16[576,768]{1,0:T(8,128)(2,1)S(1)}, u32[]{:S(2)}, u32[]{:S(2)}) collective-permute-start(bf16[576,768]{1,0:T(8,128)(2,1)} %get-tuple-element.488), channel_id=1, source_target_pairs={{4,0},{0,4},{12,8},{8,12},{20,16},{16,20},{28,24},{24,28},{5,1},{1... | collective-permute-start | bytes 2654216 | tf_op jit(solution)/shard_map/ppermute | solution.py:1081
  201.6 18.4 %collective-permute-start.48 = (bf16[256,1536]{1,0:T(8,128)(2,1)S(1)}, bf16[256,1536]{1,0:T(8,128)(2,1)S(1)}, u32[]{:S(2)}, u32[]{:S(2)}) collective-permute-start(bf16[256,1536]{1,0:T(8,128)(2,1)S(1)} %get-tuple-element.483), channel_id=1, source_target_pairs={{1,0},{0,1},{3,2},{2,3},{5,4},{4,5},{7,6},{6,7},{9,8},{8,9},{11,10... | collective-permute-start | bytes 2359304 | tf_op jit(solution)/shard_map/ppermute | solution.py:1085
  201.9 12.3 %collective-permute-start.51 = (bf16[192,768]{1,0:T(8,128)(2,1)S(1)}, bf16[192,768]{1,0:T(8,128)(2,1)S(1)}, u32[]{:S(2)}, u32[]{:S(2)}) collective-permute-start(bf16[192,768]{1,0:T(8,128)(2,1)S(1)} %get-tuple-element.569), channel_id=1, source_target_pairs={{8,0},{12,4},{16,8},{20,12},{24,16},{28,20},{0,24},{4,28},{9,1},{1... | collective-permute-start | bytes 884744 | tf_op jit(solution)/shard_map/ppermute | solution.py:1072
  202.8 17.2 %collective-permute-start.50 = (bf16[192,768]{1,0:T(8,128)(2,1)S(1)}, bf16[192,768]{1,0:T(8,128)(2,1)S(1)}, u32[]{:S(2)}, u32[]{:S(2)}) collective-permute-start(bf16[192,768]{1,0:T(8,128)(2,1)S(1)} %get-tuple-element.570), channel_id=1, source_target_pairs={{24,0},{28,4},{0,8},{4,12},{8,16},{12,20},{16,24},{20,28},{25,1},{... | collective-permute-start | bytes 884744 | tf_op jit(solution)/shard_map/ppermute | solution.py:1072
  222.4 24.9 %collective-permute-start.53 = (bf16[256,1536]{1,0:T(8,128)(2,1)S(1)}, bf16[256,1536]{1,0:T(8,128)(2,1)S(1)}, u32[]{:S(2)}, u32[]{:S(2)}) collective-permute-start(bf16[256,1536]{1,0:T(8,128)(2,1)S(1)} %add_convert_fusion.1), channel_id=1, source_target_pairs={{2,0},{3,1},{0,2},{1,3},{6,4},{7,5},{4,6},{5,7},{10,8},{11,9},{8,1... | collective-permute-start | bytes 2359304 | tf_op jit(solution)/shard_map/ppermute | solution.py:1085
  223.3 23.9 %collective-permute-start.57 = (bf16[192,1536]{1,0:T(8,128)(2,1)S(1)}, bf16[192,1536]{1,0:T(8,128)(2,1)S(1)}, u32[]{:S(2)}, u32[]{:S(2)}) collective-permute-start(bf16[192,1536]{1,0:T(8,128)(2,1)S(1)} %pad_maximum_fusion), channel_id=1, source_target_pairs={{4,0},{0,4},{12,8},{8,12},{20,16},{16,20},{28,24},{24,28},{5,1},{1... | collective-permute-start | bytes 1769480 | tf_op jit(solution)/shard_map/ppermute | solution.py:1081
  224.1 19.2 %collective-permute-start.56 = (bf16[880,128]{1,0:T(8,128)(2,1)S(1)}, bf16[880,128]{1,0:T(8,128)(2,1)S(1)}, u32[]{:S(2)}, u32[]{:S(2)}) collective-permute-start(bf16[880,128]{1,0:T(8,128)(2,1)S(1)} %pad_maximum_fusion.2), channel_id=1, source_target_pairs={{4,0},{0,4},{12,8},{8,12},{20,16},{16,20},{28,24},{24,28},{5,1},{1... | collective-permute-start | bytes 675848 | tf_op jit(solution)/shard_map/ppermute | solution.py:1081
  225.5 17.8 %collective-permute-start.54 = (bf16[192,768]{1,0:T(8,128)(2,1)S(1)}, bf16[192,768]{1,0:T(8,128)(2,1)S(1)}, u32[]{:S(2)}, u32[]{:S(2)}) collective-permute-start(bf16[192,768]{1,0:T(8,128)(2,1)S(1)} %get-tuple-element.505), channel_id=1, source_target_pairs={{24,0},{28,4},{0,8},{4,12},{8,16},{12,20},{16,24},{20,28},{25,1},{... | collective-permute-start | bytes 884744 | tf_op jit(solution)/shard_map/ppermute | solution.py:1072
  225.5 21.7 %collective-permute-start.55 = (bf16[192,768]{1,0:T(8,128)(2,1)S(1)}, bf16[192,768]{1,0:T(8,128)(2,1)S(1)}, u32[]{:S(2)}, u32[]{:S(2)}) collective-permute-start(bf16[192,768]{1,0:T(8,128)(2,1)S(1)} %get-tuple-element.506), channel_id=1, source_target_pairs={{16,0},{20,4},{24,8},{28,12},{0,16},{4,20},{8,24},{12,28},{17,1},{... | collective-permute-start | bytes 884744 | tf_op jit(solution)/shard_map/ppermute | solution.py:1072
  249.6 11.3 %collective-permute-start.63 = (bf16[304,128]{1,0:T(8,128)(2,1)S(1)}, bf16[304,128]{1,0:T(8,128)(2,1)S(1)}, u32[]{:S(2)}, u32[]{:S(2)}) collective-permute-start(bf16[304,128]{1,0:T(8,128)(2,1)S(1)} %get-tuple-element.576), channel_id=1, source_target_pairs={{24,0},{28,4},{0,8},{4,12},{8,16},{12,20},{16,24},{20,28},{25,1},{... | collective-permute-start | bytes 233480 | tf_op jit(solution)/shard_map/ppermute | solution.py:1072
  249.7 11.2 %collective-permute-start.62 = (bf16[304,128]{1,0:T(8,128)(2,1)S(1)}, bf16[304,128]{1,0:T(8,128)(2,1)S(1)}, u32[]{:S(2)}, u32[]{:S(2)}) collective-permute-start(bf16[304,128]{1,0:T(8,128)(2,1)S(1)} %get-tuple-element.577), channel_id=1, source_target_pairs={{16,0},{20,4},{24,8},{28,12},{0,16},{4,20},{8,24},{12,28},{17,1},{... | collective-permute-start | bytes 233480 | tf_op jit(solution)/shard_map/ppermute | solution.py:1072
  249.8 11.1 %collective-permute-start.64 = (bf16[192,768]{1,0:T(8,128)(2,1)S(1)}, bf16[192,768]{1,0:T(8,128)(2,1)S(1)}, u32[]{:S(2)}, u32[]{:S(2)}) collective-permute-start(bf16[192,768]{1,0:T(8,128)(2,1)S(1)} %copy-done.66), channel_id=1, source_target_pairs={{4,0},{0,4},{12,8},{8,12},{20,16},{16,20},{28,24},{24,28},{5,1},{1... | collective-permute-start | bytes 884744 | tf_op jit(solution)/shard_map/ppermute | solution.py:1081
  251.2 12.4 %collective-permute-start.61 = (bf16[208,896]{1,0:T(8,128)(2,1)S(1)}, bf16[208,896]{1,0:T(8,128)(2,1)S(1)}, u32[]{:S(2)}, u32[]{:S(2)}) collective-permute-start(bf16[208,896]{1,0:T(8,128)(2,1)S(1)} %pad_maximum_fusion.1), channel_id=1, source_target_pairs={{8,0},{12,4},{16,8},{20,12},{24,16},{28,20},{0,24},{4,28},{9,1},{1... | collective-permute-start | bytes 1118216 | tf_op jit(solution)/shard_map/ppermute | solution.py:1072
  254.3 23.8 %collective-permute-start.58 = (bf16[256,1536]{1,0:T(8,128)(2,1)S(1)}, bf16[256,1536]{1,0:T(8,128)(2,1)S(1)}, u32[]{:S(2)}, u32[]{:S(2)}) collective-permute-start(bf16[256,1536]{1,0:T(8,128)(2,1)S(1)} %norm_backward.1.refs_0_), channel_id=1, source_target_pairs={{2,0},{3,1},{0,2},{1,3},{6,4},{7,5},{4,6},{5,7},{10,8},{11,9},{8,1... | collective-permute-start | bytes 2359304 | tf_op jit(solution)/shard_map/ppermute | solution.py:1085
  264.4 10.2 %collective-permute-start.67 = (f32[240,128]{1,0:T(8,128)S(1)}, f32[240,128]{1,0:T(8,128)S(1)}, u32[]{:S(2)}, u32[]{:S(2)}) collective-permute-start(f32[240,128]{1,0:T(8,128)S(1)} %get-tuple-element.553.refs_0_), channel_id=1, source_target_pairs={{3,0},{2,1},{1,2},{0,3},{7,4},{6,5},{5,6},{4,7},{11,8},{10,9},{9,1... | collective-permute-start | bytes 368648 | tf_op jit(solution)/shard_map/ppermute | solution.py:1085
  264.4 12.9 %collective-permute-start.66 = (f32[240,128]{1,0:T(8,128)S(1)}, f32[240,128]{1,0:T(8,128)S(1)}, u32[]{:S(2)}, u32[]{:S(2)}) collective-permute-start(f32[240,128]{1,0:T(8,128)S(1)} %get-tuple-element.553.refs_0_), channel_id=1, source_target_pairs={{2,0},{3,1},{0,2},{1,3},{6,4},{7,5},{4,6},{5,7},{10,8},{11,9},{8,1... | collective-permute-start | bytes 368648 | tf_op jit(solution)/shard_map/ppermute | solution.py:1085
  265.6 11.7 %collective-permute-start.65 = (f32[240,128]{1,0:T(8,128)S(1)}, f32[240,128]{1,0:T(8,128)S(1)}, u32[]{:S(2)}, u32[]{:S(2)}) collective-permute-start(f32[240,128]{1,0:T(8,128)S(1)} %get-tuple-element.553.refs_0_), channel_id=1, source_target_pairs={{1,0},{0,1},{3,2},{2,3},{5,4},{4,5},{7,6},{6,7},{9,8},{8,9},{11,10... | collective-permute-start | bytes 368648 | tf_op jit(solution)/shard_map/ppermute | solution.py:1085
  (71 other events, 911.3 us)

commit v7 on v6

--- a/solution.py
+++ b/solution.py
@@ -78,9 +78,11 @@
 
 def step_parts(step_pre, heads):
     raw = step_pre + heads[0:1, :]
-    steps = jnp.maximum(raw, 0.0) + jnp.log1p(jnp.exp(-jnp.abs(raw)))
+    small = jnp.exp(-jnp.abs(raw))
+    steps = jnp.maximum(raw, 0.0) + jnp.log1p(small)
+    slope = jnp.where(raw >= 0.0, 1.0, small) / (1.0 + small)
     rates = -jnp.exp(heads[1:2, :])
-    return raw, steps, rates
+    return slope, steps, rates
 
 
 def triangle(lower):
@@ -168,7 +170,7 @@
     expand = expand_ref[...]
     x_act = act_ref[...]
     b_mat, c_mat = bcact_ref[:, :LANES], bcact_ref[:, LANES:]
-    raw, steps, rates = step_parts(st_ref[...], heads_ref)
+    slope, steps, rates = step_parts(st_ref[...], heads_ref)
     lower = triangle(True)
     cum = exact_left(lower.astype(bf16), steps * rates)
     cum_t = cum.T
@@ -224,7 +226,7 @@
     sums = gather_heads(sums, expand_t)
     dlog = exact_left(upper.astype(bf16), flow) + sums[0:1, :]
     dstep = dstep + rates * dlog
-    draw = dstep * sigmoid(raw)
+    draw = dstep * slope
     dst_ref[...] = pltpu.roll(draw, WIDTH, 1).astype(bf16)
     dst_t_ref[...] = draw.T[0:16, :].astype(bf16)
     dheads_ref[0:1, :] += jnp.sum(draw, axis=0, keepdims=True)
@@ -249,7 +251,12 @@
     dx_ref[...] = conv_back(du_scr, du, x_now, conv_ref, dconv_ref).astype(dx_ref.dtype)
     dubc = jnp.concatenate([db, dc], axis=1) * bcslope_ref[...]
     dbc = conv_back(dubc_scr, dubc, bc_now, bct_ref, dbct_ref).astype(bf16)
-    dbc_ref[...] = dbc
+    swapped = jnp.concatenate([dbc[:, LANES:], dbc[:, :LANES]], axis=1)
+    ordered = jnp.where((rank_ref[0] & 2) == 2, swapped, dbc)
+    swapped = jnp.concatenate(
+        [pltpu.roll(ordered[:, :LANES].astype(f32), WIDTH, 1), pltpu.roll(ordered[:, LANES:].astype(f32), WIDTH, 1)], axis=1
+    ).astype(bf16)
+    dbc_ref[...] = jnp.where((rank_ref[0] & 1) == 1, swapped, ordered)
     share = 2 * LANES // 4
     turned = dbc.T
     for member in range(4):
@@ -340,11 +347,11 @@
             pl.BlockSpec((8, LANES), whole),
         ],
         out_shape=[
-            hbm((tokens, channels), bf16),
-            hbm((tokens, 2 * LANES), bf16),
+            jax.ShapeDtypeStruct((tokens, channels), bf16),
+            jax.ShapeDtypeStruct((tokens, 2 * LANES), bf16),
             hbm((LANES, tokens), bf16),
             hbm((LANES, tokens), bf16),
-            hbm((tokens, LANES), bf16),
+            jax.ShapeDtypeStruct((tokens, LANES), bf16),
             hbm((16, tokens), bf16),
             jax.ShapeDtypeStruct((8, channels), f32),
             jax.ShapeDtypeStruct((8, 2 * LANES), f32),
@@ -446,20 +453,19 @@
     )(hidden, gain_rows)
 
 
-def pack_kernel(rank_ref, in_ref, bc_ref, step_ref, a_ref, b_ref, scratch):
-    channels = b_ref.shape[1]
+def pack_kernel(rank_ref, in_ref, bc_ref, step_ref, a_ref, scratch):
     rows, width = bc_ref.shape
+    channels = in_ref.shape[2]
     share = width // 4
     heads = step_ref.shape[0]
-    b_ref[...] = in_ref[:, 0, :].astype(bf16)
     a_ref[:, :channels] = in_ref[:, 1, :].astype(bf16)
     scratch[...] = jnp.zeros_like(scratch)
     scratch[share:share + heads, 0:rows] = step_ref[...]
     step = scratch[...].T[0:rows, :]
     own = bc_ref[:, 0:LANES]
     for member in range(1, 4):
-        moved = pltpu.roll(bc_ref[...], width - member * share, 1)[:, 0:LANES]
-        own = jnp.where(rank_ref[0] == member, moved, own)
+        turned = pltpu.roll(bc_ref[...], width - member * share, 1)[:, 0:LANES]
+        own = jnp.where(rank_ref[0] == member, turned, own)
     lane = lax.broadcasted_iota(jnp.int32, (rows, LANES), 1)
     a_ref[:, channels:] = jnp.where(lane < share, own, step).astype(bf16)
 
@@ -470,16 +476,31 @@
     return pl.pallas_call(
         pack_kernel,
         in_specs=[pl.BlockSpec(memory_space=pltpu.SMEM), vmem, vmem, vmem],
-        out_specs=[vmem, vmem],
-        out_shape=[
-            jax.ShapeDtypeStruct((rows, channels + LANES), bf16),
-            hbm((rows, channels), bf16),
-        ],
+        out_specs=vmem,
+        out_shape=jax.ShapeDtypeStruct((rows, channels + LANES), bf16),
         scratch_shapes=[pltpu.VMEM((LANES, 2 * LANES), f32)],
         compiler_params=params(),
         cost_estimate=cost(2),
         name="pack",
-    )(rank, from_hbm(in_weight), from_hbm(bc_weight), step_t)
+    )(rank, from_hbm(in_weight), from_hbm(bc_weight), from_hbm(step_t))
+
+
+def pack_gate_kernel(in_ref, b_ref):
+    b_ref[...] = in_ref[:, 0, :].astype(bf16)
+
+
+def pack_gate(in_weight):
+    rows, _, channels = in_weight.shape
+    vmem = pl.BlockSpec(memory_space=pltpu.VMEM)
+    return pl.pallas_call(
+        pack_gate_kernel,
+        in_specs=[vmem],
+        out_specs=vmem,
+        out_shape=hbm((rows, channels), bf16),
+        compiler_params=params(),
+        cost_estimate=cost(2),
+        name="pack_gate",
+    )(from_hbm(in_weight))
 
 
 def columns_kernel(rank_ref, *refs, count):
@@ -855,14 +876,15 @@
     )(rank, gated_out, w_out)
 
 
-def term_kernel(rank_ref, gx_ref, wx_ref, gg_ref, wg_ref, gs_ref, ws_ref, gb_ref, wbt_ref, hidden_ref, inv_ref, *refs, apart):
-    dgain_ref, outs = refs[-1], refs[:-1]
+def term_kernel(rank_ref, gx_ref, wx_ref, gg_ref, wg_ref, gs_ref, ws_ref, gb_ref, hidden_ref, inv_ref, *refs, apart):
+    wbt_refs, outs, dgain_ref = refs[:4], refs[4:-1], refs[-1]
+    w_bct = jnp.concatenate([ref[...] for ref in wbt_refs], axis=0)
     gain = None
     for r, out in zip(apart, outs):
         rows = out.shape[0]
         span = pl.ds(pl.multiple_of((rank_ref[0] ^ r) * rows, rows), rows)
         total = dot_nt(gx_ref[span, :], wx_ref[...]) + dot_nt(gg_ref[span, :], wg_ref[...])
-        total = total + dot_nt(gs_ref[span, :], ws_ref[...]) + dot_nn(gb_ref[span, :], wbt_ref[...])
+        total = total + dot_nt(gs_ref[span, :], ws_ref[...]) + dot_nn(gb_ref[span, :], w_bct)
         out[...] = total.astype(bf16)
         normed = hidden_ref[span, :].astype(f32) * row_to_column(inv_ref[0:1, span])
         own = jnp.sum(total * normed, axis=0, keepdims=True)
@@ -888,10 +910,10 @@
             pl.BlockSpec(dstep.shape, whole),
             pl.BlockSpec((TILE_D, LANES), lambda i: (i, 0)),
             pl.BlockSpec(dbc.shape, whole),
-            pl.BlockSpec((w_bct.shape[0], TILE_D), lambda i: (0, i)),
             pl.BlockSpec((tokens, TILE_D), lambda i: (0, i)),
             pl.BlockSpec(inv_rms.shape, whole),
-        ],
+        ]
+        + [pl.BlockSpec((w.shape[0], TILE_D), lambda i: (0, i)) for w in w_bct],
         out_specs=[pl.BlockSpec((rows, TILE_D), lambda i: (0, i))] * len(apart) + [pl.BlockSpec((8, LANES), lambda i: (i, 0))],
         out_shape=[jax.ShapeDtypeStruct((rows, depth), bf16)] * len(apart)
         + [jax.ShapeDtypeStruct((8 * (depth // TILE_D), LANES), f32)],
@@ -899,8 +921,7 @@
         cost_estimate=cost(20 if 2 in apart else 0.1),
         name="normed_term",
     )(
-        rank, dx, from_hbm(w_a), dgate, from_hbm(w_b), dstep, from_hbm(w_s), dbc,
-        from_hbm(w_bct), from_hbm(hidden), inv_rms,
+        rank, dx, from_hbm(w_a), dgate, from_hbm(w_b), dstep, from_hbm(w_s), dbc, from_hbm(hidden), inv_rms, *w_bct
     )
 
 
@@ -961,7 +982,7 @@
 
 def update_in(weight, moment, gate_parts, x_parts):
     rows, _, channels = weight.shape
-    size = min(rows, 48)
+    size = min(rows, 96)
     full = pl.BlockSpec((size, 2, channels), lambda i: (i, 0, 0))
     parts = [*gate_parts, *x_parts]
     return pl.pallas_call(
@@ -1185,7 +1206,7 @@
     split_sizes = (1, 1, n - 1, n - 2, 1)
     width = depth // ranks
 
-    set_a, set_b = pack(in_weight, bc_weight, step_weight.T, rank1)
+    set_a, set_b = pack(in_weight, bc_weight, step_weight.T, rank1), pack_gate(in_weight)
     set_c = out_weight.T.astype(bf16)
 
     def blocks(own, z, x):
@@ -1240,9 +1261,10 @@
     c_x = {0: inner_flip(set_c)}
     a_blocks = blocks(set_a, a_z, a_x)
     small, bc_share, w_s, w_bct_share = project_small(normed_low, a_blocks, idx, share)
-    bc_pieces = mp_pieces(bc_share)
+    bc_far, bc_near = rank_flip(bc_share, 2), rank_flip(bc_share, 1)
     x_pre, w_a = project(normed_low, a_blocks, idx, channels)
-    bc_pieces, x_pre, small, set_c, w_bct_share, w_s = fence(bc_pieces, x_pre, small, set_c, w_bct_share, w_s)
+    bc_far, x_pre, small, set_c, w_bct_share, w_s = fence(bc_far, x_pre, small, set_c, w_bct_share, w_s)
+    bc_pieces = [bc_share, bc_near, bc_far, rank_flip(bc_far, 1)]
     bc_pre, step_pre = join_small(bc_pieces, small, rank1)
     set_c, b_z, b_x, c_x, x_pre, bc_pre, step_pre, w_bct_share = fence(
         set_c, b_z, b_x, c_x, x_pre, bc_pre, step_pre, w_bct_share
@@ -1285,7 +1307,6 @@
     )
     c_blocks = [pair_sum(block(gc_here, i), block(gc_near_back, i)) for i in range(n - 2)]
     out_far = pair_sum(partial[2], out_back)
-    w_bct = join_rows(w_bct, rank1)
     c_blocks, out_far, w_bct, dmixed, gb_send = fence(c_blocks, out_far, w_bct, dmixed, gb_send)
 
     c_got = outer_send(c_blocks, near_ks) + [c_far_got]
@@ -1319,18 +1340,18 @@
     far_back = rank_flip(far_send, 1)
     operands = (dx, *operands[1:])
     near_own, near_send, gain_near = normed_term(*operands, (0, 1))
-    far_back, near_own, near_send, gain_near, ga_back, b_got = fence(
-        far_back, near_own, near_send, gain_near, ga_back, b_got
-    )
+    far_back, near_own, near_send, gain_near, ga_back = fence(far_back, near_own, near_send, gain_near, ga_back)
     near_back = rank_flip(near_send, 1)
     far = pair_sum(far_own, far_back)
     a_blocks = [pair_sum(block(ga_here, i), block(ga_back, i)) for i in range(n - 1)]
     dbc_share = pair_sum(dbc_pair[:share], dbc_got)
     dsmall_t = jnp.concatenate([dbc_share, dstep_t, jnp.zeros((LANES - share - 16, tokens), bf16)], axis=0)
     gs_own, gs_here, gs_send = weight_grad(normed_t, dsmall_t, idx_s, (1, n - 1, n), turned=True)
-    far, a_blocks, near_back, gs_send, gc_own1, gb_own1 = fence(far, a_blocks, near_back, gs_send, gc_own1, gb_own1)
-
-    early, late = near_ks[:(n - 2) // 2], near_ks[(n - 2) // 2:]
+    far, a_blocks, near_back, gs_send, gc_own1, gb_own1, b_got = fence(
+        far, a_blocks, near_back, gs_send, gc_own1, gb_own1, b_got
+    )
+
+    early, late = [], near_ks
     got = rank_flip(far, 2)
     a_got = dict(zip([far_k, *early], outer_send([a_blocks[-1], *a_blocks[:len(early)]], [far_k, *early])))
     cut = lambda v: [v[:, i:i + LANES] for i in range(0, v.shape[1], LANES)]
@@ -1380,6 +1401,7 @@
         [(ga_own, 0), (a_own_got, 0)] + [(a_got[k], 0) for k in (far_k, *early)] + [(v, 0) for v in late_got],
     )
     input_grad = join_rows([mine, mine_near, mine_far, mine_far_near], rank1)
+    exchanged, mine_far_near = fence(exchanged, mine_far_near)
     bc_m, bc_w, totals_shared = update_bc(bc_weight, bc_moment, exchanged, rank1)
 
     resid = lax.dynamic_slice_in_dim(hidden, rank * width, width, 1).astype(f32)

time: 284 us -> 273 us (0.961)
  waiting for transfers between devices: 71 us -> 61.9 us
  starting transfers between devices: 65.8 us -> 61.6 us
  other arithmetic: 11.3 us -> 15 us
    ppermute x29, waiting for transfers between devices: 15.1 us -> 4.54 us  [rank_flip(): lax.ppermute(v, 'mp', [(m ^ bit, m) for m in range(lax.axis_size('mp'))])]
    ppermute x19, waiting for transfers between devices: 20.4 us -> 27 us  [inner_flip(): lax.ppermute(v, 'dp', [(d ^ 1, d) for d in range(lax.axis_size('dp'))])]
    ppermute x20 -> x19, waiting for transfers between devices: 35.5 us -> 30.3 us  [outer_from(): lax.ppermute(v, 'dp', [((o + k) % n * 2 + x, o * 2 + x) for o in range(n)...]
    ppermute x20 -> x19, starting transfers between devices: 29 us -> 26.7 us  [outer_from(): lax.ppermute(v, 'dp', [((o + k) % n * 2 + x, o * 2 + x) for o in range(n)...]
  transfers between devices with their start and end apart: 68 -> 67, of which waited for: 23 -> 21; matrix products, arithmetic and copies ran while one was open for 5% -> 7% of each run, Pallas kernels for 41% -> 43%
where the time goes in v7:
time: 273 us
  Pallas kernels  125 us (46%)
  waiting for transfers between devices  61.9 us (23%)
  starting transfers between devices  61.6 us (23%)
  other arithmetic  15 us (5%)
  local copies, waits for them, and re-layouts  7.11 us (3%)
    ppermute x19, waiting for transfers between devices, outer_from(): lax.ppermute(v, 'dp', [((o + k) % n * 2 + x, o * 2 + x) for o in range(n)...  30.3 us
    ppermute x19, waiting for transfers between devices, inner_flip(): lax.ppermute(v, 'dp', [(d ^ 1, d) for d in range(lax.axis_size('dp'))])  27 us
    ppermute x19, starting transfers between devices, outer_from(): lax.ppermute(v, 'dp', [((o + k) % n * 2 + x, o * 2 + x) for o in range(n)...  26.7 us
    ppermute x19, starting transfers between devices, inner_flip(): lax.ppermute(v, 'dp', [(d ^ 1, d) for d in range(lax.axis_size('dp'))])  20.6 us
    pallas_call x1, Pallas kernels, ssd_backward(): pl.pallas_call(ssd_backward_kernel, grid=(count,), in_specs=[pl.BlockSpec...  20 us
    pallas_call x4, Pallas kernels, weight_grad(): pl.pallas_call(functools.partial(weight_grad_kernel, rows=rows, turned=tu...  18.9 us
    ppermute x29, starting transfers between devices, rank_flip(): lax.ppermute(v, 'mp', [(m ^ bit, m) for m in range(lax.axis_size('mp'))])  14.3 us
    pallas_call x1, Pallas kernels, ssd_forward(): pl.pallas_call(ssd_forward_kernel, grid=(count,), in_specs=common_specs(l...  14.2 us
  transfers between devices with their start and end apart: 67, of which 21 were waited for; matrix products, arithmetic and copies ran while one was open for 7% of the time, Pallas kernels for 43%

profile of v7, /device:TPU:0, one launch (start us, length us, event | category | flops | bytes accessed | tf_op | source)
XLA Modules:
  0.0 272.6 jit_solution(2504588519123946754)
XLA Ops:
  0.7 2.8 %pack.1.refs_0_ = bf16[192,896]{1,0:T(8,128)(2,1)S(1)} custom-call(s32[1]{0:T(128)} %bitcast.8.rank_ref, f32[192,2,768]{2,1,0:T(2,128)} %w_ref.2, f32[192,256]{1,0:T(8,128)} %w_ref.3, f32[12,192]{1,0:T(8,128)} %bitcast.47), custom_call_target="tpu_custom_call" | custom-call | flops 2000000000 | bytes 4000000 | tf_op jit(solution)/shard_map/pack/pallas_call | solution.py:476
  3.6 3.1 %collective-permute-start.3 = (bf16[192,896]{1,0:T(8,128)(2,1)S(1)}, bf16[192,896]{1,0:T(8,128)(2,1)}, u32[]{:S(2)}, u32[]{:S(2)}) collective-permute-start(bf16[192,896]{1,0:T(8,128)(2,1)S(1)} %pack.1.refs_0_), channel_id=1, source_target_pairs={{24,0},{28,4},{0,8},{4,12},{8,16},{12,20},{16,24},{20,28},{25,1},{... | collective-permute-start | bytes 1032200 | tf_op jit(solution)/shard_map/ppermute | solution.py:1093
  6.6 1.5 collective-permute-start.1
  8.1 2.2 collective-permute-start
  10.4 1.5 collective-permute-start.6
  19.6 3.7 %prepare.1 = (bf16[1024,1536]{1,0:T(8,128)(2,1)}, bf16[1536,1024]{1,0:T(8,128)(2,1)}, f32[8,1024]{1,0:T(8,128)S(1)}) custom-call(bf16[1024,1536]{1,0:T(8,128)(2,1)S(1)} %copy-done.1, f32[8,1536]{1,0:T(8,128)S(1)} %pad.53.gain_ref), custom_call_target="tpu_custom_call" | custom-call | flops 12000000000 | bytes 24000000 | tf_op jit(solution)/shard_map/prepare/pallas_call | solution.py:440
  25.9 1.5 collective-permute-start.4
  27.4 2.6 pack_gate.1.refs_0_
  30.7 5.8 %collective-permute-done.5.refs_6_ = bf16[192,896]{1,0:T(8,128)(2,1)S(1)} collective-permute-done((bf16[192,896]{1,0:T(8,128)(2,1)}, bf16[192,896]{1,0:T(8,128)(2,1)S(1)}, u32[]{:S(2)}, u32[]{:S(2)}) %collective-permute-start.5) | collective-permute-done | bytes 344096 | tf_op jit(solution)/shard_map/ppermute | solution.py:1102
  36.5 6.1 %collective-permute-done.2.refs_4_ = bf16[192,896]{1,0:T(8,128)(2,1)S(1)} collective-permute-done((bf16[192,896]{1,0:T(8,128)(2,1)S(1)}, bf16[192,896]{1,0:T(8,128)(2,1)S(1)}, u32[]{:S(2)}, u32[]{:S(2)}) %collective-permute-start.2) | collective-permute-done | bytes 344096 | tf_op jit(solution)/shard_map/ppermute | solution.py:1093
  43.9 1.6 collective-permute-start.8
  45.4 2.2 collective-permute-start.7
  47.7 1.5 collective-permute-start.10
  49.2 3.4 %join_columns.1 = (bf16[1024,1536]{1,0:T(8,128)(2,1)S(1)}, bf16[1536,1024]{1,0:T(8,128)(2,1)S(1)}) custom-call(s32[1]{0:T(128)} %bitcast.8.rank_ref, bf16[1024,384]{1,0:T(8,128)(2,1)} %refs_0_.1, bf16[1024,384]{1,0:T(8,128)(2,1)} %collective-permute-done.11.refs_1_, bf16[1024,384]{1,0:T(8,128)(2,1)} %collective-permute-done.6.refs_2_, ...), custom_call_target="tpu_custom_call" | custom-call | flops 12000000000 | bytes 24000000 | tf_op jit(solution)/shard_map/join_columns/pallas_call | solution.py:519
  53.3 2.4 collective-permute-done.8.refs_3_
  55.8 5.1 %collective-permute-done.7.refs_2_ = bf16[192,768]{1,0:T(8,128)(2,1)S(1)} collective-permute-done((bf16[192,768]{1,0:T(8,128)(2,1)}, bf16[192,768]{1,0:T(8,128)(2,1)S(1)}, u32[]{:S(2)}, u32[]{:S(2)}) %collective-permute-start.7) | collective-permute-done | bytes 294944 | tf_op jit(solution)/shard_map/ppermute | solution.py:1093
  60.8 1.5 collective-permute-start.16
  62.9 1.6 collective-permute-start.14
  64.5 3.8 %project_small.1 = (f32[128,1024]{1,0:T(8,128)S(1)}, bf16[64,1024]{1,0:T(8,128)(2,1)S(1)}, bf16[1536,128]{1,0:T(8,128)(2,1)}, bf16[64,1536]{1,0:T(8,128)(2,1)}) custom-call(s32[8]{0:T(128)S(1)} %stack.88.idx_ref, bf16[1024,1536]{1,0:T(8,128)(2,1)S(1)} %copy-done.3, bf16[192,896]{1,0:T(8,128)(2,1)S(1)} %pack.1.refs_0_, ...), custom_call_target="tpu_custom_call" | custom-call | flops 20000000000 | bytes 40000000 | tf_op jit(solution)/shard_map/project_small/pallas_call | solution.py:598
  68.8 5.7 %project.1 = (f32[1024,768]{1,0:T(8,128)}, bf16[1536,768]{1,0:T(8,128)(2,1)}) custom-call(s32[8]{0:T(128)S(1)} %stack.88.idx_ref, bf16[1024,1536]{1,0:T(8,128)(2,1)S(1)} %copy-done.3, bf16[192,896]{1,0:T(8,128)(2,1)S(1)} %pack.1.refs_0_, bf16[192,896]{1,0:T(8,128)(2,1)} %collective-permute-done.1.refs_1_, bf16[192,896]{1,0:T(8,128)(2,1)} %collective-permute-done.refs_2_, ...), custom_call_target="tpu_custom_call" | custom-call | flops 100000000 | bytes 200000 | tf_op jit(solution)/shard_map/project/pallas_call | solution.py:634
  76.0 1.3 join_small.1
  78.4 3.3 %collective-permute-start.21 = (bf16[192,768]{1,0:T(8,128)(2,1)}, bf16[192,768]{1,0:T(8,128)(2,1)S(1)}, u32[]{:S(2)}, u32[]{:S(2)}) collective-permute-start(bf16[192,768]{1,0:T(8,128)(2,1)} %convert_bitcast_fusion.refs_0_), channel_id=1, source_target_pairs={{8,0},{12,4},{16,8},{20,12},{24,16},{28,20},{0,24},{4,28},{9,1},{1... | collective-permute-start | bytes 884744 | tf_op jit(solution)/shard_map/ppermute | solution.py:1093
  81.8 1.5 collective-permute-start.19
  83.8 14.2 %ssd_forward.1 = (f32[1024,768]{1,0:T(8,128)}, bf16[8,128,768]{2,1,0:T(8,128)(2,1)}, f32[1024,768]{1,0:T(8,128)}, bf16[1024,768]{1,0:T(8,128)(2,1)}, bf16[1024,7...) custom-call(f32[1024,768]{1,0:T(8,128)} %get-tuple-element.335.x_ref, ...), custom_call_target="tpu_custom_call" | custom-call | flops 14000000000 | bytes 40000000 | tf_op jit(solution)/shard_map/ssd_forward/pallas_call | solution.py:293
  98.0 1.5 collective-permute-start.27
  100.1 6.9 %gate_forward.1 = (f32[1024,768]{1,0:T(8,128)S(1)}, f32[8,1024]{1,0:T(8,128)S(1)}, bf16[1536,768]{1,0:T(8,128)(2,1)}) custom-call(s32[8]{0:T(128)S(1)} %stack.88.idx_ref, bf16[1024,1536]{1,0:T(8,128)(2,1)S(1)} %copy-done.3, f32[1024,768]{1,0:T(8,128)} %get-tuple-element.375.mixed_ref, bf16[192,768]{1,0:T(8,128)(2,1)S(1)} %copy-done.10, ...), custom_call_target="tpu_custom_call" | custom-call | flops 100000000 | bytes 200000 | tf_op jit(solution)/shard_map/gate_forward/pallas_call | solution.py:676
  108.1 2.3 collective-permute-done.25
  111.6 1.4 collective-permute-done.26.refs_4_
  113.6 1.5 collective-permute-start.30
  115.1 1.3 gated_norm.1.rhs_ref.lhs_ref
  116.4 5.3 %weight_grad.4 = (bf16[192,768]{1,0:T(8,128)(2,1)}, bf16[192,768]{1,0:T(8,128)(2,1)}, bf16[576,768]{1,0:T(8,128)(2,1)}, bf16[384,768]{1,0:T(8,128)(2,1)}, bf16[192,768]{1,0:T(8,128)(2,1)}) custom-call(s32[8]{0:T(128)S(1)} %stack.88.idx_ref, bf16[1536,1024]{1,0:T(8,128)(2,1)S(1)} %get-tuple-element.376.lhs_ref, bf16[1024,768]{1,0:T(8,128)(2,1)S(1)} %gated_norm.1.rhs_ref.lhs_ref), custom_call_target="tpu_custom_call" | custom-call | flops 100000000 | bytes 200000 | tf_op jit(solution)/shard_map/weight_grad/pallas_call | solution.py:831
  122.0 1.3 collective-permute-start.35
  123.3 4.8 %grad_gout.1 = (f32[1024,768]{1,0:T(8,128)S(1)}, f32[8,1024]{1,0:T(8,128)S(1)}, bf16[1536,768]{1,0:T(8,128)(2,1)S(1)}) custom-call(s32[8]{0:T(128)S(1)} %stack.88.idx_ref, bf16[1024,1536]{1,0:T(8,128)(2,1)S(1)} %get-tuple-element.385.cot_ref, f32[1024,768]{1,0:T(8,128)S(1)} %get-tuple-element.374.gate_ref, f32[1024,768]{1,0:T(8,128)S(1)} %copy-done, ...), custom_call_target="tpu_custom_call" | custom-call | flops 20000000000 | bytes 40000000 | tf_op jit(solution)/shard_map/grad_gout/pallas_call | solution.py:742
  129.0 1.1 collective-permute-start.32
  130.1 6.1 %out_partial.1 = (bf16[1024,384]{1,0:T(8,128)(2,1)}, bf16[1024,384]{1,0:T(8,128)(2,1)}, bf16[1024,384]{1,0:T(8,128)(2,1)}, bf16[1024,384]{1,0:T(8,128)(2,1)}) custom-call(s32[1]{0:T(128)} %bitcast.8.rank_ref, bf16[1024,768]{1,0:T(8,128)(2,1)S(1)} %gated_norm.1.rhs_ref.lhs_ref, bf16[1536,768]{1,0:T(8,128)(2,1)S(1)} %get-tuple-element.395.w_ref), custom_call_target="tpu_custom_call" | custom-call | flops 100000000 | bytes 200000 | tf_op jit(solution)/shard_map/out_partial/pallas_call | solution.py:861
  137.3 1.7 collective-permute-start.36
  139.7 6.1 %gate_backward.1 = (bf16[1024,768]{1,0:T(8,128)(2,1)S(1)}, bf16[1024,768]{1,0:T(8,128)(2,1)S(1)}, f32[8,768]{1,0:T(8,128)S(1)}) custom-call(f32[1024,768]{1,0:T(8,128)} %copy-done.4, f32[1024,768]{1,0:T(8,128)} %copy-done.6, f32[1024,768]{1,0:T(8,128)} %get-tuple-element.375.mixed_ref, f32[8,1024]{1,0:T(8,128)S(1)} %add_add_fusion.1.square_ref, ...), custom_call_target="tpu_custom_call" | custom-call | flops 100000000 | bytes 200000 | tf_op jit(solution)/shard_map/gate_backward/pallas_call | solution.py:793
  145.7 5.4 %weight_grad.5 = (bf16[192,768]{1,0:T(8,128)(2,1)}, bf16[192,768]{1,0:T(8,128)(2,1)}, bf16[576,768]{1,0:T(8,128)(2,1)}, bf16[576,768]{1,0:T(8,128)(2,1)}) custom-call(s32[8]{0:T(128)S(1)} %stack.88.idx_ref, bf16[1536,1024]{1,0:T(8,128)(2,1)S(1)} %copy-done.2, bf16[1024,768]{1,0:T(8,128)(2,1)S(1)} %get-tuple-element.411.rhs_ref.gg_ref), custom_call_target="tpu_custom_call" | custom-call | flops 100000000 | bytes 200000 | tf_op jit(solution)/shard_map/weight_grad/pallas_call | solution.py:831
  152.6 1.3 add_convert_fusion.9
  154.0 1.5 add_convert_fusion.2
  155.6 3.8 %collective-permute-start.41 = (bf16[192,768]{1,0:T(8,128)(2,1)S(1)}, bf16[192,768]{1,0:T(8,128)(2,1)S(1)}, u32[]{:S(2)}, u32[]{:S(2)}) collective-permute-start(bf16[192,768]{1,0:T(8,128)(2,1)S(1)} %get-tuple-element.432), channel_id=1, source_target_pairs={{8,0},{12,4},{16,8},{20,12},{24,16},{28,20},{0,24},{4,28},{9,1},{1... | collective-permute-start | bytes 884744 | tf_op jit(solution)/shard_map/ppermute | solution.py:1093
  159.4 1.1 collective-permute-start.43
  160.5 1.3 collective-permute-start.42
  161.8 20.0 %ssd_backward.1 = (bf16[1024,768]{1,0:T(8,128)(2,1)S(1)}, bf16[1024,256]{1,0:T(8,128)(2,1)S(1)}, bf16[128,1024]{1,0:T(8,128)(2,1)}, bf16[128,1024]{1,0:T(8,128)(...) custom-call(s32[1]{0:T(128)} %bitcast.8.rank_ref, ...), custom_call_target="tpu_custom_call" | custom-call | flops 28000000000 | bytes 40000000 | tf_op jit(solution)/shard_map/ssd_backward/pallas_call | solution.py:332
  183.0 5.3 %weight_grad.6 = (bf16[192,768]{1,0:T(8,128)(2,1)}, bf16[192,768]{1,0:T(8,128)(2,1)}, bf16[576,768]{1,0:T(8,128)(2,1)}, bf16[576,768]{1,0:T(8,128)(2,1)}) custom-call(s32[8]{0:T(128)S(1)} %stack.88.idx_ref, bf16[1536,1024]{1,0:T(8,128)(2,1)S(1)} %copy-done.2, bf16[1024,768]{1,0:T(8,128)(2,1)S(1)} %get-tuple-element.485.rhs_ref.gx_ref), custom_call_target="tpu_custom_call" | custom-call | flops 20000000000 | bytes 40000000 | tf_op jit(solution)/shard_map/weight_grad/pallas_call | solution.py:831
  189.5 1.4 collective-permute-start.49
  190.9 7.0 %normed_term.2 = (bf16[256,1536]{1,0:T(8,128)(2,1)S(1)}, bf16[256,1536]{1,0:T(8,128)(2,1)S(1)}, f32[32,128]{1,0:T(8,128)S(1)}) custom-call(s32[1]{0:T(128)} %bitcast.8.rank_ref, bf16[1024,768]{1,0:T(8,128)(2,1)S(1)} %get-tuple-element.485.rhs_ref.gx_ref, bf16[1536,768]{1,0:T(8,128)(2,1)} %get-tuple-element.467.wx_ref, ...), custom_call_target="tpu_custom_call" | custom-call | flops 20000000000 | bytes 40000000 | tf_op jit(solution)/shard_map/normed_term/pallas_call | solution.py:901
  198.2 1.9 collective-permute-start.52
  200.3 7.0 %normed_term.3 = (bf16[256,1536]{1,0:T(8,128)(2,1)S(1)}, bf16[256,1536]{1,0:T(8,128)(2,1)S(1)}, f32[32,128]{1,0:T(8,128)S(1)}) custom-call(s32[1]{0:T(128)} %bitcast.8.rank_ref, bf16[1024,768]{1,0:T(8,128)(2,1)S(1)} %get-tuple-element.485.rhs_ref.gx_ref, bf16[1536,768]{1,0:T(8,128)(2,1)} %get-tuple-element.467.wx_ref, ...), custom_call_target="tpu_custom_call" | custom-call | flops 100000000 | bytes 200000 | tf_op jit(solution)/shard_map/normed_term/pallas_call | solution.py:901
  207.4 2.9 %weight_grad.7 = (bf16[192,128]{1,0:T(8,128)(2,1)}, bf16[576,128]{1,0:T(8,128)(2,1)}, bf16[768,128]{1,0:T(8,128)(2,1)}) custom-call(s32[8]{0:T(128)S(1)} %stack.102.idx_ref, bf16[1536,1024]{1,0:T(8,128)(2,1)S(1)} %copy-done.2, bf16[128,1024]{1,0:T(8,128)(2,1)S(1)} %maximum_maximum_fusion.rhs_ref), custom_call_target="tpu_custom_call" | custom-call | flops 100000000 | bytes 200000 | tf_op jit(solution)/shard_map/weight_grad/pallas_call | solution.py:831
  210.2 1.3 collective-permute-done.49
  212.0 4.3 %collective-permute-done.51.refs_2_ = bf16[192,768]{1,0:T(8,128)(2,1)S(1)} collective-permute-done((bf16[192,768]{1,0:T(8,128)(2,1)S(1)}, bf16[192,768]{1,0:T(8,128)(2,1)S(1)}, u32[]{:S(2)}, u32[]{:S(2)}) %collective-permute-start.51) | collective-permute-done | bytes 294944 | tf_op jit(solution)/shard_map/ppermute | solution.py:1093
  218.1 1.3 collective-permute-start.55
  220.4 16.5 %collective-permute-done.55 = bf16[880,128]{1,0:T(8,128)(2,1)S(1)} collective-permute-done((bf16[880,128]{1,0:T(8,128)(2,1)S(1)}, bf16[880,128]{1,0:T(8,128)(2,1)S(1)}, u32[]{:S(2)}, u32[]{:S(2)}) %collective-permute-start.55) | collective-permute-done | bytes 225312 | tf_op jit(solution)/shard_map/ppermute | solution.py:1102
  236.9 2.2 norm_backward.1.refs_0_
  240.1 1.2 collective-permute-start.63
  241.4 1.7 collective-permute-start.61
  243.4 1.1 collective-permute-start.57
  244.5 2.1 multiply_subtract_fusion
  246.6 2.4 add_convert_fusion
  250.0 3.2 %collective-permute-done.61.refs_9_.refs_2_ = bf16[208,896]{1,0:T(8,128)(2,1)S(1)} collective-permute-done((bf16[208,896]{1,0:T(8,128)(2,1)S(1)}, bf16[208,896]{1,0:T(8,128)(2,1)S(1)}, u32[]{:S(2)}, u32[]{:S(2)}) %collective-permute-start.61) | collective-permute-done | bytes 372768 | tf_op jit(solution)/shard_map/ppermute | solution.py:1093
  253.2 6.8 %collective-permute-done.60.refs_8_.refs_1_ = bf16[208,896]{1,0:T(8,128)(2,1)S(1)} collective-permute-done((bf16[208,896]{1,0:T(8,128)(2,1)S(1)}, bf16[208,896]{1,0:T(8,128)(2,1)S(1)}, u32[]{:S(2)}, u32[]{:S(2)}) %collective-permute-start.60) | collective-permute-done | bytes 372768 | tf_op jit(solution)/shard_map/ppermute | solution.py:1093
  262.8 4.1 %update_in.1 = (f32[192,2,768]{2,1,0:T(2,128)}, f32[192,2,768]{2,1,0:T(2,128)}) custom-call(f32[192,2,768]{2,1,0:T(2,128)} %w_ref.2, f32[192,2,768]{2,1,0:T(2,128)} %m_ref.2, bf16[192,768]{1,0:T(8,128)(2,1)S(1)} %copy-done.9, bf16[192,1536]{1,0:T(8,128)(2,1)S(1)} %collective-permute-done.56.refs_1_, bf16[192,768]{1,0:T(8,128)(2,1)S(1)} %collective-permute-done.51.refs_2_, ...), custom_call_target="tpu_custom_call" | custom-call | flops 100000000 | bytes 200000 | tf_op jit(solution)/shard_map/update_in/pallas_call | solution.py:988
  270.7 1.9 join_rows.1
  (310 shorter events, 39.8 us)
Async XLA Ops:
  3.6 21.8 %collective-permute-start.3 = (bf16[192,896]{1,0:T(8,128)(2,1)S(1)}, bf16[192,896]{1,0:T(8,128)(2,1)}, u32[]{:S(2)}, u32[]{:S(2)}) collective-permute-start(bf16[192,896]{1,0:T(8,128)(2,1)S(1)} %pack.1.refs_0_), channel_id=1, source_target_pairs={{24,0},{28,4},{0,8},{4,12},{8,16},{12,20},{16,24},{20,28},{25,1},{... | collective-permute-start | bytes 1032200 | tf_op jit(solution)/shard_map/ppermute | solution.py:1093
  6.6 17.9 %collective-permute-start.1 = (bf16[192,896]{1,0:T(8,128)(2,1)S(1)}, bf16[192,896]{1,0:T(8,128)(2,1)}, u32[]{:S(2)}, u32[]{:S(2)}) collective-permute-start(bf16[192,896]{1,0:T(8,128)(2,1)S(1)} %pack.1.refs_0_), channel_id=1, source_target_pairs={{4,0},{0,4},{12,8},{8,12},{20,16},{16,20},{28,24},{24,28},{5,1},{1... | collective-permute-start | bytes 1032200 | tf_op jit(solution)/shard_map/ppermute | solution.py:1102
  8.1 17.8 %collective-permute-start = (bf16[192,896]{1,0:T(8,128)(2,1)S(1)}, bf16[192,896]{1,0:T(8,128)(2,1)}, u32[]{:S(2)}, u32[]{:S(2)}) collective-permute-start(bf16[192,896]{1,0:T(8,128)(2,1)S(1)} %pack.1.refs_0_), channel_id=1, source_target_pairs={{8,0},{12,4},{16,8},{20,12},{24,16},{28,20},{0,24},{4,28},{9,1},{1... | collective-permute-start | bytes 1032200 | tf_op jit(solution)/shard_map/ppermute | solution.py:1093
  10.4 32.8 %collective-permute-start.6 = (bf16[1024,384]{1,0:T(8,128)(2,1)}, bf16[1024,384]{1,0:T(8,128)(2,1)}, u32[]{:S(2)}, u32[]{:S(2)}) collective-permute-start(bf16[1024,384]{1,0:T(8,128)(2,1)} %refs_0_.1), channel_id=1, source_target_pairs={{2,0},{3,1},{0,2},{1,3},{6,4},{7,5},{4,6},{5,7},{10,8},{11,9},{8,1... | collective-permute-start | bytes 2359304 | tf_op jit(solution)/shard_map/ppermute | solution.py:1106
  11.9 35.8 %collective-permute-start.11 = (bf16[1024,384]{1,0:T(8,128)(2,1)}, bf16[1024,384]{1,0:T(8,128)(2,1)}, u32[]{:S(2)}, u32[]{:S(2)}) collective-permute-start(bf16[1024,384]{1,0:T(8,128)(2,1)} %refs_0_.1), channel_id=1, source_target_pairs={{1,0},{0,1},{3,2},{2,3},{5,4},{4,5},{7,6},{6,7},{9,8},{8,9},{11,10... | collective-permute-start | bytes 2359304 | tf_op jit(solution)/shard_map/ppermute | solution.py:1106
  24.5 18.0 %collective-permute-start.2 = (bf16[192,896]{1,0:T(8,128)(2,1)S(1)}, bf16[192,896]{1,0:T(8,128)(2,1)S(1)}, u32[]{:S(2)}, u32[]{:S(2)}) collective-permute-start(bf16[192,896]{1,0:T(8,128)(2,1)S(1)} %pack.1.refs_0_), channel_id=1, source_target_pairs={{16,0},{20,4},{24,8},{28,12},{0,16},{4,20},{8,24},{12,28},{17,1},{... | collective-permute-start | bytes 1032200 | tf_op jit(solution)/shard_map/ppermute | solution.py:1093
  25.4 11.1 %collective-permute-start.5 = (bf16[192,896]{1,0:T(8,128)(2,1)}, bf16[192,896]{1,0:T(8,128)(2,1)S(1)}, u32[]{:S(2)}, u32[]{:S(2)}) collective-permute-start(bf16[192,896]{1,0:T(8,128)(2,1)} %collective-permute-done.3.refs_3_), channel_id=1, source_target_pairs={{4,0},{0,4},{12,8},{8,12},{20,16},{16,20},{28,24},{24,28},{5,1},{1... | collective-permute-start | bytes 1032200 | tf_op jit(solution)/shard_map/ppermute | solution.py:1102
  25.9 17.2 %collective-permute-start.4 = (bf16[192,896]{1,0:T(8,128)(2,1)}, bf16[192,896]{1,0:T(8,128)(2,1)S(1)}, u32[]{:S(2)}, u32[]{:S(2)}) collective-permute-start(bf16[192,896]{1,0:T(8,128)(2,1)} %collective-permute-done.refs_2_), channel_id=1, source_target_pairs={{4,0},{0,4},{12,8},{8,12},{20,16},{16,20},{28,24},{24,28},{5,1},{1... | collective-permute-start | bytes 1032200 | tf_op jit(solution)/shard_map/ppermute | solution.py:1102
  43.2 6.0 %collective-permute-start.12 = (bf16[1024,384]{1,0:T(8,128)(2,1)}, bf16[1024,384]{1,0:T(8,128)(2,1)S(1)}, u32[]{:S(2)}, u32[]{:S(2)}) collective-permute-start(bf16[1024,384]{1,0:T(8,128)(2,1)} %collective-permute-done.6.refs_2_), channel_id=1, source_target_pairs={{1,0},{0,1},{3,2},{2,3},{5,4},{4,5},{7,6},{6,7},{9,8},{8,9},{11,10... | collective-permute-start | bytes 2359304 | tf_op jit(solution)/shard_map/ppermute | solution.py:1106
  43.3 10.1 %collective-permute-start.9 = (bf16[192,768]{1,0:T(8,128)(2,1)}, bf16[192,768]{1,0:T(8,128)(2,1)S(1)}, u32[]{:S(2)}, u32[]{:S(2)}) collective-permute-start(bf16[192,768]{1,0:T(8,128)(2,1)} %pack_gate.1.refs_0_), channel_id=1, source_target_pairs={{4,0},{0,4},{12,8},{8,12},{20,16},{16,20},{28,24},{24,28},{5,1},{1... | collective-permute-start | bytes 884744 | tf_op jit(solution)/shard_map/ppermute | solution.py:1102
  43.9 11.9 %collective-permute-start.8 = (bf16[192,768]{1,0:T(8,128)(2,1)}, bf16[192,768]{1,0:T(8,128)(2,1)S(1)}, u32[]{:S(2)}, u32[]{:S(2)}) collective-permute-start(bf16[192,768]{1,0:T(8,128)(2,1)} %pack_gate.1.refs_0_), channel_id=1, source_target_pairs={{24,0},{28,4},{0,8},{4,12},{8,16},{12,20},{16,24},{20,28},{25,1},{... | collective-permute-start | bytes 884744 | tf_op jit(solution)/shard_map/ppermute | solution.py:1093
  45.4 15.4 %collective-permute-start.7 = (bf16[192,768]{1,0:T(8,128)(2,1)}, bf16[192,768]{1,0:T(8,128)(2,1)S(1)}, u32[]{:S(2)}, u32[]{:S(2)}) collective-permute-start(bf16[192,768]{1,0:T(8,128)(2,1)} %pack_gate.1.refs_0_), channel_id=1, source_target_pairs={{8,0},{12,4},{16,8},{20,12},{24,16},{28,20},{0,24},{4,28},{9,1},{1... | collective-permute-start | bytes 884744 | tf_op jit(solution)/shard_map/ppermute | solution.py:1093
  47.7 13.1 %collective-permute-start.10 = (bf16[192,896]{1,0:T(8,128)(2,1)S(1)}, bf16[192,896]{1,0:T(8,128)(2,1)S(1)}, u32[]{:S(2)}, u32[]{:S(2)}) collective-permute-start(bf16[192,896]{1,0:T(8,128)(2,1)S(1)} %collective-permute-done.2.refs_4_), channel_id=1, source_target_pairs={{4,0},{0,4},{12,8},{8,12},{20,16},{16,20},{28,24},{24,28},{5,1},{1... | collective-permute-start | bytes 1032200 | tf_op jit(solution)/shard_map/ppermute | solution.py:1102
  60.8 16.5 %collective-permute-start.16 = (bf16[192,768]{1,0:T(8,128)(2,1)}, bf16[192,768]{1,0:T(8,128)(2,1)S(1)}, u32[]{:S(2)}, u32[]{:S(2)}) collective-permute-start(bf16[192,768]{1,0:T(8,128)(2,1)} %convert_bitcast_fusion.refs_0_), channel_id=1, source_target_pairs={{4,0},{0,4},{12,8},{8,12},{20,16},{16,20},{28,24},{24,28},{5,1},{1... | collective-permute-start | bytes 884744 | tf_op jit(solution)/shard_map/ppermute | solution.py:1102
  62.3 15.0 %collective-permute-start.15 = (bf16[192,768]{1,0:T(8,128)(2,1)S(1)}, bf16[192,768]{1,0:T(8,128)(2,1)S(1)}, u32[]{:S(2)}, u32[]{:S(2)}) collective-permute-start(bf16[192,768]{1,0:T(8,128)(2,1)S(1)} %collective-permute-done.7.refs_2_), channel_id=1, source_target_pairs={{4,0},{0,4},{12,8},{8,12},{20,16},{16,20},{28,24},{24,28},{5,1},{1... | collective-permute-start | bytes 884744 | tf_op jit(solution)/shard_map/ppermute | solution.py:1102
  62.9 15.1 %collective-permute-start.14 = (bf16[192,768]{1,0:T(8,128)(2,1)S(1)}, bf16[192,768]{1,0:T(8,128)(2,1)S(1)}, u32[]{:S(2)}, u32[]{:S(2)}) collective-permute-start(bf16[192,768]{1,0:T(8,128)(2,1)S(1)} %copy-done.10), channel_id=1, source_target_pairs={{16,0},{20,4},{24,8},{28,12},{0,16},{4,20},{8,24},{12,28},{17,1},{... | collective-permute-start | bytes 884744 | tf_op jit(solution)/shard_map/ppermute | solution.py:1093
  68.3 6.2 %collective-permute-start.13 = (bf16[64,1024]{1,0:T(8,128)(2,1)S(1)}, bf16[64,1024]{1,0:T(8,128)(2,1)S(1)}, u32[]{:S(2)}, u32[]{:S(2)}) collective-permute-start(bf16[64,1024]{1,0:T(8,128)(2,1)S(1)} %get-tuple-element.318.refs_0_), channel_id=1, source_target_pairs={{2,0},{3,1},{0,2},{1,3},{6,4},{7,5},{4,6},{5,7},{10,8},{11,9},{8,1... | collective-permute-start | bytes 393224 | tf_op jit(solution)/shard_map/ppermute | solution.py:1106
  68.8 6.2 %collective-permute-start.17 = (bf16[64,1024]{1,0:T(8,128)(2,1)S(1)}, bf16[64,1024]{1,0:T(8,128)(2,1)S(1)}, u32[]{:S(2)}, u32[]{:S(2)}) collective-permute-start(bf16[64,1024]{1,0:T(8,128)(2,1)S(1)} %get-tuple-element.318.refs_0_), channel_id=1, source_target_pairs={{1,0},{0,1},{3,2},{2,3},{5,4},{4,5},{7,6},{6,7},{9,8},{8,9},{11,10... | collective-permute-start | bytes 393224 | tf_op jit(solution)/shard_map/ppermute | solution.py:1106
  77.9 20.1 %collective-permute-start.22 = (bf16[192,768]{1,0:T(8,128)(2,1)}, bf16[192,768]{1,0:T(8,128)(2,1)S(1)}, u32[]{:S(2)}, u32[]{:S(2)}) collective-permute-start(bf16[192,768]{1,0:T(8,128)(2,1)} %convert_bitcast_fusion.refs_0_), channel_id=1, source_target_pairs={{24,0},{28,4},{0,8},{4,12},{8,16},{12,20},{16,24},{20,28},{25,1},{... | collective-permute-start | bytes 884744 | tf_op jit(solution)/shard_map/ppermute | solution.py:1093
  78.4 19.6 %collective-permute-start.21 = (bf16[192,768]{1,0:T(8,128)(2,1)}, bf16[192,768]{1,0:T(8,128)(2,1)S(1)}, u32[]{:S(2)}, u32[]{:S(2)}) collective-permute-start(bf16[192,768]{1,0:T(8,128)(2,1)} %convert_bitcast_fusion.refs_0_), channel_id=1, source_target_pairs={{8,0},{12,4},{16,8},{20,12},{24,16},{28,20},{0,24},{4,28},{9,1},{1... | collective-permute-start | bytes 884744 | tf_op jit(solution)/shard_map/ppermute | solution.py:1093
  81.8 16.2 %collective-permute-start.19 = (bf16[192,768]{1,0:T(8,128)(2,1)S(1)}, bf16[192,768]{1,0:T(8,128)(2,1)S(1)}, u32[]{:S(2)}, u32[]{:S(2)}) collective-permute-start(bf16[192,768]{1,0:T(8,128)(2,1)S(1)} %collective-permute-done.14.refs_4_), channel_id=1, source_target_pairs={{4,0},{0,4},{12,8},{8,12},{20,16},{16,20},{28,24},{24,28},{5,1},{1... | collective-permute-start | bytes 884744 | tf_op jit(solution)/shard_map/ppermute | solution.py:1102
  83.3 14.8 %collective-permute-start.20 = (bf16[192,768]{1,0:T(8,128)(2,1)S(1)}, bf16[192,768]{1,0:T(8,128)(2,1)S(1)}, u32[]{:S(2)}, u32[]{:S(2)}) collective-permute-start(bf16[192,768]{1,0:T(8,128)(2,1)S(1)} %collective-permute-done.8.refs_3_), channel_id=1, source_target_pairs={{4,0},{0,4},{12,8},{8,12},{20,16},{16,20},{28,24},{24,28},{5,1},{1... | collective-permute-start | bytes 884744 | tf_op jit(solution)/shard_map/ppermute | solution.py:1102
  98.0 13.6 %collective-permute-start.27 = (bf16[192,768]{1,0:T(8,128)(2,1)S(1)}, bf16[192,768]{1,0:T(8,128)(2,1)S(1)}, u32[]{:S(2)}, u32[]{:S(2)}) collective-permute-start(bf16[192,768]{1,0:T(8,128)(2,1)S(1)} %collective-permute-done.21.refs_2_), channel_id=1, source_target_pairs={{4,0},{0,4},{12,8},{8,12},{20,16},{16,20},{28,24},{24,28},{5,1},{1... | collective-permute-start | bytes 884744 | tf_op jit(solution)/shard_map/ppermute | solution.py:1102
  99.6 13.4 %collective-permute-start.26 = (bf16[192,768]{1,0:T(8,128)(2,1)}, bf16[192,768]{1,0:T(8,128)(2,1)S(1)}, u32[]{:S(2)}, u32[]{:S(2)}) collective-permute-start(bf16[192,768]{1,0:T(8,128)(2,1)} %convert_bitcast_fusion.refs_0_), channel_id=1, source_target_pairs={{16,0},{20,4},{24,8},{28,12},{0,16},{4,20},{8,24},{12,28},{17,1},{... | collective-permute-start | bytes 884744 | tf_op jit(solution)/shard_map/ppermute | solution.py:1093
  99.6 13.4 %collective-permute-start.28 = (bf16[192,768]{1,0:T(8,128)(2,1)S(1)}, bf16[192,768]{1,0:T(8,128)(2,1)S(1)}, u32[]{:S(2)}, u32[]{:S(2)}) collective-permute-start(bf16[192,768]{1,0:T(8,128)(2,1)S(1)} %collective-permute-done.22.refs_3_), channel_id=1, source_target_pairs={{4,0},{0,4},{12,8},{8,12},{20,16},{16,20},{28,24},{24,28},{5,1},{1... | collective-permute-start | bytes 884744 | tf_op jit(solution)/shard_map/ppermute | solution.py:1102
  107.1 3.3 %collective-permute-start.25 = (f32[8,1024]{1,0:T(8,128)S(1)}, f32[8,1024]{1,0:T(8,128)S(1)}, u32[]{:S(2)}, u32[]{:S(2)}) collective-permute-start(f32[8,1024]{1,0:T(8,128)S(1)} %get-tuple-element.362), channel_id=1, source_target_pairs={{3,0},{2,1},{1,2},{0,3},{7,4},{6,5},{5,6},{4,7},{11,8},{10,9},{9,1... | collective-permute-start | bytes 98312 | tf_op jit(solution)/shard_map/ppermute | solution.py:1106
  107.1 4.2 %collective-permute-start.24 = (f32[8,1024]{1,0:T(8,128)S(1)}, f32[8,1024]{1,0:T(8,128)S(1)}, u32[]{:S(2)}, u32[]{:S(2)}) collective-permute-start(f32[8,1024]{1,0:T(8,128)S(1)} %get-tuple-element.362), channel_id=1, source_target_pairs={{2,0},{3,1},{0,2},{1,3},{6,4},{7,5},{4,6},{5,7},{10,8},{11,9},{8,1... | collective-permute-start | bytes 98312 | tf_op jit(solution)/shard_map/ppermute | solution.py:1106
  113.0 8.9 %collective-permute-start.29 = (bf16[192,768]{1,0:T(8,128)(2,1)S(1)}, bf16[192,768]{1,0:T(8,128)(2,1)S(1)}, u32[]{:S(2)}, u32[]{:S(2)}) collective-permute-start(bf16[192,768]{1,0:T(8,128)(2,1)S(1)} %collective-permute-done.26.refs_4_), channel_id=1, source_target_pairs={{4,0},{0,4},{12,8},{8,12},{20,16},{16,20},{28,24},{24,28},{5,1},{1... | collective-permute-start | bytes 884744 | tf_op jit(solution)/shard_map/ppermute | solution.py:1102
  113.6 8.1 %collective-permute-start.30 = (bf16[64,1536]{1,0:T(8,128)(2,1)}, bf16[64,1536]{1,0:T(8,128)(2,1)S(1)}, u32[]{:S(2)}, u32[]{:S(2)}) collective-permute-start(bf16[64,1536]{1,0:T(8,128)(2,1)} %get-tuple-element.473.refs_0_), channel_id=1, source_target_pairs={{2,0},{3,1},{0,2},{1,3},{6,4},{7,5},{4,6},{5,7},{10,8},{11,9},{8,1... | collective-permute-start | bytes 589832 | tf_op jit(solution)/shard_map/ppermute | solution.py:1106
  122.0 14.2 %collective-permute-start.35 = (bf16[192,768]{1,0:T(8,128)(2,1)}, bf16[192,768]{1,0:T(8,128)(2,1)S(1)}, u32[]{:S(2)}, u32[]{:S(2)}) collective-permute-start(bf16[192,768]{1,0:T(8,128)(2,1)} %get-tuple-element.402), channel_id=1, source_target_pairs={{4,0},{0,4},{12,8},{8,12},{20,16},{16,20},{28,24},{24,28},{5,1},{1... | collective-permute-start | bytes 884744 | tf_op jit(solution)/shard_map/ppermute | solution.py:1102
  128.1 8.0 %collective-permute-start.34 = (f32[8,1024]{1,0:T(8,128)S(1)}, f32[8,1024]{1,0:T(8,128)S(1)}, u32[]{:S(2)}, u32[]{:S(2)}) collective-permute-start(f32[8,1024]{1,0:T(8,128)S(1)} %get-tuple-element.392), channel_id=1, source_target_pairs={{3,0},{2,1},{1,2},{0,3},{7,4},{6,5},{5,6},{4,7},{11,8},{10,9},{9,1... | collective-permute-start | bytes 98312 | tf_op jit(solution)/shard_map/ppermute | solution.py:1106
  128.2 8.0 %collective-permute-start.33 = (f32[8,1024]{1,0:T(8,128)S(1)}, f32[8,1024]{1,0:T(8,128)S(1)}, u32[]{:S(2)}, u32[]{:S(2)}) collective-permute-start(f32[8,1024]{1,0:T(8,128)S(1)} %get-tuple-element.392), channel_id=1, source_target_pairs={{2,0},{3,1},{0,2},{1,3},{6,4},{7,5},{4,6},{5,7},{10,8},{11,9},{8,1... | collective-permute-start | bytes 98312 | tf_op jit(solution)/shard_map/ppermute | solution.py:1106
  129.0 7.2 %collective-permute-start.32 = (f32[8,1024]{1,0:T(8,128)S(1)}, f32[8,1024]{1,0:T(8,128)S(1)}, u32[]{:S(2)}, u32[]{:S(2)}) collective-permute-start(f32[8,1024]{1,0:T(8,128)S(1)} %get-tuple-element.392), channel_id=1, source_target_pairs={{1,0},{0,1},{3,2},{2,3},{5,4},{4,5},{7,6},{6,7},{9,8},{8,9},{11,10... | collective-permute-start | bytes 98312 | tf_op jit(solution)/shard_map/ppermute | solution.py:1106
  136.2 16.4 %collective-permute-start.39 = (bf16[1024,384]{1,0:T(8,128)(2,1)}, bf16[1024,384]{1,0:T(8,128)(2,1)}, u32[]{:S(2)}, u32[]{:S(2)}) collective-permute-start(bf16[1024,384]{1,0:T(8,128)(2,1)} %get-tuple-element.406), channel_id=1, source_target_pairs={{1,0},{0,1},{3,2},{2,3},{5,4},{4,5},{7,6},{6,7},{9,8},{8,9},{11,10... | collective-permute-start | bytes 2359304 | tf_op jit(solution)/shard_map/ppermute | solution.py:1106
  136.3 15.8 %collective-permute-start.31 = (bf16[384,768]{1,0:T(8,128)(2,1)S(1)}, bf16[384,768]{1,0:T(8,128)(2,1)}, u32[]{:S(2)}, u32[]{:S(2)}) collective-permute-start(bf16[384,768]{1,0:T(8,128)(2,1)S(1)} %copy-done.63), channel_id=1, source_target_pairs={{4,0},{0,4},{12,8},{8,12},{20,16},{16,20},{28,24},{24,28},{5,1},{1... | collective-permute-start | bytes 1769480 | tf_op jit(solution)/shard_map/ppermute | solution.py:1102
  137.3 15.3 %collective-permute-start.36 = (bf16[192,768]{1,0:T(8,128)(2,1)S(1)}, bf16[192,768]{1,0:T(8,128)(2,1)}, u32[]{:S(2)}, u32[]{:S(2)}) collective-permute-start(bf16[192,768]{1,0:T(8,128)(2,1)S(1)} %add_convert_fusion.11), channel_id=1, source_target_pairs={{16,0},{20,4},{24,8},{28,12},{0,16},{4,20},{8,24},{12,28},{17,1},{... | collective-permute-start | bytes 884744 | tf_op jit(solution)/shard_map/ppermute | solution.py:1093
  139.0 12.1 %collective-permute-start.37 = (bf16[64,1536]{1,0:T(8,128)(2,1)}, bf16[64,1536]{1,0:T(8,128)(2,1)S(1)}, u32[]{:S(2)}, u32[]{:S(2)}) collective-permute-start(bf16[64,1536]{1,0:T(8,128)(2,1)} %get-tuple-element.473.refs_0_), channel_id=1, source_target_pairs={{1,0},{0,1},{3,2},{2,3},{5,4},{4,5},{7,6},{6,7},{9,8},{8,9},{11,10... | collective-permute-start | bytes 589832 | tf_op jit(solution)/shard_map/ppermute | solution.py:1106
  139.0 12.1 %collective-permute-start.38 = (bf16[64,1536]{1,0:T(8,128)(2,1)S(1)}, bf16[64,1536]{1,0:T(8,128)(2,1)S(1)}, u32[]{:S(2)}, u32[]{:S(2)}) collective-permute-start(bf16[64,1536]{1,0:T(8,128)(2,1)S(1)} %collective-permute-done.30.refs_2_), channel_id=1, source_target_pairs={{1,0},{0,1},{3,2},{2,3},{5,4},{4,5},{7,6},{6,7},{9,8},{8,9},{11,10... | collective-permute-start | bytes 589832 | tf_op jit(solution)/shard_map/ppermute | solution.py:1106
  155.5 26.3 %collective-permute-start.40 = (bf16[192,768]{1,0:T(8,128)(2,1)S(1)}, bf16[192,768]{1,0:T(8,128)(2,1)S(1)}, u32[]{:S(2)}, u32[]{:S(2)}) collective-permute-start(bf16[192,768]{1,0:T(8,128)(2,1)S(1)} %get-tuple-element.431), channel_id=1, source_target_pairs={{24,0},{28,4},{0,8},{4,12},{8,16},{12,20},{16,24},{20,28},{25,1},{... | collective-permute-start | bytes 884744 | tf_op jit(solution)/shard_map/ppermute | solution.py:1093
  155.6 26.2 %collective-permute-start.41 = (bf16[192,768]{1,0:T(8,128)(2,1)S(1)}, bf16[192,768]{1,0:T(8,128)(2,1)S(1)}, u32[]{:S(2)}, u32[]{:S(2)}) collective-permute-start(bf16[192,768]{1,0:T(8,128)(2,1)S(1)} %get-tuple-element.432), channel_id=1, source_target_pairs={{8,0},{12,4},{16,8},{20,12},{24,16},{28,20},{0,24},{4,28},{9,1},{1... | collective-permute-start | bytes 884744 | tf_op jit(solution)/shard_map/ppermute | solution.py:1093
  159.4 22.4 %collective-permute-start.43 = (bf16[1024,384]{1,0:T(8,128)(2,1)S(1)}, bf16[1024,384]{1,0:T(8,128)(2,1)S(1)}, u32[]{:S(2)}, u32[]{:S(2)}) collective-permute-start(bf16[1024,384]{1,0:T(8,128)(2,1)S(1)} %add_convert_fusion.2), channel_id=1, source_target_pairs={{2,0},{3,1},{0,2},{1,3},{6,4},{7,5},{4,6},{5,7},{10,8},{11,9},{8,1... | collective-permute-start | bytes 2359304 | tf_op jit(solution)/shard_map/ppermute | solution.py:1106
  160.5 27.9 %collective-permute-start.45 = (bf16[1024,384]{1,0:T(8,128)(2,1)S(1)}, bf16[1024,384]{1,0:T(8,128)(2,1)S(1)}, u32[]{:S(2)}, u32[]{:S(2)}) collective-permute-start(bf16[1024,384]{1,0:T(8,128)(2,1)S(1)} %copy-done.62), channel_id=1, source_target_pairs={{1,0},{0,1},{3,2},{2,3},{5,4},{4,5},{7,6},{6,7},{9,8},{8,9},{11,10... | collective-permute-start | bytes 2359304 | tf_op jit(solution)/shard_map/ppermute | solution.py:1106
  160.5 22.3 %collective-permute-start.42 = (bf16[576,768]{1,0:T(8,128)(2,1)}, bf16[576,768]{1,0:T(8,128)(2,1)S(1)}, u32[]{:S(2)}, u32[]{:S(2)}) collective-permute-start(bf16[576,768]{1,0:T(8,128)(2,1)} %get-tuple-element.434), channel_id=1, source_target_pairs={{4,0},{0,4},{12,8},{8,12},{20,16},{16,20},{28,24},{24,28},{5,1},{1... | collective-permute-start | bytes 2654216 | tf_op jit(solution)/shard_map/ppermute | solution.py:1102
  182.8 5.6 %collective-permute-start.44 = (bf16[128,1024]{1,0:T(8,128)(2,1)}, bf16[128,1024]{1,0:T(8,128)(2,1)S(1)}, u32[]{:S(2)}, u32[]{:S(2)}) collective-permute-start(bf16[128,1024]{1,0:T(8,128)(2,1)} %get-tuple-element.462), channel_id=1, source_target_pairs={{1,0},{0,1},{3,2},{2,3},{5,4},{4,5},{7,6},{6,7},{9,8},{8,9},{11,10... | collective-permute-start | bytes 786440 | tf_op jit(solution)/shard_map/ppermute | solution.py:1106
  182.9 15.0 %collective-permute-start.47 = (bf16[192,768]{1,0:T(8,128)(2,1)S(1)}, bf16[192,768]{1,0:T(8,128)(2,1)S(1)}, u32[]{:S(2)}, u32[]{:S(2)}) collective-permute-start(bf16[192,768]{1,0:T(8,128)(2,1)S(1)} %add_convert_fusion.8), channel_id=1, source_target_pairs={{16,0},{20,4},{24,8},{28,12},{0,16},{4,20},{8,24},{12,28},{17,1},{... | collective-permute-start | bytes 884744 | tf_op jit(solution)/shard_map/ppermute | solution.py:1093
  188.5 9.4 %collective-permute-start.46 = (bf16[64,1024]{1,0:T(8,128)(2,1)S(1)}, bf16[64,1024]{1,0:T(8,128)(2,1)S(1)}, u32[]{:S(2)}, u32[]{:S(2)}) collective-permute-start(bf16[64,1024]{1,0:T(8,128)(2,1)S(1)} %slice.312), channel_id=1, source_target_pairs={{2,0},{3,1},{0,2},{1,3},{6,4},{7,5},{4,6},{5,7},{10,8},{11,9},{8,1... | collective-permute-start | bytes 393224 | tf_op jit(solution)/shard_map/ppermute | solution.py:1106
  189.5 22.0 %collective-permute-start.49 = (bf16[576,768]{1,0:T(8,128)(2,1)}, bf16[576,768]{1,0:T(8,128)(2,1)S(1)}, u32[]{:S(2)}, u32[]{:S(2)}) collective-permute-start(bf16[576,768]{1,0:T(8,128)(2,1)} %get-tuple-element.489), channel_id=1, source_target_pairs={{4,0},{0,4},{12,8},{8,12},{20,16},{16,20},{28,24},{24,28},{5,1},{1... | collective-permute-start | bytes 2654216 | tf_op jit(solution)/shard_map/ppermute | solution.py:1102
  197.9 13.6 %collective-permute-start.48 = (bf16[256,1536]{1,0:T(8,128)(2,1)S(1)}, bf16[256,1536]{1,0:T(8,128)(2,1)S(1)}, u32[]{:S(2)}, u32[]{:S(2)}) collective-permute-start(bf16[256,1536]{1,0:T(8,128)(2,1)S(1)} %get-tuple-element.484), channel_id=1, source_target_pairs={{1,0},{0,1},{3,2},{2,3},{5,4},{4,5},{7,6},{6,7},{9,8},{8,9},{11,10... | collective-permute-start | bytes 2359304 | tf_op jit(solution)/shard_map/ppermute | solution.py:1106
  198.2 13.8 %collective-permute-start.52 = (bf16[192,768]{1,0:T(8,128)(2,1)S(1)}, bf16[192,768]{1,0:T(8,128)(2,1)S(1)}, u32[]{:S(2)}, u32[]{:S(2)}) collective-permute-start(bf16[192,768]{1,0:T(8,128)(2,1)S(1)} %get-tuple-element.572), channel_id=1, source_target_pairs={{8,0},{12,4},{16,8},{20,12},{24,16},{28,20},{0,24},{4,28},{9,1},{1... | collective-permute-start | bytes 884744 | tf_op jit(solution)/shard_map/ppermute | solution.py:1093
  200.1 16.2 %collective-permute-start.51 = (bf16[192,768]{1,0:T(8,128)(2,1)S(1)}, bf16[192,768]{1,0:T(8,128)(2,1)S(1)}, u32[]{:S(2)}, u32[]{:S(2)}) collective-permute-start(bf16[192,768]{1,0:T(8,128)(2,1)S(1)} %get-tuple-element.573), channel_id=1, source_target_pairs={{24,0},{28,4},{0,8},{4,12},{8,16},{12,20},{16,24},{20,28},{25,1},{... | collective-permute-start | bytes 884744 | tf_op jit(solution)/shard_map/ppermute | solution.py:1093
  211.5 4.8 %collective-permute-start.50 = (bf16[256,1536]{1,0:T(8,128)(2,1)S(1)}, bf16[256,1536]{1,0:T(8,128)(2,1)S(1)}, u32[]{:S(2)}, u32[]{:S(2)}) collective-permute-start(bf16[256,1536]{1,0:T(8,128)(2,1)S(1)} %get-tuple-element.493), channel_id=1, source_target_pairs={{1,0},{0,1},{3,2},{2,3},{5,4},{4,5},{7,6},{6,7},{9,8},{8,9},{11,10... | collective-permute-start | bytes 2359304 | tf_op jit(solution)/shard_map/ppermute | solution.py:1106
  216.3 20.6 %collective-permute-start.53 = (bf16[256,1536]{1,0:T(8,128)(2,1)S(1)}, bf16[256,1536]{1,0:T(8,128)(2,1)S(1)}, u32[]{:S(2)}, u32[]{:S(2)}) collective-permute-start(bf16[256,1536]{1,0:T(8,128)(2,1)S(1)} %add_convert_fusion.1), channel_id=1, source_target_pairs={{2,0},{3,1},{0,2},{1,3},{6,4},{7,5},{4,6},{5,7},{10,8},{11,9},{8,1... | collective-permute-start | bytes 2359304 | tf_op jit(solution)/shard_map/ppermute | solution.py:1106
  217.3 19.6 %collective-permute-start.56 = (bf16[192,1536]{1,0:T(8,128)(2,1)S(1)}, bf16[192,1536]{1,0:T(8,128)(2,1)S(1)}, u32[]{:S(2)}, u32[]{:S(2)}) collective-permute-start(bf16[192,1536]{1,0:T(8,128)(2,1)S(1)} %pad_maximum_fusion), channel_id=1, source_target_pairs={{4,0},{0,4},{12,8},{8,12},{20,16},{16,20},{28,24},{24,28},{5,1},{1... | collective-permute-start | bytes 1769480 | tf_op jit(solution)/shard_map/ppermute | solution.py:1102
  218.1 18.7 %collective-permute-start.55 = (bf16[880,128]{1,0:T(8,128)(2,1)S(1)}, bf16[880,128]{1,0:T(8,128)(2,1)S(1)}, u32[]{:S(2)}, u32[]{:S(2)}) collective-permute-start(bf16[880,128]{1,0:T(8,128)(2,1)S(1)} %pad_maximum_fusion.3), channel_id=1, source_target_pairs={{4,0},{0,4},{12,8},{8,12},{20,16},{16,20},{28,24},{24,28},{5,1},{1... | collective-permute-start | bytes 675848 | tf_op jit(solution)/shard_map/ppermute | solution.py:1102
  219.5 17.4 %collective-permute-start.54 = (bf16[192,768]{1,0:T(8,128)(2,1)S(1)}, bf16[192,768]{1,0:T(8,128)(2,1)S(1)}, u32[]{:S(2)}, u32[]{:S(2)}) collective-permute-start(bf16[192,768]{1,0:T(8,128)(2,1)S(1)} %get-tuple-element.506), channel_id=1, source_target_pairs={{16,0},{20,4},{24,8},{28,12},{0,16},{4,20},{8,24},{12,28},{17,1},{... | collective-permute-start | bytes 884744 | tf_op jit(solution)/shard_map/ppermute | solution.py:1093
  239.3 10.7 %collective-permute-start.62 = (bf16[304,128]{1,0:T(8,128)(2,1)S(1)}, bf16[304,128]{1,0:T(8,128)(2,1)S(1)}, u32[]{:S(2)}, u32[]{:S(2)}) collective-permute-start(bf16[304,128]{1,0:T(8,128)(2,1)S(1)} %pad_maximum_fusion.4), channel_id=1, source_target_pairs={{16,0},{20,4},{24,8},{28,12},{0,16},{4,20},{8,24},{12,28},{17,1},{... | collective-permute-start | bytes 233480 | tf_op jit(solution)/shard_map/ppermute | solution.py:1093
  240.1 9.9 %collective-permute-start.63 = (bf16[192,768]{1,0:T(8,128)(2,1)S(1)}, bf16[192,768]{1,0:T(8,128)(2,1)S(1)}, u32[]{:S(2)}, u32[]{:S(2)}) collective-permute-start(bf16[192,768]{1,0:T(8,128)(2,1)S(1)} %copy-done.64), channel_id=1, source_target_pairs={{4,0},{0,4},{12,8},{8,12},{20,16},{16,20},{28,24},{24,28},{5,1},{1... | collective-permute-start | bytes 884744 | tf_op jit(solution)/shard_map/ppermute | solution.py:1102
  241.4 11.9 %collective-permute-start.61 = (bf16[208,896]{1,0:T(8,128)(2,1)S(1)}, bf16[208,896]{1,0:T(8,128)(2,1)S(1)}, u32[]{:S(2)}, u32[]{:S(2)}) collective-permute-start(bf16[208,896]{1,0:T(8,128)(2,1)S(1)} %get-tuple-element.582), channel_id=1, source_target_pairs={{8,0},{12,4},{16,8},{20,12},{24,16},{28,20},{0,24},{4,28},{9,1},{1... | collective-permute-start | bytes 1118216 | tf_op jit(solution)/shard_map/ppermute | solution.py:1093
  243.0 17.0 %collective-permute-start.60 = (bf16[208,896]{1,0:T(8,128)(2,1)S(1)}, bf16[208,896]{1,0:T(8,128)(2,1)S(1)}, u32[]{:S(2)}, u32[]{:S(2)}) collective-permute-start(bf16[208,896]{1,0:T(8,128)(2,1)S(1)} %get-tuple-element.583), channel_id=1, source_target_pairs={{24,0},{28,4},{0,8},{4,12},{8,16},{12,20},{16,24},{20,28},{25,1},{... | collective-permute-start | bytes 1118216 | tf_op jit(solution)/shard_map/ppermute | solution.py:1093
  243.4 19.2 %collective-permute-start.57 = (bf16[256,1536]{1,0:T(8,128)(2,1)S(1)}, bf16[256,1536]{1,0:T(8,128)(2,1)S(1)}, u32[]{:S(2)}, u32[]{:S(2)}) collective-permute-start(bf16[256,1536]{1,0:T(8,128)(2,1)S(1)} %norm_backward.1.refs_0_), channel_id=1, source_target_pairs={{2,0},{3,1},{0,2},{1,3},{6,4},{7,5},{4,6},{5,7},{10,8},{11,9},{8,1... | collective-permute-start | bytes 2359304 | tf_op jit(solution)/shard_map/ppermute | solution.py:1106
  260.7 7.8 %collective-permute-start.66 = (f32[240,128]{1,0:T(8,128)S(1)}, f32[240,128]{1,0:T(8,128)S(1)}, u32[]{:S(2)}, u32[]{:S(2)}) collective-permute-start(f32[240,128]{1,0:T(8,128)S(1)} %get-tuple-element.556.refs_0_), channel_id=1, source_target_pairs={{3,0},{2,1},{1,2},{0,3},{7,4},{6,5},{5,6},{4,7},{11,8},{10,9},{9,1... | collective-permute-start | bytes 368648 | tf_op jit(solution)/shard_map/ppermute | solution.py:1106
  260.7 7.8 %collective-permute-start.65 = (f32[240,128]{1,0:T(8,128)S(1)}, f32[240,128]{1,0:T(8,128)S(1)}, u32[]{:S(2)}, u32[]{:S(2)}) collective-permute-start(f32[240,128]{1,0:T(8,128)S(1)} %get-tuple-element.556.refs_0_), channel_id=1, source_target_pairs={{2,0},{3,1},{0,2},{1,3},{6,4},{7,5},{4,6},{5,7},{10,8},{11,9},{8,1... | collective-permute-start | bytes 368648 | tf_op jit(solution)/shard_map/ppermute | solution.py:1106
  261.6 7.0 %collective-permute-start.64 = (f32[240,128]{1,0:T(8,128)S(1)}, f32[240,128]{1,0:T(8,128)S(1)}, u32[]{:S(2)}, u32[]{:S(2)}) collective-permute-start(f32[240,128]{1,0:T(8,128)S(1)} %get-tuple-element.556.refs_0_), channel_id=1, source_target_pairs={{1,0},{0,1},{3,2},{2,3},{5,4},{4,5},{7,6},{6,7},{9,8},{8,9},{11,10... | collective-permute-start | bytes 368648 | tf_op jit(solution)/shard_map/ppermute | solution.py:1106
  262.6 5.9 %collective-permute-start.59 = (bf16[256,1536]{1,0:T(8,128)(2,1)S(1)}, bf16[256,1536]{1,0:T(8,128)(2,1)S(1)}, u32[]{:S(2)}, u32[]{:S(2)}) collective-permute-start(bf16[256,1536]{1,0:T(8,128)(2,1)S(1)} %collective-permute-done.57.refs_2_), channel_id=1, source_target_pairs={{1,0},{0,1},{3,2},{2,3},{5,4},{4,5},{7,6},{6,7},{9,8},{8,9},{11,10... | collective-permute-start | bytes 2359304 | tf_op jit(solution)/shard_map/ppermute | solution.py:1106
  (68 other events, 790.6 us)

commit v8 on v7

--- a/solution.py
+++ b/solution.py
@@ -404,7 +404,7 @@
 
 
 TILE = 256
-TILE_D = 384
+TILE_D = 512
 
 
 def fill(dest, pieces, idx_ref):
@@ -1206,7 +1206,7 @@
     split_sizes = (1, 1, n - 1, n - 2, 1)
     width = depth // ranks
 
-    set_a, set_b = pack(in_weight, bc_weight, step_weight.T, rank1), pack_gate(in_weight)
+    set_a = pack(in_weight, bc_weight, step_weight.T, rank1)
     set_c = out_weight.T.astype(bf16)
 
     def blocks(own, z, x):
@@ -1235,7 +1235,8 @@
 
     a_z = outer_all(set_a, near_ks)
     a_x = {0: inner_flip(set_a)}
-    far_a, a_x[0] = fence(set_a, a_x[0])
+    far_a, a_x[0], hidden, segments, in_gate = fence(set_a, a_x[0], hidden, segments, in_weight)
+    set_b = pack_gate(in_gate)
     a_z[far_k] = outer_from(far_a, far_k)
     cot_far = rank_flip(cotangent, 2)
     gain_rows = pad_rows(norm_gain[None])

time: 273 us -> 271 us (level)
  Pallas kernels: 125 us -> 122 us
    ppermute x19, waiting for transfers between devices: 27 us -> 34.5 us  [inner_flip(): lax.ppermute(v, 'dp', [(d ^ 1, d) for d in range(lax.axis_size('dp'))])]
    ppermute x19, waiting for transfers between devices: 30.3 us -> 24.3 us  [outer_from(): lax.ppermute(v, 'dp', [((o + k) % n * 2 + x, o * 2 + x) for o in range(n)...]
    ppermute x19, starting transfers between devices: 26.7 us -> 29.5 us  [outer_from(): lax.ppermute(v, 'dp', [((o + k) % n * 2 + x, o * 2 + x) for o in range(n)...]
  transfers between devices with their start and end apart: 67 -> 67, of which waited for: 21 -> 21; matrix products, arithmetic and copies ran while one was open for 7% -> 5% of each run, Pallas kernels for 43% -> 42%
where the time goes in v8:
time: 271 us; the launch traced here: 270 us
  Pallas kernels  122 us (45%)
  starting transfers between devices  64.2 us (24%)
  waiting for transfers between devices  63.3 us (23%)
  other arithmetic  14.3 us (5%)
  local copies, waits for them, and re-layouts  5.08 us (2%)
    ppermute x19, waiting for transfers between devices, inner_flip(): lax.ppermute(v, 'dp', [(d ^ 1, d) for d in range(lax.axis_size('dp'))])  34.5 us
    ppermute x19, starting transfers between devices, outer_from(): lax.ppermute(v, 'dp', [((o + k) % n * 2 + x, o * 2 + x) for o in range(n)...  29.5 us
    ppermute x19, waiting for transfers between devices, outer_from(): lax.ppermute(v, 'dp', [((o + k) % n * 2 + x, o * 2 + x) for o in range(n)...  24.3 us
    ppermute x19, starting transfers between devices, inner_flip(): lax.ppermute(v, 'dp', [(d ^ 1, d) for d in range(lax.axis_size('dp'))])  19.9 us
    pallas_call x1, Pallas kernels, ssd_backward(): pl.pallas_call(ssd_backward_kernel, grid=(count,), in_specs=[pl.BlockSpec...  19.1 us
    pallas_call x4, Pallas kernels, weight_grad(): pl.pallas_call(functools.partial(weight_grad_kernel, rows=rows, turned=tu...  18 us
    ppermute x29, starting transfers between devices, rank_flip(): lax.ppermute(v, 'mp', [(m ^ bit, m) for m in range(lax.axis_size('mp'))])  14.8 us
    pallas_call x1, Pallas kernels, ssd_forward(): pl.pallas_call(ssd_forward_kernel, grid=(count,), in_specs=common_specs(l...  14.2 us
  transfers between devices with their start and end apart: 67, of which 21 were waited for; matrix products, arithmetic and copies ran while one was open for 5% of the time, Pallas kernels for 42%

profile of v8, /device:TPU:0, one launch (start us, length us, event | category | flops | bytes accessed | tf_op | source)
XLA Modules:
  0.0 270.3 jit_solution(1817434009781780123)
XLA Ops:
  0.7 2.8 %pack.1.refs_0_ = bf16[192,896]{1,0:T(8,128)(2,1)S(1)} custom-call(s32[1]{0:T(128)} %bitcast.rank_ref, f32[192,2,768]{2,1,0:T(2,128)} %w_ref.2, f32[192,256]{1,0:T(8,128)} %w_ref.3, f32[12,192]{1,0:T(8,128)} %bitcast.47), custom_call_target="tpu_custom_call" | custom-call | flops 2000000000 | bytes 4000000 | tf_op jit(solution)/shard_map/pack/pallas_call | solution.py:476
  3.6 3.1 %collective-permute-start.3 = (bf16[192,896]{1,0:T(8,128)(2,1)S(1)}, bf16[192,896]{1,0:T(8,128)(2,1)}, u32[]{:S(2)}, u32[]{:S(2)}) collective-permute-start(bf16[192,896]{1,0:T(8,128)(2,1)S(1)} %pack.1.refs_0_), channel_id=1, source_target_pairs={{24,0},{28,4},{0,8},{4,12},{8,16},{12,20},{16,24},{20,28},{25,1},{... | collective-permute-start | bytes 1032200 | tf_op jit(solution)/shard_map/ppermute | solution.py:1093
  6.7 2.1 collective-permute-start.1
  8.7 1.6 collective-permute-start
  10.4 1.5 collective-permute-start.6
  16.1 2.2 collective-permute-done.refs_1_
  20.6 3.7 %prepare.1 = (bf16[1024,1536]{1,0:T(8,128)(2,1)}, bf16[1536,1024]{1,0:T(8,128)(2,1)}, f32[8,1024]{1,0:T(8,128)S(1)}) custom-call(bf16[1024,1536]{1,0:T(8,128)(2,1)S(1)} %copy-done.1, f32[8,1536]{1,0:T(8,128)S(1)} %copy-done.15), custom_call_target="tpu_custom_call" | custom-call | flops 12000000000 | bytes 24000000 | tf_op jit(solution)/shard_map/prepare/pallas_call | solution.py:440
  24.6 1.5 collective-permute-start.5
  27.5 2.8 %pack_gate.1.refs_0_ = bf16[192,768]{1,0:T(8,128)(2,1)} custom-call(f32[192,2,768]{2,1,0:T(2,128)} %w_ref.2), custom_call_target="tpu_custom_call" | custom-call | flops 2000000000 | bytes 4000000 | tf_op jit(solution)/shard_map/pack_gate/pallas_call | solution.py:495
  30.2 5.6 %collective-permute-done.5.refs_6_ = bf16[192,896]{1,0:T(8,128)(2,1)S(1)} collective-permute-done((bf16[192,896]{1,0:T(8,128)(2,1)}, bf16[192,896]{1,0:T(8,128)(2,1)S(1)}, u32[]{:S(2)}, u32[]{:S(2)}) %collective-permute-start.5) | collective-permute-done | bytes 344096 | tf_op jit(solution)/shard_map/ppermute | solution.py:1102
  35.8 4.5 %collective-permute-done.4.refs_5_ = bf16[192,896]{1,0:T(8,128)(2,1)S(1)} collective-permute-done((bf16[192,896]{1,0:T(8,128)(2,1)}, bf16[192,896]{1,0:T(8,128)(2,1)S(1)}, u32[]{:S(2)}, u32[]{:S(2)}) %collective-permute-start.4) | collective-permute-done | bytes 344096 | tf_op jit(solution)/shard_map/ppermute | solution.py:1102
  40.6 1.5 collective-permute-start.9
  42.1 1.6 collective-permute-start.8
  43.7 2.2 collective-permute-start.7
  46.5 3.4 %join_columns.1 = (bf16[1024,1536]{1,0:T(8,128)(2,1)S(1)}, bf16[1536,1024]{1,0:T(8,128)(2,1)S(1)}) custom-call(s32[1]{0:T(128)} %bitcast.rank_ref, bf16[1024,384]{1,0:T(8,128)(2,1)} %refs_0_.1, bf16[1024,384]{1,0:T(8,128)(2,1)} %collective-permute-done.11.refs_1_, bf16[1024,384]{1,0:T(8,128)(2,1)} %collective-permute-done.6.refs_2_, ...), custom_call_target="tpu_custom_call" | custom-call | flops 12000000000 | bytes 24000000 | tf_op jit(solution)/shard_map/join_columns/pallas_call | solution.py:519
  50.7 3.4 %collective-permute-done.8.refs_3_ = bf16[192,768]{1,0:T(8,128)(2,1)S(1)} collective-permute-done((bf16[192,768]{1,0:T(8,128)(2,1)}, bf16[192,768]{1,0:T(8,128)(2,1)S(1)}, u32[]{:S(2)}, u32[]{:S(2)}) %collective-permute-start.8) | collective-permute-done | bytes 294944 | tf_op jit(solution)/shard_map/ppermute | solution.py:1093
  54.1 5.3 %collective-permute-done.7.refs_2_ = bf16[192,768]{1,0:T(8,128)(2,1)S(1)} collective-permute-done((bf16[192,768]{1,0:T(8,128)(2,1)}, bf16[192,768]{1,0:T(8,128)(2,1)S(1)}, u32[]{:S(2)}, u32[]{:S(2)}) %collective-permute-start.7) | collective-permute-done | bytes 294944 | tf_op jit(solution)/shard_map/ppermute | solution.py:1093
  60.0 1.5 collective-permute-start.15
  61.4 1.5 collective-permute-start.14
  63.0 3.9 %project_small.1 = (f32[128,1024]{1,0:T(8,128)S(1)}, bf16[64,1024]{1,0:T(8,128)(2,1)S(1)}, bf16[1536,128]{1,0:T(8,128)(2,1)}, bf16[64,1536]{1,0:T(8,128)(2,1)}) custom-call(s32[8]{0:T(128)S(1)} %stack.88.idx_ref, bf16[1024,1536]{1,0:T(8,128)(2,1)S(1)} %copy-done.3, bf16[192,896]{1,0:T(8,128)(2,1)S(1)} %pack.1.refs_0_, bf16[192,896]{1,0:T(8,128)(2,1)S(1)} %copy-done.10, ...), custom_call_target="tpu_custom_call" | custom-call | flops 20000000000 | bytes 40000000 | tf_op jit(solution)/shard_map/project_small/pallas_call | solution.py:598
  66.8 1.6 collective-permute-start.13
  68.4 5.7 %project.1 = (f32[1024,768]{1,0:T(8,128)}, bf16[1536,768]{1,0:T(8,128)(2,1)}) custom-call(s32[8]{0:T(128)S(1)} %stack.88.idx_ref, bf16[1024,1536]{1,0:T(8,128)(2,1)S(1)} %copy-done.3, bf16[192,896]{1,0:T(8,128)(2,1)S(1)} %pack.1.refs_0_, bf16[192,896]{1,0:T(8,128)(2,1)S(1)} %copy-done.10, bf16[192,896]{1,0:T(8,128)(2,1)} %collective-permute-done.1.refs_2_, ...), custom_call_target="tpu_custom_call" | custom-call | flops 100000000 | bytes 200000 | tf_op jit(solution)/shard_map/project/pallas_call | solution.py:634
  75.6 1.3 join_small.1
  77.9 3.0 %collective-permute-start.21 = (bf16[192,768]{1,0:T(8,128)(2,1)S(1)}, bf16[192,768]{1,0:T(8,128)(2,1)S(1)}, u32[]{:S(2)}, u32[]{:S(2)}) collective-permute-start(bf16[192,768]{1,0:T(8,128)(2,1)S(1)} %copy-done.14), channel_id=1, source_target_pairs={{8,0},{12,4},{16,8},{20,12},{24,16},{28,20},{0,24},{4,28},{9,1},{1... | collective-permute-start | bytes 884744 | tf_op jit(solution)/shard_map/ppermute | solution.py:1093
  80.9 1.3 collective-permute-start.19
  82.9 14.2 %ssd_forward.1 = (f32[1024,768]{1,0:T(8,128)}, bf16[8,128,768]{2,1,0:T(8,128)(2,1)}, f32[1024,768]{1,0:T(8,128)}, bf16[1024,768]{1,0:T(8,128)(2,1)}, bf16[1024,7...) custom-call(f32[1024,768]{1,0:T(8,128)} %get-tuple-element.341.x_ref, ...), custom_call_target="tpu_custom_call" | custom-call | flops 14000000000 | bytes 40000000 | tf_op jit(solution)/shard_map/ssd_forward/pallas_call | solution.py:293
  97.1 1.3 collective-permute-start.27
  99.2 6.9 %gate_forward.1 = (f32[1024,768]{1,0:T(8,128)S(1)}, f32[8,1024]{1,0:T(8,128)S(1)}, bf16[1536,768]{1,0:T(8,128)(2,1)}) custom-call(s32[8]{0:T(128)S(1)} %stack.88.idx_ref, bf16[1024,1536]{1,0:T(8,128)(2,1)S(1)} %copy-done.3, f32[1024,768]{1,0:T(8,128)} %get-tuple-element.381.mixed_ref, bf16[192,768]{1,0:T(8,128)(2,1)S(1)} %copy-done.12, ...), custom_call_target="tpu_custom_call" | custom-call | flops 100000000 | bytes 200000 | tf_op jit(solution)/shard_map/gate_forward/pallas_call | solution.py:676
  106.1 1.5 collective-permute-start.24
  107.6 2.2 collective-permute-done.25
  111.7 1.2 collective-permute-start.29
  113.4 1.3 gated_norm.1.rhs_ref.lhs_ref
  114.8 5.1 %weight_grad.4 = (bf16[192,768]{1,0:T(8,128)(2,1)}, bf16[192,768]{1,0:T(8,128)(2,1)}, bf16[576,768]{1,0:T(8,128)(2,1)}, bf16[384,768]{1,0:T(8,128)(2,1)}, bf16[192,768]{1,0:T(8,128)(2,1)}) custom-call(s32[8]{0:T(128)S(1)} %stack.88.idx_ref, bf16[1536,1024]{1,0:T(8,128)(2,1)S(1)} %get-tuple-element.382.lhs_ref, bf16[1024,768]{1,0:T(8,128)(2,1)S(1)} %gated_norm.1.rhs_ref.lhs_ref), custom_call_target="tpu_custom_call" | custom-call | flops 100000000 | bytes 200000 | tf_op jit(solution)/shard_map/weight_grad/pallas_call | solution.py:831
  121.7 4.5 %grad_gout.1 = (f32[1024,768]{1,0:T(8,128)S(1)}, f32[8,1024]{1,0:T(8,128)S(1)}, bf16[1536,768]{1,0:T(8,128)(2,1)S(1)}) custom-call(s32[8]{0:T(128)S(1)} %stack.88.idx_ref, bf16[1024,1536]{1,0:T(8,128)(2,1)S(1)} %get-tuple-element.391.cot_ref, f32[1024,768]{1,0:T(8,128)S(1)} %get-tuple-element.380.gate_ref, f32[1024,768]{1,0:T(8,128)S(1)} %copy-done, ...), custom_call_target="tpu_custom_call" | custom-call | flops 20000000000 | bytes 40000000 | tf_op jit(solution)/shard_map/grad_gout/pallas_call | solution.py:742
  126.9 1.3 collective-permute-start.32
  128.1 6.1 %out_partial.1 = (bf16[1024,384]{1,0:T(8,128)(2,1)}, bf16[1024,384]{1,0:T(8,128)(2,1)}, bf16[1024,384]{1,0:T(8,128)(2,1)}, bf16[1024,384]{1,0:T(8,128)(2,1)}) custom-call(s32[1]{0:T(128)} %bitcast.rank_ref, bf16[1024,768]{1,0:T(8,128)(2,1)S(1)} %gated_norm.1.rhs_ref.lhs_ref, bf16[1536,768]{1,0:T(8,128)(2,1)S(1)} %get-tuple-element.401.w_ref), custom_call_target="tpu_custom_call" | custom-call | flops 100000000 | bytes 200000 | tf_op jit(solution)/shard_map/out_partial/pallas_call | solution.py:861
  135.4 2.6 collective-permute-start.36
  138.7 6.1 %gate_backward.1 = (bf16[1024,768]{1,0:T(8,128)(2,1)S(1)}, bf16[1024,768]{1,0:T(8,128)(2,1)S(1)}, f32[8,768]{1,0:T(8,128)S(1)}) custom-call(f32[1024,768]{1,0:T(8,128)} %copy-done.4, f32[1024,768]{1,0:T(8,128)} %copy-done.6, f32[1024,768]{1,0:T(8,128)} %get-tuple-element.381.mixed_ref, f32[8,1024]{1,0:T(8,128)S(1)} %add_add_fusion.1.square_ref, ...), custom_call_target="tpu_custom_call" | custom-call | flops 100000000 | bytes 200000 | tf_op jit(solution)/shard_map/gate_backward/pallas_call | solution.py:793
  144.8 5.1 %weight_grad.5 = (bf16[192,768]{1,0:T(8,128)(2,1)}, bf16[192,768]{1,0:T(8,128)(2,1)}, bf16[576,768]{1,0:T(8,128)(2,1)}, bf16[576,768]{1,0:T(8,128)(2,1)}) custom-call(s32[8]{0:T(128)S(1)} %stack.88.idx_ref, bf16[1536,1024]{1,0:T(8,128)(2,1)S(1)} %copy-done.2, bf16[1024,768]{1,0:T(8,128)(2,1)S(1)} %get-tuple-element.417.rhs_ref.gg_ref), custom_call_target="tpu_custom_call" | custom-call | flops 100000000 | bytes 200000 | tf_op jit(solution)/shard_map/weight_grad/pallas_call | solution.py:831
  151.5 1.3 add_convert_fusion.9
  152.8 1.5 add_convert_fusion.2
  154.4 3.8 %collective-permute-start.41 = (bf16[192,768]{1,0:T(8,128)(2,1)S(1)}, bf16[192,768]{1,0:T(8,128)(2,1)S(1)}, u32[]{:S(2)}, u32[]{:S(2)}) collective-permute-start(bf16[192,768]{1,0:T(8,128)(2,1)S(1)} %get-tuple-element.438), channel_id=1, source_target_pairs={{8,0},{12,4},{16,8},{20,12},{24,16},{28,20},{0,24},{4,28},{9,1},{1... | collective-permute-start | bytes 884744 | tf_op jit(solution)/shard_map/ppermute | solution.py:1093
  160.1 19.1 %ssd_backward.1 = (bf16[1024,768]{1,0:T(8,128)(2,1)S(1)}, bf16[1024,256]{1,0:T(8,128)(2,1)S(1)}, bf16[128,1024]{1,0:T(8,128)(2,1)}, bf16[128,1024]{1,0:T(8,128)(...) custom-call(s32[1]{0:T(128)} %bitcast.rank_ref, ...), custom_call_target="tpu_custom_call" | custom-call | flops 28000000000 | bytes 40000000 | tf_op jit(solution)/shard_map/ssd_backward/pallas_call | solution.py:332
  179.2 2.3 collective-permute-done.42
  181.8 5.1 %weight_grad.6 = (bf16[192,768]{1,0:T(8,128)(2,1)}, bf16[192,768]{1,0:T(8,128)(2,1)}, bf16[576,768]{1,0:T(8,128)(2,1)}, bf16[576,768]{1,0:T(8,128)(2,1)}) custom-call(s32[8]{0:T(128)S(1)} %stack.88.idx_ref, bf16[1536,1024]{1,0:T(8,128)(2,1)S(1)} %copy-done.2, bf16[1024,768]{1,0:T(8,128)(2,1)S(1)} %get-tuple-element.491.rhs_ref.gx_ref), custom_call_target="tpu_custom_call" | custom-call | flops 20000000000 | bytes 40000000 | tf_op jit(solution)/shard_map/weight_grad/pallas_call | solution.py:831
  189.1 6.1 %normed_term.2 = (bf16[256,1536]{1,0:T(8,128)(2,1)S(1)}, bf16[256,1536]{1,0:T(8,128)(2,1)S(1)}, f32[24,128]{1,0:T(8,128)S(1)}) custom-call(s32[1]{0:T(128)} %bitcast.rank_ref, bf16[1024,768]{1,0:T(8,128)(2,1)S(1)} %get-tuple-element.491.rhs_ref.gx_ref, bf16[1536,768]{1,0:T(8,128)(2,1)} %get-tuple-element.473.wx_ref, ...), custom_call_target="tpu_custom_call" | custom-call | flops 20000000000 | bytes 40000000 | tf_op jit(solution)/shard_map/normed_term/pallas_call | solution.py:901
  195.2 1.2 collective-permute-done.47.refs_4_
  196.6 2.1 collective-permute-start.52
  198.7 6.1 %normed_term.3 = (bf16[256,1536]{1,0:T(8,128)(2,1)S(1)}, bf16[256,1536]{1,0:T(8,128)(2,1)S(1)}, f32[24,128]{1,0:T(8,128)S(1)}) custom-call(s32[1]{0:T(128)} %bitcast.rank_ref, bf16[1024,768]{1,0:T(8,128)(2,1)S(1)} %get-tuple-element.491.rhs_ref.gx_ref, bf16[1536,768]{1,0:T(8,128)(2,1)} %get-tuple-element.473.wx_ref, ...), custom_call_target="tpu_custom_call" | custom-call | flops 100000000 | bytes 200000 | tf_op jit(solution)/shard_map/normed_term/pallas_call | solution.py:901
  205.0 2.7 weight_grad.7
  207.6 2.5 collective-permute-done.49
  210.6 2.9 %collective-permute-done.51.refs_2_ = bf16[192,768]{1,0:T(8,128)(2,1)S(1)} collective-permute-done((bf16[192,768]{1,0:T(8,128)(2,1)S(1)}, bf16[192,768]{1,0:T(8,128)(2,1)S(1)}, u32[]{:S(2)}, u32[]{:S(2)}) %collective-permute-start.51) | collective-permute-done | bytes 294944 | tf_op jit(solution)/shard_map/ppermute | solution.py:1093
  214.5 1.3 collective-permute-start.56
  216.7 1.6 collective-permute-start.54
  218.6 15.5 %collective-permute-done.55 = bf16[880,128]{1,0:T(8,128)(2,1)S(1)} collective-permute-done((bf16[880,128]{1,0:T(8,128)(2,1)S(1)}, bf16[880,128]{1,0:T(8,128)(2,1)S(1)}, u32[]{:S(2)}, u32[]{:S(2)}) %collective-permute-start.55) | collective-permute-done | bytes 225312 | tf_op jit(solution)/shard_map/ppermute | solution.py:1102
  234.1 2.2 norm_backward.1.refs_0_
  236.5 2.1 collective-permute-start.62
  239.4 1.5 collective-permute-start.61
  242.6 2.1 multiply_subtract_fusion
  244.7 2.4 add_convert_fusion
  248.0 3.3 %collective-permute-done.61.refs_9_.refs_2_ = bf16[208,896]{1,0:T(8,128)(2,1)S(1)} collective-permute-done((bf16[208,896]{1,0:T(8,128)(2,1)S(1)}, bf16[208,896]{1,0:T(8,128)(2,1)S(1)}, u32[]{:S(2)}, u32[]{:S(2)}) %collective-permute-start.61) | collective-permute-done | bytes 372768 | tf_op jit(solution)/shard_map/ppermute | solution.py:1093
  251.3 6.5 %collective-permute-done.60.refs_8_.refs_1_ = bf16[208,896]{1,0:T(8,128)(2,1)S(1)} collective-permute-done((bf16[208,896]{1,0:T(8,128)(2,1)S(1)}, bf16[208,896]{1,0:T(8,128)(2,1)S(1)}, u32[]{:S(2)}, u32[]{:S(2)}) %collective-permute-start.60) | collective-permute-done | bytes 372768 | tf_op jit(solution)/shard_map/ppermute | solution.py:1093
  260.6 4.1 %update_in.1 = (f32[192,2,768]{2,1,0:T(2,128)}, f32[192,2,768]{2,1,0:T(2,128)}) custom-call(f32[192,2,768]{2,1,0:T(2,128)} %w_ref.2, f32[192,2,768]{2,1,0:T(2,128)} %m_ref.2, bf16[192,768]{1,0:T(8,128)(2,1)S(1)} %copy-done.11, bf16[192,1536]{1,0:T(8,128)(2,1)S(1)} %collective-permute-done.56.refs_1_, bf16[192,768]{1,0:T(8,128)(2,1)S(1)} %collective-permute-done.51.refs_2_, ...), custom_call_target="tpu_custom_call" | custom-call | flops 100000000 | bytes 200000 | tf_op jit(solution)/shard_map/update_in/pallas_call | solution.py:988
  268.5 1.9 join_rows.1
  (298 shorter events, 39.6 us)
Async XLA Ops:
  3.6 21.0 %collective-permute-start.3 = (bf16[192,896]{1,0:T(8,128)(2,1)S(1)}, bf16[192,896]{1,0:T(8,128)(2,1)}, u32[]{:S(2)}, u32[]{:S(2)}) collective-permute-start(bf16[192,896]{1,0:T(8,128)(2,1)S(1)} %pack.1.refs_0_), channel_id=1, source_target_pairs={{24,0},{28,4},{0,8},{4,12},{8,16},{12,20},{16,24},{20,28},{25,1},{... | collective-permute-start | bytes 1032200 | tf_op jit(solution)/shard_map/ppermute | solution.py:1093
  6.7 19.7 %collective-permute-start.1 = (bf16[192,896]{1,0:T(8,128)(2,1)S(1)}, bf16[192,896]{1,0:T(8,128)(2,1)}, u32[]{:S(2)}, u32[]{:S(2)}) collective-permute-start(bf16[192,896]{1,0:T(8,128)(2,1)S(1)} %pack.1.refs_0_), channel_id=1, source_target_pairs={{8,0},{12,4},{16,8},{20,12},{24,16},{28,20},{0,24},{4,28},{9,1},{1... | collective-permute-start | bytes 1032200 | tf_op jit(solution)/shard_map/ppermute | solution.py:1093
  8.7 9.5 %collective-permute-start = (bf16[192,896]{1,0:T(8,128)(2,1)S(1)}, bf16[192,896]{1,0:T(8,128)(2,1)S(1)}, u32[]{:S(2)}, u32[]{:S(2)}) collective-permute-start(bf16[192,896]{1,0:T(8,128)(2,1)S(1)} %pack.1.refs_0_), channel_id=1, source_target_pairs={{4,0},{0,4},{12,8},{8,12},{20,16},{16,20},{28,24},{24,28},{5,1},{1... | collective-permute-start | bytes 1032200 | tf_op jit(solution)/shard_map/ppermute | solution.py:1102
  10.4 30.0 %collective-permute-start.6 = (bf16[1024,384]{1,0:T(8,128)(2,1)}, bf16[1024,384]{1,0:T(8,128)(2,1)}, u32[]{:S(2)}, u32[]{:S(2)}) collective-permute-start(bf16[1024,384]{1,0:T(8,128)(2,1)} %refs_0_.1), channel_id=1, source_target_pairs={{2,0},{3,1},{0,2},{1,3},{6,4},{7,5},{4,6},{5,7},{10,8},{11,9},{8,1... | collective-permute-start | bytes 2359304 | tf_op jit(solution)/shard_map/ppermute | solution.py:1106
  11.9 34.0 %collective-permute-start.11 = (bf16[1024,384]{1,0:T(8,128)(2,1)}, bf16[1024,384]{1,0:T(8,128)(2,1)}, u32[]{:S(2)}, u32[]{:S(2)}) collective-permute-start(bf16[1024,384]{1,0:T(8,128)(2,1)} %refs_0_.1), channel_id=1, source_target_pairs={{1,0},{0,1},{3,2},{2,3},{5,4},{4,5},{7,6},{6,7},{9,8},{8,9},{11,10... | collective-permute-start | bytes 2359304 | tf_op jit(solution)/shard_map/ppermute | solution.py:1106
  19.2 21.2 %collective-permute-start.2 = (bf16[192,896]{1,0:T(8,128)(2,1)S(1)}, bf16[192,896]{1,0:T(8,128)(2,1)}, u32[]{:S(2)}, u32[]{:S(2)}) collective-permute-start(bf16[192,896]{1,0:T(8,128)(2,1)S(1)} %pack.1.refs_0_), channel_id=1, source_target_pairs={{16,0},{20,4},{24,8},{28,12},{0,16},{4,20},{8,24},{12,28},{17,1},{... | collective-permute-start | bytes 1032200 | tf_op jit(solution)/shard_map/ppermute | solution.py:1093
  24.6 11.2 %collective-permute-start.5 = (bf16[192,896]{1,0:T(8,128)(2,1)}, bf16[192,896]{1,0:T(8,128)(2,1)S(1)}, u32[]{:S(2)}, u32[]{:S(2)}) collective-permute-start(bf16[192,896]{1,0:T(8,128)(2,1)} %collective-permute-done.3.refs_3_), channel_id=1, source_target_pairs={{4,0},{0,4},{12,8},{8,12},{20,16},{16,20},{28,24},{24,28},{5,1},{1... | collective-permute-start | bytes 1032200 | tf_op jit(solution)/shard_map/ppermute | solution.py:1102
  26.4 14.0 %collective-permute-start.4 = (bf16[192,896]{1,0:T(8,128)(2,1)}, bf16[192,896]{1,0:T(8,128)(2,1)S(1)}, u32[]{:S(2)}, u32[]{:S(2)}) collective-permute-start(bf16[192,896]{1,0:T(8,128)(2,1)} %collective-permute-done.1.refs_2_), channel_id=1, source_target_pairs={{4,0},{0,4},{12,8},{8,12},{20,16},{16,20},{28,24},{24,28},{5,1},{1... | collective-permute-start | bytes 1032200 | tf_op jit(solution)/shard_map/ppermute | solution.py:1102
  40.4 6.1 %collective-permute-start.12 = (bf16[1024,384]{1,0:T(8,128)(2,1)}, bf16[1024,384]{1,0:T(8,128)(2,1)S(1)}, u32[]{:S(2)}, u32[]{:S(2)}) collective-permute-start(bf16[1024,384]{1,0:T(8,128)(2,1)} %collective-permute-done.6.refs_2_), channel_id=1, source_target_pairs={{1,0},{0,1},{3,2},{2,3},{5,4},{4,5},{7,6},{6,7},{9,8},{8,9},{11,10... | collective-permute-start | bytes 2359304 | tf_op jit(solution)/shard_map/ppermute | solution.py:1106
  40.6 10.1 %collective-permute-start.9 = (bf16[192,768]{1,0:T(8,128)(2,1)}, bf16[192,768]{1,0:T(8,128)(2,1)S(1)}, u32[]{:S(2)}, u32[]{:S(2)}) collective-permute-start(bf16[192,768]{1,0:T(8,128)(2,1)} %pack_gate.1.refs_0_), channel_id=1, source_target_pairs={{4,0},{0,4},{12,8},{8,12},{20,16},{16,20},{28,24},{24,28},{5,1},{1... | collective-permute-start | bytes 884744 | tf_op jit(solution)/shard_map/ppermute | solution.py:1102
  42.1 12.0 %collective-permute-start.8 = (bf16[192,768]{1,0:T(8,128)(2,1)}, bf16[192,768]{1,0:T(8,128)(2,1)S(1)}, u32[]{:S(2)}, u32[]{:S(2)}) collective-permute-start(bf16[192,768]{1,0:T(8,128)(2,1)} %pack_gate.1.refs_0_), channel_id=1, source_target_pairs={{24,0},{28,4},{0,8},{4,12},{8,16},{12,20},{16,24},{20,28},{25,1},{... | collective-permute-start | bytes 884744 | tf_op jit(solution)/shard_map/ppermute | solution.py:1093
  43.7 15.7 %collective-permute-start.7 = (bf16[192,768]{1,0:T(8,128)(2,1)}, bf16[192,768]{1,0:T(8,128)(2,1)S(1)}, u32[]{:S(2)}, u32[]{:S(2)}) collective-permute-start(bf16[192,768]{1,0:T(8,128)(2,1)} %pack_gate.1.refs_0_), channel_id=1, source_target_pairs={{8,0},{12,4},{16,8},{20,12},{24,16},{28,20},{0,24},{4,28},{9,1},{1... | collective-permute-start | bytes 884744 | tf_op jit(solution)/shard_map/ppermute | solution.py:1093
  46.0 13.5 %collective-permute-start.10 = (bf16[192,896]{1,0:T(8,128)(2,1)}, bf16[192,896]{1,0:T(8,128)(2,1)S(1)}, u32[]{:S(2)}, u32[]{:S(2)}) collective-permute-start(bf16[192,896]{1,0:T(8,128)(2,1)} %collective-permute-done.2.refs_4_), channel_id=1, source_target_pairs={{4,0},{0,4},{12,8},{8,12},{20,16},{16,20},{28,24},{24,28},{5,1},{1... | collective-permute-start | bytes 1032200 | tf_op jit(solution)/shard_map/ppermute | solution.py:1102
  59.4 17.5 %collective-permute-start.16 = (bf16[192,768]{1,0:T(8,128)(2,1)S(1)}, bf16[192,768]{1,0:T(8,128)(2,1)S(1)}, u32[]{:S(2)}, u32[]{:S(2)}) collective-permute-start(bf16[192,768]{1,0:T(8,128)(2,1)S(1)} %copy-done.14), channel_id=1, source_target_pairs={{4,0},{0,4},{12,8},{8,12},{20,16},{16,20},{28,24},{24,28},{5,1},{1... | collective-permute-start | bytes 884744 | tf_op jit(solution)/shard_map/ppermute | solution.py:1102
  60.0 17.0 %collective-permute-start.15 = (bf16[192,768]{1,0:T(8,128)(2,1)S(1)}, bf16[192,768]{1,0:T(8,128)(2,1)S(1)}, u32[]{:S(2)}, u32[]{:S(2)}) collective-permute-start(bf16[192,768]{1,0:T(8,128)(2,1)S(1)} %collective-permute-done.7.refs_2_), channel_id=1, source_target_pairs={{4,0},{0,4},{12,8},{8,12},{20,16},{16,20},{28,24},{24,28},{5,1},{1... | collective-permute-start | bytes 884744 | tf_op jit(solution)/shard_map/ppermute | solution.py:1102
  61.4 15.5 %collective-permute-start.14 = (bf16[192,768]{1,0:T(8,128)(2,1)S(1)}, bf16[192,768]{1,0:T(8,128)(2,1)S(1)}, u32[]{:S(2)}, u32[]{:S(2)}) collective-permute-start(bf16[192,768]{1,0:T(8,128)(2,1)S(1)} %copy-done.12), channel_id=1, source_target_pairs={{16,0},{20,4},{24,8},{28,12},{0,16},{4,20},{8,24},{12,28},{17,1},{... | collective-permute-start | bytes 884744 | tf_op jit(solution)/shard_map/ppermute | solution.py:1093
  66.8 7.3 %collective-permute-start.13 = (bf16[64,1024]{1,0:T(8,128)(2,1)S(1)}, bf16[64,1024]{1,0:T(8,128)(2,1)S(1)}, u32[]{:S(2)}, u32[]{:S(2)}) collective-permute-start(bf16[64,1024]{1,0:T(8,128)(2,1)S(1)} %get-tuple-element.324.refs_0_), channel_id=1, source_target_pairs={{2,0},{3,1},{0,2},{1,3},{6,4},{7,5},{4,6},{5,7},{10,8},{11,9},{8,1... | collective-permute-start | bytes 393224 | tf_op jit(solution)/shard_map/ppermute | solution.py:1106
  68.4 6.2 %collective-permute-start.17 = (bf16[64,1024]{1,0:T(8,128)(2,1)S(1)}, bf16[64,1024]{1,0:T(8,128)(2,1)S(1)}, u32[]{:S(2)}, u32[]{:S(2)}) collective-permute-start(bf16[64,1024]{1,0:T(8,128)(2,1)S(1)} %get-tuple-element.324.refs_0_), channel_id=1, source_target_pairs={{1,0},{0,1},{3,2},{2,3},{5,4},{4,5},{7,6},{6,7},{9,8},{8,9},{11,10... | collective-permute-start | bytes 393224 | tf_op jit(solution)/shard_map/ppermute | solution.py:1106
  77.0 20.1 %collective-permute-start.22 = (bf16[192,768]{1,0:T(8,128)(2,1)S(1)}, bf16[192,768]{1,0:T(8,128)(2,1)S(1)}, u32[]{:S(2)}, u32[]{:S(2)}) collective-permute-start(bf16[192,768]{1,0:T(8,128)(2,1)S(1)} %copy-done.14), channel_id=1, source_target_pairs={{24,0},{28,4},{0,8},{4,12},{8,16},{12,20},{16,24},{20,28},{25,1},{... | collective-permute-start | bytes 884744 | tf_op jit(solution)/shard_map/ppermute | solution.py:1093
  77.9 19.2 %collective-permute-start.21 = (bf16[192,768]{1,0:T(8,128)(2,1)S(1)}, bf16[192,768]{1,0:T(8,128)(2,1)S(1)}, u32[]{:S(2)}, u32[]{:S(2)}) collective-permute-start(bf16[192,768]{1,0:T(8,128)(2,1)S(1)} %copy-done.14), channel_id=1, source_target_pairs={{8,0},{12,4},{16,8},{20,12},{24,16},{28,20},{0,24},{4,28},{9,1},{1... | collective-permute-start | bytes 884744 | tf_op jit(solution)/shard_map/ppermute | solution.py:1093
  80.9 16.2 %collective-permute-start.19 = (bf16[192,768]{1,0:T(8,128)(2,1)S(1)}, bf16[192,768]{1,0:T(8,128)(2,1)S(1)}, u32[]{:S(2)}, u32[]{:S(2)}) collective-permute-start(bf16[192,768]{1,0:T(8,128)(2,1)S(1)} %collective-permute-done.14.refs_4_), channel_id=1, source_target_pairs={{4,0},{0,4},{12,8},{8,12},{20,16},{16,20},{28,24},{24,28},{5,1},{1... | collective-permute-start | bytes 884744 | tf_op jit(solution)/shard_map/ppermute | solution.py:1102
  82.1 15.0 %collective-permute-start.20 = (bf16[192,768]{1,0:T(8,128)(2,1)S(1)}, bf16[192,768]{1,0:T(8,128)(2,1)S(1)}, u32[]{:S(2)}, u32[]{:S(2)}) collective-permute-start(bf16[192,768]{1,0:T(8,128)(2,1)S(1)} %collective-permute-done.8.refs_3_), channel_id=1, source_target_pairs={{4,0},{0,4},{12,8},{8,12},{20,16},{16,20},{28,24},{24,28},{5,1},{1... | collective-permute-start | bytes 884744 | tf_op jit(solution)/shard_map/ppermute | solution.py:1102
  97.1 13.9 %collective-permute-start.27 = (bf16[192,768]{1,0:T(8,128)(2,1)S(1)}, bf16[192,768]{1,0:T(8,128)(2,1)S(1)}, u32[]{:S(2)}, u32[]{:S(2)}) collective-permute-start(bf16[192,768]{1,0:T(8,128)(2,1)S(1)} %collective-permute-done.21.refs_2_), channel_id=1, source_target_pairs={{4,0},{0,4},{12,8},{8,12},{20,16},{16,20},{28,24},{24,28},{5,1},{1... | collective-permute-start | bytes 884744 | tf_op jit(solution)/shard_map/ppermute | solution.py:1102
  98.5 13.2 %collective-permute-start.26 = (bf16[192,768]{1,0:T(8,128)(2,1)S(1)}, bf16[192,768]{1,0:T(8,128)(2,1)S(1)}, u32[]{:S(2)}, u32[]{:S(2)}) collective-permute-start(bf16[192,768]{1,0:T(8,128)(2,1)S(1)} %copy-done.14), channel_id=1, source_target_pairs={{16,0},{20,4},{24,8},{28,12},{0,16},{4,20},{8,24},{12,28},{17,1},{... | collective-permute-start | bytes 884744 | tf_op jit(solution)/shard_map/ppermute | solution.py:1093
  98.5 13.2 %collective-permute-start.28 = (bf16[192,768]{1,0:T(8,128)(2,1)S(1)}, bf16[192,768]{1,0:T(8,128)(2,1)S(1)}, u32[]{:S(2)}, u32[]{:S(2)}) collective-permute-start(bf16[192,768]{1,0:T(8,128)(2,1)S(1)} %collective-permute-done.22.refs_3_), channel_id=1, source_target_pairs={{4,0},{0,4},{12,8},{8,12},{20,16},{16,20},{28,24},{24,28},{5,1},{1... | collective-permute-start | bytes 884744 | tf_op jit(solution)/shard_map/ppermute | solution.py:1102
  106.1 3.7 %collective-permute-start.25 = (f32[8,1024]{1,0:T(8,128)S(1)}, f32[8,1024]{1,0:T(8,128)S(1)}, u32[]{:S(2)}, u32[]{:S(2)}) collective-permute-start(f32[8,1024]{1,0:T(8,128)S(1)} %get-tuple-element.368), channel_id=1, source_target_pairs={{3,0},{2,1},{1,2},{0,3},{7,4},{6,5},{5,6},{4,7},{11,8},{10,9},{9,1... | collective-permute-start | bytes 98312 | tf_op jit(solution)/shard_map/ppermute | solution.py:1106
  106.1 4.0 %collective-permute-start.24 = (f32[8,1024]{1,0:T(8,128)S(1)}, f32[8,1024]{1,0:T(8,128)S(1)}, u32[]{:S(2)}, u32[]{:S(2)}) collective-permute-start(f32[8,1024]{1,0:T(8,128)S(1)} %get-tuple-element.368), channel_id=1, source_target_pairs={{2,0},{3,1},{0,2},{1,3},{6,4},{7,5},{4,6},{5,7},{10,8},{11,9},{8,1... | collective-permute-start | bytes 98312 | tf_op jit(solution)/shard_map/ppermute | solution.py:1106
  111.7 8.9 %collective-permute-start.29 = (bf16[192,768]{1,0:T(8,128)(2,1)S(1)}, bf16[192,768]{1,0:T(8,128)(2,1)S(1)}, u32[]{:S(2)}, u32[]{:S(2)}) collective-permute-start(bf16[192,768]{1,0:T(8,128)(2,1)S(1)} %collective-permute-done.26.refs_4_), channel_id=1, source_target_pairs={{4,0},{0,4},{12,8},{8,12},{20,16},{16,20},{28,24},{24,28},{5,1},{1... | collective-permute-start | bytes 884744 | tf_op jit(solution)/shard_map/ppermute | solution.py:1102
  112.9 7.0 %collective-permute-start.30 = (bf16[64,1536]{1,0:T(8,128)(2,1)}, bf16[64,1536]{1,0:T(8,128)(2,1)S(1)}, u32[]{:S(2)}, u32[]{:S(2)}) collective-permute-start(bf16[64,1536]{1,0:T(8,128)(2,1)} %get-tuple-element.479.refs_0_), channel_id=1, source_target_pairs={{2,0},{3,1},{0,2},{1,3},{6,4},{7,5},{4,6},{5,7},{10,8},{11,9},{8,1... | collective-permute-start | bytes 589832 | tf_op jit(solution)/shard_map/ppermute | solution.py:1106
  120.6 13.6 %collective-permute-start.35 = (bf16[192,768]{1,0:T(8,128)(2,1)}, bf16[192,768]{1,0:T(8,128)(2,1)S(1)}, u32[]{:S(2)}, u32[]{:S(2)}) collective-permute-start(bf16[192,768]{1,0:T(8,128)(2,1)} %get-tuple-element.408), channel_id=1, source_target_pairs={{4,0},{0,4},{12,8},{8,12},{20,16},{16,20},{28,24},{24,28},{5,1},{1... | collective-permute-start | bytes 884744 | tf_op jit(solution)/shard_map/ppermute | solution.py:1102
  126.2 8.0 %collective-permute-start.34 = (f32[8,1024]{1,0:T(8,128)S(1)}, f32[8,1024]{1,0:T(8,128)S(1)}, u32[]{:S(2)}, u32[]{:S(2)}) collective-permute-start(f32[8,1024]{1,0:T(8,128)S(1)} %get-tuple-element.398), channel_id=1, source_target_pairs={{3,0},{2,1},{1,2},{0,3},{7,4},{6,5},{5,6},{4,7},{11,8},{10,9},{9,1... | collective-permute-start | bytes 98312 | tf_op jit(solution)/shard_map/ppermute | solution.py:1106
  126.3 7.9 %collective-permute-start.33 = (f32[8,1024]{1,0:T(8,128)S(1)}, f32[8,1024]{1,0:T(8,128)S(1)}, u32[]{:S(2)}, u32[]{:S(2)}) collective-permute-start(f32[8,1024]{1,0:T(8,128)S(1)} %get-tuple-element.398), channel_id=1, source_target_pairs={{2,0},{3,1},{0,2},{1,3},{6,4},{7,5},{4,6},{5,7},{10,8},{11,9},{8,1... | collective-permute-start | bytes 98312 | tf_op jit(solution)/shard_map/ppermute | solution.py:1106
  126.9 7.4 %collective-permute-start.32 = (f32[8,1024]{1,0:T(8,128)S(1)}, f32[8,1024]{1,0:T(8,128)S(1)}, u32[]{:S(2)}, u32[]{:S(2)}) collective-permute-start(f32[8,1024]{1,0:T(8,128)S(1)} %get-tuple-element.398), channel_id=1, source_target_pairs={{1,0},{0,1},{3,2},{2,3},{5,4},{4,5},{7,6},{6,7},{9,8},{8,9},{11,10... | collective-permute-start | bytes 98312 | tf_op jit(solution)/shard_map/ppermute | solution.py:1106
  134.3 17.2 %collective-permute-start.39 = (bf16[1024,384]{1,0:T(8,128)(2,1)}, bf16[1024,384]{1,0:T(8,128)(2,1)}, u32[]{:S(2)}, u32[]{:S(2)}) collective-permute-start(bf16[1024,384]{1,0:T(8,128)(2,1)} %get-tuple-element.412), channel_id=1, source_target_pairs={{1,0},{0,1},{3,2},{2,3},{5,4},{4,5},{7,6},{6,7},{9,8},{8,9},{11,10... | collective-permute-start | bytes 2359304 | tf_op jit(solution)/shard_map/ppermute | solution.py:1106
  134.3 16.1 %collective-permute-start.31 = (bf16[384,768]{1,0:T(8,128)(2,1)}, bf16[384,768]{1,0:T(8,128)(2,1)}, u32[]{:S(2)}, u32[]{:S(2)}) collective-permute-start(bf16[384,768]{1,0:T(8,128)(2,1)} %get-tuple-element.389), channel_id=1, source_target_pairs={{4,0},{0,4},{12,8},{8,12},{20,16},{16,20},{28,24},{24,28},{5,1},{1... | collective-permute-start | bytes 1769480 | tf_op jit(solution)/shard_map/ppermute | solution.py:1102
  135.4 16.1 %collective-permute-start.36 = (bf16[192,768]{1,0:T(8,128)(2,1)S(1)}, bf16[192,768]{1,0:T(8,128)(2,1)}, u32[]{:S(2)}, u32[]{:S(2)}) collective-permute-start(bf16[192,768]{1,0:T(8,128)(2,1)S(1)} %add_convert_fusion.11), channel_id=1, source_target_pairs={{16,0},{20,4},{24,8},{28,12},{0,16},{4,20},{8,24},{12,28},{17,1},{... | collective-permute-start | bytes 884744 | tf_op jit(solution)/shard_map/ppermute | solution.py:1093
  138.0 11.9 %collective-permute-start.37 = (bf16[64,1536]{1,0:T(8,128)(2,1)}, bf16[64,1536]{1,0:T(8,128)(2,1)S(1)}, u32[]{:S(2)}, u32[]{:S(2)}) collective-permute-start(bf16[64,1536]{1,0:T(8,128)(2,1)} %get-tuple-element.479.refs_0_), channel_id=1, source_target_pairs={{1,0},{0,1},{3,2},{2,3},{5,4},{4,5},{7,6},{6,7},{9,8},{8,9},{11,10... | collective-permute-start | bytes 589832 | tf_op jit(solution)/shard_map/ppermute | solution.py:1106
  138.0 11.9 %collective-permute-start.38 = (bf16[64,1536]{1,0:T(8,128)(2,1)S(1)}, bf16[64,1536]{1,0:T(8,128)(2,1)S(1)}, u32[]{:S(2)}, u32[]{:S(2)}) collective-permute-start(bf16[64,1536]{1,0:T(8,128)(2,1)S(1)} %collective-permute-done.30.refs_2_), channel_id=1, source_target_pairs={{1,0},{0,1},{3,2},{2,3},{5,4},{4,5},{7,6},{6,7},{9,8},{8,9},{11,10... | collective-permute-start | bytes 589832 | tf_op jit(solution)/shard_map/ppermute | solution.py:1106
  154.3 24.9 %collective-permute-start.40 = (bf16[192,768]{1,0:T(8,128)(2,1)S(1)}, bf16[192,768]{1,0:T(8,128)(2,1)S(1)}, u32[]{:S(2)}, u32[]{:S(2)}) collective-permute-start(bf16[192,768]{1,0:T(8,128)(2,1)S(1)} %get-tuple-element.437), channel_id=1, source_target_pairs={{24,0},{28,4},{0,8},{4,12},{8,16},{12,20},{16,24},{20,28},{25,1},{... | collective-permute-start | bytes 884744 | tf_op jit(solution)/shard_map/ppermute | solution.py:1093
  154.4 24.9 %collective-permute-start.41 = (bf16[192,768]{1,0:T(8,128)(2,1)S(1)}, bf16[192,768]{1,0:T(8,128)(2,1)S(1)}, u32[]{:S(2)}, u32[]{:S(2)}) collective-permute-start(bf16[192,768]{1,0:T(8,128)(2,1)S(1)} %get-tuple-element.438), channel_id=1, source_target_pairs={{8,0},{12,4},{16,8},{20,12},{24,16},{28,20},{0,24},{4,28},{9,1},{1... | collective-permute-start | bytes 884744 | tf_op jit(solution)/shard_map/ppermute | solution.py:1093
  158.2 21.1 %collective-permute-start.43 = (bf16[1024,384]{1,0:T(8,128)(2,1)S(1)}, bf16[1024,384]{1,0:T(8,128)(2,1)S(1)}, u32[]{:S(2)}, u32[]{:S(2)}) collective-permute-start(bf16[1024,384]{1,0:T(8,128)(2,1)S(1)} %add_convert_fusion.2), channel_id=1, source_target_pairs={{2,0},{3,1},{0,2},{1,3},{6,4},{7,5},{4,6},{5,7},{10,8},{11,9},{8,1... | collective-permute-start | bytes 2359304 | tf_op jit(solution)/shard_map/ppermute | solution.py:1106
  159.3 27.7 %collective-permute-start.45 = (bf16[1024,384]{1,0:T(8,128)(2,1)S(1)}, bf16[1024,384]{1,0:T(8,128)(2,1)S(1)}, u32[]{:S(2)}, u32[]{:S(2)}) collective-permute-start(bf16[1024,384]{1,0:T(8,128)(2,1)S(1)} %copy-done.57), channel_id=1, source_target_pairs={{1,0},{0,1},{3,2},{2,3},{5,4},{4,5},{7,6},{6,7},{9,8},{8,9},{11,10... | collective-permute-start | bytes 2359304 | tf_op jit(solution)/shard_map/ppermute | solution.py:1106
  159.3 22.3 %collective-permute-start.42 = (bf16[576,768]{1,0:T(8,128)(2,1)}, bf16[576,768]{1,0:T(8,128)(2,1)S(1)}, u32[]{:S(2)}, u32[]{:S(2)}) collective-permute-start(bf16[576,768]{1,0:T(8,128)(2,1)} %get-tuple-element.440), channel_id=1, source_target_pairs={{4,0},{0,4},{12,8},{8,12},{20,16},{16,20},{28,24},{24,28},{5,1},{1... | collective-permute-start | bytes 2654216 | tf_op jit(solution)/shard_map/ppermute | solution.py:1102
  181.6 5.4 %collective-permute-start.44 = (bf16[128,1024]{1,0:T(8,128)(2,1)}, bf16[128,1024]{1,0:T(8,128)(2,1)S(1)}, u32[]{:S(2)}, u32[]{:S(2)}) collective-permute-start(bf16[128,1024]{1,0:T(8,128)(2,1)} %get-tuple-element.468), channel_id=1, source_target_pairs={{1,0},{0,1},{3,2},{2,3},{5,4},{4,5},{7,6},{6,7},{9,8},{8,9},{11,10... | collective-permute-start | bytes 786440 | tf_op jit(solution)/shard_map/ppermute | solution.py:1106
  181.8 14.6 %collective-permute-start.47 = (bf16[192,768]{1,0:T(8,128)(2,1)S(1)}, bf16[192,768]{1,0:T(8,128)(2,1)S(1)}, u32[]{:S(2)}, u32[]{:S(2)}) collective-permute-start(bf16[192,768]{1,0:T(8,128)(2,1)S(1)} %add_convert_fusion.8), channel_id=1, source_target_pairs={{16,0},{20,4},{24,8},{28,12},{0,16},{4,20},{8,24},{12,28},{17,1},{... | collective-permute-start | bytes 884744 | tf_op jit(solution)/shard_map/ppermute | solution.py:1093
  187.1 9.2 %collective-permute-start.46 = (bf16[64,1024]{1,0:T(8,128)(2,1)S(1)}, bf16[64,1024]{1,0:T(8,128)(2,1)S(1)}, u32[]{:S(2)}, u32[]{:S(2)}) collective-permute-start(bf16[64,1024]{1,0:T(8,128)(2,1)S(1)} %slice.308), channel_id=1, source_target_pairs={{2,0},{3,1},{0,2},{1,3},{6,4},{7,5},{4,6},{5,7},{10,8},{11,9},{8,1... | collective-permute-start | bytes 393224 | tf_op jit(solution)/shard_map/ppermute | solution.py:1106
  188.1 22.0 %collective-permute-start.49 = (bf16[576,768]{1,0:T(8,128)(2,1)}, bf16[576,768]{1,0:T(8,128)(2,1)S(1)}, u32[]{:S(2)}, u32[]{:S(2)}) collective-permute-start(bf16[576,768]{1,0:T(8,128)(2,1)} %get-tuple-element.495), channel_id=1, source_target_pairs={{4,0},{0,4},{12,8},{8,12},{20,16},{16,20},{28,24},{24,28},{5,1},{1... | collective-permute-start | bytes 2654216 | tf_op jit(solution)/shard_map/ppermute | solution.py:1102
  196.4 13.7 %collective-permute-start.48 = (bf16[256,1536]{1,0:T(8,128)(2,1)S(1)}, bf16[256,1536]{1,0:T(8,128)(2,1)S(1)}, u32[]{:S(2)}, u32[]{:S(2)}) collective-permute-start(bf16[256,1536]{1,0:T(8,128)(2,1)S(1)} %get-tuple-element.490), channel_id=1, source_target_pairs={{1,0},{0,1},{3,2},{2,3},{5,4},{4,5},{7,6},{6,7},{9,8},{8,9},{11,10... | collective-permute-start | bytes 2359304 | tf_op jit(solution)/shard_map/ppermute | solution.py:1106
  196.6 14.0 %collective-permute-start.52 = (bf16[192,768]{1,0:T(8,128)(2,1)S(1)}, bf16[192,768]{1,0:T(8,128)(2,1)S(1)}, u32[]{:S(2)}, u32[]{:S(2)}) collective-permute-start(bf16[192,768]{1,0:T(8,128)(2,1)S(1)} %get-tuple-element.578), channel_id=1, source_target_pairs={{8,0},{12,4},{16,8},{20,12},{24,16},{28,20},{0,24},{4,28},{9,1},{1... | collective-permute-start | bytes 884744 | tf_op jit(solution)/shard_map/ppermute | solution.py:1093
  198.7 14.8 %collective-permute-start.51 = (bf16[192,768]{1,0:T(8,128)(2,1)S(1)}, bf16[192,768]{1,0:T(8,128)(2,1)S(1)}, u32[]{:S(2)}, u32[]{:S(2)}) collective-permute-start(bf16[192,768]{1,0:T(8,128)(2,1)S(1)} %get-tuple-element.579), channel_id=1, source_target_pairs={{24,0},{28,4},{0,8},{4,12},{8,16},{12,20},{16,24},{20,28},{25,1},{... | collective-permute-start | bytes 884744 | tf_op jit(solution)/shard_map/ppermute | solution.py:1093
  210.1 3.4 %collective-permute-start.50 = (bf16[256,1536]{1,0:T(8,128)(2,1)S(1)}, bf16[256,1536]{1,0:T(8,128)(2,1)S(1)}, u32[]{:S(2)}, u32[]{:S(2)}) collective-permute-start(bf16[256,1536]{1,0:T(8,128)(2,1)S(1)} %get-tuple-element.499), channel_id=1, source_target_pairs={{1,0},{0,1},{3,2},{2,3},{5,4},{4,5},{7,6},{6,7},{9,8},{8,9},{11,10... | collective-permute-start | bytes 2359304 | tf_op jit(solution)/shard_map/ppermute | solution.py:1106
  213.5 20.6 %collective-permute-start.53 = (bf16[256,1536]{1,0:T(8,128)(2,1)S(1)}, bf16[256,1536]{1,0:T(8,128)(2,1)S(1)}, u32[]{:S(2)}, u32[]{:S(2)}) collective-permute-start(bf16[256,1536]{1,0:T(8,128)(2,1)S(1)} %add_convert_fusion.1), channel_id=1, source_target_pairs={{2,0},{3,1},{0,2},{1,3},{6,4},{7,5},{4,6},{5,7},{10,8},{11,9},{8,1... | collective-permute-start | bytes 2359304 | tf_op jit(solution)/shard_map/ppermute | solution.py:1106
  214.5 19.6 %collective-permute-start.56 = (bf16[192,1536]{1,0:T(8,128)(2,1)S(1)}, bf16[192,1536]{1,0:T(8,128)(2,1)S(1)}, u32[]{:S(2)}, u32[]{:S(2)}) collective-permute-start(bf16[192,1536]{1,0:T(8,128)(2,1)S(1)} %pad_maximum_fusion), channel_id=1, source_target_pairs={{4,0},{0,4},{12,8},{8,12},{20,16},{16,20},{28,24},{24,28},{5,1},{1... | collective-permute-start | bytes 1769480 | tf_op jit(solution)/shard_map/ppermute | solution.py:1102
  215.9 18.2 %collective-permute-start.55 = (bf16[880,128]{1,0:T(8,128)(2,1)S(1)}, bf16[880,128]{1,0:T(8,128)(2,1)S(1)}, u32[]{:S(2)}, u32[]{:S(2)}) collective-permute-start(bf16[880,128]{1,0:T(8,128)(2,1)S(1)} %pad_maximum_fusion.3), channel_id=1, source_target_pairs={{4,0},{0,4},{12,8},{8,12},{20,16},{16,20},{28,24},{24,28},{5,1},{1... | collective-permute-start | bytes 675848 | tf_op jit(solution)/shard_map/ppermute | solution.py:1102
  216.7 17.4 %collective-permute-start.54 = (bf16[192,768]{1,0:T(8,128)(2,1)S(1)}, bf16[192,768]{1,0:T(8,128)(2,1)S(1)}, u32[]{:S(2)}, u32[]{:S(2)}) collective-permute-start(bf16[192,768]{1,0:T(8,128)(2,1)S(1)} %get-tuple-element.512), channel_id=1, source_target_pairs={{16,0},{20,4},{24,8},{28,12},{0,16},{4,20},{8,24},{12,28},{17,1},{... | collective-permute-start | bytes 884744 | tf_op jit(solution)/shard_map/ppermute | solution.py:1093
  236.5 11.5 %collective-permute-start.62 = (bf16[304,128]{1,0:T(8,128)(2,1)S(1)}, bf16[304,128]{1,0:T(8,128)(2,1)S(1)}, u32[]{:S(2)}, u32[]{:S(2)}) collective-permute-start(bf16[304,128]{1,0:T(8,128)(2,1)S(1)} %pad_maximum_fusion.4), channel_id=1, source_target_pairs={{16,0},{20,4},{24,8},{28,12},{0,16},{4,20},{8,24},{12,28},{17,1},{... | collective-permute-start | bytes 233480 | tf_op jit(solution)/shard_map/ppermute | solution.py:1093
  238.6 9.4 %collective-permute-start.63 = (bf16[192,768]{1,0:T(8,128)(2,1)S(1)}, bf16[192,768]{1,0:T(8,128)(2,1)S(1)}, u32[]{:S(2)}, u32[]{:S(2)}) collective-permute-start(bf16[192,768]{1,0:T(8,128)(2,1)S(1)} %copy-done.58), channel_id=1, source_target_pairs={{4,0},{0,4},{12,8},{8,12},{20,16},{16,20},{28,24},{24,28},{5,1},{1... | collective-permute-start | bytes 884744 | tf_op jit(solution)/shard_map/ppermute | solution.py:1102
  239.4 11.8 %collective-permute-start.61 = (bf16[208,896]{1,0:T(8,128)(2,1)S(1)}, bf16[208,896]{1,0:T(8,128)(2,1)S(1)}, u32[]{:S(2)}, u32[]{:S(2)}) collective-permute-start(bf16[208,896]{1,0:T(8,128)(2,1)S(1)} %get-tuple-element.588), channel_id=1, source_target_pairs={{8,0},{12,4},{16,8},{20,12},{24,16},{28,20},{0,24},{4,28},{9,1},{1... | collective-permute-start | bytes 1118216 | tf_op jit(solution)/shard_map/ppermute | solution.py:1093
  240.9 16.9 %collective-permute-start.60 = (bf16[208,896]{1,0:T(8,128)(2,1)S(1)}, bf16[208,896]{1,0:T(8,128)(2,1)S(1)}, u32[]{:S(2)}, u32[]{:S(2)}) collective-permute-start(bf16[208,896]{1,0:T(8,128)(2,1)S(1)} %get-tuple-element.589), channel_id=1, source_target_pairs={{24,0},{28,4},{0,8},{4,12},{8,16},{12,20},{16,24},{20,28},{25,1},{... | collective-permute-start | bytes 1118216 | tf_op jit(solution)/shard_map/ppermute | solution.py:1093
  241.5 18.8 %collective-permute-start.57 = (bf16[256,1536]{1,0:T(8,128)(2,1)S(1)}, bf16[256,1536]{1,0:T(8,128)(2,1)S(1)}, u32[]{:S(2)}, u32[]{:S(2)}) collective-permute-start(bf16[256,1536]{1,0:T(8,128)(2,1)S(1)} %norm_backward.1.refs_0_), channel_id=1, source_target_pairs={{2,0},{3,1},{0,2},{1,3},{6,4},{7,5},{4,6},{5,7},{10,8},{11,9},{8,1... | collective-permute-start | bytes 2359304 | tf_op jit(solution)/shard_map/ppermute | solution.py:1106
  258.5 7.8 %collective-permute-start.66 = (f32[232,128]{1,0:T(8,128)S(1)}, f32[232,128]{1,0:T(8,128)S(1)}, u32[]{:S(2)}, u32[]{:S(2)}) collective-permute-start(f32[232,128]{1,0:T(8,128)S(1)} %get-tuple-element.562.refs_0_), channel_id=1, source_target_pairs={{3,0},{2,1},{1,2},{0,3},{7,4},{6,5},{5,6},{4,7},{11,8},{10,9},{9,1... | collective-permute-start | bytes 356360 | tf_op jit(solution)/shard_map/ppermute | solution.py:1106
  258.5 7.8 %collective-permute-start.65 = (f32[232,128]{1,0:T(8,128)S(1)}, f32[232,128]{1,0:T(8,128)S(1)}, u32[]{:S(2)}, u32[]{:S(2)}) collective-permute-start(f32[232,128]{1,0:T(8,128)S(1)} %get-tuple-element.562.refs_0_), channel_id=1, source_target_pairs={{2,0},{3,1},{0,2},{1,3},{6,4},{7,5},{4,6},{5,7},{10,8},{11,9},{8,1... | collective-permute-start | bytes 356360 | tf_op jit(solution)/shard_map/ppermute | solution.py:1106
  259.5 6.8 %collective-permute-start.64 = (f32[232,128]{1,0:T(8,128)S(1)}, f32[232,128]{1,0:T(8,128)S(1)}, u32[]{:S(2)}, u32[]{:S(2)}) collective-permute-start(f32[232,128]{1,0:T(8,128)S(1)} %get-tuple-element.562.refs_0_), channel_id=1, source_target_pairs={{1,0},{0,1},{3,2},{2,3},{5,4},{4,5},{7,6},{6,7},{9,8},{8,9},{11,10... | collective-permute-start | bytes 356360 | tf_op jit(solution)/shard_map/ppermute | solution.py:1106
  260.4 5.9 %collective-permute-start.59 = (bf16[256,1536]{1,0:T(8,128)(2,1)S(1)}, bf16[256,1536]{1,0:T(8,128)(2,1)S(1)}, u32[]{:S(2)}, u32[]{:S(2)}) collective-permute-start(bf16[256,1536]{1,0:T(8,128)(2,1)S(1)} %collective-permute-done.57.refs_2_), channel_id=1, source_target_pairs={{1,0},{0,1},{3,2},{2,3},{5,4},{4,5},{7,6},{6,7},{9,8},{8,9},{11,10... | collective-permute-start | bytes 2359304 | tf_op jit(solution)/shard_map/ppermute | solution.py:1106
  (62 other events, 748.0 us)

commit v9 on v8

--- a/solution.py
+++ b/solution.py
@@ -403,7 +403,7 @@
     return (head[:, None] == channel[None, :]).astype(bf16), (channel[:, None] == head[None, :]).astype(bf16)
 
 
-TILE = 256
+TILE = 512
 TILE_D = 512
 
 
@@ -417,7 +417,7 @@
             s += 1
 
 
-def params(mib=18):
+def params(mib=24):
     return pltpu.CompilerParams(vmem_limit_bytes=mib * MIB)
 
 
@@ -918,7 +918,7 @@
         out_shape=[jax.ShapeDtypeStruct((rows, depth), bf16)] * len(apart)
         + [jax.ShapeDtypeStruct((8 * (depth // TILE_D), LANES), f32)],
         compiler_params=params(32),
-        cost_estimate=cost(20 if 2 in apart else 0.1),
+        cost_estimate=cost(5 if 2 in apart else 5),
         name="normed_term",
     )(
         rank, dx, from_hbm(w_a), dgate, from_hbm(w_b), dstep, from_hbm(w_s), dbc, from_hbm(hidden), inv_rms, *w_bct

time: 271 us -> 269 us (level)
  other arithmetic: 14.3 us -> 11.1 us
  Pallas kernels: 122 us -> 119 us
    ppermute x19, waiting for transfers between devices: 34.5 us -> 39 us  [inner_flip(): lax.ppermute(v, 'dp', [(d ^ 1, d) for d in range(lax.axis_size('dp'))])]
    ppermute x19, waiting for transfers between devices: 24.3 us -> 20.7 us  [outer_from(): lax.ppermute(v, 'dp', [((o + k) % n * 2 + x, o * 2 + x) for o in range(n)...]
  transfers between devices with their start and end apart: 67 -> 67, of which waited for: 21 -> 22; matrix products, arithmetic and copies ran while one was open for 5% -> 5% of each run, Pallas kernels for 42% -> 42%
where the time goes in v9:
time: 269 us; the launch traced here: 268 us
  Pallas kernels  119 us (44%)
  waiting for transfers between devices  65.6 us (24%)
  starting transfers between devices  65.5 us (24%)
  other arithmetic  11.1 us (4%)
  local copies, waits for them, and re-layouts  5.23 us (2%)
    ppermute x19, waiting for transfers between devices, inner_flip(): lax.ppermute(v, 'dp', [(d ^ 1, d) for d in range(lax.axis_size('dp'))])  39 us
    ppermute x19, starting transfers between devices, outer_from(): lax.ppermute(v, 'dp', [((o + k) % n * 2 + x, o * 2 + x) for o in range(n)...  30.6 us
    ppermute x19, waiting for transfers between devices, outer_from(): lax.ppermute(v, 'dp', [((o + k) % n * 2 + x, o * 2 + x) for o in range(n)...  20.7 us
    ppermute x19, starting transfers between devices, inner_flip(): lax.ppermute(v, 'dp', [(d ^ 1, d) for d in range(lax.axis_size('dp'))])  19.7 us
    pallas_call x1, Pallas kernels, ssd_backward(): pl.pallas_call(ssd_backward_kernel, grid=(count,), in_specs=[pl.BlockSpec...  19.4 us
    pallas_call x4, Pallas kernels, weight_grad(): pl.pallas_call(functools.partial(weight_grad_kernel, rows=rows, turned=tu...  18.1 us
    ppermute x29, starting transfers between devices, rank_flip(): lax.ppermute(v, 'mp', [(m ^ bit, m) for m in range(lax.axis_size('mp'))])  15.2 us
    pallas_call x1, Pallas kernels, ssd_forward(): pl.pallas_call(ssd_forward_kernel, grid=(count,), in_specs=common_specs(l...  14.2 us
  transfers between devices with their start and end apart: 67, of which 22 were waited for; matrix products, arithmetic and copies ran while one was open for 5% of the time, Pallas kernels for 42%

profile of v9, /device:TPU:0, one launch (start us, length us, event | category | flops | bytes accessed | tf_op | source)
XLA Modules:
  0.0 268.3 jit_solution(16255418422161791121)
XLA Ops:
  0.7 2.8 %pack.1.refs_0_ = bf16[192,896]{1,0:T(8,128)(2,1)S(1)} custom-call(s32[1]{0:T(128)} %bitcast.rank_ref, f32[192,2,768]{2,1,0:T(2,128)} %w_ref.2, f32[192,256]{1,0:T(8,128)} %w_ref.3, f32[12,192]{1,0:T(8,128)} %bitcast.47), custom_call_target="tpu_custom_call" | custom-call | flops 2000000000 | bytes 4000000 | tf_op jit(solution)/shard_map/pack/pallas_call | solution.py:476
  3.6 3.1 %collective-permute-start.3 = (bf16[192,896]{1,0:T(8,128)(2,1)S(1)}, bf16[192,896]{1,0:T(8,128)(2,1)}, u32[]{:S(2)}, u32[]{:S(2)}) collective-permute-start(bf16[192,896]{1,0:T(8,128)(2,1)S(1)} %pack.1.refs_0_), channel_id=1, source_target_pairs={{24,0},{28,4},{0,8},{4,12},{8,16},{12,20},{16,24},{20,28},{25,1},{... | collective-permute-start | bytes 1032200 | tf_op jit(solution)/shard_map/ppermute | solution.py:1093
  6.7 2.1 collective-permute-start.1
  8.7 1.6 collective-permute-start
  10.4 1.5 collective-permute-start.6
  14.9 3.3 %collective-permute-done.refs_1_ = bf16[192,896]{1,0:T(8,128)(2,1)S(1)} collective-permute-done((bf16[192,896]{1,0:T(8,128)(2,1)S(1)}, bf16[192,896]{1,0:T(8,128)(2,1)S(1)}, u32[]{:S(2)}, u32[]{:S(2)}) %collective-permute-start) | collective-permute-done | bytes 344096 | tf_op jit(solution)/shard_map/ppermute | solution.py:1102
  20.6 3.6 %prepare.1 = (bf16[1024,1536]{1,0:T(8,128)(2,1)}, bf16[1536,1024]{1,0:T(8,128)(2,1)}, f32[8,1024]{1,0:T(8,128)S(1)}) custom-call(bf16[1024,1536]{1,0:T(8,128)(2,1)S(1)} %copy-done.4, f32[8,1536]{1,0:T(8,128)S(1)} %copy-done.15), custom_call_target="tpu_custom_call" | custom-call | flops 12000000000 | bytes 24000000 | tf_op jit(solution)/shard_map/prepare/pallas_call | solution.py:440
  25.1 1.5 collective-permute-start.5
  28.0 2.8 %pack_gate.1.refs_0_ = bf16[192,768]{1,0:T(8,128)(2,1)} custom-call(f32[192,2,768]{2,1,0:T(2,128)} %w_ref.2), custom_call_target="tpu_custom_call" | custom-call | flops 2000000000 | bytes 4000000 | tf_op jit(solution)/shard_map/pack_gate/pallas_call | solution.py:495
  30.8 5.6 %collective-permute-done.5.refs_6_ = bf16[192,896]{1,0:T(8,128)(2,1)S(1)} collective-permute-done((bf16[192,896]{1,0:T(8,128)(2,1)}, bf16[192,896]{1,0:T(8,128)(2,1)S(1)}, u32[]{:S(2)}, u32[]{:S(2)}) %collective-permute-start.5) | collective-permute-done | bytes 344096 | tf_op jit(solution)/shard_map/ppermute | solution.py:1102
  36.3 4.5 %collective-permute-done.4.refs_5_ = bf16[192,896]{1,0:T(8,128)(2,1)S(1)} collective-permute-done((bf16[192,896]{1,0:T(8,128)(2,1)}, bf16[192,896]{1,0:T(8,128)(2,1)S(1)}, u32[]{:S(2)}, u32[]{:S(2)}) %collective-permute-start.4) | collective-permute-done | bytes 344096 | tf_op jit(solution)/shard_map/ppermute | solution.py:1102
  41.1 1.6 collective-permute-start.9
  42.6 1.6 collective-permute-start.8
  44.2 2.2 collective-permute-start.7
  47.0 2.5 join_columns.1
  49.5 1.7 collective-permute-done.9.refs_1_
  51.2 3.4 %collective-permute-done.8.refs_3_ = bf16[192,768]{1,0:T(8,128)(2,1)S(1)} collective-permute-done((bf16[192,768]{1,0:T(8,128)(2,1)}, bf16[192,768]{1,0:T(8,128)(2,1)S(1)}, u32[]{:S(2)}, u32[]{:S(2)}) %collective-permute-start.8) | collective-permute-done | bytes 294944 | tf_op jit(solution)/shard_map/ppermute | solution.py:1093
  54.5 5.0 %collective-permute-done.7.refs_2_ = bf16[192,768]{1,0:T(8,128)(2,1)S(1)} collective-permute-done((bf16[192,768]{1,0:T(8,128)(2,1)}, bf16[192,768]{1,0:T(8,128)(2,1)S(1)}, u32[]{:S(2)}, u32[]{:S(2)}) %collective-permute-start.7) | collective-permute-done | bytes 294944 | tf_op jit(solution)/shard_map/ppermute | solution.py:1093
  60.1 1.5 collective-permute-start.15
  61.6 1.4 collective-permute-start.14
  63.0 3.3 %project_small.1 = (f32[128,1024]{1,0:T(8,128)S(1)}, bf16[64,1024]{1,0:T(8,128)(2,1)S(1)}, bf16[1536,128]{1,0:T(8,128)(2,1)}, bf16[64,1536]{1,0:T(8,128)(2,1)}) custom-call(s32[8]{0:T(128)S(1)} %stack.88.idx_ref, bf16[1024,1536]{1,0:T(8,128)(2,1)S(1)} %copy-done.2, bf16[192,896]{1,0:T(8,128)(2,1)S(1)} %pack.1.refs_0_, bf16[192,896]{1,0:T(8,128)(2,1)S(1)} %copy-done.10, ...), custom_call_target="tpu_custom_call" | custom-call | flops 20000000000 | bytes 40000000 | tf_op jit(solution)/shard_map/project_small/pallas_call | solution.py:598
  66.3 1.5 collective-permute-start.13
  67.8 5.9 %project.1 = (f32[1024,768]{1,0:T(8,128)}, bf16[1536,768]{1,0:T(8,128)(2,1)}) custom-call(s32[8]{0:T(128)S(1)} %stack.88.idx_ref, bf16[1024,1536]{1,0:T(8,128)(2,1)S(1)} %copy-done.2, bf16[192,896]{1,0:T(8,128)(2,1)S(1)} %pack.1.refs_0_, bf16[192,896]{1,0:T(8,128)(2,1)S(1)} %copy-done.10, bf16[192,896]{1,0:T(8,128)(2,1)} %collective-permute-done.1.refs_2_, ...), custom_call_target="tpu_custom_call" | custom-call | flops 100000000 | bytes 200000 | tf_op jit(solution)/shard_map/project/pallas_call | solution.py:634
  77.6 2.9 %collective-permute-start.21 = (bf16[192,768]{1,0:T(8,128)(2,1)S(1)}, bf16[192,768]{1,0:T(8,128)(2,1)S(1)}, u32[]{:S(2)}, u32[]{:S(2)}) collective-permute-start(bf16[192,768]{1,0:T(8,128)(2,1)S(1)} %copy-done.14), channel_id=1, source_target_pairs={{8,0},{12,4},{16,8},{20,12},{24,16},{28,20},{0,24},{4,28},{9,1},{1... | collective-permute-start | bytes 884744 | tf_op jit(solution)/shard_map/ppermute | solution.py:1093
  81.3 1.2 collective-permute-start.20
  82.5 14.2 %ssd_forward.1 = (f32[1024,768]{1,0:T(8,128)}, bf16[8,128,768]{2,1,0:T(8,128)(2,1)}, f32[1024,768]{1,0:T(8,128)}, bf16[1024,768]{1,0:T(8,128)(2,1)}, bf16[1024,7...) custom-call(f32[1024,768]{1,0:T(8,128)} %get-tuple-element.341.x_ref, ...), custom_call_target="tpu_custom_call" | custom-call | flops 14000000000 | bytes 40000000 | tf_op jit(solution)/shard_map/ssd_forward/pallas_call | solution.py:293
  97.7 1.2 collective-permute-start.28
  98.9 6.5 %gate_forward.1 = (f32[1024,768]{1,0:T(8,128)S(1)}, f32[8,1024]{1,0:T(8,128)S(1)}, bf16[1536,768]{1,0:T(8,128)(2,1)}) custom-call(s32[8]{0:T(128)S(1)} %stack.88.idx_ref, bf16[1024,1536]{1,0:T(8,128)(2,1)S(1)} %copy-done.2, f32[1024,768]{1,0:T(8,128)} %get-tuple-element.381.mixed_ref, bf16[192,768]{1,0:T(8,128)(2,1)S(1)} %copy-done.12, ...), custom_call_target="tpu_custom_call" | custom-call | flops 100000000 | bytes 200000 | tf_op jit(solution)/shard_map/gate_forward/pallas_call | solution.py:676
  105.4 1.6 collective-permute-start.24
  106.9 2.0 collective-permute-done.25
  111.0 1.5 collective-permute-start.29
  113.0 1.1 gated_norm.1.rhs_ref.lhs_ref
  114.2 5.1 %weight_grad.4 = (bf16[192,768]{1,0:T(8,128)(2,1)}, bf16[192,768]{1,0:T(8,128)(2,1)}, bf16[576,768]{1,0:T(8,128)(2,1)}, bf16[384,768]{1,0:T(8,128)(2,1)}, bf16[192,768]{1,0:T(8,128)(2,1)}) custom-call(s32[8]{0:T(128)S(1)} %stack.88.idx_ref, bf16[1536,1024]{1,0:T(8,128)(2,1)S(1)} %get-tuple-element.382.lhs_ref, bf16[1024,768]{1,0:T(8,128)(2,1)S(1)} %gated_norm.1.rhs_ref.lhs_ref), custom_call_target="tpu_custom_call" | custom-call | flops 100000000 | bytes 200000 | tf_op jit(solution)/shard_map/weight_grad/pallas_call | solution.py:831
  120.0 1.5 collective-permute-start.35
  121.5 4.1 %grad_gout.1 = (f32[1024,768]{1,0:T(8,128)S(1)}, f32[8,1024]{1,0:T(8,128)S(1)}, bf16[1536,768]{1,0:T(8,128)(2,1)S(1)}) custom-call(s32[8]{0:T(128)S(1)} %stack.88.idx_ref, bf16[1024,1536]{1,0:T(8,128)(2,1)S(1)} %get-tuple-element.391.cot_ref, f32[1024,768]{1,0:T(8,128)S(1)} %get-tuple-element.380.gate_ref, f32[1024,768]{1,0:T(8,128)S(1)} %copy-done, ...), custom_call_target="tpu_custom_call" | custom-call | flops 20000000000 | bytes 40000000 | tf_op jit(solution)/shard_map/grad_gout/pallas_call | solution.py:742
  126.2 1.3 collective-permute-start.32
  127.5 6.1 %out_partial.1 = (bf16[1024,384]{1,0:T(8,128)(2,1)}, bf16[1024,384]{1,0:T(8,128)(2,1)}, bf16[1024,384]{1,0:T(8,128)(2,1)}, bf16[1024,384]{1,0:T(8,128)(2,1)}) custom-call(s32[1]{0:T(128)} %bitcast.rank_ref, bf16[1024,768]{1,0:T(8,128)(2,1)S(1)} %gated_norm.1.rhs_ref.lhs_ref, bf16[1536,768]{1,0:T(8,128)(2,1)S(1)} %get-tuple-element.401.w_ref), custom_call_target="tpu_custom_call" | custom-call | flops 100000000 | bytes 200000 | tf_op jit(solution)/shard_map/out_partial/pallas_call | solution.py:861
  134.4 2.3 collective-permute-start.36
  137.4 5.9 %gate_backward.1 = (bf16[1024,768]{1,0:T(8,128)(2,1)S(1)}, bf16[1024,768]{1,0:T(8,128)(2,1)S(1)}, f32[8,768]{1,0:T(8,128)S(1)}) custom-call(f32[1024,768]{1,0:T(8,128)} %copy-done.3, f32[1024,768]{1,0:T(8,128)} %copy-done.6, f32[1024,768]{1,0:T(8,128)} %get-tuple-element.381.mixed_ref, f32[8,1024]{1,0:T(8,128)S(1)} %add_add_fusion.1.square_ref, ...), custom_call_target="tpu_custom_call" | custom-call | flops 100000000 | bytes 200000 | tf_op jit(solution)/shard_map/gate_backward/pallas_call | solution.py:793
  143.3 5.2 %weight_grad.5 = (bf16[192,768]{1,0:T(8,128)(2,1)}, bf16[192,768]{1,0:T(8,128)(2,1)}, bf16[576,768]{1,0:T(8,128)(2,1)}, bf16[576,768]{1,0:T(8,128)(2,1)}) custom-call(s32[8]{0:T(128)S(1)} %stack.88.idx_ref, bf16[1536,1024]{1,0:T(8,128)(2,1)S(1)} %copy-done.1, bf16[1024,768]{1,0:T(8,128)(2,1)S(1)} %get-tuple-element.417.rhs_ref.gg_ref), custom_call_target="tpu_custom_call" | custom-call | flops 100000000 | bytes 200000 | tf_op jit(solution)/shard_map/weight_grad/pallas_call | solution.py:831
  148.5 1.2 collective-permute-done.31
  151.5 3.8 %collective-permute-start.41 = (bf16[192,768]{1,0:T(8,128)(2,1)S(1)}, bf16[192,768]{1,0:T(8,128)(2,1)S(1)}, u32[]{:S(2)}, u32[]{:S(2)}) collective-permute-start(bf16[192,768]{1,0:T(8,128)(2,1)S(1)} %get-tuple-element.438), channel_id=1, source_target_pairs={{8,0},{12,4},{16,8},{20,12},{24,16},{28,20},{0,24},{4,28},{9,1},{1... | collective-permute-start | bytes 884744 | tf_op jit(solution)/shard_map/ppermute | solution.py:1093
  155.3 1.2 collective-permute-start.43
  157.2 19.4 %ssd_backward.1 = (bf16[1024,768]{1,0:T(8,128)(2,1)S(1)}, bf16[1024,256]{1,0:T(8,128)(2,1)S(1)}, bf16[128,1024]{1,0:T(8,128)(2,1)}, bf16[128,1024]{1,0:T(8,128)(...) custom-call(s32[1]{0:T(128)} %bitcast.rank_ref, ...), custom_call_target="tpu_custom_call" | custom-call | flops 28000000000 | bytes 40000000 | tf_op jit(solution)/shard_map/ssd_backward/pallas_call | solution.py:332
  176.7 1.9 collective-permute-done.42
  178.9 5.1 %weight_grad.6 = (bf16[192,768]{1,0:T(8,128)(2,1)}, bf16[192,768]{1,0:T(8,128)(2,1)}, bf16[576,768]{1,0:T(8,128)(2,1)}, bf16[576,768]{1,0:T(8,128)(2,1)}) custom-call(s32[8]{0:T(128)S(1)} %stack.88.idx_ref, bf16[1536,1024]{1,0:T(8,128)(2,1)S(1)} %copy-done.1, bf16[1024,768]{1,0:T(8,128)(2,1)S(1)} %get-tuple-element.491.rhs_ref.gx_ref), custom_call_target="tpu_custom_call" | custom-call | flops 20000000000 | bytes 40000000 | tf_op jit(solution)/shard_map/weight_grad/pallas_call | solution.py:831
  186.1 1.2 collective-permute-start.51
  188.1 6.1 %normed_term.2 = (bf16[256,1536]{1,0:T(8,128)(2,1)S(1)}, bf16[256,1536]{1,0:T(8,128)(2,1)S(1)}, f32[24,128]{1,0:T(8,128)S(1)}) custom-call(s32[1]{0:T(128)} %bitcast.rank_ref, bf16[1024,768]{1,0:T(8,128)(2,1)S(1)} %get-tuple-element.491.rhs_ref.gx_ref, bf16[1536,768]{1,0:T(8,128)(2,1)} %get-tuple-element.473.wx_ref, ...), custom_call_target="tpu_custom_call" | custom-call | flops 5000000000 | bytes 10000000 | tf_op jit(solution)/shard_map/normed_term/pallas_call | solution.py:901
  194.4 2.7 weight_grad.7
  197.1 6.1 %normed_term.3 = (bf16[256,1536]{1,0:T(8,128)(2,1)S(1)}, bf16[256,1536]{1,0:T(8,128)(2,1)S(1)}, f32[24,128]{1,0:T(8,128)S(1)}) custom-call(s32[1]{0:T(128)} %bitcast.rank_ref, bf16[1024,768]{1,0:T(8,128)(2,1)S(1)} %get-tuple-element.491.rhs_ref.gx_ref, bf16[1536,768]{1,0:T(8,128)(2,1)} %get-tuple-element.473.wx_ref, ...), custom_call_target="tpu_custom_call" | custom-call | flops 5000000000 | bytes 10000000 | tf_op jit(solution)/shard_map/normed_term/pallas_call | solution.py:901
  203.2 5.3 %collective-permute-done.49 = bf16[576,768]{1,0:T(8,128)(2,1)S(1)} collective-permute-done((bf16[576,768]{1,0:T(8,128)(2,1)S(1)}, bf16[576,768]{1,0:T(8,128)(2,1)S(1)}, u32[]{:S(2)}, u32[]{:S(2)}) %collective-permute-start.49) | collective-permute-done | bytes 884768 | tf_op jit(solution)/shard_map/ppermute | solution.py:1102
  209.1 1.8 collective-permute-done.50
  210.8 1.2 collective-permute-start.53
  212.8 1.5 collective-permute-start.55
  214.3 2.6 collective-permute-start.54
  217.1 14.9 %collective-permute-done.55 = bf16[880,128]{1,0:T(8,128)(2,1)S(1)} collective-permute-done((bf16[880,128]{1,0:T(8,128)(2,1)S(1)}, bf16[880,128]{1,0:T(8,128)(2,1)S(1)}, u32[]{:S(2)}, u32[]{:S(2)}) %collective-permute-start.55) | collective-permute-done | bytes 225312 | tf_op jit(solution)/shard_map/ppermute | solution.py:1102
  232.1 2.2 norm_backward.1.refs_0_
  234.5 2.7 collective-permute-start.62
  237.8 1.3 collective-permute-start.61
  242.0 2.5 add_convert_fusion
  245.4 4.5 %collective-permute-done.61.refs_9_.refs_2_ = bf16[208,896]{1,0:T(8,128)(2,1)S(1)} collective-permute-done((bf16[208,896]{1,0:T(8,128)(2,1)S(1)}, bf16[208,896]{1,0:T(8,128)(2,1)S(1)}, u32[]{:S(2)}, u32[]{:S(2)}) %collective-permute-start.61) | collective-permute-done | bytes 372768 | tf_op jit(solution)/shard_map/ppermute | solution.py:1093
  249.8 5.9 %collective-permute-done.60.refs_8_.refs_1_ = bf16[208,896]{1,0:T(8,128)(2,1)S(1)} collective-permute-done((bf16[208,896]{1,0:T(8,128)(2,1)S(1)}, bf16[208,896]{1,0:T(8,128)(2,1)S(1)}, u32[]{:S(2)}, u32[]{:S(2)}) %collective-permute-start.60) | collective-permute-done | bytes 372768 | tf_op jit(solution)/shard_map/ppermute | solution.py:1093
  258.5 4.1 %update_in.1 = (f32[192,2,768]{2,1,0:T(2,128)}, f32[192,2,768]{2,1,0:T(2,128)}) custom-call(f32[192,2,768]{2,1,0:T(2,128)} %w_ref.2, f32[192,2,768]{2,1,0:T(2,128)} %m_ref.2, bf16[192,768]{1,0:T(8,128)(2,1)S(1)} %copy-done.11, bf16[192,1536]{1,0:T(8,128)(2,1)S(1)} %collective-permute-done.56.refs_1_, bf16[192,768]{1,0:T(8,128)(2,1)S(1)} %collective-permute-done.51.refs_2_, ...), custom_call_target="tpu_custom_call" | custom-call | flops 100000000 | bytes 200000 | tf_op jit(solution)/shard_map/update_in/pallas_call | solution.py:988
  266.4 1.9 join_rows.1
  (302 shorter events, 38.0 us)
Async XLA Ops:
  3.6 21.5 %collective-permute-start.3 = (bf16[192,896]{1,0:T(8,128)(2,1)S(1)}, bf16[192,896]{1,0:T(8,128)(2,1)}, u32[]{:S(2)}, u32[]{:S(2)}) collective-permute-start(bf16[192,896]{1,0:T(8,128)(2,1)S(1)} %pack.1.refs_0_), channel_id=1, source_target_pairs={{24,0},{28,4},{0,8},{4,12},{8,16},{12,20},{16,24},{20,28},{25,1},{... | collective-permute-start | bytes 1032200 | tf_op jit(solution)/shard_map/ppermute | solution.py:1093
  6.7 20.2 %collective-permute-start.1 = (bf16[192,896]{1,0:T(8,128)(2,1)S(1)}, bf16[192,896]{1,0:T(8,128)(2,1)}, u32[]{:S(2)}, u32[]{:S(2)}) collective-permute-start(bf16[192,896]{1,0:T(8,128)(2,1)S(1)} %pack.1.refs_0_), channel_id=1, source_target_pairs={{8,0},{12,4},{16,8},{20,12},{24,16},{28,20},{0,24},{4,28},{9,1},{1... | collective-permute-start | bytes 1032200 | tf_op jit(solution)/shard_map/ppermute | solution.py:1093
  8.7 9.5 %collective-permute-start = (bf16[192,896]{1,0:T(8,128)(2,1)S(1)}, bf16[192,896]{1,0:T(8,128)(2,1)S(1)}, u32[]{:S(2)}, u32[]{:S(2)}) collective-permute-start(bf16[192,896]{1,0:T(8,128)(2,1)S(1)} %pack.1.refs_0_), channel_id=1, source_target_pairs={{4,0},{0,4},{12,8},{8,12},{20,16},{16,20},{28,24},{24,28},{5,1},{1... | collective-permute-start | bytes 1032200 | tf_op jit(solution)/shard_map/ppermute | solution.py:1102
  10.4 30.5 %collective-permute-start.6 = (bf16[1024,384]{1,0:T(8,128)(2,1)}, bf16[1024,384]{1,0:T(8,128)(2,1)}, u32[]{:S(2)}, u32[]{:S(2)}) collective-permute-start(bf16[1024,384]{1,0:T(8,128)(2,1)} %refs_0_.1), channel_id=1, source_target_pairs={{2,0},{3,1},{0,2},{1,3},{6,4},{7,5},{4,6},{5,7},{10,8},{11,9},{8,1... | collective-permute-start | bytes 2359304 | tf_op jit(solution)/shard_map/ppermute | solution.py:1106
  11.9 34.5 %collective-permute-start.11 = (bf16[1024,384]{1,0:T(8,128)(2,1)}, bf16[1024,384]{1,0:T(8,128)(2,1)}, u32[]{:S(2)}, u32[]{:S(2)}) collective-permute-start(bf16[1024,384]{1,0:T(8,128)(2,1)} %refs_0_.1), channel_id=1, source_target_pairs={{1,0},{0,1},{3,2},{2,3},{5,4},{4,5},{7,6},{6,7},{9,8},{8,9},{11,10... | collective-permute-start | bytes 2359304 | tf_op jit(solution)/shard_map/ppermute | solution.py:1106
  19.2 21.7 %collective-permute-start.2 = (bf16[192,896]{1,0:T(8,128)(2,1)S(1)}, bf16[192,896]{1,0:T(8,128)(2,1)}, u32[]{:S(2)}, u32[]{:S(2)}) collective-permute-start(bf16[192,896]{1,0:T(8,128)(2,1)S(1)} %pack.1.refs_0_), channel_id=1, source_target_pairs={{16,0},{20,4},{24,8},{28,12},{0,16},{4,20},{8,24},{12,28},{17,1},{... | collective-permute-start | bytes 1032200 | tf_op jit(solution)/shard_map/ppermute | solution.py:1093
  25.1 11.2 %collective-permute-start.5 = (bf16[192,896]{1,0:T(8,128)(2,1)}, bf16[192,896]{1,0:T(8,128)(2,1)S(1)}, u32[]{:S(2)}, u32[]{:S(2)}) collective-permute-start(bf16[192,896]{1,0:T(8,128)(2,1)} %collective-permute-done.3.refs_3_), channel_id=1, source_target_pairs={{4,0},{0,4},{12,8},{8,12},{20,16},{16,20},{28,24},{24,28},{5,1},{1... | collective-permute-start | bytes 1032200 | tf_op jit(solution)/shard_map/ppermute | solution.py:1102
  26.9 14.0 %collective-permute-start.4 = (bf16[192,896]{1,0:T(8,128)(2,1)}, bf16[192,896]{1,0:T(8,128)(2,1)S(1)}, u32[]{:S(2)}, u32[]{:S(2)}) collective-permute-start(bf16[192,896]{1,0:T(8,128)(2,1)} %collective-permute-done.1.refs_2_), channel_id=1, source_target_pairs={{4,0},{0,4},{12,8},{8,12},{20,16},{16,20},{28,24},{24,28},{5,1},{1... | collective-permute-start | bytes 1032200 | tf_op jit(solution)/shard_map/ppermute | solution.py:1102
  40.9 6.1 %collective-permute-start.12 = (bf16[1024,384]{1,0:T(8,128)(2,1)}, bf16[1024,384]{1,0:T(8,128)(2,1)S(1)}, u32[]{:S(2)}, u32[]{:S(2)}) collective-permute-start(bf16[1024,384]{1,0:T(8,128)(2,1)} %collective-permute-done.6.refs_2_), channel_id=1, source_target_pairs={{1,0},{0,1},{3,2},{2,3},{5,4},{4,5},{7,6},{6,7},{9,8},{8,9},{11,10... | collective-permute-start | bytes 2359304 | tf_op jit(solution)/shard_map/ppermute | solution.py:1106
  41.1 10.1 %collective-permute-start.9 = (bf16[192,768]{1,0:T(8,128)(2,1)}, bf16[192,768]{1,0:T(8,128)(2,1)S(1)}, u32[]{:S(2)}, u32[]{:S(2)}) collective-permute-start(bf16[192,768]{1,0:T(8,128)(2,1)} %pack_gate.1.refs_0_), channel_id=1, source_target_pairs={{4,0},{0,4},{12,8},{8,12},{20,16},{16,20},{28,24},{24,28},{5,1},{1... | collective-permute-start | bytes 884744 | tf_op jit(solution)/shard_map/ppermute | solution.py:1102
  42.6 11.9 %collective-permute-start.8 = (bf16[192,768]{1,0:T(8,128)(2,1)}, bf16[192,768]{1,0:T(8,128)(2,1)S(1)}, u32[]{:S(2)}, u32[]{:S(2)}) collective-permute-start(bf16[192,768]{1,0:T(8,128)(2,1)} %pack_gate.1.refs_0_), channel_id=1, source_target_pairs={{24,0},{28,4},{0,8},{4,12},{8,16},{12,20},{16,24},{20,28},{25,1},{... | collective-permute-start | bytes 884744 | tf_op jit(solution)/shard_map/ppermute | solution.py:1093
  44.2 15.3 %collective-permute-start.7 = (bf16[192,768]{1,0:T(8,128)(2,1)}, bf16[192,768]{1,0:T(8,128)(2,1)S(1)}, u32[]{:S(2)}, u32[]{:S(2)}) collective-permute-start(bf16[192,768]{1,0:T(8,128)(2,1)} %pack_gate.1.refs_0_), channel_id=1, source_target_pairs={{8,0},{12,4},{16,8},{20,12},{24,16},{28,20},{0,24},{4,28},{9,1},{1... | collective-permute-start | bytes 884744 | tf_op jit(solution)/shard_map/ppermute | solution.py:1093
  46.5 13.1 %collective-permute-start.10 = (bf16[192,896]{1,0:T(8,128)(2,1)}, bf16[192,896]{1,0:T(8,128)(2,1)S(1)}, u32[]{:S(2)}, u32[]{:S(2)}) collective-permute-start(bf16[192,896]{1,0:T(8,128)(2,1)} %collective-permute-done.2.refs_4_), channel_id=1, source_target_pairs={{4,0},{0,4},{12,8},{8,12},{20,16},{16,20},{28,24},{24,28},{5,1},{1... | collective-permute-start | bytes 1032200 | tf_op jit(solution)/shard_map/ppermute | solution.py:1102
  59.5 16.6 %collective-permute-start.16 = (bf16[192,768]{1,0:T(8,128)(2,1)S(1)}, bf16[192,768]{1,0:T(8,128)(2,1)S(1)}, u32[]{:S(2)}, u32[]{:S(2)}) collective-permute-start(bf16[192,768]{1,0:T(8,128)(2,1)S(1)} %copy-done.14), channel_id=1, source_target_pairs={{4,0},{0,4},{12,8},{8,12},{20,16},{16,20},{28,24},{24,28},{5,1},{1... | collective-permute-start | bytes 884744 | tf_op jit(solution)/shard_map/ppermute | solution.py:1102
  60.1 16.1 %collective-permute-start.15 = (bf16[192,768]{1,0:T(8,128)(2,1)S(1)}, bf16[192,768]{1,0:T(8,128)(2,1)S(1)}, u32[]{:S(2)}, u32[]{:S(2)}) collective-permute-start(bf16[192,768]{1,0:T(8,128)(2,1)S(1)} %collective-permute-done.7.refs_2_), channel_id=1, source_target_pairs={{4,0},{0,4},{12,8},{8,12},{20,16},{16,20},{28,24},{24,28},{5,1},{1... | collective-permute-start | bytes 884744 | tf_op jit(solution)/shard_map/ppermute | solution.py:1102
  61.6 15.1 %collective-permute-start.14 = (bf16[192,768]{1,0:T(8,128)(2,1)S(1)}, bf16[192,768]{1,0:T(8,128)(2,1)S(1)}, u32[]{:S(2)}, u32[]{:S(2)}) collective-permute-start(bf16[192,768]{1,0:T(8,128)(2,1)S(1)} %copy-done.12), channel_id=1, source_target_pairs={{16,0},{20,4},{24,8},{28,12},{0,16},{4,20},{8,24},{12,28},{17,1},{... | collective-permute-start | bytes 884744 | tf_op jit(solution)/shard_map/ppermute | solution.py:1093
  66.3 7.5 %collective-permute-start.13 = (bf16[64,1024]{1,0:T(8,128)(2,1)S(1)}, bf16[64,1024]{1,0:T(8,128)(2,1)S(1)}, u32[]{:S(2)}, u32[]{:S(2)}) collective-permute-start(bf16[64,1024]{1,0:T(8,128)(2,1)S(1)} %get-tuple-element.324.refs_0_), channel_id=1, source_target_pairs={{2,0},{3,1},{0,2},{1,3},{6,4},{7,5},{4,6},{5,7},{10,8},{11,9},{8,1... | collective-permute-start | bytes 393224 | tf_op jit(solution)/shard_map/ppermute | solution.py:1106
  67.8 6.4 %collective-permute-start.17 = (bf16[64,1024]{1,0:T(8,128)(2,1)S(1)}, bf16[64,1024]{1,0:T(8,128)(2,1)S(1)}, u32[]{:S(2)}, u32[]{:S(2)}) collective-permute-start(bf16[64,1024]{1,0:T(8,128)(2,1)S(1)} %get-tuple-element.324.refs_0_), channel_id=1, source_target_pairs={{1,0},{0,1},{3,2},{2,3},{5,4},{4,5},{7,6},{6,7},{9,8},{8,9},{11,10... | collective-permute-start | bytes 393224 | tf_op jit(solution)/shard_map/ppermute | solution.py:1106
  76.6 20.1 %collective-permute-start.22 = (bf16[192,768]{1,0:T(8,128)(2,1)S(1)}, bf16[192,768]{1,0:T(8,128)(2,1)S(1)}, u32[]{:S(2)}, u32[]{:S(2)}) collective-permute-start(bf16[192,768]{1,0:T(8,128)(2,1)S(1)} %copy-done.14), channel_id=1, source_target_pairs={{24,0},{28,4},{0,8},{4,12},{8,16},{12,20},{16,24},{20,28},{25,1},{... | collective-permute-start | bytes 884744 | tf_op jit(solution)/shard_map/ppermute | solution.py:1093
  77.6 19.2 %collective-permute-start.21 = (bf16[192,768]{1,0:T(8,128)(2,1)S(1)}, bf16[192,768]{1,0:T(8,128)(2,1)S(1)}, u32[]{:S(2)}, u32[]{:S(2)}) collective-permute-start(bf16[192,768]{1,0:T(8,128)(2,1)S(1)} %copy-done.14), channel_id=1, source_target_pairs={{8,0},{12,4},{16,8},{20,12},{24,16},{28,20},{0,24},{4,28},{9,1},{1... | collective-permute-start | bytes 884744 | tf_op jit(solution)/shard_map/ppermute | solution.py:1093
  80.5 16.3 %collective-permute-start.19 = (bf16[192,768]{1,0:T(8,128)(2,1)S(1)}, bf16[192,768]{1,0:T(8,128)(2,1)S(1)}, u32[]{:S(2)}, u32[]{:S(2)}) collective-permute-start(bf16[192,768]{1,0:T(8,128)(2,1)S(1)} %collective-permute-done.14.refs_4_), channel_id=1, source_target_pairs={{4,0},{0,4},{12,8},{8,12},{20,16},{16,20},{28,24},{24,28},{5,1},{1... | collective-permute-start | bytes 884744 | tf_op jit(solution)/shard_map/ppermute | solution.py:1102
  81.3 15.4 %collective-permute-start.20 = (bf16[192,768]{1,0:T(8,128)(2,1)S(1)}, bf16[192,768]{1,0:T(8,128)(2,1)S(1)}, u32[]{:S(2)}, u32[]{:S(2)}) collective-permute-start(bf16[192,768]{1,0:T(8,128)(2,1)S(1)} %collective-permute-done.8.refs_3_), channel_id=1, source_target_pairs={{4,0},{0,4},{12,8},{8,12},{20,16},{16,20},{28,24},{24,28},{5,1},{1... | collective-permute-start | bytes 884744 | tf_op jit(solution)/shard_map/ppermute | solution.py:1102
  96.8 13.4 %collective-permute-start.27 = (bf16[192,768]{1,0:T(8,128)(2,1)S(1)}, bf16[192,768]{1,0:T(8,128)(2,1)S(1)}, u32[]{:S(2)}, u32[]{:S(2)}) collective-permute-start(bf16[192,768]{1,0:T(8,128)(2,1)S(1)} %collective-permute-done.21.refs_2_), channel_id=1, source_target_pairs={{4,0},{0,4},{12,8},{8,12},{20,16},{16,20},{28,24},{24,28},{5,1},{1... | collective-permute-start | bytes 884744 | tf_op jit(solution)/shard_map/ppermute | solution.py:1102
  97.7 13.4 %collective-permute-start.26 = (bf16[192,768]{1,0:T(8,128)(2,1)S(1)}, bf16[192,768]{1,0:T(8,128)(2,1)S(1)}, u32[]{:S(2)}, u32[]{:S(2)}) collective-permute-start(bf16[192,768]{1,0:T(8,128)(2,1)S(1)} %copy-done.14), channel_id=1, source_target_pairs={{16,0},{20,4},{24,8},{28,12},{0,16},{4,20},{8,24},{12,28},{17,1},{... | collective-permute-start | bytes 884744 | tf_op jit(solution)/shard_map/ppermute | solution.py:1093
  97.7 13.4 %collective-permute-start.28 = (bf16[192,768]{1,0:T(8,128)(2,1)S(1)}, bf16[192,768]{1,0:T(8,128)(2,1)S(1)}, u32[]{:S(2)}, u32[]{:S(2)}) collective-permute-start(bf16[192,768]{1,0:T(8,128)(2,1)S(1)} %collective-permute-done.22.refs_3_), channel_id=1, source_target_pairs={{4,0},{0,4},{12,8},{8,12},{20,16},{16,20},{28,24},{24,28},{5,1},{1... | collective-permute-start | bytes 884744 | tf_op jit(solution)/shard_map/ppermute | solution.py:1102
  105.3 3.6 %collective-permute-start.25 = (f32[8,1024]{1,0:T(8,128)S(1)}, f32[8,1024]{1,0:T(8,128)S(1)}, u32[]{:S(2)}, u32[]{:S(2)}) collective-permute-start(f32[8,1024]{1,0:T(8,128)S(1)} %get-tuple-element.368), channel_id=1, source_target_pairs={{3,0},{2,1},{1,2},{0,3},{7,4},{6,5},{5,6},{4,7},{11,8},{10,9},{9,1... | collective-permute-start | bytes 98312 | tf_op jit(solution)/shard_map/ppermute | solution.py:1106
  105.4 4.0 %collective-permute-start.24 = (f32[8,1024]{1,0:T(8,128)S(1)}, f32[8,1024]{1,0:T(8,128)S(1)}, u32[]{:S(2)}, u32[]{:S(2)}) collective-permute-start(f32[8,1024]{1,0:T(8,128)S(1)} %get-tuple-element.368), channel_id=1, source_target_pairs={{2,0},{3,1},{0,2},{1,3},{6,4},{7,5},{4,6},{5,7},{10,8},{11,9},{8,1... | collective-permute-start | bytes 98312 | tf_op jit(solution)/shard_map/ppermute | solution.py:1106
  111.0 8.9 %collective-permute-start.29 = (bf16[192,768]{1,0:T(8,128)(2,1)S(1)}, bf16[192,768]{1,0:T(8,128)(2,1)S(1)}, u32[]{:S(2)}, u32[]{:S(2)}) collective-permute-start(bf16[192,768]{1,0:T(8,128)(2,1)S(1)} %collective-permute-done.26.refs_4_), channel_id=1, source_target_pairs={{4,0},{0,4},{12,8},{8,12},{20,16},{16,20},{28,24},{24,28},{5,1},{1... | collective-permute-start | bytes 884744 | tf_op jit(solution)/shard_map/ppermute | solution.py:1102
  112.5 6.9 %collective-permute-start.30 = (bf16[64,1536]{1,0:T(8,128)(2,1)}, bf16[64,1536]{1,0:T(8,128)(2,1)}, u32[]{:S(2)}, u32[]{:S(2)}) collective-permute-start(bf16[64,1536]{1,0:T(8,128)(2,1)} %get-tuple-element.479.refs_0_), channel_id=1, source_target_pairs={{2,0},{3,1},{0,2},{1,3},{6,4},{7,5},{4,6},{5,7},{10,8},{11,9},{8,1... | collective-permute-start | bytes 589832 | tf_op jit(solution)/shard_map/ppermute | solution.py:1106
  120.0 13.7 %collective-permute-start.35 = (bf16[192,768]{1,0:T(8,128)(2,1)}, bf16[192,768]{1,0:T(8,128)(2,1)S(1)}, u32[]{:S(2)}, u32[]{:S(2)}) collective-permute-start(bf16[192,768]{1,0:T(8,128)(2,1)} %get-tuple-element.408), channel_id=1, source_target_pairs={{4,0},{0,4},{12,8},{8,12},{20,16},{16,20},{28,24},{24,28},{5,1},{1... | collective-permute-start | bytes 884744 | tf_op jit(solution)/shard_map/ppermute | solution.py:1102
  125.6 8.0 %collective-permute-start.34 = (f32[8,1024]{1,0:T(8,128)S(1)}, f32[8,1024]{1,0:T(8,128)S(1)}, u32[]{:S(2)}, u32[]{:S(2)}) collective-permute-start(f32[8,1024]{1,0:T(8,128)S(1)} %get-tuple-element.398), channel_id=1, source_target_pairs={{3,0},{2,1},{1,2},{0,3},{7,4},{6,5},{5,6},{4,7},{11,8},{10,9},{9,1... | collective-permute-start | bytes 98312 | tf_op jit(solution)/shard_map/ppermute | solution.py:1106
  125.6 7.9 %collective-permute-start.33 = (f32[8,1024]{1,0:T(8,128)S(1)}, f32[8,1024]{1,0:T(8,128)S(1)}, u32[]{:S(2)}, u32[]{:S(2)}) collective-permute-start(f32[8,1024]{1,0:T(8,128)S(1)} %get-tuple-element.398), channel_id=1, source_target_pairs={{2,0},{3,1},{0,2},{1,3},{6,4},{7,5},{4,6},{5,7},{10,8},{11,9},{8,1... | collective-permute-start | bytes 98312 | tf_op jit(solution)/shard_map/ppermute | solution.py:1106
  126.2 7.4 %collective-permute-start.32 = (f32[8,1024]{1,0:T(8,128)S(1)}, f32[8,1024]{1,0:T(8,128)S(1)}, u32[]{:S(2)}, u32[]{:S(2)}) collective-permute-start(f32[8,1024]{1,0:T(8,128)S(1)} %get-tuple-element.398), channel_id=1, source_target_pairs={{1,0},{0,1},{3,2},{2,3},{5,4},{4,5},{7,6},{6,7},{9,8},{8,9},{11,10... | collective-permute-start | bytes 98312 | tf_op jit(solution)/shard_map/ppermute | solution.py:1106
  133.6 16.7 %collective-permute-start.39 = (bf16[1024,384]{1,0:T(8,128)(2,1)}, bf16[1024,384]{1,0:T(8,128)(2,1)S(1)}, u32[]{:S(2)}, u32[]{:S(2)}) collective-permute-start(bf16[1024,384]{1,0:T(8,128)(2,1)} %get-tuple-element.412), channel_id=1, source_target_pairs={{1,0},{0,1},{3,2},{2,3},{5,4},{4,5},{7,6},{6,7},{9,8},{8,9},{11,10... | collective-permute-start | bytes 2359304 | tf_op jit(solution)/shard_map/ppermute | solution.py:1106
  133.7 16.0 %collective-permute-start.31 = (bf16[384,768]{1,0:T(8,128)(2,1)}, bf16[384,768]{1,0:T(8,128)(2,1)S(1)}, u32[]{:S(2)}, u32[]{:S(2)}) collective-permute-start(bf16[384,768]{1,0:T(8,128)(2,1)} %get-tuple-element.389), channel_id=1, source_target_pairs={{4,0},{0,4},{12,8},{8,12},{20,16},{16,20},{28,24},{24,28},{5,1},{1... | collective-permute-start | bytes 1769480 | tf_op jit(solution)/shard_map/ppermute | solution.py:1102
  134.4 15.9 %collective-permute-start.36 = (bf16[192,768]{1,0:T(8,128)(2,1)S(1)}, bf16[192,768]{1,0:T(8,128)(2,1)S(1)}, u32[]{:S(2)}, u32[]{:S(2)}) collective-permute-start(bf16[192,768]{1,0:T(8,128)(2,1)S(1)} %add_convert_fusion.11), channel_id=1, source_target_pairs={{16,0},{20,4},{24,8},{28,12},{0,16},{4,20},{8,24},{12,28},{17,1},{... | collective-permute-start | bytes 884744 | tf_op jit(solution)/shard_map/ppermute | solution.py:1093
  136.7 11.8 %collective-permute-start.37 = (bf16[64,1536]{1,0:T(8,128)(2,1)}, bf16[64,1536]{1,0:T(8,128)(2,1)S(1)}, u32[]{:S(2)}, u32[]{:S(2)}) collective-permute-start(bf16[64,1536]{1,0:T(8,128)(2,1)} %get-tuple-element.479.refs_0_), channel_id=1, source_target_pairs={{1,0},{0,1},{3,2},{2,3},{5,4},{4,5},{7,6},{6,7},{9,8},{8,9},{11,10... | collective-permute-start | bytes 589832 | tf_op jit(solution)/shard_map/ppermute | solution.py:1106
  136.7 11.8 %collective-permute-start.38 = (bf16[64,1536]{1,0:T(8,128)(2,1)}, bf16[64,1536]{1,0:T(8,128)(2,1)S(1)}, u32[]{:S(2)}, u32[]{:S(2)}) collective-permute-start(bf16[64,1536]{1,0:T(8,128)(2,1)} %collective-permute-done.30.refs_2_), channel_id=1, source_target_pairs={{1,0},{0,1},{3,2},{2,3},{5,4},{4,5},{7,6},{6,7},{9,8},{8,9},{11,10... | collective-permute-start | bytes 589832 | tf_op jit(solution)/shard_map/ppermute | solution.py:1106
  151.4 25.2 %collective-permute-start.40 = (bf16[192,768]{1,0:T(8,128)(2,1)S(1)}, bf16[192,768]{1,0:T(8,128)(2,1)S(1)}, u32[]{:S(2)}, u32[]{:S(2)}) collective-permute-start(bf16[192,768]{1,0:T(8,128)(2,1)S(1)} %get-tuple-element.437), channel_id=1, source_target_pairs={{24,0},{28,4},{0,8},{4,12},{8,16},{12,20},{16,24},{20,28},{25,1},{... | collective-permute-start | bytes 884744 | tf_op jit(solution)/shard_map/ppermute | solution.py:1093
  151.5 25.2 %collective-permute-start.41 = (bf16[192,768]{1,0:T(8,128)(2,1)S(1)}, bf16[192,768]{1,0:T(8,128)(2,1)S(1)}, u32[]{:S(2)}, u32[]{:S(2)}) collective-permute-start(bf16[192,768]{1,0:T(8,128)(2,1)S(1)} %get-tuple-element.438), channel_id=1, source_target_pairs={{8,0},{12,4},{16,8},{20,12},{24,16},{28,20},{0,24},{4,28},{9,1},{1... | collective-permute-start | bytes 884744 | tf_op jit(solution)/shard_map/ppermute | solution.py:1093
  155.3 21.4 %collective-permute-start.43 = (bf16[1024,384]{1,0:T(8,128)(2,1)S(1)}, bf16[1024,384]{1,0:T(8,128)(2,1)S(1)}, u32[]{:S(2)}, u32[]{:S(2)}) collective-permute-start(bf16[1024,384]{1,0:T(8,128)(2,1)S(1)} %add_convert_fusion.2), channel_id=1, source_target_pairs={{2,0},{3,1},{0,2},{1,3},{6,4},{7,5},{4,6},{5,7},{10,8},{11,9},{8,1... | collective-permute-start | bytes 2359304 | tf_op jit(solution)/shard_map/ppermute | solution.py:1106
  156.5 27.6 %collective-permute-start.45 = (bf16[1024,384]{1,0:T(8,128)(2,1)S(1)}, bf16[1024,384]{1,0:T(8,128)(2,1)S(1)}, u32[]{:S(2)}, u32[]{:S(2)}) collective-permute-start(bf16[1024,384]{1,0:T(8,128)(2,1)S(1)} %copy-done.59), channel_id=1, source_target_pairs={{1,0},{0,1},{3,2},{2,3},{5,4},{4,5},{7,6},{6,7},{9,8},{8,9},{11,10... | collective-permute-start | bytes 2359304 | tf_op jit(solution)/shard_map/ppermute | solution.py:1106
  156.5 22.1 %collective-permute-start.42 = (bf16[576,768]{1,0:T(8,128)(2,1)S(1)}, bf16[576,768]{1,0:T(8,128)(2,1)S(1)}, u32[]{:S(2)}, u32[]{:S(2)}) collective-permute-start(bf16[576,768]{1,0:T(8,128)(2,1)S(1)} %copy-done.58), channel_id=1, source_target_pairs={{4,0},{0,4},{12,8},{8,12},{20,16},{16,20},{28,24},{24,28},{5,1},{1... | collective-permute-start | bytes 2654216 | tf_op jit(solution)/shard_map/ppermute | solution.py:1102
  178.7 5.4 %collective-permute-start.44 = (bf16[128,1024]{1,0:T(8,128)(2,1)}, bf16[128,1024]{1,0:T(8,128)(2,1)S(1)}, u32[]{:S(2)}, u32[]{:S(2)}) collective-permute-start(bf16[128,1024]{1,0:T(8,128)(2,1)} %get-tuple-element.468), channel_id=1, source_target_pairs={{1,0},{0,1},{3,2},{2,3},{5,4},{4,5},{7,6},{6,7},{9,8},{8,9},{11,10... | collective-permute-start | bytes 786440 | tf_op jit(solution)/shard_map/ppermute | solution.py:1106
  178.9 15.3 %collective-permute-start.47 = (bf16[192,768]{1,0:T(8,128)(2,1)S(1)}, bf16[192,768]{1,0:T(8,128)(2,1)S(1)}, u32[]{:S(2)}, u32[]{:S(2)}) collective-permute-start(bf16[192,768]{1,0:T(8,128)(2,1)S(1)} %add_convert_fusion.8), channel_id=1, source_target_pairs={{16,0},{20,4},{24,8},{28,12},{0,16},{4,20},{8,24},{12,28},{17,1},{... | collective-permute-start | bytes 884744 | tf_op jit(solution)/shard_map/ppermute | solution.py:1093
  184.2 10.0 %collective-permute-start.46 = (bf16[64,1024]{1,0:T(8,128)(2,1)S(1)}, bf16[64,1024]{1,0:T(8,128)(2,1)S(1)}, u32[]{:S(2)}, u32[]{:S(2)}) collective-permute-start(bf16[64,1024]{1,0:T(8,128)(2,1)S(1)} %slice.308), channel_id=1, source_target_pairs={{2,0},{3,1},{0,2},{1,3},{6,4},{7,5},{4,6},{5,7},{10,8},{11,9},{8,1... | collective-permute-start | bytes 393224 | tf_op jit(solution)/shard_map/ppermute | solution.py:1106
  185.2 23.8 %collective-permute-start.52 = (bf16[192,768]{1,0:T(8,128)(2,1)S(1)}, bf16[192,768]{1,0:T(8,128)(2,1)S(1)}, u32[]{:S(2)}, u32[]{:S(2)}) collective-permute-start(bf16[192,768]{1,0:T(8,128)(2,1)S(1)} %get-tuple-element.578), channel_id=1, source_target_pairs={{8,0},{12,4},{16,8},{20,12},{24,16},{28,20},{0,24},{4,28},{9,1},{1... | collective-permute-start | bytes 884744 | tf_op jit(solution)/shard_map/ppermute | solution.py:1093
  186.1 22.9 %collective-permute-start.51 = (bf16[192,768]{1,0:T(8,128)(2,1)S(1)}, bf16[192,768]{1,0:T(8,128)(2,1)S(1)}, u32[]{:S(2)}, u32[]{:S(2)}) collective-permute-start(bf16[192,768]{1,0:T(8,128)(2,1)S(1)} %get-tuple-element.579), channel_id=1, source_target_pairs={{24,0},{28,4},{0,8},{4,12},{8,16},{12,20},{16,24},{20,28},{25,1},{... | collective-permute-start | bytes 884744 | tf_op jit(solution)/shard_map/ppermute | solution.py:1093
  187.3 21.2 %collective-permute-start.49 = (bf16[576,768]{1,0:T(8,128)(2,1)S(1)}, bf16[576,768]{1,0:T(8,128)(2,1)S(1)}, u32[]{:S(2)}, u32[]{:S(2)}) collective-permute-start(bf16[576,768]{1,0:T(8,128)(2,1)S(1)} %copy-done.57), channel_id=1, source_target_pairs={{4,0},{0,4},{12,8},{8,12},{20,16},{16,20},{28,24},{24,28},{5,1},{1... | collective-permute-start | bytes 2654216 | tf_op jit(solution)/shard_map/ppermute | solution.py:1102
  194.2 14.3 %collective-permute-start.48 = (bf16[256,1536]{1,0:T(8,128)(2,1)S(1)}, bf16[256,1536]{1,0:T(8,128)(2,1)S(1)}, u32[]{:S(2)}, u32[]{:S(2)}) collective-permute-start(bf16[256,1536]{1,0:T(8,128)(2,1)S(1)} %get-tuple-element.490), channel_id=1, source_target_pairs={{1,0},{0,1},{3,2},{2,3},{5,4},{4,5},{7,6},{6,7},{9,8},{8,9},{11,10... | collective-permute-start | bytes 2359304 | tf_op jit(solution)/shard_map/ppermute | solution.py:1106
  210.8 21.3 %collective-permute-start.53 = (bf16[256,1536]{1,0:T(8,128)(2,1)S(1)}, bf16[256,1536]{1,0:T(8,128)(2,1)S(1)}, u32[]{:S(2)}, u32[]{:S(2)}) collective-permute-start(bf16[256,1536]{1,0:T(8,128)(2,1)S(1)} %add_convert_fusion.1), channel_id=1, source_target_pairs={{2,0},{3,1},{0,2},{1,3},{6,4},{7,5},{4,6},{5,7},{10,8},{11,9},{8,1... | collective-permute-start | bytes 2359304 | tf_op jit(solution)/shard_map/ppermute | solution.py:1106
  212.1 20.0 %collective-permute-start.56 = (bf16[192,1536]{1,0:T(8,128)(2,1)S(1)}, bf16[192,1536]{1,0:T(8,128)(2,1)S(1)}, u32[]{:S(2)}, u32[]{:S(2)}) collective-permute-start(bf16[192,1536]{1,0:T(8,128)(2,1)S(1)} %pad_maximum_fusion), channel_id=1, source_target_pairs={{4,0},{0,4},{12,8},{8,12},{20,16},{16,20},{28,24},{24,28},{5,1},{1... | collective-permute-start | bytes 1769480 | tf_op jit(solution)/shard_map/ppermute | solution.py:1102
  212.8 19.3 %collective-permute-start.55 = (bf16[880,128]{1,0:T(8,128)(2,1)S(1)}, bf16[880,128]{1,0:T(8,128)(2,1)S(1)}, u32[]{:S(2)}, u32[]{:S(2)}) collective-permute-start(bf16[880,128]{1,0:T(8,128)(2,1)S(1)} %pad_maximum_fusion.3), channel_id=1, source_target_pairs={{4,0},{0,4},{12,8},{8,12},{20,16},{16,20},{28,24},{24,28},{5,1},{1... | collective-permute-start | bytes 675848 | tf_op jit(solution)/shard_map/ppermute | solution.py:1102
  214.3 17.8 %collective-permute-start.54 = (bf16[192,768]{1,0:T(8,128)(2,1)S(1)}, bf16[192,768]{1,0:T(8,128)(2,1)S(1)}, u32[]{:S(2)}, u32[]{:S(2)}) collective-permute-start(bf16[192,768]{1,0:T(8,128)(2,1)S(1)} %get-tuple-element.512), channel_id=1, source_target_pairs={{16,0},{20,4},{24,8},{28,12},{0,16},{4,20},{8,24},{12,28},{17,1},{... | collective-permute-start | bytes 884744 | tf_op jit(solution)/shard_map/ppermute | solution.py:1093
  234.5 10.9 %collective-permute-start.62 = (bf16[304,128]{1,0:T(8,128)(2,1)S(1)}, bf16[304,128]{1,0:T(8,128)(2,1)S(1)}, u32[]{:S(2)}, u32[]{:S(2)}) collective-permute-start(bf16[304,128]{1,0:T(8,128)(2,1)S(1)} %pad_maximum_fusion.4), channel_id=1, source_target_pairs={{16,0},{20,4},{24,8},{28,12},{0,16},{4,20},{8,24},{12,28},{17,1},{... | collective-permute-start | bytes 233480 | tf_op jit(solution)/shard_map/ppermute | solution.py:1093
  237.2 8.2 %collective-permute-start.63 = (bf16[192,768]{1,0:T(8,128)(2,1)S(1)}, bf16[192,768]{1,0:T(8,128)(2,1)S(1)}, u32[]{:S(2)}, u32[]{:S(2)}) collective-permute-start(bf16[192,768]{1,0:T(8,128)(2,1)S(1)} %copy-done.60), channel_id=1, source_target_pairs={{4,0},{0,4},{12,8},{8,12},{20,16},{16,20},{28,24},{24,28},{5,1},{1... | collective-permute-start | bytes 884744 | tf_op jit(solution)/shard_map/ppermute | solution.py:1102
  237.8 12.0 %collective-permute-start.61 = (bf16[208,896]{1,0:T(8,128)(2,1)S(1)}, bf16[208,896]{1,0:T(8,128)(2,1)S(1)}, u32[]{:S(2)}, u32[]{:S(2)}) collective-permute-start(bf16[208,896]{1,0:T(8,128)(2,1)S(1)} %get-tuple-element.588), channel_id=1, source_target_pairs={{8,0},{12,4},{16,8},{20,12},{24,16},{28,20},{0,24},{4,28},{9,1},{1... | collective-permute-start | bytes 1118216 | tf_op jit(solution)/shard_map/ppermute | solution.py:1093
  239.1 16.6 %collective-permute-start.60 = (bf16[208,896]{1,0:T(8,128)(2,1)S(1)}, bf16[208,896]{1,0:T(8,128)(2,1)S(1)}, u32[]{:S(2)}, u32[]{:S(2)}) collective-permute-start(bf16[208,896]{1,0:T(8,128)(2,1)S(1)} %get-tuple-element.589), channel_id=1, source_target_pairs={{24,0},{28,4},{0,8},{4,12},{8,16},{12,20},{16,24},{20,28},{25,1},{... | collective-permute-start | bytes 1118216 | tf_op jit(solution)/shard_map/ppermute | solution.py:1093
  239.9 18.4 %collective-permute-start.57 = (bf16[256,1536]{1,0:T(8,128)(2,1)S(1)}, bf16[256,1536]{1,0:T(8,128)(2,1)S(1)}, u32[]{:S(2)}, u32[]{:S(2)}) collective-permute-start(bf16[256,1536]{1,0:T(8,128)(2,1)S(1)} %norm_backward.1.refs_0_), channel_id=1, source_target_pairs={{2,0},{3,1},{0,2},{1,3},{6,4},{7,5},{4,6},{5,7},{10,8},{11,9},{8,1... | collective-permute-start | bytes 2359304 | tf_op jit(solution)/shard_map/ppermute | solution.py:1106
  256.5 7.8 %collective-permute-start.66 = (f32[232,128]{1,0:T(8,128)S(1)}, f32[232,128]{1,0:T(8,128)S(1)}, u32[]{:S(2)}, u32[]{:S(2)}) collective-permute-start(f32[232,128]{1,0:T(8,128)S(1)} %get-tuple-element.562.refs_0_), channel_id=1, source_target_pairs={{3,0},{2,1},{1,2},{0,3},{7,4},{6,5},{5,6},{4,7},{11,8},{10,9},{9,1... | collective-permute-start | bytes 356360 | tf_op jit(solution)/shard_map/ppermute | solution.py:1106
  256.5 7.8 %collective-permute-start.65 = (f32[232,128]{1,0:T(8,128)S(1)}, f32[232,128]{1,0:T(8,128)S(1)}, u32[]{:S(2)}, u32[]{:S(2)}) collective-permute-start(f32[232,128]{1,0:T(8,128)S(1)} %get-tuple-element.562.refs_0_), channel_id=1, source_target_pairs={{2,0},{3,1},{0,2},{1,3},{6,4},{7,5},{4,6},{5,7},{10,8},{11,9},{8,1... | collective-permute-start | bytes 356360 | tf_op jit(solution)/shard_map/ppermute | solution.py:1106
  257.4 6.9 %collective-permute-start.64 = (f32[232,128]{1,0:T(8,128)S(1)}, f32[232,128]{1,0:T(8,128)S(1)}, u32[]{:S(2)}, u32[]{:S(2)}) collective-permute-start(f32[232,128]{1,0:T(8,128)S(1)} %get-tuple-element.562.refs_0_), channel_id=1, source_target_pairs={{1,0},{0,1},{3,2},{2,3},{5,4},{4,5},{7,6},{6,7},{9,8},{8,9},{11,10... | collective-permute-start | bytes 356360 | tf_op jit(solution)/shard_map/ppermute | solution.py:1106
  258.3 5.9 %collective-permute-start.59 = (bf16[256,1536]{1,0:T(8,128)(2,1)S(1)}, bf16[256,1536]{1,0:T(8,128)(2,1)S(1)}, u32[]{:S(2)}, u32[]{:S(2)}) collective-permute-start(bf16[256,1536]{1,0:T(8,128)(2,1)S(1)} %collective-permute-done.57.refs_2_), channel_id=1, source_target_pairs={{1,0},{0,1},{3,2},{2,3},{5,4},{4,5},{7,6},{6,7},{9,8},{8,9},{11,10... | collective-permute-start | bytes 2359304 | tf_op jit(solution)/shard_map/ppermute | solution.py:1106
  263.8 2.6 collective-permute-start.58
  (64 other events, 718.2 us)

commit v10 on v9

--- a/solution.py
+++ b/solution.py
@@ -876,17 +876,17 @@
     )(rank, gated_out, w_out)
 
 
-def term_kernel(rank_ref, gx_ref, wx_ref, gg_ref, wg_ref, gs_ref, ws_ref, gb_ref, hidden_ref, inv_ref, *refs, apart):
-    wbt_refs, outs, dgain_ref = refs[:4], refs[4:-1], refs[-1]
+def term_kernel(rank_ref, gx_ref, wx_ref, gg_ref, wg_ref, gs_ref, ws_ref, gb_ref, inv_ref, *refs, apart):
+    hidden_refs, wbt_refs, outs, dgain_ref = refs[:len(apart)], refs[len(apart):len(apart) + 4], refs[len(apart) + 4:-1], refs[-1]
     w_bct = jnp.concatenate([ref[...] for ref in wbt_refs], axis=0)
     gain = None
-    for r, out in zip(apart, outs):
+    for r, out, hidden_ref in zip(apart, outs, hidden_refs):
         rows = out.shape[0]
         span = pl.ds(pl.multiple_of((rank_ref[0] ^ r) * rows, rows), rows)
         total = dot_nt(gx_ref[span, :], wx_ref[...]) + dot_nt(gg_ref[span, :], wg_ref[...])
         total = total + dot_nt(gs_ref[span, :], ws_ref[...]) + dot_nn(gb_ref[span, :], w_bct)
         out[...] = total.astype(bf16)
-        normed = hidden_ref[span, :].astype(f32) * row_to_column(inv_ref[0:1, span])
+        normed = hidden_ref[...].astype(f32) * row_to_column(inv_ref[0:1, span])
         own = jnp.sum(total * normed, axis=0, keepdims=True)
         gain = own if gain is None else gain + own
     cut = [gain[:, i:i + LANES] for i in range(0, gain.shape[1], LANES)]
@@ -897,31 +897,33 @@
     tokens, channels = dx.shape
     depth = w_a.shape[0]
     rows = tokens // ranks
-    whole = lambda i: (0, 0)
+    whole = lambda i, rank_ref: (0, 0)
     return pl.pallas_call(
         functools.partial(term_kernel, apart=apart),
+        grid_spec=pltpu.PrefetchScalarGridSpec(
+        num_scalar_prefetch=1,
         grid=(depth // TILE_D,),
         in_specs=[
-            pl.BlockSpec(memory_space=pltpu.SMEM),
             pl.BlockSpec(dx.shape, whole),
-            pl.BlockSpec((TILE_D, channels), lambda i: (i, 0)),
+            pl.BlockSpec((TILE_D, channels), lambda i, rank_ref: (i, 0)),
             pl.BlockSpec(dgate.shape, whole),
-            pl.BlockSpec((TILE_D, channels), lambda i: (i, 0)),
+            pl.BlockSpec((TILE_D, channels), lambda i, rank_ref: (i, 0)),
             pl.BlockSpec(dstep.shape, whole),
-            pl.BlockSpec((TILE_D, LANES), lambda i: (i, 0)),
+            pl.BlockSpec((TILE_D, LANES), lambda i, rank_ref: (i, 0)),
             pl.BlockSpec(dbc.shape, whole),
-            pl.BlockSpec((tokens, TILE_D), lambda i: (0, i)),
             pl.BlockSpec(inv_rms.shape, whole),
         ]
-        + [pl.BlockSpec((w.shape[0], TILE_D), lambda i: (0, i)) for w in w_bct],
-        out_specs=[pl.BlockSpec((rows, TILE_D), lambda i: (0, i))] * len(apart) + [pl.BlockSpec((8, LANES), lambda i: (i, 0))],
+        + [pl.BlockSpec((rows, TILE_D), functools.partial(lambda r, i, rank_ref: (rank_ref[0] ^ r, i), r)) for r in apart]
+        + [pl.BlockSpec((w.shape[0], TILE_D), lambda i, rank_ref: (0, i)) for w in w_bct],
+        out_specs=[pl.BlockSpec((rows, TILE_D), lambda i, rank_ref: (0, i))] * len(apart) + [pl.BlockSpec((8, LANES), lambda i, rank_ref: (i, 0))],
+        ),
         out_shape=[jax.ShapeDtypeStruct((rows, depth), bf16)] * len(apart)
         + [jax.ShapeDtypeStruct((8 * (depth // TILE_D), LANES), f32)],
         compiler_params=params(32),
         cost_estimate=cost(5 if 2 in apart else 5),
         name="normed_term",
     )(
-        rank, dx, from_hbm(w_a), dgate, from_hbm(w_b), dstep, from_hbm(w_s), dbc, from_hbm(hidden), inv_rms, *w_bct
+        rank, dx, from_hbm(w_a), dgate, from_hbm(w_b), dstep, from_hbm(w_s), dbc, inv_rms, *[from_hbm(hidden) for _ in apart], *w_bct
     )
 
 

time: 269 us -> 269 us (level)
  no operation moved by 1% of the time
where the time goes in v10:
time: 269 us; the launch traced here: 268 us
  Pallas kernels  118 us (44%)
  waiting for transfers between devices  66.2 us (25%)
  starting transfers between devices  65.5 us (24%)
  other arithmetic  11.1 us (4%)
  local copies, waits for them, and re-layouts  5.23 us (2%)
    ppermute x19, waiting for transfers between devices, inner_flip(): lax.ppermute(v, 'dp', [(d ^ 1, d) for d in range(lax.axis_size('dp'))])  39.6 us
    ppermute x19, starting transfers between devices, outer_from(): lax.ppermute(v, 'dp', [((o + k) % n * 2 + x, o * 2 + x) for o in range(n)...  30.6 us
    ppermute x19, waiting for transfers between devices, outer_from(): lax.ppermute(v, 'dp', [((o + k) % n * 2 + x, o * 2 + x) for o in range(n)...  20.7 us
    ppermute x19, starting transfers between devices, inner_flip(): lax.ppermute(v, 'dp', [(d ^ 1, d) for d in range(lax.axis_size('dp'))])  19.7 us
    pallas_call x1, Pallas kernels, ssd_backward(): pl.pallas_call(ssd_backward_kernel, grid=(count,), in_specs=[pl.BlockSpec...  19.4 us
    pallas_call x4, Pallas kernels, weight_grad(): pl.pallas_call(functools.partial(weight_grad_kernel, rows=rows, turned=tu...  18.1 us
    ppermute x29, starting transfers between devices, rank_flip(): lax.ppermute(v, 'mp', [(m ^ bit, m) for m in range(lax.axis_size('mp'))])  15.2 us
    pallas_call x1, Pallas kernels, ssd_forward(): pl.pallas_call(ssd_forward_kernel, grid=(count,), in_specs=common_specs(l...  14.2 us
  transfers between devices with their start and end apart: 67, of which 22 were waited for; matrix products, arithmetic and copies ran while one was open for 5% of the time, Pallas kernels for 42%

profile of v10, /device:TPU:0, one launch (start us, length us, event | category | flops | bytes accessed | tf_op | source)
XLA Modules:
  0.0 268.3 jit_solution(14463082712271223698)
XLA Ops:
  0.7 2.8 %pack.1.refs_0_ = bf16[192,896]{1,0:T(8,128)(2,1)S(1)} custom-call(s32[1]{0:T(128)} %bitcast.rank_ref, f32[192,2,768]{2,1,0:T(2,128)} %w_ref.2, f32[192,256]{1,0:T(8,128)} %w_ref.3, f32[12,192]{1,0:T(8,128)} %bitcast.47), custom_call_target="tpu_custom_call" | custom-call | flops 2000000000 | bytes 4000000 | tf_op jit(solution)/shard_map/pack/pallas_call | solution.py:476
  3.6 3.1 %collective-permute-start.3 = (bf16[192,896]{1,0:T(8,128)(2,1)S(1)}, bf16[192,896]{1,0:T(8,128)(2,1)}, u32[]{:S(2)}, u32[]{:S(2)}) collective-permute-start(bf16[192,896]{1,0:T(8,128)(2,1)S(1)} %pack.1.refs_0_), channel_id=1, source_target_pairs={{24,0},{28,4},{0,8},{4,12},{8,16},{12,20},{16,24},{20,28},{25,1},{... | collective-permute-start | bytes 1032200 | tf_op jit(solution)/shard_map/ppermute | solution.py:1095
  6.7 2.1 collective-permute-start.1
  8.7 1.6 collective-permute-start
  10.4 1.5 collective-permute-start.6
  14.9 3.3 %collective-permute-done.refs_1_ = bf16[192,896]{1,0:T(8,128)(2,1)S(1)} collective-permute-done((bf16[192,896]{1,0:T(8,128)(2,1)S(1)}, bf16[192,896]{1,0:T(8,128)(2,1)S(1)}, u32[]{:S(2)}, u32[]{:S(2)}) %collective-permute-start) | collective-permute-done | bytes 344096 | tf_op jit(solution)/shard_map/ppermute | solution.py:1104
  20.6 3.6 %prepare.1 = (bf16[1024,1536]{1,0:T(8,128)(2,1)}, bf16[1536,1024]{1,0:T(8,128)(2,1)}, f32[8,1024]{1,0:T(8,128)S(1)}) custom-call(bf16[1024,1536]{1,0:T(8,128)(2,1)S(1)} %copy-done.4, f32[8,1536]{1,0:T(8,128)S(1)} %copy-done.15), custom_call_target="tpu_custom_call" | custom-call | flops 12000000000 | bytes 24000000 | tf_op jit(solution)/shard_map/prepare/pallas_call | solution.py:440
  25.1 1.5 collective-permute-start.5
  28.0 2.8 %pack_gate.1.refs_0_ = bf16[192,768]{1,0:T(8,128)(2,1)} custom-call(f32[192,2,768]{2,1,0:T(2,128)} %w_ref.2), custom_call_target="tpu_custom_call" | custom-call | flops 2000000000 | bytes 4000000 | tf_op jit(solution)/shard_map/pack_gate/pallas_call | solution.py:495
  30.8 5.6 %collective-permute-done.5.refs_6_ = bf16[192,896]{1,0:T(8,128)(2,1)S(1)} collective-permute-done((bf16[192,896]{1,0:T(8,128)(2,1)}, bf16[192,896]{1,0:T(8,128)(2,1)S(1)}, u32[]{:S(2)}, u32[]{:S(2)}) %collective-permute-start.5) | collective-permute-done | bytes 344096 | tf_op jit(solution)/shard_map/ppermute | solution.py:1104
  36.3 4.5 %collective-permute-done.4.refs_5_ = bf16[192,896]{1,0:T(8,128)(2,1)S(1)} collective-permute-done((bf16[192,896]{1,0:T(8,128)(2,1)}, bf16[192,896]{1,0:T(8,128)(2,1)S(1)}, u32[]{:S(2)}, u32[]{:S(2)}) %collective-permute-start.4) | collective-permute-done | bytes 344096 | tf_op jit(solution)/shard_map/ppermute | solution.py:1104
  41.1 1.6 collective-permute-start.9
  42.6 1.6 collective-permute-start.8
  44.2 2.2 collective-permute-start.7
  47.0 2.5 join_columns.1
  49.5 1.7 collective-permute-done.9.refs_1_
  51.2 3.4 %collective-permute-done.8.refs_3_ = bf16[192,768]{1,0:T(8,128)(2,1)S(1)} collective-permute-done((bf16[192,768]{1,0:T(8,128)(2,1)}, bf16[192,768]{1,0:T(8,128)(2,1)S(1)}, u32[]{:S(2)}, u32[]{:S(2)}) %collective-permute-start.8) | collective-permute-done | bytes 294944 | tf_op jit(solution)/shard_map/ppermute | solution.py:1095
  54.5 5.0 %collective-permute-done.7.refs_2_ = bf16[192,768]{1,0:T(8,128)(2,1)S(1)} collective-permute-done((bf16[192,768]{1,0:T(8,128)(2,1)}, bf16[192,768]{1,0:T(8,128)(2,1)S(1)}, u32[]{:S(2)}, u32[]{:S(2)}) %collective-permute-start.7) | collective-permute-done | bytes 294944 | tf_op jit(solution)/shard_map/ppermute | solution.py:1095
  60.1 1.5 collective-permute-start.15
  61.6 1.4 collective-permute-start.14
  63.0 3.3 %project_small.1 = (f32[128,1024]{1,0:T(8,128)S(1)}, bf16[64,1024]{1,0:T(8,128)(2,1)S(1)}, bf16[1536,128]{1,0:T(8,128)(2,1)}, bf16[64,1536]{1,0:T(8,128)(2,1)}) custom-call(s32[8]{0:T(128)S(1)} %stack.88.idx_ref, bf16[1024,1536]{1,0:T(8,128)(2,1)S(1)} %copy-done.2, bf16[192,896]{1,0:T(8,128)(2,1)S(1)} %pack.1.refs_0_, bf16[192,896]{1,0:T(8,128)(2,1)S(1)} %copy-done.10, ...), custom_call_target="tpu_custom_call" | custom-call | flops 20000000000 | bytes 40000000 | tf_op jit(solution)/shard_map/project_small/pallas_call | solution.py:598
  66.3 1.5 collective-permute-start.13
  67.8 5.9 %project.1 = (f32[1024,768]{1,0:T(8,128)}, bf16[1536,768]{1,0:T(8,128)(2,1)}) custom-call(s32[8]{0:T(128)S(1)} %stack.88.idx_ref, bf16[1024,1536]{1,0:T(8,128)(2,1)S(1)} %copy-done.2, bf16[192,896]{1,0:T(8,128)(2,1)S(1)} %pack.1.refs_0_, bf16[192,896]{1,0:T(8,128)(2,1)S(1)} %copy-done.10, bf16[192,896]{1,0:T(8,128)(2,1)} %collective-permute-done.1.refs_2_, ...), custom_call_target="tpu_custom_call" | custom-call | flops 100000000 | bytes 200000 | tf_op jit(solution)/shard_map/project/pallas_call | solution.py:634
  77.6 2.9 %collective-permute-start.21 = (bf16[192,768]{1,0:T(8,128)(2,1)S(1)}, bf16[192,768]{1,0:T(8,128)(2,1)S(1)}, u32[]{:S(2)}, u32[]{:S(2)}) collective-permute-start(bf16[192,768]{1,0:T(8,128)(2,1)S(1)} %copy-done.14), channel_id=1, source_target_pairs={{8,0},{12,4},{16,8},{20,12},{24,16},{28,20},{0,24},{4,28},{9,1},{1... | collective-permute-start | bytes 884744 | tf_op jit(solution)/shard_map/ppermute | solution.py:1095
  81.3 1.2 collective-permute-start.20
  82.5 14.2 %ssd_forward.1 = (f32[1024,768]{1,0:T(8,128)}, bf16[8,128,768]{2,1,0:T(8,128)(2,1)}, f32[1024,768]{1,0:T(8,128)}, bf16[1024,768]{1,0:T(8,128)(2,1)}, bf16[1024,7...) custom-call(f32[1024,768]{1,0:T(8,128)} %get-tuple-element.341.x_ref, ...), custom_call_target="tpu_custom_call" | custom-call | flops 14000000000 | bytes 40000000 | tf_op jit(solution)/shard_map/ssd_forward/pallas_call | solution.py:293
  97.7 1.2 collective-permute-start.28
  98.9 6.5 %gate_forward.1 = (f32[1024,768]{1,0:T(8,128)S(1)}, f32[8,1024]{1,0:T(8,128)S(1)}, bf16[1536,768]{1,0:T(8,128)(2,1)}) custom-call(s32[8]{0:T(128)S(1)} %stack.88.idx_ref, bf16[1024,1536]{1,0:T(8,128)(2,1)S(1)} %copy-done.2, f32[1024,768]{1,0:T(8,128)} %get-tuple-element.381.mixed_ref, bf16[192,768]{1,0:T(8,128)(2,1)S(1)} %copy-done.12, ...), custom_call_target="tpu_custom_call" | custom-call | flops 100000000 | bytes 200000 | tf_op jit(solution)/shard_map/gate_forward/pallas_call | solution.py:676
  105.4 1.6 collective-permute-start.24
  106.9 2.0 collective-permute-done.25
  111.0 1.5 collective-permute-start.29
  113.0 1.1 gated_norm.1.rhs_ref.lhs_ref
  114.2 5.1 %weight_grad.4 = (bf16[192,768]{1,0:T(8,128)(2,1)}, bf16[192,768]{1,0:T(8,128)(2,1)}, bf16[576,768]{1,0:T(8,128)(2,1)}, bf16[384,768]{1,0:T(8,128)(2,1)}, bf16[192,768]{1,0:T(8,128)(2,1)}) custom-call(s32[8]{0:T(128)S(1)} %stack.88.idx_ref, bf16[1536,1024]{1,0:T(8,128)(2,1)S(1)} %get-tuple-element.382.lhs_ref, bf16[1024,768]{1,0:T(8,128)(2,1)S(1)} %gated_norm.1.rhs_ref.lhs_ref), custom_call_target="tpu_custom_call" | custom-call | flops 100000000 | bytes 200000 | tf_op jit(solution)/shard_map/weight_grad/pallas_call | solution.py:831
  120.0 1.5 collective-permute-start.35
  121.5 4.1 %grad_gout.1 = (f32[1024,768]{1,0:T(8,128)S(1)}, f32[8,1024]{1,0:T(8,128)S(1)}, bf16[1536,768]{1,0:T(8,128)(2,1)S(1)}) custom-call(s32[8]{0:T(128)S(1)} %stack.88.idx_ref, bf16[1024,1536]{1,0:T(8,128)(2,1)S(1)} %get-tuple-element.391.cot_ref, f32[1024,768]{1,0:T(8,128)S(1)} %get-tuple-element.380.gate_ref, f32[1024,768]{1,0:T(8,128)S(1)} %copy-done, ...), custom_call_target="tpu_custom_call" | custom-call | flops 20000000000 | bytes 40000000 | tf_op jit(solution)/shard_map/grad_gout/pallas_call | solution.py:742
  126.2 1.3 collective-permute-start.32
  127.5 6.1 %out_partial.1 = (bf16[1024,384]{1,0:T(8,128)(2,1)}, bf16[1024,384]{1,0:T(8,128)(2,1)}, bf16[1024,384]{1,0:T(8,128)(2,1)}, bf16[1024,384]{1,0:T(8,128)(2,1)}) custom-call(s32[1]{0:T(128)} %bitcast.rank_ref, bf16[1024,768]{1,0:T(8,128)(2,1)S(1)} %gated_norm.1.rhs_ref.lhs_ref, bf16[1536,768]{1,0:T(8,128)(2,1)S(1)} %get-tuple-element.401.w_ref), custom_call_target="tpu_custom_call" | custom-call | flops 100000000 | bytes 200000 | tf_op jit(solution)/shard_map/out_partial/pallas_call | solution.py:861
  134.4 2.3 collective-permute-start.36
  137.4 5.9 %gate_backward.1 = (bf16[1024,768]{1,0:T(8,128)(2,1)S(1)}, bf16[1024,768]{1,0:T(8,128)(2,1)S(1)}, f32[8,768]{1,0:T(8,128)S(1)}) custom-call(f32[1024,768]{1,0:T(8,128)} %copy-done.3, f32[1024,768]{1,0:T(8,128)} %copy-done.6, f32[1024,768]{1,0:T(8,128)} %get-tuple-element.381.mixed_ref, f32[8,1024]{1,0:T(8,128)S(1)} %add_add_fusion.1.square_ref, ...), custom_call_target="tpu_custom_call" | custom-call | flops 100000000 | bytes 200000 | tf_op jit(solution)/shard_map/gate_backward/pallas_call | solution.py:793
  143.3 5.2 %weight_grad.5 = (bf16[192,768]{1,0:T(8,128)(2,1)}, bf16[192,768]{1,0:T(8,128)(2,1)}, bf16[576,768]{1,0:T(8,128)(2,1)}, bf16[576,768]{1,0:T(8,128)(2,1)}) custom-call(s32[8]{0:T(128)S(1)} %stack.88.idx_ref, bf16[1536,1024]{1,0:T(8,128)(2,1)S(1)} %copy-done.1, bf16[1024,768]{1,0:T(8,128)(2,1)S(1)} %get-tuple-element.417.rhs_ref.gg_ref), custom_call_target="tpu_custom_call" | custom-call | flops 100000000 | bytes 200000 | tf_op jit(solution)/shard_map/weight_grad/pallas_call | solution.py:831
  148.5 1.2 collective-permute-done.31
  151.5 3.8 %collective-permute-start.41 = (bf16[192,768]{1,0:T(8,128)(2,1)S(1)}, bf16[192,768]{1,0:T(8,128)(2,1)S(1)}, u32[]{:S(2)}, u32[]{:S(2)}) collective-permute-start(bf16[192,768]{1,0:T(8,128)(2,1)S(1)} %get-tuple-element.438), channel_id=1, source_target_pairs={{8,0},{12,4},{16,8},{20,12},{24,16},{28,20},{0,24},{4,28},{9,1},{1... | collective-permute-start | bytes 884744 | tf_op jit(solution)/shard_map/ppermute | solution.py:1095
  155.3 1.2 collective-permute-start.43
  157.2 19.4 %ssd_backward.1 = (bf16[1024,768]{1,0:T(8,128)(2,1)S(1)}, bf16[1024,256]{1,0:T(8,128)(2,1)S(1)}, bf16[128,1024]{1,0:T(8,128)(2,1)}, bf16[128,1024]{1,0:T(8,128)(...) custom-call(s32[1]{0:T(128)} %bitcast.rank_ref, ...), custom_call_target="tpu_custom_call" | custom-call | flops 28000000000 | bytes 40000000 | tf_op jit(solution)/shard_map/ssd_backward/pallas_call | solution.py:332
  176.7 1.9 collective-permute-done.42
  178.9 5.1 %weight_grad.6 = (bf16[192,768]{1,0:T(8,128)(2,1)}, bf16[192,768]{1,0:T(8,128)(2,1)}, bf16[576,768]{1,0:T(8,128)(2,1)}, bf16[576,768]{1,0:T(8,128)(2,1)}) custom-call(s32[8]{0:T(128)S(1)} %stack.88.idx_ref, bf16[1536,1024]{1,0:T(8,128)(2,1)S(1)} %copy-done.1, bf16[1024,768]{1,0:T(8,128)(2,1)S(1)} %get-tuple-element.491.rhs_ref.gx_ref), custom_call_target="tpu_custom_call" | custom-call | flops 20000000000 | bytes 40000000 | tf_op jit(solution)/shard_map/weight_grad/pallas_call | solution.py:831
  186.1 1.2 collective-permute-start.51
  188.1 5.8 %normed_term.2 = (bf16[256,1536]{1,0:T(8,128)(2,1)S(1)}, bf16[256,1536]{1,0:T(8,128)(2,1)S(1)}, f32[24,128]{1,0:T(8,128)S(1)}) custom-call(s32[1]{0:T(128)} %bitcast.rank_ref, bf16[1024,768]{1,0:T(8,128)(2,1)S(1)} %get-tuple-element.491.rhs_ref.gx_ref, bf16[1536,768]{1,0:T(8,128)(2,1)} %get-tuple-element.473.wx_ref, ...), custom_call_target="tpu_custom_call" | custom-call | flops 5000000000 | bytes 10000000 | tf_op jit(solution)/shard_map/normed_term/pallas_call | solution.py:901
  194.1 2.7 weight_grad.7
  196.8 5.8 %normed_term.3 = (bf16[256,1536]{1,0:T(8,128)(2,1)S(1)}, bf16[256,1536]{1,0:T(8,128)(2,1)S(1)}, f32[24,128]{1,0:T(8,128)S(1)}) custom-call(s32[1]{0:T(128)} %bitcast.rank_ref, bf16[1024,768]{1,0:T(8,128)(2,1)S(1)} %get-tuple-element.491.rhs_ref.gx_ref, bf16[1536,768]{1,0:T(8,128)(2,1)} %get-tuple-element.473.wx_ref, ...), custom_call_target="tpu_custom_call" | custom-call | flops 5000000000 | bytes 10000000 | tf_op jit(solution)/shard_map/normed_term/pallas_call | solution.py:901
  202.6 5.9 %collective-permute-done.49 = bf16[576,768]{1,0:T(8,128)(2,1)S(1)} collective-permute-done((bf16[576,768]{1,0:T(8,128)(2,1)S(1)}, bf16[576,768]{1,0:T(8,128)(2,1)S(1)}, u32[]{:S(2)}, u32[]{:S(2)}) %collective-permute-start.49) | collective-permute-done | bytes 884768 | tf_op jit(solution)/shard_map/ppermute | solution.py:1104
  209.1 1.8 collective-permute-done.50
  210.8 1.2 collective-permute-start.53
  212.8 1.5 collective-permute-start.55
  214.3 2.6 collective-permute-start.54
  217.1 14.9 %collective-permute-done.55 = bf16[880,128]{1,0:T(8,128)(2,1)S(1)} collective-permute-done((bf16[880,128]{1,0:T(8,128)(2,1)S(1)}, bf16[880,128]{1,0:T(8,128)(2,1)S(1)}, u32[]{:S(2)}, u32[]{:S(2)}) %collective-permute-start.55) | collective-permute-done | bytes 225312 | tf_op jit(solution)/shard_map/ppermute | solution.py:1104
  232.1 2.2 norm_backward.1.refs_0_
  234.5 2.7 collective-permute-start.62
  237.8 1.3 collective-permute-start.61
  242.0 2.5 add_convert_fusion
  245.4 4.5 %collective-permute-done.61.refs_9_.refs_2_ = bf16[208,896]{1,0:T(8,128)(2,1)S(1)} collective-permute-done((bf16[208,896]{1,0:T(8,128)(2,1)S(1)}, bf16[208,896]{1,0:T(8,128)(2,1)S(1)}, u32[]{:S(2)}, u32[]{:S(2)}) %collective-permute-start.61) | collective-permute-done | bytes 372768 | tf_op jit(solution)/shard_map/ppermute | solution.py:1095
  249.8 5.9 %collective-permute-done.60.refs_8_.refs_1_ = bf16[208,896]{1,0:T(8,128)(2,1)S(1)} collective-permute-done((bf16[208,896]{1,0:T(8,128)(2,1)S(1)}, bf16[208,896]{1,0:T(8,128)(2,1)S(1)}, u32[]{:S(2)}, u32[]{:S(2)}) %collective-permute-start.60) | collective-permute-done | bytes 372768 | tf_op jit(solution)/shard_map/ppermute | solution.py:1095
  258.5 4.1 %update_in.1 = (f32[192,2,768]{2,1,0:T(2,128)}, f32[192,2,768]{2,1,0:T(2,128)}) custom-call(f32[192,2,768]{2,1,0:T(2,128)} %w_ref.2, f32[192,2,768]{2,1,0:T(2,128)} %m_ref.2, bf16[192,768]{1,0:T(8,128)(2,1)S(1)} %copy-done.11, bf16[192,1536]{1,0:T(8,128)(2,1)S(1)} %collective-permute-done.56.refs_1_, bf16[192,768]{1,0:T(8,128)(2,1)S(1)} %collective-permute-done.51.refs_2_, ...), custom_call_target="tpu_custom_call" | custom-call | flops 100000000 | bytes 200000 | tf_op jit(solution)/shard_map/update_in/pallas_call | solution.py:990
  266.4 1.9 join_rows.1
  (302 shorter events, 38.0 us)
Async XLA Ops:
  3.6 21.5 %collective-permute-start.3 = (bf16[192,896]{1,0:T(8,128)(2,1)S(1)}, bf16[192,896]{1,0:T(8,128)(2,1)}, u32[]{:S(2)}, u32[]{:S(2)}) collective-permute-start(bf16[192,896]{1,0:T(8,128)(2,1)S(1)} %pack.1.refs_0_), channel_id=1, source_target_pairs={{24,0},{28,4},{0,8},{4,12},{8,16},{12,20},{16,24},{20,28},{25,1},{... | collective-permute-start | bytes 1032200 | tf_op jit(solution)/shard_map/ppermute | solution.py:1095
  6.7 20.2 %collective-permute-start.1 = (bf16[192,896]{1,0:T(8,128)(2,1)S(1)}, bf16[192,896]{1,0:T(8,128)(2,1)}, u32[]{:S(2)}, u32[]{:S(2)}) collective-permute-start(bf16[192,896]{1,0:T(8,128)(2,1)S(1)} %pack.1.refs_0_), channel_id=1, source_target_pairs={{8,0},{12,4},{16,8},{20,12},{24,16},{28,20},{0,24},{4,28},{9,1},{1... | collective-permute-start | bytes 1032200 | tf_op jit(solution)/shard_map/ppermute | solution.py:1095
  8.7 9.5 %collective-permute-start = (bf16[192,896]{1,0:T(8,128)(2,1)S(1)}, bf16[192,896]{1,0:T(8,128)(2,1)S(1)}, u32[]{:S(2)}, u32[]{:S(2)}) collective-permute-start(bf16[192,896]{1,0:T(8,128)(2,1)S(1)} %pack.1.refs_0_), channel_id=1, source_target_pairs={{4,0},{0,4},{12,8},{8,12},{20,16},{16,20},{28,24},{24,28},{5,1},{1... | collective-permute-start | bytes 1032200 | tf_op jit(solution)/shard_map/ppermute | solution.py:1104
  10.4 30.5 %collective-permute-start.6 = (bf16[1024,384]{1,0:T(8,128)(2,1)}, bf16[1024,384]{1,0:T(8,128)(2,1)}, u32[]{:S(2)}, u32[]{:S(2)}) collective-permute-start(bf16[1024,384]{1,0:T(8,128)(2,1)} %refs_0_.1), channel_id=1, source_target_pairs={{2,0},{3,1},{0,2},{1,3},{6,4},{7,5},{4,6},{5,7},{10,8},{11,9},{8,1... | collective-permute-start | bytes 2359304 | tf_op jit(solution)/shard_map/ppermute | solution.py:1108
  11.9 34.5 %collective-permute-start.11 = (bf16[1024,384]{1,0:T(8,128)(2,1)}, bf16[1024,384]{1,0:T(8,128)(2,1)}, u32[]{:S(2)}, u32[]{:S(2)}) collective-permute-start(bf16[1024,384]{1,0:T(8,128)(2,1)} %refs_0_.1), channel_id=1, source_target_pairs={{1,0},{0,1},{3,2},{2,3},{5,4},{4,5},{7,6},{6,7},{9,8},{8,9},{11,10... | collective-permute-start | bytes 2359304 | tf_op jit(solution)/shard_map/ppermute | solution.py:1108
  19.2 21.7 %collective-permute-start.2 = (bf16[192,896]{1,0:T(8,128)(2,1)S(1)}, bf16[192,896]{1,0:T(8,128)(2,1)}, u32[]{:S(2)}, u32[]{:S(2)}) collective-permute-start(bf16[192,896]{1,0:T(8,128)(2,1)S(1)} %pack.1.refs_0_), channel_id=1, source_target_pairs={{16,0},{20,4},{24,8},{28,12},{0,16},{4,20},{8,24},{12,28},{17,1},{... | collective-permute-start | bytes 1032200 | tf_op jit(solution)/shard_map/ppermute | solution.py:1095
  25.1 11.2 %collective-permute-start.5 = (bf16[192,896]{1,0:T(8,128)(2,1)}, bf16[192,896]{1,0:T(8,128)(2,1)S(1)}, u32[]{:S(2)}, u32[]{:S(2)}) collective-permute-start(bf16[192,896]{1,0:T(8,128)(2,1)} %collective-permute-done.3.refs_3_), channel_id=1, source_target_pairs={{4,0},{0,4},{12,8},{8,12},{20,16},{16,20},{28,24},{24,28},{5,1},{1... | collective-permute-start | bytes 1032200 | tf_op jit(solution)/shard_map/ppermute | solution.py:1104
  26.9 14.0 %collective-permute-start.4 = (bf16[192,896]{1,0:T(8,128)(2,1)}, bf16[192,896]{1,0:T(8,128)(2,1)S(1)}, u32[]{:S(2)}, u32[]{:S(2)}) collective-permute-start(bf16[192,896]{1,0:T(8,128)(2,1)} %collective-permute-done.1.refs_2_), channel_id=1, source_target_pairs={{4,0},{0,4},{12,8},{8,12},{20,16},{16,20},{28,24},{24,28},{5,1},{1... | collective-permute-start | bytes 1032200 | tf_op jit(solution)/shard_map/ppermute | solution.py:1104
  40.9 6.1 %collective-permute-start.12 = (bf16[1024,384]{1,0:T(8,128)(2,1)}, bf16[1024,384]{1,0:T(8,128)(2,1)S(1)}, u32[]{:S(2)}, u32[]{:S(2)}) collective-permute-start(bf16[1024,384]{1,0:T(8,128)(2,1)} %collective-permute-done.6.refs_2_), channel_id=1, source_target_pairs={{1,0},{0,1},{3,2},{2,3},{5,4},{4,5},{7,6},{6,7},{9,8},{8,9},{11,10... | collective-permute-start | bytes 2359304 | tf_op jit(solution)/shard_map/ppermute | solution.py:1108
  41.1 10.1 %collective-permute-start.9 = (bf16[192,768]{1,0:T(8,128)(2,1)}, bf16[192,768]{1,0:T(8,128)(2,1)S(1)}, u32[]{:S(2)}, u32[]{:S(2)}) collective-permute-start(bf16[192,768]{1,0:T(8,128)(2,1)} %pack_gate.1.refs_0_), channel_id=1, source_target_pairs={{4,0},{0,4},{12,8},{8,12},{20,16},{16,20},{28,24},{24,28},{5,1},{1... | collective-permute-start | bytes 884744 | tf_op jit(solution)/shard_map/ppermute | solution.py:1104
  42.6 11.9 %collective-permute-start.8 = (bf16[192,768]{1,0:T(8,128)(2,1)}, bf16[192,768]{1,0:T(8,128)(2,1)S(1)}, u32[]{:S(2)}, u32[]{:S(2)}) collective-permute-start(bf16[192,768]{1,0:T(8,128)(2,1)} %pack_gate.1.refs_0_), channel_id=1, source_target_pairs={{24,0},{28,4},{0,8},{4,12},{8,16},{12,20},{16,24},{20,28},{25,1},{... | collective-permute-start | bytes 884744 | tf_op jit(solution)/shard_map/ppermute | solution.py:1095
  44.2 15.3 %collective-permute-start.7 = (bf16[192,768]{1,0:T(8,128)(2,1)}, bf16[192,768]{1,0:T(8,128)(2,1)S(1)}, u32[]{:S(2)}, u32[]{:S(2)}) collective-permute-start(bf16[192,768]{1,0:T(8,128)(2,1)} %pack_gate.1.refs_0_), channel_id=1, source_target_pairs={{8,0},{12,4},{16,8},{20,12},{24,16},{28,20},{0,24},{4,28},{9,1},{1... | collective-permute-start | bytes 884744 | tf_op jit(solution)/shard_map/ppermute | solution.py:1095
  46.5 13.1 %collective-permute-start.10 = (bf16[192,896]{1,0:T(8,128)(2,1)}, bf16[192,896]{1,0:T(8,128)(2,1)S(1)}, u32[]{:S(2)}, u32[]{:S(2)}) collective-permute-start(bf16[192,896]{1,0:T(8,128)(2,1)} %collective-permute-done.2.refs_4_), channel_id=1, source_target_pairs={{4,0},{0,4},{12,8},{8,12},{20,16},{16,20},{28,24},{24,28},{5,1},{1... | collective-permute-start | bytes 1032200 | tf_op jit(solution)/shard_map/ppermute | solution.py:1104
  59.5 16.6 %collective-permute-start.16 = (bf16[192,768]{1,0:T(8,128)(2,1)S(1)}, bf16[192,768]{1,0:T(8,128)(2,1)S(1)}, u32[]{:S(2)}, u32[]{:S(2)}) collective-permute-start(bf16[192,768]{1,0:T(8,128)(2,1)S(1)} %copy-done.14), channel_id=1, source_target_pairs={{4,0},{0,4},{12,8},{8,12},{20,16},{16,20},{28,24},{24,28},{5,1},{1... | collective-permute-start | bytes 884744 | tf_op jit(solution)/shard_map/ppermute | solution.py:1104
  60.1 16.1 %collective-permute-start.15 = (bf16[192,768]{1,0:T(8,128)(2,1)S(1)}, bf16[192,768]{1,0:T(8,128)(2,1)S(1)}, u32[]{:S(2)}, u32[]{:S(2)}) collective-permute-start(bf16[192,768]{1,0:T(8,128)(2,1)S(1)} %collective-permute-done.7.refs_2_), channel_id=1, source_target_pairs={{4,0},{0,4},{12,8},{8,12},{20,16},{16,20},{28,24},{24,28},{5,1},{1... | collective-permute-start | bytes 884744 | tf_op jit(solution)/shard_map/ppermute | solution.py:1104
  61.6 15.1 %collective-permute-start.14 = (bf16[192,768]{1,0:T(8,128)(2,1)S(1)}, bf16[192,768]{1,0:T(8,128)(2,1)S(1)}, u32[]{:S(2)}, u32[]{:S(2)}) collective-permute-start(bf16[192,768]{1,0:T(8,128)(2,1)S(1)} %copy-done.12), channel_id=1, source_target_pairs={{16,0},{20,4},{24,8},{28,12},{0,16},{4,20},{8,24},{12,28},{17,1},{... | collective-permute-start | bytes 884744 | tf_op jit(solution)/shard_map/ppermute | solution.py:1095
  66.3 7.5 %collective-permute-start.13 = (bf16[64,1024]{1,0:T(8,128)(2,1)S(1)}, bf16[64,1024]{1,0:T(8,128)(2,1)S(1)}, u32[]{:S(2)}, u32[]{:S(2)}) collective-permute-start(bf16[64,1024]{1,0:T(8,128)(2,1)S(1)} %get-tuple-element.324.refs_0_), channel_id=1, source_target_pairs={{2,0},{3,1},{0,2},{1,3},{6,4},{7,5},{4,6},{5,7},{10,8},{11,9},{8,1... | collective-permute-start | bytes 393224 | tf_op jit(solution)/shard_map/ppermute | solution.py:1108
  67.8 6.4 %collective-permute-start.17 = (bf16[64,1024]{1,0:T(8,128)(2,1)S(1)}, bf16[64,1024]{1,0:T(8,128)(2,1)S(1)}, u32[]{:S(2)}, u32[]{:S(2)}) collective-permute-start(bf16[64,1024]{1,0:T(8,128)(2,1)S(1)} %get-tuple-element.324.refs_0_), channel_id=1, source_target_pairs={{1,0},{0,1},{3,2},{2,3},{5,4},{4,5},{7,6},{6,7},{9,8},{8,9},{11,10... | collective-permute-start | bytes 393224 | tf_op jit(solution)/shard_map/ppermute | solution.py:1108
  76.6 20.1 %collective-permute-start.22 = (bf16[192,768]{1,0:T(8,128)(2,1)S(1)}, bf16[192,768]{1,0:T(8,128)(2,1)S(1)}, u32[]{:S(2)}, u32[]{:S(2)}) collective-permute-start(bf16[192,768]{1,0:T(8,128)(2,1)S(1)} %copy-done.14), channel_id=1, source_target_pairs={{24,0},{28,4},{0,8},{4,12},{8,16},{12,20},{16,24},{20,28},{25,1},{... | collective-permute-start | bytes 884744 | tf_op jit(solution)/shard_map/ppermute | solution.py:1095
  77.6 19.2 %collective-permute-start.21 = (bf16[192,768]{1,0:T(8,128)(2,1)S(1)}, bf16[192,768]{1,0:T(8,128)(2,1)S(1)}, u32[]{:S(2)}, u32[]{:S(2)}) collective-permute-start(bf16[192,768]{1,0:T(8,128)(2,1)S(1)} %copy-done.14), channel_id=1, source_target_pairs={{8,0},{12,4},{16,8},{20,12},{24,16},{28,20},{0,24},{4,28},{9,1},{1... | collective-permute-start | bytes 884744 | tf_op jit(solution)/shard_map/ppermute | solution.py:1095
  80.5 16.3 %collective-permute-start.19 = (bf16[192,768]{1,0:T(8,128)(2,1)S(1)}, bf16[192,768]{1,0:T(8,128)(2,1)S(1)}, u32[]{:S(2)}, u32[]{:S(2)}) collective-permute-start(bf16[192,768]{1,0:T(8,128)(2,1)S(1)} %collective-permute-done.14.refs_4_), channel_id=1, source_target_pairs={{4,0},{0,4},{12,8},{8,12},{20,16},{16,20},{28,24},{24,28},{5,1},{1... | collective-permute-start | bytes 884744 | tf_op jit(solution)/shard_map/ppermute | solution.py:1104
  81.3 15.4 %collective-permute-start.20 = (bf16[192,768]{1,0:T(8,128)(2,1)S(1)}, bf16[192,768]{1,0:T(8,128)(2,1)S(1)}, u32[]{:S(2)}, u32[]{:S(2)}) collective-permute-start(bf16[192,768]{1,0:T(8,128)(2,1)S(1)} %collective-permute-done.8.refs_3_), channel_id=1, source_target_pairs={{4,0},{0,4},{12,8},{8,12},{20,16},{16,20},{28,24},{24,28},{5,1},{1... | collective-permute-start | bytes 884744 | tf_op jit(solution)/shard_map/ppermute | solution.py:1104
  96.8 13.4 %collective-permute-start.27 = (bf16[192,768]{1,0:T(8,128)(2,1)S(1)}, bf16[192,768]{1,0:T(8,128)(2,1)S(1)}, u32[]{:S(2)}, u32[]{:S(2)}) collective-permute-start(bf16[192,768]{1,0:T(8,128)(2,1)S(1)} %collective-permute-done.21.refs_2_), channel_id=1, source_target_pairs={{4,0},{0,4},{12,8},{8,12},{20,16},{16,20},{28,24},{24,28},{5,1},{1... | collective-permute-start | bytes 884744 | tf_op jit(solution)/shard_map/ppermute | solution.py:1104
  97.7 13.4 %collective-permute-start.26 = (bf16[192,768]{1,0:T(8,128)(2,1)S(1)}, bf16[192,768]{1,0:T(8,128)(2,1)S(1)}, u32[]{:S(2)}, u32[]{:S(2)}) collective-permute-start(bf16[192,768]{1,0:T(8,128)(2,1)S(1)} %copy-done.14), channel_id=1, source_target_pairs={{16,0},{20,4},{24,8},{28,12},{0,16},{4,20},{8,24},{12,28},{17,1},{... | collective-permute-start | bytes 884744 | tf_op jit(solution)/shard_map/ppermute | solution.py:1095
  97.7 13.4 %collective-permute-start.28 = (bf16[192,768]{1,0:T(8,128)(2,1)S(1)}, bf16[192,768]{1,0:T(8,128)(2,1)S(1)}, u32[]{:S(2)}, u32[]{:S(2)}) collective-permute-start(bf16[192,768]{1,0:T(8,128)(2,1)S(1)} %collective-permute-done.22.refs_3_), channel_id=1, source_target_pairs={{4,0},{0,4},{12,8},{8,12},{20,16},{16,20},{28,24},{24,28},{5,1},{1... | collective-permute-start | bytes 884744 | tf_op jit(solution)/shard_map/ppermute | solution.py:1104
  105.3 3.6 %collective-permute-start.25 = (f32[8,1024]{1,0:T(8,128)S(1)}, f32[8,1024]{1,0:T(8,128)S(1)}, u32[]{:S(2)}, u32[]{:S(2)}) collective-permute-start(f32[8,1024]{1,0:T(8,128)S(1)} %get-tuple-element.368), channel_id=1, source_target_pairs={{3,0},{2,1},{1,2},{0,3},{7,4},{6,5},{5,6},{4,7},{11,8},{10,9},{9,1... | collective-permute-start | bytes 98312 | tf_op jit(solution)/shard_map/ppermute | solution.py:1108
  105.4 4.0 %collective-permute-start.24 = (f32[8,1024]{1,0:T(8,128)S(1)}, f32[8,1024]{1,0:T(8,128)S(1)}, u32[]{:S(2)}, u32[]{:S(2)}) collective-permute-start(f32[8,1024]{1,0:T(8,128)S(1)} %get-tuple-element.368), channel_id=1, source_target_pairs={{2,0},{3,1},{0,2},{1,3},{6,4},{7,5},{4,6},{5,7},{10,8},{11,9},{8,1... | collective-permute-start | bytes 98312 | tf_op jit(solution)/shard_map/ppermute | solution.py:1108
  111.0 8.9 %collective-permute-start.29 = (bf16[192,768]{1,0:T(8,128)(2,1)S(1)}, bf16[192,768]{1,0:T(8,128)(2,1)S(1)}, u32[]{:S(2)}, u32[]{:S(2)}) collective-permute-start(bf16[192,768]{1,0:T(8,128)(2,1)S(1)} %collective-permute-done.26.refs_4_), channel_id=1, source_target_pairs={{4,0},{0,4},{12,8},{8,12},{20,16},{16,20},{28,24},{24,28},{5,1},{1... | collective-permute-start | bytes 884744 | tf_op jit(solution)/shard_map/ppermute | solution.py:1104
  112.5 6.9 %collective-permute-start.30 = (bf16[64,1536]{1,0:T(8,128)(2,1)}, bf16[64,1536]{1,0:T(8,128)(2,1)}, u32[]{:S(2)}, u32[]{:S(2)}) collective-permute-start(bf16[64,1536]{1,0:T(8,128)(2,1)} %get-tuple-element.479.refs_2_), channel_id=1, source_target_pairs={{2,0},{3,1},{0,2},{1,3},{6,4},{7,5},{4,6},{5,7},{10,8},{11,9},{8,1... | collective-permute-start | bytes 589832 | tf_op jit(solution)/shard_map/ppermute | solution.py:1108
  120.0 13.7 %collective-permute-start.35 = (bf16[192,768]{1,0:T(8,128)(2,1)}, bf16[192,768]{1,0:T(8,128)(2,1)S(1)}, u32[]{:S(2)}, u32[]{:S(2)}) collective-permute-start(bf16[192,768]{1,0:T(8,128)(2,1)} %get-tuple-element.408), channel_id=1, source_target_pairs={{4,0},{0,4},{12,8},{8,12},{20,16},{16,20},{28,24},{24,28},{5,1},{1... | collective-permute-start | bytes 884744 | tf_op jit(solution)/shard_map/ppermute | solution.py:1104
  125.6 8.0 %collective-permute-start.34 = (f32[8,1024]{1,0:T(8,128)S(1)}, f32[8,1024]{1,0:T(8,128)S(1)}, u32[]{:S(2)}, u32[]{:S(2)}) collective-permute-start(f32[8,1024]{1,0:T(8,128)S(1)} %get-tuple-element.398), channel_id=1, source_target_pairs={{3,0},{2,1},{1,2},{0,3},{7,4},{6,5},{5,6},{4,7},{11,8},{10,9},{9,1... | collective-permute-start | bytes 98312 | tf_op jit(solution)/shard_map/ppermute | solution.py:1108
  125.6 7.9 %collective-permute-start.33 = (f32[8,1024]{1,0:T(8,128)S(1)}, f32[8,1024]{1,0:T(8,128)S(1)}, u32[]{:S(2)}, u32[]{:S(2)}) collective-permute-start(f32[8,1024]{1,0:T(8,128)S(1)} %get-tuple-element.398), channel_id=1, source_target_pairs={{2,0},{3,1},{0,2},{1,3},{6,4},{7,5},{4,6},{5,7},{10,8},{11,9},{8,1... | collective-permute-start | bytes 98312 | tf_op jit(solution)/shard_map/ppermute | solution.py:1108
  126.2 7.4 %collective-permute-start.32 = (f32[8,1024]{1,0:T(8,128)S(1)}, f32[8,1024]{1,0:T(8,128)S(1)}, u32[]{:S(2)}, u32[]{:S(2)}) collective-permute-start(f32[8,1024]{1,0:T(8,128)S(1)} %get-tuple-element.398), channel_id=1, source_target_pairs={{1,0},{0,1},{3,2},{2,3},{5,4},{4,5},{7,6},{6,7},{9,8},{8,9},{11,10... | collective-permute-start | bytes 98312 | tf_op jit(solution)/shard_map/ppermute | solution.py:1108
  133.6 16.7 %collective-permute-start.39 = (bf16[1024,384]{1,0:T(8,128)(2,1)}, bf16[1024,384]{1,0:T(8,128)(2,1)S(1)}, u32[]{:S(2)}, u32[]{:S(2)}) collective-permute-start(bf16[1024,384]{1,0:T(8,128)(2,1)} %get-tuple-element.412), channel_id=1, source_target_pairs={{1,0},{0,1},{3,2},{2,3},{5,4},{4,5},{7,6},{6,7},{9,8},{8,9},{11,10... | collective-permute-start | bytes 2359304 | tf_op jit(solution)/shard_map/ppermute | solution.py:1108
  133.7 16.0 %collective-permute-start.31 = (bf16[384,768]{1,0:T(8,128)(2,1)}, bf16[384,768]{1,0:T(8,128)(2,1)S(1)}, u32[]{:S(2)}, u32[]{:S(2)}) collective-permute-start(bf16[384,768]{1,0:T(8,128)(2,1)} %get-tuple-element.389), channel_id=1, source_target_pairs={{4,0},{0,4},{12,8},{8,12},{20,16},{16,20},{28,24},{24,28},{5,1},{1... | collective-permute-start | bytes 1769480 | tf_op jit(solution)/shard_map/ppermute | solution.py:1104
  134.4 15.9 %collective-permute-start.36 = (bf16[192,768]{1,0:T(8,128)(2,1)S(1)}, bf16[192,768]{1,0:T(8,128)(2,1)S(1)}, u32[]{:S(2)}, u32[]{:S(2)}) collective-permute-start(bf16[192,768]{1,0:T(8,128)(2,1)S(1)} %add_convert_fusion.11), channel_id=1, source_target_pairs={{16,0},{20,4},{24,8},{28,12},{0,16},{4,20},{8,24},{12,28},{17,1},{... | collective-permute-start | bytes 884744 | tf_op jit(solution)/shard_map/ppermute | solution.py:1095
  136.7 11.8 %collective-permute-start.37 = (bf16[64,1536]{1,0:T(8,128)(2,1)}, bf16[64,1536]{1,0:T(8,128)(2,1)S(1)}, u32[]{:S(2)}, u32[]{:S(2)}) collective-permute-start(bf16[64,1536]{1,0:T(8,128)(2,1)} %get-tuple-element.479.refs_2_), channel_id=1, source_target_pairs={{1,0},{0,1},{3,2},{2,3},{5,4},{4,5},{7,6},{6,7},{9,8},{8,9},{11,10... | collective-permute-start | bytes 589832 | tf_op jit(solution)/shard_map/ppermute | solution.py:1108
  136.7 11.8 %collective-permute-start.38 = (bf16[64,1536]{1,0:T(8,128)(2,1)}, bf16[64,1536]{1,0:T(8,128)(2,1)S(1)}, u32[]{:S(2)}, u32[]{:S(2)}) collective-permute-start(bf16[64,1536]{1,0:T(8,128)(2,1)} %collective-permute-done.30.refs_4_), channel_id=1, source_target_pairs={{1,0},{0,1},{3,2},{2,3},{5,4},{4,5},{7,6},{6,7},{9,8},{8,9},{11,10... | collective-permute-start | bytes 589832 | tf_op jit(solution)/shard_map/ppermute | solution.py:1108
  151.4 25.2 %collective-permute-start.40 = (bf16[192,768]{1,0:T(8,128)(2,1)S(1)}, bf16[192,768]{1,0:T(8,128)(2,1)S(1)}, u32[]{:S(2)}, u32[]{:S(2)}) collective-permute-start(bf16[192,768]{1,0:T(8,128)(2,1)S(1)} %get-tuple-element.437), channel_id=1, source_target_pairs={{24,0},{28,4},{0,8},{4,12},{8,16},{12,20},{16,24},{20,28},{25,1},{... | collective-permute-start | bytes 884744 | tf_op jit(solution)/shard_map/ppermute | solution.py:1095
  151.5 25.2 %collective-permute-start.41 = (bf16[192,768]{1,0:T(8,128)(2,1)S(1)}, bf16[192,768]{1,0:T(8,128)(2,1)S(1)}, u32[]{:S(2)}, u32[]{:S(2)}) collective-permute-start(bf16[192,768]{1,0:T(8,128)(2,1)S(1)} %get-tuple-element.438), channel_id=1, source_target_pairs={{8,0},{12,4},{16,8},{20,12},{24,16},{28,20},{0,24},{4,28},{9,1},{1... | collective-permute-start | bytes 884744 | tf_op jit(solution)/shard_map/ppermute | solution.py:1095
  155.3 21.4 %collective-permute-start.43 = (bf16[1024,384]{1,0:T(8,128)(2,1)S(1)}, bf16[1024,384]{1,0:T(8,128)(2,1)S(1)}, u32[]{:S(2)}, u32[]{:S(2)}) collective-permute-start(bf16[1024,384]{1,0:T(8,128)(2,1)S(1)} %add_convert_fusion.2), channel_id=1, source_target_pairs={{2,0},{3,1},{0,2},{1,3},{6,4},{7,5},{4,6},{5,7},{10,8},{11,9},{8,1... | collective-permute-start | bytes 2359304 | tf_op jit(solution)/shard_map/ppermute | solution.py:1108
  156.5 27.6 %collective-permute-start.45 = (bf16[1024,384]{1,0:T(8,128)(2,1)S(1)}, bf16[1024,384]{1,0:T(8,128)(2,1)S(1)}, u32[]{:S(2)}, u32[]{:S(2)}) collective-permute-start(bf16[1024,384]{1,0:T(8,128)(2,1)S(1)} %copy-done.59), channel_id=1, source_target_pairs={{1,0},{0,1},{3,2},{2,3},{5,4},{4,5},{7,6},{6,7},{9,8},{8,9},{11,10... | collective-permute-start | bytes 2359304 | tf_op jit(solution)/shard_map/ppermute | solution.py:1108
  156.5 22.1 %collective-permute-start.42 = (bf16[576,768]{1,0:T(8,128)(2,1)S(1)}, bf16[576,768]{1,0:T(8,128)(2,1)S(1)}, u32[]{:S(2)}, u32[]{:S(2)}) collective-permute-start(bf16[576,768]{1,0:T(8,128)(2,1)S(1)} %copy-done.58), channel_id=1, source_target_pairs={{4,0},{0,4},{12,8},{8,12},{20,16},{16,20},{28,24},{24,28},{5,1},{1... | collective-permute-start | bytes 2654216 | tf_op jit(solution)/shard_map/ppermute | solution.py:1104
  178.7 5.4 %collective-permute-start.44 = (bf16[128,1024]{1,0:T(8,128)(2,1)}, bf16[128,1024]{1,0:T(8,128)(2,1)S(1)}, u32[]{:S(2)}, u32[]{:S(2)}) collective-permute-start(bf16[128,1024]{1,0:T(8,128)(2,1)} %get-tuple-element.468), channel_id=1, source_target_pairs={{1,0},{0,1},{3,2},{2,3},{5,4},{4,5},{7,6},{6,7},{9,8},{8,9},{11,10... | collective-permute-start | bytes 786440 | tf_op jit(solution)/shard_map/ppermute | solution.py:1108
  178.9 15.0 %collective-permute-start.47 = (bf16[192,768]{1,0:T(8,128)(2,1)S(1)}, bf16[192,768]{1,0:T(8,128)(2,1)S(1)}, u32[]{:S(2)}, u32[]{:S(2)}) collective-permute-start(bf16[192,768]{1,0:T(8,128)(2,1)S(1)} %add_convert_fusion.8), channel_id=1, source_target_pairs={{16,0},{20,4},{24,8},{28,12},{0,16},{4,20},{8,24},{12,28},{17,1},{... | collective-permute-start | bytes 884744 | tf_op jit(solution)/shard_map/ppermute | solution.py:1095
  184.2 9.7 %collective-permute-start.46 = (bf16[64,1024]{1,0:T(8,128)(2,1)S(1)}, bf16[64,1024]{1,0:T(8,128)(2,1)S(1)}, u32[]{:S(2)}, u32[]{:S(2)}) collective-permute-start(bf16[64,1024]{1,0:T(8,128)(2,1)S(1)} %slice.308), channel_id=1, source_target_pairs={{2,0},{3,1},{0,2},{1,3},{6,4},{7,5},{4,6},{5,7},{10,8},{11,9},{8,1... | collective-permute-start | bytes 393224 | tf_op jit(solution)/shard_map/ppermute | solution.py:1108
  185.2 23.8 %collective-permute-start.52 = (bf16[192,768]{1,0:T(8,128)(2,1)S(1)}, bf16[192,768]{1,0:T(8,128)(2,1)S(1)}, u32[]{:S(2)}, u32[]{:S(2)}) collective-permute-start(bf16[192,768]{1,0:T(8,128)(2,1)S(1)} %get-tuple-element.578), channel_id=1, source_target_pairs={{8,0},{12,4},{16,8},{20,12},{24,16},{28,20},{0,24},{4,28},{9,1},{1... | collective-permute-start | bytes 884744 | tf_op jit(solution)/shard_map/ppermute | solution.py:1095
  186.1 22.9 %collective-permute-start.51 = (bf16[192,768]{1,0:T(8,128)(2,1)S(1)}, bf16[192,768]{1,0:T(8,128)(2,1)S(1)}, u32[]{:S(2)}, u32[]{:S(2)}) collective-permute-start(bf16[192,768]{1,0:T(8,128)(2,1)S(1)} %get-tuple-element.579), channel_id=1, source_target_pairs={{24,0},{28,4},{0,8},{4,12},{8,16},{12,20},{16,24},{20,28},{25,1},{... | collective-permute-start | bytes 884744 | tf_op jit(solution)/shard_map/ppermute | solution.py:1095
  187.3 21.2 %collective-permute-start.49 = (bf16[576,768]{1,0:T(8,128)(2,1)S(1)}, bf16[576,768]{1,0:T(8,128)(2,1)S(1)}, u32[]{:S(2)}, u32[]{:S(2)}) collective-permute-start(bf16[576,768]{1,0:T(8,128)(2,1)S(1)} %copy-done.57), channel_id=1, source_target_pairs={{4,0},{0,4},{12,8},{8,12},{20,16},{16,20},{28,24},{24,28},{5,1},{1... | collective-permute-start | bytes 2654216 | tf_op jit(solution)/shard_map/ppermute | solution.py:1104
  193.9 14.6 %collective-permute-start.48 = (bf16[256,1536]{1,0:T(8,128)(2,1)S(1)}, bf16[256,1536]{1,0:T(8,128)(2,1)S(1)}, u32[]{:S(2)}, u32[]{:S(2)}) collective-permute-start(bf16[256,1536]{1,0:T(8,128)(2,1)S(1)} %get-tuple-element.490), channel_id=1, source_target_pairs={{1,0},{0,1},{3,2},{2,3},{5,4},{4,5},{7,6},{6,7},{9,8},{8,9},{11,10... | collective-permute-start | bytes 2359304 | tf_op jit(solution)/shard_map/ppermute | solution.py:1108
  210.8 21.3 %collective-permute-start.53 = (bf16[256,1536]{1,0:T(8,128)(2,1)S(1)}, bf16[256,1536]{1,0:T(8,128)(2,1)S(1)}, u32[]{:S(2)}, u32[]{:S(2)}) collective-permute-start(bf16[256,1536]{1,0:T(8,128)(2,1)S(1)} %add_convert_fusion.1), channel_id=1, source_target_pairs={{2,0},{3,1},{0,2},{1,3},{6,4},{7,5},{4,6},{5,7},{10,8},{11,9},{8,1... | collective-permute-start | bytes 2359304 | tf_op jit(solution)/shard_map/ppermute | solution.py:1108
  212.1 20.0 %collective-permute-start.56 = (bf16[192,1536]{1,0:T(8,128)(2,1)S(1)}, bf16[192,1536]{1,0:T(8,128)(2,1)S(1)}, u32[]{:S(2)}, u32[]{:S(2)}) collective-permute-start(bf16[192,1536]{1,0:T(8,128)(2,1)S(1)} %pad_maximum_fusion), channel_id=1, source_target_pairs={{4,0},{0,4},{12,8},{8,12},{20,16},{16,20},{28,24},{24,28},{5,1},{1... | collective-permute-start | bytes 1769480 | tf_op jit(solution)/shard_map/ppermute | solution.py:1104
  212.8 19.3 %collective-permute-start.55 = (bf16[880,128]{1,0:T(8,128)(2,1)S(1)}, bf16[880,128]{1,0:T(8,128)(2,1)S(1)}, u32[]{:S(2)}, u32[]{:S(2)}) collective-permute-start(bf16[880,128]{1,0:T(8,128)(2,1)S(1)} %pad_maximum_fusion.3), channel_id=1, source_target_pairs={{4,0},{0,4},{12,8},{8,12},{20,16},{16,20},{28,24},{24,28},{5,1},{1... | collective-permute-start | bytes 675848 | tf_op jit(solution)/shard_map/ppermute | solution.py:1104
  214.3 17.8 %collective-permute-start.54 = (bf16[192,768]{1,0:T(8,128)(2,1)S(1)}, bf16[192,768]{1,0:T(8,128)(2,1)S(1)}, u32[]{:S(2)}, u32[]{:S(2)}) collective-permute-start(bf16[192,768]{1,0:T(8,128)(2,1)S(1)} %get-tuple-element.512), channel_id=1, source_target_pairs={{16,0},{20,4},{24,8},{28,12},{0,16},{4,20},{8,24},{12,28},{17,1},{... | collective-permute-start | bytes 884744 | tf_op jit(solution)/shard_map/ppermute | solution.py:1095
  234.5 10.9 %collective-permute-start.62 = (bf16[304,128]{1,0:T(8,128)(2,1)S(1)}, bf16[304,128]{1,0:T(8,128)(2,1)S(1)}, u32[]{:S(2)}, u32[]{:S(2)}) collective-permute-start(bf16[304,128]{1,0:T(8,128)(2,1)S(1)} %pad_maximum_fusion.4), channel_id=1, source_target_pairs={{16,0},{20,4},{24,8},{28,12},{0,16},{4,20},{8,24},{12,28},{17,1},{... | collective-permute-start | bytes 233480 | tf_op jit(solution)/shard_map/ppermute | solution.py:1095
  237.2 8.2 %collective-permute-start.63 = (bf16[192,768]{1,0:T(8,128)(2,1)S(1)}, bf16[192,768]{1,0:T(8,128)(2,1)S(1)}, u32[]{:S(2)}, u32[]{:S(2)}) collective-permute-start(bf16[192,768]{1,0:T(8,128)(2,1)S(1)} %copy-done.60), channel_id=1, source_target_pairs={{4,0},{0,4},{12,8},{8,12},{20,16},{16,20},{28,24},{24,28},{5,1},{1... | collective-permute-start | bytes 884744 | tf_op jit(solution)/shard_map/ppermute | solution.py:1104
  237.8 12.0 %collective-permute-start.61 = (bf16[208,896]{1,0:T(8,128)(2,1)S(1)}, bf16[208,896]{1,0:T(8,128)(2,1)S(1)}, u32[]{:S(2)}, u32[]{:S(2)}) collective-permute-start(bf16[208,896]{1,0:T(8,128)(2,1)S(1)} %get-tuple-element.588), channel_id=1, source_target_pairs={{8,0},{12,4},{16,8},{20,12},{24,16},{28,20},{0,24},{4,28},{9,1},{1... | collective-permute-start | bytes 1118216 | tf_op jit(solution)/shard_map/ppermute | solution.py:1095
  239.1 16.6 %collective-permute-start.60 = (bf16[208,896]{1,0:T(8,128)(2,1)S(1)}, bf16[208,896]{1,0:T(8,128)(2,1)S(1)}, u32[]{:S(2)}, u32[]{:S(2)}) collective-permute-start(bf16[208,896]{1,0:T(8,128)(2,1)S(1)} %get-tuple-element.589), channel_id=1, source_target_pairs={{24,0},{28,4},{0,8},{4,12},{8,16},{12,20},{16,24},{20,28},{25,1},{... | collective-permute-start | bytes 1118216 | tf_op jit(solution)/shard_map/ppermute | solution.py:1095
  239.9 18.4 %collective-permute-start.57 = (bf16[256,1536]{1,0:T(8,128)(2,1)S(1)}, bf16[256,1536]{1,0:T(8,128)(2,1)S(1)}, u32[]{:S(2)}, u32[]{:S(2)}) collective-permute-start(bf16[256,1536]{1,0:T(8,128)(2,1)S(1)} %norm_backward.1.refs_0_), channel_id=1, source_target_pairs={{2,0},{3,1},{0,2},{1,3},{6,4},{7,5},{4,6},{5,7},{10,8},{11,9},{8,1... | collective-permute-start | bytes 2359304 | tf_op jit(solution)/shard_map/ppermute | solution.py:1108
  256.5 7.8 %collective-permute-start.66 = (f32[232,128]{1,0:T(8,128)S(1)}, f32[232,128]{1,0:T(8,128)S(1)}, u32[]{:S(2)}, u32[]{:S(2)}) collective-permute-start(f32[232,128]{1,0:T(8,128)S(1)} %get-tuple-element.562.refs_0_), channel_id=1, source_target_pairs={{3,0},{2,1},{1,2},{0,3},{7,4},{6,5},{5,6},{4,7},{11,8},{10,9},{9,1... | collective-permute-start | bytes 356360 | tf_op jit(solution)/shard_map/ppermute | solution.py:1108
  256.5 7.8 %collective-permute-start.65 = (f32[232,128]{1,0:T(8,128)S(1)}, f32[232,128]{1,0:T(8,128)S(1)}, u32[]{:S(2)}, u32[]{:S(2)}) collective-permute-start(f32[232,128]{1,0:T(8,128)S(1)} %get-tuple-element.562.refs_0_), channel_id=1, source_target_pairs={{2,0},{3,1},{0,2},{1,3},{6,4},{7,5},{4,6},{5,7},{10,8},{11,9},{8,1... | collective-permute-start | bytes 356360 | tf_op jit(solution)/shard_map/ppermute | solution.py:1108
  257.4 6.9 %collective-permute-start.64 = (f32[232,128]{1,0:T(8,128)S(1)}, f32[232,128]{1,0:T(8,128)S(1)}, u32[]{:S(2)}, u32[]{:S(2)}) collective-permute-start(f32[232,128]{1,0:T(8,128)S(1)} %get-tuple-element.562.refs_0_), channel_id=1, source_target_pairs={{1,0},{0,1},{3,2},{2,3},{5,4},{4,5},{7,6},{6,7},{9,8},{8,9},{11,10... | collective-permute-start | bytes 356360 | tf_op jit(solution)/shard_map/ppermute | solution.py:1108
  258.3 5.9 %collective-permute-start.59 = (bf16[256,1536]{1,0:T(8,128)(2,1)S(1)}, bf16[256,1536]{1,0:T(8,128)(2,1)S(1)}, u32[]{:S(2)}, u32[]{:S(2)}) collective-permute-start(bf16[256,1536]{1,0:T(8,128)(2,1)S(1)} %collective-permute-done.57.refs_2_), channel_id=1, source_target_pairs={{1,0},{0,1},{3,2},{2,3},{5,4},{4,5},{7,6},{6,7},{9,8},{8,9},{11,10... | collective-permute-start | bytes 2359304 | tf_op jit(solution)/shard_map/ppermute | solution.py:1108
  263.8 2.6 collective-permute-start.58
  (64 other events, 718.5 us)
